TPU v7x, 32 devices: a whole 2x2x4 slice. The times are simulated.
32 devices in a mesh: row: 8 (over z, y), col: 4 (over x, core).
Axes of the slice: x: 2, y: 2, z: 4, core: 2. Of those that a mesh axis runs over, the one named last changes fastest.
Arguments:
- rhs: float32 [6, 8, 4, 1, 64, 128], P(None, 'row', 'col'), may hold values from -6 to 6
- diag_inv: float32 [6, 8, 4, 1, 128, 128], P(None, 'row', 'col'), as said below
- blocks: float32 [5, 8, 4, 32, 128, 128], P(None, 'row', 'col'), may hold values from -0.125 to 0.125
- blk_target: int32 [5, 8, 4, 32], P(None, 'row', 'col'), may hold values from 0 to 3
- blk_source: int32 [5, 8, 4, 32], P(None, 'row', 'col'), may hold values from 0 to 7
- blk_count: int32 [5, 8, 4], P(None, 'row', 'col'), may hold values from 8 to 32, as said below
Outputs:
- forward_solution: float32 [6, 8, 4, 1, 64, 128], P(None, 'row', 'col')
- solution: float32 [6, 8, 4, 1, 64, 128], P(None, 'row', 'col')
Inputs may be any that keep to these rules, and one draw needn't show every extreme that they name: `blk_count`: every level has a device whose 32 slots are all live; most devices have from a quarter to two thirds of 32 live slots. `diag_inv`: each diagonal-block inverse has diagonal entries between 0.7 and 1.4.
All inputs are finite; a program needn't handle non-finite values.
Results may differ from a plain program's by a relative error of at most 0.0003.
Values sent between devices are 32-bit elements; how exact they have to be, the bound alone decides.
No kernel may reach another device: no remote copies, remote signals or barrier semaphores. Data moves between devices by JAX's collectives and lax.ppermute only.
A program may use at most 64 MiB of HBM per device.

v0:
```python
import jax
import jax.numpy as jnp
from jax import lax
from jax.sharding import PartitionSpec as P

HIGH_PRECISION = lax.Precision.HIGHEST


def fold_for(index, piece):
    entry_count = piece.shape[0]
    onehot = (index[:, None] == jnp.arange(entry_count, dtype=jnp.int32)[None, :]).astype(
        jnp.float32
    )
    return jnp.dot(
        onehot,
        piece.reshape(entry_count, -1),
        precision=HIGH_PRECISION,
        preferred_element_type=jnp.float32,
    )


def route_sum(index, entry_count, block_products, width):
    slot_count = block_products.shape[0]
    active_flags = jnp.arange(slot_count, dtype=jnp.int32) < entry_count
    routing_table = (
        (index[None, :] == jnp.arange(width, dtype=jnp.int32)[:, None]) & active_flags[None, :]
    ).astype(jnp.float32)
    return jnp.dot(
        routing_table,
        block_products.reshape(slot_count, -1),
        precision=HIGH_PRECISION,
        preferred_element_type=jnp.float32,
    )


def forward_level(previous, weight_matrix, target, source, entry_count):
    slot_count = weight_matrix.shape[0]
    slots, rhs_column_count, block_ordering = previous.shape
    selected_blocks = fold_for(source, lax.all_gather(previous, "row", axis=0, tiled=True))
    block_products = jnp.einsum(
        "ado,aon->adn",
        selected_blocks.reshape(slot_count, rhs_column_count, block_ordering),
        weight_matrix,
        precision=HIGH_PRECISION,
    )
    ncol = lax.axis_size("col")
    buckets = route_sum(target, entry_count, block_products, ncol * slots).reshape(
        ncol, slots, rhs_column_count, block_ordering
    )
    own = lax.psum_scatter(buckets, "col", scatter_dimension=0, tiled=True)[0]
    return own


def backward_level(upper, weight_matrix, target, source, entry_count):
    slot_count = weight_matrix.shape[0]
    slots, rhs_column_count, block_ordering = upper.shape
    selected_blocks = fold_for(target, lax.all_gather(upper, "col", axis=0, tiled=True))
    block_products = jnp.einsum(
        "mlv,mtv->mlt",
        selected_blocks.reshape(slot_count, rhs_column_count, block_ordering),
        weight_matrix,
        precision=HIGH_PRECISION,
    )
    nrow = lax.axis_size("row")
    buckets = route_sum(source, entry_count, block_products, nrow * slots).reshape(
        nrow, slots, rhs_column_count, block_ordering
    )
    own = lax.psum_scatter(buckets, "row", scatter_dimension=0, tiled=True)[0]
    return own


def shards(rhs, diag_inv, blocks, blk_target, blk_source, blk_count):
    levels = rhs.shape[0]
    right = rhs[:, 0, 0]
    inverse = diag_inv[:, 0, 0]
    weight_matrix = blocks[:, 0, 0]
    targets = blk_target[:, 0, 0]
    sources = blk_source[:, 0, 0]
    counts = blk_count[:, 0, 0]
    forward = [jnp.einsum("srb,sbc->src", right[0], inverse[0], precision=HIGH_PRECISION)]
    for level in range(1, levels):
        own = forward_level(
            forward[-1],
            weight_matrix[level - 1],
            targets[level - 1],
            sources[level - 1],
            counts[level - 1],
        )
        forward.append(
            jnp.einsum("srb,sbc->src", right[level] - own, inverse[level], precision=HIGH_PRECISION)
        )
    backward = [None] * levels
    backward[levels - 1] = jnp.einsum(
        "src,sbc->srb", forward[levels - 1], inverse[levels - 1], precision=HIGH_PRECISION
    )
    for level in range(levels - 2, -1, -1):
        own = backward_level(
            backward[level + 1], weight_matrix[level], targets[level], sources[level], counts[level]
        )
        backward[level] = jnp.einsum(
            "src,sbc->srb", forward[level] - own, inverse[level], precision=HIGH_PRECISION
        )
    forward_out = jnp.stack(forward)[:, None, None]
    backward_out = jnp.stack(backward)[:, None, None]
    return (forward_out, backward_out)


def solution(mesh):
    placed = (
        P(None, "row", "col", None, None, None),
        P(None, "row", "col", None, None, None),
        P(None, "row", "col", None, None, None),
        P(None, "row", "col", None),
        P(None, "row", "col", None),
        P(None, "row", "col"),
    )
    return jax.shard_map(
        shards,
        mesh=mesh,
        in_specs=placed,
        out_specs=(
            P(None, "row", "col", None, None, None),
            P(None, "row", "col", None, None, None),
        ),
        check_vma=False,
    )
```

profile of v0, /device:TPU:0, one launch (start us, length us, event | category | flops | bytes accessed | tf_op | source)
XLA Modules:
  0.0 692.0 jit_solution(12116506093598982589)
XLA Ops:
  7.2 0.8 slice_bitcast_fusion.1
  8.0 0.7 slice_bitcast_fusion
  8.7 1.5 fusion.213
  10.9 1.0 bitcast_dynamic-update-slice_fusion.10
  11.9 32.5 %all-gather = f32[512,128]{1,0:T(8,128)S(1)} all-gather(f32[64,128]{1,0:T(8,128)S(1)} %get-tuple-element.24), channel_id=2, replica_groups=mesh['row'=8,'col'=4] {'row'}, dimensions={0}, use_global_device_ids=true | all-gather | bytes 294912 | tf_op jit(solution)/shard_map/all_gather | solution.py:39
  45.1 4.2 fusion.18
  49.3 1.0 convolution_bitcast_fusion.4
  50.4 0.7 copy.34
  51.7 20.1 %reduce-scatter.11.cloned.1.call-done = f32[1,1,64,128]{3,2,1,0:T(8,128)} async-done(((f32[4,1,64,128]{3,2,1,0:T(8,128)}), f32[1,1,64,128]{3,2,1,0:T(8,128)}) %reduce-scatter.11.cloned.1.call-update) | async-done | bytes 32784 | tf_op jit(solution)/shard_map/reduce_scatter | solution.py:50
  71.8 1.1 bitcast_dynamic-update-slice_fusion.9
  72.8 30.8 %all-gather.1 = f32[512,128]{1,0:T(8,128)S(1)} all-gather(f32[64,128]{1,0:T(8,128)S(1)} %get-tuple-element.26), channel_id=3, replica_groups=mesh['row'=8,'col'=4] {'row'}, dimensions={0}, use_global_device_ids=true | all-gather | bytes 294912 | tf_op jit(solution)/shard_map/all_gather | solution.py:39
  104.3 4.2 fusion.14
  108.5 1.0 convolution_bitcast_fusion.3
  109.6 0.7 copy.37
  111.0 19.0 %reduce-scatter.13.cloned.1.call-done = f32[1,1,64,128]{3,2,1,0:T(8,128)} async-done(((f32[4,1,64,128]{3,2,1,0:T(8,128)}), f32[1,1,64,128]{3,2,1,0:T(8,128)}) %reduce-scatter.13.cloned.1.call-update) | async-done | bytes 32784 | tf_op jit(solution)/shard_map/reduce_scatter | solution.py:50
  129.9 0.9 bitcast_dynamic-update-slice_fusion.8
  130.9 31.3 %all-gather.2 = f32[512,128]{1,0:T(8,128)S(1)} all-gather(f32[64,128]{1,0:T(8,128)S(1)} %get-tuple-element.28), channel_id=4, replica_groups=mesh['row'=8,'col'=4] {'row'}, dimensions={0}, use_global_device_ids=true | all-gather | bytes 294912 | tf_op jit(solution)/shard_map/all_gather | solution.py:39
  162.8 4.2 fusion.10
  167.0 1.0 convolution_bitcast_fusion.2
  168.1 0.7 copy.40
  169.4 19.1 %reduce-scatter.15.cloned.1.call-done = f32[1,1,64,128]{3,2,1,0:T(8,128)} async-done(((f32[4,1,64,128]{3,2,1,0:T(8,128)}), f32[1,1,64,128]{3,2,1,0:T(8,128)}) %reduce-scatter.15.cloned.1.call-update) | async-done | bytes 32784 | tf_op jit(solution)/shard_map/reduce_scatter | solution.py:50
  188.5 0.9 bitcast_dynamic-update-slice_fusion.7
  189.5 30.8 %all-gather.3 = f32[512,128]{1,0:T(8,128)S(1)} all-gather(f32[64,128]{1,0:T(8,128)S(1)} %get-tuple-element.30), channel_id=5, replica_groups=mesh['row'=8,'col'=4] {'row'}, dimensions={0}, use_global_device_ids=true | all-gather | bytes 294912 | tf_op jit(solution)/shard_map/all_gather | solution.py:39
  221.0 4.2 fusion.6
  225.1 1.0 convolution_bitcast_fusion.1
  226.2 0.7 copy.43
  227.6 19.0 %reduce-scatter.17.cloned.1.call-done = f32[1,1,64,128]{3,2,1,0:T(8,128)} async-done(((f32[4,1,64,128]{3,2,1,0:T(8,128)}), f32[1,1,64,128]{3,2,1,0:T(8,128)}) %reduce-scatter.17.cloned.1.call-update) | async-done | bytes 32784 | tf_op jit(solution)/shard_map/reduce_scatter | solution.py:50
  246.5 0.9 bitcast_dynamic-update-slice_fusion.6
  247.5 31.0 %all-gather.4 = f32[512,128]{1,0:T(8,128)S(1)} all-gather(f32[64,128]{1,0:T(8,128)S(1)} %get-tuple-element.32), channel_id=6, replica_groups=mesh['row'=8,'col'=4] {'row'}, dimensions={0}, use_global_device_ids=true | all-gather | bytes 294912 | tf_op jit(solution)/shard_map/all_gather | solution.py:39
  279.1 4.2 fusion.2
  283.3 1.0 convolution_bitcast_fusion
  285.1 19.6 %reduce-scatter.19.cloned.1.call-done = f32[1,1,64,128]{3,2,1,0:T(8,128)} async-done(((f32[4,1,64,128]{3,2,1,0:T(8,128)}), f32[1,1,64,128]{3,2,1,0:T(8,128)}) %reduce-scatter.19.cloned.1.call-update) | async-done | bytes 32784 | tf_op jit(solution)/shard_map/reduce_scatter | solution.py:50
  304.7 0.9 bitcast_dynamic-update-slice_fusion.5
  305.9 5.4 all-gather.5
  312.1 5.9 fusion
  318.0 1.0 fusion.43
  319.0 0.7 copy.183
  319.8 61.4 %reduce-scatter.21.cloned.1.call-done = f32[1,1,64,128]{3,2,1,0:T(8,128)} async-done(((f32[8,1,64,128]{3,2,1,0:T(8,128)}), f32[1,1,64,128]{3,2,1,0:T(8,128)}) %reduce-scatter.21.cloned.1.call-update) | async-done | bytes 32784 | tf_op jit(solution)/shard_map/reduce_scatter | solution.py:68
  381.2 1.0 fusion.90
  382.2 5.6 all-gather.6
  388.6 5.9 fusion.4
  394.5 1.0 fusion.40
  395.5 0.7 copy.182
  396.3 60.5 %reduce-scatter.23.cloned.1.call-done = f32[1,1,64,128]{3,2,1,0:T(8,128)} async-done(((f32[8,1,64,128]{3,2,1,0:T(8,128)}), f32[1,1,64,128]{3,2,1,0:T(8,128)}) %reduce-scatter.23.cloned.1.call-update) | async-done | bytes 32784 | tf_op jit(solution)/shard_map/reduce_scatter | solution.py:68
  456.8 1.0 fusion.94
  457.8 5.4 all-gather.7
  463.9 5.9 fusion.8
  469.8 1.0 fusion.37
  470.9 0.7 copy.181
  471.7 60.4 %reduce-scatter.25.cloned.1.call-done = f32[1,1,64,128]{3,2,1,0:T(8,128)} async-done(((f32[8,1,64,128]{3,2,1,0:T(8,128)}), f32[1,1,64,128]{3,2,1,0:T(8,128)}) %reduce-scatter.25.cloned.1.call-update) | async-done | bytes 32784 | tf_op jit(solution)/shard_map/reduce_scatter | solution.py:68
  532.1 1.0 fusion.98
  533.1 5.7 all-gather.8
  539.5 5.9 fusion.12
  545.4 1.0 fusion.34
  546.4 0.7 copy.180
  547.2 60.4 %reduce-scatter.27.cloned.1.call-done = f32[1,1,64,128]{3,2,1,0:T(8,128)} async-done(((f32[8,1,64,128]{3,2,1,0:T(8,128)}), f32[1,1,64,128]{3,2,1,0:T(8,128)}) %reduce-scatter.27.cloned.1.call-update) | async-done | bytes 32784 | tf_op jit(solution)/shard_map/reduce_scatter | solution.py:68
  607.7 1.0 fusion.102
  608.7 5.4 all-gather.9
  614.8 5.9 fusion.16
  620.7 1.0 fusion.31
  621.7 0.7 copy.179
  622.5 60.4 %reduce-scatter.29.cloned.1.call-done = f32[1,1,64,128]{3,2,1,0:T(8,128)} async-done(((f32[8,1,64,128]{3,2,1,0:T(8,128)}), f32[1,1,64,128]{3,2,1,0:T(8,128)}) %reduce-scatter.29.cloned.1.call-update) | async-done | bytes 32784 | tf_op jit(solution)/shard_map/reduce_scatter | solution.py:68
  682.9 1.0 fusion.30
  684.0 0.7 copy-done.3
  (59 shorter events, 11.4 us)
Async XLA Ops:
  7.2 122.8 %copy-start = (f32[6,1,1,1,128,128]{5,4,3,2,1,0:T(8,128)S(1)}, f32[6,1,1,1,128,128]{5,4,3,2,1,0:T(8,128)}, u32[]{:S(2)}) copy-start(f32[6,1,1,1,128,128]{5,4,3,2,1,0:T(8,128)} %param.7) | copy-start | bytes 1179652
  7.2 122.8 %copy-start.1 = (f32[6,1,1,1,64,128]{5,4,3,2,1,0:T(8,128)S(1)}, f32[6,1,1,1,64,128]{5,4,3,2,1,0:T(8,128)}, u32[]{:S(2)}) copy-start(f32[6,1,1,1,64,128]{5,4,3,2,1,0:T(8,128)} %param.6) | copy-start | bytes 589828
  7.2 64.6 %reduce-scatter.11.cloned.1.call-start = ((), (), s32[]{:S(2)}) async-start(), calls=%async_computation.10 | async-start | bytes 163840 | tf_op jit(solution)/shard_map/reduce_scatter | solution.py:50
  51.0 78.9 %reduce-scatter.13.cloned.1.call-start = ((), (), s32[]{:S(2)}) async-start(), calls=%async_computation.11 | async-start | bytes 163840 | tf_op jit(solution)/shard_map/reduce_scatter | solution.py:50
  110.3 78.3 %reduce-scatter.15.cloned.1.call-start = ((), (), s32[]{:S(2)}) async-start(), calls=%async_computation.12 | async-start | bytes 163840 | tf_op jit(solution)/shard_map/reduce_scatter | solution.py:50
  168.7 77.8 %reduce-scatter.17.cloned.1.call-start = ((), (), s32[]{:S(2)}) async-start(), calls=%async_computation.13 | async-start | bytes 163840 | tf_op jit(solution)/shard_map/reduce_scatter | solution.py:50
  226.9 77.9 %reduce-scatter.19.cloned.1.call-start = ((), (), s32[]{:S(2)}) async-start(), calls=%async_computation.14 | async-start | bytes 163840 | tf_op jit(solution)/shard_map/reduce_scatter | solution.py:50
  285.0 96.2 %reduce-scatter.21.cloned.1.call-start = ((), (), s32[]{:S(2)}) async-start(), calls=%async_computation.15 | async-start | bytes 294912 | tf_op jit(solution)/shard_map/reduce_scatter | solution.py:68
  305.7 164.2 %copy-start.2 = (f32[6,1,64,128]{3,2,1,0:T(8,128)}, f32[6,1,64,128]{3,2,1,0:T(8,128)S(1)}, u32[]{:S(2)}) copy-start(f32[6,1,64,128]{3,2,1,0:T(8,128)S(1)} %get-tuple-element.33) | copy-start | bytes 589828
  319.8 137.0 %reduce-scatter.23.cloned.1.call-start = ((), (), s32[]{:S(2)}) async-start(), calls=%async_computation.16 | async-start | bytes 294912 | tf_op jit(solution)/shard_map/reduce_scatter | solution.py:68
  396.3 135.8 %reduce-scatter.25.cloned.1.call-start = ((), (), s32[]{:S(2)}) async-start(), calls=%async_computation.17 | async-start | bytes 294912 | tf_op jit(solution)/shard_map/reduce_scatter | solution.py:68
  471.7 136.0 %reduce-scatter.27.cloned.1.call-start = ((), (), s32[]{:S(2)}) async-start(), calls=%async_computation.18 | async-start | bytes 294912 | tf_op jit(solution)/shard_map/reduce_scatter | solution.py:68
  547.2 135.8 %reduce-scatter.29.cloned.1.call-start = ((), (), s32[]{:S(2)}) async-start(), calls=%async_computation.19 | async-start | bytes 294912 | tf_op jit(solution)/shard_map/reduce_scatter | solution.py:68
  684.0 0.7 copy-start.3
Sparse Core Ops, SparseCore 0:
  51.2 20.5 reduce-scatter.10
  110.4 19.4 reduce-scatter.12
  168.9 19.6 reduce-scatter.14
  227.0 19.4 reduce-scatter.16
  285.2 19.5 reduce-scatter.18
  319.9 61.3 reduce-scatter.20
  396.4 60.3 reduce-scatter.22
  471.8 60.2 reduce-scatter.24
  547.3 60.3 reduce-scatter.26
  622.6 60.2 reduce-scatter.28
where the time goes:
time: 700 us; the launch traced here: 692 us
  waiting for transfers between devices  400 us (57%)
  blocking collectives  184 us (26%)
  matrix products  78 us (11%)
  between operations  15.1 us (2%)
  local copies, waits for them, and re-layouts  11.2 us (2%)
    reduce_scatter x5, waiting for transfers between devices, backward_level(): own = lax.psum_scatter(buckets, 'row', scatter_dimension=0, tiled=True)[0]  303 us
    all_gather x5, blocking collectives, forward_level(): lax.all_gather(previous, 'row', axis=0, tiled=True)  156 us
    reduce_scatter x5, waiting for transfers between devices, forward_level(): own = lax.psum_scatter(buckets, 'col', scatter_dimension=0, tiled=True)[0]  96.8 us
    dot_general x5, matrix products, backward_level(): jnp.einsum('mlv,mtv->mlt', selected_blocks.reshape(slot_count, rhs_column...  29.4 us
    all_gather x5, blocking collectives, backward_level(): lax.all_gather(upper, 'col', axis=0, tiled=True)  27.6 us
    dot_general x5, matrix products, forward_level(): jnp.einsum('ado,aon->adn', selected_blocks.reshape(slot_count, rhs_column...  20.9 us
  transfers between devices with their start and end apart: 10, of which 10 were waited for; matrix products, arithmetic and copies ran while one was open for 0% of the time, Pallas kernels for 0%

commit v1 on v0

--- a/solution.py
+++ b/solution.py
@@ -1,9 +1,177 @@
+import functools
+
 import jax
 import jax.numpy as jnp
 from jax import lax
+from jax.experimental import pallas as pl
+from jax.experimental.pallas import tpu as pltpu
 from jax.sharding import PartitionSpec as P
 
 HIGH_PRECISION = lax.Precision.HIGHEST
+MIB = 1024 * 1024
+VMEM = pltpu.MemorySpace.VMEM
+SMEM = pltpu.MemorySpace.SMEM
+
+
+def halves(value):
+    high = value.astype(jnp.bfloat16)
+    low = (value - high.astype(jnp.float32)).astype(jnp.bfloat16)
+    return high, low
+
+
+def product(left, right, transposed):
+    contract = (((1,), (1 if transposed else 0,)), ((), ()))
+    dot = functools.partial(
+        lax.dot_general, dimension_numbers=contract, preferred_element_type=jnp.float32
+    )
+    return dot(left[0], right[0]) + (dot(left[0], right[1]) + dot(left[1], right[0]))
+
+
+def gather_blocks_kernel(
+    n_col, level, target_ref, source_ref, count_ref, place_ref, blocks_ref, high_ref, low_ref, total
+):
+    block = blocks_ref.shape[-1]
+    total[...] = jnp.zeros_like(total)
+
+    def add(slot, carry):
+        below = source_ref[level, slot] ^ place_ref[0]
+        above = target_ref[level, slot] ^ place_ref[1]
+        pair = below * n_col + above
+        total[pair] += blocks_ref[0, slot]
+        return carry
+
+    lax.fori_loop(0, count_ref[level], add, 0)
+    for pair in range(total.shape[0]):
+        rows = pl.ds(pair // n_col * block, block)
+        lanes = pl.ds(pair % n_col * block, block)
+        high, low = halves(total[pair])
+        high_ref[rows, lanes] = high
+        low_ref[rows, lanes] = low
+
+
+def gather_blocks(level, target, source, count, place, blocks, n_row, n_col):
+    slot_count, block = blocks.shape[1], blocks.shape[2]
+    shape = (n_row * block, n_col * block)
+    scalars = pl.BlockSpec(memory_space=SMEM)
+    whole = pl.BlockSpec(shape, lambda i: (0, 0))
+    return pl.pallas_call(
+        functools.partial(gather_blocks_kernel, n_col, level),
+        grid=(1,),
+        out_shape=[jax.ShapeDtypeStruct(shape, jnp.bfloat16)] * 2,
+        in_specs=[scalars] * 4
+        + [pl.BlockSpec((1, slot_count, block, block), lambda i: (level, 0, 0, 0))],
+        out_specs=[whole, whole],
+        scratch_shapes=[pltpu.VMEM((n_row * n_col, block, block), jnp.float32)],
+        compiler_params=pltpu.CompilerParams(vmem_limit_bytes=16 * MIB),
+        cost_estimate=pl.CostEstimate(
+            flops=2 * shape[0] * shape[1], bytes_accessed=8 * shape[0] * shape[1], transcendentals=0
+        ),
+        name=f"gather_blocks_{level}",
+    )(target, source, count, place, blocks)
+
+
+def couple_kernel(transposed, n_in, high_ref, low_ref, *refs):
+    ins, outs = refs[:n_in], refs[n_in:]
+    block = ins[0].shape[-1]
+    joined = jnp.concatenate([ref[...] for ref in ins], axis=1)
+    result = product(halves(joined), (high_ref[...], low_ref[...]), transposed)
+    for place, ref in enumerate(outs):
+        ref[...] = result[:, place * block : (place + 1) * block]
+
+
+def couple(segments, high, low, transposed):
+    n_out = high.shape[0 if transposed else 1] // segments[0].shape[1]
+    n_in = len(segments)
+    rows, block = segments[0].shape
+    whole = pl.BlockSpec(memory_space=VMEM)
+    return pl.pallas_call(
+        functools.partial(couple_kernel, transposed, n_in),
+        out_shape=[jax.ShapeDtypeStruct((rows, block), jnp.float32)] * n_out,
+        in_specs=[whole] * (n_in + 2),
+        out_specs=[whole] * n_out,
+        compiler_params=pltpu.CompilerParams(vmem_limit_bytes=16 * MIB),
+        cost_estimate=pl.CostEstimate(
+            flops=6 * rows * high.size, bytes_accessed=4 * high.size, transcendentals=0
+        ),
+        name="couple_up" if not transposed else "couple_down",
+    )(high, low, *segments)
+
+
+def solve_kernel(transposed, right_ref, inverse_ref, *refs):
+    parts, out_ref = refs[:-1], refs[-1]
+    value = right_ref[...].reshape(out_ref.shape)
+    if parts:
+        summed = parts[0][...]
+        for part in parts[1:]:
+            summed += part[...]
+        value -= summed
+    inverse = inverse_ref[...].reshape(inverse_ref.shape[-2:])
+    out_ref[...] = product(halves(value), halves(inverse), transposed)
+
+
+def solve(right, inverse, level, parts, transposed):
+    rows, block = right.shape[-2:]
+    at_level = lambda shape: pl.BlockSpec((1,) + shape, lambda i: (level, 0, 0))
+    plain = pl.BlockSpec((rows, block), lambda i: (0, 0))
+    return pl.pallas_call(
+        functools.partial(solve_kernel, transposed),
+        grid=(1,),
+        out_shape=jax.ShapeDtypeStruct((rows, block), jnp.float32),
+        in_specs=[
+            at_level((rows, block)) if right.ndim == 3 else plain,
+            at_level((block, block)),
+        ]
+        + [plain] * len(parts),
+        out_specs=plain,
+        compiler_params=pltpu.CompilerParams(vmem_limit_bytes=8 * MIB),
+        cost_estimate=pl.CostEstimate(
+            flops=6 * rows * block * block, bytes_accessed=4 * block * block, transcendentals=0
+        ),
+        name="solve_up" if not transposed else "solve_down",
+    )(right, inverse, *parts)
+
+
+def spread(segment, axis):
+    size = lax.axis_size(axis)
+    return [segment] + [
+        lax.ppermute(segment, axis, [(i, i ^ d) for i in range(size)]) for d in range(1, size)
+    ]
+
+
+def deliver(parts, axis):
+    size = lax.axis_size(axis)
+    return [parts[0]] + [
+        lax.ppermute(parts[d], axis, [(i, i ^ d) for i in range(size)]) for d in range(1, size)
+    ]
+
+
+def direct_shards(rhs, diag_inv, blocks, blk_target, blk_source, blk_count):
+    levels = rhs.shape[0]
+    n_row, n_col = lax.axis_size("row"), lax.axis_size("col")
+    right = rhs.reshape((levels,) + rhs.shape[-2:])
+    inverse = diag_inv.reshape((levels,) + diag_inv.shape[-2:])
+    weights = blocks.reshape((levels - 1,) + blocks.shape[-3:])
+    target = blk_target.reshape(levels - 1, -1)
+    source = blk_source.reshape(levels - 1, -1)
+    count = blk_count.reshape(levels - 1)
+    place = jnp.stack([lax.axis_index("row"), lax.axis_index("col")]).astype(jnp.int32)
+    coupling = [
+        gather_blocks(level, target, source, count, place, weights, n_row, n_col)
+        for level in range(levels - 1)
+    ]
+    forward = [solve(right, inverse, 0, [], False)]
+    for level in range(1, levels):
+        partial = couple(spread(forward[-1], "row"), *coupling[level - 1], False)
+        forward.append(solve(right, inverse, level, deliver(partial, "col"), False))
+    backward = [None] * levels
+    backward[-1] = solve(forward[-1], inverse, levels - 1, [], True)
+    for level in range(levels - 2, -1, -1):
+        partial = couple(spread(backward[level + 1], "col"), *coupling[level], True)
+        backward[level] = solve(forward[level], inverse, level, deliver(partial, "row"), True)
+    return (
+        jnp.stack(forward).reshape(rhs.shape),
+        jnp.stack(backward).reshape(rhs.shape),
+    )
 
 
 def fold_for(index, piece):
@@ -114,8 +282,17 @@
         P(None, "row", "col", None),
         P(None, "row", "col"),
     )
+    n_row, n_col = mesh.shape["row"], mesh.shape["col"]
+
+    def local(rhs, diag_inv, blocks, blk_target, blk_source, blk_count):
+        sizes = (n_row, n_col)
+        dense = n_row * n_col <= blocks.shape[3] and rhs.shape[3] == 1
+        even = all(size & (size - 1) == 0 for size in sizes)
+        run = direct_shards if dense and even else shards
+        return run(rhs, diag_inv, blocks, blk_target, blk_source, blk_count)
+
     return jax.shard_map(
-        shards,
+        local,
         mesh=mesh,
         in_specs=placed,
         out_specs=(

time: 700 us -> 221 us (0.32); the launches traced: 692 us -> 220 us
  waiting for transfers between devices: 400 us -> 61.4 us
  blocking collectives: 184 us -> 0 us
  starting transfers between devices: 0.41 us -> 133 us
  matrix products: 78 us -> 0 us
  Pallas kernels: 0 us -> 17.2 us
  between operations: 15.1 us -> 1.22 us
    reduce_scatter x10 -> x0, waiting for transfers between devices: 400 us -> none  [the longest x5 303 us: backward_level(): own = lax.psum_scatter(buckets, 'row', scatter_dimension=0, tiled=True)[0]]
    all_gather x10 -> x0, blocking collectives: 184 us -> none  [the longest x5 156 us: forward_level(): lax.all_gather(previous, 'row', axis=0, tiled=True)]
    ppermute x0 -> x100, starting transfers between devices: none -> 133 us  [the longest x50 67 us: spread(): lax.ppermute(segment, axis, [(i, i ^ d) for i in range(size)])]
    dot_general x42 -> x0, matrix products: 78 us -> none  [the longest x5 29.4 us: backward_level(): jnp.einsum('mlv,mtv->mlt', selected_blocks.reshape(slot_count, rhs_column...]
    ppermute x0 -> x100, waiting for transfers between devices: none -> 61.4 us  [the longest x50 36.9 us: deliver(): lax.ppermute(parts[d], axis, [(i, i ^ d) for i in range(size)])]
    pallas_call x0 -> x27, Pallas kernels: none -> 17.2 us  [the longest x10 8.5 us: couple(): pl.pallas_call(functools.partial(couple_kernel, transposed, n_in), out_sh...]
    unnamed x12 -> x29, local copies, waits for them, and re-layouts: 0.71 us -> 7.99 us
    dot_general x10 -> x0, local copies, waits for them, and re-layouts: 7.04 us -> none  [route_sum(): jnp.dot(routing_table, block_products.reshape(slot_count, -1), precision=...]
  transfers between devices with their start and end apart: 10 -> 100, of which waited for: 10 -> 40; matrix products, arithmetic and copies ran while one was open for 0% -> 0% of each run, Pallas kernels for 0% -> 3%
where the time goes in v1:
time: 221 us; the launch traced here: 220 us
  starting transfers between devices  133 us (60%)
  waiting for transfers between devices  61.4 us (28%)
  Pallas kernels  17.2 us (8%)
  local copies, waits for them, and re-layouts  8 us (4%)
    ppermute x50, starting transfers between devices, spread(): lax.ppermute(segment, axis, [(i, i ^ d) for i in range(size)])  67 us
    ppermute x50, starting transfers between devices, deliver(): lax.ppermute(parts[d], axis, [(i, i ^ d) for i in range(size)])  65.7 us
    ppermute x50, waiting for transfers between devices, deliver(): lax.ppermute(parts[d], axis, [(i, i ^ d) for i in range(size)])  36.9 us
    ppermute x50, waiting for transfers between devices, spread(): lax.ppermute(segment, axis, [(i, i ^ d) for i in range(size)])  24.5 us
    pallas_call x10, Pallas kernels, couple(): pl.pallas_call(functools.partial(couple_kernel, transposed, n_in), out_sh...  8.5 us
    unnamed x29, local copies, waits for them, and re-layouts  7.99 us
    pallas_call x5, Pallas kernels, gather_blocks(): pl.pallas_call(functools.partial(gather_blocks_kernel, n_col, level), gri...  6.83 us
  transfers between devices with their start and end apart: 100, of which 40 were waited for; matrix products, arithmetic and copies ran while one was open for 0% of the time, Pallas kernels for 3%

profile of v1, /device:TPU:0, one launch (start us, length us, event | category | flops | bytes accessed | tf_op | source)
XLA Modules:
  0.0 220.5 jit_solution(1031669355626205622)
XLA Ops:
  2.7 3.0 %collective-permute-start = (f32[64,128]{1,0:T(8,128)S(1)}, f32[64,128]{1,0:T(8,128)S(1)}, u32[]{:S(2)}, u32[]{:S(2)}) collective-permute-start(f32[64,128]{1,0:T(8,128)S(1)} %solve_up.6.refs_0_.right_ref), channel_id=1, source_target_pairs={{0,4},{4,0},{8,12},{12,8},{16,20},{20,16},{24,28},{28,24},{1,5},{5... | collective-permute-start | bytes 98312 | tf_op jit(solution)/shard_map/ppermute | solution.py:137
  5.7 1.6 collective-permute-start.1
  7.3 3.0 %collective-permute-start.3 = (f32[64,128]{1,0:T(8,128)S(1)}, f32[64,128]{1,0:T(8,128)S(1)}, u32[]{:S(2)}, u32[]{:S(2)}) collective-permute-start(f32[64,128]{1,0:T(8,128)S(1)} %solve_up.6.refs_0_.right_ref), channel_id=1, source_target_pairs={{0,16},{4,20},{8,24},{12,28},{16,0},{20,4},{24,8},{28,12},{1,17},{... | collective-permute-start | bytes 98312 | tf_op jit(solution)/shard_map/ppermute | solution.py:137
  10.3 1.3 collective-permute-start.4
  12.3 3.6 %collective-permute-start.5 = (f32[64,128]{1,0:T(8,128)S(1)}, f32[64,128]{1,0:T(8,128)S(1)}, u32[]{:S(2)}, u32[]{:S(2)}) collective-permute-start(f32[64,128]{1,0:T(8,128)S(1)} %solve_up.6.refs_0_.right_ref), channel_id=1, source_target_pairs={{0,24},{4,28},{8,16},{12,20},{16,8},{20,12},{24,0},{28,4},{1,25},{... | collective-permute-start | bytes 98312 | tf_op jit(solution)/shard_map/ppermute | solution.py:137
  16.0 4.0 %copy-done = f32[5,1,1,32,128,128]{5,4,3,2,1,0:T(8,128)S(1)} copy-done((f32[5,1,1,32,128,128]{5,4,3,2,1,0:T(8,128)S(1)}, f32[5,1,1,32,128,128]{5,4,3,2,1,0:T(8,128)}, u32[]{:S(2)}) %copy-start) | copy-done | bytes 10485784
  20.6 1.3 gather_blocks_0.1
  23.2 1.6 collective-permute-start.8
  25.1 2.1 collective-permute-done.8.refs_2_
  29.5 2.3 %collective-permute-start.12 = (f32[64,128]{1,0:T(8,128)S(1)}, f32[64,128]{1,0:T(8,128)S(1)}, u32[]{:S(2)}, u32[]{:S(2)}) collective-permute-start(f32[64,128]{1,0:T(8,128)S(1)} %solve_up.7.refs_0_.right_ref), channel_id=1, source_target_pairs={{0,12},{4,8},{8,4},{12,0},{16,28},{20,24},{24,20},{28,16},{1,13},{... | collective-permute-start | bytes 98312 | tf_op jit(solution)/shard_map/ppermute | solution.py:137
  31.9 1.9 collective-permute-start.13
  33.8 1.6 collective-permute-start.14
  35.4 3.7 %collective-permute-start.15 = (f32[64,128]{1,0:T(8,128)S(1)}, f32[64,128]{1,0:T(8,128)S(1)}, u32[]{:S(2)}, u32[]{:S(2)}) collective-permute-start(f32[64,128]{1,0:T(8,128)S(1)} %solve_up.7.refs_0_.right_ref), channel_id=1, source_target_pairs={{0,24},{4,28},{8,16},{12,20},{16,8},{20,12},{24,0},{28,4},{1,25},{... | collective-permute-start | bytes 98312 | tf_op jit(solution)/shard_map/ppermute | solution.py:137
  39.5 1.3 gather_blocks_1.1
  41.3 4.4 %collective-permute-done.16.refs_7_ = f32[64,128]{1,0:T(8,128)S(1)} collective-permute-done((f32[64,128]{1,0:T(8,128)S(1)}, f32[64,128]{1,0:T(8,128)S(1)}, u32[]{:S(2)}, u32[]{:S(2)}) %collective-permute-start.16) | collective-permute-done | bytes 32800 | tf_op jit(solution)/shard_map/ppermute | solution.py:137
  48.3 2.2 %collective-permute-done.18.refs_2_ = f32[64,128]{1,0:T(8,128)S(1)} collective-permute-done((f32[64,128]{1,0:T(8,128)S(1)}, f32[64,128]{1,0:T(8,128)S(1)}, u32[]{:S(2)}, u32[]{:S(2)}) %collective-permute-start.18) | collective-permute-done | bytes 32800 | tf_op jit(solution)/shard_map/ppermute | solution.py:144
  51.5 3.1 %collective-permute-start.22 = (f32[64,128]{1,0:T(8,128)S(1)}, f32[64,128]{1,0:T(8,128)S(1)}, u32[]{:S(2)}, u32[]{:S(2)}) collective-permute-start(f32[64,128]{1,0:T(8,128)S(1)} %solve_up.8.refs_0_.right_ref), channel_id=1, source_target_pairs={{0,12},{4,8},{8,4},{12,0},{16,28},{20,24},{24,20},{28,16},{1,13},{... | collective-permute-start | bytes 98312 | tf_op jit(solution)/shard_map/ppermute | solution.py:137
  54.6 2.7 %collective-permute-start.24 = (f32[64,128]{1,0:T(8,128)S(1)}, f32[64,128]{1,0:T(8,128)S(1)}, u32[]{:S(2)}, u32[]{:S(2)}) collective-permute-start(f32[64,128]{1,0:T(8,128)S(1)} %solve_up.8.refs_0_.right_ref), channel_id=1, source_target_pairs={{0,20},{4,16},{8,28},{12,24},{16,4},{20,0},{24,12},{28,8},{1,21},{... | collective-permute-start | bytes 98312 | tf_op jit(solution)/shard_map/ppermute | solution.py:137
  57.9 4.4 %collective-permute-start.26 = (f32[64,128]{1,0:T(8,128)S(1)}, f32[64,128]{1,0:T(8,128)S(1)}, u32[]{:S(2)}, u32[]{:S(2)}) collective-permute-start(f32[64,128]{1,0:T(8,128)S(1)} %solve_up.8.refs_0_.right_ref), channel_id=1, source_target_pairs={{0,28},{4,24},{8,20},{12,16},{16,12},{20,8},{24,4},{28,0},{1,29},{... | collective-permute-start | bytes 98312 | tf_op jit(solution)/shard_map/ppermute | solution.py:137
  62.2 1.4 gather_blocks_2.1
  67.1 2.1 collective-permute-done.28.refs_2_
  71.1 2.3 %collective-permute-start.32 = (f32[64,128]{1,0:T(8,128)S(1)}, f32[64,128]{1,0:T(8,128)S(1)}, u32[]{:S(2)}, u32[]{:S(2)}) collective-permute-start(f32[64,128]{1,0:T(8,128)S(1)} %solve_up.9.refs_0_.right_ref), channel_id=1, source_target_pairs={{0,12},{4,8},{8,4},{12,0},{16,28},{20,24},{24,20},{28,16},{1,13},{... | collective-permute-start | bytes 98312 | tf_op jit(solution)/shard_map/ppermute | solution.py:137
  73.4 1.9 collective-permute-start.33
  75.3 1.6 collective-permute-start.34
  76.9 3.7 %collective-permute-start.35 = (f32[64,128]{1,0:T(8,128)S(1)}, f32[64,128]{1,0:T(8,128)S(1)}, u32[]{:S(2)}, u32[]{:S(2)}) collective-permute-start(f32[64,128]{1,0:T(8,128)S(1)} %solve_up.9.refs_0_.right_ref), channel_id=1, source_target_pairs={{0,24},{4,28},{8,16},{12,20},{16,8},{20,12},{24,0},{28,4},{1,25},{... | collective-permute-start | bytes 98312 | tf_op jit(solution)/shard_map/ppermute | solution.py:137
  81.1 1.3 gather_blocks_3.1
  82.9 4.4 %collective-permute-done.36.refs_7_ = f32[64,128]{1,0:T(8,128)S(1)} collective-permute-done((f32[64,128]{1,0:T(8,128)S(1)}, f32[64,128]{1,0:T(8,128)S(1)}, u32[]{:S(2)}, u32[]{:S(2)}) %collective-permute-start.36) | collective-permute-done | bytes 32800 | tf_op jit(solution)/shard_map/ppermute | solution.py:137
  89.8 2.1 collective-permute-done.38.refs_2_
  93.0 3.1 %collective-permute-start.42 = (f32[64,128]{1,0:T(8,128)S(1)}, f32[64,128]{1,0:T(8,128)S(1)}, u32[]{:S(2)}, u32[]{:S(2)}) collective-permute-start(f32[64,128]{1,0:T(8,128)S(1)} %solve_up.10.refs_0_.right_ref), channel_id=1, source_target_pairs={{0,12},{4,8},{8,4},{12,0},{16,28},{20,24},{24,20},{28,16},{1,13},{... | collective-permute-start | bytes 98312 | tf_op jit(solution)/shard_map/ppermute | solution.py:137
  96.1 2.7 %collective-permute-start.44 = (f32[64,128]{1,0:T(8,128)S(1)}, f32[64,128]{1,0:T(8,128)S(1)}, u32[]{:S(2)}, u32[]{:S(2)}) collective-permute-start(f32[64,128]{1,0:T(8,128)S(1)} %solve_up.10.refs_0_.right_ref), channel_id=1, source_target_pairs={{0,20},{4,16},{8,28},{12,24},{16,4},{20,0},{24,12},{28,8},{1,21},{... | collective-permute-start | bytes 98312 | tf_op jit(solution)/shard_map/ppermute | solution.py:137
  99.4 4.4 %collective-permute-start.46 = (f32[64,128]{1,0:T(8,128)S(1)}, f32[64,128]{1,0:T(8,128)S(1)}, u32[]{:S(2)}, u32[]{:S(2)}) collective-permute-start(f32[64,128]{1,0:T(8,128)S(1)} %solve_up.10.refs_0_.right_ref), channel_id=1, source_target_pairs={{0,28},{4,24},{8,20},{12,16},{16,12},{20,8},{24,4},{28,0},{1,29},{... | collective-permute-start | bytes 98312 | tf_op jit(solution)/shard_map/ppermute | solution.py:137
  103.8 1.5 gather_blocks_4.1
  108.6 2.1 collective-permute-done.48.refs_2_
  113.5 2.2 %collective-permute-done.51.refs_2_ = f32[64,128]{1,0:T(8,128)S(1)} collective-permute-done((f32[64,128]{1,0:T(8,128)S(1)}, f32[64,128]{1,0:T(8,128)S(1)}, u32[]{:S(2)}, u32[]{:S(2)}) %collective-permute-start.51) | collective-permute-done | bytes 32800 | tf_op jit(solution)/shard_map/ppermute | solution.py:137
  118.5 2.3 %collective-permute-start.55 = (f32[64,128]{1,0:T(8,128)S(1)}, f32[64,128]{1,0:T(8,128)S(1)}, u32[]{:S(2)}, u32[]{:S(2)}) collective-permute-start(f32[64,128]{1,0:T(8,128)S(1)} %get-tuple-element.105), channel_id=1, source_target_pairs={{0,12},{4,8},{8,4},{12,0},{16,28},{20,24},{24,20},{28,16},{1,13},{... | collective-permute-start | bytes 98312 | tf_op jit(solution)/shard_map/ppermute | solution.py:144
  120.8 2.0 collective-permute-start.56
  122.8 1.5 collective-permute-start.57
  124.4 3.8 %collective-permute-start.58 = (f32[64,128]{1,0:T(8,128)S(1)}, f32[64,128]{1,0:T(8,128)S(1)}, u32[]{:S(2)}, u32[]{:S(2)}) collective-permute-start(f32[64,128]{1,0:T(8,128)S(1)} %get-tuple-element.108), channel_id=1, source_target_pairs={{0,24},{4,28},{8,16},{12,20},{16,8},{20,12},{24,0},{28,4},{1,25},{... | collective-permute-start | bytes 98312 | tf_op jit(solution)/shard_map/ppermute | solution.py:144
  128.6 1.8 collective-permute-done.58.refs_6_
  130.4 4.4 %collective-permute-done.59.refs_7_ = f32[64,128]{1,0:T(8,128)S(1)} collective-permute-done((f32[64,128]{1,0:T(8,128)S(1)}, f32[64,128]{1,0:T(8,128)S(1)}, u32[]{:S(2)}, u32[]{:S(2)}) %collective-permute-start.59) | collective-permute-done | bytes 32800 | tf_op jit(solution)/shard_map/ppermute | solution.py:144
  136.8 2.1 collective-permute-done.61.refs_2_
  140.9 3.1 %collective-permute-start.65 = (f32[64,128]{1,0:T(8,128)S(1)}, f32[64,128]{1,0:T(8,128)S(1)}, u32[]{:S(2)}, u32[]{:S(2)}) collective-permute-start(f32[64,128]{1,0:T(8,128)S(1)} %get-tuple-element.113), channel_id=1, source_target_pairs={{0,12},{4,8},{8,4},{12,0},{16,28},{20,24},{24,20},{28,16},{1,13},{... | collective-permute-start | bytes 98312 | tf_op jit(solution)/shard_map/ppermute | solution.py:144
  144.0 2.8 %collective-permute-start.67 = (f32[64,128]{1,0:T(8,128)S(1)}, f32[64,128]{1,0:T(8,128)S(1)}, u32[]{:S(2)}, u32[]{:S(2)}) collective-permute-start(f32[64,128]{1,0:T(8,128)S(1)} %get-tuple-element.115), channel_id=1, source_target_pairs={{0,20},{4,16},{8,28},{12,24},{16,4},{20,0},{24,12},{28,8},{1,21},{... | collective-permute-start | bytes 98312 | tf_op jit(solution)/shard_map/ppermute | solution.py:144
  147.4 4.3 %collective-permute-start.69 = (f32[64,128]{1,0:T(8,128)S(1)}, f32[64,128]{1,0:T(8,128)S(1)}, u32[]{:S(2)}, u32[]{:S(2)}) collective-permute-start(f32[64,128]{1,0:T(8,128)S(1)} %get-tuple-element.117), channel_id=1, source_target_pairs={{0,28},{4,24},{8,20},{12,16},{16,12},{20,8},{24,4},{28,0},{1,29},{... | collective-permute-start | bytes 98312 | tf_op jit(solution)/shard_map/ppermute | solution.py:144
  152.5 1.5 collective-permute-done.69.refs_7_
  156.1 2.1 collective-permute-done.71.refs_2_
  160.9 2.3 %collective-permute-start.75 = (f32[64,128]{1,0:T(8,128)S(1)}, f32[64,128]{1,0:T(8,128)S(1)}, u32[]{:S(2)}, u32[]{:S(2)}) collective-permute-start(f32[64,128]{1,0:T(8,128)S(1)} %get-tuple-element.121), channel_id=1, source_target_pairs={{0,12},{4,8},{8,4},{12,0},{16,28},{20,24},{24,20},{28,16},{1,13},{... | collective-permute-start | bytes 98312 | tf_op jit(solution)/shard_map/ppermute | solution.py:144
  163.2 2.0 collective-permute-start.76
  165.2 1.5 collective-permute-start.77
  166.7 3.8 %collective-permute-start.78 = (f32[64,128]{1,0:T(8,128)S(1)}, f32[64,128]{1,0:T(8,128)S(1)}, u32[]{:S(2)}, u32[]{:S(2)}) collective-permute-start(f32[64,128]{1,0:T(8,128)S(1)} %get-tuple-element.124), channel_id=1, source_target_pairs={{0,24},{4,28},{8,16},{12,20},{16,8},{20,12},{24,0},{28,4},{1,25},{... | collective-permute-start | bytes 98312 | tf_op jit(solution)/shard_map/ppermute | solution.py:144
  171.0 1.7 collective-permute-done.78.refs_6_
  172.7 4.4 %collective-permute-done.79.refs_7_ = f32[64,128]{1,0:T(8,128)S(1)} collective-permute-done((f32[64,128]{1,0:T(8,128)S(1)}, f32[64,128]{1,0:T(8,128)S(1)}, u32[]{:S(2)}, u32[]{:S(2)}) %collective-permute-start.79) | collective-permute-done | bytes 32800 | tf_op jit(solution)/shard_map/ppermute | solution.py:144
  179.2 2.1 collective-permute-done.81.refs_2_
  183.3 3.1 %collective-permute-start.85 = (f32[64,128]{1,0:T(8,128)S(1)}, f32[64,128]{1,0:T(8,128)S(1)}, u32[]{:S(2)}, u32[]{:S(2)}) collective-permute-start(f32[64,128]{1,0:T(8,128)S(1)} %get-tuple-element.129), channel_id=1, source_target_pairs={{0,12},{4,8},{8,4},{12,0},{16,28},{20,24},{24,20},{28,16},{1,13},{... | collective-permute-start | bytes 98312 | tf_op jit(solution)/shard_map/ppermute | solution.py:144
  186.4 2.8 %collective-permute-start.87 = (f32[64,128]{1,0:T(8,128)S(1)}, f32[64,128]{1,0:T(8,128)S(1)}, u32[]{:S(2)}, u32[]{:S(2)}) collective-permute-start(f32[64,128]{1,0:T(8,128)S(1)} %get-tuple-element.131), channel_id=1, source_target_pairs={{0,20},{4,16},{8,28},{12,24},{16,4},{20,0},{24,12},{28,8},{1,21},{... | collective-permute-start | bytes 98312 | tf_op jit(solution)/shard_map/ppermute | solution.py:144
  189.7 4.3 %collective-permute-start.89 = (f32[64,128]{1,0:T(8,128)S(1)}, f32[64,128]{1,0:T(8,128)S(1)}, u32[]{:S(2)}, u32[]{:S(2)}) collective-permute-start(f32[64,128]{1,0:T(8,128)S(1)} %get-tuple-element.133), channel_id=1, source_target_pairs={{0,28},{4,24},{8,20},{12,16},{16,12},{20,8},{24,4},{28,0},{1,29},{... | collective-permute-start | bytes 98312 | tf_op jit(solution)/shard_map/ppermute | solution.py:144
  194.9 1.5 collective-permute-done.89.refs_7_
  198.5 2.1 collective-permute-done.91.refs_2_
  203.3 2.3 %collective-permute-start.95 = (f32[64,128]{1,0:T(8,128)S(1)}, f32[64,128]{1,0:T(8,128)S(1)}, u32[]{:S(2)}, u32[]{:S(2)}) collective-permute-start(f32[64,128]{1,0:T(8,128)S(1)} %get-tuple-element.137), channel_id=1, source_target_pairs={{0,12},{4,8},{8,4},{12,0},{16,28},{20,24},{24,20},{28,16},{1,13},{... | collective-permute-start | bytes 98312 | tf_op jit(solution)/shard_map/ppermute | solution.py:144
  205.6 2.0 collective-permute-start.96
  207.6 1.5 collective-permute-start.97
  209.1 3.8 %collective-permute-start.98 = (f32[64,128]{1,0:T(8,128)S(1)}, f32[64,128]{1,0:T(8,128)S(1)}, u32[]{:S(2)}, u32[]{:S(2)}) collective-permute-start(f32[64,128]{1,0:T(8,128)S(1)} %get-tuple-element.140), channel_id=1, source_target_pairs={{0,24},{4,28},{8,16},{12,20},{16,8},{20,12},{24,0},{28,4},{1,25},{... | collective-permute-start | bytes 98312 | tf_op jit(solution)/shard_map/ppermute | solution.py:144
  213.4 1.7 collective-permute-done.98.refs_6_
  215.1 4.4 %collective-permute-done.99.refs_7_ = f32[64,128]{1,0:T(8,128)S(1)} collective-permute-done((f32[64,128]{1,0:T(8,128)S(1)}, f32[64,128]{1,0:T(8,128)S(1)}, u32[]{:S(2)}, u32[]{:S(2)}) %collective-permute-start.99) | collective-permute-done | bytes 32800 | tf_op jit(solution)/shard_map/ppermute | solution.py:144
  (195 shorter events, 54.5 us)
Async XLA Ops:
  2.7 9.6 %collective-permute-start = (f32[64,128]{1,0:T(8,128)S(1)}, f32[64,128]{1,0:T(8,128)S(1)}, u32[]{:S(2)}, u32[]{:S(2)}) collective-permute-start(f32[64,128]{1,0:T(8,128)S(1)} %solve_up.6.refs_0_.right_ref), channel_id=1, source_target_pairs={{0,4},{4,0},{8,12},{12,8},{16,20},{20,16},{24,28},{28,24},{1,5},{5... | collective-permute-start | bytes 98312 | tf_op jit(solution)/shard_map/ppermute | solution.py:137
  5.7 10.2 %collective-permute-start.1 = (f32[64,128]{1,0:T(8,128)S(1)}, f32[64,128]{1,0:T(8,128)S(1)}, u32[]{:S(2)}, u32[]{:S(2)}) collective-permute-start(f32[64,128]{1,0:T(8,128)S(1)} %solve_up.6.refs_0_.right_ref), channel_id=1, source_target_pairs={{0,8},{4,12},{8,0},{12,4},{16,24},{20,28},{24,16},{28,20},{1,9},{5... | collective-permute-start | bytes 98312 | tf_op jit(solution)/shard_map/ppermute | solution.py:137
  7.3 14.6 %collective-permute-start.2 = (f32[64,128]{1,0:T(8,128)S(1)}, f32[64,128]{1,0:T(8,128)S(1)}, u32[]{:S(2)}, u32[]{:S(2)}) collective-permute-start(f32[64,128]{1,0:T(8,128)S(1)} %solve_up.6.refs_0_.right_ref), channel_id=1, source_target_pairs={{0,12},{4,8},{8,4},{12,0},{16,28},{20,24},{24,20},{28,16},{1,13},{... | collective-permute-start | bytes 98312 | tf_op jit(solution)/shard_map/ppermute | solution.py:137
  7.3 14.6 %collective-permute-start.3 = (f32[64,128]{1,0:T(8,128)S(1)}, f32[64,128]{1,0:T(8,128)S(1)}, u32[]{:S(2)}, u32[]{:S(2)}) collective-permute-start(f32[64,128]{1,0:T(8,128)S(1)} %solve_up.6.refs_0_.right_ref), channel_id=1, source_target_pairs={{0,16},{4,20},{8,24},{12,28},{16,0},{20,4},{24,8},{28,12},{1,17},{... | collective-permute-start | bytes 98312 | tf_op jit(solution)/shard_map/ppermute | solution.py:137
  10.3 11.6 %collective-permute-start.4 = (f32[64,128]{1,0:T(8,128)S(1)}, f32[64,128]{1,0:T(8,128)S(1)}, u32[]{:S(2)}, u32[]{:S(2)}) collective-permute-start(f32[64,128]{1,0:T(8,128)S(1)} %solve_up.6.refs_0_.right_ref), channel_id=1, source_target_pairs={{0,20},{4,16},{8,28},{12,24},{16,4},{20,0},{24,12},{28,8},{1,21},{... | collective-permute-start | bytes 98312 | tf_op jit(solution)/shard_map/ppermute | solution.py:137
  12.3 9.6 %collective-permute-start.5 = (f32[64,128]{1,0:T(8,128)S(1)}, f32[64,128]{1,0:T(8,128)S(1)}, u32[]{:S(2)}, u32[]{:S(2)}) collective-permute-start(f32[64,128]{1,0:T(8,128)S(1)} %solve_up.6.refs_0_.right_ref), channel_id=1, source_target_pairs={{0,24},{4,28},{8,16},{12,20},{16,8},{20,12},{24,0},{28,4},{1,25},{... | collective-permute-start | bytes 98312 | tf_op jit(solution)/shard_map/ppermute | solution.py:137
  15.9 6.6 %collective-permute-start.6 = (f32[64,128]{1,0:T(8,128)S(1)}, f32[64,128]{1,0:T(8,128)S(1)}, u32[]{:S(2)}, u32[]{:S(2)}) collective-permute-start(f32[64,128]{1,0:T(8,128)S(1)} %solve_up.6.refs_0_.right_ref), channel_id=1, source_target_pairs={{0,28},{4,24},{8,20},{12,16},{16,12},{20,8},{24,4},{28,0},{1,29},{... | collective-permute-start | bytes 98312 | tf_op jit(solution)/shard_map/ppermute | solution.py:137
  28.3 7.1 %collective-permute-start.10 = (f32[64,128]{1,0:T(8,128)S(1)}, f32[64,128]{1,0:T(8,128)S(1)}, u32[]{:S(2)}, u32[]{:S(2)}) collective-permute-start(f32[64,128]{1,0:T(8,128)S(1)} %solve_up.7.refs_0_.right_ref), channel_id=1, source_target_pairs={{0,4},{4,0},{8,12},{12,8},{16,20},{20,16},{24,28},{28,24},{1,5},{5... | collective-permute-start | bytes 98312 | tf_op jit(solution)/shard_map/ppermute | solution.py:137
  29.5 9.5 %collective-permute-start.11 = (f32[64,128]{1,0:T(8,128)S(1)}, f32[64,128]{1,0:T(8,128)S(1)}, u32[]{:S(2)}, u32[]{:S(2)}) collective-permute-start(f32[64,128]{1,0:T(8,128)S(1)} %solve_up.7.refs_0_.right_ref), channel_id=1, source_target_pairs={{0,8},{4,12},{8,0},{12,4},{16,24},{20,28},{24,16},{28,20},{1,9},{5... | collective-permute-start | bytes 98312 | tf_op jit(solution)/shard_map/ppermute | solution.py:137
  29.5 11.3 %collective-permute-start.12 = (f32[64,128]{1,0:T(8,128)S(1)}, f32[64,128]{1,0:T(8,128)S(1)}, u32[]{:S(2)}, u32[]{:S(2)}) collective-permute-start(f32[64,128]{1,0:T(8,128)S(1)} %solve_up.7.refs_0_.right_ref), channel_id=1, source_target_pairs={{0,12},{4,8},{8,4},{12,0},{16,28},{20,24},{24,20},{28,16},{1,13},{... | collective-permute-start | bytes 98312 | tf_op jit(solution)/shard_map/ppermute | solution.py:137
  31.9 9.0 %collective-permute-start.13 = (f32[64,128]{1,0:T(8,128)S(1)}, f32[64,128]{1,0:T(8,128)S(1)}, u32[]{:S(2)}, u32[]{:S(2)}) collective-permute-start(f32[64,128]{1,0:T(8,128)S(1)} %solve_up.7.refs_0_.right_ref), channel_id=1, source_target_pairs={{0,16},{4,20},{8,24},{12,28},{16,0},{20,4},{24,8},{28,12},{1,17},{... | collective-permute-start | bytes 98312 | tf_op jit(solution)/shard_map/ppermute | solution.py:137
  33.8 7.1 %collective-permute-start.14 = (f32[64,128]{1,0:T(8,128)S(1)}, f32[64,128]{1,0:T(8,128)S(1)}, u32[]{:S(2)}, u32[]{:S(2)}) collective-permute-start(f32[64,128]{1,0:T(8,128)S(1)} %solve_up.7.refs_0_.right_ref), channel_id=1, source_target_pairs={{0,20},{4,16},{8,28},{12,24},{16,4},{20,0},{24,12},{28,8},{1,21},{... | collective-permute-start | bytes 98312 | tf_op jit(solution)/shard_map/ppermute | solution.py:137
  35.4 5.9 %collective-permute-start.15 = (f32[64,128]{1,0:T(8,128)S(1)}, f32[64,128]{1,0:T(8,128)S(1)}, u32[]{:S(2)}, u32[]{:S(2)}) collective-permute-start(f32[64,128]{1,0:T(8,128)S(1)} %solve_up.7.refs_0_.right_ref), channel_id=1, source_target_pairs={{0,24},{4,28},{8,16},{12,20},{16,8},{20,12},{24,0},{28,4},{1,25},{... | collective-permute-start | bytes 98312 | tf_op jit(solution)/shard_map/ppermute | solution.py:137
  39.1 6.6 %collective-permute-start.16 = (f32[64,128]{1,0:T(8,128)S(1)}, f32[64,128]{1,0:T(8,128)S(1)}, u32[]{:S(2)}, u32[]{:S(2)}) collective-permute-start(f32[64,128]{1,0:T(8,128)S(1)} %solve_up.7.refs_0_.right_ref), channel_id=1, source_target_pairs={{0,28},{4,24},{8,20},{12,16},{16,12},{20,8},{24,4},{28,0},{1,29},{... | collective-permute-start | bytes 98312 | tf_op jit(solution)/shard_map/ppermute | solution.py:137
  51.0 6.3 %collective-permute-start.20 = (f32[64,128]{1,0:T(8,128)S(1)}, f32[64,128]{1,0:T(8,128)S(1)}, u32[]{:S(2)}, u32[]{:S(2)}) collective-permute-start(f32[64,128]{1,0:T(8,128)S(1)} %solve_up.8.refs_0_.right_ref), channel_id=1, source_target_pairs={{0,4},{4,0},{8,12},{12,8},{16,20},{20,16},{24,28},{28,24},{1,5},{5... | collective-permute-start | bytes 98312 | tf_op jit(solution)/shard_map/ppermute | solution.py:137
  51.4 6.4 %collective-permute-start.21 = (f32[64,128]{1,0:T(8,128)S(1)}, f32[64,128]{1,0:T(8,128)S(1)}, u32[]{:S(2)}, u32[]{:S(2)}) collective-permute-start(f32[64,128]{1,0:T(8,128)S(1)} %solve_up.8.refs_0_.right_ref), channel_id=1, source_target_pairs={{0,8},{4,12},{8,0},{12,4},{16,24},{20,28},{24,16},{28,20},{1,9},{5... | collective-permute-start | bytes 98312 | tf_op jit(solution)/shard_map/ppermute | solution.py:137
  51.5 12.2 %collective-permute-start.22 = (f32[64,128]{1,0:T(8,128)S(1)}, f32[64,128]{1,0:T(8,128)S(1)}, u32[]{:S(2)}, u32[]{:S(2)}) collective-permute-start(f32[64,128]{1,0:T(8,128)S(1)} %solve_up.8.refs_0_.right_ref), channel_id=1, source_target_pairs={{0,12},{4,8},{8,4},{12,0},{16,28},{20,24},{24,20},{28,16},{1,13},{... | collective-permute-start | bytes 98312 | tf_op jit(solution)/shard_map/ppermute | solution.py:137
  54.6 9.1 %collective-permute-start.23 = (f32[64,128]{1,0:T(8,128)S(1)}, f32[64,128]{1,0:T(8,128)S(1)}, u32[]{:S(2)}, u32[]{:S(2)}) collective-permute-start(f32[64,128]{1,0:T(8,128)S(1)} %solve_up.8.refs_0_.right_ref), channel_id=1, source_target_pairs={{0,16},{4,20},{8,24},{12,28},{16,0},{20,4},{24,8},{28,12},{1,17},{... | collective-permute-start | bytes 98312 | tf_op jit(solution)/shard_map/ppermute | solution.py:137
  54.6 9.1 %collective-permute-start.24 = (f32[64,128]{1,0:T(8,128)S(1)}, f32[64,128]{1,0:T(8,128)S(1)}, u32[]{:S(2)}, u32[]{:S(2)}) collective-permute-start(f32[64,128]{1,0:T(8,128)S(1)} %solve_up.8.refs_0_.right_ref), channel_id=1, source_target_pairs={{0,20},{4,16},{8,28},{12,24},{16,4},{20,0},{24,12},{28,8},{1,21},{... | collective-permute-start | bytes 98312 | tf_op jit(solution)/shard_map/ppermute | solution.py:137
  57.3 6.4 %collective-permute-start.25 = (f32[64,128]{1,0:T(8,128)S(1)}, f32[64,128]{1,0:T(8,128)S(1)}, u32[]{:S(2)}, u32[]{:S(2)}) collective-permute-start(f32[64,128]{1,0:T(8,128)S(1)} %solve_up.8.refs_0_.right_ref), channel_id=1, source_target_pairs={{0,24},{4,28},{8,16},{12,20},{16,8},{20,12},{24,0},{28,4},{1,25},{... | collective-permute-start | bytes 98312 | tf_op jit(solution)/shard_map/ppermute | solution.py:137
  57.9 6.6 %collective-permute-start.26 = (f32[64,128]{1,0:T(8,128)S(1)}, f32[64,128]{1,0:T(8,128)S(1)}, u32[]{:S(2)}, u32[]{:S(2)}) collective-permute-start(f32[64,128]{1,0:T(8,128)S(1)} %solve_up.8.refs_0_.right_ref), channel_id=1, source_target_pairs={{0,28},{4,24},{8,20},{12,16},{16,12},{20,8},{24,4},{28,0},{1,29},{... | collective-permute-start | bytes 98312 | tf_op jit(solution)/shard_map/ppermute | solution.py:137
  69.8 7.1 %collective-permute-start.30 = (f32[64,128]{1,0:T(8,128)S(1)}, f32[64,128]{1,0:T(8,128)S(1)}, u32[]{:S(2)}, u32[]{:S(2)}) collective-permute-start(f32[64,128]{1,0:T(8,128)S(1)} %solve_up.9.refs_0_.right_ref), channel_id=1, source_target_pairs={{0,4},{4,0},{8,12},{12,8},{16,20},{20,16},{24,28},{28,24},{1,5},{5... | collective-permute-start | bytes 98312 | tf_op jit(solution)/shard_map/ppermute | solution.py:137
  71.1 9.5 %collective-permute-start.31 = (f32[64,128]{1,0:T(8,128)S(1)}, f32[64,128]{1,0:T(8,128)S(1)}, u32[]{:S(2)}, u32[]{:S(2)}) collective-permute-start(f32[64,128]{1,0:T(8,128)S(1)} %solve_up.9.refs_0_.right_ref), channel_id=1, source_target_pairs={{0,8},{4,12},{8,0},{12,4},{16,24},{20,28},{24,16},{28,20},{1,9},{5... | collective-permute-start | bytes 98312 | tf_op jit(solution)/shard_map/ppermute | solution.py:137
  71.1 11.3 %collective-permute-start.32 = (f32[64,128]{1,0:T(8,128)S(1)}, f32[64,128]{1,0:T(8,128)S(1)}, u32[]{:S(2)}, u32[]{:S(2)}) collective-permute-start(f32[64,128]{1,0:T(8,128)S(1)} %solve_up.9.refs_0_.right_ref), channel_id=1, source_target_pairs={{0,12},{4,8},{8,4},{12,0},{16,28},{20,24},{24,20},{28,16},{1,13},{... | collective-permute-start | bytes 98312 | tf_op jit(solution)/shard_map/ppermute | solution.py:137
  73.4 9.0 %collective-permute-start.33 = (f32[64,128]{1,0:T(8,128)S(1)}, f32[64,128]{1,0:T(8,128)S(1)}, u32[]{:S(2)}, u32[]{:S(2)}) collective-permute-start(f32[64,128]{1,0:T(8,128)S(1)} %solve_up.9.refs_0_.right_ref), channel_id=1, source_target_pairs={{0,16},{4,20},{8,24},{12,28},{16,0},{20,4},{24,8},{28,12},{1,17},{... | collective-permute-start | bytes 98312 | tf_op jit(solution)/shard_map/ppermute | solution.py:137
  75.3 7.1 %collective-permute-start.34 = (f32[64,128]{1,0:T(8,128)S(1)}, f32[64,128]{1,0:T(8,128)S(1)}, u32[]{:S(2)}, u32[]{:S(2)}) collective-permute-start(f32[64,128]{1,0:T(8,128)S(1)} %solve_up.9.refs_0_.right_ref), channel_id=1, source_target_pairs={{0,20},{4,16},{8,28},{12,24},{16,4},{20,0},{24,12},{28,8},{1,21},{... | collective-permute-start | bytes 98312 | tf_op jit(solution)/shard_map/ppermute | solution.py:137
  80.6 6.6 %collective-permute-start.36 = (f32[64,128]{1,0:T(8,128)S(1)}, f32[64,128]{1,0:T(8,128)S(1)}, u32[]{:S(2)}, u32[]{:S(2)}) collective-permute-start(f32[64,128]{1,0:T(8,128)S(1)} %solve_up.9.refs_0_.right_ref), channel_id=1, source_target_pairs={{0,28},{4,24},{8,20},{12,16},{16,12},{20,8},{24,4},{28,0},{1,29},{... | collective-permute-start | bytes 98312 | tf_op jit(solution)/shard_map/ppermute | solution.py:137
  92.6 6.3 %collective-permute-start.40 = (f32[64,128]{1,0:T(8,128)S(1)}, f32[64,128]{1,0:T(8,128)S(1)}, u32[]{:S(2)}, u32[]{:S(2)}) collective-permute-start(f32[64,128]{1,0:T(8,128)S(1)} %solve_up.10.refs_0_.right_ref), channel_id=1, source_target_pairs={{0,4},{4,0},{8,12},{12,8},{16,20},{20,16},{24,28},{28,24},{1,5},{5... | collective-permute-start | bytes 98312 | tf_op jit(solution)/shard_map/ppermute | solution.py:137
  93.0 6.4 %collective-permute-start.41 = (f32[64,128]{1,0:T(8,128)S(1)}, f32[64,128]{1,0:T(8,128)S(1)}, u32[]{:S(2)}, u32[]{:S(2)}) collective-permute-start(f32[64,128]{1,0:T(8,128)S(1)} %solve_up.10.refs_0_.right_ref), channel_id=1, source_target_pairs={{0,8},{4,12},{8,0},{12,4},{16,24},{20,28},{24,16},{28,20},{1,9},{5... | collective-permute-start | bytes 98312 | tf_op jit(solution)/shard_map/ppermute | solution.py:137
  93.0 12.3 %collective-permute-start.42 = (f32[64,128]{1,0:T(8,128)S(1)}, f32[64,128]{1,0:T(8,128)S(1)}, u32[]{:S(2)}, u32[]{:S(2)}) collective-permute-start(f32[64,128]{1,0:T(8,128)S(1)} %solve_up.10.refs_0_.right_ref), channel_id=1, source_target_pairs={{0,12},{4,8},{8,4},{12,0},{16,28},{20,24},{24,20},{28,16},{1,13},{... | collective-permute-start | bytes 98312 | tf_op jit(solution)/shard_map/ppermute | solution.py:137
  96.1 9.2 %collective-permute-start.43 = (f32[64,128]{1,0:T(8,128)S(1)}, f32[64,128]{1,0:T(8,128)S(1)}, u32[]{:S(2)}, u32[]{:S(2)}) collective-permute-start(f32[64,128]{1,0:T(8,128)S(1)} %solve_up.10.refs_0_.right_ref), channel_id=1, source_target_pairs={{0,16},{4,20},{8,24},{12,28},{16,0},{20,4},{24,8},{28,12},{1,17},{... | collective-permute-start | bytes 98312 | tf_op jit(solution)/shard_map/ppermute | solution.py:137
  96.1 9.2 %collective-permute-start.44 = (f32[64,128]{1,0:T(8,128)S(1)}, f32[64,128]{1,0:T(8,128)S(1)}, u32[]{:S(2)}, u32[]{:S(2)}) collective-permute-start(f32[64,128]{1,0:T(8,128)S(1)} %solve_up.10.refs_0_.right_ref), channel_id=1, source_target_pairs={{0,20},{4,16},{8,28},{12,24},{16,4},{20,0},{24,12},{28,8},{1,21},{... | collective-permute-start | bytes 98312 | tf_op jit(solution)/shard_map/ppermute | solution.py:137
  98.8 6.5 %collective-permute-start.45 = (f32[64,128]{1,0:T(8,128)S(1)}, f32[64,128]{1,0:T(8,128)S(1)}, u32[]{:S(2)}, u32[]{:S(2)}) collective-permute-start(f32[64,128]{1,0:T(8,128)S(1)} %solve_up.10.refs_0_.right_ref), channel_id=1, source_target_pairs={{0,24},{4,28},{8,16},{12,20},{16,8},{20,12},{24,0},{28,4},{1,25},{... | collective-permute-start | bytes 98312 | tf_op jit(solution)/shard_map/ppermute | solution.py:137
  99.4 6.6 %collective-permute-start.46 = (f32[64,128]{1,0:T(8,128)S(1)}, f32[64,128]{1,0:T(8,128)S(1)}, u32[]{:S(2)}, u32[]{:S(2)}) collective-permute-start(f32[64,128]{1,0:T(8,128)S(1)} %solve_up.10.refs_0_.right_ref), channel_id=1, source_target_pairs={{0,28},{4,24},{8,20},{12,16},{16,12},{20,8},{24,4},{28,0},{1,29},{... | collective-permute-start | bytes 98312 | tf_op jit(solution)/shard_map/ppermute | solution.py:137
  117.3 7.1 %collective-permute-start.53 = (f32[64,128]{1,0:T(8,128)S(1)}, f32[64,128]{1,0:T(8,128)S(1)}, u32[]{:S(2)}, u32[]{:S(2)}) collective-permute-start(f32[64,128]{1,0:T(8,128)S(1)} %get-tuple-element.103), channel_id=1, source_target_pairs={{0,4},{4,0},{8,12},{12,8},{16,20},{20,16},{24,28},{28,24},{1,5},{5... | collective-permute-start | bytes 98312 | tf_op jit(solution)/shard_map/ppermute | solution.py:144
  118.5 9.6 %collective-permute-start.54 = (f32[64,128]{1,0:T(8,128)S(1)}, f32[64,128]{1,0:T(8,128)S(1)}, u32[]{:S(2)}, u32[]{:S(2)}) collective-permute-start(f32[64,128]{1,0:T(8,128)S(1)} %get-tuple-element.104), channel_id=1, source_target_pairs={{0,8},{4,12},{8,0},{12,4},{16,24},{20,28},{24,16},{28,20},{1,9},{5... | collective-permute-start | bytes 98312 | tf_op jit(solution)/shard_map/ppermute | solution.py:144
  118.5 10.0 %collective-permute-start.55 = (f32[64,128]{1,0:T(8,128)S(1)}, f32[64,128]{1,0:T(8,128)S(1)}, u32[]{:S(2)}, u32[]{:S(2)}) collective-permute-start(f32[64,128]{1,0:T(8,128)S(1)} %get-tuple-element.105), channel_id=1, source_target_pairs={{0,12},{4,8},{8,4},{12,0},{16,28},{20,24},{24,20},{28,16},{1,13},{... | collective-permute-start | bytes 98312 | tf_op jit(solution)/shard_map/ppermute | solution.py:144
  120.8 7.7 %collective-permute-start.56 = (f32[64,128]{1,0:T(8,128)S(1)}, f32[64,128]{1,0:T(8,128)S(1)}, u32[]{:S(2)}, u32[]{:S(2)}) collective-permute-start(f32[64,128]{1,0:T(8,128)S(1)} %get-tuple-element.106), channel_id=1, source_target_pairs={{0,16},{4,20},{8,24},{12,28},{16,0},{20,4},{24,8},{28,12},{1,17},{... | collective-permute-start | bytes 98312 | tf_op jit(solution)/shard_map/ppermute | solution.py:144
  124.4 6.0 %collective-permute-start.58 = (f32[64,128]{1,0:T(8,128)S(1)}, f32[64,128]{1,0:T(8,128)S(1)}, u32[]{:S(2)}, u32[]{:S(2)}) collective-permute-start(f32[64,128]{1,0:T(8,128)S(1)} %get-tuple-element.108), channel_id=1, source_target_pairs={{0,24},{4,28},{8,16},{12,20},{16,8},{20,12},{24,0},{28,4},{1,25},{... | collective-permute-start | bytes 98312 | tf_op jit(solution)/shard_map/ppermute | solution.py:144
  128.1 6.6 %collective-permute-start.59 = (f32[64,128]{1,0:T(8,128)S(1)}, f32[64,128]{1,0:T(8,128)S(1)}, u32[]{:S(2)}, u32[]{:S(2)}) collective-permute-start(f32[64,128]{1,0:T(8,128)S(1)} %get-tuple-element.109), channel_id=1, source_target_pairs={{0,28},{4,24},{8,20},{12,16},{16,12},{20,8},{24,4},{28,0},{1,29},{... | collective-permute-start | bytes 98312 | tf_op jit(solution)/shard_map/ppermute | solution.py:144
  140.4 6.3 %collective-permute-start.63 = (f32[64,128]{1,0:T(8,128)S(1)}, f32[64,128]{1,0:T(8,128)S(1)}, u32[]{:S(2)}, u32[]{:S(2)}) collective-permute-start(f32[64,128]{1,0:T(8,128)S(1)} %get-tuple-element.111), channel_id=1, source_target_pairs={{0,4},{4,0},{8,12},{12,8},{16,20},{20,16},{24,28},{28,24},{1,5},{5... | collective-permute-start | bytes 98312 | tf_op jit(solution)/shard_map/ppermute | solution.py:144
  140.9 6.5 %collective-permute-start.64 = (f32[64,128]{1,0:T(8,128)S(1)}, f32[64,128]{1,0:T(8,128)S(1)}, u32[]{:S(2)}, u32[]{:S(2)}) collective-permute-start(f32[64,128]{1,0:T(8,128)S(1)} %get-tuple-element.112), channel_id=1, source_target_pairs={{0,8},{4,12},{8,0},{12,4},{16,24},{20,28},{24,16},{28,20},{1,9},{5... | collective-permute-start | bytes 98312 | tf_op jit(solution)/shard_map/ppermute | solution.py:144
  140.9 10.7 %collective-permute-start.65 = (f32[64,128]{1,0:T(8,128)S(1)}, f32[64,128]{1,0:T(8,128)S(1)}, u32[]{:S(2)}, u32[]{:S(2)}) collective-permute-start(f32[64,128]{1,0:T(8,128)S(1)} %get-tuple-element.113), channel_id=1, source_target_pairs={{0,12},{4,8},{8,4},{12,0},{16,28},{20,24},{24,20},{28,16},{1,13},{... | collective-permute-start | bytes 98312 | tf_op jit(solution)/shard_map/ppermute | solution.py:144
  144.0 7.7 %collective-permute-start.66 = (f32[64,128]{1,0:T(8,128)S(1)}, f32[64,128]{1,0:T(8,128)S(1)}, u32[]{:S(2)}, u32[]{:S(2)}) collective-permute-start(f32[64,128]{1,0:T(8,128)S(1)} %get-tuple-element.114), channel_id=1, source_target_pairs={{0,16},{4,20},{8,24},{12,28},{16,0},{20,4},{24,8},{28,12},{1,17},{... | collective-permute-start | bytes 98312 | tf_op jit(solution)/shard_map/ppermute | solution.py:144
  144.0 7.7 %collective-permute-start.67 = (f32[64,128]{1,0:T(8,128)S(1)}, f32[64,128]{1,0:T(8,128)S(1)}, u32[]{:S(2)}, u32[]{:S(2)}) collective-permute-start(f32[64,128]{1,0:T(8,128)S(1)} %get-tuple-element.115), channel_id=1, source_target_pairs={{0,20},{4,16},{8,28},{12,24},{16,4},{20,0},{24,12},{28,8},{1,21},{... | collective-permute-start | bytes 98312 | tf_op jit(solution)/shard_map/ppermute | solution.py:144
  147.4 6.6 %collective-permute-start.69 = (f32[64,128]{1,0:T(8,128)S(1)}, f32[64,128]{1,0:T(8,128)S(1)}, u32[]{:S(2)}, u32[]{:S(2)}) collective-permute-start(f32[64,128]{1,0:T(8,128)S(1)} %get-tuple-element.117), channel_id=1, source_target_pairs={{0,28},{4,24},{8,20},{12,16},{16,12},{20,8},{24,4},{28,0},{1,29},{... | collective-permute-start | bytes 98312 | tf_op jit(solution)/shard_map/ppermute | solution.py:144
  159.6 7.1 %collective-permute-start.73 = (f32[64,128]{1,0:T(8,128)S(1)}, f32[64,128]{1,0:T(8,128)S(1)}, u32[]{:S(2)}, u32[]{:S(2)}) collective-permute-start(f32[64,128]{1,0:T(8,128)S(1)} %get-tuple-element.119), channel_id=1, source_target_pairs={{0,4},{4,0},{8,12},{12,8},{16,20},{20,16},{24,28},{28,24},{1,5},{5... | collective-permute-start | bytes 98312 | tf_op jit(solution)/shard_map/ppermute | solution.py:144
  160.9 9.6 %collective-permute-start.74 = (f32[64,128]{1,0:T(8,128)S(1)}, f32[64,128]{1,0:T(8,128)S(1)}, u32[]{:S(2)}, u32[]{:S(2)}) collective-permute-start(f32[64,128]{1,0:T(8,128)S(1)} %get-tuple-element.120), channel_id=1, source_target_pairs={{0,8},{4,12},{8,0},{12,4},{16,24},{20,28},{24,16},{28,20},{1,9},{5... | collective-permute-start | bytes 98312 | tf_op jit(solution)/shard_map/ppermute | solution.py:144
  160.9 10.0 %collective-permute-start.75 = (f32[64,128]{1,0:T(8,128)S(1)}, f32[64,128]{1,0:T(8,128)S(1)}, u32[]{:S(2)}, u32[]{:S(2)}) collective-permute-start(f32[64,128]{1,0:T(8,128)S(1)} %get-tuple-element.121), channel_id=1, source_target_pairs={{0,12},{4,8},{8,4},{12,0},{16,28},{20,24},{24,20},{28,16},{1,13},{... | collective-permute-start | bytes 98312 | tf_op jit(solution)/shard_map/ppermute | solution.py:144
  163.2 7.7 %collective-permute-start.76 = (f32[64,128]{1,0:T(8,128)S(1)}, f32[64,128]{1,0:T(8,128)S(1)}, u32[]{:S(2)}, u32[]{:S(2)}) collective-permute-start(f32[64,128]{1,0:T(8,128)S(1)} %get-tuple-element.122), channel_id=1, source_target_pairs={{0,16},{4,20},{8,24},{12,28},{16,0},{20,4},{24,8},{28,12},{1,17},{... | collective-permute-start | bytes 98312 | tf_op jit(solution)/shard_map/ppermute | solution.py:144
  166.7 6.0 %collective-permute-start.78 = (f32[64,128]{1,0:T(8,128)S(1)}, f32[64,128]{1,0:T(8,128)S(1)}, u32[]{:S(2)}, u32[]{:S(2)}) collective-permute-start(f32[64,128]{1,0:T(8,128)S(1)} %get-tuple-element.124), channel_id=1, source_target_pairs={{0,24},{4,28},{8,16},{12,20},{16,8},{20,12},{24,0},{28,4},{1,25},{... | collective-permute-start | bytes 98312 | tf_op jit(solution)/shard_map/ppermute | solution.py:144
  170.5 6.6 %collective-permute-start.79 = (f32[64,128]{1,0:T(8,128)S(1)}, f32[64,128]{1,0:T(8,128)S(1)}, u32[]{:S(2)}, u32[]{:S(2)}) collective-permute-start(f32[64,128]{1,0:T(8,128)S(1)} %get-tuple-element.125), channel_id=1, source_target_pairs={{0,28},{4,24},{8,20},{12,16},{16,12},{20,8},{24,4},{28,0},{1,29},{... | collective-permute-start | bytes 98312 | tf_op jit(solution)/shard_map/ppermute | solution.py:144
  182.8 6.3 %collective-permute-start.83 = (f32[64,128]{1,0:T(8,128)S(1)}, f32[64,128]{1,0:T(8,128)S(1)}, u32[]{:S(2)}, u32[]{:S(2)}) collective-permute-start(f32[64,128]{1,0:T(8,128)S(1)} %get-tuple-element.127), channel_id=1, source_target_pairs={{0,4},{4,0},{8,12},{12,8},{16,20},{20,16},{24,28},{28,24},{1,5},{5... | collective-permute-start | bytes 98312 | tf_op jit(solution)/shard_map/ppermute | solution.py:144
  183.3 6.5 %collective-permute-start.84 = (f32[64,128]{1,0:T(8,128)S(1)}, f32[64,128]{1,0:T(8,128)S(1)}, u32[]{:S(2)}, u32[]{:S(2)}) collective-permute-start(f32[64,128]{1,0:T(8,128)S(1)} %get-tuple-element.128), channel_id=1, source_target_pairs={{0,8},{4,12},{8,0},{12,4},{16,24},{20,28},{24,16},{28,20},{1,9},{5... | collective-permute-start | bytes 98312 | tf_op jit(solution)/shard_map/ppermute | solution.py:144
  183.3 10.7 %collective-permute-start.85 = (f32[64,128]{1,0:T(8,128)S(1)}, f32[64,128]{1,0:T(8,128)S(1)}, u32[]{:S(2)}, u32[]{:S(2)}) collective-permute-start(f32[64,128]{1,0:T(8,128)S(1)} %get-tuple-element.129), channel_id=1, source_target_pairs={{0,12},{4,8},{8,4},{12,0},{16,28},{20,24},{24,20},{28,16},{1,13},{... | collective-permute-start | bytes 98312 | tf_op jit(solution)/shard_map/ppermute | solution.py:144
  186.4 7.7 %collective-permute-start.86 = (f32[64,128]{1,0:T(8,128)S(1)}, f32[64,128]{1,0:T(8,128)S(1)}, u32[]{:S(2)}, u32[]{:S(2)}) collective-permute-start(f32[64,128]{1,0:T(8,128)S(1)} %get-tuple-element.130), channel_id=1, source_target_pairs={{0,16},{4,20},{8,24},{12,28},{16,0},{20,4},{24,8},{28,12},{1,17},{... | collective-permute-start | bytes 98312 | tf_op jit(solution)/shard_map/ppermute | solution.py:144
  186.4 7.7 %collective-permute-start.87 = (f32[64,128]{1,0:T(8,128)S(1)}, f32[64,128]{1,0:T(8,128)S(1)}, u32[]{:S(2)}, u32[]{:S(2)}) collective-permute-start(f32[64,128]{1,0:T(8,128)S(1)} %get-tuple-element.131), channel_id=1, source_target_pairs={{0,20},{4,16},{8,28},{12,24},{16,4},{20,0},{24,12},{28,8},{1,21},{... | collective-permute-start | bytes 98312 | tf_op jit(solution)/shard_map/ppermute | solution.py:144
  189.7 6.6 %collective-permute-start.89 = (f32[64,128]{1,0:T(8,128)S(1)}, f32[64,128]{1,0:T(8,128)S(1)}, u32[]{:S(2)}, u32[]{:S(2)}) collective-permute-start(f32[64,128]{1,0:T(8,128)S(1)} %get-tuple-element.133), channel_id=1, source_target_pairs={{0,28},{4,24},{8,20},{12,16},{16,12},{20,8},{24,4},{28,0},{1,29},{... | collective-permute-start | bytes 98312 | tf_op jit(solution)/shard_map/ppermute | solution.py:144
  202.0 7.1 %collective-permute-start.93 = (f32[64,128]{1,0:T(8,128)S(1)}, f32[64,128]{1,0:T(8,128)S(1)}, u32[]{:S(2)}, u32[]{:S(2)}) collective-permute-start(f32[64,128]{1,0:T(8,128)S(1)} %get-tuple-element.135), channel_id=1, source_target_pairs={{0,4},{4,0},{8,12},{12,8},{16,20},{20,16},{24,28},{28,24},{1,5},{5... | collective-permute-start | bytes 98312 | tf_op jit(solution)/shard_map/ppermute | solution.py:144
  203.3 9.6 %collective-permute-start.94 = (f32[64,128]{1,0:T(8,128)S(1)}, f32[64,128]{1,0:T(8,128)S(1)}, u32[]{:S(2)}, u32[]{:S(2)}) collective-permute-start(f32[64,128]{1,0:T(8,128)S(1)} %get-tuple-element.136), channel_id=1, source_target_pairs={{0,8},{4,12},{8,0},{12,4},{16,24},{20,28},{24,16},{28,20},{1,9},{5... | collective-permute-start | bytes 98312 | tf_op jit(solution)/shard_map/ppermute | solution.py:144
  203.3 10.0 %collective-permute-start.95 = (f32[64,128]{1,0:T(8,128)S(1)}, f32[64,128]{1,0:T(8,128)S(1)}, u32[]{:S(2)}, u32[]{:S(2)}) collective-permute-start(f32[64,128]{1,0:T(8,128)S(1)} %get-tuple-element.137), channel_id=1, source_target_pairs={{0,12},{4,8},{8,4},{12,0},{16,28},{20,24},{24,20},{28,16},{1,13},{... | collective-permute-start | bytes 98312 | tf_op jit(solution)/shard_map/ppermute | solution.py:144
  205.6 7.7 %collective-permute-start.96 = (f32[64,128]{1,0:T(8,128)S(1)}, f32[64,128]{1,0:T(8,128)S(1)}, u32[]{:S(2)}, u32[]{:S(2)}) collective-permute-start(f32[64,128]{1,0:T(8,128)S(1)} %get-tuple-element.138), channel_id=1, source_target_pairs={{0,16},{4,20},{8,24},{12,28},{16,0},{20,4},{24,8},{28,12},{1,17},{... | collective-permute-start | bytes 98312 | tf_op jit(solution)/shard_map/ppermute | solution.py:144
  209.1 6.0 %collective-permute-start.98 = (f32[64,128]{1,0:T(8,128)S(1)}, f32[64,128]{1,0:T(8,128)S(1)}, u32[]{:S(2)}, u32[]{:S(2)}) collective-permute-start(f32[64,128]{1,0:T(8,128)S(1)} %get-tuple-element.140), channel_id=1, source_target_pairs={{0,24},{4,28},{8,16},{12,20},{16,8},{20,12},{24,0},{28,4},{1,25},{... | collective-permute-start | bytes 98312 | tf_op jit(solution)/shard_map/ppermute | solution.py:144
  212.9 6.6 %collective-permute-start.99 = (f32[64,128]{1,0:T(8,128)S(1)}, f32[64,128]{1,0:T(8,128)S(1)}, u32[]{:S(2)}, u32[]{:S(2)}) collective-permute-start(f32[64,128]{1,0:T(8,128)S(1)} %get-tuple-element.141), channel_id=1, source_target_pairs={{0,28},{4,24},{8,20},{12,16},{16,12},{20,8},{24,4},{28,0},{1,29},{... | collective-permute-start | bytes 98312 | tf_op jit(solution)/shard_map/ppermute | solution.py:144
  (45 other events, 211.7 us)

commit v2 on v1

--- a/solution.py
+++ b/solution.py
@@ -34,7 +34,7 @@
     total[...] = jnp.zeros_like(total)
 
     def add(slot, carry):
-        below = source_ref[level, slot] ^ place_ref[0]
+        below = source_ref[level, slot]
         above = target_ref[level, slot] ^ place_ref[1]
         pair = below * n_col + above
         total[pair] += blocks_ref[0, slot]
@@ -73,22 +73,33 @@
 def couple_kernel(transposed, n_in, high_ref, low_ref, *refs):
     ins, outs = refs[:n_in], refs[n_in:]
     block = ins[0].shape[-1]
-    joined = jnp.concatenate([ref[...] for ref in ins], axis=1)
+    if transposed:
+        segments = [ref[...] for ref in ins]
+    else:
+        segments = [ins[0][place] for place in range(ins[0].shape[0])]
+    joined = jnp.concatenate(segments, axis=1)
     result = product(halves(joined), (high_ref[...], low_ref[...]), transposed)
-    for place, ref in enumerate(outs):
-        ref[...] = result[:, place * block : (place + 1) * block]
+    for place in range(result.shape[1] // block):
+        piece = result[:, place * block : (place + 1) * block]
+        if transposed:
+            outs[0][place] = piece
+        else:
+            outs[place][...] = piece
 
 
 def couple(segments, high, low, transposed):
-    n_out = high.shape[0 if transposed else 1] // segments[0].shape[1]
     n_in = len(segments)
-    rows, block = segments[0].shape
+    rows, block = segments[0].shape[-2:]
+    n_out = high.shape[0 if transposed else 1] // block
+    segment = jax.ShapeDtypeStruct((rows, block), jnp.float32)
+    stacked = jax.ShapeDtypeStruct((n_out, rows, block), jnp.float32)
+    out_shape = [stacked] if transposed else [segment] * n_out
     whole = pl.BlockSpec(memory_space=VMEM)
     return pl.pallas_call(
         functools.partial(couple_kernel, transposed, n_in),
-        out_shape=[jax.ShapeDtypeStruct((rows, block), jnp.float32)] * n_out,
+        out_shape=out_shape,
         in_specs=[whole] * (n_in + 2),
-        out_specs=[whole] * n_out,
+        out_specs=[whole] * len(out_shape),
         compiler_params=pltpu.CompilerParams(vmem_limit_bytes=16 * MIB),
         cost_estimate=pl.CostEstimate(
             flops=6 * rows * high.size, bytes_accessed=4 * high.size, transcendentals=0
@@ -97,32 +108,46 @@
     )(high, low, *segments)
 
 
-def solve_kernel(transposed, right_ref, inverse_ref, *refs):
-    parts, out_ref = refs[:-1], refs[-1]
-    value = right_ref[...].reshape(out_ref.shape)
-    if parts:
-        summed = parts[0][...]
-        for part in parts[1:]:
-            summed += part[...]
+def solve_kernel(transposed, n_parts, right_ref, inverse_ref, *refs):
+    parts, outs = refs[:n_parts], refs[n_parts:]
+    value = right_ref[...].reshape(outs[0].shape)
+    pieces = []
+    for part in parts:
+        if len(part.shape) == 3:
+            pieces += [part[place] for place in range(part.shape[0])]
+        else:
+            pieces.append(part[...])
+    if pieces:
+        summed = pieces[0]
+        for piece in pieces[1:]:
+            summed += piece
         value -= summed
     inverse = inverse_ref[...].reshape(inverse_ref.shape[-2:])
-    out_ref[...] = product(halves(value), halves(inverse), transposed)
-
-
-def solve(right, inverse, level, parts, transposed):
+    result = product(halves(value), halves(inverse), transposed)
+    outs[0][...] = result
+    for copies in outs[1:]:
+        for place in range(copies.shape[0]):
+            copies[place] = result
+
+
+def solve(right, inverse, level, parts, transposed, copies=0):
     rows, block = right.shape[-2:]
     at_level = lambda shape: pl.BlockSpec((1,) + shape, lambda i: (level, 0, 0))
     plain = pl.BlockSpec((rows, block), lambda i: (0, 0))
+    spec_of = lambda part: pl.BlockSpec(part.shape, lambda i: (0,) * part.ndim)
+    out_shape = [jax.ShapeDtypeStruct((rows, block), jnp.float32)]
+    if copies:
+        out_shape.append(jax.ShapeDtypeStruct((copies, rows, block), jnp.float32))
     return pl.pallas_call(
-        functools.partial(solve_kernel, transposed),
+        functools.partial(solve_kernel, transposed, len(parts)),
         grid=(1,),
-        out_shape=jax.ShapeDtypeStruct((rows, block), jnp.float32),
+        out_shape=out_shape,
         in_specs=[
             at_level((rows, block)) if right.ndim == 3 else plain,
             at_level((block, block)),
         ]
-        + [plain] * len(parts),
-        out_specs=plain,
+        + [spec_of(part) for part in parts],
+        out_specs=[spec_of(out) for out in out_shape],
         compiler_params=pltpu.CompilerParams(vmem_limit_bytes=8 * MIB),
         cost_estimate=pl.CostEstimate(
             flops=6 * rows * block * block, bytes_accessed=4 * block * block, transcendentals=0
@@ -159,15 +184,20 @@
         gather_blocks(level, target, source, count, place, weights, n_row, n_col)
         for level in range(levels - 1)
     ]
-    forward = [solve(right, inverse, 0, [], False)]
+    exchange = lambda stacked: lax.all_to_all(stacked, "row", 0, 0, tiled=True)
+    first, copies = solve(right, inverse, 0, [], False, n_row)
+    forward = [first]
     for level in range(1, levels):
-        partial = couple(spread(forward[-1], "row"), *coupling[level - 1], False)
-        forward.append(solve(right, inverse, level, deliver(partial, "col"), False))
+        partial = couple([exchange(copies)], *coupling[level - 1], False)
+        more = n_row if level < levels - 1 else 0
+        solved = solve(right, inverse, level, deliver(partial, "col"), False, more)
+        forward.append(solved[0])
+        copies = solved[-1]
     backward = [None] * levels
-    backward[-1] = solve(forward[-1], inverse, levels - 1, [], True)
+    backward[-1] = solve(forward[-1], inverse, levels - 1, [], True)[0]
     for level in range(levels - 2, -1, -1):
-        partial = couple(spread(backward[level + 1], "col"), *coupling[level], True)
-        backward[level] = solve(forward[level], inverse, level, deliver(partial, "row"), True)
+        (partial,) = couple(spread(backward[level + 1], "col"), *coupling[level], True)
+        backward[level] = solve(forward[level], inverse, level, [exchange(partial)], True)[0]
     return (
         jnp.stack(forward).reshape(rhs.shape),
         jnp.stack(backward).reshape(rhs.shape),

time: 221 us -> 213 us (0.964)
  starting transfers between devices: 133 us -> 50 us
  blocking collectives: 0 us -> 38.5 us
  local copies, waits for them, and re-layouts: 8 us -> 44.5 us
  waiting for transfers between devices: 61.4 us -> 54.6 us
  Pallas kernels: 17.2 us -> 22.1 us
    ppermute x50 -> x15, starting transfers between devices: 67 us -> 9.66 us  [spread(): lax.ppermute(segment, axis, [(i, i ^ d) for i in range(size)])]
    ppermute x50 -> x15, starting transfers between devices: 65.7 us -> 9.94 us  [deliver(): lax.ppermute(parts[d], axis, [(i, i ^ d) for i in range(size)])]
    all_to_all x0 -> x3, blocking collectives: none -> 38.5 us  [direct_shards(): exchange = lambda stacked: lax.all_to_all(stacked, 'row', 0, 0, tiled=True)]
    unnamed x29 -> x81, local copies, waits for them, and re-layouts: 7.99 us -> 44.4 us
    all_to_all x0 -> x7, starting transfers between devices: none -> 30.4 us  [direct_shards(): exchange = lambda stacked: lax.all_to_all(stacked, 'row', 0, 0, tiled=True)]
    all_to_all x0 -> x7, waiting for transfers between devices: none -> 28.5 us  [direct_shards(): exchange = lambda stacked: lax.all_to_all(stacked, 'row', 0, 0, tiled=True)]
    ppermute x50 -> x15, waiting for transfers between devices: 36.9 us -> 13 us  [deliver(): lax.ppermute(parts[d], axis, [(i, i ^ d) for i in range(size)])]
    ppermute x50 -> x15, waiting for transfers between devices: 24.5 us -> 13.1 us  [spread(): lax.ppermute(segment, axis, [(i, i ^ d) for i in range(size)])]
  transfers between devices with their start and end apart: 100 -> 37, of which waited for: 40 -> 27; matrix products, arithmetic and copies ran while one was open for 0% -> 0% of each run, Pallas kernels for 3% -> 3%
where the time goes in v2:
time: 213 us; the launch traced here: 211 us
  waiting for transfers between devices  54.6 us (26%)
  starting transfers between devices  50 us (23%)
  local copies, waits for them, and re-layouts  44.5 us (21%)
  blocking collectives  38.5 us (18%)
  Pallas kernels  22.1 us (10%)
    unnamed x81, local copies, waits for them, and re-layouts  44.4 us
    all_to_all x3, blocking collectives, direct_shards(): exchange = lambda stacked: lax.all_to_all(stacked, 'row', 0, 0, tiled=True)  38.5 us
    all_to_all x7, starting transfers between devices, direct_shards(): exchange = lambda stacked: lax.all_to_all(stacked, 'row', 0, 0, tiled=True)  30.4 us
    all_to_all x7, waiting for transfers between devices, direct_shards(): exchange = lambda stacked: lax.all_to_all(stacked, 'row', 0, 0, tiled=True)  28.5 us
    ppermute x15, waiting for transfers between devices, spread(): lax.ppermute(segment, axis, [(i, i ^ d) for i in range(size)])  13.1 us
    ppermute x15, waiting for transfers between devices, deliver(): lax.ppermute(parts[d], axis, [(i, i ^ d) for i in range(size)])  13 us
    pallas_call x10, Pallas kernels, couple(): pl.pallas_call(functools.partial(couple_kernel, transposed, n_in), out_sh...  9.95 us
    ppermute x15, starting transfers between devices, deliver(): lax.ppermute(parts[d], axis, [(i, i ^ d) for i in range(size)])  9.94 us
  transfers between devices with their start and end apart: 37, of which 27 were waited for; matrix products, arithmetic and copies ran while one was open for 0% of the time, Pallas kernels for 3%

profile of v2, /device:TPU:0, one launch (start us, length us, event | category | flops | bytes accessed | tf_op | source)
XLA Modules:
  0.0 210.8 jit_solution(1887461637411211905)
XLA Ops:
  0.7 1.0 copy-done.5
  3.5 7.3 %all-to-all-start = ((f32[8,64,128]{2,1,0:T(8,128)}), f32[8,64,128]{2,1,0:T(8,128)S(1)}, u32[]{:S(2)}, u32[]{:S(2)}) async-start(f32[8,64,128]{2,1,0:T(8,128)} %get-tuple-element.45), calls=%async_computation | async-start | bytes 524288 | tf_op jit(solution)/shard_map/all_to_all | solution.py:187
  11.5 4.0 %copy-done = f32[5,1,1,32,128,128]{5,4,3,2,1,0:T(8,128)S(1)} copy-done((f32[5,1,1,32,128,128]{5,4,3,2,1,0:T(8,128)S(1)}, f32[5,1,1,32,128,128]{5,4,3,2,1,0:T(8,128)}, u32[]{:S(2)}) %copy-start) | copy-done | bytes 10485784
  16.2 1.4 gather_blocks_0.1
  17.5 2.1 %all-to-all-done.refs_0_ = f32[8,64,128]{2,1,0:T(8,128)S(1)} async-done(((f32[8,64,128]{2,1,0:T(8,128)}), f32[8,64,128]{2,1,0:T(8,128)S(1)}, u32[]{:S(2)}, u32[]{:S(2)}) %all-to-all-start) | async-done | bytes 262176 | tf_op jit(solution)/shard_map/all_to_all | solution.py:187
  20.4 1.6 collective-permute-start.1
  22.3 2.1 %collective-permute-done.1.refs_2_ = f32[64,128]{1,0:T(8,128)S(1)} collective-permute-done((f32[64,128]{1,0:T(8,128)S(1)}, f32[64,128]{1,0:T(8,128)S(1)}, u32[]{:S(2)}, u32[]{:S(2)}) %collective-permute-start.1) | collective-permute-done | bytes 32800 | tf_op jit(solution)/shard_map/ppermute | solution.py:169
  26.2 3.8 %all-to-all-start.1 = ((f32[8,64,128]{2,1,0:T(8,128)}), f32[8,64,128]{2,1,0:T(8,128)S(1)}, u32[]{:S(2)}, u32[]{:S(2)}) async-start(f32[8,64,128]{2,1,0:T(8,128)} %get-tuple-element.53), calls=%async_computation.1 | async-start | bytes 524288 | tf_op jit(solution)/shard_map/all_to_all | solution.py:187
  30.0 4.0 %copy-done.1 = f32[5,1,1,32,128,128]{5,4,3,2,1,0:T(8,128)S(1)} copy-done((f32[5,1,1,32,128,128]{5,4,3,2,1,0:T(8,128)S(1)}, f32[5,1,1,32,128,128]{5,4,3,2,1,0:T(8,128)}, u32[]{:S(2)}) %copy-start.1) | copy-done | bytes 10485784
  34.0 1.3 gather_blocks_1.1
  37.2 2.0 all-to-all-done.1.refs_0_
  39.2 1.2 copy-done.10
  40.5 1.2 copy-done.13
  44.3 2.1 %collective-permute-done.4.refs_2_ = f32[64,128]{1,0:T(8,128)S(1)} collective-permute-done((f32[64,128]{1,0:T(8,128)S(1)}, f32[64,128]{1,0:T(8,128)S(1)}, u32[]{:S(2)}, u32[]{:S(2)}) %collective-permute-start.4) | collective-permute-done | bytes 32800 | tf_op jit(solution)/shard_map/ppermute | solution.py:169
  47.7 4.1 %all-to-all-start.2 = ((f32[8,64,128]{2,1,0:T(8,128)}), f32[8,64,128]{2,1,0:T(8,128)S(1)}, u32[]{:S(2)}, u32[]{:S(2)}) async-start(f32[8,64,128]{2,1,0:T(8,128)} %get-tuple-element.61), calls=%async_computation.2 | async-start | bytes 524288 | tf_op jit(solution)/shard_map/all_to_all | solution.py:187
  51.8 4.0 %copy-done.2 = f32[5,1,1,32,128,128]{5,4,3,2,1,0:T(8,128)S(1)} copy-done((f32[5,1,1,32,128,128]{5,4,3,2,1,0:T(8,128)S(1)}, f32[5,1,1,32,128,128]{5,4,3,2,1,0:T(8,128)}, u32[]{:S(2)}) %copy-start.2) | copy-done | bytes 10485784
  55.7 1.3 gather_blocks_2.1
  58.0 1.0 copy-done.18
  59.0 2.0 all-to-all-done.2.refs_0_
  61.0 1.2 copy-done.16
  62.2 1.2 copy-done.19
  64.2 1.2 collective-permute-start.7
  66.0 2.1 %collective-permute-done.7.refs_2_ = f32[64,128]{1,0:T(8,128)S(1)} collective-permute-done((f32[64,128]{1,0:T(8,128)S(1)}, f32[64,128]{1,0:T(8,128)S(1)}, u32[]{:S(2)}, u32[]{:S(2)}) %collective-permute-start.7) | collective-permute-done | bytes 32800 | tf_op jit(solution)/shard_map/ppermute | solution.py:169
  69.6 4.1 %all-to-all-start.3 = ((f32[8,64,128]{2,1,0:T(8,128)}), f32[8,64,128]{2,1,0:T(8,128)S(1)}, u32[]{:S(2)}, u32[]{:S(2)}) async-start(f32[8,64,128]{2,1,0:T(8,128)} %get-tuple-element.69), calls=%async_computation.3 | async-start | bytes 524288 | tf_op jit(solution)/shard_map/all_to_all | solution.py:187
  73.7 4.0 %copy-done.3 = f32[5,1,1,32,128,128]{5,4,3,2,1,0:T(8,128)S(1)} copy-done((f32[5,1,1,32,128,128]{5,4,3,2,1,0:T(8,128)S(1)}, f32[5,1,1,32,128,128]{5,4,3,2,1,0:T(8,128)}, u32[]{:S(2)}) %copy-start.3) | copy-done | bytes 10485784
  77.7 1.3 gather_blocks_3.1
  80.9 2.0 all-to-all-done.3.refs_0_
  82.9 1.2 copy-done.22
  84.2 1.2 copy-done.25
  86.0 1.0 collective-permute-start.10
  87.0 1.2 collective-permute-start.9
  88.2 1.8 collective-permute-done.10.refs_2_
  91.5 4.0 %all-to-all-start.4 = ((f32[8,64,128]{2,1,0:T(8,128)}), f32[8,64,128]{2,1,0:T(8,128)S(1)}, u32[]{:S(2)}, u32[]{:S(2)}) async-start(f32[8,64,128]{2,1,0:T(8,128)} %get-tuple-element.77), calls=%async_computation.4 | async-start | bytes 524288 | tf_op jit(solution)/shard_map/all_to_all | solution.py:187
  95.5 4.0 %copy-done.4 = f32[5,1,1,32,128,128]{5,4,3,2,1,0:T(8,128)S(1)} copy-done((f32[5,1,1,32,128,128]{5,4,3,2,1,0:T(8,128)S(1)}, f32[5,1,1,32,128,128]{5,4,3,2,1,0:T(8,128)}, u32[]{:S(2)}) %copy-start.4) | copy-done | bytes 10485784
  99.5 1.3 gather_blocks_4.1
  100.8 1.1 copy-done.27
  101.8 1.0 copy-done.29
  102.9 1.8 all-to-all-done.4.refs_0_
  104.7 1.4 copy-done.28
  106.1 1.4 copy-done.30
  110.1 2.1 %collective-permute-done.13.refs_2_ = f32[64,128]{1,0:T(8,128)S(1)} collective-permute-done((f32[64,128]{1,0:T(8,128)S(1)}, f32[64,128]{1,0:T(8,128)S(1)}, u32[]{:S(2)}, u32[]{:S(2)}) %collective-permute-start.13) | collective-permute-done | bytes 32800 | tf_op jit(solution)/shard_map/ppermute | solution.py:169
  113.1 1.1 collective-permute-start.16
  114.8 2.2 %collective-permute-done.16.refs_2_ = f32[64,128]{1,0:T(8,128)S(1)} collective-permute-done((f32[64,128]{1,0:T(8,128)S(1)}, f32[64,128]{1,0:T(8,128)S(1)}, u32[]{:S(2)}, u32[]{:S(2)}) %collective-permute-start.16) | collective-permute-done | bytes 32800 | tf_op jit(solution)/shard_map/ppermute | solution.py:162
  117.7 1.1 couple_down.5
  118.7 13.3 %all_to_all.50.refs_0_ = f32[8,64,128]{2,1,0:T(8,128)S(1)} all-to-all(f32[8,64,128]{2,1,0:T(8,128)S(1)} %couple_down.5), channel_id=1, replica_groups=mesh['row'=8,'col'=4] {'row'}, dimensions={0} | all-to-all | bytes 524288 | tf_op jit(solution)/shard_map/all_to_all | solution.py:187
  132.2 1.2 collective-permute-start.19
  134.1 2.1 %collective-permute-done.19.refs_2_ = f32[64,128]{1,0:T(8,128)S(1)} collective-permute-done((f32[64,128]{1,0:T(8,128)S(1)}, f32[64,128]{1,0:T(8,128)S(1)}, u32[]{:S(2)}, u32[]{:S(2)}) %collective-permute-start.19) | collective-permute-done | bytes 32800 | tf_op jit(solution)/shard_map/ppermute | solution.py:162
  136.8 1.2 copy-done.23
  138.0 1.2 copy-done.26
  139.2 1.1 couple_down.6
  140.3 12.6 %all_to_all.51.refs_0_ = f32[8,64,128]{2,1,0:T(8,128)S(1)} all-to-all(f32[8,64,128]{2,1,0:T(8,128)S(1)} %couple_down.6), channel_id=1, replica_groups=mesh['row'=8,'col'=4] {'row'}, dimensions={0} | all-to-all | bytes 524288 | tf_op jit(solution)/shard_map/all_to_all | solution.py:187
  153.1 1.0 collective-permute-start.22
  155.0 2.1 %collective-permute-done.22.refs_2_ = f32[64,128]{1,0:T(8,128)S(1)} collective-permute-done((f32[64,128]{1,0:T(8,128)S(1)}, f32[64,128]{1,0:T(8,128)S(1)}, u32[]{:S(2)}, u32[]{:S(2)}) %collective-permute-start.22) | collective-permute-done | bytes 32800 | tf_op jit(solution)/shard_map/ppermute | solution.py:162
  157.5 1.1 couple_down.7
  158.6 12.6 %all_to_all.52.refs_0_ = f32[8,64,128]{2,1,0:T(8,128)S(1)} all-to-all(f32[8,64,128]{2,1,0:T(8,128)S(1)} %couple_down.7), channel_id=1, replica_groups=mesh['row'=8,'col'=4] {'row'}, dimensions={0} | all-to-all | bytes 524288 | tf_op jit(solution)/shard_map/all_to_all | solution.py:187
  171.4 1.2 collective-permute-start.25
  173.3 2.1 %collective-permute-done.25.refs_2_ = f32[64,128]{1,0:T(8,128)S(1)} collective-permute-done((f32[64,128]{1,0:T(8,128)S(1)}, f32[64,128]{1,0:T(8,128)S(1)}, u32[]{:S(2)}, u32[]{:S(2)}) %collective-permute-start.25) | collective-permute-done | bytes 32800 | tf_op jit(solution)/shard_map/ppermute | solution.py:162
  175.9 1.8 couple_down.8
  177.7 3.6 %all-to-all-start.8 = ((f32[8,64,128]{2,1,0:T(8,128)}), f32[8,64,128]{2,1,0:T(8,128)S(1)}, u32[]{:S(2)}, u32[]{:S(2)}) async-start(f32[8,64,128]{2,1,0:T(8,128)} %couple_down.8), calls=%async_computation.8 | async-start | bytes 524288 | tf_op jit(solution)/shard_map/all_to_all | solution.py:187
  181.3 9.3 %all-to-all-done.8.refs_0_ = f32[8,64,128]{2,1,0:T(8,128)S(1)} async-done(((f32[8,64,128]{2,1,0:T(8,128)}), f32[8,64,128]{2,1,0:T(8,128)S(1)}, u32[]{:S(2)}, u32[]{:S(2)}) %all-to-all-start.8) | async-done | bytes 262176 | tf_op jit(solution)/shard_map/all_to_all | solution.py:187
  192.7 2.1 %collective-permute-done.28.refs_2_ = f32[64,128]{1,0:T(8,128)S(1)} collective-permute-done((f32[64,128]{1,0:T(8,128)S(1)}, f32[64,128]{1,0:T(8,128)S(1)}, u32[]{:S(2)}, u32[]{:S(2)}) %collective-permute-start.28) | collective-permute-done | bytes 32800 | tf_op jit(solution)/shard_map/ppermute | solution.py:162
  195.2 1.8 couple_down.9
  197.0 3.6 %all-to-all-start.9 = ((f32[8,64,128]{2,1,0:T(8,128)}), f32[8,64,128]{2,1,0:T(8,128)S(1)}, u32[]{:S(2)}, u32[]{:S(2)}) async-start(f32[8,64,128]{2,1,0:T(8,128)} %couple_down.9), calls=%async_computation.9 | async-start | bytes 524288 | tf_op jit(solution)/shard_map/all_to_all | solution.py:187
  200.6 9.3 %all-to-all-done.9.refs_0_ = f32[8,64,128]{2,1,0:T(8,128)S(1)} async-done(((f32[8,64,128]{2,1,0:T(8,128)}), f32[8,64,128]{2,1,0:T(8,128)S(1)}, u32[]{:S(2)}, u32[]{:S(2)}) %all-to-all-start.9) | async-done | bytes 262176 | tf_op jit(solution)/shard_map/all_to_all | solution.py:187
  (124 shorter events, 32.2 us)
Async XLA Ops:
  0.6 29.4 %copy-start.32 = (s32[5,1,1]{0,2,1:T(1,128)S(1)}, s32[5,1,1]{0,2,1:T(1,128)}, u32[]{:S(2)}) copy-start(s32[5,1,1]{0,2,1:T(1,128)} %param.11) | copy-start | bytes 64
  0.6 1.0 copy-start.5
  2.6 22.7 %copy-start.6 = (f32[6,1,1,1,128,128]{5,4,3,2,1,0:T(8,128)S(1)}, f32[6,1,1,1,128,128]{5,4,3,2,1,0:T(8,128)}, u32[]{:S(2)}) copy-start(f32[6,1,1,1,128,128]{5,4,3,2,1,0:T(8,128)} %param.7) | copy-start | bytes 1179652
  2.6 22.7 %copy-start.8 = (f32[6,1,1,1,64,128]{5,4,3,2,1,0:T(8,128)S(1)}, f32[6,1,1,1,64,128]{5,4,3,2,1,0:T(8,128)}, u32[]{:S(2)}) copy-start(f32[6,1,1,1,64,128]{5,4,3,2,1,0:T(8,128)} %param.6) | copy-start | bytes 589828
  3.5 16.2 %all-to-all-start = ((f32[8,64,128]{2,1,0:T(8,128)}), f32[8,64,128]{2,1,0:T(8,128)S(1)}, u32[]{:S(2)}, u32[]{:S(2)}) async-start(f32[8,64,128]{2,1,0:T(8,128)} %get-tuple-element.45), calls=%async_computation | async-start | bytes 524288 | tf_op jit(solution)/shard_map/all_to_all | solution.py:187
  11.5 4.0 %copy-start = (f32[5,1,1,32,128,128]{5,4,3,2,1,0:T(8,128)S(1)}, f32[5,1,1,32,128,128]{5,4,3,2,1,0:T(8,128)}, u32[]{:S(2)}) copy-start(f32[5,1,1,32,128,128]{5,4,3,2,1,0:T(8,128)} %param.8) | copy-start | bytes 31457284
  20.3 1.9 collective-permute-start
  20.4 4.0 %collective-permute-start.1 = (f32[64,128]{1,0:T(8,128)S(1)}, f32[64,128]{1,0:T(8,128)S(1)}, u32[]{:S(2)}, u32[]{:S(2)}) collective-permute-start(f32[64,128]{1,0:T(8,128)S(1)} %get-tuple-element.48), channel_id=1, source_target_pairs={{0,2},{1,3},{2,0},{3,1},{4,6},{5,7},{6,4},{7,5},{8,10},{9,11},{10,... | collective-permute-start | bytes 98312 | tf_op jit(solution)/shard_map/ppermute | solution.py:169
  22.0 3.3 %collective-permute-start.2 = (f32[64,128]{1,0:T(8,128)S(1)}, f32[64,128]{1,0:T(8,128)S(1)}, u32[]{:S(2)}, u32[]{:S(2)}) collective-permute-start(f32[64,128]{1,0:T(8,128)S(1)} %get-tuple-element.49), channel_id=1, source_target_pairs={{0,3},{1,2},{2,1},{3,0},{4,7},{5,6},{6,5},{7,4},{8,11},{9,10},{10,... | collective-permute-start | bytes 98312 | tf_op jit(solution)/shard_map/ppermute | solution.py:169
  26.2 13.0 %all-to-all-start.1 = ((f32[8,64,128]{2,1,0:T(8,128)}), f32[8,64,128]{2,1,0:T(8,128)S(1)}, u32[]{:S(2)}, u32[]{:S(2)}) async-start(f32[8,64,128]{2,1,0:T(8,128)} %get-tuple-element.53), calls=%async_computation.1 | async-start | bytes 524288 | tf_op jit(solution)/shard_map/all_to_all | solution.py:187
  30.0 4.0 %copy-start.1 = (f32[5,1,1,32,128,128]{5,4,3,2,1,0:T(8,128)S(1)}, f32[5,1,1,32,128,128]{5,4,3,2,1,0:T(8,128)}, u32[]{:S(2)}) copy-start(f32[5,1,1,32,128,128]{5,4,3,2,1,0:T(8,128)} %param.8) | copy-start | bytes 31457284
  39.2 1.2 copy-start.10
  40.5 1.2 copy-start.13
  42.4 1.9 collective-permute-start.3
  42.4 4.0 %collective-permute-start.4 = (f32[64,128]{1,0:T(8,128)S(1)}, f32[64,128]{1,0:T(8,128)S(1)}, u32[]{:S(2)}, u32[]{:S(2)}) collective-permute-start(f32[64,128]{1,0:T(8,128)S(1)} %get-tuple-element.56), channel_id=1, source_target_pairs={{0,2},{1,3},{2,0},{3,1},{4,6},{5,7},{6,4},{7,5},{8,10},{9,11},{10,... | collective-permute-start | bytes 98312 | tf_op jit(solution)/shard_map/ppermute | solution.py:169
  43.4 3.4 %collective-permute-start.5 = (f32[64,128]{1,0:T(8,128)S(1)}, f32[64,128]{1,0:T(8,128)S(1)}, u32[]{:S(2)}, u32[]{:S(2)}) collective-permute-start(f32[64,128]{1,0:T(8,128)S(1)} %get-tuple-element.57), channel_id=1, source_target_pairs={{0,3},{1,2},{2,1},{3,0},{4,7},{5,6},{6,5},{7,4},{8,11},{9,10},{10,... | collective-permute-start | bytes 98312 | tf_op jit(solution)/shard_map/ppermute | solution.py:169
  47.7 13.3 %all-to-all-start.2 = ((f32[8,64,128]{2,1,0:T(8,128)}), f32[8,64,128]{2,1,0:T(8,128)S(1)}, u32[]{:S(2)}, u32[]{:S(2)}) async-start(f32[8,64,128]{2,1,0:T(8,128)} %get-tuple-element.61), calls=%async_computation.2 | async-start | bytes 524288 | tf_op jit(solution)/shard_map/all_to_all | solution.py:187
  51.8 4.0 %copy-start.2 = (f32[5,1,1,32,128,128]{5,4,3,2,1,0:T(8,128)S(1)}, f32[5,1,1,32,128,128]{5,4,3,2,1,0:T(8,128)}, u32[]{:S(2)}) copy-start(f32[5,1,1,32,128,128]{5,4,3,2,1,0:T(8,128)} %param.8) | copy-start | bytes 31457284
  58.0 1.0 copy-start.18
  61.0 1.2 copy-start.16
  62.2 1.2 copy-start.19
  64.1 1.9 collective-permute-start.6
  64.2 4.0 %collective-permute-start.7 = (f32[64,128]{1,0:T(8,128)S(1)}, f32[64,128]{1,0:T(8,128)S(1)}, u32[]{:S(2)}, u32[]{:S(2)}) collective-permute-start(f32[64,128]{1,0:T(8,128)S(1)} %get-tuple-element.64), channel_id=1, source_target_pairs={{0,2},{1,3},{2,0},{3,1},{4,6},{5,7},{6,4},{7,5},{8,10},{9,11},{10,... | collective-permute-start | bytes 98312 | tf_op jit(solution)/shard_map/ppermute | solution.py:169
  65.3 3.3 %collective-permute-start.8 = (f32[64,128]{1,0:T(8,128)S(1)}, f32[64,128]{1,0:T(8,128)S(1)}, u32[]{:S(2)}, u32[]{:S(2)}) collective-permute-start(f32[64,128]{1,0:T(8,128)S(1)} %get-tuple-element.65), channel_id=1, source_target_pairs={{0,3},{1,2},{2,1},{3,0},{4,7},{5,6},{6,5},{7,4},{8,11},{9,10},{10,... | collective-permute-start | bytes 98312 | tf_op jit(solution)/shard_map/ppermute | solution.py:169
  69.6 13.4 %all-to-all-start.3 = ((f32[8,64,128]{2,1,0:T(8,128)}), f32[8,64,128]{2,1,0:T(8,128)S(1)}, u32[]{:S(2)}, u32[]{:S(2)}) async-start(f32[8,64,128]{2,1,0:T(8,128)} %get-tuple-element.69), calls=%async_computation.3 | async-start | bytes 524288 | tf_op jit(solution)/shard_map/all_to_all | solution.py:187
  73.7 4.0 %copy-start.3 = (f32[5,1,1,32,128,128]{5,4,3,2,1,0:T(8,128)S(1)}, f32[5,1,1,32,128,128]{5,4,3,2,1,0:T(8,128)}, u32[]{:S(2)}) copy-start(f32[5,1,1,32,128,128]{5,4,3,2,1,0:T(8,128)} %param.8) | copy-start | bytes 31457284
  82.9 1.2 copy-start.22
  84.2 1.2 copy-start.25
  86.0 4.0 %collective-permute-start.10 = (f32[64,128]{1,0:T(8,128)S(1)}, f32[64,128]{1,0:T(8,128)S(1)}, u32[]{:S(2)}, u32[]{:S(2)}) collective-permute-start(f32[64,128]{1,0:T(8,128)S(1)} %get-tuple-element.72), channel_id=1, source_target_pairs={{0,2},{1,3},{2,0},{3,1},{4,6},{5,7},{6,4},{7,5},{8,10},{9,11},{10,... | collective-permute-start | bytes 98312 | tf_op jit(solution)/shard_map/ppermute | solution.py:169
  87.0 3.6 %collective-permute-start.11 = (f32[64,128]{1,0:T(8,128)S(1)}, f32[64,128]{1,0:T(8,128)S(1)}, u32[]{:S(2)}, u32[]{:S(2)}) collective-permute-start(f32[64,128]{1,0:T(8,128)S(1)} %get-tuple-element.73), channel_id=1, source_target_pairs={{0,3},{1,2},{2,1},{3,0},{4,7},{5,6},{6,5},{7,4},{8,11},{9,10},{10,... | collective-permute-start | bytes 98312 | tf_op jit(solution)/shard_map/ppermute | solution.py:169
  87.0 3.6 %collective-permute-start.9 = (f32[64,128]{1,0:T(8,128)S(1)}, f32[64,128]{1,0:T(8,128)S(1)}, u32[]{:S(2)}, u32[]{:S(2)}) collective-permute-start(f32[64,128]{1,0:T(8,128)S(1)} %get-tuple-element.71), channel_id=1, source_target_pairs={{0,1},{1,0},{2,3},{3,2},{4,5},{5,4},{6,7},{7,6},{8,9},{9,8},{10,11... | collective-permute-start | bytes 98312 | tf_op jit(solution)/shard_map/ppermute | solution.py:169
  91.5 13.2 %all-to-all-start.4 = ((f32[8,64,128]{2,1,0:T(8,128)}), f32[8,64,128]{2,1,0:T(8,128)S(1)}, u32[]{:S(2)}, u32[]{:S(2)}) async-start(f32[8,64,128]{2,1,0:T(8,128)} %get-tuple-element.77), calls=%async_computation.4 | async-start | bytes 524288 | tf_op jit(solution)/shard_map/all_to_all | solution.py:187
  95.5 4.0 %copy-start.4 = (f32[5,1,1,32,128,128]{5,4,3,2,1,0:T(8,128)S(1)}, f32[5,1,1,32,128,128]{5,4,3,2,1,0:T(8,128)}, u32[]{:S(2)}) copy-start(f32[5,1,1,32,128,128]{5,4,3,2,1,0:T(8,128)} %param.8) | copy-start | bytes 31457284
  100.8 1.1 copy-start.27
  101.8 1.0 copy-start.29
  104.7 52.8 %copy-start.17 = (bf16[1024,512]{1,0:T(8,128)(2,1)S(1)}, bf16[1024,512]{1,0:T(8,128)(2,1)}, u32[]{:S(2)}) copy-start(bf16[1024,512]{1,0:T(8,128)(2,1)} %copy-done.15) | copy-start | bytes 3145732
  104.7 52.8 %copy-start.20 = (bf16[1024,512]{1,0:T(8,128)(2,1)S(1)}, bf16[1024,512]{1,0:T(8,128)(2,1)}, u32[]{:S(2)}) copy-start(bf16[1024,512]{1,0:T(8,128)(2,1)} %copy-done.18) | copy-start | bytes 3145732
  104.7 71.3 %copy-start.11 = (bf16[1024,512]{1,0:T(8,128)(2,1)S(1)}, bf16[1024,512]{1,0:T(8,128)(2,1)}, u32[]{:S(2)}) copy-start(bf16[1024,512]{1,0:T(8,128)(2,1)} %copy-done.9) | copy-start | bytes 3145732
  104.7 71.3 %copy-start.14 = (bf16[1024,512]{1,0:T(8,128)(2,1)S(1)}, bf16[1024,512]{1,0:T(8,128)(2,1)}, u32[]{:S(2)}) copy-start(bf16[1024,512]{1,0:T(8,128)(2,1)} %copy-done.12) | copy-start | bytes 3145732
  104.7 1.4 copy-start.28
  106.1 1.4 copy-start.30
  108.1 1.9 collective-permute-start.12
  108.2 4.0 %collective-permute-start.13 = (f32[64,128]{1,0:T(8,128)S(1)}, f32[64,128]{1,0:T(8,128)S(1)}, u32[]{:S(2)}, u32[]{:S(2)}) collective-permute-start(f32[64,128]{1,0:T(8,128)S(1)} %get-tuple-element.80), channel_id=1, source_target_pairs={{0,2},{1,3},{2,0},{3,1},{4,6},{5,7},{6,4},{7,5},{8,10},{9,11},{10,... | collective-permute-start | bytes 98312 | tf_op jit(solution)/shard_map/ppermute | solution.py:169
  109.2 3.4 %collective-permute-start.14 = (f32[64,128]{1,0:T(8,128)S(1)}, f32[64,128]{1,0:T(8,128)S(1)}, u32[]{:S(2)}, u32[]{:S(2)}) collective-permute-start(f32[64,128]{1,0:T(8,128)S(1)} %get-tuple-element.81), channel_id=1, source_target_pairs={{0,3},{1,2},{2,1},{3,0},{4,7},{5,6},{6,5},{7,4},{8,11},{9,10},{10,... | collective-permute-start | bytes 98312 | tf_op jit(solution)/shard_map/ppermute | solution.py:169
  112.9 1.9 collective-permute-start.15
  113.1 3.9 %collective-permute-start.16 = (f32[64,128]{1,0:T(8,128)S(1)}, f32[64,128]{1,0:T(8,128)S(1)}, u32[]{:S(2)}, u32[]{:S(2)}) collective-permute-start(f32[64,128]{1,0:T(8,128)S(1)} %solve_down.6.refs_0_), channel_id=1, source_target_pairs={{0,2},{1,3},{2,0},{3,1},{4,6},{5,7},{6,4},{7,5},{8,10},{9,11},{10,... | collective-permute-start | bytes 98312 | tf_op jit(solution)/shard_map/ppermute | solution.py:162
  114.2 3.4 %collective-permute-start.17 = (f32[64,128]{1,0:T(8,128)S(1)}, f32[64,128]{1,0:T(8,128)S(1)}, u32[]{:S(2)}, u32[]{:S(2)}) collective-permute-start(f32[64,128]{1,0:T(8,128)S(1)} %solve_down.6.refs_0_), channel_id=1, source_target_pairs={{0,3},{1,2},{2,1},{3,0},{4,7},{5,6},{6,5},{7,4},{8,11},{9,10},{10,... | collective-permute-start | bytes 98312 | tf_op jit(solution)/shard_map/ppermute | solution.py:162
  132.2 1.9 collective-permute-start.18
  132.2 4.0 %collective-permute-start.19 = (f32[64,128]{1,0:T(8,128)S(1)}, f32[64,128]{1,0:T(8,128)S(1)}, u32[]{:S(2)}, u32[]{:S(2)}) collective-permute-start(f32[64,128]{1,0:T(8,128)S(1)} %solve_down.7.refs_0_), channel_id=1, source_target_pairs={{0,2},{1,3},{2,0},{3,1},{4,6},{5,7},{6,4},{7,5},{8,10},{9,11},{10,... | collective-permute-start | bytes 98312 | tf_op jit(solution)/shard_map/ppermute | solution.py:162
  133.4 3.3 %collective-permute-start.20 = (f32[64,128]{1,0:T(8,128)S(1)}, f32[64,128]{1,0:T(8,128)S(1)}, u32[]{:S(2)}, u32[]{:S(2)}) collective-permute-start(f32[64,128]{1,0:T(8,128)S(1)} %solve_down.7.refs_0_), channel_id=1, source_target_pairs={{0,3},{1,2},{2,1},{3,0},{4,7},{5,6},{6,5},{7,4},{8,11},{9,10},{10,... | collective-permute-start | bytes 98312 | tf_op jit(solution)/shard_map/ppermute | solution.py:162
  136.8 1.2 copy-start.23
  138.0 1.2 copy-start.26
  153.1 1.9 collective-permute-start.21
  153.1 4.0 %collective-permute-start.22 = (f32[64,128]{1,0:T(8,128)S(1)}, f32[64,128]{1,0:T(8,128)S(1)}, u32[]{:S(2)}, u32[]{:S(2)}) collective-permute-start(f32[64,128]{1,0:T(8,128)S(1)} %solve_down.8.refs_0_), channel_id=1, source_target_pairs={{0,2},{1,3},{2,0},{3,1},{4,6},{5,7},{6,4},{7,5},{8,10},{9,11},{10,... | collective-permute-start | bytes 98312 | tf_op jit(solution)/shard_map/ppermute | solution.py:162
  154.1 3.3 %collective-permute-start.23 = (f32[64,128]{1,0:T(8,128)S(1)}, f32[64,128]{1,0:T(8,128)S(1)}, u32[]{:S(2)}, u32[]{:S(2)}) collective-permute-start(f32[64,128]{1,0:T(8,128)S(1)} %solve_down.8.refs_0_), channel_id=1, source_target_pairs={{0,3},{1,2},{2,1},{3,0},{4,7},{5,6},{6,5},{7,4},{8,11},{9,10},{10,... | collective-permute-start | bytes 98312 | tf_op jit(solution)/shard_map/ppermute | solution.py:162
  171.4 1.9 collective-permute-start.24
  171.4 4.0 %collective-permute-start.25 = (f32[64,128]{1,0:T(8,128)S(1)}, f32[64,128]{1,0:T(8,128)S(1)}, u32[]{:S(2)}, u32[]{:S(2)}) collective-permute-start(f32[64,128]{1,0:T(8,128)S(1)} %solve_down.9.refs_0_), channel_id=1, source_target_pairs={{0,2},{1,3},{2,0},{3,1},{4,6},{5,7},{6,4},{7,5},{8,10},{9,11},{10,... | collective-permute-start | bytes 98312 | tf_op jit(solution)/shard_map/ppermute | solution.py:162
  172.6 3.3 %collective-permute-start.26 = (f32[64,128]{1,0:T(8,128)S(1)}, f32[64,128]{1,0:T(8,128)S(1)}, u32[]{:S(2)}, u32[]{:S(2)}) collective-permute-start(f32[64,128]{1,0:T(8,128)S(1)} %solve_down.9.refs_0_), channel_id=1, source_target_pairs={{0,3},{1,2},{2,1},{3,0},{4,7},{5,6},{6,5},{7,4},{8,11},{9,10},{10,... | collective-permute-start | bytes 98312 | tf_op jit(solution)/shard_map/ppermute | solution.py:162
  177.7 12.9 %all-to-all-start.8 = ((f32[8,64,128]{2,1,0:T(8,128)}), f32[8,64,128]{2,1,0:T(8,128)S(1)}, u32[]{:S(2)}, u32[]{:S(2)}) async-start(f32[8,64,128]{2,1,0:T(8,128)} %couple_down.8), calls=%async_computation.8 | async-start | bytes 524288 | tf_op jit(solution)/shard_map/all_to_all | solution.py:187
  190.8 1.9 collective-permute-start.27
  190.9 4.0 %collective-permute-start.28 = (f32[64,128]{1,0:T(8,128)S(1)}, f32[64,128]{1,0:T(8,128)S(1)}, u32[]{:S(2)}, u32[]{:S(2)}) collective-permute-start(f32[64,128]{1,0:T(8,128)S(1)} %solve_down.10.refs_0_), channel_id=1, source_target_pairs={{0,2},{1,3},{2,0},{3,1},{4,6},{5,7},{6,4},{7,5},{8,10},{9,11},{10,... | collective-permute-start | bytes 98312 | tf_op jit(solution)/shard_map/ppermute | solution.py:162
  191.8 3.3 %collective-permute-start.29 = (f32[64,128]{1,0:T(8,128)S(1)}, f32[64,128]{1,0:T(8,128)S(1)}, u32[]{:S(2)}, u32[]{:S(2)}) collective-permute-start(f32[64,128]{1,0:T(8,128)S(1)} %solve_down.10.refs_0_), channel_id=1, source_target_pairs={{0,3},{1,2},{2,1},{3,0},{4,7},{5,6},{6,5},{7,4},{8,11},{9,10},{10,... | collective-permute-start | bytes 98312 | tf_op jit(solution)/shard_map/ppermute | solution.py:162
  197.0 12.9 %all-to-all-start.9 = ((f32[8,64,128]{2,1,0:T(8,128)}), f32[8,64,128]{2,1,0:T(8,128)S(1)}, u32[]{:S(2)}, u32[]{:S(2)}) async-start(f32[8,64,128]{2,1,0:T(8,128)} %couple_down.9), calls=%async_computation.9 | async-start | bytes 524288 | tf_op jit(solution)/shard_map/all_to_all | solution.py:187
  200.6 9.6 %copy-start.34 = (f32[6,64,128]{2,1,0:T(8,128)}, f32[6,64,128]{2,1,0:T(8,128)S(1)}, u32[]{:S(2)}) copy-start(f32[6,64,128]{2,1,0:T(8,128)S(1)} %bitcast_dynamic-update-slice_fusion.6) | copy-start | bytes 589828
  (8 other events, 7.1 us)

commit v3 on v1

--- a/solution.py
+++ b/solution.py
@@ -70,79 +70,187 @@
     )(target, source, count, place, blocks)
 
 
-def couple_kernel(transposed, n_in, high_ref, low_ref, *refs):
-    ins, outs = refs[:n_in], refs[n_in:]
-    block = ins[0].shape[-1]
-    joined = jnp.concatenate([ref[...] for ref in ins], axis=1)
-    result = product(halves(joined), (high_ref[...], low_ref[...]), transposed)
-    for place, ref in enumerate(outs):
-        ref[...] = result[:, place * block : (place + 1) * block]
-
-
-def couple(segments, high, low, transposed):
-    n_out = high.shape[0 if transposed else 1] // segments[0].shape[1]
-    n_in = len(segments)
-    rows, block = segments[0].shape
+def read(term, refs):
+    number, place = term
+    return refs[number][...] if place is None else refs[number][place]
+
+
+def total_of(terms, refs):
+    value = read(terms[0], refs)
+    for term in terms[1:]:
+        value += read(term, refs)
+    return value
+
+
+def write(ref, values):
+    if len(ref.shape) == 2:
+        ref[...] = values[0]
+    else:
+        for place, value in enumerate(values):
+            ref[place] = value
+
+
+class Operands:
+    def __init__(self):
+        self.arrays = []
+
+    def term(self, piece):
+        array, place = piece
+        for number, known in enumerate(self.arrays):
+            if known is array:
+                return number, place
+        self.arrays.append(array)
+        return len(self.arrays) - 1, place
+
+
+def message_shape(group, rows, block):
+    shape = (rows, block) if len(group) == 1 else (len(group), rows, block)
+    return jax.ShapeDtypeStruct(shape, jnp.float32)
+
+
+def combine_kernel(sums, *refs):
+    write(refs[-1], [total_of(terms, refs[:-1]) for terms in sums])
+
+
+def combine(sums):
+    if len(sums) == 1 and len(sums[0]) == 1 and sums[0][0][1] is None:
+        return sums[0][0][0]
+    operands = Operands()
+    terms = [[operands.term(piece) for piece in pieces] for pieces in sums]
+    rows, block = operands.arrays[0].shape[-2:]
     whole = pl.BlockSpec(memory_space=VMEM)
     return pl.pallas_call(
-        functools.partial(couple_kernel, transposed, n_in),
-        out_shape=[jax.ShapeDtypeStruct((rows, block), jnp.float32)] * n_out,
-        in_specs=[whole] * (n_in + 2),
-        out_specs=[whole] * n_out,
+        functools.partial(combine_kernel, terms),
+        out_shape=message_shape(sums, rows, block),
+        in_specs=[whole] * len(operands.arrays),
+        out_specs=whole,
+        compiler_params=pltpu.CompilerParams(vmem_limit_bytes=4 * MIB),
+        cost_estimate=pl.CostEstimate(
+            flops=rows * block * len(sums), bytes_accessed=rows * block, transcendentals=0
+        ),
+        name="combine",
+    )(*operands.arrays)
+
+
+def couple_kernel(transposed, terms, groups, high_ref, low_ref, *refs):
+    n_out = len(groups)
+    ins, outs = refs[:-n_out], refs[-n_out:]
+    block = ins[0].shape[-1]
+    joined = jnp.concatenate([read(term, ins) for term in terms], axis=1)
+    result = product(halves(joined), (high_ref[...], low_ref[...]), transposed)
+    for group, ref in zip(groups, outs):
+        write(ref, [result[:, place * block : (place + 1) * block] for place in group])
+
+
+def couple(pieces, high, low, groups, transposed):
+    operands = Operands()
+    terms = [operands.term(pieces[partner]) for partner in range(len(pieces))]
+    rows, block = operands.arrays[0].shape[-2:]
+    whole = pl.BlockSpec(memory_space=VMEM)
+    messages = pl.pallas_call(
+        functools.partial(couple_kernel, transposed, terms, groups),
+        out_shape=[message_shape(group, rows, block) for group in groups],
+        in_specs=[whole] * (2 + len(operands.arrays)),
+        out_specs=[whole] * len(groups),
         compiler_params=pltpu.CompilerParams(vmem_limit_bytes=16 * MIB),
         cost_estimate=pl.CostEstimate(
             flops=6 * rows * high.size, bytes_accessed=4 * high.size, transcendentals=0
         ),
         name="couple_up" if not transposed else "couple_down",
-    )(high, low, *segments)
-
-
-def solve_kernel(transposed, right_ref, inverse_ref, *refs):
-    parts, out_ref = refs[:-1], refs[-1]
+    )(high, low, *operands.arrays)
+    return dict(zip(groups, messages))
+
+
+def solve_kernel(transposed, terms, right_ref, inverse_ref, *refs):
+    ins, out_ref = refs[:-1], refs[-1]
     value = right_ref[...].reshape(out_ref.shape)
-    if parts:
-        summed = parts[0][...]
-        for part in parts[1:]:
-            summed += part[...]
-        value -= summed
+    if terms:
+        value -= total_of(terms, ins)
     inverse = inverse_ref[...].reshape(inverse_ref.shape[-2:])
     out_ref[...] = product(halves(value), halves(inverse), transposed)
 
 
-def solve(right, inverse, level, parts, transposed):
+def solve(right, inverse, level, pieces, transposed):
     rows, block = right.shape[-2:]
+    operands = Operands()
+    terms = [operands.term(piece) for piece in pieces]
     at_level = lambda shape: pl.BlockSpec((1,) + shape, lambda i: (level, 0, 0))
-    plain = pl.BlockSpec((rows, block), lambda i: (0, 0))
+    spec_of = lambda part: pl.BlockSpec(part.shape, lambda i: (0,) * part.ndim)
+    out_shape = jax.ShapeDtypeStruct((rows, block), jnp.float32)
     return pl.pallas_call(
-        functools.partial(solve_kernel, transposed),
+        functools.partial(solve_kernel, transposed, terms),
         grid=(1,),
-        out_shape=jax.ShapeDtypeStruct((rows, block), jnp.float32),
+        out_shape=out_shape,
         in_specs=[
-            at_level((rows, block)) if right.ndim == 3 else plain,
+            at_level((rows, block)) if right.ndim == 3 else spec_of(right),
             at_level((block, block)),
         ]
-        + [plain] * len(parts),
-        out_specs=plain,
+        + [spec_of(part) for part in operands.arrays],
+        out_specs=spec_of(out_shape),
         compiler_params=pltpu.CompilerParams(vmem_limit_bytes=8 * MIB),
         cost_estimate=pl.CostEstimate(
             flops=6 * rows * block * block, bytes_accessed=4 * block * block, transcendentals=0
         ),
         name="solve_up" if not transposed else "solve_down",
-    )(right, inverse, *parts)
+    )(right, inverse, *operands.arrays)
+
+
+def depth_of(partner):
+    return bin(partner).count("1")
+
+
+def bits_of(size):
+    return [1 << place for place in range(size.bit_length() - 1)]
+
+
+def messages_of(held, bit):
+    depths = sorted({depth_of(partner) for partner in held})
+    return [
+        tuple(partner | bit for partner in sorted(held) if depth_of(partner) == depth)
+        for depth in depths
+    ]
+
+
+def exchange(message, axis, bit):
+    size = lax.axis_size(axis)
+    return lax.ppermute(message, axis, [(i, i ^ bit) for i in range(size)])
+
+
+def pieces_of(message, count):
+    return [(message, place if count > 1 else None) for place in range(count)]
 
 
 def spread(segment, axis):
+    held = {0: (segment, None)}
+    for bit in reversed(bits_of(lax.axis_size(axis))):
+        gained = {}
+        for group in messages_of(held, bit):
+            message = exchange(combine([[held[d ^ bit]] for d in group]), axis, bit)
+            gained.update(zip(group, pieces_of(message, len(group))))
+        held.update(gained)
+    return held
+
+
+def delivery_groups(size):
+    bit = 1
+    rest = [d for d in range(size) if not d & bit]
+    return tuple(reversed(messages_of(rest, bit))) + tuple((d,) for d in rest)
+
+
+def deliver(messages, axis):
     size = lax.axis_size(axis)
-    return [segment] + [
-        lax.ppermute(segment, axis, [(i, i ^ d) for i in range(size)]) for d in range(1, size)
-    ]
-
-
-def deliver(parts, axis):
-    size = lax.axis_size(axis)
-    return [parts[0]] + [
-        lax.ppermute(parts[d], axis, [(i, i ^ d) for i in range(size)]) for d in range(1, size)
-    ]
+    held = {}
+    for group, message in messages.items():
+        held.update({d: [piece] for d, piece in zip(group, pieces_of(message, len(group)))})
+    for bit in bits_of(size):
+        kept = [d for d in held if not d & bit]
+        for group in reversed(messages_of(kept, bit)):
+            message = messages.get(group) if bit == 1 else combine([held[d] for d in group])
+            message = exchange(message, axis, bit)
+            for d, piece in zip(group, pieces_of(message, len(group))):
+                held[d ^ bit].append(piece)
+        held = {d: held[d] for d in kept}
+    return held[0]
 
 
 def direct_shards(rhs, diag_inv, blocks, blk_target, blk_source, blk_count):
@@ -159,14 +267,15 @@
         gather_blocks(level, target, source, count, place, weights, n_row, n_col)
         for level in range(levels - 1)
     ]
+    over_row, over_col = delivery_groups(n_row), delivery_groups(n_col)
     forward = [solve(right, inverse, 0, [], False)]
     for level in range(1, levels):
-        partial = couple(spread(forward[-1], "row"), *coupling[level - 1], False)
+        partial = couple(spread(forward[-1], "row"), *coupling[level - 1], over_col, False)
         forward.append(solve(right, inverse, level, deliver(partial, "col"), False))
     backward = [None] * levels
     backward[-1] = solve(forward[-1], inverse, levels - 1, [], True)
     for level in range(levels - 2, -1, -1):
-        partial = couple(spread(backward[level + 1], "col"), *coupling[level], True)
+        partial = couple(spread(backward[level + 1], "col"), *coupling[level], over_row, True)
         backward[level] = solve(forward[level], inverse, level, deliver(partial, "row"), True)
     return (
         jnp.stack(forward).reshape(rhs.shape),

time: 221 us -> 213 us (0.964)
  starting transfers between devices: 133 us -> 97.4 us
  waiting for transfers between devices: 61.4 us -> 88.3 us
    ppermute x100 -> x90, starting transfers between devices: 133 us -> 97.4 us  [exchange(): return lax.ppermute(message, axis, [(i, i ^ bit) for i in range(size)])]
    ppermute x100 -> x90, waiting for transfers between devices: 61.4 us -> 88.3 us  [exchange(): return lax.ppermute(message, axis, [(i, i ^ bit) for i in range(size)])]
    pallas_call x22 -> x47, Pallas kernels: 10.4 us -> 10.5 us  [the longest x10 8.5 us: couple(): pl.pallas_call(functools.partial(couple_kernel, transposed, terms, groups...]
  transfers between devices with their start and end apart: 100 -> 90, of which waited for: 40 -> 56; matrix products, arithmetic and copies ran while one was open for 0% -> 0% of each run, Pallas kernels for 3% -> 3%
where the time goes in v3:
time: 213 us
  starting transfers between devices  97.4 us (46%)
  waiting for transfers between devices  88.3 us (41%)
  Pallas kernels  17.8 us (8%)
  local copies, waits for them, and re-layouts  8 us (4%)
    ppermute x90, starting transfers between devices, exchange(): return lax.ppermute(message, axis, [(i, i ^ bit) for i in range(size)])  97.4 us
    ppermute x90, waiting for transfers between devices, exchange(): return lax.ppermute(message, axis, [(i, i ^ bit) for i in range(size)])  88.3 us
    pallas_call x10, Pallas kernels, couple(): pl.pallas_call(functools.partial(couple_kernel, transposed, terms, groups...  8.5 us
    unnamed x29, local copies, waits for them, and re-layouts  7.99 us
    pallas_call x5, Pallas kernels, gather_blocks(): pl.pallas_call(functools.partial(gather_blocks_kernel, n_col, level), gri...  7.3 us
  transfers between devices with their start and end apart: 90, of which 56 were waited for; matrix products, arithmetic and copies ran while one was open for 0% of the time, Pallas kernels for 3%

profile of v3, /device:TPU:0, one launch (start us, length us, event | category | flops | bytes accessed | tf_op | source)
XLA Modules:
  0.0 212.7 jit_solution(13228630050815202182)
XLA Ops:
  2.7 4.1 %collective-permute-start.2 = (f32[64,128]{1,0:T(8,128)S(1)}, f32[64,128]{1,0:T(8,128)S(1)}, u32[]{:S(2)}, u32[]{:S(2)}) collective-permute-start(f32[64,128]{1,0:T(8,128)S(1)} %solve_up.6.refs_0_.right_ref), channel_id=1, source_target_pairs={{0,16},{4,20},{8,24},{12,28},{16,0},{20,4},{24,8},{28,12},{1,17},{... | collective-permute-start | bytes 98312 | tf_op jit(solution)/shard_map/ppermute | solution.py:216
  6.8 1.6 collective-permute-start.1
  11.3 1.6 collective-permute-start.3
  14.8 4.0 %copy-done = f32[5,1,1,32,128,128]{5,4,3,2,1,0:T(8,128)S(1)} copy-done((f32[5,1,1,32,128,128]{5,4,3,2,1,0:T(8,128)S(1)}, f32[5,1,1,32,128,128]{5,4,3,2,1,0:T(8,128)}, u32[]{:S(2)}) %copy-start) | copy-done | bytes 10485784
  24.2 2.5 %collective-permute-done.8.refs_2_ = f32[64,128]{1,0:T(8,128)S(1)} collective-permute-done((f32[64,128]{1,0:T(8,128)S(1)}, f32[64,128]{1,0:T(8,128)S(1)}, u32[]{:S(2)}, u32[]{:S(2)}) %collective-permute-start.8) | collective-permute-done | bytes 32800 | tf_op jit(solution)/shard_map/ppermute | solution.py:216
  28.2 2.9 %collective-permute-start.11 = (f32[64,128]{1,0:T(8,128)S(1)}, f32[64,128]{1,0:T(8,128)S(1)}, u32[]{:S(2)}, u32[]{:S(2)}) collective-permute-start(f32[64,128]{1,0:T(8,128)S(1)} %solve_up.7.refs_0_.right_ref), channel_id=1, source_target_pairs={{0,16},{4,20},{8,24},{12,28},{16,0},{20,4},{24,8},{28,12},{1,17},{... | collective-permute-start | bytes 98312 | tf_op jit(solution)/shard_map/ppermute | solution.py:216
  31.2 2.2 %collective-permute-done.11.refs_1_.refs_4_ = f32[64,128]{1,0:T(8,128)S(1)} collective-permute-done((f32[64,128]{1,0:T(8,128)S(1)}, f32[64,128]{1,0:T(8,128)S(1)}, u32[]{:S(2)}, u32[]{:S(2)}) %collective-permute-start.11) | collective-permute-done | bytes 32800 | tf_op jit(solution)/shard_map/ppermute | solution.py:216
  37.5 1.8 collective-permute-start.14
  44.8 2.4 %collective-permute-done.17.refs_2_ = f32[64,128]{1,0:T(8,128)S(1)} collective-permute-done((f32[64,128]{1,0:T(8,128)S(1)}, f32[64,128]{1,0:T(8,128)S(1)}, u32[]{:S(2)}, u32[]{:S(2)}) %collective-permute-start.17) | collective-permute-done | bytes 32800 | tf_op jit(solution)/shard_map/ppermute | solution.py:216
  48.7 2.0 collective-permute-start.20
  51.6 1.9 collective-permute-done.20.refs_1_.refs_4_
  54.6 1.7 collective-permute-start.22
  56.5 2.0 collective-permute-done.22.refs_5_
  59.4 1.6 gather_blocks_2.1
  65.8 2.5 %collective-permute-done.26.refs_2_ = f32[64,128]{1,0:T(8,128)S(1)} collective-permute-done((f32[64,128]{1,0:T(8,128)S(1)}, f32[64,128]{1,0:T(8,128)S(1)}, u32[]{:S(2)}, u32[]{:S(2)}) %collective-permute-start.26) | collective-permute-done | bytes 32800 | tf_op jit(solution)/shard_map/ppermute | solution.py:216
  68.5 1.8 collective-permute-start.28
  70.2 2.6 %collective-permute-start.29 = (f32[64,128]{1,0:T(8,128)S(1)}, f32[64,128]{1,0:T(8,128)S(1)}, u32[]{:S(2)}, u32[]{:S(2)}) collective-permute-start(f32[64,128]{1,0:T(8,128)S(1)} %solve_up.9.refs_0_.right_ref), channel_id=1, source_target_pairs={{0,16},{4,20},{8,24},{12,28},{16,0},{20,4},{24,8},{28,12},{1,17},{... | collective-permute-start | bytes 98312 | tf_op jit(solution)/shard_map/ppermute | solution.py:216
  72.8 2.3 %collective-permute-done.29.refs_1_.refs_4_ = f32[64,128]{1,0:T(8,128)S(1)} collective-permute-done((f32[64,128]{1,0:T(8,128)S(1)}, f32[64,128]{1,0:T(8,128)S(1)}, u32[]{:S(2)}, u32[]{:S(2)}) %collective-permute-start.29) | collective-permute-done | bytes 32800 | tf_op jit(solution)/shard_map/ppermute | solution.py:216
  77.4 1.8 collective-permute-done.31.refs_5_
  79.2 1.9 collective-permute-start.32
  86.6 2.4 %collective-permute-done.35.refs_2_ = f32[64,128]{1,0:T(8,128)S(1)} collective-permute-done((f32[64,128]{1,0:T(8,128)S(1)}, f32[64,128]{1,0:T(8,128)S(1)}, u32[]{:S(2)}, u32[]{:S(2)}) %collective-permute-start.35) | collective-permute-done | bytes 32800 | tf_op jit(solution)/shard_map/ppermute | solution.py:216
  90.2 2.0 collective-permute-start.38
  93.1 1.9 collective-permute-done.38.refs_1_.refs_4_
  96.1 1.9 collective-permute-start.40
  98.2 1.8 collective-permute-done.40.refs_5_
  107.3 2.4 %collective-permute-done.44.refs_2_ = f32[64,128]{1,0:T(8,128)S(1)} collective-permute-done((f32[64,128]{1,0:T(8,128)S(1)}, f32[64,128]{1,0:T(8,128)S(1)}, u32[]{:S(2)}, u32[]{:S(2)}) %collective-permute-start.44) | collective-permute-done | bytes 32800 | tf_op jit(solution)/shard_map/ppermute | solution.py:216
  111.7 2.4 %collective-permute-done.46.refs_2_ = f32[64,128]{1,0:T(8,128)S(1)} collective-permute-done((f32[64,128]{1,0:T(8,128)S(1)}, f32[64,128]{1,0:T(8,128)S(1)}, u32[]{:S(2)}, u32[]{:S(2)}) %collective-permute-start.46) | collective-permute-done | bytes 32800 | tf_op jit(solution)/shard_map/ppermute | solution.py:216
  118.5 2.2 %collective-permute-done.51.refs_1_ = f32[64,128]{1,0:T(8,128)S(1)} collective-permute-done((f32[64,128]{1,0:T(8,128)S(1)}, f32[64,128]{1,0:T(8,128)S(1)}, u32[]{:S(2)}, u32[]{:S(2)}) %collective-permute-start.51) | collective-permute-done | bytes 32800 | tf_op jit(solution)/shard_map/ppermute | solution.py:216
  120.7 1.8 collective-permute-start.52
  122.5 2.1 %collective-permute-done.52.refs_2_ = f32[64,128]{1,0:T(8,128)S(1)} collective-permute-done((f32[64,128]{1,0:T(8,128)S(1)}, f32[64,128]{1,0:T(8,128)S(1)}, u32[]{:S(2)}, u32[]{:S(2)}) %collective-permute-start.52) | collective-permute-done | bytes 32800 | tf_op jit(solution)/shard_map/ppermute | solution.py:216
  124.6 2.5 %collective-permute-start.53 = (f32[64,128]{1,0:T(8,128)S(1)}, f32[64,128]{1,0:T(8,128)S(1)}, u32[]{:S(2)}, u32[]{:S(2)}) collective-permute-start(f32[64,128]{1,0:T(8,128)S(1)} %combine.37), channel_id=1, source_target_pairs={{0,16},{4,20},{8,24},{12,28},{16,0},{20,4},{24,8},{28,12},{1,17},{... | collective-permute-start | bytes 98312 | tf_op jit(solution)/shard_map/ppermute | solution.py:216
  127.1 1.9 collective-permute-start.50
  131.2 1.7 collective-permute-start.55
  132.9 2.3 %collective-permute-done.55.refs_2_ = f32[64,128]{1,0:T(8,128)S(1)} collective-permute-done((f32[64,128]{1,0:T(8,128)S(1)}, f32[64,128]{1,0:T(8,128)S(1)}, u32[]{:S(2)}, u32[]{:S(2)}) %collective-permute-start.55) | collective-permute-done | bytes 32800 | tf_op jit(solution)/shard_map/ppermute | solution.py:216
  137.6 1.9 collective-permute-start.58
  139.5 2.1 %collective-permute-done.60.refs_1_ = f32[64,128]{1,0:T(8,128)S(1)} collective-permute-done((f32[64,128]{1,0:T(8,128)S(1)}, f32[64,128]{1,0:T(8,128)S(1)}, u32[]{:S(2)}, u32[]{:S(2)}) %collective-permute-start.60) | collective-permute-done | bytes 32800 | tf_op jit(solution)/shard_map/ppermute | solution.py:216
  141.7 1.9 collective-permute-start.61
  143.6 2.0 collective-permute-done.61.refs_2_
  146.6 1.9 collective-permute-start.59
  148.5 2.0 collective-permute-done.62.refs_3_
  151.0 1.7 collective-permute-start.64
  152.7 2.3 %collective-permute-done.64.refs_2_ = f32[64,128]{1,0:T(8,128)S(1)} collective-permute-done((f32[64,128]{1,0:T(8,128)S(1)}, f32[64,128]{1,0:T(8,128)S(1)}, u32[]{:S(2)}, u32[]{:S(2)}) %collective-permute-start.64) | collective-permute-done | bytes 32800 | tf_op jit(solution)/shard_map/ppermute | solution.py:216
  157.4 2.0 collective-permute-start.67
  159.3 2.1 %collective-permute-done.69.refs_1_ = f32[64,128]{1,0:T(8,128)S(1)} collective-permute-done((f32[64,128]{1,0:T(8,128)S(1)}, f32[64,128]{1,0:T(8,128)S(1)}, u32[]{:S(2)}, u32[]{:S(2)}) %collective-permute-start.69) | collective-permute-done | bytes 32800 | tf_op jit(solution)/shard_map/ppermute | solution.py:216
  161.5 1.7 collective-permute-start.70
  163.2 2.2 %collective-permute-done.70.refs_2_ = f32[64,128]{1,0:T(8,128)S(1)} collective-permute-done((f32[64,128]{1,0:T(8,128)S(1)}, f32[64,128]{1,0:T(8,128)S(1)}, u32[]{:S(2)}, u32[]{:S(2)}) %collective-permute-start.70) | collective-permute-done | bytes 32800 | tf_op jit(solution)/shard_map/ppermute | solution.py:216
  165.4 2.2 %collective-permute-start.71 = (f32[64,128]{1,0:T(8,128)S(1)}, f32[64,128]{1,0:T(8,128)S(1)}, u32[]{:S(2)}, u32[]{:S(2)}) collective-permute-start(f32[64,128]{1,0:T(8,128)S(1)} %combine.43), channel_id=1, source_target_pairs={{0,16},{4,20},{8,24},{12,28},{16,0},{20,4},{24,8},{28,12},{1,17},{... | collective-permute-start | bytes 98312 | tf_op jit(solution)/shard_map/ppermute | solution.py:216
  167.6 1.7 collective-permute-start.68
  171.7 1.7 collective-permute-start.73
  173.3 2.3 %collective-permute-done.73.refs_2_ = f32[64,128]{1,0:T(8,128)S(1)} collective-permute-done((f32[64,128]{1,0:T(8,128)S(1)}, f32[64,128]{1,0:T(8,128)S(1)}, u32[]{:S(2)}, u32[]{:S(2)}) %collective-permute-start.73) | collective-permute-done | bytes 32800 | tf_op jit(solution)/shard_map/ppermute | solution.py:216
  178.0 2.0 collective-permute-start.76
  180.0 2.1 %collective-permute-done.78.refs_1_ = f32[64,128]{1,0:T(8,128)S(1)} collective-permute-done((f32[64,128]{1,0:T(8,128)S(1)}, f32[64,128]{1,0:T(8,128)S(1)}, u32[]{:S(2)}, u32[]{:S(2)}) %collective-permute-start.78) | collective-permute-done | bytes 32800 | tf_op jit(solution)/shard_map/ppermute | solution.py:216
  182.1 1.7 collective-permute-start.79
  183.8 2.2 %collective-permute-done.79.refs_2_ = f32[64,128]{1,0:T(8,128)S(1)} collective-permute-done((f32[64,128]{1,0:T(8,128)S(1)}, f32[64,128]{1,0:T(8,128)S(1)}, u32[]{:S(2)}, u32[]{:S(2)}) %collective-permute-start.79) | collective-permute-done | bytes 32800 | tf_op jit(solution)/shard_map/ppermute | solution.py:216
  187.0 2.0 collective-permute-start.77
  189.1 1.9 collective-permute-done.80.refs_3_
  191.5 1.7 collective-permute-start.82
  193.1 2.3 %collective-permute-done.82.refs_2_ = f32[64,128]{1,0:T(8,128)S(1)} collective-permute-done((f32[64,128]{1,0:T(8,128)S(1)}, f32[64,128]{1,0:T(8,128)S(1)}, u32[]{:S(2)}, u32[]{:S(2)}) %collective-permute-start.82) | collective-permute-done | bytes 32800 | tf_op jit(solution)/shard_map/ppermute | solution.py:216
  197.8 2.0 collective-permute-start.85
  199.8 2.1 %collective-permute-done.87.refs_1_ = f32[64,128]{1,0:T(8,128)S(1)} collective-permute-done((f32[64,128]{1,0:T(8,128)S(1)}, f32[64,128]{1,0:T(8,128)S(1)}, u32[]{:S(2)}, u32[]{:S(2)}) %collective-permute-start.87) | collective-permute-done | bytes 32800 | tf_op jit(solution)/shard_map/ppermute | solution.py:216
  201.9 1.7 collective-permute-start.88
  203.6 2.2 %collective-permute-done.88.refs_2_ = f32[64,128]{1,0:T(8,128)S(1)} collective-permute-done((f32[64,128]{1,0:T(8,128)S(1)}, f32[64,128]{1,0:T(8,128)S(1)}, u32[]{:S(2)}, u32[]{:S(2)}) %collective-permute-start.88) | collective-permute-done | bytes 32800 | tf_op jit(solution)/shard_map/ppermute | solution.py:216
  205.9 2.0 collective-permute-start.89
  207.8 1.7 collective-permute-start.86
  (200 shorter events, 77.8 us)
Async XLA Ops:
  2.7 7.2 %collective-permute-start.2 = (f32[64,128]{1,0:T(8,128)S(1)}, f32[64,128]{1,0:T(8,128)S(1)}, u32[]{:S(2)}, u32[]{:S(2)}) collective-permute-start(f32[64,128]{1,0:T(8,128)S(1)} %solve_up.6.refs_0_.right_ref), channel_id=1, source_target_pairs={{0,16},{4,20},{8,24},{12,28},{16,0},{20,4},{24,8},{28,12},{1,17},{... | collective-permute-start | bytes 98312 | tf_op jit(solution)/shard_map/ppermute | solution.py:216
  6.8 4.5 %collective-permute-start.1 = (f32[64,128]{1,0:T(8,128)S(1)}, f32[64,128]{1,0:T(8,128)S(1)}, u32[]{:S(2)}, u32[]{:S(2)}) collective-permute-start(f32[64,128]{1,0:T(8,128)S(1)} %solve_up.6.refs_0_.right_ref), channel_id=1, source_target_pairs={{0,8},{4,12},{8,0},{12,4},{16,24},{20,28},{24,16},{28,20},{1,9},{5... | collective-permute-start | bytes 98312 | tf_op jit(solution)/shard_map/ppermute | solution.py:216
  8.4 12.4 %collective-permute-start = (f32[64,128]{1,0:T(8,128)S(1)}, f32[64,128]{1,0:T(8,128)S(1)}, u32[]{:S(2)}, u32[]{:S(2)}) collective-permute-start(f32[64,128]{1,0:T(8,128)S(1)} %solve_up.6.refs_0_.right_ref), channel_id=1, source_target_pairs={{0,4},{4,0},{8,12},{12,8},{16,20},{20,16},{24,28},{28,24},{1,5},{5... | collective-permute-start | bytes 98312 | tf_op jit(solution)/shard_map/ppermute | solution.py:216
  9.9 3.9 %collective-permute-start.4 = (f32[64,128]{1,0:T(8,128)S(1)}, f32[64,128]{1,0:T(8,128)S(1)}, u32[]{:S(2)}, u32[]{:S(2)}) collective-permute-start(f32[64,128]{1,0:T(8,128)S(1)} %collective-permute-done.2.refs_1_.refs_4_), channel_id=1, source_target_pairs={{0,8},{4,12},{8,0},{12,4},{16,24},{20,28},{24,16},{28,20},{1,9},{5... | collective-permute-start | bytes 98312 | tf_op jit(solution)/shard_map/ppermute | solution.py:216
  11.3 9.5 %collective-permute-start.3 = (f32[2,64,128]{2,1,0:T(8,128)S(1)}, f32[2,64,128]{2,1,0:T(8,128)S(1)}, u32[]{:S(2)}, u32[]{:S(2)}) collective-permute-start(f32[2,64,128]{2,1,0:T(8,128)S(1)} %combine.25), channel_id=1, source_target_pairs={{0,4},{4,0},{8,12},{12,8},{16,20},{20,16},{24,28},{28,24},{1,5},{5... | collective-permute-start | bytes 196616 | tf_op jit(solution)/shard_map/ppermute | solution.py:216
  13.8 7.0 %collective-permute-start.5 = (f32[64,128]{1,0:T(8,128)S(1)}, f32[64,128]{1,0:T(8,128)S(1)}, u32[]{:S(2)}, u32[]{:S(2)}) collective-permute-start(f32[64,128]{1,0:T(8,128)S(1)} %collective-permute-done.4.refs_5_), channel_id=1, source_target_pairs={{0,4},{4,0},{8,12},{12,8},{16,20},{20,16},{24,28},{28,24},{1,5},{5... | collective-permute-start | bytes 98312 | tf_op jit(solution)/shard_map/ppermute | solution.py:216
  22.8 3.9 %collective-permute-start.8 = (f32[64,128]{1,0:T(8,128)S(1)}, f32[64,128]{1,0:T(8,128)S(1)}, u32[]{:S(2)}, u32[]{:S(2)}) collective-permute-start(f32[64,128]{1,0:T(8,128)S(1)} %combine.26), channel_id=1, source_target_pairs={{0,2},{1,3},{2,0},{3,1},{4,6},{5,7},{6,4},{7,5},{8,10},{9,11},{10,... | collective-permute-start | bytes 98312 | tf_op jit(solution)/shard_map/ppermute | solution.py:216
  26.9 4.3 %collective-permute-start.10 = (f32[64,128]{1,0:T(8,128)S(1)}, f32[64,128]{1,0:T(8,128)S(1)}, u32[]{:S(2)}, u32[]{:S(2)}) collective-permute-start(f32[64,128]{1,0:T(8,128)S(1)} %solve_up.7.refs_0_.right_ref), channel_id=1, source_target_pairs={{0,8},{4,12},{8,0},{12,4},{16,24},{20,28},{24,16},{28,20},{1,9},{5... | collective-permute-start | bytes 98312 | tf_op jit(solution)/shard_map/ppermute | solution.py:216
  28.2 5.2 %collective-permute-start.11 = (f32[64,128]{1,0:T(8,128)S(1)}, f32[64,128]{1,0:T(8,128)S(1)}, u32[]{:S(2)}, u32[]{:S(2)}) collective-permute-start(f32[64,128]{1,0:T(8,128)S(1)} %solve_up.7.refs_0_.right_ref), channel_id=1, source_target_pairs={{0,16},{4,20},{8,24},{12,28},{16,0},{20,4},{24,8},{28,12},{1,17},{... | collective-permute-start | bytes 98312 | tf_op jit(solution)/shard_map/ppermute | solution.py:216
  33.3 7.4 %collective-permute-start.12 = (f32[2,64,128]{2,1,0:T(8,128)S(1)}, f32[2,64,128]{2,1,0:T(8,128)S(1)}, u32[]{:S(2)}, u32[]{:S(2)}) collective-permute-start(f32[2,64,128]{2,1,0:T(8,128)S(1)} %combine.27), channel_id=1, source_target_pairs={{0,4},{4,0},{8,12},{12,8},{16,20},{20,16},{24,28},{28,24},{1,5},{5... | collective-permute-start | bytes 196616 | tf_op jit(solution)/shard_map/ppermute | solution.py:216
  33.5 3.9 %collective-permute-start.13 = (f32[64,128]{1,0:T(8,128)S(1)}, f32[64,128]{1,0:T(8,128)S(1)}, u32[]{:S(2)}, u32[]{:S(2)}) collective-permute-start(f32[64,128]{1,0:T(8,128)S(1)} %collective-permute-done.11.refs_1_.refs_4_), channel_id=1, source_target_pairs={{0,8},{4,12},{8,0},{12,4},{16,24},{20,28},{24,16},{28,20},{1,9},{5... | collective-permute-start | bytes 98312 | tf_op jit(solution)/shard_map/ppermute | solution.py:216
  34.8 6.0 %collective-permute-start.9 = (f32[64,128]{1,0:T(8,128)S(1)}, f32[64,128]{1,0:T(8,128)S(1)}, u32[]{:S(2)}, u32[]{:S(2)}) collective-permute-start(f32[64,128]{1,0:T(8,128)S(1)} %solve_up.7.refs_0_.right_ref), channel_id=1, source_target_pairs={{0,4},{4,0},{8,12},{12,8},{16,20},{20,16},{24,28},{28,24},{1,5},{5... | collective-permute-start | bytes 98312 | tf_op jit(solution)/shard_map/ppermute | solution.py:216
  43.3 3.9 %collective-permute-start.17 = (f32[64,128]{1,0:T(8,128)S(1)}, f32[64,128]{1,0:T(8,128)S(1)}, u32[]{:S(2)}, u32[]{:S(2)}) collective-permute-start(f32[64,128]{1,0:T(8,128)S(1)} %combine.28), channel_id=1, source_target_pairs={{0,2},{1,3},{2,0},{3,1},{4,6},{5,7},{6,4},{7,5},{8,10},{9,11},{10,... | collective-permute-start | bytes 98312 | tf_op jit(solution)/shard_map/ppermute | solution.py:216
  47.4 4.2 %collective-permute-start.19 = (f32[64,128]{1,0:T(8,128)S(1)}, f32[64,128]{1,0:T(8,128)S(1)}, u32[]{:S(2)}, u32[]{:S(2)}) collective-permute-start(f32[64,128]{1,0:T(8,128)S(1)} %solve_up.8.refs_0_.right_ref), channel_id=1, source_target_pairs={{0,8},{4,12},{8,0},{12,4},{16,24},{20,28},{24,16},{28,20},{1,9},{5... | collective-permute-start | bytes 98312 | tf_op jit(solution)/shard_map/ppermute | solution.py:216
  48.7 4.8 %collective-permute-start.20 = (f32[64,128]{1,0:T(8,128)S(1)}, f32[64,128]{1,0:T(8,128)S(1)}, u32[]{:S(2)}, u32[]{:S(2)}) collective-permute-start(f32[64,128]{1,0:T(8,128)S(1)} %solve_up.8.refs_0_.right_ref), channel_id=1, source_target_pairs={{0,16},{4,20},{8,24},{12,28},{16,0},{20,4},{24,8},{28,12},{1,17},{... | collective-permute-start | bytes 98312 | tf_op jit(solution)/shard_map/ppermute | solution.py:216
  53.5 7.6 %collective-permute-start.21 = (f32[2,64,128]{2,1,0:T(8,128)S(1)}, f32[2,64,128]{2,1,0:T(8,128)S(1)}, u32[]{:S(2)}, u32[]{:S(2)}) collective-permute-start(f32[2,64,128]{2,1,0:T(8,128)S(1)} %combine.29), channel_id=1, source_target_pairs={{0,4},{4,0},{8,12},{12,8},{16,20},{20,16},{24,28},{28,24},{1,5},{5... | collective-permute-start | bytes 196616 | tf_op jit(solution)/shard_map/ppermute | solution.py:216
  54.6 3.9 %collective-permute-start.22 = (f32[64,128]{1,0:T(8,128)S(1)}, f32[64,128]{1,0:T(8,128)S(1)}, u32[]{:S(2)}, u32[]{:S(2)}) collective-permute-start(f32[64,128]{1,0:T(8,128)S(1)} %collective-permute-done.20.refs_1_.refs_4_), channel_id=1, source_target_pairs={{0,8},{4,12},{8,0},{12,4},{16,24},{20,28},{24,16},{28,20},{1,9},{5... | collective-permute-start | bytes 98312 | tf_op jit(solution)/shard_map/ppermute | solution.py:216
  56.3 4.7 %collective-permute-start.18 = (f32[64,128]{1,0:T(8,128)S(1)}, f32[64,128]{1,0:T(8,128)S(1)}, u32[]{:S(2)}, u32[]{:S(2)}) collective-permute-start(f32[64,128]{1,0:T(8,128)S(1)} %solve_up.8.refs_0_.right_ref), channel_id=1, source_target_pairs={{0,4},{4,0},{8,12},{12,8},{16,20},{20,16},{24,28},{28,24},{1,5},{5... | collective-permute-start | bytes 98312 | tf_op jit(solution)/shard_map/ppermute | solution.py:216
  58.5 3.9 %collective-permute-start.23 = (f32[64,128]{1,0:T(8,128)S(1)}, f32[64,128]{1,0:T(8,128)S(1)}, u32[]{:S(2)}, u32[]{:S(2)}) collective-permute-start(f32[64,128]{1,0:T(8,128)S(1)} %collective-permute-done.22.refs_5_), channel_id=1, source_target_pairs={{0,4},{4,0},{8,12},{12,8},{16,20},{20,16},{24,28},{28,24},{1,5},{5... | collective-permute-start | bytes 98312 | tf_op jit(solution)/shard_map/ppermute | solution.py:216
  64.4 3.9 %collective-permute-start.26 = (f32[64,128]{1,0:T(8,128)S(1)}, f32[64,128]{1,0:T(8,128)S(1)}, u32[]{:S(2)}, u32[]{:S(2)}) collective-permute-start(f32[64,128]{1,0:T(8,128)S(1)} %combine.30), channel_id=1, source_target_pairs={{0,2},{1,3},{2,0},{3,1},{4,6},{5,7},{6,4},{7,5},{8,10},{9,11},{10,... | collective-permute-start | bytes 98312 | tf_op jit(solution)/shard_map/ppermute | solution.py:216
  68.5 4.4 %collective-permute-start.28 = (f32[64,128]{1,0:T(8,128)S(1)}, f32[64,128]{1,0:T(8,128)S(1)}, u32[]{:S(2)}, u32[]{:S(2)}) collective-permute-start(f32[64,128]{1,0:T(8,128)S(1)} %solve_up.9.refs_0_.right_ref), channel_id=1, source_target_pairs={{0,8},{4,12},{8,0},{12,4},{16,24},{20,28},{24,16},{28,20},{1,9},{5... | collective-permute-start | bytes 98312 | tf_op jit(solution)/shard_map/ppermute | solution.py:216
  70.2 4.9 %collective-permute-start.29 = (f32[64,128]{1,0:T(8,128)S(1)}, f32[64,128]{1,0:T(8,128)S(1)}, u32[]{:S(2)}, u32[]{:S(2)}) collective-permute-start(f32[64,128]{1,0:T(8,128)S(1)} %solve_up.9.refs_0_.right_ref), channel_id=1, source_target_pairs={{0,16},{4,20},{8,24},{12,28},{16,0},{20,4},{24,8},{28,12},{1,17},{... | collective-permute-start | bytes 98312 | tf_op jit(solution)/shard_map/ppermute | solution.py:216
  75.2 7.4 %collective-permute-start.30 = (f32[2,64,128]{2,1,0:T(8,128)S(1)}, f32[2,64,128]{2,1,0:T(8,128)S(1)}, u32[]{:S(2)}, u32[]{:S(2)}) collective-permute-start(f32[2,64,128]{2,1,0:T(8,128)S(1)} %combine.31), channel_id=1, source_target_pairs={{0,4},{4,0},{8,12},{12,8},{16,20},{20,16},{24,28},{28,24},{1,5},{5... | collective-permute-start | bytes 196616 | tf_op jit(solution)/shard_map/ppermute | solution.py:216
  75.2 3.9 %collective-permute-start.31 = (f32[64,128]{1,0:T(8,128)S(1)}, f32[64,128]{1,0:T(8,128)S(1)}, u32[]{:S(2)}, u32[]{:S(2)}) collective-permute-start(f32[64,128]{1,0:T(8,128)S(1)} %collective-permute-done.29.refs_1_.refs_4_), channel_id=1, source_target_pairs={{0,8},{4,12},{8,0},{12,4},{16,24},{20,28},{24,16},{28,20},{1,9},{5... | collective-permute-start | bytes 98312 | tf_op jit(solution)/shard_map/ppermute | solution.py:216
  76.3 6.3 %collective-permute-start.27 = (f32[64,128]{1,0:T(8,128)S(1)}, f32[64,128]{1,0:T(8,128)S(1)}, u32[]{:S(2)}, u32[]{:S(2)}) collective-permute-start(f32[64,128]{1,0:T(8,128)S(1)} %solve_up.9.refs_0_.right_ref), channel_id=1, source_target_pairs={{0,4},{4,0},{8,12},{12,8},{16,20},{20,16},{24,28},{28,24},{1,5},{5... | collective-permute-start | bytes 98312 | tf_op jit(solution)/shard_map/ppermute | solution.py:216
  79.2 3.9 %collective-permute-start.32 = (f32[64,128]{1,0:T(8,128)S(1)}, f32[64,128]{1,0:T(8,128)S(1)}, u32[]{:S(2)}, u32[]{:S(2)}) collective-permute-start(f32[64,128]{1,0:T(8,128)S(1)} %collective-permute-done.31.refs_5_), channel_id=1, source_target_pairs={{0,4},{4,0},{8,12},{12,8},{16,20},{20,16},{24,28},{28,24},{1,5},{5... | collective-permute-start | bytes 98312 | tf_op jit(solution)/shard_map/ppermute | solution.py:216
  85.0 3.9 %collective-permute-start.35 = (f32[64,128]{1,0:T(8,128)S(1)}, f32[64,128]{1,0:T(8,128)S(1)}, u32[]{:S(2)}, u32[]{:S(2)}) collective-permute-start(f32[64,128]{1,0:T(8,128)S(1)} %combine.32), channel_id=1, source_target_pairs={{0,2},{1,3},{2,0},{3,1},{4,6},{5,7},{6,4},{7,5},{8,10},{9,11},{10,... | collective-permute-start | bytes 98312 | tf_op jit(solution)/shard_map/ppermute | solution.py:216
  89.1 4.0 %collective-permute-start.37 = (f32[64,128]{1,0:T(8,128)S(1)}, f32[64,128]{1,0:T(8,128)S(1)}, u32[]{:S(2)}, u32[]{:S(2)}) collective-permute-start(f32[64,128]{1,0:T(8,128)S(1)} %solve_up.10.refs_0_.right_ref), channel_id=1, source_target_pairs={{0,8},{4,12},{8,0},{12,4},{16,24},{20,28},{24,16},{28,20},{1,9},{5... | collective-permute-start | bytes 98312 | tf_op jit(solution)/shard_map/ppermute | solution.py:216
  90.2 4.8 %collective-permute-start.38 = (f32[64,128]{1,0:T(8,128)S(1)}, f32[64,128]{1,0:T(8,128)S(1)}, u32[]{:S(2)}, u32[]{:S(2)}) collective-permute-start(f32[64,128]{1,0:T(8,128)S(1)} %solve_up.10.refs_0_.right_ref), channel_id=1, source_target_pairs={{0,16},{4,20},{8,24},{12,28},{16,0},{20,4},{24,8},{28,12},{1,17},{... | collective-permute-start | bytes 98312 | tf_op jit(solution)/shard_map/ppermute | solution.py:216
  95.0 7.4 %collective-permute-start.39 = (f32[2,64,128]{2,1,0:T(8,128)S(1)}, f32[2,64,128]{2,1,0:T(8,128)S(1)}, u32[]{:S(2)}, u32[]{:S(2)}) collective-permute-start(f32[2,64,128]{2,1,0:T(8,128)S(1)} %combine.33), channel_id=1, source_target_pairs={{0,4},{4,0},{8,12},{12,8},{16,20},{20,16},{24,28},{28,24},{1,5},{5... | collective-permute-start | bytes 196616 | tf_op jit(solution)/shard_map/ppermute | solution.py:216
  96.1 3.9 %collective-permute-start.40 = (f32[64,128]{1,0:T(8,128)S(1)}, f32[64,128]{1,0:T(8,128)S(1)}, u32[]{:S(2)}, u32[]{:S(2)}) collective-permute-start(f32[64,128]{1,0:T(8,128)S(1)} %collective-permute-done.38.refs_1_.refs_4_), channel_id=1, source_target_pairs={{0,8},{4,12},{8,0},{12,4},{16,24},{20,28},{24,16},{28,20},{1,9},{5... | collective-permute-start | bytes 98312 | tf_op jit(solution)/shard_map/ppermute | solution.py:216
  98.0 4.4 %collective-permute-start.36 = (f32[64,128]{1,0:T(8,128)S(1)}, f32[64,128]{1,0:T(8,128)S(1)}, u32[]{:S(2)}, u32[]{:S(2)}) collective-permute-start(f32[64,128]{1,0:T(8,128)S(1)} %solve_up.10.refs_0_.right_ref), channel_id=1, source_target_pairs={{0,4},{4,0},{8,12},{12,8},{16,20},{20,16},{24,28},{28,24},{1,5},{5... | collective-permute-start | bytes 98312 | tf_op jit(solution)/shard_map/ppermute | solution.py:216
  100.0 3.9 %collective-permute-start.41 = (f32[64,128]{1,0:T(8,128)S(1)}, f32[64,128]{1,0:T(8,128)S(1)}, u32[]{:S(2)}, u32[]{:S(2)}) collective-permute-start(f32[64,128]{1,0:T(8,128)S(1)} %collective-permute-done.40.refs_5_), channel_id=1, source_target_pairs={{0,4},{4,0},{8,12},{12,8},{16,20},{20,16},{24,28},{28,24},{1,5},{5... | collective-permute-start | bytes 98312 | tf_op jit(solution)/shard_map/ppermute | solution.py:216
  105.9 3.9 %collective-permute-start.44 = (f32[64,128]{1,0:T(8,128)S(1)}, f32[64,128]{1,0:T(8,128)S(1)}, u32[]{:S(2)}, u32[]{:S(2)}) collective-permute-start(f32[64,128]{1,0:T(8,128)S(1)} %combine.34), channel_id=1, source_target_pairs={{0,2},{1,3},{2,0},{3,1},{4,6},{5,7},{6,4},{7,5},{8,10},{9,11},{10,... | collective-permute-start | bytes 98312 | tf_op jit(solution)/shard_map/ppermute | solution.py:216
  110.1 4.0 %collective-permute-start.46 = (f32[64,128]{1,0:T(8,128)S(1)}, f32[64,128]{1,0:T(8,128)S(1)}, u32[]{:S(2)}, u32[]{:S(2)}) collective-permute-start(f32[64,128]{1,0:T(8,128)S(1)} %solve_down.6.refs_0_), channel_id=1, source_target_pairs={{0,2},{1,3},{2,0},{3,1},{4,6},{5,7},{6,4},{7,5},{8,10},{9,11},{10,... | collective-permute-start | bytes 98312 | tf_op jit(solution)/shard_map/ppermute | solution.py:216
  116.4 4.3 %collective-permute-start.51 = (f32[64,128]{1,0:T(8,128)S(1)}, f32[64,128]{1,0:T(8,128)S(1)}, u32[]{:S(2)}, u32[]{:S(2)}) collective-permute-start(f32[64,128]{1,0:T(8,128)S(1)} %get-tuple-element.103), channel_id=1, source_target_pairs={{0,4},{4,0},{8,12},{12,8},{16,20},{20,16},{24,28},{28,24},{1,5},{5... | collective-permute-start | bytes 98312 | tf_op jit(solution)/shard_map/ppermute | solution.py:216
  117.3 7.3 %collective-permute-start.49 = (f32[2,64,128]{2,1,0:T(8,128)S(1)}, f32[2,64,128]{2,1,0:T(8,128)S(1)}, u32[]{:S(2)}, u32[]{:S(2)}) collective-permute-start(f32[2,64,128]{2,1,0:T(8,128)S(1)} %get-tuple-element.100), channel_id=1, source_target_pairs={{0,4},{4,0},{8,12},{12,8},{16,20},{20,16},{24,28},{28,24},{1,5},{5... | collective-permute-start | bytes 196616 | tf_op jit(solution)/shard_map/ppermute | solution.py:216
  122.5 6.6 %collective-permute-start.48 = (f32[64,128]{1,0:T(8,128)S(1)}, f32[64,128]{1,0:T(8,128)S(1)}, u32[]{:S(2)}, u32[]{:S(2)}) collective-permute-start(f32[64,128]{1,0:T(8,128)S(1)} %get-tuple-element.98), channel_id=1, source_target_pairs={{0,4},{4,0},{8,12},{12,8},{16,20},{20,16},{24,28},{28,24},{1,5},{5... | collective-permute-start | bytes 98312 | tf_op jit(solution)/shard_map/ppermute | solution.py:216
  124.6 4.9 %collective-permute-start.53 = (f32[64,128]{1,0:T(8,128)S(1)}, f32[64,128]{1,0:T(8,128)S(1)}, u32[]{:S(2)}, u32[]{:S(2)}) collective-permute-start(f32[64,128]{1,0:T(8,128)S(1)} %combine.37), channel_id=1, source_target_pairs={{0,16},{4,20},{8,24},{12,28},{16,0},{20,4},{24,8},{28,12},{1,17},{... | collective-permute-start | bytes 98312 | tf_op jit(solution)/shard_map/ppermute | solution.py:216
  131.2 4.0 %collective-permute-start.55 = (f32[64,128]{1,0:T(8,128)S(1)}, f32[64,128]{1,0:T(8,128)S(1)}, u32[]{:S(2)}, u32[]{:S(2)}) collective-permute-start(f32[64,128]{1,0:T(8,128)S(1)} %solve_down.7.refs_0_), channel_id=1, source_target_pairs={{0,2},{1,3},{2,0},{3,1},{4,6},{5,7},{6,4},{7,5},{8,10},{9,11},{10,... | collective-permute-start | bytes 98312 | tf_op jit(solution)/shard_map/ppermute | solution.py:216
  137.4 4.2 %collective-permute-start.60 = (f32[64,128]{1,0:T(8,128)S(1)}, f32[64,128]{1,0:T(8,128)S(1)}, u32[]{:S(2)}, u32[]{:S(2)}) collective-permute-start(f32[64,128]{1,0:T(8,128)S(1)} %get-tuple-element.110), channel_id=1, source_target_pairs={{0,4},{4,0},{8,12},{12,8},{16,20},{20,16},{24,28},{28,24},{1,5},{5... | collective-permute-start | bytes 98312 | tf_op jit(solution)/shard_map/ppermute | solution.py:216
  137.6 8.0 %collective-permute-start.58 = (f32[2,64,128]{2,1,0:T(8,128)S(1)}, f32[2,64,128]{2,1,0:T(8,128)S(1)}, u32[]{:S(2)}, u32[]{:S(2)}) collective-permute-start(f32[2,64,128]{2,1,0:T(8,128)S(1)} %get-tuple-element.107), channel_id=1, source_target_pairs={{0,4},{4,0},{8,12},{12,8},{16,20},{20,16},{24,28},{28,24},{1,5},{5... | collective-permute-start | bytes 196616 | tf_op jit(solution)/shard_map/ppermute | solution.py:216
  143.6 4.9 %collective-permute-start.57 = (f32[64,128]{1,0:T(8,128)S(1)}, f32[64,128]{1,0:T(8,128)S(1)}, u32[]{:S(2)}, u32[]{:S(2)}) collective-permute-start(f32[64,128]{1,0:T(8,128)S(1)} %get-tuple-element.105), channel_id=1, source_target_pairs={{0,4},{4,0},{8,12},{12,8},{16,20},{20,16},{24,28},{28,24},{1,5},{5... | collective-permute-start | bytes 98312 | tf_op jit(solution)/shard_map/ppermute | solution.py:216
  145.6 4.9 %collective-permute-start.62 = (f32[64,128]{1,0:T(8,128)S(1)}, f32[64,128]{1,0:T(8,128)S(1)}, u32[]{:S(2)}, u32[]{:S(2)}) collective-permute-start(f32[64,128]{1,0:T(8,128)S(1)} %combine.40), channel_id=1, source_target_pairs={{0,16},{4,20},{8,24},{12,28},{16,0},{20,4},{24,8},{28,12},{1,17},{... | collective-permute-start | bytes 98312 | tf_op jit(solution)/shard_map/ppermute | solution.py:216
  146.6 4.3 %collective-permute-start.59 = (f32[64,128]{1,0:T(8,128)S(1)}, f32[64,128]{1,0:T(8,128)S(1)}, u32[]{:S(2)}, u32[]{:S(2)}) collective-permute-start(f32[64,128]{1,0:T(8,128)S(1)} %combine.38), channel_id=1, source_target_pairs={{0,8},{4,12},{8,0},{12,4},{16,24},{20,28},{24,16},{28,20},{1,9},{5... | collective-permute-start | bytes 98312 | tf_op jit(solution)/shard_map/ppermute | solution.py:216
  151.0 4.0 %collective-permute-start.64 = (f32[64,128]{1,0:T(8,128)S(1)}, f32[64,128]{1,0:T(8,128)S(1)}, u32[]{:S(2)}, u32[]{:S(2)}) collective-permute-start(f32[64,128]{1,0:T(8,128)S(1)} %solve_down.8.refs_0_), channel_id=1, source_target_pairs={{0,2},{1,3},{2,0},{3,1},{4,6},{5,7},{6,4},{7,5},{8,10},{9,11},{10,... | collective-permute-start | bytes 98312 | tf_op jit(solution)/shard_map/ppermute | solution.py:216
  157.2 4.2 %collective-permute-start.69 = (f32[64,128]{1,0:T(8,128)S(1)}, f32[64,128]{1,0:T(8,128)S(1)}, u32[]{:S(2)}, u32[]{:S(2)}) collective-permute-start(f32[64,128]{1,0:T(8,128)S(1)} %get-tuple-element.117), channel_id=1, source_target_pairs={{0,4},{4,0},{8,12},{12,8},{16,20},{20,16},{24,28},{28,24},{1,5},{5... | collective-permute-start | bytes 98312 | tf_op jit(solution)/shard_map/ppermute | solution.py:216
  157.4 8.0 %collective-permute-start.67 = (f32[2,64,128]{2,1,0:T(8,128)S(1)}, f32[2,64,128]{2,1,0:T(8,128)S(1)}, u32[]{:S(2)}, u32[]{:S(2)}) collective-permute-start(f32[2,64,128]{2,1,0:T(8,128)S(1)} %get-tuple-element.114), channel_id=1, source_target_pairs={{0,4},{4,0},{8,12},{12,8},{16,20},{20,16},{24,28},{28,24},{1,5},{5... | collective-permute-start | bytes 196616 | tf_op jit(solution)/shard_map/ppermute | solution.py:216
  161.5 3.9 %collective-permute-start.70 = (f32[64,128]{1,0:T(8,128)S(1)}, f32[64,128]{1,0:T(8,128)S(1)}, u32[]{:S(2)}, u32[]{:S(2)}) collective-permute-start(f32[64,128]{1,0:T(8,128)S(1)} %combine.42), channel_id=1, source_target_pairs={{0,8},{4,12},{8,0},{12,4},{16,24},{20,28},{24,16},{28,20},{1,9},{5... | collective-permute-start | bytes 98312 | tf_op jit(solution)/shard_map/ppermute | solution.py:216
  163.2 6.0 %collective-permute-start.66 = (f32[64,128]{1,0:T(8,128)S(1)}, f32[64,128]{1,0:T(8,128)S(1)}, u32[]{:S(2)}, u32[]{:S(2)}) collective-permute-start(f32[64,128]{1,0:T(8,128)S(1)} %get-tuple-element.112), channel_id=1, source_target_pairs={{0,4},{4,0},{8,12},{12,8},{16,20},{20,16},{24,28},{28,24},{1,5},{5... | collective-permute-start | bytes 98312 | tf_op jit(solution)/shard_map/ppermute | solution.py:216
  165.4 4.9 %collective-permute-start.71 = (f32[64,128]{1,0:T(8,128)S(1)}, f32[64,128]{1,0:T(8,128)S(1)}, u32[]{:S(2)}, u32[]{:S(2)}) collective-permute-start(f32[64,128]{1,0:T(8,128)S(1)} %combine.43), channel_id=1, source_target_pairs={{0,16},{4,20},{8,24},{12,28},{16,0},{20,4},{24,8},{28,12},{1,17},{... | collective-permute-start | bytes 98312 | tf_op jit(solution)/shard_map/ppermute | solution.py:216
  167.6 3.9 %collective-permute-start.68 = (f32[64,128]{1,0:T(8,128)S(1)}, f32[64,128]{1,0:T(8,128)S(1)}, u32[]{:S(2)}, u32[]{:S(2)}) collective-permute-start(f32[64,128]{1,0:T(8,128)S(1)} %combine.41), channel_id=1, source_target_pairs={{0,8},{4,12},{8,0},{12,4},{16,24},{20,28},{24,16},{28,20},{1,9},{5... | collective-permute-start | bytes 98312 | tf_op jit(solution)/shard_map/ppermute | solution.py:216
  171.7 4.0 %collective-permute-start.73 = (f32[64,128]{1,0:T(8,128)S(1)}, f32[64,128]{1,0:T(8,128)S(1)}, u32[]{:S(2)}, u32[]{:S(2)}) collective-permute-start(f32[64,128]{1,0:T(8,128)S(1)} %solve_down.9.refs_0_), channel_id=1, source_target_pairs={{0,2},{1,3},{2,0},{3,1},{4,6},{5,7},{6,4},{7,5},{8,10},{9,11},{10,... | collective-permute-start | bytes 98312 | tf_op jit(solution)/shard_map/ppermute | solution.py:216
  177.9 4.2 %collective-permute-start.78 = (f32[64,128]{1,0:T(8,128)S(1)}, f32[64,128]{1,0:T(8,128)S(1)}, u32[]{:S(2)}, u32[]{:S(2)}) collective-permute-start(f32[64,128]{1,0:T(8,128)S(1)} %get-tuple-element.124), channel_id=1, source_target_pairs={{0,4},{4,0},{8,12},{12,8},{16,20},{20,16},{24,28},{28,24},{1,5},{5... | collective-permute-start | bytes 98312 | tf_op jit(solution)/shard_map/ppermute | solution.py:216
  178.0 8.1 %collective-permute-start.76 = (f32[2,64,128]{2,1,0:T(8,128)S(1)}, f32[2,64,128]{2,1,0:T(8,128)S(1)}, u32[]{:S(2)}, u32[]{:S(2)}) collective-permute-start(f32[2,64,128]{2,1,0:T(8,128)S(1)} %get-tuple-element.121), channel_id=1, source_target_pairs={{0,4},{4,0},{8,12},{12,8},{16,20},{20,16},{24,28},{28,24},{1,5},{5... | collective-permute-start | bytes 196616 | tf_op jit(solution)/shard_map/ppermute | solution.py:216
  182.1 3.9 %collective-permute-start.79 = (f32[64,128]{1,0:T(8,128)S(1)}, f32[64,128]{1,0:T(8,128)S(1)}, u32[]{:S(2)}, u32[]{:S(2)}) collective-permute-start(f32[64,128]{1,0:T(8,128)S(1)} %combine.45), channel_id=1, source_target_pairs={{0,8},{4,12},{8,0},{12,4},{16,24},{20,28},{24,16},{28,20},{1,9},{5... | collective-permute-start | bytes 98312 | tf_op jit(solution)/shard_map/ppermute | solution.py:216
  183.8 5.3 %collective-permute-start.75 = (f32[64,128]{1,0:T(8,128)S(1)}, f32[64,128]{1,0:T(8,128)S(1)}, u32[]{:S(2)}, u32[]{:S(2)}) collective-permute-start(f32[64,128]{1,0:T(8,128)S(1)} %get-tuple-element.119), channel_id=1, source_target_pairs={{0,4},{4,0},{8,12},{12,8},{16,20},{20,16},{24,28},{28,24},{1,5},{5... | collective-permute-start | bytes 98312 | tf_op jit(solution)/shard_map/ppermute | solution.py:216
  186.1 4.9 %collective-permute-start.80 = (f32[64,128]{1,0:T(8,128)S(1)}, f32[64,128]{1,0:T(8,128)S(1)}, u32[]{:S(2)}, u32[]{:S(2)}) collective-permute-start(f32[64,128]{1,0:T(8,128)S(1)} %combine.46), channel_id=1, source_target_pairs={{0,16},{4,20},{8,24},{12,28},{16,0},{20,4},{24,8},{28,12},{1,17},{... | collective-permute-start | bytes 98312 | tf_op jit(solution)/shard_map/ppermute | solution.py:216
  187.0 4.2 %collective-permute-start.77 = (f32[64,128]{1,0:T(8,128)S(1)}, f32[64,128]{1,0:T(8,128)S(1)}, u32[]{:S(2)}, u32[]{:S(2)}) collective-permute-start(f32[64,128]{1,0:T(8,128)S(1)} %combine.44), channel_id=1, source_target_pairs={{0,8},{4,12},{8,0},{12,4},{16,24},{20,28},{24,16},{28,20},{1,9},{5... | collective-permute-start | bytes 98312 | tf_op jit(solution)/shard_map/ppermute | solution.py:216
  191.5 4.0 %collective-permute-start.82 = (f32[64,128]{1,0:T(8,128)S(1)}, f32[64,128]{1,0:T(8,128)S(1)}, u32[]{:S(2)}, u32[]{:S(2)}) collective-permute-start(f32[64,128]{1,0:T(8,128)S(1)} %solve_down.10.refs_0_), channel_id=1, source_target_pairs={{0,2},{1,3},{2,0},{3,1},{4,6},{5,7},{6,4},{7,5},{8,10},{9,11},{10,... | collective-permute-start | bytes 98312 | tf_op jit(solution)/shard_map/ppermute | solution.py:216
  197.7 4.2 %collective-permute-start.87 = (f32[64,128]{1,0:T(8,128)S(1)}, f32[64,128]{1,0:T(8,128)S(1)}, u32[]{:S(2)}, u32[]{:S(2)}) collective-permute-start(f32[64,128]{1,0:T(8,128)S(1)} %get-tuple-element.131), channel_id=1, source_target_pairs={{0,4},{4,0},{8,12},{12,8},{16,20},{20,16},{24,28},{28,24},{1,5},{5... | collective-permute-start | bytes 98312 | tf_op jit(solution)/shard_map/ppermute | solution.py:216
  197.8 8.1 %collective-permute-start.85 = (f32[2,64,128]{2,1,0:T(8,128)S(1)}, f32[2,64,128]{2,1,0:T(8,128)S(1)}, u32[]{:S(2)}, u32[]{:S(2)}) collective-permute-start(f32[2,64,128]{2,1,0:T(8,128)S(1)} %get-tuple-element.128), channel_id=1, source_target_pairs={{0,4},{4,0},{8,12},{12,8},{16,20},{20,16},{24,28},{28,24},{1,5},{5... | collective-permute-start | bytes 196616 | tf_op jit(solution)/shard_map/ppermute | solution.py:216
  203.6 5.9 %collective-permute-start.84 = (f32[64,128]{1,0:T(8,128)S(1)}, f32[64,128]{1,0:T(8,128)S(1)}, u32[]{:S(2)}, u32[]{:S(2)}) collective-permute-start(f32[64,128]{1,0:T(8,128)S(1)} %get-tuple-element.126), channel_id=1, source_target_pairs={{0,4},{4,0},{8,12},{12,8},{16,20},{20,16},{24,28},{28,24},{1,5},{5... | collective-permute-start | bytes 98312 | tf_op jit(solution)/shard_map/ppermute | solution.py:216
  205.9 4.9 %collective-permute-start.89 = (f32[64,128]{1,0:T(8,128)S(1)}, f32[64,128]{1,0:T(8,128)S(1)}, u32[]{:S(2)}, u32[]{:S(2)}) collective-permute-start(f32[64,128]{1,0:T(8,128)S(1)} %combine.49), channel_id=1, source_target_pairs={{0,16},{4,20},{8,24},{12,28},{16,0},{20,4},{24,8},{28,12},{1,17},{... | collective-permute-start | bytes 98312 | tf_op jit(solution)/shard_map/ppermute | solution.py:216
  (35 other events, 138.8 us)

commit v4 on v1

--- a/solution.py
+++ b/solution.py
@@ -28,19 +28,26 @@
 
 
 def gather_blocks_kernel(
-    n_col, level, target_ref, source_ref, count_ref, place_ref, blocks_ref, high_ref, low_ref, total
+    n_col, level, target_ref, source_ref, count_ref, place_ref, blocks_ref, *refs
 ):
-    block = blocks_ref.shape[-1]
+    high_ref, low_ref, slots, total, arrived = refs[-5:]
+    slot_count, block = slots.shape[:2]
+    count = count_ref[level]
+
+    def fetch(slot):
+        return pltpu.make_async_copy(blocks_ref.at[level, slot], slots.at[slot], arrived.at[slot])
+
+    for slot in range(slot_count):
+        pl.when(slot < count)(fetch(slot).start)
     total[...] = jnp.zeros_like(total)
 
     def add(slot, carry):
-        below = source_ref[level, slot] ^ place_ref[0]
-        above = target_ref[level, slot] ^ place_ref[1]
-        pair = below * n_col + above
-        total[pair] += blocks_ref[0, slot]
+        fetch(slot).wait()
+        above = target_ref[level, slot] ^ place_ref[0]
+        total[source_ref[level, slot] * n_col + above] += slots[slot]
         return carry
 
-    lax.fori_loop(0, count_ref[level], add, 0)
+    lax.fori_loop(0, count, add, 0)
     for pair in range(total.shape[0]):
         rows = pl.ds(pair // n_col * block, block)
         lanes = pl.ds(pair % n_col * block, block)
@@ -49,100 +56,201 @@
         low_ref[rows, lanes] = low
 
 
-def gather_blocks(level, target, source, count, place, blocks, n_row, n_col):
+def gather_blocks(level, target, source, count, place, blocks, n_row, n_col, after):
     slot_count, block = blocks.shape[1], blocks.shape[2]
     shape = (n_row * block, n_col * block)
     scalars = pl.BlockSpec(memory_space=SMEM)
-    whole = pl.BlockSpec(shape, lambda i: (0, 0))
+    whole = pl.BlockSpec(memory_space=VMEM)
     return pl.pallas_call(
         functools.partial(gather_blocks_kernel, n_col, level),
-        grid=(1,),
         out_shape=[jax.ShapeDtypeStruct(shape, jnp.bfloat16)] * 2,
         in_specs=[scalars] * 4
-        + [pl.BlockSpec((1, slot_count, block, block), lambda i: (level, 0, 0, 0))],
+        + [pl.BlockSpec(memory_space=pltpu.MemorySpace.HBM)]
+        + [pl.BlockSpec(memory_space=pl.ANY)] * len(after),
         out_specs=[whole, whole],
-        scratch_shapes=[pltpu.VMEM((n_row * n_col, block, block), jnp.float32)],
-        compiler_params=pltpu.CompilerParams(vmem_limit_bytes=16 * MIB),
+        scratch_shapes=[
+            pltpu.VMEM((slot_count, block, block), jnp.float32),
+            pltpu.VMEM((n_row * n_col, block, block), jnp.float32),
+            pltpu.SemaphoreType.DMA((slot_count,)),
+        ],
+        compiler_params=pltpu.CompilerParams(vmem_limit_bytes=(16 if after else 51) * MIB),
         cost_estimate=pl.CostEstimate(
             flops=2 * shape[0] * shape[1], bytes_accessed=8 * shape[0] * shape[1], transcendentals=0
         ),
         name=f"gather_blocks_{level}",
-    )(target, source, count, place, blocks)
-
-
-def couple_kernel(transposed, n_in, high_ref, low_ref, *refs):
+    )(target, source, count, place, blocks, *after)
+
+
+def read(term, refs):
+    number, place = term
+    return refs[number][...] if place is None else refs[number][place]
+
+
+def total_of(terms, refs):
+    value = read(terms[0], refs)
+    for term in terms[1:]:
+        value += read(term, refs)
+    return value
+
+
+def write(ref, values):
+    if len(ref.shape) == 2:
+        ref[...] = values[0]
+    else:
+        for place, value in enumerate(values):
+            ref[place] = value
+
+
+class Operands:
+    def __init__(self):
+        self.arrays = []
+
+    def term(self, piece):
+        array, place = piece
+        for number, known in enumerate(self.arrays):
+            if known is array:
+                return number, place
+        self.arrays.append(array)
+        return len(self.arrays) - 1, place
+
+
+def couple_kernel(transposed, terms, high_ref, low_ref, *refs):
+    n_in = 1 + max(number for number, _ in terms)
     ins, outs = refs[:n_in], refs[n_in:]
     block = ins[0].shape[-1]
-    joined = jnp.concatenate([ref[...] for ref in ins], axis=1)
+    joined = jnp.concatenate([read(term, ins) for term in terms], axis=1)
     result = product(halves(joined), (high_ref[...], low_ref[...]), transposed)
-    for place, ref in enumerate(outs):
-        ref[...] = result[:, place * block : (place + 1) * block]
-
-
-def couple(segments, high, low, transposed):
-    n_out = high.shape[0 if transposed else 1] // segments[0].shape[1]
-    n_in = len(segments)
-    rows, block = segments[0].shape
+    pieces = [result[:, at : at + block] for at in range(0, result.shape[1], block)]
+    if len(outs) == 1:
+        write(outs[0], pieces)
+    else:
+        for ref, piece in zip(outs, pieces):
+            ref[...] = piece
+
+
+def couple(pieces, high, low, transposed):
+    operands = Operands()
+    terms = [operands.term(piece) for piece in pieces]
+    rows, block = operands.arrays[0].shape[-2:]
+    n_out = high.shape[0 if transposed else 1] // block
+    shapes = [(n_out, rows, block)] if transposed else [(rows, block)] * n_out
     whole = pl.BlockSpec(memory_space=VMEM)
     return pl.pallas_call(
-        functools.partial(couple_kernel, transposed, n_in),
-        out_shape=[jax.ShapeDtypeStruct((rows, block), jnp.float32)] * n_out,
-        in_specs=[whole] * (n_in + 2),
-        out_specs=[whole] * n_out,
+        functools.partial(couple_kernel, transposed, terms),
+        out_shape=[jax.ShapeDtypeStruct(shape, jnp.float32) for shape in shapes],
+        in_specs=[whole] * (2 + len(operands.arrays)),
+        out_specs=[whole] * len(shapes),
         compiler_params=pltpu.CompilerParams(vmem_limit_bytes=16 * MIB),
         cost_estimate=pl.CostEstimate(
             flops=6 * rows * high.size, bytes_accessed=4 * high.size, transcendentals=0
         ),
         name="couple_up" if not transposed else "couple_down",
-    )(high, low, *segments)
-
-
-def solve_kernel(transposed, right_ref, inverse_ref, *refs):
-    parts, out_ref = refs[:-1], refs[-1]
-    value = right_ref[...].reshape(out_ref.shape)
-    if parts:
-        summed = parts[0][...]
-        for part in parts[1:]:
-            summed += part[...]
-        value -= summed
-    inverse = inverse_ref[...].reshape(inverse_ref.shape[-2:])
-    out_ref[...] = product(halves(value), halves(inverse), transposed)
-
-
-def solve(right, inverse, level, parts, transposed):
+    )(high, low, *operands.arrays)
+
+
+def first_solve_kernel(right_ref, inverse_ref, out_ref, copies_ref, right, inverse, arrived):
+    fetches = [
+        pltpu.make_async_copy(right_ref.at[0], right, arrived.at[0]),
+        pltpu.make_async_copy(inverse_ref.at[0], inverse, arrived.at[1]),
+    ]
+    for fetch in fetches:
+        fetch.start()
+    for fetch in fetches:
+        fetch.wait()
+    result = product(halves(right[...]), halves(inverse[...]), False)
+    out_ref[...] = result
+    write(copies_ref, [result] * copies_ref.shape[0])
+
+
+def first_solve(right, inverse, n_copies):
     rows, block = right.shape[-2:]
-    at_level = lambda shape: pl.BlockSpec((1,) + shape, lambda i: (level, 0, 0))
-    plain = pl.BlockSpec((rows, block), lambda i: (0, 0))
+    whole = pl.BlockSpec(memory_space=VMEM)
     return pl.pallas_call(
-        functools.partial(solve_kernel, transposed),
-        grid=(1,),
-        out_shape=jax.ShapeDtypeStruct((rows, block), jnp.float32),
-        in_specs=[
-            at_level((rows, block)) if right.ndim == 3 else plain,
-            at_level((block, block)),
-        ]
-        + [plain] * len(parts),
-        out_specs=plain,
+        first_solve_kernel,
+        out_shape=[
+            jax.ShapeDtypeStruct((rows, block), jnp.float32),
+            jax.ShapeDtypeStruct((n_copies, rows, block), jnp.float32),
+        ],
+        in_specs=[pl.BlockSpec(memory_space=pl.ANY)] * 2,
+        out_specs=[whole] * 2,
+        scratch_shapes=[
+            pltpu.VMEM((rows, block), jnp.float32),
+            pltpu.VMEM((block, block), jnp.float32),
+            pltpu.SemaphoreType.DMA((2,)),
+        ],
+        compiler_params=pltpu.CompilerParams(vmem_limit_bytes=60 * MIB),
+        name="first_solve",
+    )(right, inverse)
+
+
+def solve_kernel(transposed, level, terms, n_ins, n_copies, *refs):
+    right_ref, inverse_ref = refs[:2]
+    ins = refs[2 : 2 + n_ins]
+    outs = refs[-2:] if n_copies else refs[-1:]
+    value = right_ref[level] if len(right_ref.shape) == 3 else right_ref[...]
+    if terms:
+        value -= total_of(terms, ins)
+    result = product(halves(value), halves(inverse_ref[level]), transposed)
+    outs[0][...] = result
+    if n_copies:
+        write(outs[1], [result] * n_copies)
+
+
+def solve(right, inverse, level, pieces, transposed, n_copies=0, after=()):
+    rows, block = right.shape[-2:]
+    operands = Operands()
+    terms = [operands.term(piece) for piece in pieces]
+    whole = pl.BlockSpec(memory_space=VMEM)
+    out_shape = [jax.ShapeDtypeStruct((rows, block), jnp.float32)]
+    if n_copies:
+        out_shape.append(jax.ShapeDtypeStruct((n_copies, rows, block), jnp.float32))
+    return pl.pallas_call(
+        functools.partial(
+            solve_kernel, transposed, level, terms, len(operands.arrays), n_copies
+        ),
+        out_shape=out_shape,
+        in_specs=[whole] * (2 + len(operands.arrays))
+        + [pl.BlockSpec(memory_space=pl.ANY)] * len(after),
+        out_specs=[whole] * len(out_shape),
         compiler_params=pltpu.CompilerParams(vmem_limit_bytes=8 * MIB),
         cost_estimate=pl.CostEstimate(
             flops=6 * rows * block * block, bytes_accessed=4 * block * block, transcendentals=0
         ),
         name="solve_up" if not transposed else "solve_down",
-    )(right, inverse, *parts)
-
-
-def spread(segment, axis):
+    )(right, inverse, *operands.arrays, *after)
+
+
+def stack_kernel(n_forward, *refs):
+    ins, (forward_ref, backward_ref) = refs[:-2], refs[-2:]
+    write(forward_ref, [ref[...] for ref in ins[:n_forward]])
+    write(backward_ref, [ref[...] for ref in ins[n_forward:]])
+
+
+def stack(forward, backward):
+    whole = pl.BlockSpec(memory_space=VMEM)
+    shape = jax.ShapeDtypeStruct((len(forward),) + forward[0].shape, jnp.float32)
+    return pl.pallas_call(
+        functools.partial(stack_kernel, len(forward)),
+        out_shape=[shape, shape],
+        in_specs=[whole] * (2 * len(forward)),
+        out_specs=[whole] * 2,
+        compiler_params=pltpu.CompilerParams(vmem_limit_bytes=8 * MIB),
+        name="stack",
+    )(*forward, *backward)
+
+
+def exchange_all(stacked, axis):
+    received = lax.all_to_all(stacked, axis, 0, 0, tiled=True)
+    return [(received, place) for place in range(stacked.shape[0])]
+
+
+def exchange_each(messages, axis):
     size = lax.axis_size(axis)
-    return [segment] + [
-        lax.ppermute(segment, axis, [(i, i ^ d) for i in range(size)]) for d in range(1, size)
+    received = [messages[0]] + [
+        lax.ppermute(messages[d], axis, [(i, i ^ d) for i in range(size)])
+        for d in range(1, size)
     ]
-
-
-def deliver(parts, axis):
-    size = lax.axis_size(axis)
-    return [parts[0]] + [
-        lax.ppermute(parts[d], axis, [(i, i ^ d) for i in range(size)]) for d in range(1, size)
-    ]
+    return [(message, None) for message in received]
 
 
 def direct_shards(rhs, diag_inv, blocks, blk_target, blk_source, blk_count):
@@ -154,24 +262,32 @@
     target = blk_target.reshape(levels - 1, -1)
     source = blk_source.reshape(levels - 1, -1)
     count = blk_count.reshape(levels - 1)
-    place = jnp.stack([lax.axis_index("row"), lax.axis_index("col")]).astype(jnp.int32)
-    coupling = [
-        gather_blocks(level, target, source, count, place, weights, n_row, n_col)
-        for level in range(levels - 1)
-    ]
-    forward = [solve(right, inverse, 0, [], False)]
+    place = lax.axis_index("col").astype(jnp.int32).reshape(1)
+    gather = lambda level, after: gather_blocks(
+        level, target, source, count, place, weights, n_row, n_col, after
+    )
+    first, copies = first_solve(right, inverse, n_row)
+    coupling = [gather(0, ())]
+    forward = [first]
     for level in range(1, levels):
-        partial = couple(spread(forward[-1], "row"), *coupling[level - 1], False)
-        forward.append(solve(right, inverse, level, deliver(partial, "col"), False))
+        partial = couple(exchange_all(copies, "row"), *coupling[level - 1], False)
+        last = level == levels - 1
+        if not last:
+            coupling.append(gather(level, (partial[0],)))
+        after = () if last else coupling[level][:1]
+        pieces = exchange_each(partial, "col")
+        solved = solve(right, inverse, level, pieces, False, 0 if last else n_row, after)
+        forward.append(solved[0])
+        copies = solved[-1]
     backward = [None] * levels
-    backward[-1] = solve(forward[-1], inverse, levels - 1, [], True)
+    (backward[-1],) = solve(forward[-1], inverse, levels - 1, [], True)
     for level in range(levels - 2, -1, -1):
-        partial = couple(spread(backward[level + 1], "col"), *coupling[level], True)
-        backward[level] = solve(forward[level], inverse, level, deliver(partial, "row"), True)
-    return (
-        jnp.stack(forward).reshape(rhs.shape),
-        jnp.stack(backward).reshape(rhs.shape),
-    )
+        pieces = exchange_each([backward[level + 1]] * n_col, "col")
+        (partial,) = couple(pieces, *coupling[level], True)
+        pieces = exchange_all(partial, "row")
+        (backward[level],) = solve(forward[level], inverse, level, pieces, True)
+    outs = stack(forward, backward)
+    return tuple(out.reshape(rhs.shape) for out in outs)
 
 
 def fold_for(index, piece):

time: 221 us -> 201 us (0.910)
  blocking collectives: 0 us -> 114 us
  starting transfers between devices: 133 us -> 26.6 us
  waiting for transfers between devices: 61.4 us -> 20.2 us
  Pallas kernels: 17.2 us -> 29.7 us
    all_to_all x0 -> x9, blocking collectives: none -> 114 us  [exchange_all(): received = lax.all_to_all(stacked, axis, 0, 0, tiled=True)]
    ppermute x100 -> x30, starting transfers between devices: 133 us -> 19.3 us  [exchange_each(): lax.ppermute(messages[d], axis, [(i, i ^ d) for i in range(size)])]
    ppermute x100 -> x30, waiting for transfers between devices: 61.4 us -> 15.1 us  [exchange_each(): lax.ppermute(messages[d], axis, [(i, i ^ d) for i in range(size)])]
    pallas_call x27 -> x28, Pallas kernels: 17.2 us -> 29.7 us  [the longest x5 16.8 us: gather_blocks(): pl.pallas_call(functools.partial(gather_blocks_kernel, n_col, level), out...]
    all_to_all x0 -> x1, starting transfers between devices: none -> 7.29 us  [exchange_all(): received = lax.all_to_all(stacked, axis, 0, 0, tiled=True)]
    all_to_all x0 -> x1, waiting for transfers between devices: none -> 5.05 us  [exchange_all(): received = lax.all_to_all(stacked, axis, 0, 0, tiled=True)]
    unnamed x29 -> x21, local copies, waits for them, and re-layouts: 7.99 us -> 9.34 us
  transfers between devices with their start and end apart: 100 -> 31, of which waited for: 40 -> 12; matrix products, arithmetic and copies ran while one was open for 0% -> 0% of each run, Pallas kernels for 3% -> 8%
where the time goes in v4:
time: 201 us
  blocking collectives  114 us (57%)
  Pallas kernels  29.7 us (15%)
  starting transfers between devices  26.6 us (13%)
  waiting for transfers between devices  20.2 us (10%)
  local copies, waits for them, and re-layouts  9.34 us (5%)
    all_to_all x9, blocking collectives, exchange_all(): received = lax.all_to_all(stacked, axis, 0, 0, tiled=True)  114 us
    ppermute x30, starting transfers between devices, exchange_each(): lax.ppermute(messages[d], axis, [(i, i ^ d) for i in range(size)])  19.3 us
    pallas_call x5, Pallas kernels, gather_blocks(): pl.pallas_call(functools.partial(gather_blocks_kernel, n_col, level), out...  16.8 us
    ppermute x30, waiting for transfers between devices, exchange_each(): lax.ppermute(messages[d], axis, [(i, i ^ d) for i in range(size)])  15.1 us
    unnamed x21, local copies, waits for them, and re-layouts  9.34 us
    pallas_call x10, Pallas kernels, couple(): pl.pallas_call(functools.partial(couple_kernel, transposed, terms), out_s...  8.51 us
    all_to_all x1, starting transfers between devices, exchange_all(): received = lax.all_to_all(stacked, axis, 0, 0, tiled=True)  7.29 us
    all_to_all x1, waiting for transfers between devices, exchange_all(): received = lax.all_to_all(stacked, axis, 0, 0, tiled=True)  5.05 us
  transfers between devices with their start and end apart: 31, of which 12 were waited for; matrix products, arithmetic and copies ran while one was open for 0% of the time, Pallas kernels for 8%

profile of v4, /device:TPU:0, one launch (start us, length us, event | category | flops | bytes accessed | tf_op | source)
XLA Modules:
  0.0 200.9 jit_solution(4541410835596089765)
XLA Ops:
  0.6 1.8 first_solve.1
  2.4 7.3 %all-to-all-start = ((f32[8,64,128]{2,1,0:T(8,128)}), f32[8,64,128]{2,1,0:T(8,128)S(1)}, u32[]{:S(2)}, u32[]{:S(2)}) async-start(f32[8,64,128]{2,1,0:T(8,128)} %get-tuple-element.47), calls=%async_computation | async-start | bytes 524288 | tf_op jit(solution)/shard_map/all_to_all | solution.py:243
  9.7 0.7 copy_bitcast_fusion
  10.4 0.7 copy-done.5
  11.1 2.5 %gather_blocks_0.1 = (bf16[1024,512]{1,0:T(8,128)(2,1)S(1)}, bf16[1024,512]{1,0:T(8,128)(2,1)S(1)}) custom-call(s32[5,32]{1,0:T(8,128)S(1)} %get-tuple-element.89.target_ref, s32[5,32]{1,0:T(8,128)S(1)} %get-tuple-element.88.source_ref, s32[5]{0:T(128)S(1)} %bitcast.40, s32[1]{0:T(128)} %bitcast.3.place_ref, f32[5,32,128,128]{3,2,1,0:T(8,128)} %bitcast.15), custom_call_target="tpu_custom_call" | custom-call | flops 1048576 | bytes 4194304 | tf_op jit(solution)/shard_map/gather_blocks_0/pallas_call | solution.py:64
  13.6 5.1 %all-to-all-done.refs_0_ = f32[8,64,128]{2,1,0:T(8,128)S(1)} async-done(((f32[8,64,128]{2,1,0:T(8,128)}), f32[8,64,128]{2,1,0:T(8,128)S(1)}, u32[]{:S(2)}, u32[]{:S(2)}) %all-to-all-start) | async-done | bytes 262176 | tf_op jit(solution)/shard_map/all_to_all | solution.py:243
  18.6 0.6 couple_up.5
  19.4 1.6 collective-permute-start.1
  20.9 0.3 collective-permute-start.2
  21.2 4.0 %copy-done = f32[5,1,1,32,128,128]{5,4,3,2,1,0:T(8,128)S(1)} copy-done((f32[5,1,1,32,128,128]{5,4,3,2,1,0:T(8,128)S(1)}, f32[5,1,1,32,128,128]{5,4,3,2,1,0:T(8,128)}, u32[]{:S(2)}) %copy-start) | copy-done | bytes 10485784
  25.2 3.1 %gather_blocks_1.1 = (bf16[1024,512]{1,0:T(8,128)(2,1)S(1)}, bf16[1024,512]{1,0:T(8,128)(2,1)S(1)}) custom-call(s32[5,32]{1,0:T(8,128)S(1)} %get-tuple-element.89.target_ref, s32[5,32]{1,0:T(8,128)S(1)} %get-tuple-element.88.source_ref, s32[5]{0:T(128)S(1)} %bitcast.41, s32[1]{0:T(128)} %bitcast.3.place_ref, f32[5,32,128,128]{3,2,1,0:T(8,128)S(1)} %bitcast.16, ...), custom_call_target="tpu_custom_call" | custom-call | flops 1048576 | bytes 4194304 | tf_op jit(solution)/shard_map/gather_blocks_1/pallas_call | solution.py:64
  28.3 0.2 solve_up.5
  28.5 13.9 %all_to_all.50.refs_0_ = f32[8,64,128]{2,1,0:T(8,128)S(1)} all-to-all(f32[8,64,128]{2,1,0:T(8,128)S(1)} %get-tuple-element.55), channel_id=1, replica_groups=mesh['row'=8,'col'=4] {'row'}, dimensions={0} | all-to-all | bytes 524288 | tf_op jit(solution)/shard_map/all_to_all | solution.py:243
  42.4 0.6 couple_up.6
  43.0 0.2 collective-permute-start.3
  43.2 0.3 collective-permute-start.4
  43.5 1.5 collective-permute-start.5
  45.0 4.0 %copy-done.1 = f32[5,1,1,32,128,128]{5,4,3,2,1,0:T(8,128)S(1)} copy-done((f32[5,1,1,32,128,128]{5,4,3,2,1,0:T(8,128)S(1)}, f32[5,1,1,32,128,128]{5,4,3,2,1,0:T(8,128)}, u32[]{:S(2)}) %copy-start.1) | copy-done | bytes 10485784
  49.0 3.6 %gather_blocks_2.1 = (bf16[1024,512]{1,0:T(8,128)(2,1)S(1)}, bf16[1024,512]{1,0:T(8,128)(2,1)S(1)}) custom-call(s32[5,32]{1,0:T(8,128)S(1)} %get-tuple-element.89.target_ref, s32[5,32]{1,0:T(8,128)S(1)} %get-tuple-element.88.source_ref, s32[5]{0:T(128)S(1)} %bitcast.42, s32[1]{0:T(128)} %bitcast.3.place_ref, f32[5,32,128,128]{3,2,1,0:T(8,128)S(1)} %bitcast.17, ...), custom_call_target="tpu_custom_call" | custom-call | flops 1048576 | bytes 4194304 | tf_op jit(solution)/shard_map/gather_blocks_2/pallas_call | solution.py:64
  52.7 0.2 solve_up.6
  52.8 13.0 %all_to_all.51.refs_0_ = f32[8,64,128]{2,1,0:T(8,128)S(1)} all-to-all(f32[8,64,128]{2,1,0:T(8,128)S(1)} %get-tuple-element.63), channel_id=1, replica_groups=mesh['row'=8,'col'=4] {'row'}, dimensions={0} | all-to-all | bytes 524288 | tf_op jit(solution)/shard_map/all_to_all | solution.py:243
  65.9 0.6 couple_up.7
  66.7 1.8 collective-permute-start.8
  68.5 2.9 %gather_blocks_3.1 = (bf16[1024,512]{1,0:T(8,128)(2,1)S(1)}, bf16[1024,512]{1,0:T(8,128)(2,1)S(1)}) custom-call(s32[5,32]{1,0:T(8,128)S(1)} %get-tuple-element.89.target_ref, s32[5,32]{1,0:T(8,128)S(1)} %get-tuple-element.88.source_ref, s32[5]{0:T(128)S(1)} %bitcast.43, s32[1]{0:T(128)} %bitcast.3.place_ref, f32[5,32,128,128]{3,2,1,0:T(8,128)S(1)} %bitcast.20, ...), custom_call_target="tpu_custom_call" | custom-call | flops 1048576 | bytes 4194304 | tf_op jit(solution)/shard_map/gather_blocks_3/pallas_call | solution.py:64
  71.6 13.5 %all_to_all.52.refs_0_ = f32[8,64,128]{2,1,0:T(8,128)S(1)} all-to-all(f32[8,64,128]{2,1,0:T(8,128)S(1)} %get-tuple-element.71), channel_id=1, replica_groups=mesh['row'=8,'col'=4] {'row'}, dimensions={0} | all-to-all | bytes 524288 | tf_op jit(solution)/shard_map/all_to_all | solution.py:243
  85.1 0.6 couple_up.8
  85.9 1.8 collective-permute-start.11
  87.7 4.7 %gather_blocks_4.1 = (bf16[1024,512]{1,0:T(8,128)(2,1)S(1)}, bf16[1024,512]{1,0:T(8,128)(2,1)S(1)}) custom-call(s32[5,32]{1,0:T(8,128)S(1)} %get-tuple-element.89.target_ref, s32[5,32]{1,0:T(8,128)S(1)} %get-tuple-element.88.source_ref, s32[5]{0:T(128)S(1)} %bitcast.44, s32[1]{0:T(128)} %bitcast.3.place_ref, f32[5,32,128,128]{3,2,1,0:T(8,128)S(1)} %bitcast.21, ...), custom_call_target="tpu_custom_call" | custom-call | flops 1048576 | bytes 4194304 | tf_op jit(solution)/shard_map/gather_blocks_4/pallas_call | solution.py:64
  92.5 0.2 solve_up.8
  92.6 11.6 %all_to_all.53.refs_0_ = f32[8,64,128]{2,1,0:T(8,128)S(1)} all-to-all(f32[8,64,128]{2,1,0:T(8,128)S(1)} %get-tuple-element.79), channel_id=1, replica_groups=mesh['row'=8,'col'=4] {'row'}, dimensions={0} | all-to-all | bytes 524288 | tf_op jit(solution)/shard_map/all_to_all | solution.py:243
  104.2 0.6 couple_up.9
  105.0 1.8 collective-permute-start.14
  106.8 2.3 %collective-permute-done.13.refs_4_ = f32[64,128]{1,0:T(8,128)S(1)} collective-permute-done((f32[64,128]{1,0:T(8,128)S(1)}, f32[64,128]{1,0:T(8,128)S(1)}, u32[]{:S(2)}, u32[]{:S(2)}) %collective-permute-start.13) | collective-permute-done | bytes 32800 | tf_op jit(solution)/shard_map/ppermute | solution.py:250
  109.4 1.1 collective-permute-start.17
  110.5 0.8 collective-permute-start.16
  111.3 1.5 collective-permute-done.17.refs_3_
  112.8 1.6 collective-permute-done.16.refs_2_
  114.5 1.1 couple_down.5
  115.5 11.8 %all_to_all.54.refs_2_ = f32[8,64,128]{2,1,0:T(8,128)S(1)} all-to-all(f32[8,64,128]{2,1,0:T(8,128)S(1)} %couple_down.5), channel_id=1, replica_groups=mesh['row'=8,'col'=4] {'row'}, dimensions={0} | all-to-all | bytes 524288 | tf_op jit(solution)/shard_map/all_to_all | solution.py:243
  127.6 0.9 collective-permute-start.19
  128.5 0.9 collective-permute-start.18
  129.4 1.5 collective-permute-done.20.refs_3_
  130.9 0.9 collective-permute-done.19.refs_2_
  131.8 1.1 couple_down.6
  132.9 12.5 %all_to_all.55.refs_2_ = f32[8,64,128]{2,1,0:T(8,128)S(1)} all-to-all(f32[8,64,128]{2,1,0:T(8,128)S(1)} %couple_down.6), channel_id=1, replica_groups=mesh['row'=8,'col'=4] {'row'}, dimensions={0} | all-to-all | bytes 524288 | tf_op jit(solution)/shard_map/all_to_all | solution.py:243
  145.6 1.0 collective-permute-start.22
  146.6 0.9 collective-permute-start.21
  147.4 1.5 collective-permute-done.23.refs_3_
  148.9 1.0 collective-permute-done.22.refs_2_
  149.9 1.1 couple_down.7
  151.0 12.6 %all_to_all.56.refs_2_ = f32[8,64,128]{2,1,0:T(8,128)S(1)} all-to-all(f32[8,64,128]{2,1,0:T(8,128)S(1)} %couple_down.7), channel_id=1, replica_groups=mesh['row'=8,'col'=4] {'row'}, dimensions={0} | all-to-all | bytes 524288 | tf_op jit(solution)/shard_map/all_to_all | solution.py:243
  163.8 1.1 collective-permute-start.25
  164.9 0.8 collective-permute-start.24
  165.6 1.5 collective-permute-done.26.refs_3_
  167.1 0.9 collective-permute-done.25.refs_2_
  168.1 1.1 couple_down.8
  169.1 12.6 %all_to_all.57.refs_2_ = f32[8,64,128]{2,1,0:T(8,128)S(1)} all-to-all(f32[8,64,128]{2,1,0:T(8,128)S(1)} %couple_down.8), channel_id=1, replica_groups=mesh['row'=8,'col'=4] {'row'}, dimensions={0} | all-to-all | bytes 524288 | tf_op jit(solution)/shard_map/all_to_all | solution.py:243
  182.0 1.1 collective-permute-start.28
  183.1 0.8 collective-permute-start.27
  183.8 1.5 collective-permute-done.29.refs_3_
  185.3 0.9 collective-permute-done.28.refs_2_
  186.2 1.1 couple_down.9
  187.3 12.7 %all_to_all.58.refs_2_ = f32[8,64,128]{2,1,0:T(8,128)S(1)} all-to-all(f32[8,64,128]{2,1,0:T(8,128)S(1)} %couple_down.9), channel_id=1, replica_groups=mesh['row'=8,'col'=4] {'row'}, dimensions={0} | all-to-all | bytes 524288 | tf_op jit(solution)/shard_map/all_to_all | solution.py:243
  200.1 0.8 stack.1
  (57 shorter events, 2.2 us)
Async XLA Ops:
  0.6 20.6 %copy-start.6 = (s32[5,1,1]{0,2,1:T(1,128)S(1)}, s32[5,1,1]{0,2,1:T(1,128)}, u32[]{:S(2)}) copy-start(s32[5,1,1]{0,2,1:T(1,128)} %param.11) | copy-start | bytes 64
  2.4 16.2 %all-to-all-start = ((f32[8,64,128]{2,1,0:T(8,128)}), f32[8,64,128]{2,1,0:T(8,128)S(1)}, u32[]{:S(2)}, u32[]{:S(2)}) async-start(f32[8,64,128]{2,1,0:T(8,128)} %get-tuple-element.47), calls=%async_computation | async-start | bytes 524288 | tf_op jit(solution)/shard_map/all_to_all | solution.py:243
  10.4 0.7 copy-start.5
  11.1 17.2 %copy-start.2 = (f32[6,1,1,1,128,128]{5,4,3,2,1,0:T(8,128)S(1)}, f32[6,1,1,1,128,128]{5,4,3,2,1,0:T(8,128)}, u32[]{:S(2)}) copy-start(f32[6,1,1,1,128,128]{5,4,3,2,1,0:T(8,128)} %param.7) | copy-start | bytes 1179652
  11.1 17.2 %copy-start.3 = (f32[6,1,1,1,64,128]{5,4,3,2,1,0:T(8,128)S(1)}, f32[6,1,1,1,64,128]{5,4,3,2,1,0:T(8,128)}, u32[]{:S(2)}) copy-start(f32[6,1,1,1,64,128]{5,4,3,2,1,0:T(8,128)} %param.6) | copy-start | bytes 589828
  19.3 9.0 %collective-permute-start = (f32[64,128]{1,0:T(8,128)S(1)}, f32[64,128]{1,0:T(8,128)S(1)}, u32[]{:S(2)}, u32[]{:S(2)}) collective-permute-start(f32[64,128]{1,0:T(8,128)S(1)} %get-tuple-element.49), channel_id=1, source_target_pairs={{0,1},{1,0},{2,3},{3,2},{4,5},{5,4},{6,7},{7,6},{8,9},{9,8},{10,11... | collective-permute-start | bytes 98312 | tf_op jit(solution)/shard_map/ppermute | solution.py:250
  19.4 8.9 %collective-permute-start.1 = (f32[64,128]{1,0:T(8,128)S(1)}, f32[64,128]{1,0:T(8,128)S(1)}, u32[]{:S(2)}, u32[]{:S(2)}) collective-permute-start(f32[64,128]{1,0:T(8,128)S(1)} %get-tuple-element.50), channel_id=1, source_target_pairs={{0,2},{1,3},{2,0},{3,1},{4,6},{5,7},{6,4},{7,5},{8,10},{9,11},{10,... | collective-permute-start | bytes 98312 | tf_op jit(solution)/shard_map/ppermute | solution.py:250
  20.9 7.4 %collective-permute-start.2 = (f32[64,128]{1,0:T(8,128)S(1)}, f32[64,128]{1,0:T(8,128)S(1)}, u32[]{:S(2)}, u32[]{:S(2)}) collective-permute-start(f32[64,128]{1,0:T(8,128)S(1)} %get-tuple-element.51), channel_id=1, source_target_pairs={{0,3},{1,2},{2,1},{3,0},{4,7},{5,6},{6,5},{7,4},{8,11},{9,10},{10,... | collective-permute-start | bytes 98312 | tf_op jit(solution)/shard_map/ppermute | solution.py:250
  21.2 4.0 %copy-start = (f32[5,1,1,32,128,128]{5,4,3,2,1,0:T(8,128)S(1)}, f32[5,1,1,32,128,128]{5,4,3,2,1,0:T(8,128)}, u32[]{:S(2)}) copy-start(f32[5,1,1,32,128,128]{5,4,3,2,1,0:T(8,128)} %param.8) | copy-start | bytes 31457284
  25.2 43.3 %slice-start = ((s8[10485760]{0:T(1024)(128)(4,1)}), s8[4194304]{0:T(1024)(128)(4,1)S(1)}, s32[]{:S(2)}) async-start(s8[10485760]{0:T(1024)(128)(4,1)} %bitcast.18), calls=%async_computation.10 | async-start | bytes 8388608
  25.2 43.3 %slice-start.1 = ((s8[10485760]{0:T(1024)(128)(4,1)}), s8[4194304]{0:T(1024)(128)(4,1)S(1)}, s32[]{:S(2)}) async-start(s8[10485760]{0:T(1024)(128)(4,1)} %bitcast.18), calls=%async_computation.11 | async-start | bytes 8388608
  43.0 9.6 %collective-permute-start.3 = (f32[64,128]{1,0:T(8,128)S(1)}, f32[64,128]{1,0:T(8,128)S(1)}, u32[]{:S(2)}, u32[]{:S(2)}) collective-permute-start(f32[64,128]{1,0:T(8,128)S(1)} %get-tuple-element.57), channel_id=1, source_target_pairs={{0,1},{1,0},{2,3},{3,2},{4,5},{5,4},{6,7},{7,6},{8,9},{9,8},{10,11... | collective-permute-start | bytes 98312 | tf_op jit(solution)/shard_map/ppermute | solution.py:250
  43.2 9.4 %collective-permute-start.4 = (f32[64,128]{1,0:T(8,128)S(1)}, f32[64,128]{1,0:T(8,128)S(1)}, u32[]{:S(2)}, u32[]{:S(2)}) collective-permute-start(f32[64,128]{1,0:T(8,128)S(1)} %get-tuple-element.58), channel_id=1, source_target_pairs={{0,2},{1,3},{2,0},{3,1},{4,6},{5,7},{6,4},{7,5},{8,10},{9,11},{10,... | collective-permute-start | bytes 98312 | tf_op jit(solution)/shard_map/ppermute | solution.py:250
  43.5 9.1 %collective-permute-start.5 = (f32[64,128]{1,0:T(8,128)S(1)}, f32[64,128]{1,0:T(8,128)S(1)}, u32[]{:S(2)}, u32[]{:S(2)}) collective-permute-start(f32[64,128]{1,0:T(8,128)S(1)} %get-tuple-element.59), channel_id=1, source_target_pairs={{0,3},{1,2},{2,1},{3,0},{4,7},{5,6},{6,5},{7,4},{8,11},{9,10},{10,... | collective-permute-start | bytes 98312 | tf_op jit(solution)/shard_map/ppermute | solution.py:250
  45.0 4.0 %copy-start.1 = (f32[5,1,1,32,128,128]{5,4,3,2,1,0:T(8,128)S(1)}, f32[5,1,1,32,128,128]{5,4,3,2,1,0:T(8,128)}, u32[]{:S(2)}) copy-start(f32[5,1,1,32,128,128]{5,4,3,2,1,0:T(8,128)} %param.8) | copy-start | bytes 31457284
  49.0 19.5 %slice-start.2 = ((s8[10485760]{0:T(1024)(128)(4,1)}), s8[2097152]{0:T(1024)(128)(4,1)S(1)}, s32[]{:S(2)}) async-start(s8[10485760]{0:T(1024)(128)(4,1)} %bitcast.18), calls=%async_computation.12 | async-start | bytes 4194304
  66.5 4.8 %collective-permute-start.6 = (f32[64,128]{1,0:T(8,128)S(1)}, f32[64,128]{1,0:T(8,128)S(1)}, u32[]{:S(2)}, u32[]{:S(2)}) collective-permute-start(f32[64,128]{1,0:T(8,128)S(1)} %get-tuple-element.65), channel_id=1, source_target_pairs={{0,1},{1,0},{2,3},{3,2},{4,5},{5,4},{6,7},{7,6},{8,9},{9,8},{10,11... | collective-permute-start | bytes 98312 | tf_op jit(solution)/shard_map/ppermute | solution.py:250
  66.6 4.8 %collective-permute-start.7 = (f32[64,128]{1,0:T(8,128)S(1)}, f32[64,128]{1,0:T(8,128)S(1)}, u32[]{:S(2)}, u32[]{:S(2)}) collective-permute-start(f32[64,128]{1,0:T(8,128)S(1)} %get-tuple-element.66), channel_id=1, source_target_pairs={{0,2},{1,3},{2,0},{3,1},{4,6},{5,7},{6,4},{7,5},{8,10},{9,11},{10,... | collective-permute-start | bytes 98312 | tf_op jit(solution)/shard_map/ppermute | solution.py:250
  66.7 4.7 %collective-permute-start.8 = (f32[64,128]{1,0:T(8,128)S(1)}, f32[64,128]{1,0:T(8,128)S(1)}, u32[]{:S(2)}, u32[]{:S(2)}) collective-permute-start(f32[64,128]{1,0:T(8,128)S(1)} %get-tuple-element.67), channel_id=1, source_target_pairs={{0,3},{1,2},{2,1},{3,0},{4,7},{5,6},{6,5},{7,4},{8,11},{9,10},{10,... | collective-permute-start | bytes 98312 | tf_op jit(solution)/shard_map/ppermute | solution.py:250
  85.8 6.7 %collective-permute-start.9 = (f32[64,128]{1,0:T(8,128)S(1)}, f32[64,128]{1,0:T(8,128)S(1)}, u32[]{:S(2)}, u32[]{:S(2)}) collective-permute-start(f32[64,128]{1,0:T(8,128)S(1)} %get-tuple-element.73), channel_id=1, source_target_pairs={{0,1},{1,0},{2,3},{3,2},{4,5},{5,4},{6,7},{7,6},{8,9},{9,8},{10,11... | collective-permute-start | bytes 98312 | tf_op jit(solution)/shard_map/ppermute | solution.py:250
  85.8 6.6 %collective-permute-start.10 = (f32[64,128]{1,0:T(8,128)S(1)}, f32[64,128]{1,0:T(8,128)S(1)}, u32[]{:S(2)}, u32[]{:S(2)}) collective-permute-start(f32[64,128]{1,0:T(8,128)S(1)} %get-tuple-element.74), channel_id=1, source_target_pairs={{0,2},{1,3},{2,0},{3,1},{4,6},{5,7},{6,4},{7,5},{8,10},{9,11},{10,... | collective-permute-start | bytes 98312 | tf_op jit(solution)/shard_map/ppermute | solution.py:250
  85.9 6.5 %collective-permute-start.11 = (f32[64,128]{1,0:T(8,128)S(1)}, f32[64,128]{1,0:T(8,128)S(1)}, u32[]{:S(2)}, u32[]{:S(2)}) collective-permute-start(f32[64,128]{1,0:T(8,128)S(1)} %get-tuple-element.75), channel_id=1, source_target_pairs={{0,3},{1,2},{2,1},{3,0},{4,7},{5,6},{6,5},{7,4},{8,11},{9,10},{10,... | collective-permute-start | bytes 98312 | tf_op jit(solution)/shard_map/ppermute | solution.py:250
  104.2 95.7 %copy-start.4 = (f32[64,128]{1,0:T(8,128)S(1)}, f32[64,128]{1,0:T(8,128)}, u32[]{:S(2)}) copy-start(f32[64,128]{1,0:T(8,128)} %get-tuple-element.44.refs_0_) | copy-start | bytes 98308
  104.8 1.9 collective-permute-start.12
  104.9 4.2 %collective-permute-start.13 = (f32[64,128]{1,0:T(8,128)S(1)}, f32[64,128]{1,0:T(8,128)S(1)}, u32[]{:S(2)}, u32[]{:S(2)}) collective-permute-start(f32[64,128]{1,0:T(8,128)S(1)} %get-tuple-element.82), channel_id=1, source_target_pairs={{0,2},{1,3},{2,0},{3,1},{4,6},{5,7},{6,4},{7,5},{8,10},{9,11},{10,... | collective-permute-start | bytes 98312 | tf_op jit(solution)/shard_map/ppermute | solution.py:250
  105.0 4.1 %collective-permute-start.14 = (f32[64,128]{1,0:T(8,128)S(1)}, f32[64,128]{1,0:T(8,128)S(1)}, u32[]{:S(2)}, u32[]{:S(2)}) collective-permute-start(f32[64,128]{1,0:T(8,128)S(1)} %get-tuple-element.83), channel_id=1, source_target_pairs={{0,3},{1,2},{2,1},{3,0},{4,7},{5,6},{6,5},{7,4},{8,11},{9,10},{10,... | collective-permute-start | bytes 98312 | tf_op jit(solution)/shard_map/ppermute | solution.py:250
  109.4 3.4 %collective-permute-start.17 = (f32[64,128]{1,0:T(8,128)S(1)}, f32[64,128]{1,0:T(8,128)S(1)}, u32[]{:S(2)}, u32[]{:S(2)}) collective-permute-start(f32[64,128]{1,0:T(8,128)S(1)} %solve_down.6.refs_0_.refs_11_), channel_id=1, source_target_pairs={{0,3},{1,2},{2,1},{3,0},{4,7},{5,6},{6,5},{7,4},{8,11},{9,10},{10,... | collective-permute-start | bytes 98312 | tf_op jit(solution)/shard_map/ppermute | solution.py:250
  110.5 3.9 %collective-permute-start.16 = (f32[64,128]{1,0:T(8,128)S(1)}, f32[64,128]{1,0:T(8,128)S(1)}, u32[]{:S(2)}, u32[]{:S(2)}) collective-permute-start(f32[64,128]{1,0:T(8,128)S(1)} %solve_down.6.refs_0_.refs_11_), channel_id=1, source_target_pairs={{0,2},{1,3},{2,0},{3,1},{4,6},{5,7},{6,4},{7,5},{8,10},{9,11},{10,... | collective-permute-start | bytes 98312 | tf_op jit(solution)/shard_map/ppermute | solution.py:250
  111.3 3.2 %collective-permute-start.15 = (f32[64,128]{1,0:T(8,128)S(1)}, f32[64,128]{1,0:T(8,128)S(1)}, u32[]{:S(2)}, u32[]{:S(2)}) collective-permute-start(f32[64,128]{1,0:T(8,128)S(1)} %solve_down.6.refs_0_.refs_11_), channel_id=1, source_target_pairs={{0,1},{1,0},{2,3},{3,2},{4,5},{5,4},{6,7},{7,6},{8,9},{9,8},{10,11... | collective-permute-start | bytes 98312 | tf_op jit(solution)/shard_map/ppermute | solution.py:250
  127.5 3.4 %collective-permute-start.20 = (f32[64,128]{1,0:T(8,128)S(1)}, f32[64,128]{1,0:T(8,128)S(1)}, u32[]{:S(2)}, u32[]{:S(2)}) collective-permute-start(f32[64,128]{1,0:T(8,128)S(1)} %solve_down.7.refs_0_.refs_10_), channel_id=1, source_target_pairs={{0,3},{1,2},{2,1},{3,0},{4,7},{5,6},{6,5},{7,4},{8,11},{9,10},{10,... | collective-permute-start | bytes 98312 | tf_op jit(solution)/shard_map/ppermute | solution.py:250
  127.6 4.3 %collective-permute-start.19 = (f32[64,128]{1,0:T(8,128)S(1)}, f32[64,128]{1,0:T(8,128)S(1)}, u32[]{:S(2)}, u32[]{:S(2)}) collective-permute-start(f32[64,128]{1,0:T(8,128)S(1)} %solve_down.7.refs_0_.refs_10_), channel_id=1, source_target_pairs={{0,2},{1,3},{2,0},{3,1},{4,6},{5,7},{6,4},{7,5},{8,10},{9,11},{10,... | collective-permute-start | bytes 98312 | tf_op jit(solution)/shard_map/ppermute | solution.py:250
  128.5 3.3 %collective-permute-start.18 = (f32[64,128]{1,0:T(8,128)S(1)}, f32[64,128]{1,0:T(8,128)S(1)}, u32[]{:S(2)}, u32[]{:S(2)}) collective-permute-start(f32[64,128]{1,0:T(8,128)S(1)} %solve_down.7.refs_0_.refs_10_), channel_id=1, source_target_pairs={{0,1},{1,0},{2,3},{3,2},{4,5},{5,4},{6,7},{7,6},{8,9},{9,8},{10,11... | collective-permute-start | bytes 98312 | tf_op jit(solution)/shard_map/ppermute | solution.py:250
  145.5 3.4 %collective-permute-start.23 = (f32[64,128]{1,0:T(8,128)S(1)}, f32[64,128]{1,0:T(8,128)S(1)}, u32[]{:S(2)}, u32[]{:S(2)}) collective-permute-start(f32[64,128]{1,0:T(8,128)S(1)} %solve_down.8.refs_0_.refs_9_), channel_id=1, source_target_pairs={{0,3},{1,2},{2,1},{3,0},{4,7},{5,6},{6,5},{7,4},{8,11},{9,10},{10,... | collective-permute-start | bytes 98312 | tf_op jit(solution)/shard_map/ppermute | solution.py:250
  145.6 4.3 %collective-permute-start.22 = (f32[64,128]{1,0:T(8,128)S(1)}, f32[64,128]{1,0:T(8,128)S(1)}, u32[]{:S(2)}, u32[]{:S(2)}) collective-permute-start(f32[64,128]{1,0:T(8,128)S(1)} %solve_down.8.refs_0_.refs_9_), channel_id=1, source_target_pairs={{0,2},{1,3},{2,0},{3,1},{4,6},{5,7},{6,4},{7,5},{8,10},{9,11},{10,... | collective-permute-start | bytes 98312 | tf_op jit(solution)/shard_map/ppermute | solution.py:250
  146.6 3.3 %collective-permute-start.21 = (f32[64,128]{1,0:T(8,128)S(1)}, f32[64,128]{1,0:T(8,128)S(1)}, u32[]{:S(2)}, u32[]{:S(2)}) collective-permute-start(f32[64,128]{1,0:T(8,128)S(1)} %solve_down.8.refs_0_.refs_9_), channel_id=1, source_target_pairs={{0,1},{1,0},{2,3},{3,2},{4,5},{5,4},{6,7},{7,6},{8,9},{9,8},{10,11... | collective-permute-start | bytes 98312 | tf_op jit(solution)/shard_map/ppermute | solution.py:250
  163.7 3.4 %collective-permute-start.26 = (f32[64,128]{1,0:T(8,128)S(1)}, f32[64,128]{1,0:T(8,128)S(1)}, u32[]{:S(2)}, u32[]{:S(2)}) collective-permute-start(f32[64,128]{1,0:T(8,128)S(1)} %solve_down.9.refs_0_.refs_8_), channel_id=1, source_target_pairs={{0,3},{1,2},{2,1},{3,0},{4,7},{5,6},{6,5},{7,4},{8,11},{9,10},{10,... | collective-permute-start | bytes 98312 | tf_op jit(solution)/shard_map/ppermute | solution.py:250
  163.8 4.3 %collective-permute-start.25 = (f32[64,128]{1,0:T(8,128)S(1)}, f32[64,128]{1,0:T(8,128)S(1)}, u32[]{:S(2)}, u32[]{:S(2)}) collective-permute-start(f32[64,128]{1,0:T(8,128)S(1)} %solve_down.9.refs_0_.refs_8_), channel_id=1, source_target_pairs={{0,2},{1,3},{2,0},{3,1},{4,6},{5,7},{6,4},{7,5},{8,10},{9,11},{10,... | collective-permute-start | bytes 98312 | tf_op jit(solution)/shard_map/ppermute | solution.py:250
  164.9 3.2 %collective-permute-start.24 = (f32[64,128]{1,0:T(8,128)S(1)}, f32[64,128]{1,0:T(8,128)S(1)}, u32[]{:S(2)}, u32[]{:S(2)}) collective-permute-start(f32[64,128]{1,0:T(8,128)S(1)} %solve_down.9.refs_0_.refs_8_), channel_id=1, source_target_pairs={{0,1},{1,0},{2,3},{3,2},{4,5},{5,4},{6,7},{7,6},{8,9},{9,8},{10,11... | collective-permute-start | bytes 98312 | tf_op jit(solution)/shard_map/ppermute | solution.py:250
  181.9 3.4 %collective-permute-start.29 = (f32[64,128]{1,0:T(8,128)S(1)}, f32[64,128]{1,0:T(8,128)S(1)}, u32[]{:S(2)}, u32[]{:S(2)}) collective-permute-start(f32[64,128]{1,0:T(8,128)S(1)} %solve_down.10.refs_0_.refs_7_), channel_id=1, source_target_pairs={{0,3},{1,2},{2,1},{3,0},{4,7},{5,6},{6,5},{7,4},{8,11},{9,10},{10,... | collective-permute-start | bytes 98312 | tf_op jit(solution)/shard_map/ppermute | solution.py:250
  182.0 4.2 %collective-permute-start.28 = (f32[64,128]{1,0:T(8,128)S(1)}, f32[64,128]{1,0:T(8,128)S(1)}, u32[]{:S(2)}, u32[]{:S(2)}) collective-permute-start(f32[64,128]{1,0:T(8,128)S(1)} %solve_down.10.refs_0_.refs_7_), channel_id=1, source_target_pairs={{0,2},{1,3},{2,0},{3,1},{4,6},{5,7},{6,4},{7,5},{8,10},{9,11},{10,... | collective-permute-start | bytes 98312 | tf_op jit(solution)/shard_map/ppermute | solution.py:250
  183.1 3.1 %collective-permute-start.27 = (f32[64,128]{1,0:T(8,128)S(1)}, f32[64,128]{1,0:T(8,128)S(1)}, u32[]{:S(2)}, u32[]{:S(2)}) collective-permute-start(f32[64,128]{1,0:T(8,128)S(1)} %solve_down.10.refs_0_.refs_7_), channel_id=1, source_target_pairs={{0,1},{1,0},{2,3},{3,2},{4,5},{5,4},{6,7},{7,6},{8,9},{9,8},{10,11... | collective-permute-start | bytes 98312 | tf_op jit(solution)/shard_map/ppermute | solution.py:250

commit v5 on v4

--- a/solution.py
+++ b/solution.py
@@ -28,57 +28,84 @@
 
 
 def gather_blocks_kernel(
-    n_col, level, target_ref, source_ref, count_ref, place_ref, blocks_ref, *refs
+    n_row, n_col, level, chunk, target_ref, source_ref, count_ref, place_ref, blocks_ref, *refs
 ):
-    high_ref, low_ref, slots, total, arrived = refs[-5:]
-    slot_count, block = slots.shape[:2]
+    total, slots, arrived = refs[-3:]
     count = count_ref[level]
-
-    def fetch(slot):
-        return pltpu.make_async_copy(blocks_ref.at[level, slot], slots.at[slot], arrived.at[slot])
-
-    for slot in range(slot_count):
-        pl.when(slot < count)(fetch(slot).start)
+    half = n_row // 2
+    side = place_ref[0] // half
+
+    def fetch(number):
+        span = pl.ds(number * chunk, chunk)
+        return pltpu.make_async_copy(
+            blocks_ref.at[level, span], slots.at[span], arrived.at[number]
+        )
+
+    for number in range(arrived.shape[0]):
+        pl.when(number * chunk < count)(fetch(number).start)
     total[...] = jnp.zeros_like(total)
 
     def add(slot, carry):
-        fetch(slot).wait()
-        above = target_ref[level, slot] ^ place_ref[0]
-        total[source_ref[level, slot] * n_col + above] += slots[slot]
+        pl.when(lax.rem(slot, chunk) == 0)(fetch(slot // chunk).wait)
+        source = source_ref[level, slot]
+        below = lax.rem(source, half) * 2 + ((source // half) ^ side)
+        above = target_ref[level, slot] ^ place_ref[1]
+        total[below * n_col + above] += slots[slot]
         return carry
 
     lax.fori_loop(0, count, add, 0)
-    for pair in range(total.shape[0]):
+
+
+def gather_blocks(level, target, source, count, place, blocks, n_row, n_col, after):
+    slot_count, block = blocks.shape[1], blocks.shape[2]
+    chunk = max(1, slot_count // 4)
+    shape = (n_row * n_col, block, block)
+    scalars = pl.BlockSpec(memory_space=SMEM)
+    return pl.pallas_call(
+        functools.partial(gather_blocks_kernel, n_row, n_col, level, chunk),
+        out_shape=jax.ShapeDtypeStruct(shape, jnp.float32),
+        in_specs=[scalars] * 4 + [pl.BlockSpec(memory_space=pl.ANY)] * (1 + len(after)),
+        out_specs=pl.BlockSpec(memory_space=VMEM),
+        scratch_shapes=[
+            pltpu.VMEM((slot_count, block, block), jnp.float32),
+            pltpu.SemaphoreType.DMA((slot_count // chunk,)),
+        ],
+        compiler_params=pltpu.CompilerParams(vmem_limit_bytes=(51 if level == 0 else 16) * MIB),
+        cost_estimate=pl.CostEstimate(
+            flops=slot_count * block * block,
+            bytes_accessed=8 * slot_count * block * block,
+            transcendentals=0,
+        ),
+        name=f"gather_blocks_{level}",
+    )(target, source, count, place, blocks, *after)
+
+
+def split_kernel(n_col, total_ref, *refs):
+    high_ref, low_ref = refs[-2:]
+    block = total_ref.shape[-1]
+    for pair in range(total_ref.shape[0]):
         rows = pl.ds(pair // n_col * block, block)
         lanes = pl.ds(pair % n_col * block, block)
-        high, low = halves(total[pair])
+        high, low = halves(total_ref[pair])
         high_ref[rows, lanes] = high
         low_ref[rows, lanes] = low
 
 
-def gather_blocks(level, target, source, count, place, blocks, n_row, n_col, after):
-    slot_count, block = blocks.shape[1], blocks.shape[2]
-    shape = (n_row * block, n_col * block)
-    scalars = pl.BlockSpec(memory_space=SMEM)
+def split(total, n_row, n_col, after):
+    block = total.shape[-1]
+    shape = jax.ShapeDtypeStruct((n_row * block, n_col * block), jnp.bfloat16)
     whole = pl.BlockSpec(memory_space=VMEM)
     return pl.pallas_call(
-        functools.partial(gather_blocks_kernel, n_col, level),
-        out_shape=[jax.ShapeDtypeStruct(shape, jnp.bfloat16)] * 2,
-        in_specs=[scalars] * 4
-        + [pl.BlockSpec(memory_space=pltpu.MemorySpace.HBM)]
-        + [pl.BlockSpec(memory_space=pl.ANY)] * len(after),
+        functools.partial(split_kernel, n_col),
+        out_shape=[shape, shape],
+        in_specs=[whole] + [pl.BlockSpec(memory_space=pl.ANY)] * len(after),
         out_specs=[whole, whole],
-        scratch_shapes=[
-            pltpu.VMEM((slot_count, block, block), jnp.float32),
-            pltpu.VMEM((n_row * n_col, block, block), jnp.float32),
-            pltpu.SemaphoreType.DMA((slot_count,)),
-        ],
-        compiler_params=pltpu.CompilerParams(vmem_limit_bytes=(16 if after else 51) * MIB),
+        compiler_params=pltpu.CompilerParams(vmem_limit_bytes=8 * MIB),
         cost_estimate=pl.CostEstimate(
-            flops=2 * shape[0] * shape[1], bytes_accessed=8 * shape[0] * shape[1], transcendentals=0
-        ),
-        name=f"gather_blocks_{level}",
-    )(target, source, count, place, blocks, *after)
+            flops=3 * total.size, bytes_accessed=8 * total.size, transcendentals=0
+        ),
+        name="split",
+    )(total, *after)
 
 
 def read(term, refs):
@@ -148,7 +175,7 @@
     )(high, low, *operands.arrays)
 
 
-def first_solve_kernel(right_ref, inverse_ref, out_ref, copies_ref, right, inverse, arrived):
+def first_solve_kernel(right_ref, inverse_ref, out_ref, right, inverse, arrived):
     fetches = [
         pltpu.make_async_copy(right_ref.at[0], right, arrived.at[0]),
         pltpu.make_async_copy(inverse_ref.at[0], inverse, arrived.at[1]),
@@ -157,22 +184,16 @@
         fetch.start()
     for fetch in fetches:
         fetch.wait()
-    result = product(halves(right[...]), halves(inverse[...]), False)
-    out_ref[...] = result
-    write(copies_ref, [result] * copies_ref.shape[0])
-
-
-def first_solve(right, inverse, n_copies):
+    out_ref[...] = product(halves(right[...]), halves(inverse[...]), False)
+
+
+def first_solve(right, inverse):
     rows, block = right.shape[-2:]
-    whole = pl.BlockSpec(memory_space=VMEM)
     return pl.pallas_call(
         first_solve_kernel,
-        out_shape=[
-            jax.ShapeDtypeStruct((rows, block), jnp.float32),
-            jax.ShapeDtypeStruct((n_copies, rows, block), jnp.float32),
-        ],
+        out_shape=jax.ShapeDtypeStruct((rows, block), jnp.float32),
         in_specs=[pl.BlockSpec(memory_space=pl.ANY)] * 2,
-        out_specs=[whole] * 2,
+        out_specs=pl.BlockSpec(memory_space=VMEM),
         scratch_shapes=[
             pltpu.VMEM((rows, block), jnp.float32),
             pltpu.VMEM((block, block), jnp.float32),
@@ -183,41 +204,58 @@
     )(right, inverse)
 
 
-def solve_kernel(transposed, level, terms, n_ins, n_copies, *refs):
+def solve_kernel(transposed, level, terms, n_ins, *refs):
     right_ref, inverse_ref = refs[:2]
-    ins = refs[2 : 2 + n_ins]
-    outs = refs[-2:] if n_copies else refs[-1:]
+    ins, out_ref = refs[2 : 2 + n_ins], refs[-1]
     value = right_ref[level] if len(right_ref.shape) == 3 else right_ref[...]
     if terms:
         value -= total_of(terms, ins)
-    result = product(halves(value), halves(inverse_ref[level]), transposed)
-    outs[0][...] = result
-    if n_copies:
-        write(outs[1], [result] * n_copies)
-
-
-def solve(right, inverse, level, pieces, transposed, n_copies=0, after=()):
+    out_ref[...] = product(halves(value), halves(inverse_ref[level]), transposed)
+
+
+def solve(right, inverse, level, pieces, transposed, after=()):
     rows, block = right.shape[-2:]
     operands = Operands()
     terms = [operands.term(piece) for piece in pieces]
     whole = pl.BlockSpec(memory_space=VMEM)
-    out_shape = [jax.ShapeDtypeStruct((rows, block), jnp.float32)]
-    if n_copies:
-        out_shape.append(jax.ShapeDtypeStruct((n_copies, rows, block), jnp.float32))
-    return pl.pallas_call(
-        functools.partial(
-            solve_kernel, transposed, level, terms, len(operands.arrays), n_copies
-        ),
-        out_shape=out_shape,
+    return pl.pallas_call(
+        functools.partial(solve_kernel, transposed, level, terms, len(operands.arrays)),
+        out_shape=jax.ShapeDtypeStruct((rows, block), jnp.float32),
         in_specs=[whole] * (2 + len(operands.arrays))
         + [pl.BlockSpec(memory_space=pl.ANY)] * len(after),
-        out_specs=[whole] * len(out_shape),
+        out_specs=whole,
         compiler_params=pltpu.CompilerParams(vmem_limit_bytes=8 * MIB),
         cost_estimate=pl.CostEstimate(
             flops=6 * rows * block * block, bytes_accessed=4 * block * block, transcendentals=0
         ),
         name="solve_up" if not transposed else "solve_down",
     )(right, inverse, *operands.arrays, *after)
+
+
+def combine_kernel(sums, n_ins, *refs):
+    ins, outs = refs[:n_ins], refs[-len(sums) :]
+    for terms, ref in zip(sums, outs):
+        write(ref, [total_of(entry, ins) for entry in terms])
+
+
+def combine(sums, after=()):
+    operands = Operands()
+    sums = [[[operands.term(piece) for piece in entry] for entry in entries] for entries in sums]
+    rows, block = operands.arrays[0].shape[-2:]
+    whole = pl.BlockSpec(memory_space=VMEM)
+    shapes = [(rows, block) if len(e) == 1 else (len(e), rows, block) for e in sums]
+    return pl.pallas_call(
+        functools.partial(combine_kernel, sums, len(operands.arrays)),
+        out_shape=[jax.ShapeDtypeStruct(shape, jnp.float32) for shape in shapes],
+        in_specs=[whole] * len(operands.arrays)
+        + [pl.BlockSpec(memory_space=pl.ANY)] * len(after),
+        out_specs=[whole] * len(sums),
+        compiler_params=pltpu.CompilerParams(vmem_limit_bytes=8 * MIB),
+        cost_estimate=pl.CostEstimate(
+            flops=rows * block, bytes_accessed=4 * rows * block, transcendentals=0
+        ),
+        name="combine",
+    )(*operands.arrays, *after)
 
 
 def stack_kernel(n_forward, *refs):
@@ -239,9 +277,32 @@
     )(*forward, *backward)
 
 
-def exchange_all(stacked, axis):
-    received = lax.all_to_all(stacked, axis, 0, 0, tiled=True)
-    return [(received, place) for place in range(stacked.shape[0])]
+def near_exchange(stacked, axis):
+    half = lax.axis_size(axis) // 2
+    groups = [list(range(half)), list(range(half, 2 * half))]
+    return lax.all_to_all(stacked, axis, 0, 0, axis_index_groups=groups, tiled=True)
+
+
+def far_exchange(segment, axis):
+    size = lax.axis_size(axis)
+    return lax.ppermute(segment, axis, [(i, i ^ (size // 2)) for i in range(size)])
+
+
+def gather_row(segment, after):
+    half = lax.axis_size("row") // 2
+    received = far_exchange(segment, "row")
+    (stacked,) = combine([[[(segment, None)], [(received, None)]] * half], after)
+    received = near_exchange(stacked, "row")
+    return [(received, place) for place in range(2 * half)]
+
+
+def deliver_row(stacked):
+    half = lax.axis_size("row") // 2
+    received = near_exchange(stacked, "row")
+    mine, other = combine(
+        [[[(received, 2 * place + side) for place in range(half)]] for side in range(2)]
+    )
+    return [(mine, None), (far_exchange(other, "row"), None)]
 
 
 def exchange_each(messages, axis):
@@ -262,30 +323,29 @@
     target = blk_target.reshape(levels - 1, -1)
     source = blk_source.reshape(levels - 1, -1)
     count = blk_count.reshape(levels - 1)
-    place = lax.axis_index("col").astype(jnp.int32).reshape(1)
+    place = jnp.stack([lax.axis_index("row"), lax.axis_index("col")]).astype(jnp.int32)
     gather = lambda level, after: gather_blocks(
         level, target, source, count, place, weights, n_row, n_col, after
     )
-    first, copies = first_solve(right, inverse, n_row)
-    coupling = [gather(0, ())]
-    forward = [first]
+    forward = [first_solve(right, inverse)]
+    total = gather(0, forward[:1])
+    coupling = []
     for level in range(1, levels):
-        partial = couple(exchange_all(copies, "row"), *coupling[level - 1], False)
-        last = level == levels - 1
-        if not last:
-            coupling.append(gather(level, (partial[0],)))
-        after = () if last else coupling[level][:1]
+        coupling.append(split(total, n_row, n_col, forward[-1:]))
+        pieces = gather_row(forward[-1], coupling[-1][:1])
+        partial = couple(pieces, *coupling[-1], False)
+        after = ()
+        if level < levels - 1:
+            total = gather(level, partial[:1])
+            after = (total,)
         pieces = exchange_each(partial, "col")
-        solved = solve(right, inverse, level, pieces, False, 0 if last else n_row, after)
-        forward.append(solved[0])
-        copies = solved[-1]
+        forward.append(solve(right, inverse, level, pieces, False, after))
     backward = [None] * levels
-    (backward[-1],) = solve(forward[-1], inverse, levels - 1, [], True)
+    backward[-1] = solve(forward[-1], inverse, levels - 1, [], True)
     for level in range(levels - 2, -1, -1):
         pieces = exchange_each([backward[level + 1]] * n_col, "col")
         (partial,) = couple(pieces, *coupling[level], True)
-        pieces = exchange_all(partial, "row")
-        (backward[level],) = solve(forward[level], inverse, level, pieces, True)
+        backward[level] = solve(forward[level], inverse, level, deliver_row(partial), True)
     outs = stack(forward, backward)
     return tuple(out.reshape(rhs.shape) for out in outs)
 
@@ -403,7 +463,7 @@
     def local(rhs, diag_inv, blocks, blk_target, blk_source, blk_count):
         sizes = (n_row, n_col)
         dense = n_row * n_col <= blocks.shape[3] and rhs.shape[3] == 1
-        even = all(size & (size - 1) == 0 for size in sizes)
+        even = all(size > 1 and size & (size - 1) == 0 for size in sizes)
         run = direct_shards if dense and even else shards
         return run(rhs, diag_inv, blocks, blk_target, blk_source, blk_count)
 

time: 201 us -> 197 us (0.980)
  waiting for transfers between devices: 20.2 us -> 59.6 us
  blocking collectives: 114 us -> 84.4 us
  local copies, waits for them, and re-layouts: 9.34 us -> 2.14 us
  Pallas kernels: 29.7 us -> 22.8 us
    ppermute x0 -> x10, waiting for transfers between devices: none -> 39.6 us  [far_exchange(): lax.ppermute(segment, axis, [(i, i ^ size // 2) for i in range(size)])]
    all_to_all x9 -> x10, blocking collectives: 114 us -> 84.4 us  [near_exchange(): lax.all_to_all(stacked, axis, 0, 0, axis_index_groups=groups, tiled=True)]
    all_to_all x1 -> x0, starting transfers between devices: 7.29 us -> none  [exchange_all(): received = lax.all_to_all(stacked, axis, 0, 0, tiled=True)]
    unnamed x21 -> x17, local copies, waits for them, and re-layouts: 9.34 us -> 2.14 us
    ppermute x0 -> x10, starting transfers between devices: none -> 7.08 us  [far_exchange(): lax.ppermute(segment, axis, [(i, i ^ size // 2) for i in range(size)])]
    pallas_call x6 -> x21, Pallas kernels: 18.5 us -> 11.8 us  [the longest x5 8.1 us: gather_blocks(): pl.pallas_call(functools.partial(gather_blocks_kernel, n_row, n_col, leve...]
    all_to_all x1 -> x0, waiting for transfers between devices: 5.05 us -> none  [exchange_all(): received = lax.all_to_all(stacked, axis, 0, 0, tiled=True)]
    ppermute x30, waiting for transfers between devices: 15.1 us -> 20 us  [exchange_each(): lax.ppermute(messages[d], axis, [(i, i ^ d) for i in range(size)])]
  transfers between devices with their start and end apart: 31 -> 40, of which waited for: 12 -> 29; matrix products, arithmetic and copies ran while one was open for 0% -> 0% of each run, Pallas kernels for 8% -> 5%
where the time goes in v5:
time: 197 us; the launch traced here: 196 us
  blocking collectives  84.4 us (43%)
  waiting for transfers between devices  59.6 us (30%)
  starting transfers between devices  26.4 us (13%)
  Pallas kernels  22.8 us (12%)
  local copies, waits for them, and re-layouts  2.14 us (1%)
    all_to_all x10, blocking collectives, near_exchange(): lax.all_to_all(stacked, axis, 0, 0, axis_index_groups=groups, tiled=True)  84.4 us
    ppermute x10, waiting for transfers between devices, far_exchange(): lax.ppermute(segment, axis, [(i, i ^ size // 2) for i in range(size)])  39.6 us
    ppermute x30, waiting for transfers between devices, exchange_each(): lax.ppermute(messages[d], axis, [(i, i ^ d) for i in range(size)])  20 us
    ppermute x30, starting transfers between devices, exchange_each(): lax.ppermute(messages[d], axis, [(i, i ^ d) for i in range(size)])  19.3 us
    pallas_call x10, Pallas kernels, couple(): pl.pallas_call(functools.partial(couple_kernel, transposed, terms), out_s...  8.5 us
    pallas_call x5, Pallas kernels, gather_blocks(): pl.pallas_call(functools.partial(gather_blocks_kernel, n_row, n_col, leve...  8.1 us
    ppermute x10, starting transfers between devices, far_exchange(): lax.ppermute(segment, axis, [(i, i ^ size // 2) for i in range(size)])  7.08 us
  transfers between devices with their start and end apart: 40, of which 29 were waited for; matrix products, arithmetic and copies ran while one was open for 0% of the time, Pallas kernels for 5%

profile of v5, /device:TPU:0, one launch (start us, length us, event | category | flops | bytes accessed | tf_op | source)
XLA Modules:
  0.0 196.4 jit_solution(16193275331717684724)
XLA Ops:
  0.6 1.8 first_solve.1.refs_0_
  2.5 4.1 %collective-permute-start = (f32[64,128]{1,0:T(8,128)}, f32[64,128]{1,0:T(8,128)S(1)}, u32[]{:S(2)}, u32[]{:S(2)}) collective-permute-start(f32[64,128]{1,0:T(8,128)} %first_solve.1.refs_0_), channel_id=1, source_target_pairs={{0,16},{4,20},{8,24},{12,28},{16,0},{20,4},{24,8},{28,12},{1,17},{... | collective-permute-start | bytes 98312 | tf_op jit(solution)/shard_map/ppermute | solution.py:288
  7.3 0.8 copy-done.2
  8.7 2.3 %gather_blocks_0.1.total_ref = f32[32,128,128]{2,1,0:T(8,128)S(1)} custom-call(s32[5,32]{1,0:T(8,128)S(1)} %get-tuple-element.89.target_ref, s32[5,32]{1,0:T(8,128)S(1)} %get-tuple-element.88.source_ref, s32[5]{0:T(128)S(1)} %bitcast.41, s32[2]{0:T(128)S(1)} %pad_add_fusion.place_ref, f32[5,32,128,128]{3,2,1,0:T(8,128)} %bitcast.16, f32[64,128]{1,0:T(8,128)S(1)} %copy-done.2), custom_call_target="tpu_custom_call" | custom-call | flops 524288 | bytes 4194304 | tf_op jit(solution)/shard_map/gather_blocks_0/pallas_call | solution.py:64
  11.4 9.6 %all_to_all.50.refs_0_ = f32[8,64,128]{2,1,0:T(8,128)S(1)} all-to-all(f32[8,64,128]{2,1,0:T(8,128)S(1)} %combine.10), channel_id=1, replica_groups={{0,4,8,12},{16,20,24,28},{1,5,9,13},{17,21,25,29},{2,6,10,14},{18,22,26..., dimensions={0} | all-to-all | bytes 524288 | tf_op jit(solution)/shard_map/all_to_all | solution.py:283
  21.8 1.8 collective-permute-start.2
  23.7 1.5 gather_blocks_1.1.refs_6_.total_ref
  25.8 1.2 collective-permute-done.3.refs_5_
  27.5 4.5 %collective-permute-done.4.refs_1_ = f32[64,128]{1,0:T(8,128)S(1)} collective-permute-done((f32[64,128]{1,0:T(8,128)S(1)}, f32[64,128]{1,0:T(8,128)S(1)}, u32[]{:S(2)}, u32[]{:S(2)}) %collective-permute-start.4) | collective-permute-done | bytes 32800 | tf_op jit(solution)/shard_map/ppermute | solution.py:288
  32.0 8.1 %all_to_all.51.refs_0_ = f32[8,64,128]{2,1,0:T(8,128)S(1)} all-to-all(f32[8,64,128]{2,1,0:T(8,128)S(1)} %combine.11), channel_id=1, replica_groups={{0,4,8,12},{16,20,24,28},{1,5,9,13},{17,21,25,29},{2,6,10,14},{18,22,26..., dimensions={0} | all-to-all | bytes 524288 | tf_op jit(solution)/shard_map/all_to_all | solution.py:283
  40.9 0.8 collective-permute-start.6
  41.7 1.0 collective-permute-start.7
  42.7 1.5 gather_blocks_2.1.refs_6_.total_ref
  46.2 4.2 %collective-permute-done.8.refs_1_ = f32[64,128]{1,0:T(8,128)S(1)} collective-permute-done((f32[64,128]{1,0:T(8,128)S(1)}, f32[64,128]{1,0:T(8,128)S(1)}, u32[]{:S(2)}, u32[]{:S(2)}) %collective-permute-start.8) | collective-permute-done | bytes 32800 | tf_op jit(solution)/shard_map/ppermute | solution.py:288
  50.4 8.1 %all_to_all.52.refs_0_ = f32[8,64,128]{2,1,0:T(8,128)S(1)} all-to-all(f32[8,64,128]{2,1,0:T(8,128)S(1)} %combine.12), channel_id=1, replica_groups={{0,4,8,12},{16,20,24,28},{1,5,9,13},{17,21,25,29},{2,6,10,14},{18,22,26..., dimensions={0} | all-to-all | bytes 524288 | tf_op jit(solution)/shard_map/all_to_all | solution.py:283
  59.3 1.0 collective-permute-start.10
  60.3 0.9 collective-permute-start.11
  61.1 1.3 gather_blocks_3.1.refs_6_.total_ref
  62.5 0.8 collective-permute-done.10.refs_4_
  64.5 4.2 %collective-permute-done.12.refs_1_ = f32[64,128]{1,0:T(8,128)S(1)} collective-permute-done((f32[64,128]{1,0:T(8,128)S(1)}, f32[64,128]{1,0:T(8,128)S(1)}, u32[]{:S(2)}, u32[]{:S(2)}) %collective-permute-start.12) | collective-permute-done | bytes 32800 | tf_op jit(solution)/shard_map/ppermute | solution.py:288
  68.7 8.1 %all_to_all.53.refs_0_ = f32[8,64,128]{2,1,0:T(8,128)S(1)} all-to-all(f32[8,64,128]{2,1,0:T(8,128)S(1)} %combine.13), channel_id=1, replica_groups={{0,4,8,12},{16,20,24,28},{1,5,9,13},{17,21,25,29},{2,6,10,14},{18,22,26..., dimensions={0} | all-to-all | bytes 524288 | tf_op jit(solution)/shard_map/all_to_all | solution.py:283
  77.5 1.1 collective-permute-start.14
  79.4 1.5 gather_blocks_4.1.refs_6_.total_ref
  82.9 4.2 %collective-permute-done.16.refs_1_ = f32[64,128]{1,0:T(8,128)S(1)} collective-permute-done((f32[64,128]{1,0:T(8,128)S(1)}, f32[64,128]{1,0:T(8,128)S(1)}, u32[]{:S(2)}, u32[]{:S(2)}) %collective-permute-start.16) | collective-permute-done | bytes 32800 | tf_op jit(solution)/shard_map/ppermute | solution.py:288
  87.1 8.1 %all_to_all.54.refs_0_ = f32[8,64,128]{2,1,0:T(8,128)S(1)} all-to-all(f32[8,64,128]{2,1,0:T(8,128)S(1)} %combine.14), channel_id=1, replica_groups={{0,4,8,12},{16,20,24,28},{1,5,9,13},{17,21,25,29},{2,6,10,14},{18,22,26..., dimensions={0} | all-to-all | bytes 524288 | tf_op jit(solution)/shard_map/all_to_all | solution.py:283
  95.9 1.0 collective-permute-start.18
  96.9 0.9 collective-permute-start.19
  97.8 2.1 %collective-permute-done.18.refs_4_ = f32[64,128]{1,0:T(8,128)S(1)} collective-permute-done((f32[64,128]{1,0:T(8,128)S(1)}, f32[64,128]{1,0:T(8,128)S(1)}, u32[]{:S(2)}, u32[]{:S(2)}) %collective-permute-start.18) | collective-permute-done | bytes 32800 | tf_op jit(solution)/shard_map/ppermute | solution.py:311
  100.6 0.9 collective-permute-start.22
  101.5 0.9 collective-permute-start.21
  102.5 1.5 collective-permute-done.22.refs_3_
  104.0 1.4 collective-permute-done.21.refs_2_
  105.4 1.1 couple_down.5
  106.5 8.1 %all_to_all.55.refs_0_ = f32[8,64,128]{2,1,0:T(8,128)S(1)} all-to-all(f32[8,64,128]{2,1,0:T(8,128)S(1)} %couple_down.5), channel_id=1, replica_groups={{0,4,8,12},{16,20,24,28},{1,5,9,13},{17,21,25,29},{2,6,10,14},{18,22,26..., dimensions={0} | all-to-all | bytes 524288 | tf_op jit(solution)/shard_map/all_to_all | solution.py:283
  115.0 4.5 %collective-permute-done.23.refs_3_ = f32[64,128]{1,0:T(8,128)S(1)} collective-permute-done((f32[64,128]{1,0:T(8,128)S(1)}, f32[64,128]{1,0:T(8,128)S(1)}, u32[]{:S(2)}, u32[]{:S(2)}) %collective-permute-start.23) | collective-permute-done | bytes 32800 | tf_op jit(solution)/shard_map/ppermute | solution.py:288
  119.8 1.0 collective-permute-start.25
  120.8 0.8 collective-permute-start.24
  121.6 1.5 collective-permute-done.26.refs_3_
  123.1 1.0 collective-permute-done.25.refs_2_
  124.1 1.1 couple_down.6
  125.1 8.7 %all_to_all.56.refs_0_ = f32[8,64,128]{2,1,0:T(8,128)S(1)} all-to-all(f32[8,64,128]{2,1,0:T(8,128)S(1)} %couple_down.6), channel_id=1, replica_groups={{0,4,8,12},{16,20,24,28},{1,5,9,13},{17,21,25,29},{2,6,10,14},{18,22,26..., dimensions={0} | all-to-all | bytes 524288 | tf_op jit(solution)/shard_map/all_to_all | solution.py:283
  134.2 4.5 %collective-permute-done.27.refs_3_ = f32[64,128]{1,0:T(8,128)S(1)} collective-permute-done((f32[64,128]{1,0:T(8,128)S(1)}, f32[64,128]{1,0:T(8,128)S(1)}, u32[]{:S(2)}, u32[]{:S(2)}) %collective-permute-start.27) | collective-permute-done | bytes 32800 | tf_op jit(solution)/shard_map/ppermute | solution.py:288
  139.0 0.9 collective-permute-start.29
  139.8 1.0 collective-permute-start.28
  140.8 1.5 collective-permute-done.30.refs_3_
  142.3 0.9 collective-permute-done.29.refs_2_
  143.2 1.1 couple_down.7
  144.2 8.5 %all_to_all.57.refs_0_ = f32[8,64,128]{2,1,0:T(8,128)S(1)} all-to-all(f32[8,64,128]{2,1,0:T(8,128)S(1)} %couple_down.7), channel_id=1, replica_groups={{0,4,8,12},{16,20,24,28},{1,5,9,13},{17,21,25,29},{2,6,10,14},{18,22,26..., dimensions={0} | all-to-all | bytes 524288 | tf_op jit(solution)/shard_map/all_to_all | solution.py:283
  153.1 4.5 %collective-permute-done.31.refs_3_ = f32[64,128]{1,0:T(8,128)S(1)} collective-permute-done((f32[64,128]{1,0:T(8,128)S(1)}, f32[64,128]{1,0:T(8,128)S(1)}, u32[]{:S(2)}, u32[]{:S(2)}) %collective-permute-start.31) | collective-permute-done | bytes 32800 | tf_op jit(solution)/shard_map/ppermute | solution.py:288
  157.9 0.8 collective-permute-start.33
  158.7 1.0 collective-permute-start.32
  159.7 1.5 collective-permute-done.34.refs_3_
  161.2 0.8 collective-permute-done.33.refs_2_
  162.1 1.1 couple_down.8
  163.1 8.5 %all_to_all.58.refs_0_ = f32[8,64,128]{2,1,0:T(8,128)S(1)} all-to-all(f32[8,64,128]{2,1,0:T(8,128)S(1)} %couple_down.8), channel_id=1, replica_groups={{0,4,8,12},{16,20,24,28},{1,5,9,13},{17,21,25,29},{2,6,10,14},{18,22,26..., dimensions={0} | all-to-all | bytes 524288 | tf_op jit(solution)/shard_map/all_to_all | solution.py:283
  172.0 4.5 %collective-permute-done.35.refs_3_ = f32[64,128]{1,0:T(8,128)S(1)} collective-permute-done((f32[64,128]{1,0:T(8,128)S(1)}, f32[64,128]{1,0:T(8,128)S(1)}, u32[]{:S(2)}, u32[]{:S(2)}) %collective-permute-start.35) | collective-permute-done | bytes 32800 | tf_op jit(solution)/shard_map/ppermute | solution.py:288
  176.8 0.9 collective-permute-start.37
  177.6 1.0 collective-permute-start.36
  178.6 1.5 collective-permute-done.38.refs_3_
  180.1 0.9 collective-permute-done.37.refs_2_
  181.0 1.1 couple_down.9
  182.0 8.5 %all_to_all.59.refs_0_ = f32[8,64,128]{2,1,0:T(8,128)S(1)} all-to-all(f32[8,64,128]{2,1,0:T(8,128)S(1)} %couple_down.9), channel_id=1, replica_groups={{0,4,8,12},{16,20,24,28},{1,5,9,13},{17,21,25,29},{2,6,10,14},{18,22,26..., dimensions={0} | all-to-all | bytes 524288 | tf_op jit(solution)/shard_map/all_to_all | solution.py:283
  190.9 4.5 %collective-permute-done.39.refs_3_ = f32[64,128]{1,0:T(8,128)S(1)} collective-permute-done((f32[64,128]{1,0:T(8,128)S(1)}, f32[64,128]{1,0:T(8,128)S(1)}, u32[]{:S(2)}, u32[]{:S(2)}) %collective-permute-start.39) | collective-permute-done | bytes 32800 | tf_op jit(solution)/shard_map/ppermute | solution.py:288
  195.6 0.8 stack.13
  (88 shorter events, 16.2 us)
Async XLA Ops:
  0.6 23.1 %slice-start = ((s8[10485760]{0:T(1024)(128)(4,1)}), s8[2097152]{0:T(1024)(128)(4,1)S(1)}, s32[]{:S(2)}) async-start(s8[10485760]{0:T(1024)(128)(4,1)} %bitcast.17), calls=%async_computation.10 | async-start | bytes 4194304
  2.5 8.9 %collective-permute-start = (f32[64,128]{1,0:T(8,128)}, f32[64,128]{1,0:T(8,128)S(1)}, u32[]{:S(2)}, u32[]{:S(2)}) collective-permute-start(f32[64,128]{1,0:T(8,128)} %first_solve.1.refs_0_), channel_id=1, source_target_pairs={{0,16},{4,20},{8,24},{12,28},{16,0},{20,4},{24,8},{28,12},{1,17},{... | collective-permute-start | bytes 98312 | tf_op jit(solution)/shard_map/ppermute | solution.py:288
  7.3 0.8 copy-start.2
  8.1 0.7 copy-start.3
  8.7 14.9 %slice-start.1 = ((s8[10485760]{0:T(1024)(128)(4,1)}), s8[4194304]{0:T(1024)(128)(4,1)S(1)}, s32[]{:S(2)}) async-start(s8[10485760]{0:T(1024)(128)(4,1)} %bitcast.17), calls=%async_computation.11 | async-start | bytes 8388608
  8.7 14.9 %slice-start.2 = ((s8[10485760]{0:T(1024)(128)(4,1)}), s8[4194304]{0:T(1024)(128)(4,1)S(1)}, s32[]{:S(2)}) async-start(s8[10485760]{0:T(1024)(128)(4,1)} %bitcast.17), calls=%async_computation.12 | async-start | bytes 8388608
  21.7 3.5 %collective-permute-start.1 = (f32[64,128]{1,0:T(8,128)S(1)}, f32[64,128]{1,0:T(8,128)S(1)}, u32[]{:S(2)}, u32[]{:S(2)}) collective-permute-start(f32[64,128]{1,0:T(8,128)S(1)} %get-tuple-element.47), channel_id=1, source_target_pairs={{0,1},{1,0},{2,3},{3,2},{4,5},{5,4},{6,7},{7,6},{8,9},{9,8},{10,11... | collective-permute-start | bytes 98312 | tf_op jit(solution)/shard_map/ppermute | solution.py:311
  21.8 4.0 %collective-permute-start.2 = (f32[64,128]{1,0:T(8,128)S(1)}, f32[64,128]{1,0:T(8,128)S(1)}, u32[]{:S(2)}, u32[]{:S(2)}) collective-permute-start(f32[64,128]{1,0:T(8,128)S(1)} %get-tuple-element.48), channel_id=1, source_target_pairs={{0,2},{1,3},{2,0},{3,1},{4,6},{5,7},{6,4},{7,5},{8,10},{9,11},{10,... | collective-permute-start | bytes 98312 | tf_op jit(solution)/shard_map/ppermute | solution.py:311
  23.6 3.3 %collective-permute-start.3 = (f32[64,128]{1,0:T(8,128)S(1)}, f32[64,128]{1,0:T(8,128)S(1)}, u32[]{:S(2)}, u32[]{:S(2)}) collective-permute-start(f32[64,128]{1,0:T(8,128)S(1)} %get-tuple-element.49), channel_id=1, source_target_pairs={{0,3},{1,2},{2,1},{3,0},{4,7},{5,6},{6,5},{7,4},{8,11},{9,10},{10,... | collective-permute-start | bytes 98312 | tf_op jit(solution)/shard_map/ppermute | solution.py:311
  23.7 3.3 %copy-start = (f32[6,1,1,1,128,128]{5,4,3,2,1,0:T(8,128)S(1)}, f32[6,1,1,1,128,128]{5,4,3,2,1,0:T(8,128)}, u32[]{:S(2)}) copy-start(f32[6,1,1,1,128,128]{5,4,3,2,1,0:T(8,128)} %param.7) | copy-start | bytes 1179652
  23.7 3.3 %copy-start.1 = (f32[6,1,1,1,64,128]{5,4,3,2,1,0:T(8,128)S(1)}, f32[6,1,1,1,64,128]{5,4,3,2,1,0:T(8,128)}, u32[]{:S(2)}) copy-start(f32[6,1,1,1,64,128]{5,4,3,2,1,0:T(8,128)} %param.6) | copy-start | bytes 589828
  27.1 4.9 %collective-permute-start.4 = (f32[64,128]{1,0:T(8,128)S(1)}, f32[64,128]{1,0:T(8,128)S(1)}, u32[]{:S(2)}, u32[]{:S(2)}) collective-permute-start(f32[64,128]{1,0:T(8,128)S(1)} %solve_up.5.refs_0_.refs_1_), channel_id=1, source_target_pairs={{0,16},{4,20},{8,24},{12,28},{16,0},{20,4},{24,8},{28,12},{1,17},{... | collective-permute-start | bytes 98312 | tf_op jit(solution)/shard_map/ppermute | solution.py:288
  32.0 10.7 %copy-start.4 = (s32[5,1,1]{0,2,1:T(1,128)S(1)}, s32[5,1,1]{0,2,1:T(1,128)}, u32[]{:S(2)}) copy-start(s32[5,1,1]{0,2,1:T(1,128)} %param.11) | copy-start | bytes 64
  40.8 3.5 %collective-permute-start.5 = (f32[64,128]{1,0:T(8,128)S(1)}, f32[64,128]{1,0:T(8,128)S(1)}, u32[]{:S(2)}, u32[]{:S(2)}) collective-permute-start(f32[64,128]{1,0:T(8,128)S(1)} %get-tuple-element.53), channel_id=1, source_target_pairs={{0,1},{1,0},{2,3},{3,2},{4,5},{5,4},{6,7},{7,6},{8,9},{9,8},{10,11... | collective-permute-start | bytes 98312 | tf_op jit(solution)/shard_map/ppermute | solution.py:311
  40.9 4.2 %collective-permute-start.6 = (f32[64,128]{1,0:T(8,128)S(1)}, f32[64,128]{1,0:T(8,128)S(1)}, u32[]{:S(2)}, u32[]{:S(2)}) collective-permute-start(f32[64,128]{1,0:T(8,128)S(1)} %get-tuple-element.54), channel_id=1, source_target_pairs={{0,2},{1,3},{2,0},{3,1},{4,6},{5,7},{6,4},{7,5},{8,10},{9,11},{10,... | collective-permute-start | bytes 98312 | tf_op jit(solution)/shard_map/ppermute | solution.py:311
  41.7 3.7 %collective-permute-start.7 = (f32[64,128]{1,0:T(8,128)S(1)}, f32[64,128]{1,0:T(8,128)S(1)}, u32[]{:S(2)}, u32[]{:S(2)}) collective-permute-start(f32[64,128]{1,0:T(8,128)S(1)} %get-tuple-element.55), channel_id=1, source_target_pairs={{0,3},{1,2},{2,1},{3,0},{4,7},{5,6},{6,5},{7,4},{8,11},{9,10},{10,... | collective-permute-start | bytes 98312 | tf_op jit(solution)/shard_map/ppermute | solution.py:311
  45.5 4.9 %collective-permute-start.8 = (f32[64,128]{1,0:T(8,128)S(1)}, f32[64,128]{1,0:T(8,128)S(1)}, u32[]{:S(2)}, u32[]{:S(2)}) collective-permute-start(f32[64,128]{1,0:T(8,128)S(1)} %solve_up.6.refs_0_.refs_2_), channel_id=1, source_target_pairs={{0,16},{4,20},{8,24},{12,28},{16,0},{20,4},{24,8},{28,12},{1,17},{... | collective-permute-start | bytes 98312 | tf_op jit(solution)/shard_map/ppermute | solution.py:288
  59.2 3.2 %collective-permute-start.9 = (f32[64,128]{1,0:T(8,128)S(1)}, f32[64,128]{1,0:T(8,128)S(1)}, u32[]{:S(2)}, u32[]{:S(2)}) collective-permute-start(f32[64,128]{1,0:T(8,128)S(1)} %get-tuple-element.59), channel_id=1, source_target_pairs={{0,1},{1,0},{2,3},{3,2},{4,5},{5,4},{6,7},{7,6},{8,9},{9,8},{10,11... | collective-permute-start | bytes 98312 | tf_op jit(solution)/shard_map/ppermute | solution.py:311
  59.3 4.0 %collective-permute-start.10 = (f32[64,128]{1,0:T(8,128)S(1)}, f32[64,128]{1,0:T(8,128)S(1)}, u32[]{:S(2)}, u32[]{:S(2)}) collective-permute-start(f32[64,128]{1,0:T(8,128)S(1)} %get-tuple-element.60), channel_id=1, source_target_pairs={{0,2},{1,3},{2,0},{3,1},{4,6},{5,7},{6,4},{7,5},{8,10},{9,11},{10,... | collective-permute-start | bytes 98312 | tf_op jit(solution)/shard_map/ppermute | solution.py:311
  60.3 3.3 %collective-permute-start.11 = (f32[64,128]{1,0:T(8,128)S(1)}, f32[64,128]{1,0:T(8,128)S(1)}, u32[]{:S(2)}, u32[]{:S(2)}) collective-permute-start(f32[64,128]{1,0:T(8,128)S(1)} %get-tuple-element.61), channel_id=1, source_target_pairs={{0,3},{1,2},{2,1},{3,0},{4,7},{5,6},{6,5},{7,4},{8,11},{9,10},{10,... | collective-permute-start | bytes 98312 | tf_op jit(solution)/shard_map/ppermute | solution.py:311
  63.8 4.9 %collective-permute-start.12 = (f32[64,128]{1,0:T(8,128)S(1)}, f32[64,128]{1,0:T(8,128)S(1)}, u32[]{:S(2)}, u32[]{:S(2)}) collective-permute-start(f32[64,128]{1,0:T(8,128)S(1)} %solve_up.7.refs_0_.refs_3_), channel_id=1, source_target_pairs={{0,16},{4,20},{8,24},{12,28},{16,0},{20,4},{24,8},{28,12},{1,17},{... | collective-permute-start | bytes 98312 | tf_op jit(solution)/shard_map/ppermute | solution.py:288
  77.5 3.4 %collective-permute-start.13 = (f32[64,128]{1,0:T(8,128)S(1)}, f32[64,128]{1,0:T(8,128)S(1)}, u32[]{:S(2)}, u32[]{:S(2)}) collective-permute-start(f32[64,128]{1,0:T(8,128)S(1)} %get-tuple-element.65), channel_id=1, source_target_pairs={{0,1},{1,0},{2,3},{3,2},{4,5},{5,4},{6,7},{7,6},{8,9},{9,8},{10,11... | collective-permute-start | bytes 98312 | tf_op jit(solution)/shard_map/ppermute | solution.py:311
  77.5 4.0 %collective-permute-start.14 = (f32[64,128]{1,0:T(8,128)S(1)}, f32[64,128]{1,0:T(8,128)S(1)}, u32[]{:S(2)}, u32[]{:S(2)}) collective-permute-start(f32[64,128]{1,0:T(8,128)S(1)} %get-tuple-element.66), channel_id=1, source_target_pairs={{0,2},{1,3},{2,0},{3,1},{4,6},{5,7},{6,4},{7,5},{8,10},{9,11},{10,... | collective-permute-start | bytes 98312 | tf_op jit(solution)/shard_map/ppermute | solution.py:311
  78.7 3.3 %collective-permute-start.15 = (f32[64,128]{1,0:T(8,128)S(1)}, f32[64,128]{1,0:T(8,128)S(1)}, u32[]{:S(2)}, u32[]{:S(2)}) collective-permute-start(f32[64,128]{1,0:T(8,128)S(1)} %get-tuple-element.67), channel_id=1, source_target_pairs={{0,3},{1,2},{2,1},{3,0},{4,7},{5,6},{6,5},{7,4},{8,11},{9,10},{10,... | collective-permute-start | bytes 98312 | tf_op jit(solution)/shard_map/ppermute | solution.py:311
  82.2 4.9 %collective-permute-start.16 = (f32[64,128]{1,0:T(8,128)S(1)}, f32[64,128]{1,0:T(8,128)S(1)}, u32[]{:S(2)}, u32[]{:S(2)}) collective-permute-start(f32[64,128]{1,0:T(8,128)S(1)} %solve_up.8.refs_0_.refs_4_), channel_id=1, source_target_pairs={{0,16},{4,20},{8,24},{12,28},{16,0},{20,4},{24,8},{28,12},{1,17},{... | collective-permute-start | bytes 98312 | tf_op jit(solution)/shard_map/ppermute | solution.py:288
  95.8 1.9 collective-permute-start.17
  95.9 4.0 %collective-permute-start.18 = (f32[64,128]{1,0:T(8,128)S(1)}, f32[64,128]{1,0:T(8,128)S(1)}, u32[]{:S(2)}, u32[]{:S(2)}) collective-permute-start(f32[64,128]{1,0:T(8,128)S(1)} %get-tuple-element.72), channel_id=1, source_target_pairs={{0,2},{1,3},{2,0},{3,1},{4,6},{5,7},{6,4},{7,5},{8,10},{9,11},{10,... | collective-permute-start | bytes 98312 | tf_op jit(solution)/shard_map/ppermute | solution.py:311
  96.9 3.3 %collective-permute-start.19 = (f32[64,128]{1,0:T(8,128)S(1)}, f32[64,128]{1,0:T(8,128)S(1)}, u32[]{:S(2)}, u32[]{:S(2)}) collective-permute-start(f32[64,128]{1,0:T(8,128)S(1)} %get-tuple-element.73), channel_id=1, source_target_pairs={{0,3},{1,2},{2,1},{3,0},{4,7},{5,6},{6,5},{7,4},{8,11},{9,10},{10,... | collective-permute-start | bytes 98312 | tf_op jit(solution)/shard_map/ppermute | solution.py:311
  100.6 3.4 %collective-permute-start.22 = (f32[64,128]{1,0:T(8,128)S(1)}, f32[64,128]{1,0:T(8,128)S(1)}, u32[]{:S(2)}, u32[]{:S(2)}) collective-permute-start(f32[64,128]{1,0:T(8,128)S(1)} %solve_down.6.refs_0_.refs_11_), channel_id=1, source_target_pairs={{0,3},{1,2},{2,1},{3,0},{4,7},{5,6},{6,5},{7,4},{8,11},{9,10},{10,... | collective-permute-start | bytes 98312 | tf_op jit(solution)/shard_map/ppermute | solution.py:311
  101.5 3.9 %collective-permute-start.21 = (f32[64,128]{1,0:T(8,128)S(1)}, f32[64,128]{1,0:T(8,128)S(1)}, u32[]{:S(2)}, u32[]{:S(2)}) collective-permute-start(f32[64,128]{1,0:T(8,128)S(1)} %solve_down.6.refs_0_.refs_11_), channel_id=1, source_target_pairs={{0,2},{1,3},{2,0},{3,1},{4,6},{5,7},{6,4},{7,5},{8,10},{9,11},{10,... | collective-permute-start | bytes 98312 | tf_op jit(solution)/shard_map/ppermute | solution.py:311
  102.5 3.0 %collective-permute-start.20 = (f32[64,128]{1,0:T(8,128)S(1)}, f32[64,128]{1,0:T(8,128)S(1)}, u32[]{:S(2)}, u32[]{:S(2)}) collective-permute-start(f32[64,128]{1,0:T(8,128)S(1)} %solve_down.6.refs_0_.refs_11_), channel_id=1, source_target_pairs={{0,1},{1,0},{2,3},{3,2},{4,5},{5,4},{6,7},{7,6},{8,9},{9,8},{10,11... | collective-permute-start | bytes 98312 | tf_op jit(solution)/shard_map/ppermute | solution.py:311
  114.6 4.9 %collective-permute-start.23 = (f32[64,128]{1,0:T(8,128)S(1)}, f32[64,128]{1,0:T(8,128)S(1)}, u32[]{:S(2)}, u32[]{:S(2)}) collective-permute-start(f32[64,128]{1,0:T(8,128)S(1)} %get-tuple-element.75), channel_id=1, source_target_pairs={{0,16},{4,20},{8,24},{12,28},{16,0},{20,4},{24,8},{28,12},{1,17},{... | collective-permute-start | bytes 98312 | tf_op jit(solution)/shard_map/ppermute | solution.py:288
  119.7 3.4 %collective-permute-start.26 = (f32[64,128]{1,0:T(8,128)S(1)}, f32[64,128]{1,0:T(8,128)S(1)}, u32[]{:S(2)}, u32[]{:S(2)}) collective-permute-start(f32[64,128]{1,0:T(8,128)S(1)} %solve_down.7.refs_0_.refs_10_), channel_id=1, source_target_pairs={{0,3},{1,2},{2,1},{3,0},{4,7},{5,6},{6,5},{7,4},{8,11},{9,10},{10,... | collective-permute-start | bytes 98312 | tf_op jit(solution)/shard_map/ppermute | solution.py:311
  119.8 4.3 %collective-permute-start.25 = (f32[64,128]{1,0:T(8,128)S(1)}, f32[64,128]{1,0:T(8,128)S(1)}, u32[]{:S(2)}, u32[]{:S(2)}) collective-permute-start(f32[64,128]{1,0:T(8,128)S(1)} %solve_down.7.refs_0_.refs_10_), channel_id=1, source_target_pairs={{0,2},{1,3},{2,0},{3,1},{4,6},{5,7},{6,4},{7,5},{8,10},{9,11},{10,... | collective-permute-start | bytes 98312 | tf_op jit(solution)/shard_map/ppermute | solution.py:311
  120.8 3.3 %collective-permute-start.24 = (f32[64,128]{1,0:T(8,128)S(1)}, f32[64,128]{1,0:T(8,128)S(1)}, u32[]{:S(2)}, u32[]{:S(2)}) collective-permute-start(f32[64,128]{1,0:T(8,128)S(1)} %solve_down.7.refs_0_.refs_10_), channel_id=1, source_target_pairs={{0,1},{1,0},{2,3},{3,2},{4,5},{5,4},{6,7},{7,6},{8,9},{9,8},{10,11... | collective-permute-start | bytes 98312 | tf_op jit(solution)/shard_map/ppermute | solution.py:311
  133.8 4.9 %collective-permute-start.27 = (f32[64,128]{1,0:T(8,128)S(1)}, f32[64,128]{1,0:T(8,128)S(1)}, u32[]{:S(2)}, u32[]{:S(2)}) collective-permute-start(f32[64,128]{1,0:T(8,128)S(1)} %get-tuple-element.77), channel_id=1, source_target_pairs={{0,16},{4,20},{8,24},{12,28},{16,0},{20,4},{24,8},{28,12},{1,17},{... | collective-permute-start | bytes 98312 | tf_op jit(solution)/shard_map/ppermute | solution.py:288
  138.9 3.4 %collective-permute-start.30 = (f32[64,128]{1,0:T(8,128)S(1)}, f32[64,128]{1,0:T(8,128)S(1)}, u32[]{:S(2)}, u32[]{:S(2)}) collective-permute-start(f32[64,128]{1,0:T(8,128)S(1)} %solve_down.8.refs_0_.refs_9_), channel_id=1, source_target_pairs={{0,3},{1,2},{2,1},{3,0},{4,7},{5,6},{6,5},{7,4},{8,11},{9,10},{10,... | collective-permute-start | bytes 98312 | tf_op jit(solution)/shard_map/ppermute | solution.py:311
  139.0 4.2 %collective-permute-start.29 = (f32[64,128]{1,0:T(8,128)S(1)}, f32[64,128]{1,0:T(8,128)S(1)}, u32[]{:S(2)}, u32[]{:S(2)}) collective-permute-start(f32[64,128]{1,0:T(8,128)S(1)} %solve_down.8.refs_0_.refs_9_), channel_id=1, source_target_pairs={{0,2},{1,3},{2,0},{3,1},{4,6},{5,7},{6,4},{7,5},{8,10},{9,11},{10,... | collective-permute-start | bytes 98312 | tf_op jit(solution)/shard_map/ppermute | solution.py:311
  139.8 3.3 %collective-permute-start.28 = (f32[64,128]{1,0:T(8,128)S(1)}, f32[64,128]{1,0:T(8,128)S(1)}, u32[]{:S(2)}, u32[]{:S(2)}) collective-permute-start(f32[64,128]{1,0:T(8,128)S(1)} %solve_down.8.refs_0_.refs_9_), channel_id=1, source_target_pairs={{0,1},{1,0},{2,3},{3,2},{4,5},{5,4},{6,7},{7,6},{8,9},{9,8},{10,11... | collective-permute-start | bytes 98312 | tf_op jit(solution)/shard_map/ppermute | solution.py:311
  152.8 4.9 %collective-permute-start.31 = (f32[64,128]{1,0:T(8,128)S(1)}, f32[64,128]{1,0:T(8,128)S(1)}, u32[]{:S(2)}, u32[]{:S(2)}) collective-permute-start(f32[64,128]{1,0:T(8,128)S(1)} %get-tuple-element.79), channel_id=1, source_target_pairs={{0,16},{4,20},{8,24},{12,28},{16,0},{20,4},{24,8},{28,12},{1,17},{... | collective-permute-start | bytes 98312 | tf_op jit(solution)/shard_map/ppermute | solution.py:288
  157.8 3.4 %collective-permute-start.34 = (f32[64,128]{1,0:T(8,128)S(1)}, f32[64,128]{1,0:T(8,128)S(1)}, u32[]{:S(2)}, u32[]{:S(2)}) collective-permute-start(f32[64,128]{1,0:T(8,128)S(1)} %solve_down.9.refs_0_.refs_8_), channel_id=1, source_target_pairs={{0,3},{1,2},{2,1},{3,0},{4,7},{5,6},{6,5},{7,4},{8,11},{9,10},{10,... | collective-permute-start | bytes 98312 | tf_op jit(solution)/shard_map/ppermute | solution.py:311
  157.9 4.2 %collective-permute-start.33 = (f32[64,128]{1,0:T(8,128)S(1)}, f32[64,128]{1,0:T(8,128)S(1)}, u32[]{:S(2)}, u32[]{:S(2)}) collective-permute-start(f32[64,128]{1,0:T(8,128)S(1)} %solve_down.9.refs_0_.refs_8_), channel_id=1, source_target_pairs={{0,2},{1,3},{2,0},{3,1},{4,6},{5,7},{6,4},{7,5},{8,10},{9,11},{10,... | collective-permute-start | bytes 98312 | tf_op jit(solution)/shard_map/ppermute | solution.py:311
  158.7 3.3 %collective-permute-start.32 = (f32[64,128]{1,0:T(8,128)S(1)}, f32[64,128]{1,0:T(8,128)S(1)}, u32[]{:S(2)}, u32[]{:S(2)}) collective-permute-start(f32[64,128]{1,0:T(8,128)S(1)} %solve_down.9.refs_0_.refs_8_), channel_id=1, source_target_pairs={{0,1},{1,0},{2,3},{3,2},{4,5},{5,4},{6,7},{7,6},{8,9},{9,8},{10,11... | collective-permute-start | bytes 98312 | tf_op jit(solution)/shard_map/ppermute | solution.py:311
  171.6 4.9 %collective-permute-start.35 = (f32[64,128]{1,0:T(8,128)S(1)}, f32[64,128]{1,0:T(8,128)S(1)}, u32[]{:S(2)}, u32[]{:S(2)}) collective-permute-start(f32[64,128]{1,0:T(8,128)S(1)} %get-tuple-element.81), channel_id=1, source_target_pairs={{0,16},{4,20},{8,24},{12,28},{16,0},{20,4},{24,8},{28,12},{1,17},{... | collective-permute-start | bytes 98312 | tf_op jit(solution)/shard_map/ppermute | solution.py:288
  176.7 3.4 %collective-permute-start.38 = (f32[64,128]{1,0:T(8,128)S(1)}, f32[64,128]{1,0:T(8,128)S(1)}, u32[]{:S(2)}, u32[]{:S(2)}) collective-permute-start(f32[64,128]{1,0:T(8,128)S(1)} %solve_down.10.refs_0_.refs_7_), channel_id=1, source_target_pairs={{0,3},{1,2},{2,1},{3,0},{4,7},{5,6},{6,5},{7,4},{8,11},{9,10},{10,... | collective-permute-start | bytes 98312 | tf_op jit(solution)/shard_map/ppermute | solution.py:311
  176.8 4.2 %collective-permute-start.37 = (f32[64,128]{1,0:T(8,128)S(1)}, f32[64,128]{1,0:T(8,128)S(1)}, u32[]{:S(2)}, u32[]{:S(2)}) collective-permute-start(f32[64,128]{1,0:T(8,128)S(1)} %solve_down.10.refs_0_.refs_7_), channel_id=1, source_target_pairs={{0,2},{1,3},{2,0},{3,1},{4,6},{5,7},{6,4},{7,5},{8,10},{9,11},{10,... | collective-permute-start | bytes 98312 | tf_op jit(solution)/shard_map/ppermute | solution.py:311
  177.6 3.3 %collective-permute-start.36 = (f32[64,128]{1,0:T(8,128)S(1)}, f32[64,128]{1,0:T(8,128)S(1)}, u32[]{:S(2)}, u32[]{:S(2)}) collective-permute-start(f32[64,128]{1,0:T(8,128)S(1)} %solve_down.10.refs_0_.refs_7_), channel_id=1, source_target_pairs={{0,1},{1,0},{2,3},{3,2},{4,5},{5,4},{6,7},{7,6},{8,9},{9,8},{10,11... | collective-permute-start | bytes 98312 | tf_op jit(solution)/shard_map/ppermute | solution.py:311
  190.6 4.9 %collective-permute-start.39 = (f32[64,128]{1,0:T(8,128)S(1)}, f32[64,128]{1,0:T(8,128)S(1)}, u32[]{:S(2)}, u32[]{:S(2)}) collective-permute-start(f32[64,128]{1,0:T(8,128)S(1)} %get-tuple-element.83), channel_id=1, source_target_pairs={{0,16},{4,20},{8,24},{12,28},{16,0},{20,4},{24,8},{28,12},{1,17},{... | collective-permute-start | bytes 98312 | tf_op jit(solution)/shard_map/ppermute | solution.py:288

commit v6 on v5

--- a/solution.py
+++ b/solution.py
@@ -31,7 +31,7 @@
     n_row, n_col, level, chunk, target_ref, source_ref, count_ref, place_ref, blocks_ref, *refs
 ):
     total, slots, arrived = refs[-3:]
-    count = count_ref[level]
+    count = count_ref[level, 0, 0]
     half = n_row // 2
     side = place_ref[0] // half
 
@@ -47,9 +47,10 @@
 
     def add(slot, carry):
         pl.when(lax.rem(slot, chunk) == 0)(fetch(slot // chunk).wait)
-        source = source_ref[level, slot]
-        below = lax.rem(source, half) * 2 + ((source // half) ^ side)
-        above = target_ref[level, slot] ^ place_ref[1]
+        source = source_ref[level, 0, 0, slot]
+        near = lax.rem(source, half) ^ lax.rem(place_ref[0], half)
+        below = near * 2 + ((source // half) ^ side)
+        above = target_ref[level, 0, 0, slot] ^ place_ref[1]
         total[below * n_col + above] += slots[slot]
         return carry
 
@@ -141,35 +142,36 @@
         return len(self.arrays) - 1, place
 
 
-def couple_kernel(transposed, terms, high_ref, low_ref, *refs):
+def couple_kernel(transposed, terms, span, high_ref, low_ref, *refs):
     n_in = 1 + max(number for number, _ in terms)
     ins, outs = refs[:n_in], refs[n_in:]
     block = ins[0].shape[-1]
     joined = jnp.concatenate([read(term, ins) for term in terms], axis=1)
-    result = product(halves(joined), (high_ref[...], low_ref[...]), transposed)
+    wanted = pl.ds(span[0] * block, (span[1] - span[0]) * block)
+    chosen = (wanted, slice(None)) if transposed else (slice(None), wanted)
+    result = product(halves(joined), (high_ref[chosen], low_ref[chosen]), transposed)
     pieces = [result[:, at : at + block] for at in range(0, result.shape[1], block)]
-    if len(outs) == 1:
-        write(outs[0], pieces)
-    else:
-        for ref, piece in zip(outs, pieces):
-            ref[...] = piece
-
-
-def couple(pieces, high, low, transposed):
+    each = len(pieces) // len(outs)
+    for number, ref in enumerate(outs):
+        write(ref, pieces[number * each : (number + 1) * each])
+
+
+def couple(pieces, high, low, transposed, span, each):
     operands = Operands()
     terms = [operands.term(piece) for piece in pieces]
     rows, block = operands.arrays[0].shape[-2:]
-    n_out = high.shape[0 if transposed else 1] // block
-    shapes = [(n_out, rows, block)] if transposed else [(rows, block)] * n_out
+    shape = (rows, block) if each == 1 else (each, rows, block)
+    n_out = (span[1] - span[0]) // each
     whole = pl.BlockSpec(memory_space=VMEM)
-    return pl.pallas_call(
-        functools.partial(couple_kernel, transposed, terms),
-        out_shape=[jax.ShapeDtypeStruct(shape, jnp.float32) for shape in shapes],
+    work = rows * block * block * len(terms) * (span[1] - span[0])
+    return pl.pallas_call(
+        functools.partial(couple_kernel, transposed, terms, span),
+        out_shape=[jax.ShapeDtypeStruct(shape, jnp.float32)] * n_out,
         in_specs=[whole] * (2 + len(operands.arrays)),
-        out_specs=[whole] * len(shapes),
+        out_specs=[whole] * n_out,
         compiler_params=pltpu.CompilerParams(vmem_limit_bytes=16 * MIB),
         cost_estimate=pl.CostEstimate(
-            flops=6 * rows * high.size, bytes_accessed=4 * high.size, transcendentals=0
+            flops=6 * work, bytes_accessed=4 * work // rows, transcendentals=0
         ),
         name="couple_up" if not transposed else "couple_down",
     )(high, low, *operands.arrays)
@@ -277,12 +279,6 @@
     )(*forward, *backward)
 
 
-def near_exchange(stacked, axis):
-    half = lax.axis_size(axis) // 2
-    groups = [list(range(half)), list(range(half, 2 * half))]
-    return lax.all_to_all(stacked, axis, 0, 0, axis_index_groups=groups, tiled=True)
-
-
 def far_exchange(segment, axis):
     size = lax.axis_size(axis)
     return lax.ppermute(segment, axis, [(i, i ^ (size // 2)) for i in range(size)])
@@ -291,27 +287,25 @@
 def gather_row(segment, after):
     half = lax.axis_size("row") // 2
     received = far_exchange(segment, "row")
-    (stacked,) = combine([[[(segment, None)], [(received, None)]] * half], after)
-    received = near_exchange(stacked, "row")
-    return [(received, place) for place in range(2 * half)]
-
-
-def deliver_row(stacked):
-    half = lax.axis_size("row") // 2
-    received = near_exchange(stacked, "row")
+    (both,) = combine([[[(segment, None)], [(received, None)]]], after)
+    messages = exchange_each([both] * half, "row")
+    return [(message, side) for message in messages for side in range(2)]
+
+
+def deliver_row(messages):
+    received = exchange_each(messages, "row")
     mine, other = combine(
-        [[[(received, 2 * place + side) for place in range(half)]] for side in range(2)]
+        [[[(message, side) for message in received]] for side in range(2)]
     )
     return [(mine, None), (far_exchange(other, "row"), None)]
 
 
 def exchange_each(messages, axis):
     size = lax.axis_size(axis)
-    received = [messages[0]] + [
-        lax.ppermute(messages[d], axis, [(i, i ^ d) for i in range(size)])
-        for d in range(1, size)
-    ]
-    return [(message, None) for message in received]
+    received = {0: messages[0]}
+    for d in reversed(range(1, len(messages))):
+        received[d] = lax.ppermute(messages[d], axis, [(i, i ^ d) for i in range(size)])
+    return [received[d] for d in range(len(messages))]
 
 
 def direct_shards(rhs, diag_inv, blocks, blk_target, blk_source, blk_count):
@@ -320,32 +314,33 @@
     right = rhs.reshape((levels,) + rhs.shape[-2:])
     inverse = diag_inv.reshape((levels,) + diag_inv.shape[-2:])
     weights = blocks.reshape((levels - 1,) + blocks.shape[-3:])
-    target = blk_target.reshape(levels - 1, -1)
-    source = blk_source.reshape(levels - 1, -1)
-    count = blk_count.reshape(levels - 1)
     place = jnp.stack([lax.axis_index("row"), lax.axis_index("col")]).astype(jnp.int32)
     gather = lambda level, after: gather_blocks(
-        level, target, source, count, place, weights, n_row, n_col, after
-    )
+        level, blk_target, blk_source, blk_count, place, weights, n_row, n_col, after
+    )
+    plain = lambda messages: [(message, None) for message in messages]
     forward = [first_solve(right, inverse)]
-    total = gather(0, forward[:1])
+    total = gather(0, ())
     coupling = []
     for level in range(1, levels):
-        coupling.append(split(total, n_row, n_col, forward[-1:]))
+        coupling.append(split(total, n_row, n_col, forward[-1:] if level > 1 else ()))
         pieces = gather_row(forward[-1], coupling[-1][:1])
-        partial = couple(pieces, *coupling[-1], False)
+        far = couple(pieces, *coupling[-1], False, (n_col // 2, n_col), 1)
+        near = couple(pieces, *coupling[-1], False, (0, n_col // 2), 1)
         after = ()
         if level < levels - 1:
-            total = gather(level, partial[:1])
+            total = gather(level, near[:1])
             after = (total,)
-        pieces = exchange_each(partial, "col")
+        pieces = plain(exchange_each(near + far, "col"))
         forward.append(solve(right, inverse, level, pieces, False, after))
     backward = [None] * levels
     backward[-1] = solve(forward[-1], inverse, levels - 1, [], True)
     for level in range(levels - 2, -1, -1):
-        pieces = exchange_each([backward[level + 1]] * n_col, "col")
-        (partial,) = couple(pieces, *coupling[level], True)
-        backward[level] = solve(forward[level], inverse, level, deliver_row(partial), True)
+        pieces = plain(exchange_each([backward[level + 1]] * n_col, "col"))
+        sent = couple(pieces, *coupling[level], True, (2, n_row), 2)
+        kept = couple(pieces, *coupling[level], True, (0, 2), 2)
+        pieces = deliver_row(kept + sent)
+        backward[level] = solve(forward[level], inverse, level, pieces, True)
     outs = stack(forward, backward)
     return tuple(out.reshape(rhs.shape) for out in outs)
 

time: 197 us -> 181 us (0.919)
  blocking collectives: 84.4 us -> 0 us
  starting transfers between devices: 26.4 us -> 62.3 us
  waiting for transfers between devices: 59.6 us -> 91.4 us
    all_to_all x10 -> x0, blocking collectives: 84.4 us -> none  [near_exchange(): lax.all_to_all(stacked, axis, 0, 0, axis_index_groups=groups, tiled=True)]
    ppermute x30 -> x60, starting transfers between devices: 19.3 us -> 56.2 us  [exchange_each(): lax.ppermute(messages[d], axis, [(i, i ^ d) for i in range(size)])]
    ppermute x30 -> x60, waiting for transfers between devices: 20 us -> 50.5 us  [exchange_each(): lax.ppermute(messages[d], axis, [(i, i ^ d) for i in range(size)])]
    pallas_call x10 -> x20, Pallas kernels: 8.5 us -> 9.75 us  [couple(): pl.pallas_call(functools.partial(couple_kernel, transposed, terms, span),...]
  transfers between devices with their start and end apart: 40 -> 70, of which waited for: 29 -> 57; matrix products, arithmetic and copies ran while one was open for 0% -> 0% of each run, Pallas kernels for 5% -> 7%
where the time goes in v6:
time: 181 us
  waiting for transfers between devices  91.4 us (50%)
  starting transfers between devices  62.3 us (34%)
  Pallas kernels  23.5 us (13%)
  local copies, waits for them, and re-layouts  2.14 us (1%)
    ppermute x60, starting transfers between devices, exchange_each(): lax.ppermute(messages[d], axis, [(i, i ^ d) for i in range(size)])  56.2 us
    ppermute x60, waiting for transfers between devices, exchange_each(): lax.ppermute(messages[d], axis, [(i, i ^ d) for i in range(size)])  50.5 us
    ppermute x10, waiting for transfers between devices, far_exchange(): lax.ppermute(segment, axis, [(i, i ^ size // 2) for i in range(size)])  41 us
    pallas_call x20, Pallas kernels, couple(): pl.pallas_call(functools.partial(couple_kernel, transposed, terms, span),...  9.75 us
    pallas_call x5, Pallas kernels, gather_blocks(): pl.pallas_call(functools.partial(gather_blocks_kernel, n_row, n_col, leve...  7.81 us
    ppermute x10, starting transfers between devices, far_exchange(): lax.ppermute(segment, axis, [(i, i ^ size // 2) for i in range(size)])  6.06 us
  transfers between devices with their start and end apart: 70, of which 57 were waited for; matrix products, arithmetic and copies ran while one was open for 0% of the time, Pallas kernels for 7%

profile of v6, /device:TPU:0, one launch (start us, length us, event | category | flops | bytes accessed | tf_op | source)
XLA Modules:
  0.0 180.6 jit_solution(6838534190019003448)
XLA Ops:
  0.6 1.7 first_solve.1.refs_0_
  2.3 4.1 %collective-permute-start = (f32[64,128]{1,0:T(8,128)}, f32[64,128]{1,0:T(8,128)S(1)}, u32[]{:S(2)}, u32[]{:S(2)}) collective-permute-start(f32[64,128]{1,0:T(8,128)} %first_solve.1.refs_0_), channel_id=1, source_target_pairs={{0,16},{4,20},{8,24},{12,28},{16,0},{20,4},{24,8},{28,12},{1,17},{... | collective-permute-start | bytes 98312 | tf_op jit(solution)/shard_map/ppermute | solution.py:284
  8.6 2.4 %gather_blocks_0.1.total_ref = f32[32,128,128]{2,1,0:T(8,128)S(1)} custom-call(s32[5,1,1,32]{3,2,1,0:T(1,128)S(1)} %copy-done.3, s32[5,1,1,32]{3,2,1,0:T(1,128)S(1)} %copy-done.5, s32[5,1,1]{2,1,0:T(1,128)S(1)} %copy.8.count_ref, s32[2]{0:T(128)S(1)} %pad_add_fusion.place_ref, f32[5,32,128,128]{3,2,1,0:T(8,128)} %bitcast.11), custom_call_target="tpu_custom_call" | custom-call | flops 524288 | bytes 4194304 | tf_op jit(solution)/shard_map/gather_blocks_0/pallas_call | solution.py:65
  11.4 2.7 %collective-permute-start.3 = (f32[2,64,128]{2,1,0:T(8,128)S(1)}, f32[2,64,128]{2,1,0:T(8,128)S(1)}, u32[]{:S(2)}, u32[]{:S(2)}) collective-permute-start(f32[2,64,128]{2,1,0:T(8,128)S(1)} %combine.10.refs_0_), channel_id=1, source_target_pairs={{0,12},{4,8},{8,4},{12,0},{16,28},{20,24},{24,20},{28,16},{1,13},{... | collective-permute-start | bytes 196616 | tf_op jit(solution)/shard_map/ppermute | solution.py:307
  15.0 2.2 %collective-permute-done.3.refs_3_ = f32[2,64,128]{2,1,0:T(8,128)S(1)} collective-permute-done((f32[2,64,128]{2,1,0:T(8,128)S(1)}, f32[2,64,128]{2,1,0:T(8,128)S(1)}, u32[]{:S(2)}, u32[]{:S(2)}) %collective-permute-start.3) | collective-permute-done | bytes 65568 | tf_op jit(solution)/shard_map/ppermute | solution.py:307
  17.2 1.2 collective-permute-done.2.refs_2_
  19.1 1.7 collective-permute-start.5
  21.9 1.3 gather_blocks_1.1.refs_6_.total_ref
  24.8 4.4 %collective-permute-done.7.refs_1_ = f32[64,128]{1,0:T(8,128)S(1)} collective-permute-done((f32[64,128]{1,0:T(8,128)S(1)}, f32[64,128]{1,0:T(8,128)S(1)}, u32[]{:S(2)}, u32[]{:S(2)}) %collective-permute-start.7) | collective-permute-done | bytes 32800 | tf_op jit(solution)/shard_map/ppermute | solution.py:284
  29.2 1.5 collective-permute-start.10
  31.2 1.5 collective-permute-start.8
  32.7 1.7 collective-permute-done.10.refs_3_
  35.9 1.3 collective-permute-start.12
  38.6 1.2 gather_blocks_2.1.refs_6_.total_ref
  41.3 4.6 %collective-permute-done.14.refs_1_ = f32[64,128]{1,0:T(8,128)S(1)} collective-permute-done((f32[64,128]{1,0:T(8,128)S(1)}, f32[64,128]{1,0:T(8,128)S(1)}, u32[]{:S(2)}, u32[]{:S(2)}) %collective-permute-start.14) | collective-permute-done | bytes 32800 | tf_op jit(solution)/shard_map/ppermute | solution.py:284
  46.0 2.0 %collective-permute-start.17 = (f32[2,64,128]{2,1,0:T(8,128)S(1)}, f32[2,64,128]{2,1,0:T(8,128)S(1)}, u32[]{:S(2)}, u32[]{:S(2)}) collective-permute-start(f32[2,64,128]{2,1,0:T(8,128)S(1)} %combine.12.refs_0_), channel_id=1, source_target_pairs={{0,12},{4,8},{8,4},{12,0},{16,28},{20,24},{24,20},{28,16},{1,13},{... | collective-permute-start | bytes 196616 | tf_op jit(solution)/shard_map/ppermute | solution.py:307
  49.5 1.7 collective-permute-done.17.refs_3_
  51.1 1.1 collective-permute-done.16.refs_2_
  54.8 1.5 collective-permute-start.18
  56.2 1.4 gather_blocks_3.1.refs_6_.total_ref
  58.7 4.5 %collective-permute-done.21.refs_1_ = f32[64,128]{1,0:T(8,128)S(1)} collective-permute-done((f32[64,128]{1,0:T(8,128)S(1)}, f32[64,128]{1,0:T(8,128)S(1)}, u32[]{:S(2)}, u32[]{:S(2)}) %collective-permute-start.21) | collective-permute-done | bytes 32800 | tf_op jit(solution)/shard_map/ppermute | solution.py:284
  63.1 1.2 collective-permute-start.24
  65.3 1.3 collective-permute-start.22
  66.6 1.7 collective-permute-done.24.refs_3_
  71.4 1.3 collective-permute-start.25
  72.7 1.4 gather_blocks_4.1.refs_6_.total_ref
  75.2 4.5 %collective-permute-done.28.refs_1_ = f32[64,128]{1,0:T(8,128)S(1)} collective-permute-done((f32[64,128]{1,0:T(8,128)S(1)}, f32[64,128]{1,0:T(8,128)S(1)}, u32[]{:S(2)}, u32[]{:S(2)}) %collective-permute-start.28) | collective-permute-done | bytes 32800 | tf_op jit(solution)/shard_map/ppermute | solution.py:284
  79.7 2.1 %collective-permute-start.31 = (f32[2,64,128]{2,1,0:T(8,128)S(1)}, f32[2,64,128]{2,1,0:T(8,128)S(1)}, u32[]{:S(2)}, u32[]{:S(2)}) collective-permute-start(f32[2,64,128]{2,1,0:T(8,128)S(1)} %combine.14.refs_0_), channel_id=1, source_target_pairs={{0,12},{4,8},{8,4},{12,0},{16,28},{20,24},{24,20},{28,16},{1,13},{... | collective-permute-start | bytes 196616 | tf_op jit(solution)/shard_map/ppermute | solution.py:307
  83.2 1.7 collective-permute-done.31.refs_3_
  84.9 1.2 collective-permute-done.30.refs_2_
  87.4 1.2 collective-permute-start.33
  88.9 1.1 collective-permute-start.32
  90.0 1.3 collective-permute-done.33.refs_4_
  94.3 1.7 collective-permute-done.37.refs_3_
  96.0 1.2 collective-permute-done.36.refs_2_
  99.6 2.0 %collective-permute-start.40 = (f32[2,64,128]{2,1,0:T(8,128)S(1)}, f32[2,64,128]{2,1,0:T(8,128)S(1)}, u32[]{:S(2)}, u32[]{:S(2)}) collective-permute-start(f32[2,64,128]{2,1,0:T(8,128)S(1)} %get-tuple-element.91), channel_id=1, source_target_pairs={{0,12},{4,8},{8,4},{12,0},{16,28},{20,24},{24,20},{28,16},{1,13},{... | collective-permute-start | bytes 196616 | tf_op jit(solution)/shard_map/ppermute | solution.py:307
  101.9 1.1 collective-permute-done.38.refs_1_
  103.2 1.5 collective-permute-done.40.refs_3_
  105.3 4.3 %collective-permute-done.41.refs_3_ = f32[64,128]{1,0:T(8,128)S(1)} collective-permute-done((f32[64,128]{1,0:T(8,128)S(1)}, f32[64,128]{1,0:T(8,128)S(1)}, u32[]{:S(2)}, u32[]{:S(2)}) %collective-permute-start.41) | collective-permute-done | bytes 32800 | tf_op jit(solution)/shard_map/ppermute | solution.py:284
  109.9 1.1 collective-permute-start.43
  111.7 1.5 collective-permute-done.44.refs_3_
  115.0 1.5 collective-permute-start.45
  116.5 1.1 collective-permute-start.46
  119.3 1.7 collective-permute-done.46.refs_2_
  121.0 1.8 collective-permute-done.47.refs_3_
  122.9 4.8 %collective-permute-done.48.refs_3_ = f32[64,128]{1,0:T(8,128)S(1)} collective-permute-done((f32[64,128]{1,0:T(8,128)S(1)}, f32[64,128]{1,0:T(8,128)S(1)}, u32[]{:S(2)}, u32[]{:S(2)}) %collective-permute-start.48) | collective-permute-done | bytes 32800 | tf_op jit(solution)/shard_map/ppermute | solution.py:284
  129.8 1.5 collective-permute-done.51.refs_3_
  133.4 1.3 collective-permute-start.53
  134.6 1.8 %collective-permute-start.54 = (f32[2,64,128]{2,1,0:T(8,128)S(1)}, f32[2,64,128]{2,1,0:T(8,128)S(1)}, u32[]{:S(2)}, u32[]{:S(2)}) collective-permute-start(f32[2,64,128]{2,1,0:T(8,128)S(1)} %get-tuple-element.101), channel_id=1, source_target_pairs={{0,12},{4,8},{8,4},{12,0},{16,28},{20,24},{24,20},{28,16},{1,13},{... | collective-permute-start | bytes 196616 | tf_op jit(solution)/shard_map/ppermute | solution.py:307
  137.8 2.0 %collective-permute-done.54.refs_3_ = f32[2,64,128]{2,1,0:T(8,128)S(1)} collective-permute-done((f32[2,64,128]{2,1,0:T(8,128)S(1)}, f32[2,64,128]{2,1,0:T(8,128)S(1)}, u32[]{:S(2)}, u32[]{:S(2)}) %collective-permute-start.54) | collective-permute-done | bytes 65568 | tf_op jit(solution)/shard_map/ppermute | solution.py:307
  140.3 4.4 %collective-permute-done.55.refs_3_ = f32[64,128]{1,0:T(8,128)S(1)} collective-permute-done((f32[64,128]{1,0:T(8,128)S(1)}, f32[64,128]{1,0:T(8,128)S(1)}, u32[]{:S(2)}, u32[]{:S(2)}) %collective-permute-start.55) | collective-permute-done | bytes 32800 | tf_op jit(solution)/shard_map/ppermute | solution.py:284
  146.8 1.5 collective-permute-done.58.refs_3_
  150.0 1.1 collective-permute-start.59
  151.2 1.1 collective-permute-start.60
  152.2 1.4 collective-permute-start.61
  154.4 1.5 collective-permute-done.60.refs_2_
  155.9 1.5 collective-permute-done.61.refs_3_
  157.6 4.7 %collective-permute-done.62.refs_3_ = f32[64,128]{1,0:T(8,128)S(1)} collective-permute-done((f32[64,128]{1,0:T(8,128)S(1)}, f32[64,128]{1,0:T(8,128)S(1)}, u32[]{:S(2)}, u32[]{:S(2)}) %collective-permute-start.62) | collective-permute-done | bytes 32800 | tf_op jit(solution)/shard_map/ppermute | solution.py:284
  163.2 1.2 collective-permute-start.63
  164.4 1.5 collective-permute-done.65.refs_3_
  168.1 1.5 collective-permute-start.67
  169.6 1.4 collective-permute-start.68
  172.6 2.1 %collective-permute-done.68.refs_3_ = f32[2,64,128]{2,1,0:T(8,128)S(1)} collective-permute-done((f32[2,64,128]{2,1,0:T(8,128)S(1)}, f32[2,64,128]{2,1,0:T(8,128)S(1)}, u32[]{:S(2)}, u32[]{:S(2)}) %collective-permute-start.68) | collective-permute-done | bytes 65568 | tf_op jit(solution)/shard_map/ppermute | solution.py:307
  174.9 4.7 %collective-permute-done.69.refs_3_ = f32[64,128]{1,0:T(8,128)S(1)} collective-permute-done((f32[64,128]{1,0:T(8,128)S(1)}, f32[64,128]{1,0:T(8,128)S(1)}, u32[]{:S(2)}, u32[]{:S(2)}) %collective-permute-start.69) | collective-permute-done | bytes 32800 | tf_op jit(solution)/shard_map/ppermute | solution.py:284
  (152 shorter events, 52.4 us)
Async XLA Ops:
  2.3 9.1 %collective-permute-start = (f32[64,128]{1,0:T(8,128)}, f32[64,128]{1,0:T(8,128)S(1)}, u32[]{:S(2)}, u32[]{:S(2)}) collective-permute-start(f32[64,128]{1,0:T(8,128)} %first_solve.1.refs_0_), channel_id=1, source_target_pairs={{0,16},{4,20},{8,24},{12,28},{16,0},{20,4},{24,8},{28,12},{1,17},{... | collective-permute-start | bytes 98312 | tf_op jit(solution)/shard_map/ppermute | solution.py:284
  11.4 5.8 %collective-permute-start.3 = (f32[2,64,128]{2,1,0:T(8,128)S(1)}, f32[2,64,128]{2,1,0:T(8,128)S(1)}, u32[]{:S(2)}, u32[]{:S(2)}) collective-permute-start(f32[2,64,128]{2,1,0:T(8,128)S(1)} %combine.10.refs_0_), channel_id=1, source_target_pairs={{0,12},{4,8},{8,4},{12,0},{16,28},{20,24},{24,20},{28,16},{1,13},{... | collective-permute-start | bytes 196616 | tf_op jit(solution)/shard_map/ppermute | solution.py:307
  14.1 4.3 %collective-permute-start.2 = (f32[2,64,128]{2,1,0:T(8,128)S(1)}, f32[2,64,128]{2,1,0:T(8,128)S(1)}, u32[]{:S(2)}, u32[]{:S(2)}) collective-permute-start(f32[2,64,128]{2,1,0:T(8,128)S(1)} %combine.10.refs_0_), channel_id=1, source_target_pairs={{0,8},{4,12},{8,0},{12,4},{16,24},{20,28},{24,16},{28,20},{1,9},{5... | collective-permute-start | bytes 196616 | tf_op jit(solution)/shard_map/ppermute | solution.py:307
  14.5 4.3 %collective-permute-start.1 = (f32[2,64,128]{2,1,0:T(8,128)S(1)}, f32[2,64,128]{2,1,0:T(8,128)S(1)}, u32[]{:S(2)}, u32[]{:S(2)}) collective-permute-start(f32[2,64,128]{2,1,0:T(8,128)S(1)} %combine.10.refs_0_), channel_id=1, source_target_pairs={{0,4},{4,0},{8,12},{12,8},{16,20},{20,16},{24,28},{28,24},{1,5},{5... | collective-permute-start | bytes 196616 | tf_op jit(solution)/shard_map/ppermute | solution.py:307
  19.1 4.1 %collective-permute-start.5 = (f32[64,128]{1,0:T(8,128)S(1)}, f32[64,128]{1,0:T(8,128)S(1)}, u32[]{:S(2)}, u32[]{:S(2)}) collective-permute-start(f32[64,128]{1,0:T(8,128)S(1)} %get-tuple-element.63), channel_id=1, source_target_pairs={{0,2},{1,3},{2,0},{3,1},{4,6},{5,7},{6,4},{7,5},{8,10},{9,11},{10,... | collective-permute-start | bytes 98312 | tf_op jit(solution)/shard_map/ppermute | solution.py:307
  20.8 3.3 %collective-permute-start.6 = (f32[64,128]{1,0:T(8,128)S(1)}, f32[64,128]{1,0:T(8,128)S(1)}, u32[]{:S(2)}, u32[]{:S(2)}) collective-permute-start(f32[64,128]{1,0:T(8,128)S(1)} %get-tuple-element.64), channel_id=1, source_target_pairs={{0,3},{1,2},{2,1},{3,0},{4,7},{5,6},{6,5},{7,4},{8,11},{9,10},{10,... | collective-permute-start | bytes 98312 | tf_op jit(solution)/shard_map/ppermute | solution.py:307
  24.3 4.9 %collective-permute-start.7 = (f32[64,128]{1,0:T(8,128)S(1)}, f32[64,128]{1,0:T(8,128)S(1)}, u32[]{:S(2)}, u32[]{:S(2)}) collective-permute-start(f32[64,128]{1,0:T(8,128)S(1)} %solve_up.5.refs_0_.refs_1_), channel_id=1, source_target_pairs={{0,16},{4,20},{8,24},{12,28},{16,0},{20,4},{24,8},{28,12},{1,17},{... | collective-permute-start | bytes 98312 | tf_op jit(solution)/shard_map/ppermute | solution.py:284
  29.2 5.2 %collective-permute-start.10 = (f32[2,64,128]{2,1,0:T(8,128)S(1)}, f32[2,64,128]{2,1,0:T(8,128)S(1)}, u32[]{:S(2)}, u32[]{:S(2)}) collective-permute-start(f32[2,64,128]{2,1,0:T(8,128)S(1)} %combine.11.refs_0_), channel_id=1, source_target_pairs={{0,12},{4,8},{8,4},{12,0},{16,28},{20,24},{24,20},{28,16},{1,13},{... | collective-permute-start | bytes 196616 | tf_op jit(solution)/shard_map/ppermute | solution.py:307
  30.8 4.3 %collective-permute-start.9 = (f32[2,64,128]{2,1,0:T(8,128)S(1)}, f32[2,64,128]{2,1,0:T(8,128)S(1)}, u32[]{:S(2)}, u32[]{:S(2)}) collective-permute-start(f32[2,64,128]{2,1,0:T(8,128)S(1)} %combine.11.refs_0_), channel_id=1, source_target_pairs={{0,8},{4,12},{8,0},{12,4},{16,24},{20,28},{24,16},{28,20},{1,9},{5... | collective-permute-start | bytes 196616 | tf_op jit(solution)/shard_map/ppermute | solution.py:307
  31.2 4.3 %collective-permute-start.8 = (f32[2,64,128]{2,1,0:T(8,128)S(1)}, f32[2,64,128]{2,1,0:T(8,128)S(1)}, u32[]{:S(2)}, u32[]{:S(2)}) collective-permute-start(f32[2,64,128]{2,1,0:T(8,128)S(1)} %combine.11.refs_0_), channel_id=1, source_target_pairs={{0,4},{4,0},{8,12},{12,8},{16,20},{20,16},{24,28},{28,24},{1,5},{5... | collective-permute-start | bytes 196616 | tf_op jit(solution)/shard_map/ppermute | solution.py:307
  35.9 4.0 %collective-permute-start.12 = (f32[64,128]{1,0:T(8,128)S(1)}, f32[64,128]{1,0:T(8,128)S(1)}, u32[]{:S(2)}, u32[]{:S(2)}) collective-permute-start(f32[64,128]{1,0:T(8,128)S(1)} %get-tuple-element.69), channel_id=1, source_target_pairs={{0,2},{1,3},{2,0},{3,1},{4,6},{5,7},{6,4},{7,5},{8,10},{9,11},{10,... | collective-permute-start | bytes 98312 | tf_op jit(solution)/shard_map/ppermute | solution.py:307
  37.2 3.4 %collective-permute-start.13 = (f32[64,128]{1,0:T(8,128)S(1)}, f32[64,128]{1,0:T(8,128)S(1)}, u32[]{:S(2)}, u32[]{:S(2)}) collective-permute-start(f32[64,128]{1,0:T(8,128)S(1)} %get-tuple-element.70), channel_id=1, source_target_pairs={{0,3},{1,2},{2,1},{3,0},{4,7},{5,6},{6,5},{7,4},{8,11},{9,10},{10,... | collective-permute-start | bytes 98312 | tf_op jit(solution)/shard_map/ppermute | solution.py:307
  40.7 5.2 %collective-permute-start.14 = (f32[64,128]{1,0:T(8,128)S(1)}, f32[64,128]{1,0:T(8,128)S(1)}, u32[]{:S(2)}, u32[]{:S(2)}) collective-permute-start(f32[64,128]{1,0:T(8,128)S(1)} %solve_up.6.refs_0_.refs_2_), channel_id=1, source_target_pairs={{0,16},{4,20},{8,24},{12,28},{16,0},{20,4},{24,8},{28,12},{1,17},{... | collective-permute-start | bytes 98312 | tf_op jit(solution)/shard_map/ppermute | solution.py:284
  46.0 5.2 %collective-permute-start.17 = (f32[2,64,128]{2,1,0:T(8,128)S(1)}, f32[2,64,128]{2,1,0:T(8,128)S(1)}, u32[]{:S(2)}, u32[]{:S(2)}) collective-permute-start(f32[2,64,128]{2,1,0:T(8,128)S(1)} %combine.12.refs_0_), channel_id=1, source_target_pairs={{0,12},{4,8},{8,4},{12,0},{16,28},{20,24},{24,20},{28,16},{1,13},{... | collective-permute-start | bytes 196616 | tf_op jit(solution)/shard_map/ppermute | solution.py:307
  48.0 4.3 %collective-permute-start.16 = (f32[2,64,128]{2,1,0:T(8,128)S(1)}, f32[2,64,128]{2,1,0:T(8,128)S(1)}, u32[]{:S(2)}, u32[]{:S(2)}) collective-permute-start(f32[2,64,128]{2,1,0:T(8,128)S(1)} %combine.12.refs_0_), channel_id=1, source_target_pairs={{0,8},{4,12},{8,0},{12,4},{16,24},{20,28},{24,16},{28,20},{1,9},{5... | collective-permute-start | bytes 196616 | tf_op jit(solution)/shard_map/ppermute | solution.py:307
  48.9 4.3 %collective-permute-start.15 = (f32[2,64,128]{2,1,0:T(8,128)S(1)}, f32[2,64,128]{2,1,0:T(8,128)S(1)}, u32[]{:S(2)}, u32[]{:S(2)}) collective-permute-start(f32[2,64,128]{2,1,0:T(8,128)S(1)} %combine.12.refs_0_), channel_id=1, source_target_pairs={{0,4},{4,0},{8,12},{12,8},{16,20},{20,16},{24,28},{28,24},{1,5},{5... | collective-permute-start | bytes 196616 | tf_op jit(solution)/shard_map/ppermute | solution.py:307
  53.6 4.2 %collective-permute-start.19 = (f32[64,128]{1,0:T(8,128)S(1)}, f32[64,128]{1,0:T(8,128)S(1)}, u32[]{:S(2)}, u32[]{:S(2)}) collective-permute-start(f32[64,128]{1,0:T(8,128)S(1)} %get-tuple-element.75), channel_id=1, source_target_pairs={{0,2},{1,3},{2,0},{3,1},{4,6},{5,7},{6,4},{7,5},{8,10},{9,11},{10,... | collective-permute-start | bytes 98312 | tf_op jit(solution)/shard_map/ppermute | solution.py:307
  54.4 3.7 %collective-permute-start.20 = (f32[64,128]{1,0:T(8,128)S(1)}, f32[64,128]{1,0:T(8,128)S(1)}, u32[]{:S(2)}, u32[]{:S(2)}) collective-permute-start(f32[64,128]{1,0:T(8,128)S(1)} %get-tuple-element.76), channel_id=1, source_target_pairs={{0,3},{1,2},{2,1},{3,0},{4,7},{5,6},{6,5},{7,4},{8,11},{9,10},{10,... | collective-permute-start | bytes 98312 | tf_op jit(solution)/shard_map/ppermute | solution.py:307
  54.8 3.3 %collective-permute-start.18 = (f32[64,128]{1,0:T(8,128)S(1)}, f32[64,128]{1,0:T(8,128)S(1)}, u32[]{:S(2)}, u32[]{:S(2)}) collective-permute-start(f32[64,128]{1,0:T(8,128)S(1)} %get-tuple-element.74), channel_id=1, source_target_pairs={{0,1},{1,0},{2,3},{3,2},{4,5},{5,4},{6,7},{7,6},{8,9},{9,8},{10,11... | collective-permute-start | bytes 98312 | tf_op jit(solution)/shard_map/ppermute | solution.py:307
  58.2 4.9 %collective-permute-start.21 = (f32[64,128]{1,0:T(8,128)S(1)}, f32[64,128]{1,0:T(8,128)S(1)}, u32[]{:S(2)}, u32[]{:S(2)}) collective-permute-start(f32[64,128]{1,0:T(8,128)S(1)} %solve_up.7.refs_0_.refs_3_), channel_id=1, source_target_pairs={{0,16},{4,20},{8,24},{12,28},{16,0},{20,4},{24,8},{28,12},{1,17},{... | collective-permute-start | bytes 98312 | tf_op jit(solution)/shard_map/ppermute | solution.py:284
  63.1 5.2 %collective-permute-start.24 = (f32[2,64,128]{2,1,0:T(8,128)S(1)}, f32[2,64,128]{2,1,0:T(8,128)S(1)}, u32[]{:S(2)}, u32[]{:S(2)}) collective-permute-start(f32[2,64,128]{2,1,0:T(8,128)S(1)} %combine.13.refs_0_), channel_id=1, source_target_pairs={{0,12},{4,8},{8,4},{12,0},{16,28},{20,24},{24,20},{28,16},{1,13},{... | collective-permute-start | bytes 196616 | tf_op jit(solution)/shard_map/ppermute | solution.py:307
  64.4 4.3 %collective-permute-start.23 = (f32[2,64,128]{2,1,0:T(8,128)S(1)}, f32[2,64,128]{2,1,0:T(8,128)S(1)}, u32[]{:S(2)}, u32[]{:S(2)}) collective-permute-start(f32[2,64,128]{2,1,0:T(8,128)S(1)} %combine.13.refs_0_), channel_id=1, source_target_pairs={{0,8},{4,12},{8,0},{12,4},{16,24},{20,28},{24,16},{28,20},{1,9},{5... | collective-permute-start | bytes 196616 | tf_op jit(solution)/shard_map/ppermute | solution.py:307
  65.3 4.3 %collective-permute-start.22 = (f32[2,64,128]{2,1,0:T(8,128)S(1)}, f32[2,64,128]{2,1,0:T(8,128)S(1)}, u32[]{:S(2)}, u32[]{:S(2)}) collective-permute-start(f32[2,64,128]{2,1,0:T(8,128)S(1)} %combine.13.refs_0_), channel_id=1, source_target_pairs={{0,4},{4,0},{8,12},{12,8},{16,20},{20,16},{24,28},{28,24},{1,5},{5... | collective-permute-start | bytes 196616 | tf_op jit(solution)/shard_map/ppermute | solution.py:307
  70.0 4.1 %collective-permute-start.26 = (f32[64,128]{1,0:T(8,128)S(1)}, f32[64,128]{1,0:T(8,128)S(1)}, u32[]{:S(2)}, u32[]{:S(2)}) collective-permute-start(f32[64,128]{1,0:T(8,128)S(1)} %get-tuple-element.81), channel_id=1, source_target_pairs={{0,2},{1,3},{2,0},{3,1},{4,6},{5,7},{6,4},{7,5},{8,10},{9,11},{10,... | collective-permute-start | bytes 98312 | tf_op jit(solution)/shard_map/ppermute | solution.py:307
  71.0 3.7 %collective-permute-start.27 = (f32[64,128]{1,0:T(8,128)S(1)}, f32[64,128]{1,0:T(8,128)S(1)}, u32[]{:S(2)}, u32[]{:S(2)}) collective-permute-start(f32[64,128]{1,0:T(8,128)S(1)} %get-tuple-element.82), channel_id=1, source_target_pairs={{0,3},{1,2},{2,1},{3,0},{4,7},{5,6},{6,5},{7,4},{8,11},{9,10},{10,... | collective-permute-start | bytes 98312 | tf_op jit(solution)/shard_map/ppermute | solution.py:307
  74.8 4.9 %collective-permute-start.28 = (f32[64,128]{1,0:T(8,128)S(1)}, f32[64,128]{1,0:T(8,128)S(1)}, u32[]{:S(2)}, u32[]{:S(2)}) collective-permute-start(f32[64,128]{1,0:T(8,128)S(1)} %solve_up.8.refs_0_.refs_4_), channel_id=1, source_target_pairs={{0,16},{4,20},{8,24},{12,28},{16,0},{20,4},{24,8},{28,12},{1,17},{... | collective-permute-start | bytes 98312 | tf_op jit(solution)/shard_map/ppermute | solution.py:284
  79.7 5.2 %collective-permute-start.31 = (f32[2,64,128]{2,1,0:T(8,128)S(1)}, f32[2,64,128]{2,1,0:T(8,128)S(1)}, u32[]{:S(2)}, u32[]{:S(2)}) collective-permute-start(f32[2,64,128]{2,1,0:T(8,128)S(1)} %combine.14.refs_0_), channel_id=1, source_target_pairs={{0,12},{4,8},{8,4},{12,0},{16,28},{20,24},{24,20},{28,16},{1,13},{... | collective-permute-start | bytes 196616 | tf_op jit(solution)/shard_map/ppermute | solution.py:307
  81.8 4.3 %collective-permute-start.30 = (f32[2,64,128]{2,1,0:T(8,128)S(1)}, f32[2,64,128]{2,1,0:T(8,128)S(1)}, u32[]{:S(2)}, u32[]{:S(2)}) collective-permute-start(f32[2,64,128]{2,1,0:T(8,128)S(1)} %combine.14.refs_0_), channel_id=1, source_target_pairs={{0,8},{4,12},{8,0},{12,4},{16,24},{20,28},{24,16},{28,20},{1,9},{5... | collective-permute-start | bytes 196616 | tf_op jit(solution)/shard_map/ppermute | solution.py:307
  82.7 4.3 %collective-permute-start.29 = (f32[2,64,128]{2,1,0:T(8,128)S(1)}, f32[2,64,128]{2,1,0:T(8,128)S(1)}, u32[]{:S(2)}, u32[]{:S(2)}) collective-permute-start(f32[2,64,128]{2,1,0:T(8,128)S(1)} %combine.14.refs_0_), channel_id=1, source_target_pairs={{0,4},{4,0},{8,12},{12,8},{16,20},{20,16},{24,28},{28,24},{1,5},{5... | collective-permute-start | bytes 196616 | tf_op jit(solution)/shard_map/ppermute | solution.py:307
  87.4 4.0 %collective-permute-start.33 = (f32[64,128]{1,0:T(8,128)S(1)}, f32[64,128]{1,0:T(8,128)S(1)}, u32[]{:S(2)}, u32[]{:S(2)}) collective-permute-start(f32[64,128]{1,0:T(8,128)S(1)} %get-tuple-element.87), channel_id=1, source_target_pairs={{0,2},{1,3},{2,0},{3,1},{4,6},{5,7},{6,4},{7,5},{8,10},{9,11},{10,... | collective-permute-start | bytes 98312 | tf_op jit(solution)/shard_map/ppermute | solution.py:307
  88.5 3.5 %collective-permute-start.34 = (f32[64,128]{1,0:T(8,128)S(1)}, f32[64,128]{1,0:T(8,128)S(1)}, u32[]{:S(2)}, u32[]{:S(2)}) collective-permute-start(f32[64,128]{1,0:T(8,128)S(1)} %get-tuple-element.88), channel_id=1, source_target_pairs={{0,3},{1,2},{2,1},{3,0},{4,7},{5,6},{6,5},{7,4},{8,11},{9,10},{10,... | collective-permute-start | bytes 98312 | tf_op jit(solution)/shard_map/ppermute | solution.py:307
  92.4 3.6 %collective-permute-start.37 = (f32[64,128]{1,0:T(8,128)S(1)}, f32[64,128]{1,0:T(8,128)S(1)}, u32[]{:S(2)}, u32[]{:S(2)}) collective-permute-start(f32[64,128]{1,0:T(8,128)S(1)} %solve_down.6.refs_0_.refs_11_), channel_id=1, source_target_pairs={{0,3},{1,2},{2,1},{3,0},{4,7},{5,6},{6,5},{7,4},{8,11},{9,10},{10,... | collective-permute-start | bytes 98312 | tf_op jit(solution)/shard_map/ppermute | solution.py:307
  93.3 3.9 %collective-permute-start.36 = (f32[64,128]{1,0:T(8,128)S(1)}, f32[64,128]{1,0:T(8,128)S(1)}, u32[]{:S(2)}, u32[]{:S(2)}) collective-permute-start(f32[64,128]{1,0:T(8,128)S(1)} %solve_down.6.refs_0_.refs_11_), channel_id=1, source_target_pairs={{0,2},{1,3},{2,0},{3,1},{4,6},{5,7},{6,4},{7,5},{8,10},{9,11},{10,... | collective-permute-start | bytes 98312 | tf_op jit(solution)/shard_map/ppermute | solution.py:307
  98.0 5.0 %collective-permute-start.38 = (f32[2,64,128]{2,1,0:T(8,128)S(1)}, f32[2,64,128]{2,1,0:T(8,128)S(1)}, u32[]{:S(2)}, u32[]{:S(2)}) collective-permute-start(f32[2,64,128]{2,1,0:T(8,128)S(1)} %get-tuple-element.89), channel_id=1, source_target_pairs={{0,4},{4,0},{8,12},{12,8},{16,20},{20,16},{24,28},{28,24},{1,5},{5... | collective-permute-start | bytes 196616 | tf_op jit(solution)/shard_map/ppermute | solution.py:307
  98.5 4.7 %collective-permute-start.39 = (f32[2,64,128]{2,1,0:T(8,128)S(1)}, f32[2,64,128]{2,1,0:T(8,128)S(1)}, u32[]{:S(2)}, u32[]{:S(2)}) collective-permute-start(f32[2,64,128]{2,1,0:T(8,128)S(1)} %get-tuple-element.90), channel_id=1, source_target_pairs={{0,8},{4,12},{8,0},{12,4},{16,24},{20,28},{24,16},{28,20},{1,9},{5... | collective-permute-start | bytes 196616 | tf_op jit(solution)/shard_map/ppermute | solution.py:307
  99.6 5.2 %collective-permute-start.40 = (f32[2,64,128]{2,1,0:T(8,128)S(1)}, f32[2,64,128]{2,1,0:T(8,128)S(1)}, u32[]{:S(2)}, u32[]{:S(2)}) collective-permute-start(f32[2,64,128]{2,1,0:T(8,128)S(1)} %get-tuple-element.91), channel_id=1, source_target_pairs={{0,12},{4,8},{8,4},{12,0},{16,28},{20,24},{24,20},{28,16},{1,13},{... | collective-permute-start | bytes 196616 | tf_op jit(solution)/shard_map/ppermute | solution.py:307
  104.7 4.9 %collective-permute-start.41 = (f32[64,128]{1,0:T(8,128)S(1)}, f32[64,128]{1,0:T(8,128)S(1)}, u32[]{:S(2)}, u32[]{:S(2)}) collective-permute-start(f32[64,128]{1,0:T(8,128)S(1)} %get-tuple-element.93), channel_id=1, source_target_pairs={{0,16},{4,20},{8,24},{12,28},{16,0},{20,4},{24,8},{28,12},{1,17},{... | collective-permute-start | bytes 98312 | tf_op jit(solution)/shard_map/ppermute | solution.py:284
  109.8 3.4 %collective-permute-start.44 = (f32[64,128]{1,0:T(8,128)S(1)}, f32[64,128]{1,0:T(8,128)S(1)}, u32[]{:S(2)}, u32[]{:S(2)}) collective-permute-start(f32[64,128]{1,0:T(8,128)S(1)} %solve_down.7.refs_0_.refs_10_), channel_id=1, source_target_pairs={{0,3},{1,2},{2,1},{3,0},{4,7},{5,6},{6,5},{7,4},{8,11},{9,10},{10,... | collective-permute-start | bytes 98312 | tf_op jit(solution)/shard_map/ppermute | solution.py:307
  109.9 4.3 %collective-permute-start.43 = (f32[64,128]{1,0:T(8,128)S(1)}, f32[64,128]{1,0:T(8,128)S(1)}, u32[]{:S(2)}, u32[]{:S(2)}) collective-permute-start(f32[64,128]{1,0:T(8,128)S(1)} %solve_down.7.refs_0_.refs_10_), channel_id=1, source_target_pairs={{0,2},{1,3},{2,0},{3,1},{4,6},{5,7},{6,4},{7,5},{8,10},{9,11},{10,... | collective-permute-start | bytes 98312 | tf_op jit(solution)/shard_map/ppermute | solution.py:307
  115.0 4.3 %collective-permute-start.45 = (f32[2,64,128]{2,1,0:T(8,128)S(1)}, f32[2,64,128]{2,1,0:T(8,128)S(1)}, u32[]{:S(2)}, u32[]{:S(2)}) collective-permute-start(f32[2,64,128]{2,1,0:T(8,128)S(1)} %get-tuple-element.94), channel_id=1, source_target_pairs={{0,4},{4,0},{8,12},{12,8},{16,20},{20,16},{24,28},{28,24},{1,5},{5... | collective-permute-start | bytes 196616 | tf_op jit(solution)/shard_map/ppermute | solution.py:307
  116.5 4.5 %collective-permute-start.46 = (f32[2,64,128]{2,1,0:T(8,128)S(1)}, f32[2,64,128]{2,1,0:T(8,128)S(1)}, u32[]{:S(2)}, u32[]{:S(2)}) collective-permute-start(f32[2,64,128]{2,1,0:T(8,128)S(1)} %get-tuple-element.95), channel_id=1, source_target_pairs={{0,8},{4,12},{8,0},{12,4},{16,24},{20,28},{24,16},{28,20},{1,9},{5... | collective-permute-start | bytes 196616 | tf_op jit(solution)/shard_map/ppermute | solution.py:307
  117.6 5.2 %collective-permute-start.47 = (f32[2,64,128]{2,1,0:T(8,128)S(1)}, f32[2,64,128]{2,1,0:T(8,128)S(1)}, u32[]{:S(2)}, u32[]{:S(2)}) collective-permute-start(f32[2,64,128]{2,1,0:T(8,128)S(1)} %get-tuple-element.96), channel_id=1, source_target_pairs={{0,12},{4,8},{8,4},{12,0},{16,28},{20,24},{24,20},{28,16},{1,13},{... | collective-permute-start | bytes 196616 | tf_op jit(solution)/shard_map/ppermute | solution.py:307
  122.8 4.9 %collective-permute-start.48 = (f32[64,128]{1,0:T(8,128)S(1)}, f32[64,128]{1,0:T(8,128)S(1)}, u32[]{:S(2)}, u32[]{:S(2)}) collective-permute-start(f32[64,128]{1,0:T(8,128)S(1)} %get-tuple-element.98), channel_id=1, source_target_pairs={{0,16},{4,20},{8,24},{12,28},{16,0},{20,4},{24,8},{28,12},{1,17},{... | collective-permute-start | bytes 98312 | tf_op jit(solution)/shard_map/ppermute | solution.py:284
  127.9 3.4 %collective-permute-start.51 = (f32[64,128]{1,0:T(8,128)S(1)}, f32[64,128]{1,0:T(8,128)S(1)}, u32[]{:S(2)}, u32[]{:S(2)}) collective-permute-start(f32[64,128]{1,0:T(8,128)S(1)} %solve_down.8.refs_0_.refs_9_), channel_id=1, source_target_pairs={{0,3},{1,2},{2,1},{3,0},{4,7},{5,6},{6,5},{7,4},{8,11},{9,10},{10,... | collective-permute-start | bytes 98312 | tf_op jit(solution)/shard_map/ppermute | solution.py:307
  127.9 4.1 %collective-permute-start.50 = (f32[64,128]{1,0:T(8,128)S(1)}, f32[64,128]{1,0:T(8,128)S(1)}, u32[]{:S(2)}, u32[]{:S(2)}) collective-permute-start(f32[64,128]{1,0:T(8,128)S(1)} %solve_down.8.refs_0_.refs_9_), channel_id=1, source_target_pairs={{0,2},{1,3},{2,0},{3,1},{4,6},{5,7},{6,4},{7,5},{8,10},{9,11},{10,... | collective-permute-start | bytes 98312 | tf_op jit(solution)/shard_map/ppermute | solution.py:307
  128.7 3.3 %collective-permute-start.49 = (f32[64,128]{1,0:T(8,128)S(1)}, f32[64,128]{1,0:T(8,128)S(1)}, u32[]{:S(2)}, u32[]{:S(2)}) collective-permute-start(f32[64,128]{1,0:T(8,128)S(1)} %solve_down.8.refs_0_.refs_9_), channel_id=1, source_target_pairs={{0,1},{1,0},{2,3},{3,2},{4,5},{5,4},{6,7},{7,6},{8,9},{9,8},{10,11... | collective-permute-start | bytes 98312 | tf_op jit(solution)/shard_map/ppermute | solution.py:307
  132.9 4.3 %collective-permute-start.52 = (f32[2,64,128]{2,1,0:T(8,128)S(1)}, f32[2,64,128]{2,1,0:T(8,128)S(1)}, u32[]{:S(2)}, u32[]{:S(2)}) collective-permute-start(f32[2,64,128]{2,1,0:T(8,128)S(1)} %get-tuple-element.99), channel_id=1, source_target_pairs={{0,4},{4,0},{8,12},{12,8},{16,20},{20,16},{24,28},{28,24},{1,5},{5... | collective-permute-start | bytes 196616 | tf_op jit(solution)/shard_map/ppermute | solution.py:307
  133.4 4.4 %collective-permute-start.53 = (f32[2,64,128]{2,1,0:T(8,128)S(1)}, f32[2,64,128]{2,1,0:T(8,128)S(1)}, u32[]{:S(2)}, u32[]{:S(2)}) collective-permute-start(f32[2,64,128]{2,1,0:T(8,128)S(1)} %get-tuple-element.100), channel_id=1, source_target_pairs={{0,8},{4,12},{8,0},{12,4},{16,24},{20,28},{24,16},{28,20},{1,9},{5... | collective-permute-start | bytes 196616 | tf_op jit(solution)/shard_map/ppermute | solution.py:307
  134.6 5.2 %collective-permute-start.54 = (f32[2,64,128]{2,1,0:T(8,128)S(1)}, f32[2,64,128]{2,1,0:T(8,128)S(1)}, u32[]{:S(2)}, u32[]{:S(2)}) collective-permute-start(f32[2,64,128]{2,1,0:T(8,128)S(1)} %get-tuple-element.101), channel_id=1, source_target_pairs={{0,12},{4,8},{8,4},{12,0},{16,28},{20,24},{24,20},{28,16},{1,13},{... | collective-permute-start | bytes 196616 | tf_op jit(solution)/shard_map/ppermute | solution.py:307
  139.8 4.9 %collective-permute-start.55 = (f32[64,128]{1,0:T(8,128)S(1)}, f32[64,128]{1,0:T(8,128)S(1)}, u32[]{:S(2)}, u32[]{:S(2)}) collective-permute-start(f32[64,128]{1,0:T(8,128)S(1)} %get-tuple-element.103), channel_id=1, source_target_pairs={{0,16},{4,20},{8,24},{12,28},{16,0},{20,4},{24,8},{28,12},{1,17},{... | collective-permute-start | bytes 98312 | tf_op jit(solution)/shard_map/ppermute | solution.py:284
  144.9 3.4 %collective-permute-start.58 = (f32[64,128]{1,0:T(8,128)S(1)}, f32[64,128]{1,0:T(8,128)S(1)}, u32[]{:S(2)}, u32[]{:S(2)}) collective-permute-start(f32[64,128]{1,0:T(8,128)S(1)} %solve_down.9.refs_0_.refs_8_), channel_id=1, source_target_pairs={{0,3},{1,2},{2,1},{3,0},{4,7},{5,6},{6,5},{7,4},{8,11},{9,10},{10,... | collective-permute-start | bytes 98312 | tf_op jit(solution)/shard_map/ppermute | solution.py:307
  145.0 4.3 %collective-permute-start.57 = (f32[64,128]{1,0:T(8,128)S(1)}, f32[64,128]{1,0:T(8,128)S(1)}, u32[]{:S(2)}, u32[]{:S(2)}) collective-permute-start(f32[64,128]{1,0:T(8,128)S(1)} %solve_down.9.refs_0_.refs_8_), channel_id=1, source_target_pairs={{0,2},{1,3},{2,0},{3,1},{4,6},{5,7},{6,4},{7,5},{8,10},{9,11},{10,... | collective-permute-start | bytes 98312 | tf_op jit(solution)/shard_map/ppermute | solution.py:307
  145.9 3.3 %collective-permute-start.56 = (f32[64,128]{1,0:T(8,128)S(1)}, f32[64,128]{1,0:T(8,128)S(1)}, u32[]{:S(2)}, u32[]{:S(2)}) collective-permute-start(f32[64,128]{1,0:T(8,128)S(1)} %solve_down.9.refs_0_.refs_8_), channel_id=1, source_target_pairs={{0,1},{1,0},{2,3},{3,2},{4,5},{5,4},{6,7},{7,6},{8,9},{9,8},{10,11... | collective-permute-start | bytes 98312 | tf_op jit(solution)/shard_map/ppermute | solution.py:307
  150.0 4.3 %collective-permute-start.59 = (f32[2,64,128]{2,1,0:T(8,128)S(1)}, f32[2,64,128]{2,1,0:T(8,128)S(1)}, u32[]{:S(2)}, u32[]{:S(2)}) collective-permute-start(f32[2,64,128]{2,1,0:T(8,128)S(1)} %get-tuple-element.104), channel_id=1, source_target_pairs={{0,4},{4,0},{8,12},{12,8},{16,20},{20,16},{24,28},{28,24},{1,5},{5... | collective-permute-start | bytes 196616 | tf_op jit(solution)/shard_map/ppermute | solution.py:307
  151.2 4.7 %collective-permute-start.60 = (f32[2,64,128]{2,1,0:T(8,128)S(1)}, f32[2,64,128]{2,1,0:T(8,128)S(1)}, u32[]{:S(2)}, u32[]{:S(2)}) collective-permute-start(f32[2,64,128]{2,1,0:T(8,128)S(1)} %get-tuple-element.105), channel_id=1, source_target_pairs={{0,8},{4,12},{8,0},{12,4},{16,24},{20,28},{24,16},{28,20},{1,9},{5... | collective-permute-start | bytes 196616 | tf_op jit(solution)/shard_map/ppermute | solution.py:307
  152.2 5.2 %collective-permute-start.61 = (f32[2,64,128]{2,1,0:T(8,128)S(1)}, f32[2,64,128]{2,1,0:T(8,128)S(1)}, u32[]{:S(2)}, u32[]{:S(2)}) collective-permute-start(f32[2,64,128]{2,1,0:T(8,128)S(1)} %get-tuple-element.106), channel_id=1, source_target_pairs={{0,12},{4,8},{8,4},{12,0},{16,28},{20,24},{24,20},{28,16},{1,13},{... | collective-permute-start | bytes 196616 | tf_op jit(solution)/shard_map/ppermute | solution.py:307
  157.4 4.9 %collective-permute-start.62 = (f32[64,128]{1,0:T(8,128)S(1)}, f32[64,128]{1,0:T(8,128)S(1)}, u32[]{:S(2)}, u32[]{:S(2)}) collective-permute-start(f32[64,128]{1,0:T(8,128)S(1)} %get-tuple-element.108), channel_id=1, source_target_pairs={{0,16},{4,20},{8,24},{12,28},{16,0},{20,4},{24,8},{28,12},{1,17},{... | collective-permute-start | bytes 98312 | tf_op jit(solution)/shard_map/ppermute | solution.py:284
  162.5 3.4 %collective-permute-start.65 = (f32[64,128]{1,0:T(8,128)S(1)}, f32[64,128]{1,0:T(8,128)S(1)}, u32[]{:S(2)}, u32[]{:S(2)}) collective-permute-start(f32[64,128]{1,0:T(8,128)S(1)} %solve_down.10.refs_0_.refs_7_), channel_id=1, source_target_pairs={{0,3},{1,2},{2,1},{3,0},{4,7},{5,6},{6,5},{7,4},{8,11},{9,10},{10,... | collective-permute-start | bytes 98312 | tf_op jit(solution)/shard_map/ppermute | solution.py:307
  162.6 4.0 %collective-permute-start.64 = (f32[64,128]{1,0:T(8,128)S(1)}, f32[64,128]{1,0:T(8,128)S(1)}, u32[]{:S(2)}, u32[]{:S(2)}) collective-permute-start(f32[64,128]{1,0:T(8,128)S(1)} %solve_down.10.refs_0_.refs_7_), channel_id=1, source_target_pairs={{0,2},{1,3},{2,0},{3,1},{4,6},{5,7},{6,4},{7,5},{8,10},{9,11},{10,... | collective-permute-start | bytes 98312 | tf_op jit(solution)/shard_map/ppermute | solution.py:307
  163.2 3.4 %collective-permute-start.63 = (f32[64,128]{1,0:T(8,128)S(1)}, f32[64,128]{1,0:T(8,128)S(1)}, u32[]{:S(2)}, u32[]{:S(2)}) collective-permute-start(f32[64,128]{1,0:T(8,128)S(1)} %solve_down.10.refs_0_.refs_7_), channel_id=1, source_target_pairs={{0,1},{1,0},{2,3},{3,2},{4,5},{5,4},{6,7},{7,6},{8,9},{9,8},{10,11... | collective-permute-start | bytes 98312 | tf_op jit(solution)/shard_map/ppermute | solution.py:307
  167.4 4.3 %collective-permute-start.66 = (f32[2,64,128]{2,1,0:T(8,128)S(1)}, f32[2,64,128]{2,1,0:T(8,128)S(1)}, u32[]{:S(2)}, u32[]{:S(2)}) collective-permute-start(f32[2,64,128]{2,1,0:T(8,128)S(1)} %get-tuple-element.109), channel_id=1, source_target_pairs={{0,4},{4,0},{8,12},{12,8},{16,20},{20,16},{24,28},{28,24},{1,5},{5... | collective-permute-start | bytes 196616 | tf_op jit(solution)/shard_map/ppermute | solution.py:307
  168.1 4.5 %collective-permute-start.67 = (f32[2,64,128]{2,1,0:T(8,128)S(1)}, f32[2,64,128]{2,1,0:T(8,128)S(1)}, u32[]{:S(2)}, u32[]{:S(2)}) collective-permute-start(f32[2,64,128]{2,1,0:T(8,128)S(1)} %get-tuple-element.110), channel_id=1, source_target_pairs={{0,8},{4,12},{8,0},{12,4},{16,24},{20,28},{24,16},{28,20},{1,9},{5... | collective-permute-start | bytes 196616 | tf_op jit(solution)/shard_map/ppermute | solution.py:307
  169.6 5.2 %collective-permute-start.68 = (f32[2,64,128]{2,1,0:T(8,128)S(1)}, f32[2,64,128]{2,1,0:T(8,128)S(1)}, u32[]{:S(2)}, u32[]{:S(2)}) collective-permute-start(f32[2,64,128]{2,1,0:T(8,128)S(1)} %get-tuple-element.111), channel_id=1, source_target_pairs={{0,12},{4,8},{8,4},{12,0},{16,28},{20,24},{24,20},{28,16},{1,13},{... | collective-permute-start | bytes 196616 | tf_op jit(solution)/shard_map/ppermute | solution.py:307
  174.8 4.9 %collective-permute-start.69 = (f32[64,128]{1,0:T(8,128)S(1)}, f32[64,128]{1,0:T(8,128)S(1)}, u32[]{:S(2)}, u32[]{:S(2)}) collective-permute-start(f32[64,128]{1,0:T(8,128)S(1)} %get-tuple-element.113), channel_id=1, source_target_pairs={{0,16},{4,20},{8,24},{12,28},{16,0},{20,4},{24,8},{28,12},{1,17},{... | collective-permute-start | bytes 98312 | tf_op jit(solution)/shard_map/ppermute | solution.py:284
  (16 other events, 70.9 us)

commit v7 on v6

--- a/solution.py
+++ b/solution.py
@@ -49,7 +49,7 @@
         pl.when(lax.rem(slot, chunk) == 0)(fetch(slot // chunk).wait)
         source = source_ref[level, 0, 0, slot]
         near = lax.rem(source, half) ^ lax.rem(place_ref[0], half)
-        below = near * 2 + ((source // half) ^ side)
+        below = ((source // half) ^ side) * half + near
         above = target_ref[level, 0, 0, slot] ^ place_ref[1]
         total[below * n_col + above] += slots[slot]
         return carry
@@ -81,8 +81,7 @@
     )(target, source, count, place, blocks, *after)
 
 
-def split_kernel(n_col, total_ref, *refs):
-    high_ref, low_ref = refs[-2:]
+def split_kernel(n_col, total_ref, high_ref, low_ref):
     block = total_ref.shape[-1]
     for pair in range(total_ref.shape[0]):
         rows = pl.ds(pair // n_col * block, block)
@@ -92,21 +91,21 @@
         low_ref[rows, lanes] = low
 
 
-def split(total, n_row, n_col, after):
+def split(total, n_row, n_col):
     block = total.shape[-1]
     shape = jax.ShapeDtypeStruct((n_row * block, n_col * block), jnp.bfloat16)
     whole = pl.BlockSpec(memory_space=VMEM)
     return pl.pallas_call(
         functools.partial(split_kernel, n_col),
         out_shape=[shape, shape],
-        in_specs=[whole] + [pl.BlockSpec(memory_space=pl.ANY)] * len(after),
+        in_specs=[whole],
         out_specs=[whole, whole],
         compiler_params=pltpu.CompilerParams(vmem_limit_bytes=8 * MIB),
         cost_estimate=pl.CostEstimate(
             flops=3 * total.size, bytes_accessed=8 * total.size, transcendentals=0
         ),
         name="split",
-    )(total, *after)
+    )(total)
 
 
 def read(term, refs):
@@ -287,17 +286,24 @@
 def gather_row(segment, after):
     half = lax.axis_size("row") // 2
     received = far_exchange(segment, "row")
-    (both,) = combine([[[(segment, None)], [(received, None)]]], after)
-    messages = exchange_each([both] * half, "row")
-    return [(message, side) for message in messages for side in range(2)]
-
-
-def deliver_row(messages):
-    received = exchange_each(messages, "row")
-    mine, other = combine(
-        [[[(message, side) for message in received]] for side in range(2)]
-    )
-    return [(mine, None), (far_exchange(other, "row"), None)]
+    (again,) = combine([[[(segment, None)]]], after)
+    mine = exchange_each([segment] + [again] * (half - 1), "row")
+    other = exchange_each([received] * half, "row")
+    return plain(mine + other)
+
+
+def deliver_row(mine, other):
+    other = exchange_each(other, "row")
+    (summed,) = combine([[plain([other[0], *reversed(other[1:])])]])
+    far = far_exchange(summed, "row")
+    later = combine([[[(message, None)]] for message in mine[1:-1]], (summed,))
+    mine = exchange_each([mine[0], *later, mine[-1]], "row")
+    (early,) = combine([[plain([far, mine[0], mine[-1]])]])
+    return plain([early, *mine[1:-1]])
+
+
+def plain(messages):
+    return [(message, None) for message in messages]
 
 
 def exchange_each(messages, axis):
@@ -318,28 +324,26 @@
     gather = lambda level, after: gather_blocks(
         level, blk_target, blk_source, blk_count, place, weights, n_row, n_col, after
     )
-    plain = lambda messages: [(message, None) for message in messages]
     forward = [first_solve(right, inverse)]
-    total = gather(0, ())
-    coupling = []
+    coupling = [split(gather(0, ()), n_row, n_col)]
     for level in range(1, levels):
-        coupling.append(split(total, n_row, n_col, forward[-1:] if level > 1 else ()))
         pieces = gather_row(forward[-1], coupling[-1][:1])
-        far = couple(pieces, *coupling[-1], False, (n_col // 2, n_col), 1)
-        near = couple(pieces, *coupling[-1], False, (0, n_col // 2), 1)
+        far = couple(pieces, *coupling[level - 1], False, (n_col // 2, n_col), 1)
+        near = couple(pieces, *coupling[level - 1], False, (0, n_col // 2), 1)
         after = ()
         if level < levels - 1:
-            total = gather(level, near[:1])
-            after = (total,)
+            coupling.append(split(gather(level, near[:1]), n_row, n_col))
+            after = coupling[-1][:1]
         pieces = plain(exchange_each(near + far, "col"))
         forward.append(solve(right, inverse, level, pieces, False, after))
     backward = [None] * levels
     backward[-1] = solve(forward[-1], inverse, levels - 1, [], True)
     for level in range(levels - 2, -1, -1):
         pieces = plain(exchange_each([backward[level + 1]] * n_col, "col"))
-        sent = couple(pieces, *coupling[level], True, (2, n_row), 2)
-        kept = couple(pieces, *coupling[level], True, (0, 2), 2)
-        pieces = deliver_row(kept + sent)
+        half = n_row // 2
+        other = couple(pieces, *coupling[level], True, (half, n_row), 1)
+        mine = couple(pieces, *coupling[level], True, (0, half), 1)
+        pieces = deliver_row(mine, other)
         backward[level] = solve(forward[level], inverse, level, pieces, True)
     outs = stack(forward, backward)
     return tuple(out.reshape(rhs.shape) for out in outs)
@@ -458,7 +462,7 @@
     def local(rhs, diag_inv, blocks, blk_target, blk_source, blk_count):
         sizes = (n_row, n_col)
         dense = n_row * n_col <= blocks.shape[3] and rhs.shape[3] == 1
-        even = all(size > 1 and size & (size - 1) == 0 for size in sizes)
+        even = n_row >= 8 and n_col >= 2 and all(size & (size - 1) == 0 for size in sizes)
         run = direct_shards if dense and even else shards
         return run(rhs, diag_inv, blocks, blk_target, blk_source, blk_count)
 

time: 181 us -> 186 us (1.028)
  starting transfers between devices: 62.3 us -> 108 us
  waiting for transfers between devices: 91.4 us -> 51.1 us
    ppermute x10, waiting for transfers between devices: 41 us -> 4.24 us  [far_exchange(): lax.ppermute(segment, axis, [(i, i ^ size // 2) for i in range(size)])]
    ppermute x60 -> x90, starting transfers between devices: 56.2 us -> 91.9 us  [exchange_each(): lax.ppermute(messages[d], axis, [(i, i ^ d) for i in range(size)])]
    ppermute x10, starting transfers between devices: 6.06 us -> 16.3 us  [far_exchange(): lax.ppermute(segment, axis, [(i, i ^ size // 2) for i in range(size)])]
    ppermute x60 -> x90, waiting for transfers between devices: 50.5 us -> 46.9 us  [exchange_each(): lax.ppermute(messages[d], axis, [(i, i ^ d) for i in range(size)])]
  transfers between devices with their start and end apart: 70 -> 100, of which waited for: 57 -> 56; matrix products, arithmetic and copies ran while one was open for 0% -> 0% of each run, Pallas kernels for 7% -> 8%
where the time goes in v7:
time: 186 us; the launch traced here: 187 us
  starting transfers between devices  108 us (58%)
  waiting for transfers between devices  51.1 us (27%)
  Pallas kernels  24 us (13%)
  local copies, waits for them, and re-layouts  2.67 us (1%)
    ppermute x90, starting transfers between devices, exchange_each(): lax.ppermute(messages[d], axis, [(i, i ^ d) for i in range(size)])  91.9 us
    ppermute x90, waiting for transfers between devices, exchange_each(): lax.ppermute(messages[d], axis, [(i, i ^ d) for i in range(size)])  46.9 us
    ppermute x10, starting transfers between devices, far_exchange(): lax.ppermute(segment, axis, [(i, i ^ size // 2) for i in range(size)])  16.3 us
    pallas_call x20, Pallas kernels, couple(): pl.pallas_call(functools.partial(couple_kernel, transposed, terms, span),...  9.73 us
    pallas_call x5, Pallas kernels, gather_blocks(): pl.pallas_call(functools.partial(gather_blocks_kernel, n_row, n_col, leve...  8.24 us
    ppermute x10, waiting for transfers between devices, far_exchange(): lax.ppermute(segment, axis, [(i, i ^ size // 2) for i in range(size)])  4.24 us
  transfers between devices with their start and end apart: 100, of which 56 were waited for; matrix products, arithmetic and copies ran while one was open for 0% of the time, Pallas kernels for 8%

profile of v7, /device:TPU:0, one launch (start us, length us, event | category | flops | bytes accessed | tf_op | source)
XLA Modules:
  0.0 187.1 jit_solution(12446205703691815284)
XLA Ops:
  0.6 1.7 first_solve.1.refs_0_
  2.3 4.1 %collective-permute-start.3 = (f32[64,128]{1,0:T(8,128)}, f32[64,128]{1,0:T(8,128)S(1)}, u32[]{:S(2)}, u32[]{:S(2)}) collective-permute-start(f32[64,128]{1,0:T(8,128)} %first_solve.1.refs_0_), channel_id=1, source_target_pairs={{0,16},{4,20},{8,24},{12,28},{16,0},{20,4},{24,8},{28,12},{1,17},{... | collective-permute-start | bytes 98312 | tf_op jit(solution)/shard_map/ppermute | solution.py:283
  8.6 2.3 %gather_blocks_0.1.total_ref = f32[32,128,128]{2,1,0:T(8,128)S(1)} custom-call(s32[5,1,1,32]{3,2,1,0:T(1,128)S(1)} %copy-done.3, s32[5,1,1,32]{3,2,1,0:T(1,128)S(1)} %copy-done.5, s32[5,1,1]{2,1,0:T(1,128)S(1)} %copy.8.count_ref, s32[2]{0:T(128)S(1)} %pad_add_fusion.place_ref, f32[5,32,128,128]{3,2,1,0:T(8,128)} %bitcast.11), custom_call_target="tpu_custom_call" | custom-call | flops 524288 | bytes 4194304 | tf_op jit(solution)/shard_map/gather_blocks_0/pallas_call | solution.py:65
  11.3 2.7 %collective-permute-start.2 = (f32[64,128]{1,0:T(8,128)S(1)}, f32[64,128]{1,0:T(8,128)S(1)}, u32[]{:S(2)}, u32[]{:S(2)}) collective-permute-start(f32[64,128]{1,0:T(8,128)S(1)} %combine.20), channel_id=1, source_target_pairs={{0,12},{4,8},{8,4},{12,0},{16,28},{20,24},{24,20},{28,16},{1,13},{... | collective-permute-start | bytes 98312 | tf_op jit(solution)/shard_map/ppermute | solution.py:313
  14.9 2.6 %collective-permute-start.6 = (f32[64,128]{1,0:T(8,128)S(1)}, f32[64,128]{1,0:T(8,128)S(1)}, u32[]{:S(2)}, u32[]{:S(2)}) collective-permute-start(f32[64,128]{1,0:T(8,128)S(1)} %collective-permute-done.3.refs_4_), channel_id=1, source_target_pairs={{0,12},{4,8},{8,4},{12,0},{16,28},{20,24},{24,20},{28,16},{1,13},{... | collective-permute-start | bytes 98312 | tf_op jit(solution)/shard_map/ppermute | solution.py:313
  18.4 1.3 collective-permute-done.6.refs_7_
  19.7 1.7 collective-permute-done.5.refs_6_
  22.2 1.8 collective-permute-start.8
  24.9 1.9 %gather_blocks_1.1.total_ref = f32[32,128,128]{2,1,0:T(8,128)S(1)} custom-call(s32[5,1,1,32]{3,2,1,0:T(1,128)S(1)} %copy-done.4, s32[5,1,1,32]{3,2,1,0:T(1,128)S(1)} %copy-done.6, s32[5,1,1]{2,1,0:T(1,128)S(1)} %copy.8.count_ref, s32[2]{0:T(128)S(1)} %pad_add_fusion.place_ref, f32[5,32,128,128]{3,2,1,0:T(8,128)S(1)} %bitcast.14, ...), custom_call_target="tpu_custom_call" | custom-call | flops 524288 | bytes 4194304 | tf_op jit(solution)/shard_map/gather_blocks_1/pallas_call | solution.py:65
  28.1 1.5 collective-permute-start.12
  29.9 1.8 collective-permute-start.10
  31.7 1.4 collective-permute-done.13.refs_4_
  33.0 1.2 collective-permute-start.16
  34.8 1.7 collective-permute-start.14
  36.5 1.3 collective-permute-done.16.refs_7_
  39.1 1.5 collective-permute-start.18
  41.8 1.3 gather_blocks_2.1.total_ref
  44.1 1.7 collective-permute-start.23
  45.7 2.5 %collective-permute-start.22 = (f32[64,128]{1,0:T(8,128)S(1)}, f32[64,128]{1,0:T(8,128)S(1)}, u32[]{:S(2)}, u32[]{:S(2)}) collective-permute-start(f32[64,128]{1,0:T(8,128)S(1)} %combine.22), channel_id=1, source_target_pairs={{0,12},{4,8},{8,4},{12,0},{16,28},{20,24},{24,20},{28,16},{1,13},{... | collective-permute-start | bytes 98312 | tf_op jit(solution)/shard_map/ppermute | solution.py:313
  49.2 2.8 %collective-permute-start.26 = (f32[64,128]{1,0:T(8,128)S(1)}, f32[64,128]{1,0:T(8,128)S(1)}, u32[]{:S(2)}, u32[]{:S(2)}) collective-permute-start(f32[64,128]{1,0:T(8,128)S(1)} %collective-permute-done.23.refs_4_), channel_id=1, source_target_pairs={{0,12},{4,8},{8,4},{12,0},{16,28},{20,24},{24,20},{28,16},{1,13},{... | collective-permute-start | bytes 98312 | tf_op jit(solution)/shard_map/ppermute | solution.py:313
  54.0 1.9 %collective-permute-done.25.refs_6_ = f32[64,128]{1,0:T(8,128)S(1)} collective-permute-done((f32[64,128]{1,0:T(8,128)S(1)}, f32[64,128]{1,0:T(8,128)S(1)}, u32[]{:S(2)}, u32[]{:S(2)}) %collective-permute-start.25) | collective-permute-done | bytes 32800 | tf_op jit(solution)/shard_map/ppermute | solution.py:313
  56.9 1.4 collective-permute-start.28
  59.6 1.3 gather_blocks_3.1.total_ref
  61.8 1.7 collective-permute-start.33
  65.0 2.0 %collective-permute-start.30 = (f32[64,128]{1,0:T(8,128)S(1)}, f32[64,128]{1,0:T(8,128)S(1)}, u32[]{:S(2)}, u32[]{:S(2)}) collective-permute-start(f32[64,128]{1,0:T(8,128)S(1)} %combine.23), channel_id=1, source_target_pairs={{0,4},{4,0},{8,12},{12,8},{16,20},{20,16},{24,28},{28,24},{1,5},{5... | collective-permute-start | bytes 98312 | tf_op jit(solution)/shard_map/ppermute | solution.py:313
  67.0 1.3 collective-permute-start.36
  68.5 2.0 %collective-permute-start.34 = (f32[64,128]{1,0:T(8,128)S(1)}, f32[64,128]{1,0:T(8,128)S(1)}, u32[]{:S(2)}, u32[]{:S(2)}) collective-permute-start(f32[64,128]{1,0:T(8,128)S(1)} %collective-permute-done.33.refs_4_), channel_id=1, source_target_pairs={{0,4},{4,0},{8,12},{12,8},{16,20},{20,16},{24,28},{28,24},{1,5},{5... | collective-permute-start | bytes 98312 | tf_op jit(solution)/shard_map/ppermute | solution.py:313
  70.5 1.3 collective-permute-done.36.refs_7_
  75.5 1.4 gather_blocks_4.1.total_ref
  77.6 1.7 collective-permute-start.43
  79.3 2.5 %collective-permute-start.42 = (f32[64,128]{1,0:T(8,128)S(1)}, f32[64,128]{1,0:T(8,128)S(1)}, u32[]{:S(2)}, u32[]{:S(2)}) collective-permute-start(f32[64,128]{1,0:T(8,128)S(1)} %combine.24), channel_id=1, source_target_pairs={{0,12},{4,8},{8,4},{12,0},{16,28},{20,24},{24,20},{28,16},{1,13},{... | collective-permute-start | bytes 98312 | tf_op jit(solution)/shard_map/ppermute | solution.py:313
  82.8 2.5 %collective-permute-start.46 = (f32[64,128]{1,0:T(8,128)S(1)}, f32[64,128]{1,0:T(8,128)S(1)}, u32[]{:S(2)}, u32[]{:S(2)}) collective-permute-start(f32[64,128]{1,0:T(8,128)S(1)} %collective-permute-done.43.refs_4_), channel_id=1, source_target_pairs={{0,12},{4,8},{8,4},{12,0},{16,28},{20,24},{24,20},{28,16},{1,13},{... | collective-permute-start | bytes 98312 | tf_op jit(solution)/shard_map/ppermute | solution.py:313
  87.8 1.5 collective-permute-done.45.refs_6_
  90.6 1.6 collective-permute-start.48
  93.3 1.3 collective-permute-done.48.refs_4_
  97.8 1.5 collective-permute-done.52.refs_3_
  99.3 1.2 collective-permute-done.51.refs_2_
  102.6 2.0 %collective-permute-start.55 = (f32[64,128]{1,0:T(8,128)S(1)}, f32[64,128]{1,0:T(8,128)S(1)}, u32[]{:S(2)}, u32[]{:S(2)}) collective-permute-start(f32[64,128]{1,0:T(8,128)S(1)} %get-tuple-element.117), channel_id=1, source_target_pairs={{0,4},{4,0},{8,12},{12,8},{16,20},{20,16},{24,28},{28,24},{1,5},{5... | collective-permute-start | bytes 98312 | tf_op jit(solution)/shard_map/ppermute | solution.py:313
  106.6 1.6 collective-permute-start.56
  108.2 2.0 %collective-permute-start.58 = (f32[64,128]{1,0:T(8,128)S(1)}, f32[64,128]{1,0:T(8,128)S(1)}, u32[]{:S(2)}, u32[]{:S(2)}) collective-permute-start(f32[64,128]{1,0:T(8,128)S(1)} %get-tuple-element.122), channel_id=1, source_target_pairs={{0,4},{4,0},{8,12},{12,8},{16,20},{20,16},{24,28},{28,24},{1,5},{5... | collective-permute-start | bytes 98312 | tf_op jit(solution)/shard_map/ppermute | solution.py:313
  112.1 2.0 %collective-permute-done.59.refs_4_ = f32[64,128]{1,0:T(8,128)S(1)} collective-permute-done((f32[64,128]{1,0:T(8,128)S(1)}, f32[64,128]{1,0:T(8,128)S(1)}, u32[]{:S(2)}, u32[]{:S(2)}) %collective-permute-start.59) | collective-permute-done | bytes 32800 | tf_op jit(solution)/shard_map/ppermute | solution.py:313
  116.2 1.5 collective-permute-done.62.refs_3_
  120.8 2.0 %collective-permute-start.65 = (f32[64,128]{1,0:T(8,128)S(1)}, f32[64,128]{1,0:T(8,128)S(1)}, u32[]{:S(2)}, u32[]{:S(2)}) collective-permute-start(f32[64,128]{1,0:T(8,128)S(1)} %get-tuple-element.127), channel_id=1, source_target_pairs={{0,4},{4,0},{8,12},{12,8},{16,20},{20,16},{24,28},{28,24},{1,5},{5... | collective-permute-start | bytes 98312 | tf_op jit(solution)/shard_map/ppermute | solution.py:313
  124.7 1.6 collective-permute-start.66
  126.3 2.3 %collective-permute-start.68 = (f32[64,128]{1,0:T(8,128)S(1)}, f32[64,128]{1,0:T(8,128)S(1)}, u32[]{:S(2)}, u32[]{:S(2)}) collective-permute-start(f32[64,128]{1,0:T(8,128)S(1)} %get-tuple-element.132), channel_id=1, source_target_pairs={{0,4},{4,0},{8,12},{12,8},{16,20},{20,16},{24,28},{28,24},{1,5},{5... | collective-permute-start | bytes 98312 | tf_op jit(solution)/shard_map/ppermute | solution.py:313
  130.5 2.0 %collective-permute-done.69.refs_4_ = f32[64,128]{1,0:T(8,128)S(1)} collective-permute-done((f32[64,128]{1,0:T(8,128)S(1)}, f32[64,128]{1,0:T(8,128)S(1)}, u32[]{:S(2)}, u32[]{:S(2)}) %collective-permute-start.69) | collective-permute-done | bytes 32800 | tf_op jit(solution)/shard_map/ppermute | solution.py:313
  134.6 1.5 collective-permute-done.72.refs_3_
  139.2 1.9 %collective-permute-start.75 = (f32[64,128]{1,0:T(8,128)S(1)}, f32[64,128]{1,0:T(8,128)S(1)}, u32[]{:S(2)}, u32[]{:S(2)}) collective-permute-start(f32[64,128]{1,0:T(8,128)S(1)} %get-tuple-element.137), channel_id=1, source_target_pairs={{0,4},{4,0},{8,12},{12,8},{16,20},{20,16},{24,28},{28,24},{1,5},{5... | collective-permute-start | bytes 98312 | tf_op jit(solution)/shard_map/ppermute | solution.py:313
  143.1 1.3 collective-permute-start.76
  144.4 2.3 %collective-permute-start.78 = (f32[64,128]{1,0:T(8,128)S(1)}, f32[64,128]{1,0:T(8,128)S(1)}, u32[]{:S(2)}, u32[]{:S(2)}) collective-permute-start(f32[64,128]{1,0:T(8,128)S(1)} %get-tuple-element.142), channel_id=1, source_target_pairs={{0,4},{4,0},{8,12},{12,8},{16,20},{20,16},{24,28},{28,24},{1,5},{5... | collective-permute-start | bytes 98312 | tf_op jit(solution)/shard_map/ppermute | solution.py:313
  148.6 2.0 %collective-permute-done.79.refs_4_ = f32[64,128]{1,0:T(8,128)S(1)} collective-permute-done((f32[64,128]{1,0:T(8,128)S(1)}, f32[64,128]{1,0:T(8,128)S(1)}, u32[]{:S(2)}, u32[]{:S(2)}) %collective-permute-start.79) | collective-permute-done | bytes 32800 | tf_op jit(solution)/shard_map/ppermute | solution.py:313
  150.9 1.4 collective-permute-start.81
  152.7 1.8 collective-permute-done.82.refs_3_
  155.6 1.4 collective-permute-start.84
  157.0 2.0 %collective-permute-start.85 = (f32[64,128]{1,0:T(8,128)S(1)}, f32[64,128]{1,0:T(8,128)S(1)}, u32[]{:S(2)}, u32[]{:S(2)}) collective-permute-start(f32[64,128]{1,0:T(8,128)S(1)} %get-tuple-element.147), channel_id=1, source_target_pairs={{0,4},{4,0},{8,12},{12,8},{16,20},{20,16},{24,28},{28,24},{1,5},{5... | collective-permute-start | bytes 98312 | tf_op jit(solution)/shard_map/ppermute | solution.py:313
  161.0 1.9 collective-permute-start.86
  162.8 2.2 %collective-permute-start.88 = (f32[64,128]{1,0:T(8,128)S(1)}, f32[64,128]{1,0:T(8,128)S(1)}, u32[]{:S(2)}, u32[]{:S(2)}) collective-permute-start(f32[64,128]{1,0:T(8,128)S(1)} %get-tuple-element.152), channel_id=1, source_target_pairs={{0,4},{4,0},{8,12},{12,8},{16,20},{20,16},{24,28},{28,24},{1,5},{5... | collective-permute-start | bytes 98312 | tf_op jit(solution)/shard_map/ppermute | solution.py:313
  166.9 2.0 %collective-permute-done.89.refs_4_ = f32[64,128]{1,0:T(8,128)S(1)} collective-permute-done((f32[64,128]{1,0:T(8,128)S(1)}, f32[64,128]{1,0:T(8,128)S(1)}, u32[]{:S(2)}, u32[]{:S(2)}) %collective-permute-start.89) | collective-permute-done | bytes 32800 | tf_op jit(solution)/shard_map/ppermute | solution.py:313
  169.2 1.8 collective-permute-start.90
  171.0 1.5 collective-permute-done.92.refs_3_
  175.6 1.7 collective-permute-start.95
  180.3 2.0 %collective-permute-start.98 = (f32[64,128]{1,0:T(8,128)S(1)}, f32[64,128]{1,0:T(8,128)S(1)}, u32[]{:S(2)}, u32[]{:S(2)}) collective-permute-start(f32[64,128]{1,0:T(8,128)S(1)} %get-tuple-element.162), channel_id=1, source_target_pairs={{0,4},{4,0},{8,12},{12,8},{16,20},{20,16},{24,28},{28,24},{1,5},{5... | collective-permute-start | bytes 98312 | tf_op jit(solution)/shard_map/ppermute | solution.py:313
  183.1 1.3 collective-permute-done.96.refs_0_
  184.4 1.8 collective-permute-done.99.refs_4_
  (222 shorter events, 70.6 us)
Async XLA Ops:
  2.3 12.6 %collective-permute-start.3 = (f32[64,128]{1,0:T(8,128)}, f32[64,128]{1,0:T(8,128)S(1)}, u32[]{:S(2)}, u32[]{:S(2)}) collective-permute-start(f32[64,128]{1,0:T(8,128)} %first_solve.1.refs_0_), channel_id=1, source_target_pairs={{0,16},{4,20},{8,24},{12,28},{16,0},{20,4},{24,8},{28,12},{1,17},{... | collective-permute-start | bytes 98312 | tf_op jit(solution)/shard_map/ppermute | solution.py:283
  11.3 6.6 %collective-permute-start.2 = (f32[64,128]{1,0:T(8,128)S(1)}, f32[64,128]{1,0:T(8,128)S(1)}, u32[]{:S(2)}, u32[]{:S(2)}) collective-permute-start(f32[64,128]{1,0:T(8,128)S(1)} %combine.20), channel_id=1, source_target_pairs={{0,12},{4,8},{8,4},{12,0},{16,28},{20,24},{24,20},{28,16},{1,13},{... | collective-permute-start | bytes 98312 | tf_op jit(solution)/shard_map/ppermute | solution.py:313
  14.0 4.4 %collective-permute-start.1 = (f32[64,128]{1,0:T(8,128)S(1)}, f32[64,128]{1,0:T(8,128)S(1)}, u32[]{:S(2)}, u32[]{:S(2)}) collective-permute-start(f32[64,128]{1,0:T(8,128)S(1)} %combine.20), channel_id=1, source_target_pairs={{0,8},{4,12},{8,0},{12,4},{16,24},{20,28},{24,16},{28,20},{1,9},{5... | collective-permute-start | bytes 98312 | tf_op jit(solution)/shard_map/ppermute | solution.py:313
  14.4 4.0 %collective-permute-start = (f32[64,128]{1,0:T(8,128)S(1)}, f32[64,128]{1,0:T(8,128)S(1)}, u32[]{:S(2)}, u32[]{:S(2)}) collective-permute-start(f32[64,128]{1,0:T(8,128)S(1)} %combine.20), channel_id=1, source_target_pairs={{0,4},{4,0},{8,12},{12,8},{16,20},{20,16},{24,28},{28,24},{1,5},{5... | collective-permute-start | bytes 98312 | tf_op jit(solution)/shard_map/ppermute | solution.py:313
  14.9 4.8 %collective-permute-start.6 = (f32[64,128]{1,0:T(8,128)S(1)}, f32[64,128]{1,0:T(8,128)S(1)}, u32[]{:S(2)}, u32[]{:S(2)}) collective-permute-start(f32[64,128]{1,0:T(8,128)S(1)} %collective-permute-done.3.refs_4_), channel_id=1, source_target_pairs={{0,12},{4,8},{8,4},{12,0},{16,28},{20,24},{24,20},{28,16},{1,13},{... | collective-permute-start | bytes 98312 | tf_op jit(solution)/shard_map/ppermute | solution.py:313
  17.5 3.9 %collective-permute-start.5 = (f32[64,128]{1,0:T(8,128)S(1)}, f32[64,128]{1,0:T(8,128)S(1)}, u32[]{:S(2)}, u32[]{:S(2)}) collective-permute-start(f32[64,128]{1,0:T(8,128)S(1)} %collective-permute-done.3.refs_4_), channel_id=1, source_target_pairs={{0,8},{4,12},{8,0},{12,4},{16,24},{20,28},{24,16},{28,20},{1,9},{5... | collective-permute-start | bytes 98312 | tf_op jit(solution)/shard_map/ppermute | solution.py:313
  17.9 3.9 %collective-permute-start.4 = (f32[64,128]{1,0:T(8,128)S(1)}, f32[64,128]{1,0:T(8,128)S(1)}, u32[]{:S(2)}, u32[]{:S(2)}) collective-permute-start(f32[64,128]{1,0:T(8,128)S(1)} %collective-permute-done.3.refs_4_), channel_id=1, source_target_pairs={{0,4},{4,0},{8,12},{12,8},{16,20},{20,16},{24,28},{28,24},{1,5},{5... | collective-permute-start | bytes 98312 | tf_op jit(solution)/shard_map/ppermute | solution.py:313
  22.2 5.0 %collective-permute-start.8 = (f32[64,128]{1,0:T(8,128)S(1)}, f32[64,128]{1,0:T(8,128)S(1)}, u32[]{:S(2)}, u32[]{:S(2)}) collective-permute-start(f32[64,128]{1,0:T(8,128)S(1)} %get-tuple-element.88), channel_id=1, source_target_pairs={{0,2},{1,3},{2,0},{3,1},{4,6},{5,7},{6,4},{7,5},{8,10},{9,11},{10,... | collective-permute-start | bytes 98312 | tf_op jit(solution)/shard_map/ppermute | solution.py:313
  28.0 5.0 %collective-permute-start.13 = (f32[64,128]{1,0:T(8,128)S(1)}, f32[64,128]{1,0:T(8,128)S(1)}, u32[]{:S(2)}, u32[]{:S(2)}) collective-permute-start(f32[64,128]{1,0:T(8,128)S(1)} %solve_up.5.refs_0_.refs_1_), channel_id=1, source_target_pairs={{0,16},{4,20},{8,24},{12,28},{16,0},{20,4},{24,8},{28,12},{1,17},{... | collective-permute-start | bytes 98312 | tf_op jit(solution)/shard_map/ppermute | solution.py:283
  28.1 6.7 %collective-permute-start.12 = (f32[64,128]{1,0:T(8,128)S(1)}, f32[64,128]{1,0:T(8,128)S(1)}, u32[]{:S(2)}, u32[]{:S(2)}) collective-permute-start(f32[64,128]{1,0:T(8,128)S(1)} %combine.21), channel_id=1, source_target_pairs={{0,12},{4,8},{8,4},{12,0},{16,28},{20,24},{24,20},{28,16},{1,13},{... | collective-permute-start | bytes 98312 | tf_op jit(solution)/shard_map/ppermute | solution.py:313
  29.6 6.9 %collective-permute-start.11 = (f32[64,128]{1,0:T(8,128)S(1)}, f32[64,128]{1,0:T(8,128)S(1)}, u32[]{:S(2)}, u32[]{:S(2)}) collective-permute-start(f32[64,128]{1,0:T(8,128)S(1)} %combine.21), channel_id=1, source_target_pairs={{0,8},{4,12},{8,0},{12,4},{16,24},{20,28},{24,16},{28,20},{1,9},{5... | collective-permute-start | bytes 98312 | tf_op jit(solution)/shard_map/ppermute | solution.py:313
  29.9 6.7 %collective-permute-start.10 = (f32[64,128]{1,0:T(8,128)S(1)}, f32[64,128]{1,0:T(8,128)S(1)}, u32[]{:S(2)}, u32[]{:S(2)}) collective-permute-start(f32[64,128]{1,0:T(8,128)S(1)} %combine.21), channel_id=1, source_target_pairs={{0,4},{4,0},{8,12},{12,8},{16,20},{20,16},{24,28},{28,24},{1,5},{5... | collective-permute-start | bytes 98312 | tf_op jit(solution)/shard_map/ppermute | solution.py:313
  33.0 4.8 %collective-permute-start.16 = (f32[64,128]{1,0:T(8,128)S(1)}, f32[64,128]{1,0:T(8,128)S(1)}, u32[]{:S(2)}, u32[]{:S(2)}) collective-permute-start(f32[64,128]{1,0:T(8,128)S(1)} %collective-permute-done.13.refs_4_), channel_id=1, source_target_pairs={{0,12},{4,8},{8,4},{12,0},{16,28},{20,24},{24,20},{28,16},{1,13},{... | collective-permute-start | bytes 98312 | tf_op jit(solution)/shard_map/ppermute | solution.py:313
  34.3 3.9 %collective-permute-start.15 = (f32[64,128]{1,0:T(8,128)S(1)}, f32[64,128]{1,0:T(8,128)S(1)}, u32[]{:S(2)}, u32[]{:S(2)}) collective-permute-start(f32[64,128]{1,0:T(8,128)S(1)} %collective-permute-done.13.refs_4_), channel_id=1, source_target_pairs={{0,8},{4,12},{8,0},{12,4},{16,24},{20,28},{24,16},{28,20},{1,9},{5... | collective-permute-start | bytes 98312 | tf_op jit(solution)/shard_map/ppermute | solution.py:313
  34.8 3.9 %collective-permute-start.14 = (f32[64,128]{1,0:T(8,128)S(1)}, f32[64,128]{1,0:T(8,128)S(1)}, u32[]{:S(2)}, u32[]{:S(2)}) collective-permute-start(f32[64,128]{1,0:T(8,128)S(1)} %collective-permute-done.13.refs_4_), channel_id=1, source_target_pairs={{0,4},{4,0},{8,12},{12,8},{16,20},{20,16},{24,28},{28,24},{1,5},{5... | collective-permute-start | bytes 98312 | tf_op jit(solution)/shard_map/ppermute | solution.py:313
  39.1 4.3 %collective-permute-start.18 = (f32[64,128]{1,0:T(8,128)S(1)}, f32[64,128]{1,0:T(8,128)S(1)}, u32[]{:S(2)}, u32[]{:S(2)}) collective-permute-start(f32[64,128]{1,0:T(8,128)S(1)} %get-tuple-element.94), channel_id=1, source_target_pairs={{0,2},{1,3},{2,0},{3,1},{4,6},{5,7},{6,4},{7,5},{8,10},{9,11},{10,... | collective-permute-start | bytes 98312 | tf_op jit(solution)/shard_map/ppermute | solution.py:313
  44.1 5.2 %collective-permute-start.23 = (f32[64,128]{1,0:T(8,128)S(1)}, f32[64,128]{1,0:T(8,128)S(1)}, u32[]{:S(2)}, u32[]{:S(2)}) collective-permute-start(f32[64,128]{1,0:T(8,128)S(1)} %solve_up.6.refs_0_.refs_2_), channel_id=1, source_target_pairs={{0,16},{4,20},{8,24},{12,28},{16,0},{20,4},{24,8},{28,12},{1,17},{... | collective-permute-start | bytes 98312 | tf_op jit(solution)/shard_map/ppermute | solution.py:283
  45.7 6.9 %collective-permute-start.22 = (f32[64,128]{1,0:T(8,128)S(1)}, f32[64,128]{1,0:T(8,128)S(1)}, u32[]{:S(2)}, u32[]{:S(2)}) collective-permute-start(f32[64,128]{1,0:T(8,128)S(1)} %combine.22), channel_id=1, source_target_pairs={{0,12},{4,8},{8,4},{12,0},{16,28},{20,24},{24,20},{28,16},{1,13},{... | collective-permute-start | bytes 98312 | tf_op jit(solution)/shard_map/ppermute | solution.py:313
  48.3 4.5 %collective-permute-start.21 = (f32[64,128]{1,0:T(8,128)S(1)}, f32[64,128]{1,0:T(8,128)S(1)}, u32[]{:S(2)}, u32[]{:S(2)}) collective-permute-start(f32[64,128]{1,0:T(8,128)S(1)} %combine.22), channel_id=1, source_target_pairs={{0,8},{4,12},{8,0},{12,4},{16,24},{20,28},{24,16},{28,20},{1,9},{5... | collective-permute-start | bytes 98312 | tf_op jit(solution)/shard_map/ppermute | solution.py:313
  49.2 4.8 %collective-permute-start.26 = (f32[64,128]{1,0:T(8,128)S(1)}, f32[64,128]{1,0:T(8,128)S(1)}, u32[]{:S(2)}, u32[]{:S(2)}) collective-permute-start(f32[64,128]{1,0:T(8,128)S(1)} %collective-permute-done.23.refs_4_), channel_id=1, source_target_pairs={{0,12},{4,8},{8,4},{12,0},{16,28},{20,24},{24,20},{28,16},{1,13},{... | collective-permute-start | bytes 98312 | tf_op jit(solution)/shard_map/ppermute | solution.py:313
  52.6 3.9 %collective-permute-start.24 = (f32[64,128]{1,0:T(8,128)S(1)}, f32[64,128]{1,0:T(8,128)S(1)}, u32[]{:S(2)}, u32[]{:S(2)}) collective-permute-start(f32[64,128]{1,0:T(8,128)S(1)} %collective-permute-done.23.refs_4_), channel_id=1, source_target_pairs={{0,4},{4,0},{8,12},{12,8},{16,20},{20,16},{24,28},{28,24},{1,5},{5... | collective-permute-start | bytes 98312 | tf_op jit(solution)/shard_map/ppermute | solution.py:313
  56.9 4.3 %collective-permute-start.28 = (f32[64,128]{1,0:T(8,128)S(1)}, f32[64,128]{1,0:T(8,128)S(1)}, u32[]{:S(2)}, u32[]{:S(2)}) collective-permute-start(f32[64,128]{1,0:T(8,128)S(1)} %get-tuple-element.100), channel_id=1, source_target_pairs={{0,2},{1,3},{2,0},{3,1},{4,6},{5,7},{6,4},{7,5},{8,10},{9,11},{10,... | collective-permute-start | bytes 98312 | tf_op jit(solution)/shard_map/ppermute | solution.py:313
  61.8 5.2 %collective-permute-start.33 = (f32[64,128]{1,0:T(8,128)S(1)}, f32[64,128]{1,0:T(8,128)S(1)}, u32[]{:S(2)}, u32[]{:S(2)}) collective-permute-start(f32[64,128]{1,0:T(8,128)S(1)} %solve_up.7.refs_0_.refs_3_), channel_id=1, source_target_pairs={{0,16},{4,20},{8,24},{12,28},{16,0},{20,4},{24,8},{28,12},{1,17},{... | collective-permute-start | bytes 98312 | tf_op jit(solution)/shard_map/ppermute | solution.py:283
  63.5 5.0 %collective-permute-start.32 = (f32[64,128]{1,0:T(8,128)S(1)}, f32[64,128]{1,0:T(8,128)S(1)}, u32[]{:S(2)}, u32[]{:S(2)}) collective-permute-start(f32[64,128]{1,0:T(8,128)S(1)} %combine.23), channel_id=1, source_target_pairs={{0,12},{4,8},{8,4},{12,0},{16,28},{20,24},{24,20},{28,16},{1,13},{... | collective-permute-start | bytes 98312 | tf_op jit(solution)/shard_map/ppermute | solution.py:313
  64.6 5.9 %collective-permute-start.31 = (f32[64,128]{1,0:T(8,128)S(1)}, f32[64,128]{1,0:T(8,128)S(1)}, u32[]{:S(2)}, u32[]{:S(2)}) collective-permute-start(f32[64,128]{1,0:T(8,128)S(1)} %combine.23), channel_id=1, source_target_pairs={{0,8},{4,12},{8,0},{12,4},{16,24},{20,28},{24,16},{28,20},{1,9},{5... | collective-permute-start | bytes 98312 | tf_op jit(solution)/shard_map/ppermute | solution.py:313
  65.0 5.6 %collective-permute-start.30 = (f32[64,128]{1,0:T(8,128)S(1)}, f32[64,128]{1,0:T(8,128)S(1)}, u32[]{:S(2)}, u32[]{:S(2)}) collective-permute-start(f32[64,128]{1,0:T(8,128)S(1)} %combine.23), channel_id=1, source_target_pairs={{0,4},{4,0},{8,12},{12,8},{16,20},{20,16},{24,28},{28,24},{1,5},{5... | collective-permute-start | bytes 98312 | tf_op jit(solution)/shard_map/ppermute | solution.py:313
  67.0 4.8 %collective-permute-start.36 = (f32[64,128]{1,0:T(8,128)S(1)}, f32[64,128]{1,0:T(8,128)S(1)}, u32[]{:S(2)}, u32[]{:S(2)}) collective-permute-start(f32[64,128]{1,0:T(8,128)S(1)} %collective-permute-done.33.refs_4_), channel_id=1, source_target_pairs={{0,12},{4,8},{8,4},{12,0},{16,28},{20,24},{24,20},{28,16},{1,13},{... | collective-permute-start | bytes 98312 | tf_op jit(solution)/shard_map/ppermute | solution.py:313
  68.5 3.9 %collective-permute-start.34 = (f32[64,128]{1,0:T(8,128)S(1)}, f32[64,128]{1,0:T(8,128)S(1)}, u32[]{:S(2)}, u32[]{:S(2)}) collective-permute-start(f32[64,128]{1,0:T(8,128)S(1)} %collective-permute-done.33.refs_4_), channel_id=1, source_target_pairs={{0,4},{4,0},{8,12},{12,8},{16,20},{20,16},{24,28},{28,24},{1,5},{5... | collective-permute-start | bytes 98312 | tf_op jit(solution)/shard_map/ppermute | solution.py:313
  72.8 4.5 %collective-permute-start.38 = (f32[64,128]{1,0:T(8,128)S(1)}, f32[64,128]{1,0:T(8,128)S(1)}, u32[]{:S(2)}, u32[]{:S(2)}) collective-permute-start(f32[64,128]{1,0:T(8,128)S(1)} %get-tuple-element.106), channel_id=1, source_target_pairs={{0,2},{1,3},{2,0},{3,1},{4,6},{5,7},{6,4},{7,5},{8,10},{9,11},{10,... | collective-permute-start | bytes 98312 | tf_op jit(solution)/shard_map/ppermute | solution.py:313
  77.6 5.2 %collective-permute-start.43 = (f32[64,128]{1,0:T(8,128)S(1)}, f32[64,128]{1,0:T(8,128)S(1)}, u32[]{:S(2)}, u32[]{:S(2)}) collective-permute-start(f32[64,128]{1,0:T(8,128)S(1)} %solve_up.8.refs_0_.refs_4_), channel_id=1, source_target_pairs={{0,16},{4,20},{8,24},{12,28},{16,0},{20,4},{24,8},{28,12},{1,17},{... | collective-permute-start | bytes 98312 | tf_op jit(solution)/shard_map/ppermute | solution.py:283
  79.3 7.0 %collective-permute-start.42 = (f32[64,128]{1,0:T(8,128)S(1)}, f32[64,128]{1,0:T(8,128)S(1)}, u32[]{:S(2)}, u32[]{:S(2)}) collective-permute-start(f32[64,128]{1,0:T(8,128)S(1)} %combine.24), channel_id=1, source_target_pairs={{0,12},{4,8},{8,4},{12,0},{16,28},{20,24},{24,20},{28,16},{1,13},{... | collective-permute-start | bytes 98312 | tf_op jit(solution)/shard_map/ppermute | solution.py:313
  81.8 4.5 %collective-permute-start.41 = (f32[64,128]{1,0:T(8,128)S(1)}, f32[64,128]{1,0:T(8,128)S(1)}, u32[]{:S(2)}, u32[]{:S(2)}) collective-permute-start(f32[64,128]{1,0:T(8,128)S(1)} %combine.24), channel_id=1, source_target_pairs={{0,8},{4,12},{8,0},{12,4},{16,24},{20,28},{24,16},{28,20},{1,9},{5... | collective-permute-start | bytes 98312 | tf_op jit(solution)/shard_map/ppermute | solution.py:313
  82.8 4.9 %collective-permute-start.46 = (f32[64,128]{1,0:T(8,128)S(1)}, f32[64,128]{1,0:T(8,128)S(1)}, u32[]{:S(2)}, u32[]{:S(2)}) collective-permute-start(f32[64,128]{1,0:T(8,128)S(1)} %collective-permute-done.43.refs_4_), channel_id=1, source_target_pairs={{0,12},{4,8},{8,4},{12,0},{16,28},{20,24},{24,20},{28,16},{1,13},{... | collective-permute-start | bytes 98312 | tf_op jit(solution)/shard_map/ppermute | solution.py:313
  86.3 3.9 %collective-permute-start.44 = (f32[64,128]{1,0:T(8,128)S(1)}, f32[64,128]{1,0:T(8,128)S(1)}, u32[]{:S(2)}, u32[]{:S(2)}) collective-permute-start(f32[64,128]{1,0:T(8,128)S(1)} %collective-permute-done.43.refs_4_), channel_id=1, source_target_pairs={{0,4},{4,0},{8,12},{12,8},{16,20},{20,16},{24,28},{28,24},{1,5},{5... | collective-permute-start | bytes 98312 | tf_op jit(solution)/shard_map/ppermute | solution.py:313
  90.6 4.0 %collective-permute-start.48 = (f32[64,128]{1,0:T(8,128)S(1)}, f32[64,128]{1,0:T(8,128)S(1)}, u32[]{:S(2)}, u32[]{:S(2)}) collective-permute-start(f32[64,128]{1,0:T(8,128)S(1)} %get-tuple-element.112), channel_id=1, source_target_pairs={{0,2},{1,3},{2,0},{3,1},{4,6},{5,7},{6,4},{7,5},{8,10},{9,11},{10,... | collective-permute-start | bytes 98312 | tf_op jit(solution)/shard_map/ppermute | solution.py:313
  101.1 5.1 %collective-permute-start.53 = (f32[64,128]{1,0:T(8,128)S(1)}, f32[64,128]{1,0:T(8,128)S(1)}, u32[]{:S(2)}, u32[]{:S(2)}) collective-permute-start(f32[64,128]{1,0:T(8,128)S(1)} %get-tuple-element.115), channel_id=1, source_target_pairs={{0,12},{4,8},{8,4},{12,0},{16,28},{20,24},{24,20},{28,16},{1,13},{... | collective-permute-start | bytes 98312 | tf_op jit(solution)/shard_map/ppermute | solution.py:313
  102.1 4.1 %collective-permute-start.54 = (f32[64,128]{1,0:T(8,128)S(1)}, f32[64,128]{1,0:T(8,128)S(1)}, u32[]{:S(2)}, u32[]{:S(2)}) collective-permute-start(f32[64,128]{1,0:T(8,128)S(1)} %get-tuple-element.116), channel_id=1, source_target_pairs={{0,8},{4,12},{8,0},{12,4},{16,24},{20,28},{24,16},{28,20},{1,9},{5... | collective-permute-start | bytes 98312 | tf_op jit(solution)/shard_map/ppermute | solution.py:313
  105.3 5.9 %collective-permute-start.57 = (f32[64,128]{1,0:T(8,128)S(1)}, f32[64,128]{1,0:T(8,128)S(1)}, u32[]{:S(2)}, u32[]{:S(2)}) collective-permute-start(f32[64,128]{1,0:T(8,128)S(1)} %get-tuple-element.119), channel_id=1, source_target_pairs={{0,12},{4,8},{8,4},{12,0},{16,28},{20,24},{24,20},{28,16},{1,13},{... | collective-permute-start | bytes 98312 | tf_op jit(solution)/shard_map/ppermute | solution.py:313
  106.6 4.9 %collective-permute-start.56 = (f32[64,128]{1,0:T(8,128)S(1)}, f32[64,128]{1,0:T(8,128)S(1)}, u32[]{:S(2)}, u32[]{:S(2)}) collective-permute-start(f32[64,128]{1,0:T(8,128)S(1)} %combine.25.refs_2_), channel_id=1, source_target_pairs={{0,16},{4,20},{8,24},{12,28},{16,0},{20,4},{24,8},{28,12},{1,17},{... | collective-permute-start | bytes 98312 | tf_op jit(solution)/shard_map/ppermute | solution.py:283
  114.4 4.2 %collective-permute-start.61 = (f32[64,128]{1,0:T(8,128)S(1)}, f32[64,128]{1,0:T(8,128)S(1)}, u32[]{:S(2)}, u32[]{:S(2)}) collective-permute-start(f32[64,128]{1,0:T(8,128)S(1)} %solve_down.7.refs_0_.refs_10_), channel_id=1, source_target_pairs={{0,2},{1,3},{2,0},{3,1},{4,6},{5,7},{6,4},{7,5},{8,10},{9,11},{10,... | collective-permute-start | bytes 98312 | tf_op jit(solution)/shard_map/ppermute | solution.py:313
  119.2 5.0 %collective-permute-start.63 = (f32[64,128]{1,0:T(8,128)S(1)}, f32[64,128]{1,0:T(8,128)S(1)}, u32[]{:S(2)}, u32[]{:S(2)}) collective-permute-start(f32[64,128]{1,0:T(8,128)S(1)} %get-tuple-element.125), channel_id=1, source_target_pairs={{0,12},{4,8},{8,4},{12,0},{16,28},{20,24},{24,20},{28,16},{1,13},{... | collective-permute-start | bytes 98312 | tf_op jit(solution)/shard_map/ppermute | solution.py:313
  119.9 4.3 %collective-permute-start.64 = (f32[64,128]{1,0:T(8,128)S(1)}, f32[64,128]{1,0:T(8,128)S(1)}, u32[]{:S(2)}, u32[]{:S(2)}) collective-permute-start(f32[64,128]{1,0:T(8,128)S(1)} %get-tuple-element.126), channel_id=1, source_target_pairs={{0,8},{4,12},{8,0},{12,4},{16,24},{20,28},{24,16},{28,20},{1,9},{5... | collective-permute-start | bytes 98312 | tf_op jit(solution)/shard_map/ppermute | solution.py:313
  123.3 6.5 %collective-permute-start.67 = (f32[64,128]{1,0:T(8,128)S(1)}, f32[64,128]{1,0:T(8,128)S(1)}, u32[]{:S(2)}, u32[]{:S(2)}) collective-permute-start(f32[64,128]{1,0:T(8,128)S(1)} %get-tuple-element.129), channel_id=1, source_target_pairs={{0,12},{4,8},{8,4},{12,0},{16,28},{20,24},{24,20},{28,16},{1,13},{... | collective-permute-start | bytes 98312 | tf_op jit(solution)/shard_map/ppermute | solution.py:313
  124.7 5.1 %collective-permute-start.66 = (f32[64,128]{1,0:T(8,128)S(1)}, f32[64,128]{1,0:T(8,128)S(1)}, u32[]{:S(2)}, u32[]{:S(2)}) collective-permute-start(f32[64,128]{1,0:T(8,128)S(1)} %combine.28.refs_2_), channel_id=1, source_target_pairs={{0,16},{4,20},{8,24},{12,28},{16,0},{20,4},{24,8},{28,12},{1,17},{... | collective-permute-start | bytes 98312 | tf_op jit(solution)/shard_map/ppermute | solution.py:283
  126.3 4.2 %collective-permute-start.68 = (f32[64,128]{1,0:T(8,128)S(1)}, f32[64,128]{1,0:T(8,128)S(1)}, u32[]{:S(2)}, u32[]{:S(2)}) collective-permute-start(f32[64,128]{1,0:T(8,128)S(1)} %get-tuple-element.132), channel_id=1, source_target_pairs={{0,4},{4,0},{8,12},{12,8},{16,20},{20,16},{24,28},{28,24},{1,5},{5... | collective-permute-start | bytes 98312 | tf_op jit(solution)/shard_map/ppermute | solution.py:313
  132.7 4.2 %collective-permute-start.71 = (f32[64,128]{1,0:T(8,128)S(1)}, f32[64,128]{1,0:T(8,128)S(1)}, u32[]{:S(2)}, u32[]{:S(2)}) collective-permute-start(f32[64,128]{1,0:T(8,128)S(1)} %solve_down.8.refs_0_.refs_9_), channel_id=1, source_target_pairs={{0,2},{1,3},{2,0},{3,1},{4,6},{5,7},{6,4},{7,5},{8,10},{9,11},{10,... | collective-permute-start | bytes 98312 | tf_op jit(solution)/shard_map/ppermute | solution.py:313
  137.5 4.9 %collective-permute-start.73 = (f32[64,128]{1,0:T(8,128)S(1)}, f32[64,128]{1,0:T(8,128)S(1)}, u32[]{:S(2)}, u32[]{:S(2)}) collective-permute-start(f32[64,128]{1,0:T(8,128)S(1)} %get-tuple-element.135), channel_id=1, source_target_pairs={{0,12},{4,8},{8,4},{12,0},{16,28},{20,24},{24,20},{28,16},{1,13},{... | collective-permute-start | bytes 98312 | tf_op jit(solution)/shard_map/ppermute | solution.py:313
  138.2 4.2 %collective-permute-start.74 = (f32[64,128]{1,0:T(8,128)S(1)}, f32[64,128]{1,0:T(8,128)S(1)}, u32[]{:S(2)}, u32[]{:S(2)}) collective-permute-start(f32[64,128]{1,0:T(8,128)S(1)} %get-tuple-element.136), channel_id=1, source_target_pairs={{0,8},{4,12},{8,0},{12,4},{16,24},{20,28},{24,16},{28,20},{1,9},{5... | collective-permute-start | bytes 98312 | tf_op jit(solution)/shard_map/ppermute | solution.py:313
  141.7 5.3 %collective-permute-start.77 = (f32[64,128]{1,0:T(8,128)S(1)}, f32[64,128]{1,0:T(8,128)S(1)}, u32[]{:S(2)}, u32[]{:S(2)}) collective-permute-start(f32[64,128]{1,0:T(8,128)S(1)} %get-tuple-element.139), channel_id=1, source_target_pairs={{0,12},{4,8},{8,4},{12,0},{16,28},{20,24},{24,20},{28,16},{1,13},{... | collective-permute-start | bytes 98312 | tf_op jit(solution)/shard_map/ppermute | solution.py:313
  143.1 4.9 %collective-permute-start.76 = (f32[64,128]{1,0:T(8,128)S(1)}, f32[64,128]{1,0:T(8,128)S(1)}, u32[]{:S(2)}, u32[]{:S(2)}) collective-permute-start(f32[64,128]{1,0:T(8,128)S(1)} %combine.31.refs_2_), channel_id=1, source_target_pairs={{0,16},{4,20},{8,24},{12,28},{16,0},{20,4},{24,8},{28,12},{1,17},{... | collective-permute-start | bytes 98312 | tf_op jit(solution)/shard_map/ppermute | solution.py:283
  144.4 4.2 %collective-permute-start.78 = (f32[64,128]{1,0:T(8,128)S(1)}, f32[64,128]{1,0:T(8,128)S(1)}, u32[]{:S(2)}, u32[]{:S(2)}) collective-permute-start(f32[64,128]{1,0:T(8,128)S(1)} %get-tuple-element.142), channel_id=1, source_target_pairs={{0,4},{4,0},{8,12},{12,8},{16,20},{20,16},{24,28},{28,24},{1,5},{5... | collective-permute-start | bytes 98312 | tf_op jit(solution)/shard_map/ppermute | solution.py:313
  150.9 4.0 %collective-permute-start.81 = (f32[64,128]{1,0:T(8,128)S(1)}, f32[64,128]{1,0:T(8,128)S(1)}, u32[]{:S(2)}, u32[]{:S(2)}) collective-permute-start(f32[64,128]{1,0:T(8,128)S(1)} %solve_down.9.refs_0_.refs_8_), channel_id=1, source_target_pairs={{0,2},{1,3},{2,0},{3,1},{4,6},{5,7},{6,4},{7,5},{8,10},{9,11},{10,... | collective-permute-start | bytes 98312 | tf_op jit(solution)/shard_map/ppermute | solution.py:313
  155.4 4.9 %collective-permute-start.83 = (f32[64,128]{1,0:T(8,128)S(1)}, f32[64,128]{1,0:T(8,128)S(1)}, u32[]{:S(2)}, u32[]{:S(2)}) collective-permute-start(f32[64,128]{1,0:T(8,128)S(1)} %get-tuple-element.145), channel_id=1, source_target_pairs={{0,12},{4,8},{8,4},{12,0},{16,28},{20,24},{24,20},{28,16},{1,13},{... | collective-permute-start | bytes 98312 | tf_op jit(solution)/shard_map/ppermute | solution.py:313
  155.6 4.7 %collective-permute-start.84 = (f32[64,128]{1,0:T(8,128)S(1)}, f32[64,128]{1,0:T(8,128)S(1)}, u32[]{:S(2)}, u32[]{:S(2)}) collective-permute-start(f32[64,128]{1,0:T(8,128)S(1)} %get-tuple-element.146), channel_id=1, source_target_pairs={{0,8},{4,12},{8,0},{12,4},{16,24},{20,28},{24,16},{28,20},{1,9},{5... | collective-permute-start | bytes 98312 | tf_op jit(solution)/shard_map/ppermute | solution.py:313
  159.6 6.5 %collective-permute-start.87 = (f32[64,128]{1,0:T(8,128)S(1)}, f32[64,128]{1,0:T(8,128)S(1)}, u32[]{:S(2)}, u32[]{:S(2)}) collective-permute-start(f32[64,128]{1,0:T(8,128)S(1)} %get-tuple-element.149), channel_id=1, source_target_pairs={{0,12},{4,8},{8,4},{12,0},{16,28},{20,24},{24,20},{28,16},{1,13},{... | collective-permute-start | bytes 98312 | tf_op jit(solution)/shard_map/ppermute | solution.py:313
  161.0 5.2 %collective-permute-start.86 = (f32[64,128]{1,0:T(8,128)S(1)}, f32[64,128]{1,0:T(8,128)S(1)}, u32[]{:S(2)}, u32[]{:S(2)}) collective-permute-start(f32[64,128]{1,0:T(8,128)S(1)} %combine.34.refs_2_), channel_id=1, source_target_pairs={{0,16},{4,20},{8,24},{12,28},{16,0},{20,4},{24,8},{28,12},{1,17},{... | collective-permute-start | bytes 98312 | tf_op jit(solution)/shard_map/ppermute | solution.py:283
  162.8 4.0 %collective-permute-start.88 = (f32[64,128]{1,0:T(8,128)S(1)}, f32[64,128]{1,0:T(8,128)S(1)}, u32[]{:S(2)}, u32[]{:S(2)}) collective-permute-start(f32[64,128]{1,0:T(8,128)S(1)} %get-tuple-element.152), channel_id=1, source_target_pairs={{0,4},{4,0},{8,12},{12,8},{16,20},{20,16},{24,28},{28,24},{1,5},{5... | collective-permute-start | bytes 98312 | tf_op jit(solution)/shard_map/ppermute | solution.py:313
  169.1 4.0 %collective-permute-start.91 = (f32[64,128]{1,0:T(8,128)S(1)}, f32[64,128]{1,0:T(8,128)S(1)}, u32[]{:S(2)}, u32[]{:S(2)}) collective-permute-start(f32[64,128]{1,0:T(8,128)S(1)} %solve_down.10.refs_0_.refs_7_), channel_id=1, source_target_pairs={{0,2},{1,3},{2,0},{3,1},{4,6},{5,7},{6,4},{7,5},{8,10},{9,11},{10,... | collective-permute-start | bytes 98312 | tf_op jit(solution)/shard_map/ppermute | solution.py:313
  169.2 4.0 %collective-permute-start.90 = (f32[64,128]{1,0:T(8,128)S(1)}, f32[64,128]{1,0:T(8,128)S(1)}, u32[]{:S(2)}, u32[]{:S(2)}) collective-permute-start(f32[64,128]{1,0:T(8,128)S(1)} %solve_down.10.refs_0_.refs_7_), channel_id=1, source_target_pairs={{0,1},{1,0},{2,3},{3,2},{4,5},{5,4},{6,7},{7,6},{8,9},{9,8},{10,11... | collective-permute-start | bytes 98312 | tf_op jit(solution)/shard_map/ppermute | solution.py:313
  173.8 5.0 %collective-permute-start.93 = (f32[64,128]{1,0:T(8,128)S(1)}, f32[64,128]{1,0:T(8,128)S(1)}, u32[]{:S(2)}, u32[]{:S(2)}) collective-permute-start(f32[64,128]{1,0:T(8,128)S(1)} %get-tuple-element.155), channel_id=1, source_target_pairs={{0,12},{4,8},{8,4},{12,0},{16,28},{20,24},{24,20},{28,16},{1,13},{... | collective-permute-start | bytes 98312 | tf_op jit(solution)/shard_map/ppermute | solution.py:313
  174.6 4.1 %collective-permute-start.94 = (f32[64,128]{1,0:T(8,128)S(1)}, f32[64,128]{1,0:T(8,128)S(1)}, u32[]{:S(2)}, u32[]{:S(2)}) collective-permute-start(f32[64,128]{1,0:T(8,128)S(1)} %get-tuple-element.156), channel_id=1, source_target_pairs={{0,8},{4,12},{8,0},{12,4},{16,24},{20,28},{24,16},{28,20},{1,9},{5... | collective-permute-start | bytes 98312 | tf_op jit(solution)/shard_map/ppermute | solution.py:313
  177.9 5.2 %collective-permute-start.97 = (f32[64,128]{1,0:T(8,128)S(1)}, f32[64,128]{1,0:T(8,128)S(1)}, u32[]{:S(2)}, u32[]{:S(2)}) collective-permute-start(f32[64,128]{1,0:T(8,128)S(1)} %get-tuple-element.159), channel_id=1, source_target_pairs={{0,12},{4,8},{8,4},{12,0},{16,28},{20,24},{24,20},{28,16},{1,13},{... | collective-permute-start | bytes 98312 | tf_op jit(solution)/shard_map/ppermute | solution.py:313
  179.5 4.9 %collective-permute-start.96 = (f32[64,128]{1,0:T(8,128)S(1)}, f32[64,128]{1,0:T(8,128)S(1)}, u32[]{:S(2)}, u32[]{:S(2)}) collective-permute-start(f32[64,128]{1,0:T(8,128)S(1)} %combine.37.refs_2_), channel_id=1, source_target_pairs={{0,16},{4,20},{8,24},{12,28},{16,0},{20,4},{24,8},{28,12},{1,17},{... | collective-permute-start | bytes 98312 | tf_op jit(solution)/shard_map/ppermute | solution.py:283
  180.3 4.1 %collective-permute-start.98 = (f32[64,128]{1,0:T(8,128)S(1)}, f32[64,128]{1,0:T(8,128)S(1)}, u32[]{:S(2)}, u32[]{:S(2)}) collective-permute-start(f32[64,128]{1,0:T(8,128)S(1)} %get-tuple-element.162), channel_id=1, source_target_pairs={{0,4},{4,0},{8,12},{12,8},{16,20},{20,16},{24,28},{28,24},{1,5},{5... | collective-permute-start | bytes 98312 | tf_op jit(solution)/shard_map/ppermute | solution.py:313
  (46 other events, 187.1 us)

commit v8 on v6

--- a/solution.py
+++ b/solution.py
@@ -28,12 +28,13 @@
 
 
 def gather_blocks_kernel(
-    n_row, n_col, level, chunk, target_ref, source_ref, count_ref, place_ref, blocks_ref, *refs
+    n_row, n_col, level, chunk, slots_ref, blocks_ref, *refs
 ):
     total, slots, arrived = refs[-3:]
-    count = count_ref[level, 0, 0]
+    slot_count = slots.shape[0]
+    count, row, col = (slots_ref[level, 2 * slot_count + place] for place in range(3))
     half = n_row // 2
-    side = place_ref[0] // half
+    side = row // half
 
     def fetch(number):
         span = pl.ds(number * chunk, chunk)
@@ -47,17 +48,17 @@
 
     def add(slot, carry):
         pl.when(lax.rem(slot, chunk) == 0)(fetch(slot // chunk).wait)
-        source = source_ref[level, 0, 0, slot]
-        near = lax.rem(source, half) ^ lax.rem(place_ref[0], half)
+        source = slots_ref[level, slot_count + slot]
+        near = lax.rem(source, half) ^ lax.rem(row, half)
         below = near * 2 + ((source // half) ^ side)
-        above = target_ref[level, 0, 0, slot] ^ place_ref[1]
+        above = slots_ref[level, slot] ^ col
         total[below * n_col + above] += slots[slot]
         return carry
 
     lax.fori_loop(0, count, add, 0)
 
 
-def gather_blocks(level, target, source, count, place, blocks, n_row, n_col, after):
+def gather_blocks(level, slots, blocks, n_row, n_col, after):
     slot_count, block = blocks.shape[1], blocks.shape[2]
     chunk = max(1, slot_count // 4)
     shape = (n_row * n_col, block, block)
@@ -65,7 +66,7 @@
     return pl.pallas_call(
         functools.partial(gather_blocks_kernel, n_row, n_col, level, chunk),
         out_shape=jax.ShapeDtypeStruct(shape, jnp.float32),
-        in_specs=[scalars] * 4 + [pl.BlockSpec(memory_space=pl.ANY)] * (1 + len(after)),
+        in_specs=[scalars] + [pl.BlockSpec(memory_space=pl.ANY)] * (1 + len(after)),
         out_specs=pl.BlockSpec(memory_space=VMEM),
         scratch_shapes=[
             pltpu.VMEM((slot_count, block, block), jnp.float32),
@@ -78,26 +79,27 @@
             transcendentals=0,
         ),
         name=f"gather_blocks_{level}",
-    )(target, source, count, place, blocks, *after)
-
-
-def split_kernel(n_col, total_ref, *refs):
+    )(slots, blocks, *after)
+
+
+def split_kernel(n_col, flipped, total_ref, *refs):
     high_ref, low_ref = refs[-2:]
     block = total_ref.shape[-1]
     for pair in range(total_ref.shape[0]):
-        rows = pl.ds(pair // n_col * block, block)
-        lanes = pl.ds(pair % n_col * block, block)
-        high, low = halves(total_ref[pair])
+        at = (pair % n_col, pair // n_col) if flipped else (pair // n_col, pair % n_col)
+        rows, lanes = (pl.ds(place * block, block) for place in at)
+        high, low = halves(total_ref[pair].T if flipped else total_ref[pair])
         high_ref[rows, lanes] = high
         low_ref[rows, lanes] = low
 
 
-def split(total, n_row, n_col, after):
+def split(total, n_row, n_col, flipped, after):
     block = total.shape[-1]
-    shape = jax.ShapeDtypeStruct((n_row * block, n_col * block), jnp.bfloat16)
+    sizes = (n_col, n_row) if flipped else (n_row, n_col)
+    shape = jax.ShapeDtypeStruct(tuple(size * block for size in sizes), jnp.bfloat16)
     whole = pl.BlockSpec(memory_space=VMEM)
     return pl.pallas_call(
-        functools.partial(split_kernel, n_col),
+        functools.partial(split_kernel, n_col, flipped),
         out_shape=[shape, shape],
         in_specs=[whole] + [pl.BlockSpec(memory_space=pl.ANY)] * len(after),
         out_specs=[whole, whole],
@@ -105,7 +107,7 @@
         cost_estimate=pl.CostEstimate(
             flops=3 * total.size, bytes_accessed=8 * total.size, transcendentals=0
         ),
-        name="split",
+        name="flip" if flipped else "split",
     )(total, *after)
 
 
@@ -142,21 +144,20 @@
         return len(self.arrays) - 1, place
 
 
-def couple_kernel(transposed, terms, span, high_ref, low_ref, *refs):
+def couple_kernel(terms, span, high_ref, low_ref, *refs):
     n_in = 1 + max(number for number, _ in terms)
     ins, outs = refs[:n_in], refs[n_in:]
     block = ins[0].shape[-1]
     joined = jnp.concatenate([read(term, ins) for term in terms], axis=1)
     wanted = pl.ds(span[0] * block, (span[1] - span[0]) * block)
-    chosen = (wanted, slice(None)) if transposed else (slice(None), wanted)
-    result = product(halves(joined), (high_ref[chosen], low_ref[chosen]), transposed)
+    result = product(halves(joined), (high_ref[:, wanted], low_ref[:, wanted]), False)
     pieces = [result[:, at : at + block] for at in range(0, result.shape[1], block)]
     each = len(pieces) // len(outs)
     for number, ref in enumerate(outs):
         write(ref, pieces[number * each : (number + 1) * each])
 
 
-def couple(pieces, high, low, transposed, span, each):
+def couple(pieces, high, low, span, each):
     operands = Operands()
     terms = [operands.term(piece) for piece in pieces]
     rows, block = operands.arrays[0].shape[-2:]
@@ -165,7 +166,7 @@
     whole = pl.BlockSpec(memory_space=VMEM)
     work = rows * block * block * len(terms) * (span[1] - span[0])
     return pl.pallas_call(
-        functools.partial(couple_kernel, transposed, terms, span),
+        functools.partial(couple_kernel, terms, span),
         out_shape=[jax.ShapeDtypeStruct(shape, jnp.float32)] * n_out,
         in_specs=[whole] * (2 + len(operands.arrays)),
         out_specs=[whole] * n_out,
@@ -173,7 +174,7 @@
         cost_estimate=pl.CostEstimate(
             flops=6 * work, bytes_accessed=4 * work // rows, transcendentals=0
         ),
-        name="couple_up" if not transposed else "couple_down",
+        name="couple",
     )(high, low, *operands.arrays)
 
 
@@ -260,23 +261,21 @@
     )(*operands.arrays, *after)
 
 
-def stack_kernel(n_forward, *refs):
-    ins, (forward_ref, backward_ref) = refs[:-2], refs[-2:]
-    write(forward_ref, [ref[...] for ref in ins[:n_forward]])
-    write(backward_ref, [ref[...] for ref in ins[n_forward:]])
-
-
-def stack(forward, backward):
+def stack_kernel(n_ins, *refs):
+    write(refs[-1], [ref[...] for ref in refs[:n_ins]])
+
+
+def stack(segments, after=()):
     whole = pl.BlockSpec(memory_space=VMEM)
-    shape = jax.ShapeDtypeStruct((len(forward),) + forward[0].shape, jnp.float32)
-    return pl.pallas_call(
-        functools.partial(stack_kernel, len(forward)),
-        out_shape=[shape, shape],
-        in_specs=[whole] * (2 * len(forward)),
-        out_specs=[whole] * 2,
+    shape = (len(segments),) + segments[0].shape
+    return pl.pallas_call(
+        functools.partial(stack_kernel, len(segments)),
+        out_shape=jax.ShapeDtypeStruct(shape, jnp.float32),
+        in_specs=[whole] * len(segments) + [pl.BlockSpec(memory_space=pl.ANY)] * len(after),
+        out_specs=whole,
         compiler_params=pltpu.CompilerParams(vmem_limit_bytes=8 * MIB),
         name="stack",
-    )(*forward, *backward)
+    )(*segments, *after)
 
 
 def far_exchange(segment, axis):
@@ -295,7 +294,10 @@
 def deliver_row(messages):
     received = exchange_each(messages, "row")
     mine, other = combine(
-        [[[(message, side) for message in received]] for side in range(2)]
+        [
+            [[(message, side) for message in [received[0], *reversed(received[1:])]]]
+            for side in range(2)
+        ]
     )
     return [(mine, None), (far_exchange(other, "row"), None)]
 
@@ -314,35 +316,50 @@
     right = rhs.reshape((levels,) + rhs.shape[-2:])
     inverse = diag_inv.reshape((levels,) + diag_inv.shape[-2:])
     weights = blocks.reshape((levels - 1,) + blocks.shape[-3:])
-    place = jnp.stack([lax.axis_index("row"), lax.axis_index("col")]).astype(jnp.int32)
-    gather = lambda level, after: gather_blocks(
-        level, blk_target, blk_source, blk_count, place, weights, n_row, n_col, after
-    )
-    plain = lambda messages: [(message, None) for message in messages]
+    here = [lax.axis_index(axis).astype(jnp.int32) for axis in ("row", "col")]
+    slots = jnp.concatenate(
+        [blk_target.reshape(levels - 1, -1), blk_source.reshape(levels - 1, -1)]
+        + [blk_count.reshape(levels - 1, 1)]
+        + [jnp.full((levels - 1, 1), index) for index in here],
+        axis=1,
+    )
+    gather = lambda level, after: gather_blocks(level, slots, weights, n_row, n_col, after)
+    tidy = lambda level, flipped, after: split(totals[level], n_row, n_col, flipped, after)
     forward = [first_solve(right, inverse)]
-    total = gather(0, ())
-    coupling = []
+    totals = [gather(0, ())]
+    up, down = [], []
     for level in range(1, levels):
-        coupling.append(split(total, n_row, n_col, forward[-1:] if level > 1 else ()))
-        pieces = gather_row(forward[-1], coupling[-1][:1])
-        far = couple(pieces, *coupling[-1], False, (n_col // 2, n_col), 1)
-        near = couple(pieces, *coupling[-1], False, (0, n_col // 2), 1)
-        after = ()
+        solved = forward[-1:]
+        up.append(tidy(level - 1, False, solved if level > 1 else ()))
+        if level > 1:
+            down.append(tidy(level - 2, True, solved))
+        pieces = gather_row(forward[-1], [pair[0] for pair in up[-1:] + down[-1:]])
+        far = couple(pieces, *up[-1], (n_col // 2, n_col), 1)
+        near = couple(pieces, *up[-1], (0, n_col // 2), 1)
         if level < levels - 1:
-            total = gather(level, near[:1])
-            after = (total,)
+            totals.append(gather(level, near[:1]))
+            after = totals[-1:]
+        else:
+            down.append(tidy(level - 1, True, near[:1]))
+            after = down[-1][:1]
         pieces = plain(exchange_each(near + far, "col"))
         forward.append(solve(right, inverse, level, pieces, False, after))
     backward = [None] * levels
     backward[-1] = solve(forward[-1], inverse, levels - 1, [], True)
     for level in range(levels - 2, -1, -1):
         pieces = plain(exchange_each([backward[level + 1]] * n_col, "col"))
-        sent = couple(pieces, *coupling[level], True, (2, n_row), 2)
-        kept = couple(pieces, *coupling[level], True, (0, 2), 2)
+        sent = couple(pieces, *down[level], (2, n_row), 2)
+        kept = couple(pieces, *down[level], (0, 2), 2)
+        if level == levels - 2:
+            forward_out = stack(forward, kept[:1])
         pieces = deliver_row(kept + sent)
-        backward[level] = solve(forward[level], inverse, level, pieces, True)
-    outs = stack(forward, backward)
-    return tuple(out.reshape(rhs.shape) for out in outs)
+        after = (forward_out,) if level == levels - 2 else ()
+        backward[level] = solve(forward[level], inverse, level, pieces, True, after)
+    return forward_out.reshape(rhs.shape), stack(backward).reshape(rhs.shape)
+
+
+def plain(messages):
+    return [(message, None) for message in messages]
 
 
 def fold_for(index, piece):

time: 181 us -> 177 us (0.978)
  waiting for transfers between devices: 91.4 us -> 82.2 us
  Pallas kernels: 23.5 us -> 26.3 us
  starting transfers between devices: 62.3 us -> 64.8 us
    ppermute x10, waiting for transfers between devices: 41 us -> 35 us  [far_exchange(): lax.ppermute(segment, axis, [(i, i ^ size // 2) for i in range(size)])]
    ppermute x60, waiting for transfers between devices: 50.5 us -> 47.2 us  [exchange_each(): lax.ppermute(messages[d], axis, [(i, i ^ d) for i in range(size)])]
    ppermute x10, starting transfers between devices: 6.06 us -> 8.6 us  [far_exchange(): lax.ppermute(segment, axis, [(i, i ^ size // 2) for i in range(size)])]
    pallas_call x26 -> x32, Pallas kernels: 12.2 us -> 14.6 us  [the longest x20 7.89 us: couple(): pl.pallas_call(functools.partial(couple_kernel, terms, span), out_shape=[...]
  transfers between devices with their start and end apart: 70 -> 70, of which waited for: 57 -> 52; matrix products, arithmetic and copies ran while one was open for 0% -> 1% of each run, Pallas kernels for 7% -> 10%
where the time goes in v8:
time: 177 us
  waiting for transfers between devices  82.2 us (46%)
  starting transfers between devices  64.8 us (37%)
  Pallas kernels  26.3 us (15%)
  local copies, waits for them, and re-layouts  2.48 us (1%)
    ppermute x60, starting transfers between devices, exchange_each(): lax.ppermute(messages[d], axis, [(i, i ^ d) for i in range(size)])  56.2 us
    ppermute x60, waiting for transfers between devices, exchange_each(): lax.ppermute(messages[d], axis, [(i, i ^ d) for i in range(size)])  47.2 us
    ppermute x10, waiting for transfers between devices, far_exchange(): lax.ppermute(segment, axis, [(i, i ^ size // 2) for i in range(size)])  35 us
    ppermute x10, starting transfers between devices, far_exchange(): lax.ppermute(segment, axis, [(i, i ^ size // 2) for i in range(size)])  8.6 us
    pallas_call x5, Pallas kernels, gather_blocks(): pl.pallas_call(functools.partial(gather_blocks_kernel, n_row, n_col, leve...  8.2 us
    pallas_call x20, Pallas kernels, couple(): pl.pallas_call(functools.partial(couple_kernel, terms, span), out_shape=[...  7.89 us
    pallas_call x10, Pallas kernels, split(): pl.pallas_call(functools.partial(split_kernel, n_col, flipped), out_shape...  5.3 us
  transfers between devices with their start and end apart: 70, of which 52 were waited for; matrix products, arithmetic and copies ran while one was open for 1% of the time, Pallas kernels for 10%

profile of v8, /device:TPU:0, one launch (start us, length us, event | category | flops | bytes accessed | tf_op | source)
XLA Modules:
  0.0 176.9 jit_solution(357620235638330382)
XLA Ops:
  0.6 1.7 first_solve.1.refs_0_
  2.3 4.1 %collective-permute-start = (f32[64,128]{1,0:T(8,128)}, f32[64,128]{1,0:T(8,128)S(1)}, u32[]{:S(2)}, u32[]{:S(2)}) collective-permute-start(f32[64,128]{1,0:T(8,128)} %first_solve.1.refs_0_), channel_id=1, source_target_pairs={{0,16},{4,20},{8,24},{12,28},{16,0},{20,4},{24,8},{28,12},{1,17},{... | collective-permute-start | bytes 98312 | tf_op jit(solution)/shard_map/ppermute | solution.py:283
  7.9 2.2 %gather_blocks_0.1.total_ref = f32[32,128,128]{2,1,0:T(8,128)S(1)} custom-call(s32[5,67]{1,0:T(8,128)S(1)} %concatenate.3.slots_ref, f32[5,32,128,128]{3,2,1,0:T(8,128)} %bitcast.14), custom_call_target="tpu_custom_call" | custom-call | flops 524288 | bytes 4194304 | tf_op jit(solution)/shard_map/gather_blocks_0/pallas_call | solution.py:66
  10.5 2.8 %collective-permute-start.3 = (f32[2,64,128]{2,1,0:T(8,128)S(1)}, f32[2,64,128]{2,1,0:T(8,128)S(1)}, u32[]{:S(2)}, u32[]{:S(2)}) collective-permute-start(f32[2,64,128]{2,1,0:T(8,128)S(1)} %combine.10.refs_0_), channel_id=1, source_target_pairs={{0,12},{4,8},{8,4},{12,0},{16,28},{20,24},{24,20},{28,16},{1,13},{... | collective-permute-start | bytes 196616 | tf_op jit(solution)/shard_map/ppermute | solution.py:309
  14.1 2.3 %collective-permute-done.3.refs_3_ = f32[2,64,128]{2,1,0:T(8,128)S(1)} collective-permute-done((f32[2,64,128]{2,1,0:T(8,128)S(1)}, f32[2,64,128]{2,1,0:T(8,128)S(1)}, u32[]{:S(2)}, u32[]{:S(2)}) %collective-permute-start.3) | collective-permute-done | bytes 65568 | tf_op jit(solution)/shard_map/ppermute | solution.py:309
  16.4 1.2 collective-permute-done.2.refs_2_
  18.3 1.7 collective-permute-start.5
  21.0 1.4 gather_blocks_1.1.refs_6_.total_ref
  25.4 3.0 %collective-permute-done.7.refs_1_ = f32[64,128]{1,0:T(8,128)S(1)} collective-permute-done((f32[64,128]{1,0:T(8,128)S(1)}, f32[64,128]{1,0:T(8,128)S(1)}, u32[]{:S(2)}, u32[]{:S(2)}) %collective-permute-start.7) | collective-permute-done | bytes 32800 | tf_op jit(solution)/shard_map/ppermute | solution.py:283
  28.3 1.6 collective-permute-start.10
  30.4 1.4 collective-permute-start.8
  31.8 1.7 collective-permute-done.10.refs_3_
  36.4 1.4 collective-permute-start.11
  37.8 1.8 %gather_blocks_2.1.refs_6_.total_ref = f32[32,128,128]{2,1,0:T(8,128)S(1)} custom-call(s32[5,67]{1,0:T(8,128)S(1)} %concatenate.3.slots_ref, f32[5,32,128,128]{3,2,1,0:T(8,128)S(1)} %bitcast.18, f32[64,128]{1,0:T(8,128)S(1)} %get-tuple-element.76.refs_0_.refs_2_), custom_call_target="tpu_custom_call" | custom-call | flops 524288 | bytes 4194304 | tf_op jit(solution)/shard_map/gather_blocks_2/pallas_call | solution.py:66
  41.7 3.3 %collective-permute-done.14.refs_1_ = f32[64,128]{1,0:T(8,128)S(1)} collective-permute-done((f32[64,128]{1,0:T(8,128)S(1)}, f32[64,128]{1,0:T(8,128)S(1)}, u32[]{:S(2)}, u32[]{:S(2)}) %collective-permute-start.14) | collective-permute-done | bytes 32800 | tf_op jit(solution)/shard_map/ppermute | solution.py:283
  45.0 2.1 %collective-permute-start.17 = (f32[2,64,128]{2,1,0:T(8,128)S(1)}, f32[2,64,128]{2,1,0:T(8,128)S(1)}, u32[]{:S(2)}, u32[]{:S(2)}) collective-permute-start(f32[2,64,128]{2,1,0:T(8,128)S(1)} %combine.12.refs_0_), channel_id=1, source_target_pairs={{0,12},{4,8},{8,4},{12,0},{16,28},{20,24},{24,20},{28,16},{1,13},{... | collective-permute-start | bytes 196616 | tf_op jit(solution)/shard_map/ppermute | solution.py:309
  48.5 1.7 collective-permute-done.17.refs_3_
  50.2 1.2 collective-permute-done.16.refs_2_
  52.6 1.0 collective-permute-start.19
  54.0 1.3 collective-permute-start.18
  55.3 1.4 gather_blocks_3.1.refs_6_.total_ref
  59.0 3.5 %collective-permute-done.21.refs_1_ = f32[64,128]{1,0:T(8,128)S(1)} collective-permute-done((f32[64,128]{1,0:T(8,128)S(1)}, f32[64,128]{1,0:T(8,128)S(1)}, u32[]{:S(2)}, u32[]{:S(2)}) %collective-permute-start.21) | collective-permute-done | bytes 32800 | tf_op jit(solution)/shard_map/ppermute | solution.py:283
  62.5 1.0 collective-permute-start.24
  64.4 1.5 collective-permute-start.22
  66.0 1.7 collective-permute-done.24.refs_3_
  70.5 1.3 collective-permute-start.25
  71.8 1.5 gather_blocks_4.1.refs_6_.total_ref
  75.3 3.5 %collective-permute-done.28.refs_1_ = f32[64,128]{1,0:T(8,128)S(1)} collective-permute-done((f32[64,128]{1,0:T(8,128)S(1)}, f32[64,128]{1,0:T(8,128)S(1)}, u32[]{:S(2)}, u32[]{:S(2)}) %collective-permute-start.28) | collective-permute-done | bytes 32800 | tf_op jit(solution)/shard_map/ppermute | solution.py:283
  78.8 2.0 %collective-permute-start.31 = (f32[2,64,128]{2,1,0:T(8,128)S(1)}, f32[2,64,128]{2,1,0:T(8,128)S(1)}, u32[]{:S(2)}, u32[]{:S(2)}) collective-permute-start(f32[2,64,128]{2,1,0:T(8,128)S(1)} %combine.14.refs_0_), channel_id=1, source_target_pairs={{0,12},{4,8},{8,4},{12,0},{16,28},{20,24},{24,20},{28,16},{1,13},{... | collective-permute-start | bytes 196616 | tf_op jit(solution)/shard_map/ppermute | solution.py:309
  82.3 1.8 %collective-permute-done.31.refs_3_ = f32[2,64,128]{2,1,0:T(8,128)S(1)} collective-permute-done((f32[2,64,128]{2,1,0:T(8,128)S(1)}, f32[2,64,128]{2,1,0:T(8,128)S(1)}, u32[]{:S(2)}, u32[]{:S(2)}) %collective-permute-start.31) | collective-permute-done | bytes 65568 | tf_op jit(solution)/shard_map/ppermute | solution.py:309
  84.1 1.0 collective-permute-done.30.refs_2_
  86.5 1.1 collective-permute-start.33
  88.0 1.2 collective-permute-start.32
  92.3 1.0 collective-permute-start.36
  93.4 1.5 collective-permute-done.37.refs_3_
  95.0 1.2 collective-permute-done.36.refs_2_
  96.7 1.0 collective-permute-start.38
  97.8 1.0 collective-permute-start.39
  98.8 1.5 collective-permute-start.40
  100.6 1.4 collective-permute-done.38.refs_1_
  102.0 1.0 collective-permute-done.40.refs_3_
  104.2 3.7 %collective-permute-done.41.refs_3_ = f32[64,128]{1,0:T(8,128)S(1)} collective-permute-done((f32[64,128]{1,0:T(8,128)S(1)}, f32[64,128]{1,0:T(8,128)S(1)}, u32[]{:S(2)}, u32[]{:S(2)}) %collective-permute-start.41) | collective-permute-done | bytes 32800 | tf_op jit(solution)/shard_map/ppermute | solution.py:283
  109.1 1.1 collective-permute-start.43
  111.0 1.5 collective-permute-done.44.refs_3_
  113.9 2.1 %collective-permute-start.45 = (f32[2,64,128]{2,1,0:T(8,128)S(1)}, f32[2,64,128]{2,1,0:T(8,128)S(1)}, u32[]{:S(2)}, u32[]{:S(2)}) collective-permute-start(f32[2,64,128]{2,1,0:T(8,128)S(1)} %get-tuple-element.112), channel_id=1, source_target_pairs={{0,12},{4,8},{8,4},{12,0},{16,28},{20,24},{24,20},{28,16},{1,13},{... | collective-permute-start | bytes 196616 | tf_op jit(solution)/shard_map/ppermute | solution.py:309
  117.7 2.1 %collective-permute-done.45.refs_1_ = f32[2,64,128]{2,1,0:T(8,128)S(1)} collective-permute-done((f32[2,64,128]{2,1,0:T(8,128)S(1)}, f32[2,64,128]{2,1,0:T(8,128)S(1)}, u32[]{:S(2)}, u32[]{:S(2)}) %collective-permute-start.45) | collective-permute-done | bytes 65568 | tf_op jit(solution)/shard_map/ppermute | solution.py:309
  121.6 4.6 %collective-permute-done.48.refs_3_ = f32[64,128]{1,0:T(8,128)S(1)} collective-permute-done((f32[64,128]{1,0:T(8,128)S(1)}, f32[64,128]{1,0:T(8,128)S(1)}, u32[]{:S(2)}, u32[]{:S(2)}) %collective-permute-start.48) | collective-permute-done | bytes 32800 | tf_op jit(solution)/shard_map/ppermute | solution.py:283
  126.4 1.0 collective-permute-start.50
  128.2 1.5 collective-permute-done.51.refs_3_
  131.2 1.2 collective-permute-start.52
  132.4 1.0 collective-permute-start.53
  133.4 1.3 collective-permute-start.54
  135.0 2.0 %collective-permute-done.52.refs_1_ = f32[2,64,128]{2,1,0:T(8,128)S(1)} collective-permute-done((f32[2,64,128]{2,1,0:T(8,128)S(1)}, f32[2,64,128]{2,1,0:T(8,128)S(1)}, u32[]{:S(2)}, u32[]{:S(2)}) %collective-permute-start.52) | collective-permute-done | bytes 65568 | tf_op jit(solution)/shard_map/ppermute | solution.py:309
  138.1 4.5 %collective-permute-done.55.refs_3_ = f32[64,128]{1,0:T(8,128)S(1)} collective-permute-done((f32[64,128]{1,0:T(8,128)S(1)}, f32[64,128]{1,0:T(8,128)S(1)}, u32[]{:S(2)}, u32[]{:S(2)}) %collective-permute-start.55) | collective-permute-done | bytes 32800 | tf_op jit(solution)/shard_map/ppermute | solution.py:283
  144.8 1.5 collective-permute-done.58.refs_3_
  147.7 1.9 %collective-permute-start.59 = (f32[2,64,128]{2,1,0:T(8,128)S(1)}, f32[2,64,128]{2,1,0:T(8,128)S(1)}, u32[]{:S(2)}, u32[]{:S(2)}) collective-permute-start(f32[2,64,128]{2,1,0:T(8,128)S(1)} %get-tuple-element.122), channel_id=1, source_target_pairs={{0,12},{4,8},{8,4},{12,0},{16,28},{20,24},{24,20},{28,16},{1,13},{... | collective-permute-start | bytes 196616 | tf_op jit(solution)/shard_map/ppermute | solution.py:309
  151.5 2.1 %collective-permute-done.59.refs_1_ = f32[2,64,128]{2,1,0:T(8,128)S(1)} collective-permute-done((f32[2,64,128]{2,1,0:T(8,128)S(1)}, f32[2,64,128]{2,1,0:T(8,128)S(1)}, u32[]{:S(2)}, u32[]{:S(2)}) %collective-permute-start.59) | collective-permute-done | bytes 65568 | tf_op jit(solution)/shard_map/ppermute | solution.py:309
  155.1 4.6 %collective-permute-done.62.refs_3_ = f32[64,128]{1,0:T(8,128)S(1)} collective-permute-done((f32[64,128]{1,0:T(8,128)S(1)}, f32[64,128]{1,0:T(8,128)S(1)}, u32[]{:S(2)}, u32[]{:S(2)}) %collective-permute-start.62) | collective-permute-done | bytes 32800 | tf_op jit(solution)/shard_map/ppermute | solution.py:283
  160.7 1.1 collective-permute-start.63
  161.8 1.5 collective-permute-done.65.refs_3_
  164.5 1.4 collective-permute-start.66
  166.8 1.2 collective-permute-start.68
  168.4 2.0 %collective-permute-done.66.refs_1_ = f32[2,64,128]{2,1,0:T(8,128)S(1)} collective-permute-done((f32[2,64,128]{2,1,0:T(8,128)S(1)}, f32[2,64,128]{2,1,0:T(8,128)S(1)}, u32[]{:S(2)}, u32[]{:S(2)}) %collective-permute-start.66) | collective-permute-done | bytes 65568 | tf_op jit(solution)/shard_map/ppermute | solution.py:309
  171.6 4.4 %collective-permute-done.69.refs_3_ = f32[64,128]{1,0:T(8,128)S(1)} collective-permute-done((f32[64,128]{1,0:T(8,128)S(1)}, f32[64,128]{1,0:T(8,128)S(1)}, u32[]{:S(2)}, u32[]{:S(2)}) %collective-permute-start.69) | collective-permute-done | bytes 32800 | tf_op jit(solution)/shard_map/ppermute | solution.py:283
  (155 shorter events, 55.7 us)
Async XLA Ops:
  2.3 8.2 %collective-permute-start = (f32[64,128]{1,0:T(8,128)}, f32[64,128]{1,0:T(8,128)S(1)}, u32[]{:S(2)}, u32[]{:S(2)}) collective-permute-start(f32[64,128]{1,0:T(8,128)} %first_solve.1.refs_0_), channel_id=1, source_target_pairs={{0,16},{4,20},{8,24},{12,28},{16,0},{20,4},{24,8},{28,12},{1,17},{... | collective-permute-start | bytes 98312 | tf_op jit(solution)/shard_map/ppermute | solution.py:283
  10.5 5.9 %collective-permute-start.3 = (f32[2,64,128]{2,1,0:T(8,128)S(1)}, f32[2,64,128]{2,1,0:T(8,128)S(1)}, u32[]{:S(2)}, u32[]{:S(2)}) collective-permute-start(f32[2,64,128]{2,1,0:T(8,128)S(1)} %combine.10.refs_0_), channel_id=1, source_target_pairs={{0,12},{4,8},{8,4},{12,0},{16,28},{20,24},{24,20},{28,16},{1,13},{... | collective-permute-start | bytes 196616 | tf_op jit(solution)/shard_map/ppermute | solution.py:309
  13.3 4.3 %collective-permute-start.2 = (f32[2,64,128]{2,1,0:T(8,128)S(1)}, f32[2,64,128]{2,1,0:T(8,128)S(1)}, u32[]{:S(2)}, u32[]{:S(2)}) collective-permute-start(f32[2,64,128]{2,1,0:T(8,128)S(1)} %combine.10.refs_0_), channel_id=1, source_target_pairs={{0,8},{4,12},{8,0},{12,4},{16,24},{20,28},{24,16},{28,20},{1,9},{5... | collective-permute-start | bytes 196616 | tf_op jit(solution)/shard_map/ppermute | solution.py:309
  13.6 4.3 %collective-permute-start.1 = (f32[2,64,128]{2,1,0:T(8,128)S(1)}, f32[2,64,128]{2,1,0:T(8,128)S(1)}, u32[]{:S(2)}, u32[]{:S(2)}) collective-permute-start(f32[2,64,128]{2,1,0:T(8,128)S(1)} %combine.10.refs_0_), channel_id=1, source_target_pairs={{0,4},{4,0},{8,12},{12,8},{16,20},{20,16},{24,28},{28,24},{1,5},{5... | collective-permute-start | bytes 196616 | tf_op jit(solution)/shard_map/ppermute | solution.py:309
  18.3 4.1 %collective-permute-start.5 = (f32[64,128]{1,0:T(8,128)S(1)}, f32[64,128]{1,0:T(8,128)S(1)}, u32[]{:S(2)}, u32[]{:S(2)}) collective-permute-start(f32[64,128]{1,0:T(8,128)S(1)} %get-tuple-element.71), channel_id=1, source_target_pairs={{0,2},{1,3},{2,0},{3,1},{4,6},{5,7},{6,4},{7,5},{8,10},{9,11},{10,... | collective-permute-start | bytes 98312 | tf_op jit(solution)/shard_map/ppermute | solution.py:309
  19.9 3.3 %collective-permute-start.6 = (f32[64,128]{1,0:T(8,128)S(1)}, f32[64,128]{1,0:T(8,128)S(1)}, u32[]{:S(2)}, u32[]{:S(2)}) collective-permute-start(f32[64,128]{1,0:T(8,128)S(1)} %get-tuple-element.72), channel_id=1, source_target_pairs={{0,3},{1,2},{2,1},{3,0},{4,7},{5,6},{6,5},{7,4},{8,11},{9,10},{10,... | collective-permute-start | bytes 98312 | tf_op jit(solution)/shard_map/ppermute | solution.py:309
  23.5 4.9 %collective-permute-start.7 = (f32[64,128]{1,0:T(8,128)S(1)}, f32[64,128]{1,0:T(8,128)S(1)}, u32[]{:S(2)}, u32[]{:S(2)}) collective-permute-start(f32[64,128]{1,0:T(8,128)S(1)} %solve_up.5.refs_0_.refs_1_), channel_id=1, source_target_pairs={{0,16},{4,20},{8,24},{12,28},{16,0},{20,4},{24,8},{28,12},{1,17},{... | collective-permute-start | bytes 98312 | tf_op jit(solution)/shard_map/ppermute | solution.py:283
  28.3 5.2 %collective-permute-start.10 = (f32[2,64,128]{2,1,0:T(8,128)S(1)}, f32[2,64,128]{2,1,0:T(8,128)S(1)}, u32[]{:S(2)}, u32[]{:S(2)}) collective-permute-start(f32[2,64,128]{2,1,0:T(8,128)S(1)} %combine.11.refs_0_), channel_id=1, source_target_pairs={{0,12},{4,8},{8,4},{12,0},{16,28},{20,24},{24,20},{28,16},{1,13},{... | collective-permute-start | bytes 196616 | tf_op jit(solution)/shard_map/ppermute | solution.py:309
  30.0 4.3 %collective-permute-start.9 = (f32[2,64,128]{2,1,0:T(8,128)S(1)}, f32[2,64,128]{2,1,0:T(8,128)S(1)}, u32[]{:S(2)}, u32[]{:S(2)}) collective-permute-start(f32[2,64,128]{2,1,0:T(8,128)S(1)} %combine.11.refs_0_), channel_id=1, source_target_pairs={{0,8},{4,12},{8,0},{12,4},{16,24},{20,28},{24,16},{28,20},{1,9},{5... | collective-permute-start | bytes 196616 | tf_op jit(solution)/shard_map/ppermute | solution.py:309
  30.4 4.3 %collective-permute-start.8 = (f32[2,64,128]{2,1,0:T(8,128)S(1)}, f32[2,64,128]{2,1,0:T(8,128)S(1)}, u32[]{:S(2)}, u32[]{:S(2)}) collective-permute-start(f32[2,64,128]{2,1,0:T(8,128)S(1)} %combine.11.refs_0_), channel_id=1, source_target_pairs={{0,4},{4,0},{8,12},{12,8},{16,20},{20,16},{24,28},{28,24},{1,5},{5... | collective-permute-start | bytes 196616 | tf_op jit(solution)/shard_map/ppermute | solution.py:309
  35.1 4.5 %collective-permute-start.12 = (f32[64,128]{1,0:T(8,128)S(1)}, f32[64,128]{1,0:T(8,128)S(1)}, u32[]{:S(2)}, u32[]{:S(2)}) collective-permute-start(f32[64,128]{1,0:T(8,128)S(1)} %get-tuple-element.78), channel_id=1, source_target_pairs={{0,2},{1,3},{2,0},{3,1},{4,6},{5,7},{6,4},{7,5},{8,10},{9,11},{10,... | collective-permute-start | bytes 98312 | tf_op jit(solution)/shard_map/ppermute | solution.py:309
  35.9 3.7 %collective-permute-start.13 = (f32[64,128]{1,0:T(8,128)S(1)}, f32[64,128]{1,0:T(8,128)S(1)}, u32[]{:S(2)}, u32[]{:S(2)}) collective-permute-start(f32[64,128]{1,0:T(8,128)S(1)} %get-tuple-element.79), channel_id=1, source_target_pairs={{0,3},{1,2},{2,1},{3,0},{4,7},{5,6},{6,5},{7,4},{8,11},{9,10},{10,... | collective-permute-start | bytes 98312 | tf_op jit(solution)/shard_map/ppermute | solution.py:309
  36.4 3.3 %collective-permute-start.11 = (f32[64,128]{1,0:T(8,128)S(1)}, f32[64,128]{1,0:T(8,128)S(1)}, u32[]{:S(2)}, u32[]{:S(2)}) collective-permute-start(f32[64,128]{1,0:T(8,128)S(1)} %get-tuple-element.77), channel_id=1, source_target_pairs={{0,1},{1,0},{2,3},{3,2},{4,5},{5,4},{6,7},{7,6},{8,9},{9,8},{10,11... | collective-permute-start | bytes 98312 | tf_op jit(solution)/shard_map/ppermute | solution.py:309
  39.8 5.2 %collective-permute-start.14 = (f32[64,128]{1,0:T(8,128)S(1)}, f32[64,128]{1,0:T(8,128)S(1)}, u32[]{:S(2)}, u32[]{:S(2)}) collective-permute-start(f32[64,128]{1,0:T(8,128)S(1)} %solve_up.6.refs_0_.refs_2_), channel_id=1, source_target_pairs={{0,16},{4,20},{8,24},{12,28},{16,0},{20,4},{24,8},{28,12},{1,17},{... | collective-permute-start | bytes 98312 | tf_op jit(solution)/shard_map/ppermute | solution.py:283
  45.0 5.2 %collective-permute-start.17 = (f32[2,64,128]{2,1,0:T(8,128)S(1)}, f32[2,64,128]{2,1,0:T(8,128)S(1)}, u32[]{:S(2)}, u32[]{:S(2)}) collective-permute-start(f32[2,64,128]{2,1,0:T(8,128)S(1)} %combine.12.refs_0_), channel_id=1, source_target_pairs={{0,12},{4,8},{8,4},{12,0},{16,28},{20,24},{24,20},{28,16},{1,13},{... | collective-permute-start | bytes 196616 | tf_op jit(solution)/shard_map/ppermute | solution.py:309
  47.1 4.3 %collective-permute-start.16 = (f32[2,64,128]{2,1,0:T(8,128)S(1)}, f32[2,64,128]{2,1,0:T(8,128)S(1)}, u32[]{:S(2)}, u32[]{:S(2)}) collective-permute-start(f32[2,64,128]{2,1,0:T(8,128)S(1)} %combine.12.refs_0_), channel_id=1, source_target_pairs={{0,8},{4,12},{8,0},{12,4},{16,24},{20,28},{24,16},{28,20},{1,9},{5... | collective-permute-start | bytes 196616 | tf_op jit(solution)/shard_map/ppermute | solution.py:309
  47.9 4.3 %collective-permute-start.15 = (f32[2,64,128]{2,1,0:T(8,128)S(1)}, f32[2,64,128]{2,1,0:T(8,128)S(1)}, u32[]{:S(2)}, u32[]{:S(2)}) collective-permute-start(f32[2,64,128]{2,1,0:T(8,128)S(1)} %combine.12.refs_0_), channel_id=1, source_target_pairs={{0,4},{4,0},{8,12},{12,8},{16,20},{20,16},{24,28},{28,24},{1,5},{5... | collective-permute-start | bytes 196616 | tf_op jit(solution)/shard_map/ppermute | solution.py:309
  52.6 4.1 %collective-permute-start.19 = (f32[64,128]{1,0:T(8,128)S(1)}, f32[64,128]{1,0:T(8,128)S(1)}, u32[]{:S(2)}, u32[]{:S(2)}) collective-permute-start(f32[64,128]{1,0:T(8,128)S(1)} %get-tuple-element.85), channel_id=1, source_target_pairs={{0,2},{1,3},{2,0},{3,1},{4,6},{5,7},{6,4},{7,5},{8,10},{9,11},{10,... | collective-permute-start | bytes 98312 | tf_op jit(solution)/shard_map/ppermute | solution.py:309
  53.6 3.6 %collective-permute-start.20 = (f32[64,128]{1,0:T(8,128)S(1)}, f32[64,128]{1,0:T(8,128)S(1)}, u32[]{:S(2)}, u32[]{:S(2)}) collective-permute-start(f32[64,128]{1,0:T(8,128)S(1)} %get-tuple-element.86), channel_id=1, source_target_pairs={{0,3},{1,2},{2,1},{3,0},{4,7},{5,6},{6,5},{7,4},{8,11},{9,10},{10,... | collective-permute-start | bytes 98312 | tf_op jit(solution)/shard_map/ppermute | solution.py:309
  57.4 5.1 %collective-permute-start.21 = (f32[64,128]{1,0:T(8,128)S(1)}, f32[64,128]{1,0:T(8,128)S(1)}, u32[]{:S(2)}, u32[]{:S(2)}) collective-permute-start(f32[64,128]{1,0:T(8,128)S(1)} %solve_up.7.refs_0_.refs_3_), channel_id=1, source_target_pairs={{0,16},{4,20},{8,24},{12,28},{16,0},{20,4},{24,8},{28,12},{1,17},{... | collective-permute-start | bytes 98312 | tf_op jit(solution)/shard_map/ppermute | solution.py:283
  62.5 5.2 %collective-permute-start.24 = (f32[2,64,128]{2,1,0:T(8,128)S(1)}, f32[2,64,128]{2,1,0:T(8,128)S(1)}, u32[]{:S(2)}, u32[]{:S(2)}) collective-permute-start(f32[2,64,128]{2,1,0:T(8,128)S(1)} %combine.13.refs_0_), channel_id=1, source_target_pairs={{0,12},{4,8},{8,4},{12,0},{16,28},{20,24},{24,20},{28,16},{1,13},{... | collective-permute-start | bytes 196616 | tf_op jit(solution)/shard_map/ppermute | solution.py:309
  63.5 4.3 %collective-permute-start.23 = (f32[2,64,128]{2,1,0:T(8,128)S(1)}, f32[2,64,128]{2,1,0:T(8,128)S(1)}, u32[]{:S(2)}, u32[]{:S(2)}) collective-permute-start(f32[2,64,128]{2,1,0:T(8,128)S(1)} %combine.13.refs_0_), channel_id=1, source_target_pairs={{0,8},{4,12},{8,0},{12,4},{16,24},{20,28},{24,16},{28,20},{1,9},{5... | collective-permute-start | bytes 196616 | tf_op jit(solution)/shard_map/ppermute | solution.py:309
  64.4 4.3 %collective-permute-start.22 = (f32[2,64,128]{2,1,0:T(8,128)S(1)}, f32[2,64,128]{2,1,0:T(8,128)S(1)}, u32[]{:S(2)}, u32[]{:S(2)}) collective-permute-start(f32[2,64,128]{2,1,0:T(8,128)S(1)} %combine.13.refs_0_), channel_id=1, source_target_pairs={{0,4},{4,0},{8,12},{12,8},{16,20},{20,16},{24,28},{28,24},{1,5},{5... | collective-permute-start | bytes 196616 | tf_op jit(solution)/shard_map/ppermute | solution.py:309
  69.1 4.1 %collective-permute-start.26 = (f32[64,128]{1,0:T(8,128)S(1)}, f32[64,128]{1,0:T(8,128)S(1)}, u32[]{:S(2)}, u32[]{:S(2)}) collective-permute-start(f32[64,128]{1,0:T(8,128)S(1)} %get-tuple-element.92), channel_id=1, source_target_pairs={{0,2},{1,3},{2,0},{3,1},{4,6},{5,7},{6,4},{7,5},{8,10},{9,11},{10,... | collective-permute-start | bytes 98312 | tf_op jit(solution)/shard_map/ppermute | solution.py:309
  70.1 3.7 %collective-permute-start.27 = (f32[64,128]{1,0:T(8,128)S(1)}, f32[64,128]{1,0:T(8,128)S(1)}, u32[]{:S(2)}, u32[]{:S(2)}) collective-permute-start(f32[64,128]{1,0:T(8,128)S(1)} %get-tuple-element.93), channel_id=1, source_target_pairs={{0,3},{1,2},{2,1},{3,0},{4,7},{5,6},{6,5},{7,4},{8,11},{9,10},{10,... | collective-permute-start | bytes 98312 | tf_op jit(solution)/shard_map/ppermute | solution.py:309
  70.5 3.3 %collective-permute-start.25 = (f32[64,128]{1,0:T(8,128)S(1)}, f32[64,128]{1,0:T(8,128)S(1)}, u32[]{:S(2)}, u32[]{:S(2)}) collective-permute-start(f32[64,128]{1,0:T(8,128)S(1)} %get-tuple-element.91), channel_id=1, source_target_pairs={{0,1},{1,0},{2,3},{3,2},{4,5},{5,4},{6,7},{7,6},{8,9},{9,8},{10,11... | collective-permute-start | bytes 98312 | tf_op jit(solution)/shard_map/ppermute | solution.py:309
  73.9 4.9 %collective-permute-start.28 = (f32[64,128]{1,0:T(8,128)S(1)}, f32[64,128]{1,0:T(8,128)S(1)}, u32[]{:S(2)}, u32[]{:S(2)}) collective-permute-start(f32[64,128]{1,0:T(8,128)S(1)} %solve_up.8.refs_0_.refs_4_), channel_id=1, source_target_pairs={{0,16},{4,20},{8,24},{12,28},{16,0},{20,4},{24,8},{28,12},{1,17},{... | collective-permute-start | bytes 98312 | tf_op jit(solution)/shard_map/ppermute | solution.py:283
  78.8 5.3 %collective-permute-start.31 = (f32[2,64,128]{2,1,0:T(8,128)S(1)}, f32[2,64,128]{2,1,0:T(8,128)S(1)}, u32[]{:S(2)}, u32[]{:S(2)}) collective-permute-start(f32[2,64,128]{2,1,0:T(8,128)S(1)} %combine.14.refs_0_), channel_id=1, source_target_pairs={{0,12},{4,8},{8,4},{12,0},{16,28},{20,24},{24,20},{28,16},{1,13},{... | collective-permute-start | bytes 196616 | tf_op jit(solution)/shard_map/ppermute | solution.py:309
  80.9 4.3 %collective-permute-start.30 = (f32[2,64,128]{2,1,0:T(8,128)S(1)}, f32[2,64,128]{2,1,0:T(8,128)S(1)}, u32[]{:S(2)}, u32[]{:S(2)}) collective-permute-start(f32[2,64,128]{2,1,0:T(8,128)S(1)} %combine.14.refs_0_), channel_id=1, source_target_pairs={{0,8},{4,12},{8,0},{12,4},{16,24},{20,28},{24,16},{28,20},{1,9},{5... | collective-permute-start | bytes 196616 | tf_op jit(solution)/shard_map/ppermute | solution.py:309
  81.8 4.3 %collective-permute-start.29 = (f32[2,64,128]{2,1,0:T(8,128)S(1)}, f32[2,64,128]{2,1,0:T(8,128)S(1)}, u32[]{:S(2)}, u32[]{:S(2)}) collective-permute-start(f32[2,64,128]{2,1,0:T(8,128)S(1)} %combine.14.refs_0_), channel_id=1, source_target_pairs={{0,4},{4,0},{8,12},{12,8},{16,20},{20,16},{24,28},{28,24},{1,5},{5... | collective-permute-start | bytes 196616 | tf_op jit(solution)/shard_map/ppermute | solution.py:309
  86.5 4.0 %collective-permute-start.33 = (f32[64,128]{1,0:T(8,128)S(1)}, f32[64,128]{1,0:T(8,128)S(1)}, u32[]{:S(2)}, u32[]{:S(2)}) collective-permute-start(f32[64,128]{1,0:T(8,128)S(1)} %get-tuple-element.99), channel_id=1, source_target_pairs={{0,2},{1,3},{2,0},{3,1},{4,6},{5,7},{6,4},{7,5},{8,10},{9,11},{10,... | collective-permute-start | bytes 98312 | tf_op jit(solution)/shard_map/ppermute | solution.py:309
  87.6 3.6 %collective-permute-start.34 = (f32[64,128]{1,0:T(8,128)S(1)}, f32[64,128]{1,0:T(8,128)S(1)}, u32[]{:S(2)}, u32[]{:S(2)}) collective-permute-start(f32[64,128]{1,0:T(8,128)S(1)} %get-tuple-element.100), channel_id=1, source_target_pairs={{0,3},{1,2},{2,1},{3,0},{4,7},{5,6},{6,5},{7,4},{8,11},{9,10},{10,... | collective-permute-start | bytes 98312 | tf_op jit(solution)/shard_map/ppermute | solution.py:309
  91.5 3.5 %collective-permute-start.37 = (f32[64,128]{1,0:T(8,128)S(1)}, f32[64,128]{1,0:T(8,128)S(1)}, u32[]{:S(2)}, u32[]{:S(2)}) collective-permute-start(f32[64,128]{1,0:T(8,128)S(1)} %solve_down.6.refs_0_.refs_5_), channel_id=1, source_target_pairs={{0,3},{1,2},{2,1},{3,0},{4,7},{5,6},{6,5},{7,4},{8,11},{9,10},{10,... | collective-permute-start | bytes 98312 | tf_op jit(solution)/shard_map/ppermute | solution.py:309
  92.3 3.9 %collective-permute-start.36 = (f32[64,128]{1,0:T(8,128)S(1)}, f32[64,128]{1,0:T(8,128)S(1)}, u32[]{:S(2)}, u32[]{:S(2)}) collective-permute-start(f32[64,128]{1,0:T(8,128)S(1)} %solve_down.6.refs_0_.refs_5_), channel_id=1, source_target_pairs={{0,2},{1,3},{2,0},{3,1},{4,6},{5,7},{6,4},{7,5},{8,10},{9,11},{10,... | collective-permute-start | bytes 98312 | tf_op jit(solution)/shard_map/ppermute | solution.py:309
  96.7 5.2 %collective-permute-start.38 = (f32[2,64,128]{2,1,0:T(8,128)S(1)}, f32[2,64,128]{2,1,0:T(8,128)S(1)}, u32[]{:S(2)}, u32[]{:S(2)}) collective-permute-start(f32[2,64,128]{2,1,0:T(8,128)S(1)} %get-tuple-element.107), channel_id=1, source_target_pairs={{0,12},{4,8},{8,4},{12,0},{16,28},{20,24},{24,20},{28,16},{1,13},{... | collective-permute-start | bytes 196616 | tf_op jit(solution)/shard_map/ppermute | solution.py:309
  97.8 4.3 %collective-permute-start.39 = (f32[2,64,128]{2,1,0:T(8,128)S(1)}, f32[2,64,128]{2,1,0:T(8,128)S(1)}, u32[]{:S(2)}, u32[]{:S(2)}) collective-permute-start(f32[2,64,128]{2,1,0:T(8,128)S(1)} %get-tuple-element.108), channel_id=1, source_target_pairs={{0,8},{4,12},{8,0},{12,4},{16,24},{20,28},{24,16},{28,20},{1,9},{5... | collective-permute-start | bytes 196616 | tf_op jit(solution)/shard_map/ppermute | solution.py:309
  98.8 4.3 %collective-permute-start.40 = (f32[2,64,128]{2,1,0:T(8,128)S(1)}, f32[2,64,128]{2,1,0:T(8,128)S(1)}, u32[]{:S(2)}, u32[]{:S(2)}) collective-permute-start(f32[2,64,128]{2,1,0:T(8,128)S(1)} %get-tuple-element.109), channel_id=1, source_target_pairs={{0,4},{4,0},{8,12},{12,8},{16,20},{20,16},{24,28},{28,24},{1,5},{5... | collective-permute-start | bytes 196616 | tf_op jit(solution)/shard_map/ppermute | solution.py:309
  103.1 4.9 %collective-permute-start.41 = (f32[64,128]{1,0:T(8,128)S(1)}, f32[64,128]{1,0:T(8,128)S(1)}, u32[]{:S(2)}, u32[]{:S(2)}) collective-permute-start(f32[64,128]{1,0:T(8,128)S(1)} %get-tuple-element.111), channel_id=1, source_target_pairs={{0,16},{4,20},{8,24},{12,28},{16,0},{20,4},{24,8},{28,12},{1,17},{... | collective-permute-start | bytes 98312 | tf_op jit(solution)/shard_map/ppermute | solution.py:283
  109.0 3.4 %collective-permute-start.44 = (f32[64,128]{1,0:T(8,128)S(1)}, f32[64,128]{1,0:T(8,128)S(1)}, u32[]{:S(2)}, u32[]{:S(2)}) collective-permute-start(f32[64,128]{1,0:T(8,128)S(1)} %solve_down.7.refs_0_.refs_4_), channel_id=1, source_target_pairs={{0,3},{1,2},{2,1},{3,0},{4,7},{5,6},{6,5},{7,4},{8,11},{9,10},{10,... | collective-permute-start | bytes 98312 | tf_op jit(solution)/shard_map/ppermute | solution.py:309
  109.1 4.3 %collective-permute-start.43 = (f32[64,128]{1,0:T(8,128)S(1)}, f32[64,128]{1,0:T(8,128)S(1)}, u32[]{:S(2)}, u32[]{:S(2)}) collective-permute-start(f32[64,128]{1,0:T(8,128)S(1)} %solve_down.7.refs_0_.refs_4_), channel_id=1, source_target_pairs={{0,2},{1,3},{2,0},{3,1},{4,6},{5,7},{6,4},{7,5},{8,10},{9,11},{10,... | collective-permute-start | bytes 98312 | tf_op jit(solution)/shard_map/ppermute | solution.py:309
  113.9 5.9 %collective-permute-start.45 = (f32[2,64,128]{2,1,0:T(8,128)S(1)}, f32[2,64,128]{2,1,0:T(8,128)S(1)}, u32[]{:S(2)}, u32[]{:S(2)}) collective-permute-start(f32[2,64,128]{2,1,0:T(8,128)S(1)} %get-tuple-element.112), channel_id=1, source_target_pairs={{0,12},{4,8},{8,4},{12,0},{16,28},{20,24},{24,20},{28,16},{1,13},{... | collective-permute-start | bytes 196616 | tf_op jit(solution)/shard_map/ppermute | solution.py:309
  116.0 4.5 %collective-permute-start.46 = (f32[2,64,128]{2,1,0:T(8,128)S(1)}, f32[2,64,128]{2,1,0:T(8,128)S(1)}, u32[]{:S(2)}, u32[]{:S(2)}) collective-permute-start(f32[2,64,128]{2,1,0:T(8,128)S(1)} %get-tuple-element.113), channel_id=1, source_target_pairs={{0,8},{4,12},{8,0},{12,4},{16,24},{20,28},{24,16},{28,20},{1,9},{5... | collective-permute-start | bytes 196616 | tf_op jit(solution)/shard_map/ppermute | solution.py:309
  117.0 4.3 %collective-permute-start.47 = (f32[2,64,128]{2,1,0:T(8,128)S(1)}, f32[2,64,128]{2,1,0:T(8,128)S(1)}, u32[]{:S(2)}, u32[]{:S(2)}) collective-permute-start(f32[2,64,128]{2,1,0:T(8,128)S(1)} %get-tuple-element.114), channel_id=1, source_target_pairs={{0,4},{4,0},{8,12},{12,8},{16,20},{20,16},{24,28},{28,24},{1,5},{5... | collective-permute-start | bytes 196616 | tf_op jit(solution)/shard_map/ppermute | solution.py:309
  121.3 4.9 %collective-permute-start.48 = (f32[64,128]{1,0:T(8,128)S(1)}, f32[64,128]{1,0:T(8,128)S(1)}, u32[]{:S(2)}, u32[]{:S(2)}) collective-permute-start(f32[64,128]{1,0:T(8,128)S(1)} %get-tuple-element.116), channel_id=1, source_target_pairs={{0,16},{4,20},{8,24},{12,28},{16,0},{20,4},{24,8},{28,12},{1,17},{... | collective-permute-start | bytes 98312 | tf_op jit(solution)/shard_map/ppermute | solution.py:283
  126.3 3.4 %collective-permute-start.51 = (f32[64,128]{1,0:T(8,128)S(1)}, f32[64,128]{1,0:T(8,128)S(1)}, u32[]{:S(2)}, u32[]{:S(2)}) collective-permute-start(f32[64,128]{1,0:T(8,128)S(1)} %solve_down.8.refs_0_.refs_3_), channel_id=1, source_target_pairs={{0,3},{1,2},{2,1},{3,0},{4,7},{5,6},{6,5},{7,4},{8,11},{9,10},{10,... | collective-permute-start | bytes 98312 | tf_op jit(solution)/shard_map/ppermute | solution.py:309
  126.4 4.3 %collective-permute-start.50 = (f32[64,128]{1,0:T(8,128)S(1)}, f32[64,128]{1,0:T(8,128)S(1)}, u32[]{:S(2)}, u32[]{:S(2)}) collective-permute-start(f32[64,128]{1,0:T(8,128)S(1)} %solve_down.8.refs_0_.refs_3_), channel_id=1, source_target_pairs={{0,2},{1,3},{2,0},{3,1},{4,6},{5,7},{6,4},{7,5},{8,10},{9,11},{10,... | collective-permute-start | bytes 98312 | tf_op jit(solution)/shard_map/ppermute | solution.py:309
  131.2 5.8 %collective-permute-start.52 = (f32[2,64,128]{2,1,0:T(8,128)S(1)}, f32[2,64,128]{2,1,0:T(8,128)S(1)}, u32[]{:S(2)}, u32[]{:S(2)}) collective-permute-start(f32[2,64,128]{2,1,0:T(8,128)S(1)} %get-tuple-element.117), channel_id=1, source_target_pairs={{0,12},{4,8},{8,4},{12,0},{16,28},{20,24},{24,20},{28,16},{1,13},{... | collective-permute-start | bytes 196616 | tf_op jit(solution)/shard_map/ppermute | solution.py:309
  132.4 4.6 %collective-permute-start.53 = (f32[2,64,128]{2,1,0:T(8,128)S(1)}, f32[2,64,128]{2,1,0:T(8,128)S(1)}, u32[]{:S(2)}, u32[]{:S(2)}) collective-permute-start(f32[2,64,128]{2,1,0:T(8,128)S(1)} %get-tuple-element.118), channel_id=1, source_target_pairs={{0,8},{4,12},{8,0},{12,4},{16,24},{20,28},{24,16},{28,20},{1,9},{5... | collective-permute-start | bytes 196616 | tf_op jit(solution)/shard_map/ppermute | solution.py:309
  133.4 4.3 %collective-permute-start.54 = (f32[2,64,128]{2,1,0:T(8,128)S(1)}, f32[2,64,128]{2,1,0:T(8,128)S(1)}, u32[]{:S(2)}, u32[]{:S(2)}) collective-permute-start(f32[2,64,128]{2,1,0:T(8,128)S(1)} %get-tuple-element.119), channel_id=1, source_target_pairs={{0,4},{4,0},{8,12},{12,8},{16,20},{20,16},{24,28},{28,24},{1,5},{5... | collective-permute-start | bytes 196616 | tf_op jit(solution)/shard_map/ppermute | solution.py:309
  137.8 4.9 %collective-permute-start.55 = (f32[64,128]{1,0:T(8,128)S(1)}, f32[64,128]{1,0:T(8,128)S(1)}, u32[]{:S(2)}, u32[]{:S(2)}) collective-permute-start(f32[64,128]{1,0:T(8,128)S(1)} %get-tuple-element.121), channel_id=1, source_target_pairs={{0,16},{4,20},{8,24},{12,28},{16,0},{20,4},{24,8},{28,12},{1,17},{... | collective-permute-start | bytes 98312 | tf_op jit(solution)/shard_map/ppermute | solution.py:283
  142.8 3.4 %collective-permute-start.58 = (f32[64,128]{1,0:T(8,128)S(1)}, f32[64,128]{1,0:T(8,128)S(1)}, u32[]{:S(2)}, u32[]{:S(2)}) collective-permute-start(f32[64,128]{1,0:T(8,128)S(1)} %solve_down.9.refs_0_.refs_2_), channel_id=1, source_target_pairs={{0,3},{1,2},{2,1},{3,0},{4,7},{5,6},{6,5},{7,4},{8,11},{9,10},{10,... | collective-permute-start | bytes 98312 | tf_op jit(solution)/shard_map/ppermute | solution.py:309
  142.9 4.3 %collective-permute-start.57 = (f32[64,128]{1,0:T(8,128)S(1)}, f32[64,128]{1,0:T(8,128)S(1)}, u32[]{:S(2)}, u32[]{:S(2)}) collective-permute-start(f32[64,128]{1,0:T(8,128)S(1)} %solve_down.9.refs_0_.refs_2_), channel_id=1, source_target_pairs={{0,2},{1,3},{2,0},{3,1},{4,6},{5,7},{6,4},{7,5},{8,10},{9,11},{10,... | collective-permute-start | bytes 98312 | tf_op jit(solution)/shard_map/ppermute | solution.py:309
  143.8 3.3 %collective-permute-start.56 = (f32[64,128]{1,0:T(8,128)S(1)}, f32[64,128]{1,0:T(8,128)S(1)}, u32[]{:S(2)}, u32[]{:S(2)}) collective-permute-start(f32[64,128]{1,0:T(8,128)S(1)} %solve_down.9.refs_0_.refs_2_), channel_id=1, source_target_pairs={{0,1},{1,0},{2,3},{3,2},{4,5},{5,4},{6,7},{7,6},{8,9},{9,8},{10,11... | collective-permute-start | bytes 98312 | tf_op jit(solution)/shard_map/ppermute | solution.py:309
  147.7 5.9 %collective-permute-start.59 = (f32[2,64,128]{2,1,0:T(8,128)S(1)}, f32[2,64,128]{2,1,0:T(8,128)S(1)}, u32[]{:S(2)}, u32[]{:S(2)}) collective-permute-start(f32[2,64,128]{2,1,0:T(8,128)S(1)} %get-tuple-element.122), channel_id=1, source_target_pairs={{0,12},{4,8},{8,4},{12,0},{16,28},{20,24},{24,20},{28,16},{1,13},{... | collective-permute-start | bytes 196616 | tf_op jit(solution)/shard_map/ppermute | solution.py:309
  149.6 4.5 %collective-permute-start.60 = (f32[2,64,128]{2,1,0:T(8,128)S(1)}, f32[2,64,128]{2,1,0:T(8,128)S(1)}, u32[]{:S(2)}, u32[]{:S(2)}) collective-permute-start(f32[2,64,128]{2,1,0:T(8,128)S(1)} %get-tuple-element.123), channel_id=1, source_target_pairs={{0,8},{4,12},{8,0},{12,4},{16,24},{20,28},{24,16},{28,20},{1,9},{5... | collective-permute-start | bytes 196616 | tf_op jit(solution)/shard_map/ppermute | solution.py:309
  150.5 4.3 %collective-permute-start.61 = (f32[2,64,128]{2,1,0:T(8,128)S(1)}, f32[2,64,128]{2,1,0:T(8,128)S(1)}, u32[]{:S(2)}, u32[]{:S(2)}) collective-permute-start(f32[2,64,128]{2,1,0:T(8,128)S(1)} %get-tuple-element.124), channel_id=1, source_target_pairs={{0,4},{4,0},{8,12},{12,8},{16,20},{20,16},{24,28},{28,24},{1,5},{5... | collective-permute-start | bytes 196616 | tf_op jit(solution)/shard_map/ppermute | solution.py:309
  154.8 4.9 %collective-permute-start.62 = (f32[64,128]{1,0:T(8,128)S(1)}, f32[64,128]{1,0:T(8,128)S(1)}, u32[]{:S(2)}, u32[]{:S(2)}) collective-permute-start(f32[64,128]{1,0:T(8,128)S(1)} %get-tuple-element.126), channel_id=1, source_target_pairs={{0,16},{4,20},{8,24},{12,28},{16,0},{20,4},{24,8},{28,12},{1,17},{... | collective-permute-start | bytes 98312 | tf_op jit(solution)/shard_map/ppermute | solution.py:283
  159.8 3.4 %collective-permute-start.65 = (f32[64,128]{1,0:T(8,128)S(1)}, f32[64,128]{1,0:T(8,128)S(1)}, u32[]{:S(2)}, u32[]{:S(2)}) collective-permute-start(f32[64,128]{1,0:T(8,128)S(1)} %solve_down.10.refs_0_.refs_1_), channel_id=1, source_target_pairs={{0,3},{1,2},{2,1},{3,0},{4,7},{5,6},{6,5},{7,4},{8,11},{9,10},{10,... | collective-permute-start | bytes 98312 | tf_op jit(solution)/shard_map/ppermute | solution.py:309
  159.9 4.1 %collective-permute-start.64 = (f32[64,128]{1,0:T(8,128)S(1)}, f32[64,128]{1,0:T(8,128)S(1)}, u32[]{:S(2)}, u32[]{:S(2)}) collective-permute-start(f32[64,128]{1,0:T(8,128)S(1)} %solve_down.10.refs_0_.refs_1_), channel_id=1, source_target_pairs={{0,2},{1,3},{2,0},{3,1},{4,6},{5,7},{6,4},{7,5},{8,10},{9,11},{10,... | collective-permute-start | bytes 98312 | tf_op jit(solution)/shard_map/ppermute | solution.py:309
  160.7 3.3 %collective-permute-start.63 = (f32[64,128]{1,0:T(8,128)S(1)}, f32[64,128]{1,0:T(8,128)S(1)}, u32[]{:S(2)}, u32[]{:S(2)}) collective-permute-start(f32[64,128]{1,0:T(8,128)S(1)} %solve_down.10.refs_0_.refs_1_), channel_id=1, source_target_pairs={{0,1},{1,0},{2,3},{3,2},{4,5},{5,4},{6,7},{7,6},{8,9},{9,8},{10,11... | collective-permute-start | bytes 98312 | tf_op jit(solution)/shard_map/ppermute | solution.py:309
  164.5 5.8 %collective-permute-start.66 = (f32[2,64,128]{2,1,0:T(8,128)S(1)}, f32[2,64,128]{2,1,0:T(8,128)S(1)}, u32[]{:S(2)}, u32[]{:S(2)}) collective-permute-start(f32[2,64,128]{2,1,0:T(8,128)S(1)} %get-tuple-element.127), channel_id=1, source_target_pairs={{0,12},{4,8},{8,4},{12,0},{16,28},{20,24},{24,20},{28,16},{1,13},{... | collective-permute-start | bytes 196616 | tf_op jit(solution)/shard_map/ppermute | solution.py:309
  165.9 4.4 %collective-permute-start.67 = (f32[2,64,128]{2,1,0:T(8,128)S(1)}, f32[2,64,128]{2,1,0:T(8,128)S(1)}, u32[]{:S(2)}, u32[]{:S(2)}) collective-permute-start(f32[2,64,128]{2,1,0:T(8,128)S(1)} %get-tuple-element.128), channel_id=1, source_target_pairs={{0,8},{4,12},{8,0},{12,4},{16,24},{20,28},{24,16},{28,20},{1,9},{5... | collective-permute-start | bytes 196616 | tf_op jit(solution)/shard_map/ppermute | solution.py:309
  166.8 4.3 %collective-permute-start.68 = (f32[2,64,128]{2,1,0:T(8,128)S(1)}, f32[2,64,128]{2,1,0:T(8,128)S(1)}, u32[]{:S(2)}, u32[]{:S(2)}) collective-permute-start(f32[2,64,128]{2,1,0:T(8,128)S(1)} %get-tuple-element.129), channel_id=1, source_target_pairs={{0,4},{4,0},{8,12},{12,8},{16,20},{20,16},{24,28},{28,24},{1,5},{5... | collective-permute-start | bytes 196616 | tf_op jit(solution)/shard_map/ppermute | solution.py:309
  171.1 4.9 %collective-permute-start.69 = (f32[64,128]{1,0:T(8,128)S(1)}, f32[64,128]{1,0:T(8,128)S(1)}, u32[]{:S(2)}, u32[]{:S(2)}) collective-permute-start(f32[64,128]{1,0:T(8,128)S(1)} %get-tuple-element.131), channel_id=1, source_target_pairs={{0,16},{4,20},{8,24},{12,28},{16,0},{20,4},{24,8},{28,12},{1,17},{... | collective-permute-start | bytes 98312 | tf_op jit(solution)/shard_map/ppermute | solution.py:283
  (13 other events, 63.8 us)

commit v9 on v8

--- a/solution.py
+++ b/solution.py
@@ -50,6 +50,7 @@
         pl.when(lax.rem(slot, chunk) == 0)(fetch(slot // chunk).wait)
         source = slots_ref[level, slot_count + slot]
         near = lax.rem(source, half) ^ lax.rem(row, half)
+        near = jnp.where(lax.rem(col, 2) == 1, mirrored(near, half), near)
         below = near * 2 + ((source // half) ^ side)
         above = slots_ref[level, slot] ^ col
         total[below * n_col + above] += slots[slot]
@@ -283,16 +284,35 @@
     return lax.ppermute(segment, axis, [(i, i ^ (size // 2)) for i in range(size)])
 
 
+def mirrored(number, size):
+    bits = size.bit_length() - 1
+    return sum(((number >> bit) & 1) << (bits - 1 - bit) for bit in range(bits))
+
+
+def near_exchange(messages):
+    n_row, n_col = lax.axis_size("row"), lax.axis_size("col")
+    half = n_row // 2
+    received = {0: messages[0]}
+    for d in reversed(range(1, half)):
+        pairs = []
+        for row in range(n_row):
+            for col in range(n_col):
+                partner = row ^ (mirrored(d, half) if col % 2 else d)
+                pairs.append((row * n_col + col, partner * n_col + col))
+        received[d] = lax.ppermute(messages[d], ("row", "col"), pairs)
+    return [received[d] for d in range(half)]
+
+
 def gather_row(segment, after):
     half = lax.axis_size("row") // 2
     received = far_exchange(segment, "row")
     (both,) = combine([[[(segment, None)], [(received, None)]]], after)
-    messages = exchange_each([both] * half, "row")
+    messages = near_exchange([both] * half)
     return [(message, side) for message in messages for side in range(2)]
 
 
 def deliver_row(messages):
-    received = exchange_each(messages, "row")
+    received = near_exchange(messages)
     mine, other = combine(
         [
             [[(message, side) for message in [received[0], *reversed(received[1:])]]]
@@ -342,7 +362,7 @@
         else:
             down.append(tidy(level - 1, True, near[:1]))
             after = down[-1][:1]
-        pieces = plain(exchange_each(near + far, "col"))
+        pieces = plain(reversed(exchange_each(near + far, "col")))
         forward.append(solve(right, inverse, level, pieces, False, after))
     backward = [None] * levels
     backward[-1] = solve(forward[-1], inverse, levels - 1, [], True)

time: 177 us -> 176 us (level)
    ppermute x60 -> x30, starting transfers between devices: 56.2 us -> 19.8 us  [exchange_each(): lax.ppermute(messages[d], axis, [(i, i ^ d) for i in range(size)])]
    ppermute x0 -> x30, starting transfers between devices: none -> 35.3 us  [near_exchange(): received[d] = lax.ppermute(messages[d], ('row', 'col'), pairs)]
    ppermute x60 -> x30, waiting for transfers between devices: 47.2 us -> 14.3 us  [exchange_each(): lax.ppermute(messages[d], axis, [(i, i ^ d) for i in range(size)])]
    ppermute x0 -> x30, waiting for transfers between devices: none -> 31.5 us  [near_exchange(): received[d] = lax.ppermute(messages[d], ('row', 'col'), pairs)]
    ppermute x10, waiting for transfers between devices: 35 us -> 37.2 us  [far_exchange(): lax.ppermute(segment, axis, [(i, i ^ size // 2) for i in range(size)])]
  transfers between devices with their start and end apart: 70 -> 70, of which waited for: 52 -> 53; matrix products, arithmetic and copies ran while one was open for 1% -> 1% of each run, Pallas kernels for 10% -> 10%
where the time goes in v9:
time: 176 us
  waiting for transfers between devices  83.1 us (47%)
  starting transfers between devices  63.1 us (36%)
  Pallas kernels  26 us (15%)
  local copies, waits for them, and re-layouts  2.48 us (1%)
    ppermute x10, waiting for transfers between devices, far_exchange(): lax.ppermute(segment, axis, [(i, i ^ size // 2) for i in range(size)])  37.2 us
    ppermute x30, starting transfers between devices, near_exchange(): received[d] = lax.ppermute(messages[d], ('row', 'col'), pairs)  35.3 us
    ppermute x30, waiting for transfers between devices, near_exchange(): received[d] = lax.ppermute(messages[d], ('row', 'col'), pairs)  31.5 us
    ppermute x30, starting transfers between devices, exchange_each(): lax.ppermute(messages[d], axis, [(i, i ^ d) for i in range(size)])  19.8 us
    ppermute x30, waiting for transfers between devices, exchange_each(): lax.ppermute(messages[d], axis, [(i, i ^ d) for i in range(size)])  14.3 us
    ppermute x10, starting transfers between devices, far_exchange(): lax.ppermute(segment, axis, [(i, i ^ size // 2) for i in range(size)])  8.01 us
    pallas_call x20, Pallas kernels, couple(): pl.pallas_call(functools.partial(couple_kernel, terms, span), out_shape=[...  7.88 us
    pallas_call x5, Pallas kernels, gather_blocks(): pl.pallas_call(functools.partial(gather_blocks_kernel, n_row, n_col, leve...  7.88 us
  transfers between devices with their start and end apart: 70, of which 53 were waited for; matrix products, arithmetic and copies ran while one was open for 1% of the time, Pallas kernels for 10%

profile of v9, /device:TPU:0, one launch (start us, length us, event | category | flops | bytes accessed | tf_op | source)
XLA Modules:
  0.0 175.8 jit_solution(7212652373139706925)
XLA Ops:
  0.6 1.7 first_solve.1.refs_0_
  2.3 4.1 %collective-permute-start = (f32[64,128]{1,0:T(8,128)}, f32[64,128]{1,0:T(8,128)S(1)}, u32[]{:S(2)}, u32[]{:S(2)}) collective-permute-start(f32[64,128]{1,0:T(8,128)} %first_solve.1.refs_0_), channel_id=1, source_target_pairs={{0,16},{4,20},{8,24},{12,28},{16,0},{20,4},{24,8},{28,12},{1,17},{... | collective-permute-start | bytes 98312 | tf_op jit(solution)/shard_map/ppermute | solution.py:284
  7.9 2.3 %gather_blocks_0.1.total_ref = f32[32,128,128]{2,1,0:T(8,128)S(1)} custom-call(s32[5,67]{1,0:T(8,128)S(1)} %concatenate.3.slots_ref, f32[5,32,128,128]{3,2,1,0:T(8,128)} %bitcast.14), custom_call_target="tpu_custom_call" | custom-call | flops 524288 | bytes 4194304 | tf_op jit(solution)/shard_map/gather_blocks_0/pallas_call | solution.py:67
  10.6 2.8 %collective-permute-start.3 = (f32[2,64,128]{2,1,0:T(8,128)S(1)}, f32[2,64,128]{2,1,0:T(8,128)S(1)}, u32[]{:S(2)}, u32[]{:S(2)}) collective-permute-start(f32[2,64,128]{2,1,0:T(8,128)S(1)} %combine.10.refs_0_), channel_id=1, source_target_pairs={{0,12},{1,13},{2,14},{3,15},{4,8},{5,9},{6,10},{7,11},{8,4},{9,5},... | collective-permute-start | bytes 196616 | tf_op jit(solution)/shard_map/ppermute | solution.py:302
  14.2 1.8 %collective-permute-done.3.refs_3_ = f32[2,64,128]{2,1,0:T(8,128)S(1)} collective-permute-done((f32[2,64,128]{2,1,0:T(8,128)S(1)}, f32[2,64,128]{2,1,0:T(8,128)S(1)}, u32[]{:S(2)}, u32[]{:S(2)}) %collective-permute-start.3) | collective-permute-done | bytes 65568 | tf_op jit(solution)/shard_map/ppermute | solution.py:302
  16.0 1.7 collective-permute-done.2.refs_2_
  18.4 1.5 collective-permute-start.5
  20.7 1.2 gather_blocks_1.1.refs_6_.total_ref
  22.6 0.9 collective-permute-start.7
  24.6 2.9 %collective-permute-done.7.refs_1_ = f32[64,128]{1,0:T(8,128)S(1)} collective-permute-done((f32[64,128]{1,0:T(8,128)S(1)}, f32[64,128]{1,0:T(8,128)S(1)}, u32[]{:S(2)}, u32[]{:S(2)}) %collective-permute-start.7) | collective-permute-done | bytes 32800 | tf_op jit(solution)/shard_map/ppermute | solution.py:284
  27.4 1.8 %collective-permute-start.10 = (f32[2,64,128]{2,1,0:T(8,128)S(1)}, f32[2,64,128]{2,1,0:T(8,128)S(1)}, u32[]{:S(2)}, u32[]{:S(2)}) collective-permute-start(f32[2,64,128]{2,1,0:T(8,128)S(1)} %combine.11.refs_0_), channel_id=1, source_target_pairs={{0,12},{1,13},{2,14},{3,15},{4,8},{5,9},{6,10},{7,11},{8,4},{9,5},... | collective-permute-start | bytes 196616 | tf_op jit(solution)/shard_map/ppermute | solution.py:302
  29.8 1.2 collective-permute-start.8
  30.9 1.8 %collective-permute-done.10.refs_3_ = f32[2,64,128]{2,1,0:T(8,128)S(1)} collective-permute-done((f32[2,64,128]{2,1,0:T(8,128)S(1)}, f32[2,64,128]{2,1,0:T(8,128)S(1)}, u32[]{:S(2)}, u32[]{:S(2)}) %collective-permute-start.10) | collective-permute-done | bytes 65568 | tf_op jit(solution)/shard_map/ppermute | solution.py:302
  34.5 1.4 collective-permute-start.12
  36.8 1.3 gather_blocks_2.1.refs_6_.total_ref
  38.6 1.0 collective-permute-start.14
  40.7 2.8 %collective-permute-done.14.refs_1_ = f32[64,128]{1,0:T(8,128)S(1)} collective-permute-done((f32[64,128]{1,0:T(8,128)S(1)}, f32[64,128]{1,0:T(8,128)S(1)}, u32[]{:S(2)}, u32[]{:S(2)}) %collective-permute-start.14) | collective-permute-done | bytes 32800 | tf_op jit(solution)/shard_map/ppermute | solution.py:284
  43.5 2.4 %collective-permute-start.17 = (f32[2,64,128]{2,1,0:T(8,128)S(1)}, f32[2,64,128]{2,1,0:T(8,128)S(1)}, u32[]{:S(2)}, u32[]{:S(2)}) collective-permute-start(f32[2,64,128]{2,1,0:T(8,128)S(1)} %combine.12.refs_0_), channel_id=1, source_target_pairs={{0,12},{1,13},{2,14},{3,15},{4,8},{5,9},{6,10},{7,11},{8,4},{9,5},... | collective-permute-start | bytes 196616 | tf_op jit(solution)/shard_map/ppermute | solution.py:302
  47.0 1.8 %collective-permute-done.17.refs_3_ = f32[2,64,128]{2,1,0:T(8,128)S(1)} collective-permute-done((f32[2,64,128]{2,1,0:T(8,128)S(1)}, f32[2,64,128]{2,1,0:T(8,128)S(1)}, u32[]{:S(2)}, u32[]{:S(2)}) %collective-permute-start.17) | collective-permute-done | bytes 65568 | tf_op jit(solution)/shard_map/ppermute | solution.py:302
  48.8 1.4 collective-permute-done.16.refs_2_
  51.0 2.1 %collective-permute-start.19 = (f32[64,128]{1,0:T(8,128)S(1)}, f32[64,128]{1,0:T(8,128)S(1)}, u32[]{:S(2)}, u32[]{:S(2)}) collective-permute-start(f32[64,128]{1,0:T(8,128)S(1)} %get-tuple-element.84), channel_id=1, source_target_pairs={{0,2},{1,3},{2,0},{3,1},{4,6},{5,7},{6,4},{7,5},{8,10},{9,11},{10,... | collective-permute-start | bytes 98312 | tf_op jit(solution)/shard_map/ppermute | solution.py:329
  53.6 1.9 %gather_blocks_3.1.refs_6_.total_ref = f32[32,128,128]{2,1,0:T(8,128)S(1)} custom-call(s32[5,67]{1,0:T(8,128)S(1)} %concatenate.3.slots_ref, f32[5,32,128,128]{3,2,1,0:T(8,128)S(1)} %bitcast.19, f32[64,128]{1,0:T(8,128)S(1)} %get-tuple-element.86.refs_0_.refs_5_), custom_call_target="tpu_custom_call" | custom-call | flops 524288 | bytes 4194304 | tf_op jit(solution)/shard_map/gather_blocks_3/pallas_call | solution.py:67
  57.2 4.0 %collective-permute-done.21.refs_1_ = f32[64,128]{1,0:T(8,128)S(1)} collective-permute-done((f32[64,128]{1,0:T(8,128)S(1)}, f32[64,128]{1,0:T(8,128)S(1)}, u32[]{:S(2)}, u32[]{:S(2)}) %collective-permute-start.21) | collective-permute-done | bytes 32800 | tf_op jit(solution)/shard_map/ppermute | solution.py:284
  62.5 2.3 %collective-permute-start.22 = (f32[2,64,128]{2,1,0:T(8,128)S(1)}, f32[2,64,128]{2,1,0:T(8,128)S(1)}, u32[]{:S(2)}, u32[]{:S(2)}) collective-permute-start(f32[2,64,128]{2,1,0:T(8,128)S(1)} %combine.13.refs_0_), channel_id=1, source_target_pairs={{0,4},{1,9},{2,6},{3,11},{4,0},{5,13},{6,2},{7,15},{8,12},{9,1},{1... | collective-permute-start | bytes 196616 | tf_op jit(solution)/shard_map/ppermute | solution.py:302
  64.8 1.8 %collective-permute-done.24.refs_3_ = f32[2,64,128]{2,1,0:T(8,128)S(1)} collective-permute-done((f32[2,64,128]{2,1,0:T(8,128)S(1)}, f32[2,64,128]{2,1,0:T(8,128)S(1)}, u32[]{:S(2)}, u32[]{:S(2)}) %collective-permute-start.24) | collective-permute-done | bytes 65568 | tf_op jit(solution)/shard_map/ppermute | solution.py:302
  67.7 1.5 collective-permute-start.26
  70.0 1.3 gather_blocks_4.1.refs_6_.total_ref
  73.4 4.1 %collective-permute-done.28.refs_1_ = f32[64,128]{1,0:T(8,128)S(1)} collective-permute-done((f32[64,128]{1,0:T(8,128)S(1)}, f32[64,128]{1,0:T(8,128)S(1)}, u32[]{:S(2)}, u32[]{:S(2)}) %collective-permute-start.28) | collective-permute-done | bytes 32800 | tf_op jit(solution)/shard_map/ppermute | solution.py:284
  77.4 1.1 collective-permute-start.31
  78.5 1.9 %collective-permute-start.30 = (f32[2,64,128]{2,1,0:T(8,128)S(1)}, f32[2,64,128]{2,1,0:T(8,128)S(1)}, u32[]{:S(2)}, u32[]{:S(2)}) collective-permute-start(f32[2,64,128]{2,1,0:T(8,128)S(1)} %combine.14.refs_0_), channel_id=1, source_target_pairs={{0,8},{1,5},{2,10},{3,7},{4,12},{5,1},{6,14},{7,3},{8,0},{9,13},{1... | collective-permute-start | bytes 196616 | tf_op jit(solution)/shard_map/ppermute | solution.py:302
  80.9 2.2 %collective-permute-done.31.refs_3_ = f32[2,64,128]{2,1,0:T(8,128)S(1)} collective-permute-done((f32[2,64,128]{2,1,0:T(8,128)S(1)}, f32[2,64,128]{2,1,0:T(8,128)S(1)}, u32[]{:S(2)}, u32[]{:S(2)}) %collective-permute-start.31) | collective-permute-done | bytes 65568 | tf_op jit(solution)/shard_map/ppermute | solution.py:302
  83.7 1.0 collective-permute-done.29.refs_1_
  86.5 1.0 collective-permute-start.34
  90.3 1.3 collective-permute-start.36
  91.7 1.6 collective-permute-done.37.refs_3_
  95.4 1.3 collective-permute-start.39
  96.7 1.7 collective-permute-start.40
  98.6 1.8 %collective-permute-done.38.refs_1_ = f32[2,64,128]{2,1,0:T(8,128)S(1)} collective-permute-done((f32[2,64,128]{2,1,0:T(8,128)S(1)}, f32[2,64,128]{2,1,0:T(8,128)S(1)}, u32[]{:S(2)}, u32[]{:S(2)}) %collective-permute-start.38) | collective-permute-done | bytes 65568 | tf_op jit(solution)/shard_map/ppermute | solution.py:302
  102.2 4.1 %collective-permute-done.41.refs_3_ = f32[64,128]{1,0:T(8,128)S(1)} collective-permute-done((f32[64,128]{1,0:T(8,128)S(1)}, f32[64,128]{1,0:T(8,128)S(1)}, u32[]{:S(2)}, u32[]{:S(2)}) %collective-permute-start.41) | collective-permute-done | bytes 32800 | tf_op jit(solution)/shard_map/ppermute | solution.py:284
  108.2 1.2 collective-permute-start.42
  109.4 1.5 collective-permute-done.44.refs_3_
  112.1 1.5 collective-permute-start.45
  113.6 1.8 %collective-permute-start.46 = (f32[2,64,128]{2,1,0:T(8,128)S(1)}, f32[2,64,128]{2,1,0:T(8,128)S(1)}, u32[]{:S(2)}, u32[]{:S(2)}) collective-permute-start(f32[2,64,128]{2,1,0:T(8,128)S(1)} %get-tuple-element.113), channel_id=1, source_target_pairs={{0,8},{1,5},{2,10},{3,7},{4,12},{5,1},{6,14},{7,3},{8,0},{9,13},{1... | collective-permute-start | bytes 196616 | tf_op jit(solution)/shard_map/ppermute | solution.py:302
  115.9 1.5 collective-permute-done.45.refs_1_
  117.5 1.4 collective-permute-done.46.refs_2_
  119.8 4.9 %collective-permute-done.48.refs_3_ = f32[64,128]{1,0:T(8,128)S(1)} collective-permute-done((f32[64,128]{1,0:T(8,128)S(1)}, f32[64,128]{1,0:T(8,128)S(1)}, u32[]{:S(2)}, u32[]{:S(2)}) %collective-permute-start.48) | collective-permute-done | bytes 32800 | tf_op jit(solution)/shard_map/ppermute | solution.py:284
  124.9 0.9 collective-permute-start.50
  126.7 1.5 collective-permute-done.51.refs_3_
  128.2 0.9 collective-permute-done.50.refs_2_
  129.9 2.0 %collective-permute-start.53 = (f32[2,64,128]{2,1,0:T(8,128)S(1)}, f32[2,64,128]{2,1,0:T(8,128)S(1)}, u32[]{:S(2)}, u32[]{:S(2)}) collective-permute-start(f32[2,64,128]{2,1,0:T(8,128)S(1)} %get-tuple-element.118), channel_id=1, source_target_pairs={{0,8},{1,5},{2,10},{3,7},{4,12},{5,1},{6,14},{7,3},{8,0},{9,13},{1... | collective-permute-start | bytes 196616 | tf_op jit(solution)/shard_map/ppermute | solution.py:302
  131.9 1.3 collective-permute-start.54
  133.5 1.9 %collective-permute-done.52.refs_1_ = f32[2,64,128]{2,1,0:T(8,128)S(1)} collective-permute-done((f32[2,64,128]{2,1,0:T(8,128)S(1)}, f32[2,64,128]{2,1,0:T(8,128)S(1)}, u32[]{:S(2)}, u32[]{:S(2)}) %collective-permute-start.52) | collective-permute-done | bytes 65568 | tf_op jit(solution)/shard_map/ppermute | solution.py:302
  136.5 4.9 %collective-permute-done.55.refs_3_ = f32[64,128]{1,0:T(8,128)S(1)} collective-permute-done((f32[64,128]{1,0:T(8,128)S(1)}, f32[64,128]{1,0:T(8,128)S(1)}, u32[]{:S(2)}, u32[]{:S(2)}) %collective-permute-start.55) | collective-permute-done | bytes 32800 | tf_op jit(solution)/shard_map/ppermute | solution.py:284
  142.5 0.9 collective-permute-start.56
  143.5 1.5 collective-permute-done.58.refs_3_
  147.0 1.9 %collective-permute-start.60 = (f32[2,64,128]{2,1,0:T(8,128)S(1)}, f32[2,64,128]{2,1,0:T(8,128)S(1)}, u32[]{:S(2)}, u32[]{:S(2)}) collective-permute-start(f32[2,64,128]{2,1,0:T(8,128)S(1)} %get-tuple-element.123), channel_id=1, source_target_pairs={{0,8},{1,5},{2,10},{3,7},{4,12},{5,1},{6,14},{7,3},{8,0},{9,13},{1... | collective-permute-start | bytes 196616 | tf_op jit(solution)/shard_map/ppermute | solution.py:302
  148.8 1.2 collective-permute-start.61
  150.2 1.9 %collective-permute-done.59.refs_1_ = f32[2,64,128]{2,1,0:T(8,128)S(1)} collective-permute-done((f32[2,64,128]{2,1,0:T(8,128)S(1)}, f32[2,64,128]{2,1,0:T(8,128)S(1)}, u32[]{:S(2)}, u32[]{:S(2)}) %collective-permute-start.59) | collective-permute-done | bytes 65568 | tf_op jit(solution)/shard_map/ppermute | solution.py:302
  153.4 4.7 %collective-permute-done.62.refs_3_ = f32[64,128]{1,0:T(8,128)S(1)} collective-permute-done((f32[64,128]{1,0:T(8,128)S(1)}, f32[64,128]{1,0:T(8,128)S(1)}, u32[]{:S(2)}, u32[]{:S(2)}) %collective-permute-start.62) | collective-permute-done | bytes 32800 | tf_op jit(solution)/shard_map/ppermute | solution.py:284
  159.2 1.0 collective-permute-start.63
  160.2 1.5 collective-permute-done.65.refs_3_
  163.9 1.8 %collective-permute-start.67 = (f32[2,64,128]{2,1,0:T(8,128)S(1)}, f32[2,64,128]{2,1,0:T(8,128)S(1)}, u32[]{:S(2)}, u32[]{:S(2)}) collective-permute-start(f32[2,64,128]{2,1,0:T(8,128)S(1)} %get-tuple-element.128), channel_id=1, source_target_pairs={{0,8},{1,5},{2,10},{3,7},{4,12},{5,1},{6,14},{7,3},{8,0},{9,13},{1... | collective-permute-start | bytes 196616 | tf_op jit(solution)/shard_map/ppermute | solution.py:302
  166.9 2.0 %collective-permute-done.66.refs_1_ = f32[2,64,128]{2,1,0:T(8,128)S(1)} collective-permute-done((f32[2,64,128]{2,1,0:T(8,128)S(1)}, f32[2,64,128]{2,1,0:T(8,128)S(1)}, u32[]{:S(2)}, u32[]{:S(2)}) %collective-permute-start.66) | collective-permute-done | bytes 65568 | tf_op jit(solution)/shard_map/ppermute | solution.py:302
  170.1 4.8 %collective-permute-done.69.refs_3_ = f32[64,128]{1,0:T(8,128)S(1)} collective-permute-done((f32[64,128]{1,0:T(8,128)S(1)}, f32[64,128]{1,0:T(8,128)S(1)}, u32[]{:S(2)}, u32[]{:S(2)}) %collective-permute-start.69) | collective-permute-done | bytes 32800 | tf_op jit(solution)/shard_map/ppermute | solution.py:284
  (155 shorter events, 48.6 us)
Async XLA Ops:
  2.3 8.3 %collective-permute-start = (f32[64,128]{1,0:T(8,128)}, f32[64,128]{1,0:T(8,128)S(1)}, u32[]{:S(2)}, u32[]{:S(2)}) collective-permute-start(f32[64,128]{1,0:T(8,128)} %first_solve.1.refs_0_), channel_id=1, source_target_pairs={{0,16},{4,20},{8,24},{12,28},{16,0},{20,4},{24,8},{28,12},{1,17},{... | collective-permute-start | bytes 98312 | tf_op jit(solution)/shard_map/ppermute | solution.py:284
  10.6 5.3 %collective-permute-start.3 = (f32[2,64,128]{2,1,0:T(8,128)S(1)}, f32[2,64,128]{2,1,0:T(8,128)S(1)}, u32[]{:S(2)}, u32[]{:S(2)}) collective-permute-start(f32[2,64,128]{2,1,0:T(8,128)S(1)} %combine.10.refs_0_), channel_id=1, source_target_pairs={{0,12},{1,13},{2,14},{3,15},{4,8},{5,9},{6,10},{7,11},{8,4},{9,5},... | collective-permute-start | bytes 196616 | tf_op jit(solution)/shard_map/ppermute | solution.py:302
  13.4 4.3 %collective-permute-start.2 = (f32[2,64,128]{2,1,0:T(8,128)S(1)}, f32[2,64,128]{2,1,0:T(8,128)S(1)}, u32[]{:S(2)}, u32[]{:S(2)}) collective-permute-start(f32[2,64,128]{2,1,0:T(8,128)S(1)} %combine.10.refs_0_), channel_id=1, source_target_pairs={{0,8},{1,5},{2,10},{3,7},{4,12},{5,1},{6,14},{7,3},{8,0},{9,13},{1... | collective-permute-start | bytes 196616 | tf_op jit(solution)/shard_map/ppermute | solution.py:302
  13.6 4.3 %collective-permute-start.1 = (f32[2,64,128]{2,1,0:T(8,128)S(1)}, f32[2,64,128]{2,1,0:T(8,128)S(1)}, u32[]{:S(2)}, u32[]{:S(2)}) collective-permute-start(f32[2,64,128]{2,1,0:T(8,128)S(1)} %combine.10.refs_0_), channel_id=1, source_target_pairs={{0,4},{1,9},{2,6},{3,11},{4,0},{5,13},{6,2},{7,15},{8,12},{9,1},{1... | collective-permute-start | bytes 196616 | tf_op jit(solution)/shard_map/ppermute | solution.py:302
  18.3 3.7 %collective-permute-start.4 = (f32[64,128]{1,0:T(8,128)S(1)}, f32[64,128]{1,0:T(8,128)S(1)}, u32[]{:S(2)}, u32[]{:S(2)}) collective-permute-start(f32[64,128]{1,0:T(8,128)S(1)} %get-tuple-element.69), channel_id=1, source_target_pairs={{0,3},{1,2},{2,1},{3,0},{4,7},{5,6},{6,5},{7,4},{8,11},{9,10},{10,... | collective-permute-start | bytes 98312 | tf_op jit(solution)/shard_map/ppermute | solution.py:329
  18.4 4.0 %collective-permute-start.5 = (f32[64,128]{1,0:T(8,128)S(1)}, f32[64,128]{1,0:T(8,128)S(1)}, u32[]{:S(2)}, u32[]{:S(2)}) collective-permute-start(f32[64,128]{1,0:T(8,128)S(1)} %get-tuple-element.70), channel_id=1, source_target_pairs={{0,2},{1,3},{2,0},{3,1},{4,6},{5,7},{6,4},{7,5},{8,10},{9,11},{10,... | collective-permute-start | bytes 98312 | tf_op jit(solution)/shard_map/ppermute | solution.py:329
  22.6 4.9 %collective-permute-start.7 = (f32[64,128]{1,0:T(8,128)S(1)}, f32[64,128]{1,0:T(8,128)S(1)}, u32[]{:S(2)}, u32[]{:S(2)}) collective-permute-start(f32[64,128]{1,0:T(8,128)S(1)} %solve_up.5.refs_0_.refs_1_), channel_id=1, source_target_pairs={{0,16},{4,20},{8,24},{12,28},{16,0},{20,4},{24,8},{28,12},{1,17},{... | collective-permute-start | bytes 98312 | tf_op jit(solution)/shard_map/ppermute | solution.py:284
  27.4 5.3 %collective-permute-start.10 = (f32[2,64,128]{2,1,0:T(8,128)S(1)}, f32[2,64,128]{2,1,0:T(8,128)S(1)}, u32[]{:S(2)}, u32[]{:S(2)}) collective-permute-start(f32[2,64,128]{2,1,0:T(8,128)S(1)} %combine.11.refs_0_), channel_id=1, source_target_pairs={{0,12},{1,13},{2,14},{3,15},{4,8},{5,9},{6,10},{7,11},{8,4},{9,5},... | collective-permute-start | bytes 196616 | tf_op jit(solution)/shard_map/ppermute | solution.py:302
  29.2 4.3 %collective-permute-start.9 = (f32[2,64,128]{2,1,0:T(8,128)S(1)}, f32[2,64,128]{2,1,0:T(8,128)S(1)}, u32[]{:S(2)}, u32[]{:S(2)}) collective-permute-start(f32[2,64,128]{2,1,0:T(8,128)S(1)} %combine.11.refs_0_), channel_id=1, source_target_pairs={{0,8},{1,5},{2,10},{3,7},{4,12},{5,1},{6,14},{7,3},{8,0},{9,13},{1... | collective-permute-start | bytes 196616 | tf_op jit(solution)/shard_map/ppermute | solution.py:302
  29.8 4.3 %collective-permute-start.8 = (f32[2,64,128]{2,1,0:T(8,128)S(1)}, f32[2,64,128]{2,1,0:T(8,128)S(1)}, u32[]{:S(2)}, u32[]{:S(2)}) collective-permute-start(f32[2,64,128]{2,1,0:T(8,128)S(1)} %combine.11.refs_0_), channel_id=1, source_target_pairs={{0,4},{1,9},{2,6},{3,11},{4,0},{5,13},{6,2},{7,15},{8,12},{9,1},{1... | collective-permute-start | bytes 196616 | tf_op jit(solution)/shard_map/ppermute | solution.py:302
  34.4 3.7 %collective-permute-start.11 = (f32[64,128]{1,0:T(8,128)S(1)}, f32[64,128]{1,0:T(8,128)S(1)}, u32[]{:S(2)}, u32[]{:S(2)}) collective-permute-start(f32[64,128]{1,0:T(8,128)S(1)} %get-tuple-element.76), channel_id=1, source_target_pairs={{0,3},{1,2},{2,1},{3,0},{4,7},{5,6},{6,5},{7,4},{8,11},{9,10},{10,... | collective-permute-start | bytes 98312 | tf_op jit(solution)/shard_map/ppermute | solution.py:329
  34.5 4.0 %collective-permute-start.12 = (f32[64,128]{1,0:T(8,128)S(1)}, f32[64,128]{1,0:T(8,128)S(1)}, u32[]{:S(2)}, u32[]{:S(2)}) collective-permute-start(f32[64,128]{1,0:T(8,128)S(1)} %get-tuple-element.77), channel_id=1, source_target_pairs={{0,2},{1,3},{2,0},{3,1},{4,6},{5,7},{6,4},{7,5},{8,10},{9,11},{10,... | collective-permute-start | bytes 98312 | tf_op jit(solution)/shard_map/ppermute | solution.py:329
  38.6 4.9 %collective-permute-start.14 = (f32[64,128]{1,0:T(8,128)S(1)}, f32[64,128]{1,0:T(8,128)S(1)}, u32[]{:S(2)}, u32[]{:S(2)}) collective-permute-start(f32[64,128]{1,0:T(8,128)S(1)} %solve_up.6.refs_0_.refs_2_), channel_id=1, source_target_pairs={{0,16},{4,20},{8,24},{12,28},{16,0},{20,4},{24,8},{28,12},{1,17},{... | collective-permute-start | bytes 98312 | tf_op jit(solution)/shard_map/ppermute | solution.py:284
  43.5 5.3 %collective-permute-start.17 = (f32[2,64,128]{2,1,0:T(8,128)S(1)}, f32[2,64,128]{2,1,0:T(8,128)S(1)}, u32[]{:S(2)}, u32[]{:S(2)}) collective-permute-start(f32[2,64,128]{2,1,0:T(8,128)S(1)} %combine.12.refs_0_), channel_id=1, source_target_pairs={{0,12},{1,13},{2,14},{3,15},{4,8},{5,9},{6,10},{7,11},{8,4},{9,5},... | collective-permute-start | bytes 196616 | tf_op jit(solution)/shard_map/ppermute | solution.py:302
  46.0 4.3 %collective-permute-start.16 = (f32[2,64,128]{2,1,0:T(8,128)S(1)}, f32[2,64,128]{2,1,0:T(8,128)S(1)}, u32[]{:S(2)}, u32[]{:S(2)}) collective-permute-start(f32[2,64,128]{2,1,0:T(8,128)S(1)} %combine.12.refs_0_), channel_id=1, source_target_pairs={{0,8},{1,5},{2,10},{3,7},{4,12},{5,1},{6,14},{7,3},{8,0},{9,13},{1... | collective-permute-start | bytes 196616 | tf_op jit(solution)/shard_map/ppermute | solution.py:302
  46.2 4.3 %collective-permute-start.15 = (f32[2,64,128]{2,1,0:T(8,128)S(1)}, f32[2,64,128]{2,1,0:T(8,128)S(1)}, u32[]{:S(2)}, u32[]{:S(2)}) collective-permute-start(f32[2,64,128]{2,1,0:T(8,128)S(1)} %combine.12.refs_0_), channel_id=1, source_target_pairs={{0,4},{1,9},{2,6},{3,11},{4,0},{5,13},{6,2},{7,15},{8,12},{9,1},{1... | collective-permute-start | bytes 196616 | tf_op jit(solution)/shard_map/ppermute | solution.py:302
  50.9 4.6 %collective-permute-start.18 = (f32[64,128]{1,0:T(8,128)S(1)}, f32[64,128]{1,0:T(8,128)S(1)}, u32[]{:S(2)}, u32[]{:S(2)}) collective-permute-start(f32[64,128]{1,0:T(8,128)S(1)} %get-tuple-element.83), channel_id=1, source_target_pairs={{0,3},{1,2},{2,1},{3,0},{4,7},{5,6},{6,5},{7,4},{8,11},{9,10},{10,... | collective-permute-start | bytes 98312 | tf_op jit(solution)/shard_map/ppermute | solution.py:329
  51.0 4.5 %collective-permute-start.19 = (f32[64,128]{1,0:T(8,128)S(1)}, f32[64,128]{1,0:T(8,128)S(1)}, u32[]{:S(2)}, u32[]{:S(2)}) collective-permute-start(f32[64,128]{1,0:T(8,128)S(1)} %get-tuple-element.84), channel_id=1, source_target_pairs={{0,2},{1,3},{2,0},{3,1},{4,6},{5,7},{6,4},{7,5},{8,10},{9,11},{10,... | collective-permute-start | bytes 98312 | tf_op jit(solution)/shard_map/ppermute | solution.py:329
  55.7 5.6 %collective-permute-start.21 = (f32[64,128]{1,0:T(8,128)S(1)}, f32[64,128]{1,0:T(8,128)S(1)}, u32[]{:S(2)}, u32[]{:S(2)}) collective-permute-start(f32[64,128]{1,0:T(8,128)S(1)} %solve_up.7.refs_0_.refs_3_), channel_id=1, source_target_pairs={{0,16},{4,20},{8,24},{12,28},{16,0},{20,4},{24,8},{28,12},{1,17},{... | collective-permute-start | bytes 98312 | tf_op jit(solution)/shard_map/ppermute | solution.py:284
  61.3 5.3 %collective-permute-start.24 = (f32[2,64,128]{2,1,0:T(8,128)S(1)}, f32[2,64,128]{2,1,0:T(8,128)S(1)}, u32[]{:S(2)}, u32[]{:S(2)}) collective-permute-start(f32[2,64,128]{2,1,0:T(8,128)S(1)} %combine.13.refs_0_), channel_id=1, source_target_pairs={{0,12},{1,13},{2,14},{3,15},{4,8},{5,9},{6,10},{7,11},{8,4},{9,5},... | collective-permute-start | bytes 196616 | tf_op jit(solution)/shard_map/ppermute | solution.py:302
  61.9 4.7 %collective-permute-start.23 = (f32[2,64,128]{2,1,0:T(8,128)S(1)}, f32[2,64,128]{2,1,0:T(8,128)S(1)}, u32[]{:S(2)}, u32[]{:S(2)}) collective-permute-start(f32[2,64,128]{2,1,0:T(8,128)S(1)} %combine.13.refs_0_), channel_id=1, source_target_pairs={{0,8},{1,5},{2,10},{3,7},{4,12},{5,1},{6,14},{7,3},{8,0},{9,13},{1... | collective-permute-start | bytes 196616 | tf_op jit(solution)/shard_map/ppermute | solution.py:302
  62.5 4.8 %collective-permute-start.22 = (f32[2,64,128]{2,1,0:T(8,128)S(1)}, f32[2,64,128]{2,1,0:T(8,128)S(1)}, u32[]{:S(2)}, u32[]{:S(2)}) collective-permute-start(f32[2,64,128]{2,1,0:T(8,128)S(1)} %combine.13.refs_0_), channel_id=1, source_target_pairs={{0,4},{1,9},{2,6},{3,11},{4,0},{5,13},{6,2},{7,15},{8,12},{9,1},{1... | collective-permute-start | bytes 196616 | tf_op jit(solution)/shard_map/ppermute | solution.py:302
  67.6 3.7 %collective-permute-start.25 = (f32[64,128]{1,0:T(8,128)S(1)}, f32[64,128]{1,0:T(8,128)S(1)}, u32[]{:S(2)}, u32[]{:S(2)}) collective-permute-start(f32[64,128]{1,0:T(8,128)S(1)} %get-tuple-element.90), channel_id=1, source_target_pairs={{0,3},{1,2},{2,1},{3,0},{4,7},{5,6},{6,5},{7,4},{8,11},{9,10},{10,... | collective-permute-start | bytes 98312 | tf_op jit(solution)/shard_map/ppermute | solution.py:329
  67.7 4.0 %collective-permute-start.26 = (f32[64,128]{1,0:T(8,128)S(1)}, f32[64,128]{1,0:T(8,128)S(1)}, u32[]{:S(2)}, u32[]{:S(2)}) collective-permute-start(f32[64,128]{1,0:T(8,128)S(1)} %get-tuple-element.91), channel_id=1, source_target_pairs={{0,2},{1,3},{2,0},{3,1},{4,6},{5,7},{6,4},{7,5},{8,10},{9,11},{10,... | collective-permute-start | bytes 98312 | tf_op jit(solution)/shard_map/ppermute | solution.py:329
  71.8 5.6 %collective-permute-start.28 = (f32[64,128]{1,0:T(8,128)S(1)}, f32[64,128]{1,0:T(8,128)S(1)}, u32[]{:S(2)}, u32[]{:S(2)}) collective-permute-start(f32[64,128]{1,0:T(8,128)S(1)} %solve_up.8.refs_0_.refs_4_), channel_id=1, source_target_pairs={{0,16},{4,20},{8,24},{12,28},{16,0},{20,4},{24,8},{28,12},{1,17},{... | collective-permute-start | bytes 98312 | tf_op jit(solution)/shard_map/ppermute | solution.py:284
  77.4 5.7 %collective-permute-start.31 = (f32[2,64,128]{2,1,0:T(8,128)S(1)}, f32[2,64,128]{2,1,0:T(8,128)S(1)}, u32[]{:S(2)}, u32[]{:S(2)}) collective-permute-start(f32[2,64,128]{2,1,0:T(8,128)S(1)} %combine.14.refs_0_), channel_id=1, source_target_pairs={{0,12},{1,13},{2,14},{3,15},{4,8},{5,9},{6,10},{7,11},{8,4},{9,5},... | collective-permute-start | bytes 196616 | tf_op jit(solution)/shard_map/ppermute | solution.py:302
  78.5 5.2 %collective-permute-start.30 = (f32[2,64,128]{2,1,0:T(8,128)S(1)}, f32[2,64,128]{2,1,0:T(8,128)S(1)}, u32[]{:S(2)}, u32[]{:S(2)}) collective-permute-start(f32[2,64,128]{2,1,0:T(8,128)S(1)} %combine.14.refs_0_), channel_id=1, source_target_pairs={{0,8},{1,5},{2,10},{3,7},{4,12},{5,1},{6,14},{7,3},{8,0},{9,13},{1... | collective-permute-start | bytes 196616 | tf_op jit(solution)/shard_map/ppermute | solution.py:302
  80.5 4.3 %collective-permute-start.29 = (f32[2,64,128]{2,1,0:T(8,128)S(1)}, f32[2,64,128]{2,1,0:T(8,128)S(1)}, u32[]{:S(2)}, u32[]{:S(2)}) collective-permute-start(f32[2,64,128]{2,1,0:T(8,128)S(1)} %combine.14.refs_0_), channel_id=1, source_target_pairs={{0,4},{1,9},{2,6},{3,11},{4,0},{5,13},{6,2},{7,15},{8,12},{9,1},{1... | collective-permute-start | bytes 196616 | tf_op jit(solution)/shard_map/ppermute | solution.py:302
  85.1 3.4 %collective-permute-start.32 = (f32[64,128]{1,0:T(8,128)S(1)}, f32[64,128]{1,0:T(8,128)S(1)}, u32[]{:S(2)}, u32[]{:S(2)}) collective-permute-start(f32[64,128]{1,0:T(8,128)S(1)} %get-tuple-element.97), channel_id=1, source_target_pairs={{0,3},{1,2},{2,1},{3,0},{4,7},{5,6},{6,5},{7,4},{8,11},{9,10},{10,... | collective-permute-start | bytes 98312 | tf_op jit(solution)/shard_map/ppermute | solution.py:329
  85.2 4.2 %collective-permute-start.33 = (f32[64,128]{1,0:T(8,128)S(1)}, f32[64,128]{1,0:T(8,128)S(1)}, u32[]{:S(2)}, u32[]{:S(2)}) collective-permute-start(f32[64,128]{1,0:T(8,128)S(1)} %get-tuple-element.98), channel_id=1, source_target_pairs={{0,2},{1,3},{2,0},{3,1},{4,6},{5,7},{6,4},{7,5},{8,10},{9,11},{10,... | collective-permute-start | bytes 98312 | tf_op jit(solution)/shard_map/ppermute | solution.py:329
  89.8 3.5 %collective-permute-start.37 = (f32[64,128]{1,0:T(8,128)S(1)}, f32[64,128]{1,0:T(8,128)S(1)}, u32[]{:S(2)}, u32[]{:S(2)}) collective-permute-start(f32[64,128]{1,0:T(8,128)S(1)} %solve_down.6.refs_0_.refs_5_), channel_id=1, source_target_pairs={{0,3},{1,2},{2,1},{3,0},{4,7},{5,6},{6,5},{7,4},{8,11},{9,10},{10,... | collective-permute-start | bytes 98312 | tf_op jit(solution)/shard_map/ppermute | solution.py:329
  90.3 4.0 %collective-permute-start.36 = (f32[64,128]{1,0:T(8,128)S(1)}, f32[64,128]{1,0:T(8,128)S(1)}, u32[]{:S(2)}, u32[]{:S(2)}) collective-permute-start(f32[64,128]{1,0:T(8,128)S(1)} %solve_down.6.refs_0_.refs_5_), channel_id=1, source_target_pairs={{0,2},{1,3},{2,0},{3,1},{4,6},{5,7},{6,4},{7,5},{8,10},{9,11},{10,... | collective-permute-start | bytes 98312 | tf_op jit(solution)/shard_map/ppermute | solution.py:329
  94.8 5.6 %collective-permute-start.38 = (f32[2,64,128]{2,1,0:T(8,128)S(1)}, f32[2,64,128]{2,1,0:T(8,128)S(1)}, u32[]{:S(2)}, u32[]{:S(2)}) collective-permute-start(f32[2,64,128]{2,1,0:T(8,128)S(1)} %get-tuple-element.107), channel_id=1, source_target_pairs={{0,12},{1,13},{2,14},{3,15},{4,8},{5,9},{6,10},{7,11},{8,4},{9,5},... | collective-permute-start | bytes 196616 | tf_op jit(solution)/shard_map/ppermute | solution.py:302
  95.4 5.0 %collective-permute-start.39 = (f32[2,64,128]{2,1,0:T(8,128)S(1)}, f32[2,64,128]{2,1,0:T(8,128)S(1)}, u32[]{:S(2)}, u32[]{:S(2)}) collective-permute-start(f32[2,64,128]{2,1,0:T(8,128)S(1)} %get-tuple-element.108), channel_id=1, source_target_pairs={{0,8},{1,5},{2,10},{3,7},{4,12},{5,1},{6,14},{7,3},{8,0},{9,13},{1... | collective-permute-start | bytes 196616 | tf_op jit(solution)/shard_map/ppermute | solution.py:302
  96.7 4.4 %collective-permute-start.40 = (f32[2,64,128]{2,1,0:T(8,128)S(1)}, f32[2,64,128]{2,1,0:T(8,128)S(1)}, u32[]{:S(2)}, u32[]{:S(2)}) collective-permute-start(f32[2,64,128]{2,1,0:T(8,128)S(1)} %get-tuple-element.109), channel_id=1, source_target_pairs={{0,4},{1,9},{2,6},{3,11},{4,0},{5,13},{6,2},{7,15},{8,12},{9,1},{1... | collective-permute-start | bytes 196616 | tf_op jit(solution)/shard_map/ppermute | solution.py:302
  101.1 5.2 %collective-permute-start.41 = (f32[64,128]{1,0:T(8,128)S(1)}, f32[64,128]{1,0:T(8,128)S(1)}, u32[]{:S(2)}, u32[]{:S(2)}) collective-permute-start(f32[64,128]{1,0:T(8,128)S(1)} %get-tuple-element.111), channel_id=1, source_target_pairs={{0,16},{4,20},{8,24},{12,28},{16,0},{20,4},{24,8},{28,12},{1,17},{... | collective-permute-start | bytes 98312 | tf_op jit(solution)/shard_map/ppermute | solution.py:284
  107.5 3.4 %collective-permute-start.44 = (f32[64,128]{1,0:T(8,128)S(1)}, f32[64,128]{1,0:T(8,128)S(1)}, u32[]{:S(2)}, u32[]{:S(2)}) collective-permute-start(f32[64,128]{1,0:T(8,128)S(1)} %solve_down.7.refs_0_.refs_4_), channel_id=1, source_target_pairs={{0,3},{1,2},{2,1},{3,0},{4,7},{5,6},{6,5},{7,4},{8,11},{9,10},{10,... | collective-permute-start | bytes 98312 | tf_op jit(solution)/shard_map/ppermute | solution.py:329
  107.5 4.0 %collective-permute-start.43 = (f32[64,128]{1,0:T(8,128)S(1)}, f32[64,128]{1,0:T(8,128)S(1)}, u32[]{:S(2)}, u32[]{:S(2)}) collective-permute-start(f32[64,128]{1,0:T(8,128)S(1)} %solve_down.7.refs_0_.refs_4_), channel_id=1, source_target_pairs={{0,2},{1,3},{2,0},{3,1},{4,6},{5,7},{6,4},{7,5},{8,10},{9,11},{10,... | collective-permute-start | bytes 98312 | tf_op jit(solution)/shard_map/ppermute | solution.py:329
  108.2 3.4 %collective-permute-start.42 = (f32[64,128]{1,0:T(8,128)S(1)}, f32[64,128]{1,0:T(8,128)S(1)}, u32[]{:S(2)}, u32[]{:S(2)}) collective-permute-start(f32[64,128]{1,0:T(8,128)S(1)} %solve_down.7.refs_0_.refs_4_), channel_id=1, source_target_pairs={{0,1},{1,0},{2,3},{3,2},{4,5},{5,4},{6,7},{7,6},{8,9},{9,8},{10,11... | collective-permute-start | bytes 98312 | tf_op jit(solution)/shard_map/ppermute | solution.py:329
  112.1 5.3 %collective-permute-start.45 = (f32[2,64,128]{2,1,0:T(8,128)S(1)}, f32[2,64,128]{2,1,0:T(8,128)S(1)}, u32[]{:S(2)}, u32[]{:S(2)}) collective-permute-start(f32[2,64,128]{2,1,0:T(8,128)S(1)} %get-tuple-element.112), channel_id=1, source_target_pairs={{0,12},{1,13},{2,14},{3,15},{4,8},{5,9},{6,10},{7,11},{8,4},{9,5},... | collective-permute-start | bytes 196616 | tf_op jit(solution)/shard_map/ppermute | solution.py:302
  113.6 5.2 %collective-permute-start.46 = (f32[2,64,128]{2,1,0:T(8,128)S(1)}, f32[2,64,128]{2,1,0:T(8,128)S(1)}, u32[]{:S(2)}, u32[]{:S(2)}) collective-permute-start(f32[2,64,128]{2,1,0:T(8,128)S(1)} %get-tuple-element.113), channel_id=1, source_target_pairs={{0,8},{1,5},{2,10},{3,7},{4,12},{5,1},{6,14},{7,3},{8,0},{9,13},{1... | collective-permute-start | bytes 196616 | tf_op jit(solution)/shard_map/ppermute | solution.py:302
  115.4 4.3 %collective-permute-start.47 = (f32[2,64,128]{2,1,0:T(8,128)S(1)}, f32[2,64,128]{2,1,0:T(8,128)S(1)}, u32[]{:S(2)}, u32[]{:S(2)}) collective-permute-start(f32[2,64,128]{2,1,0:T(8,128)S(1)} %get-tuple-element.114), channel_id=1, source_target_pairs={{0,4},{1,9},{2,6},{3,11},{4,0},{5,13},{6,2},{7,15},{8,12},{9,1},{1... | collective-permute-start | bytes 196616 | tf_op jit(solution)/shard_map/ppermute | solution.py:302
  119.7 4.9 %collective-permute-start.48 = (f32[64,128]{1,0:T(8,128)S(1)}, f32[64,128]{1,0:T(8,128)S(1)}, u32[]{:S(2)}, u32[]{:S(2)}) collective-permute-start(f32[64,128]{1,0:T(8,128)S(1)} %get-tuple-element.116), channel_id=1, source_target_pairs={{0,16},{4,20},{8,24},{12,28},{16,0},{20,4},{24,8},{28,12},{1,17},{... | collective-permute-start | bytes 98312 | tf_op jit(solution)/shard_map/ppermute | solution.py:284
  124.8 3.4 %collective-permute-start.51 = (f32[64,128]{1,0:T(8,128)S(1)}, f32[64,128]{1,0:T(8,128)S(1)}, u32[]{:S(2)}, u32[]{:S(2)}) collective-permute-start(f32[64,128]{1,0:T(8,128)S(1)} %solve_down.8.refs_0_.refs_3_), channel_id=1, source_target_pairs={{0,3},{1,2},{2,1},{3,0},{4,7},{5,6},{6,5},{7,4},{8,11},{9,10},{10,... | collective-permute-start | bytes 98312 | tf_op jit(solution)/shard_map/ppermute | solution.py:329
  124.9 4.3 %collective-permute-start.50 = (f32[64,128]{1,0:T(8,128)S(1)}, f32[64,128]{1,0:T(8,128)S(1)}, u32[]{:S(2)}, u32[]{:S(2)}) collective-permute-start(f32[64,128]{1,0:T(8,128)S(1)} %solve_down.8.refs_0_.refs_3_), channel_id=1, source_target_pairs={{0,2},{1,3},{2,0},{3,1},{4,6},{5,7},{6,4},{7,5},{8,10},{9,11},{10,... | collective-permute-start | bytes 98312 | tf_op jit(solution)/shard_map/ppermute | solution.py:329
  125.8 3.3 %collective-permute-start.49 = (f32[64,128]{1,0:T(8,128)S(1)}, f32[64,128]{1,0:T(8,128)S(1)}, u32[]{:S(2)}, u32[]{:S(2)}) collective-permute-start(f32[64,128]{1,0:T(8,128)S(1)} %solve_down.8.refs_0_.refs_3_), channel_id=1, source_target_pairs={{0,1},{1,0},{2,3},{3,2},{4,5},{5,4},{6,7},{7,6},{8,9},{9,8},{10,11... | collective-permute-start | bytes 98312 | tf_op jit(solution)/shard_map/ppermute | solution.py:329
  129.7 5.7 %collective-permute-start.52 = (f32[2,64,128]{2,1,0:T(8,128)S(1)}, f32[2,64,128]{2,1,0:T(8,128)S(1)}, u32[]{:S(2)}, u32[]{:S(2)}) collective-permute-start(f32[2,64,128]{2,1,0:T(8,128)S(1)} %get-tuple-element.117), channel_id=1, source_target_pairs={{0,12},{1,13},{2,14},{3,15},{4,8},{5,9},{6,10},{7,11},{8,4},{9,5},... | collective-permute-start | bytes 196616 | tf_op jit(solution)/shard_map/ppermute | solution.py:302
  129.9 5.7 %collective-permute-start.53 = (f32[2,64,128]{2,1,0:T(8,128)S(1)}, f32[2,64,128]{2,1,0:T(8,128)S(1)}, u32[]{:S(2)}, u32[]{:S(2)}) collective-permute-start(f32[2,64,128]{2,1,0:T(8,128)S(1)} %get-tuple-element.118), channel_id=1, source_target_pairs={{0,8},{1,5},{2,10},{3,7},{4,12},{5,1},{6,14},{7,3},{8,0},{9,13},{1... | collective-permute-start | bytes 196616 | tf_op jit(solution)/shard_map/ppermute | solution.py:302
  131.9 4.3 %collective-permute-start.54 = (f32[2,64,128]{2,1,0:T(8,128)S(1)}, f32[2,64,128]{2,1,0:T(8,128)S(1)}, u32[]{:S(2)}, u32[]{:S(2)}) collective-permute-start(f32[2,64,128]{2,1,0:T(8,128)S(1)} %get-tuple-element.119), channel_id=1, source_target_pairs={{0,4},{1,9},{2,6},{3,11},{4,0},{5,13},{6,2},{7,15},{8,12},{9,1},{1... | collective-permute-start | bytes 196616 | tf_op jit(solution)/shard_map/ppermute | solution.py:302
  136.2 5.1 %collective-permute-start.55 = (f32[64,128]{1,0:T(8,128)S(1)}, f32[64,128]{1,0:T(8,128)S(1)}, u32[]{:S(2)}, u32[]{:S(2)}) collective-permute-start(f32[64,128]{1,0:T(8,128)S(1)} %get-tuple-element.121), channel_id=1, source_target_pairs={{0,16},{4,20},{8,24},{12,28},{16,0},{20,4},{24,8},{28,12},{1,17},{... | collective-permute-start | bytes 98312 | tf_op jit(solution)/shard_map/ppermute | solution.py:284
  141.5 3.4 %collective-permute-start.58 = (f32[64,128]{1,0:T(8,128)S(1)}, f32[64,128]{1,0:T(8,128)S(1)}, u32[]{:S(2)}, u32[]{:S(2)}) collective-permute-start(f32[64,128]{1,0:T(8,128)S(1)} %solve_down.9.refs_0_.refs_2_), channel_id=1, source_target_pairs={{0,3},{1,2},{2,1},{3,0},{4,7},{5,6},{6,5},{7,4},{8,11},{9,10},{10,... | collective-permute-start | bytes 98312 | tf_op jit(solution)/shard_map/ppermute | solution.py:329
  141.6 4.2 %collective-permute-start.57 = (f32[64,128]{1,0:T(8,128)S(1)}, f32[64,128]{1,0:T(8,128)S(1)}, u32[]{:S(2)}, u32[]{:S(2)}) collective-permute-start(f32[64,128]{1,0:T(8,128)S(1)} %solve_down.9.refs_0_.refs_2_), channel_id=1, source_target_pairs={{0,2},{1,3},{2,0},{3,1},{4,6},{5,7},{6,4},{7,5},{8,10},{9,11},{10,... | collective-permute-start | bytes 98312 | tf_op jit(solution)/shard_map/ppermute | solution.py:329
  142.5 3.3 %collective-permute-start.56 = (f32[64,128]{1,0:T(8,128)S(1)}, f32[64,128]{1,0:T(8,128)S(1)}, u32[]{:S(2)}, u32[]{:S(2)}) collective-permute-start(f32[64,128]{1,0:T(8,128)S(1)} %solve_down.9.refs_0_.refs_2_), channel_id=1, source_target_pairs={{0,1},{1,0},{2,3},{3,2},{4,5},{5,4},{6,7},{7,6},{8,9},{9,8},{10,11... | collective-permute-start | bytes 98312 | tf_op jit(solution)/shard_map/ppermute | solution.py:329
  146.4 5.7 %collective-permute-start.59 = (f32[2,64,128]{2,1,0:T(8,128)S(1)}, f32[2,64,128]{2,1,0:T(8,128)S(1)}, u32[]{:S(2)}, u32[]{:S(2)}) collective-permute-start(f32[2,64,128]{2,1,0:T(8,128)S(1)} %get-tuple-element.122), channel_id=1, source_target_pairs={{0,12},{1,13},{2,14},{3,15},{4,8},{5,9},{6,10},{7,11},{8,4},{9,5},... | collective-permute-start | bytes 196616 | tf_op jit(solution)/shard_map/ppermute | solution.py:302
  147.0 5.5 %collective-permute-start.60 = (f32[2,64,128]{2,1,0:T(8,128)S(1)}, f32[2,64,128]{2,1,0:T(8,128)S(1)}, u32[]{:S(2)}, u32[]{:S(2)}) collective-permute-start(f32[2,64,128]{2,1,0:T(8,128)S(1)} %get-tuple-element.123), channel_id=1, source_target_pairs={{0,8},{1,5},{2,10},{3,7},{4,12},{5,1},{6,14},{7,3},{8,0},{9,13},{1... | collective-permute-start | bytes 196616 | tf_op jit(solution)/shard_map/ppermute | solution.py:302
  148.8 4.3 %collective-permute-start.61 = (f32[2,64,128]{2,1,0:T(8,128)S(1)}, f32[2,64,128]{2,1,0:T(8,128)S(1)}, u32[]{:S(2)}, u32[]{:S(2)}) collective-permute-start(f32[2,64,128]{2,1,0:T(8,128)S(1)} %get-tuple-element.124), channel_id=1, source_target_pairs={{0,4},{1,9},{2,6},{3,11},{4,0},{5,13},{6,2},{7,15},{8,12},{9,1},{1... | collective-permute-start | bytes 196616 | tf_op jit(solution)/shard_map/ppermute | solution.py:302
  153.1 5.0 %collective-permute-start.62 = (f32[64,128]{1,0:T(8,128)S(1)}, f32[64,128]{1,0:T(8,128)S(1)}, u32[]{:S(2)}, u32[]{:S(2)}) collective-permute-start(f32[64,128]{1,0:T(8,128)S(1)} %get-tuple-element.126), channel_id=1, source_target_pairs={{0,16},{4,20},{8,24},{12,28},{16,0},{20,4},{24,8},{28,12},{1,17},{... | collective-permute-start | bytes 98312 | tf_op jit(solution)/shard_map/ppermute | solution.py:284
  158.3 3.4 %collective-permute-start.65 = (f32[64,128]{1,0:T(8,128)S(1)}, f32[64,128]{1,0:T(8,128)S(1)}, u32[]{:S(2)}, u32[]{:S(2)}) collective-permute-start(f32[64,128]{1,0:T(8,128)S(1)} %solve_down.10.refs_0_.refs_1_), channel_id=1, source_target_pairs={{0,3},{1,2},{2,1},{3,0},{4,7},{5,6},{6,5},{7,4},{8,11},{9,10},{10,... | collective-permute-start | bytes 98312 | tf_op jit(solution)/shard_map/ppermute | solution.py:329
  158.4 4.2 %collective-permute-start.64 = (f32[64,128]{1,0:T(8,128)S(1)}, f32[64,128]{1,0:T(8,128)S(1)}, u32[]{:S(2)}, u32[]{:S(2)}) collective-permute-start(f32[64,128]{1,0:T(8,128)S(1)} %solve_down.10.refs_0_.refs_1_), channel_id=1, source_target_pairs={{0,2},{1,3},{2,0},{3,1},{4,6},{5,7},{6,4},{7,5},{8,10},{9,11},{10,... | collective-permute-start | bytes 98312 | tf_op jit(solution)/shard_map/ppermute | solution.py:329
  159.2 3.3 %collective-permute-start.63 = (f32[64,128]{1,0:T(8,128)S(1)}, f32[64,128]{1,0:T(8,128)S(1)}, u32[]{:S(2)}, u32[]{:S(2)}) collective-permute-start(f32[64,128]{1,0:T(8,128)S(1)} %solve_down.10.refs_0_.refs_1_), channel_id=1, source_target_pairs={{0,1},{1,0},{2,3},{3,2},{4,5},{5,4},{6,7},{7,6},{8,9},{9,8},{10,11... | collective-permute-start | bytes 98312 | tf_op jit(solution)/shard_map/ppermute | solution.py:329
  163.1 5.8 %collective-permute-start.66 = (f32[2,64,128]{2,1,0:T(8,128)S(1)}, f32[2,64,128]{2,1,0:T(8,128)S(1)}, u32[]{:S(2)}, u32[]{:S(2)}) collective-permute-start(f32[2,64,128]{2,1,0:T(8,128)S(1)} %get-tuple-element.127), channel_id=1, source_target_pairs={{0,12},{1,13},{2,14},{3,15},{4,8},{5,9},{6,10},{7,11},{8,4},{9,5},... | collective-permute-start | bytes 196616 | tf_op jit(solution)/shard_map/ppermute | solution.py:302
  163.9 5.1 %collective-permute-start.67 = (f32[2,64,128]{2,1,0:T(8,128)S(1)}, f32[2,64,128]{2,1,0:T(8,128)S(1)}, u32[]{:S(2)}, u32[]{:S(2)}) collective-permute-start(f32[2,64,128]{2,1,0:T(8,128)S(1)} %get-tuple-element.128), channel_id=1, source_target_pairs={{0,8},{1,5},{2,10},{3,7},{4,12},{5,1},{6,14},{7,3},{8,0},{9,13},{1... | collective-permute-start | bytes 196616 | tf_op jit(solution)/shard_map/ppermute | solution.py:302
  165.7 4.3 %collective-permute-start.68 = (f32[2,64,128]{2,1,0:T(8,128)S(1)}, f32[2,64,128]{2,1,0:T(8,128)S(1)}, u32[]{:S(2)}, u32[]{:S(2)}) collective-permute-start(f32[2,64,128]{2,1,0:T(8,128)S(1)} %get-tuple-element.129), channel_id=1, source_target_pairs={{0,4},{1,9},{2,6},{3,11},{4,0},{5,13},{6,2},{7,15},{8,12},{9,1},{1... | collective-permute-start | bytes 196616 | tf_op jit(solution)/shard_map/ppermute | solution.py:302
  170.0 4.9 %collective-permute-start.69 = (f32[64,128]{1,0:T(8,128)S(1)}, f32[64,128]{1,0:T(8,128)S(1)}, u32[]{:S(2)}, u32[]{:S(2)}) collective-permute-start(f32[64,128]{1,0:T(8,128)S(1)} %get-tuple-element.131), channel_id=1, source_target_pairs={{0,16},{4,20},{8,24},{12,28},{16,0},{20,4},{24,8},{28,12},{1,17},{... | collective-permute-start | bytes 98312 | tf_op jit(solution)/shard_map/ppermute | solution.py:284
  (13 other events, 57.1 us)

commit v10 on v8

--- a/solution.py
+++ b/solution.py
@@ -50,6 +50,7 @@
         pl.when(lax.rem(slot, chunk) == 0)(fetch(slot // chunk).wait)
         source = slots_ref[level, slot_count + slot]
         near = lax.rem(source, half) ^ lax.rem(row, half)
+        near = jnp.where(lax.rem(col, 2) == 1, mirrored(near, half), near)
         below = near * 2 + ((source // half) ^ side)
         above = slots_ref[level, slot] ^ col
         total[below * n_col + above] += slots[slot]
@@ -283,22 +284,52 @@
     return lax.ppermute(segment, axis, [(i, i ^ (size // 2)) for i in range(size)])
 
 
+def mirrored(number, size):
+    bits = size.bit_length() - 1
+    return sum(((number >> bit) & 1) << (bits - 1 - bit) for bit in range(bits))
+
+
+def near_exchange(message, bit):
+    n_row, n_col = lax.axis_size("row"), lax.axis_size("col")
+    pairs = []
+    for row in range(n_row):
+        for col in range(n_col):
+            partner = row ^ (mirrored(bit, n_row // 2) if col % 2 else bit)
+            pairs.append((row * n_col + col, partner * n_col + col))
+    return lax.ppermute(message, ("row", "col"), pairs)
+
+
+def bits_below(size):
+    return [1 << place for place in range(size.bit_length() - 1)]
+
+
+def both_sides(message):
+    return [(message, side) for side in range(2)]
+
+
 def gather_row(segment, after):
     half = lax.axis_size("row") // 2
     received = far_exchange(segment, "row")
     (both,) = combine([[[(segment, None)], [(received, None)]]], after)
-    messages = exchange_each([both] * half, "row")
-    return [(message, side) for message in messages for side in range(2)]
+    held = {0: both}
+    for bit in reversed(bits_below(half)):
+        for d in sorted(held):
+            held[d | bit] = near_exchange(held[d], bit)
+    return [piece for d in range(half) for piece in both_sides(held[d])]
 
 
 def deliver_row(messages):
-    received = exchange_each(messages, "row")
-    mine, other = combine(
-        [
-            [[(message, side) for message in [received[0], *reversed(received[1:])]]]
-            for side in range(2)
-        ]
-    )
+    held = {d: [message] for d, message in enumerate(messages)}
+    for bit in bits_below(len(messages)):
+        for d in sorted((d for d in held if d & bit), reverse=True):
+            parts = held.pop(d)
+            message = parts[0]
+            if len(parts) > 1:
+                sides = [list(pieces) for pieces in zip(*map(both_sides, parts))]
+                (message,) = combine([sides])
+            held[d ^ bit].append(near_exchange(message, bit))
+    sides = [list(pieces) for pieces in zip(*map(both_sides, held[0]))]
+    mine, other = combine([[side] for side in sides])
     return [(mine, None), (far_exchange(other, "row"), None)]
 
 
@@ -342,17 +373,17 @@
         else:
             down.append(tidy(level - 1, True, near[:1]))
             after = down[-1][:1]
-        pieces = plain(exchange_each(near + far, "col"))
+        pieces = plain(reversed(exchange_each(near + far, "col")))
         forward.append(solve(right, inverse, level, pieces, False, after))
     backward = [None] * levels
     backward[-1] = solve(forward[-1], inverse, levels - 1, [], True)
     for level in range(levels - 2, -1, -1):
         pieces = plain(exchange_each([backward[level + 1]] * n_col, "col"))
-        sent = couple(pieces, *down[level], (2, n_row), 2)
-        kept = couple(pieces, *down[level], (0, 2), 2)
+        first = couple(pieces, *down[level], (n_row - 2, n_row), 2)
+        later = couple(pieces, *down[level], (0, n_row - 2), 2)
         if level == levels - 2:
-            forward_out = stack(forward, kept[:1])
-        pieces = deliver_row(kept + sent)
+            forward_out = stack(forward, later[:1])
+        pieces = deliver_row(later + first)
         after = (forward_out,) if level == levels - 2 else ()
         backward[level] = solve(forward[level], inverse, level, pieces, True, after)
     return forward_out.reshape(rhs.shape), stack(backward).reshape(rhs.shape)
@@ -475,7 +506,7 @@
     def local(rhs, diag_inv, blocks, blk_target, blk_source, blk_count):
         sizes = (n_row, n_col)
         dense = n_row * n_col <= blocks.shape[3] and rhs.shape[3] == 1
-        even = all(size > 1 and size & (size - 1) == 0 for size in sizes)
+        even = n_row > 2 and n_col > 1 and all(size & (size - 1) == 0 for size in sizes)
         run = direct_shards if dense and even else shards
         return run(rhs, diag_inv, blocks, blk_target, blk_source, blk_count)
 

time: 177 us -> 193 us (1.090)
  waiting for transfers between devices: 82.2 us -> 104 us
  starting transfers between devices: 64.8 us -> 58.7 us
    ppermute x0 -> x30, waiting for transfers between devices: none -> 52.6 us  [near_exchange(): return lax.ppermute(message, ('row', 'col'), pairs)]
    ppermute x60 -> x30, starting transfers between devices: 56.2 us -> 20.7 us  [exchange_each(): lax.ppermute(messages[d], axis, [(i, i ^ d) for i in range(size)])]
    ppermute x60 -> x30, waiting for transfers between devices: 47.2 us -> 14.4 us  [exchange_each(): lax.ppermute(messages[d], axis, [(i, i ^ d) for i in range(size)])]
    ppermute x0 -> x30, starting transfers between devices: none -> 31.4 us  [near_exchange(): return lax.ppermute(message, ('row', 'col'), pairs)]
    ppermute x10, waiting for transfers between devices: 35 us -> 37.4 us  [far_exchange(): lax.ppermute(segment, axis, [(i, i ^ size // 2) for i in range(size)])]
    ppermute x10, starting transfers between devices: 8.6 us -> 6.62 us  [far_exchange(): lax.ppermute(segment, axis, [(i, i ^ size // 2) for i in range(size)])]
  transfers between devices with their start and end apart: 70 -> 70, of which waited for: 52 -> 48; matrix products, arithmetic and copies ran while one was open for 1% -> 1% of each run, Pallas kernels for 10% -> 9%
where the time goes in v10:
time: 193 us; the launch traced here: 192 us
  waiting for transfers between devices  104 us (54%)
  starting transfers between devices  58.7 us (30%)
  Pallas kernels  25.6 us (13%)
  local copies, waits for them, and re-layouts  2.48 us (1%)
    ppermute x30, waiting for transfers between devices, near_exchange(): return lax.ppermute(message, ('row', 'col'), pairs)  52.6 us
    ppermute x10, waiting for transfers between devices, far_exchange(): lax.ppermute(segment, axis, [(i, i ^ size // 2) for i in range(size)])  37.4 us
    ppermute x30, starting transfers between devices, near_exchange(): return lax.ppermute(message, ('row', 'col'), pairs)  31.4 us
    ppermute x30, starting transfers between devices, exchange_each(): lax.ppermute(messages[d], axis, [(i, i ^ d) for i in range(size)])  20.7 us
    ppermute x30, waiting for transfers between devices, exchange_each(): lax.ppermute(messages[d], axis, [(i, i ^ d) for i in range(size)])  14.4 us
    pallas_call x20, Pallas kernels, couple(): pl.pallas_call(functools.partial(couple_kernel, terms, span), out_shape=[...  7.88 us
    pallas_call x5, Pallas kernels, gather_blocks(): pl.pallas_call(functools.partial(gather_blocks_kernel, n_row, n_col, leve...  7.47 us
    ppermute x10, starting transfers between devices, far_exchange(): lax.ppermute(segment, axis, [(i, i ^ size // 2) for i in range(size)])  6.62 us
  transfers between devices with their start and end apart: 70, of which 48 were waited for; matrix products, arithmetic and copies ran while one was open for 1% of the time, Pallas kernels for 9%

profile of v10, /device:TPU:0, one launch (start us, length us, event | category | flops | bytes accessed | tf_op | source)
XLA Modules:
  0.0 192.4 jit_solution(18388842974512128127)
XLA Ops:
  0.6 1.7 first_solve.1.refs_0_
  2.3 4.1 %collective-permute-start = (f32[64,128]{1,0:T(8,128)}, f32[64,128]{1,0:T(8,128)S(1)}, u32[]{:S(2)}, u32[]{:S(2)}) collective-permute-start(f32[64,128]{1,0:T(8,128)} %first_solve.1.refs_0_), channel_id=1, source_target_pairs={{0,16},{4,20},{8,24},{12,28},{16,0},{20,4},{24,8},{28,12},{1,17},{... | collective-permute-start | bytes 98312 | tf_op jit(solution)/shard_map/ppermute | solution.py:284
  7.9 2.2 %gather_blocks_0.1.total_ref = f32[32,128,128]{2,1,0:T(8,128)S(1)} custom-call(s32[5,67]{1,0:T(8,128)S(1)} %concatenate.3.slots_ref, f32[5,32,128,128]{3,2,1,0:T(8,128)} %bitcast.14), custom_call_target="tpu_custom_call" | custom-call | flops 524288 | bytes 4194304 | tf_op jit(solution)/shard_map/gather_blocks_0/pallas_call | solution.py:67
  10.5 1.6 collective-permute-start.2
  12.1 1.6 collective-permute-start.1
  13.7 1.7 collective-permute-done.2.refs_2_
  16.6 3.1 %collective-permute-done.3.refs_3_ = f32[2,64,128]{2,1,0:T(8,128)S(1)} collective-permute-done((f32[2,64,128]{2,1,0:T(8,128)S(1)}, f32[2,64,128]{2,1,0:T(8,128)S(1)}, u32[]{:S(2)}, u32[]{:S(2)}) %collective-permute-start.3) | collective-permute-done | bytes 65568 | tf_op jit(solution)/shard_map/ppermute | solution.py:299
  20.2 1.8 collective-permute-start.5
  22.5 1.2 gather_blocks_1.1.refs_6_.total_ref
  25.9 3.4 %collective-permute-done.7.refs_1_ = f32[64,128]{1,0:T(8,128)S(1)} collective-permute-done((f32[64,128]{1,0:T(8,128)S(1)}, f32[64,128]{1,0:T(8,128)S(1)}, u32[]{:S(2)}, u32[]{:S(2)}) %collective-permute-start.7) | collective-permute-done | bytes 32800 | tf_op jit(solution)/shard_map/ppermute | solution.py:284
  29.3 1.6 collective-permute-start.9
  31.9 1.6 collective-permute-done.9.refs_2_
  33.5 1.7 collective-permute-start.10
  35.2 2.6 %collective-permute-done.10.refs_3_ = f32[2,64,128]{2,1,0:T(8,128)S(1)} collective-permute-done((f32[2,64,128]{2,1,0:T(8,128)S(1)}, f32[2,64,128]{2,1,0:T(8,128)S(1)}, u32[]{:S(2)}, u32[]{:S(2)}) %collective-permute-start.10) | collective-permute-done | bytes 65568 | tf_op jit(solution)/shard_map/ppermute | solution.py:299
  38.3 2.1 %collective-permute-start.12 = (f32[64,128]{1,0:T(8,128)S(1)}, f32[64,128]{1,0:T(8,128)S(1)}, u32[]{:S(2)}, u32[]{:S(2)}) collective-permute-start(f32[64,128]{1,0:T(8,128)S(1)} %get-tuple-element.77), channel_id=1, source_target_pairs={{0,2},{1,3},{2,0},{3,1},{4,6},{5,7},{6,4},{7,5},{8,10},{9,11},{10,... | collective-permute-start | bytes 98312 | tf_op jit(solution)/shard_map/ppermute | solution.py:340
  44.1 3.5 %collective-permute-done.14.refs_1_ = f32[64,128]{1,0:T(8,128)S(1)} collective-permute-done((f32[64,128]{1,0:T(8,128)S(1)}, f32[64,128]{1,0:T(8,128)S(1)}, u32[]{:S(2)}, u32[]{:S(2)}) %collective-permute-start.14) | collective-permute-done | bytes 32800 | tf_op jit(solution)/shard_map/ppermute | solution.py:284
  47.6 1.3 collective-permute-start.16
  48.9 1.3 collective-permute-start.15
  50.2 1.7 collective-permute-done.16.refs_2_
  51.9 1.6 collective-permute-start.17
  53.5 2.7 %collective-permute-done.17.refs_3_ = f32[2,64,128]{2,1,0:T(8,128)S(1)} collective-permute-done((f32[2,64,128]{2,1,0:T(8,128)S(1)}, f32[2,64,128]{2,1,0:T(8,128)S(1)}, u32[]{:S(2)}, u32[]{:S(2)}) %collective-permute-start.17) | collective-permute-done | bytes 65568 | tf_op jit(solution)/shard_map/ppermute | solution.py:299
  56.7 1.8 collective-permute-start.19
  59.0 1.3 gather_blocks_3.1.refs_6_.total_ref
  62.3 3.7 %collective-permute-done.21.refs_1_ = f32[64,128]{1,0:T(8,128)S(1)} collective-permute-done((f32[64,128]{1,0:T(8,128)S(1)}, f32[64,128]{1,0:T(8,128)S(1)}, u32[]{:S(2)}, u32[]{:S(2)}) %collective-permute-start.21) | collective-permute-done | bytes 32800 | tf_op jit(solution)/shard_map/ppermute | solution.py:284
  67.0 1.3 collective-permute-start.22
  68.3 2.1 %collective-permute-done.23.refs_2_ = f32[2,64,128]{2,1,0:T(8,128)S(1)} collective-permute-done((f32[2,64,128]{2,1,0:T(8,128)S(1)}, f32[2,64,128]{2,1,0:T(8,128)S(1)}, u32[]{:S(2)}, u32[]{:S(2)}) %collective-permute-start.23) | collective-permute-done | bytes 65568 | tf_op jit(solution)/shard_map/ppermute | solution.py:299
  70.4 1.3 collective-permute-start.24
  71.6 3.0 %collective-permute-done.24.refs_3_ = f32[2,64,128]{2,1,0:T(8,128)S(1)} collective-permute-done((f32[2,64,128]{2,1,0:T(8,128)S(1)}, f32[2,64,128]{2,1,0:T(8,128)S(1)}, u32[]{:S(2)}, u32[]{:S(2)}) %collective-permute-start.24) | collective-permute-done | bytes 65568 | tf_op jit(solution)/shard_map/ppermute | solution.py:299
  75.1 1.7 collective-permute-start.26
  77.4 1.7 gather_blocks_4.1.refs_6_.total_ref
  81.0 3.7 %collective-permute-done.28.refs_1_ = f32[64,128]{1,0:T(8,128)S(1)} collective-permute-done((f32[64,128]{1,0:T(8,128)S(1)}, f32[64,128]{1,0:T(8,128)S(1)}, u32[]{:S(2)}, u32[]{:S(2)}) %collective-permute-start.28) | collective-permute-done | bytes 32800 | tf_op jit(solution)/shard_map/ppermute | solution.py:284
  85.1 1.4 collective-permute-start.29
  86.5 2.5 %collective-permute-done.30.refs_2_ = f32[2,64,128]{2,1,0:T(8,128)S(1)} collective-permute-done((f32[2,64,128]{2,1,0:T(8,128)S(1)}, f32[2,64,128]{2,1,0:T(8,128)S(1)}, u32[]{:S(2)}, u32[]{:S(2)}) %collective-permute-start.30) | collective-permute-done | bytes 65568 | tf_op jit(solution)/shard_map/ppermute | solution.py:299
  89.0 1.5 collective-permute-start.31
  90.6 2.7 %collective-permute-done.31.refs_3_ = f32[2,64,128]{2,1,0:T(8,128)S(1)} collective-permute-done((f32[2,64,128]{2,1,0:T(8,128)S(1)}, f32[2,64,128]{2,1,0:T(8,128)S(1)}, u32[]{:S(2)}, u32[]{:S(2)}) %collective-permute-start.31) | collective-permute-done | bytes 65568 | tf_op jit(solution)/shard_map/ppermute | solution.py:299
  93.8 2.3 %collective-permute-start.33 = (f32[64,128]{1,0:T(8,128)S(1)}, f32[64,128]{1,0:T(8,128)S(1)}, u32[]{:S(2)}, u32[]{:S(2)}) collective-permute-start(f32[64,128]{1,0:T(8,128)S(1)} %get-tuple-element.98), channel_id=1, source_target_pairs={{0,2},{1,3},{2,0},{3,1},{4,6},{5,7},{6,4},{7,5},{8,10},{9,11},{10,... | collective-permute-start | bytes 98312 | tf_op jit(solution)/shard_map/ppermute | solution.py:340
  98.5 1.3 collective-permute-start.37
  101.9 1.9 collective-permute-done.36.refs_2_
  105.0 1.7 collective-permute-start.38
  106.8 1.6 collective-permute-done.39.refs_1_
  109.4 3.4 %collective-permute-done.40.refs_2_ = f32[2,64,128]{2,1,0:T(8,128)S(1)} collective-permute-done((f32[2,64,128]{2,1,0:T(8,128)S(1)}, f32[2,64,128]{2,1,0:T(8,128)S(1)}, u32[]{:S(2)}, u32[]{:S(2)}) %collective-permute-start.40) | collective-permute-done | bytes 65568 | tf_op jit(solution)/shard_map/ppermute | solution.py:299
  113.5 4.2 %collective-permute-done.41.refs_3_ = f32[64,128]{1,0:T(8,128)S(1)} collective-permute-done((f32[64,128]{1,0:T(8,128)S(1)}, f32[64,128]{1,0:T(8,128)S(1)}, u32[]{:S(2)}, u32[]{:S(2)}) %collective-permute-start.41) | collective-permute-done | bytes 32800 | tf_op jit(solution)/shard_map/ppermute | solution.py:284
  120.8 1.5 collective-permute-done.44.refs_3_
  124.6 1.5 collective-permute-start.45
  126.2 1.6 collective-permute-done.46.refs_1_
  128.9 3.2 %collective-permute-done.47.refs_2_ = f32[2,64,128]{2,1,0:T(8,128)S(1)} collective-permute-done((f32[2,64,128]{2,1,0:T(8,128)S(1)}, f32[2,64,128]{2,1,0:T(8,128)S(1)}, u32[]{:S(2)}, u32[]{:S(2)}) %collective-permute-start.47) | collective-permute-done | bytes 65568 | tf_op jit(solution)/shard_map/ppermute | solution.py:299
  132.2 4.8 %collective-permute-done.48.refs_3_ = f32[64,128]{1,0:T(8,128)S(1)} collective-permute-done((f32[64,128]{1,0:T(8,128)S(1)}, f32[64,128]{1,0:T(8,128)S(1)}, u32[]{:S(2)}, u32[]{:S(2)}) %collective-permute-start.48) | collective-permute-done | bytes 32800 | tf_op jit(solution)/shard_map/ppermute | solution.py:284
  139.1 1.5 collective-permute-done.51.refs_3_
  144.4 1.6 collective-permute-done.53.refs_1_
  146.2 1.7 collective-permute-done.52.refs_1_
  147.8 2.5 %collective-permute-done.54.refs_2_ = f32[2,64,128]{2,1,0:T(8,128)S(1)} collective-permute-done((f32[2,64,128]{2,1,0:T(8,128)S(1)}, f32[2,64,128]{2,1,0:T(8,128)S(1)}, u32[]{:S(2)}, u32[]{:S(2)}) %collective-permute-start.54) | collective-permute-done | bytes 65568 | tf_op jit(solution)/shard_map/ppermute | solution.py:299
  150.5 4.7 %collective-permute-done.55.refs_3_ = f32[64,128]{1,0:T(8,128)S(1)} collective-permute-done((f32[64,128]{1,0:T(8,128)S(1)}, f32[64,128]{1,0:T(8,128)S(1)}, u32[]{:S(2)}, u32[]{:S(2)}) %collective-permute-start.55) | collective-permute-done | bytes 32800 | tf_op jit(solution)/shard_map/ppermute | solution.py:284
  156.1 1.2 collective-permute-start.56
  157.3 1.5 collective-permute-done.58.refs_3_
  162.5 1.6 collective-permute-done.60.refs_1_
  164.3 2.0 %collective-permute-done.59.refs_1_ = f32[2,64,128]{2,1,0:T(8,128)S(1)} collective-permute-done((f32[2,64,128]{2,1,0:T(8,128)S(1)}, f32[2,64,128]{2,1,0:T(8,128)S(1)}, u32[]{:S(2)}, u32[]{:S(2)}) %collective-permute-start.59) | collective-permute-done | bytes 65568 | tf_op jit(solution)/shard_map/ppermute | solution.py:299
  166.2 2.2 %collective-permute-done.61.refs_2_ = f32[2,64,128]{2,1,0:T(8,128)S(1)} collective-permute-done((f32[2,64,128]{2,1,0:T(8,128)S(1)}, f32[2,64,128]{2,1,0:T(8,128)S(1)}, u32[]{:S(2)}, u32[]{:S(2)}) %collective-permute-start.61) | collective-permute-done | bytes 65568 | tf_op jit(solution)/shard_map/ppermute | solution.py:299
  168.7 4.7 %collective-permute-done.62.refs_3_ = f32[64,128]{1,0:T(8,128)S(1)} collective-permute-done((f32[64,128]{1,0:T(8,128)S(1)}, f32[64,128]{1,0:T(8,128)S(1)}, u32[]{:S(2)}, u32[]{:S(2)}) %collective-permute-start.62) | collective-permute-done | bytes 32800 | tf_op jit(solution)/shard_map/ppermute | solution.py:284
  174.3 1.2 collective-permute-start.63
  175.5 1.5 collective-permute-done.65.refs_3_
  180.6 1.6 collective-permute-done.67.refs_1_
  182.4 2.0 %collective-permute-done.66.refs_1_ = f32[2,64,128]{2,1,0:T(8,128)S(1)} collective-permute-done((f32[2,64,128]{2,1,0:T(8,128)S(1)}, f32[2,64,128]{2,1,0:T(8,128)S(1)}, u32[]{:S(2)}, u32[]{:S(2)}) %collective-permute-start.66) | collective-permute-done | bytes 65568 | tf_op jit(solution)/shard_map/ppermute | solution.py:299
  184.4 2.2 %collective-permute-done.68.refs_2_ = f32[2,64,128]{2,1,0:T(8,128)S(1)} collective-permute-done((f32[2,64,128]{2,1,0:T(8,128)S(1)}, f32[2,64,128]{2,1,0:T(8,128)S(1)}, u32[]{:S(2)}, u32[]{:S(2)}) %collective-permute-start.68) | collective-permute-done | bytes 65568 | tf_op jit(solution)/shard_map/ppermute | solution.py:299
  186.8 4.7 %collective-permute-done.69.refs_3_ = f32[64,128]{1,0:T(8,128)S(1)} collective-permute-done((f32[64,128]{1,0:T(8,128)S(1)}, f32[64,128]{1,0:T(8,128)S(1)}, u32[]{:S(2)}, u32[]{:S(2)}) %collective-permute-start.69) | collective-permute-done | bytes 32800 | tf_op jit(solution)/shard_map/ppermute | solution.py:284
  (160 shorter events, 49.9 us)
Async XLA Ops:
  2.3 8.2 %collective-permute-start = (f32[64,128]{1,0:T(8,128)}, f32[64,128]{1,0:T(8,128)S(1)}, u32[]{:S(2)}, u32[]{:S(2)}) collective-permute-start(f32[64,128]{1,0:T(8,128)} %first_solve.1.refs_0_), channel_id=1, source_target_pairs={{0,16},{4,20},{8,24},{12,28},{16,0},{20,4},{24,8},{28,12},{1,17},{... | collective-permute-start | bytes 98312 | tf_op jit(solution)/shard_map/ppermute | solution.py:284
  10.5 4.9 %collective-permute-start.2 = (f32[2,64,128]{2,1,0:T(8,128)S(1)}, f32[2,64,128]{2,1,0:T(8,128)S(1)}, u32[]{:S(2)}, u32[]{:S(2)}) collective-permute-start(f32[2,64,128]{2,1,0:T(8,128)S(1)} %combine.15.refs_0_), channel_id=1, source_target_pairs={{0,8},{1,5},{2,10},{3,7},{4,12},{5,1},{6,14},{7,3},{8,0},{9,13},{1... | collective-permute-start | bytes 196616 | tf_op jit(solution)/shard_map/ppermute | solution.py:299
  12.1 4.5 %collective-permute-start.1 = (f32[2,64,128]{2,1,0:T(8,128)S(1)}, f32[2,64,128]{2,1,0:T(8,128)S(1)}, u32[]{:S(2)}, u32[]{:S(2)}) collective-permute-start(f32[2,64,128]{2,1,0:T(8,128)S(1)} %combine.15.refs_0_), channel_id=1, source_target_pairs={{0,4},{1,9},{2,6},{3,11},{4,0},{5,13},{6,2},{7,15},{8,12},{9,1},{1... | collective-permute-start | bytes 196616 | tf_op jit(solution)/shard_map/ppermute | solution.py:299
  15.5 4.3 %collective-permute-start.3 = (f32[2,64,128]{2,1,0:T(8,128)S(1)}, f32[2,64,128]{2,1,0:T(8,128)S(1)}, u32[]{:S(2)}, u32[]{:S(2)}) collective-permute-start(f32[2,64,128]{2,1,0:T(8,128)S(1)} %collective-permute-done.2.refs_2_), channel_id=1, source_target_pairs={{0,4},{1,9},{2,6},{3,11},{4,0},{5,13},{6,2},{7,15},{8,12},{9,1},{1... | collective-permute-start | bytes 196616 | tf_op jit(solution)/shard_map/ppermute | solution.py:299
  20.1 3.7 %collective-permute-start.4 = (f32[64,128]{1,0:T(8,128)S(1)}, f32[64,128]{1,0:T(8,128)S(1)}, u32[]{:S(2)}, u32[]{:S(2)}) collective-permute-start(f32[64,128]{1,0:T(8,128)S(1)} %get-tuple-element.69), channel_id=1, source_target_pairs={{0,3},{1,2},{2,1},{3,0},{4,7},{5,6},{6,5},{7,4},{8,11},{9,10},{10,... | collective-permute-start | bytes 98312 | tf_op jit(solution)/shard_map/ppermute | solution.py:340
  20.2 4.0 %collective-permute-start.5 = (f32[64,128]{1,0:T(8,128)S(1)}, f32[64,128]{1,0:T(8,128)S(1)}, u32[]{:S(2)}, u32[]{:S(2)}) collective-permute-start(f32[64,128]{1,0:T(8,128)S(1)} %get-tuple-element.70), channel_id=1, source_target_pairs={{0,2},{1,3},{2,0},{3,1},{4,6},{5,7},{6,4},{7,5},{8,10},{9,11},{10,... | collective-permute-start | bytes 98312 | tf_op jit(solution)/shard_map/ppermute | solution.py:340
  24.4 4.9 %collective-permute-start.7 = (f32[64,128]{1,0:T(8,128)S(1)}, f32[64,128]{1,0:T(8,128)S(1)}, u32[]{:S(2)}, u32[]{:S(2)}) collective-permute-start(f32[64,128]{1,0:T(8,128)S(1)} %solve_up.5.refs_0_.refs_1_), channel_id=1, source_target_pairs={{0,16},{4,20},{8,24},{12,28},{16,0},{20,4},{24,8},{28,12},{1,17},{... | collective-permute-start | bytes 98312 | tf_op jit(solution)/shard_map/ppermute | solution.py:284
  29.3 4.3 %collective-permute-start.9 = (f32[2,64,128]{2,1,0:T(8,128)S(1)}, f32[2,64,128]{2,1,0:T(8,128)S(1)}, u32[]{:S(2)}, u32[]{:S(2)}) collective-permute-start(f32[2,64,128]{2,1,0:T(8,128)S(1)} %combine.16.refs_0_), channel_id=1, source_target_pairs={{0,8},{1,5},{2,10},{3,7},{4,12},{5,1},{6,14},{7,3},{8,0},{9,13},{1... | collective-permute-start | bytes 196616 | tf_op jit(solution)/shard_map/ppermute | solution.py:299
  30.9 4.4 %collective-permute-start.8 = (f32[2,64,128]{2,1,0:T(8,128)S(1)}, f32[2,64,128]{2,1,0:T(8,128)S(1)}, u32[]{:S(2)}, u32[]{:S(2)}) collective-permute-start(f32[2,64,128]{2,1,0:T(8,128)S(1)} %combine.16.refs_0_), channel_id=1, source_target_pairs={{0,4},{1,9},{2,6},{3,11},{4,0},{5,13},{6,2},{7,15},{8,12},{9,1},{1... | collective-permute-start | bytes 196616 | tf_op jit(solution)/shard_map/ppermute | solution.py:299
  33.5 4.3 %collective-permute-start.10 = (f32[2,64,128]{2,1,0:T(8,128)S(1)}, f32[2,64,128]{2,1,0:T(8,128)S(1)}, u32[]{:S(2)}, u32[]{:S(2)}) collective-permute-start(f32[2,64,128]{2,1,0:T(8,128)S(1)} %collective-permute-done.9.refs_2_), channel_id=1, source_target_pairs={{0,4},{1,9},{2,6},{3,11},{4,0},{5,13},{6,2},{7,15},{8,12},{9,1},{1... | collective-permute-start | bytes 196616 | tf_op jit(solution)/shard_map/ppermute | solution.py:299
  38.2 3.7 %collective-permute-start.11 = (f32[64,128]{1,0:T(8,128)S(1)}, f32[64,128]{1,0:T(8,128)S(1)}, u32[]{:S(2)}, u32[]{:S(2)}) collective-permute-start(f32[64,128]{1,0:T(8,128)S(1)} %get-tuple-element.76), channel_id=1, source_target_pairs={{0,3},{1,2},{2,1},{3,0},{4,7},{5,6},{6,5},{7,4},{8,11},{9,10},{10,... | collective-permute-start | bytes 98312 | tf_op jit(solution)/shard_map/ppermute | solution.py:340
  38.3 4.3 %collective-permute-start.12 = (f32[64,128]{1,0:T(8,128)S(1)}, f32[64,128]{1,0:T(8,128)S(1)}, u32[]{:S(2)}, u32[]{:S(2)}) collective-permute-start(f32[64,128]{1,0:T(8,128)S(1)} %get-tuple-element.77), channel_id=1, source_target_pairs={{0,2},{1,3},{2,0},{3,1},{4,6},{5,7},{6,4},{7,5},{8,10},{9,11},{10,... | collective-permute-start | bytes 98312 | tf_op jit(solution)/shard_map/ppermute | solution.py:340
  42.7 4.9 %collective-permute-start.14 = (f32[64,128]{1,0:T(8,128)S(1)}, f32[64,128]{1,0:T(8,128)S(1)}, u32[]{:S(2)}, u32[]{:S(2)}) collective-permute-start(f32[64,128]{1,0:T(8,128)S(1)} %solve_up.6.refs_0_.refs_2_), channel_id=1, source_target_pairs={{0,16},{4,20},{8,24},{12,28},{16,0},{20,4},{24,8},{28,12},{1,17},{... | collective-permute-start | bytes 98312 | tf_op jit(solution)/shard_map/ppermute | solution.py:284
  47.6 4.3 %collective-permute-start.16 = (f32[2,64,128]{2,1,0:T(8,128)S(1)}, f32[2,64,128]{2,1,0:T(8,128)S(1)}, u32[]{:S(2)}, u32[]{:S(2)}) collective-permute-start(f32[2,64,128]{2,1,0:T(8,128)S(1)} %combine.17.refs_0_), channel_id=1, source_target_pairs={{0,8},{1,5},{2,10},{3,7},{4,12},{5,1},{6,14},{7,3},{8,0},{9,13},{1... | collective-permute-start | bytes 196616 | tf_op jit(solution)/shard_map/ppermute | solution.py:299
  48.9 4.6 %collective-permute-start.15 = (f32[2,64,128]{2,1,0:T(8,128)S(1)}, f32[2,64,128]{2,1,0:T(8,128)S(1)}, u32[]{:S(2)}, u32[]{:S(2)}) collective-permute-start(f32[2,64,128]{2,1,0:T(8,128)S(1)} %combine.17.refs_0_), channel_id=1, source_target_pairs={{0,4},{1,9},{2,6},{3,11},{4,0},{5,13},{6,2},{7,15},{8,12},{9,1},{1... | collective-permute-start | bytes 196616 | tf_op jit(solution)/shard_map/ppermute | solution.py:299
  51.9 4.3 %collective-permute-start.17 = (f32[2,64,128]{2,1,0:T(8,128)S(1)}, f32[2,64,128]{2,1,0:T(8,128)S(1)}, u32[]{:S(2)}, u32[]{:S(2)}) collective-permute-start(f32[2,64,128]{2,1,0:T(8,128)S(1)} %collective-permute-done.16.refs_2_), channel_id=1, source_target_pairs={{0,4},{1,9},{2,6},{3,11},{4,0},{5,13},{6,2},{7,15},{8,12},{9,1},{1... | collective-permute-start | bytes 196616 | tf_op jit(solution)/shard_map/ppermute | solution.py:299
  56.6 3.7 %collective-permute-start.18 = (f32[64,128]{1,0:T(8,128)S(1)}, f32[64,128]{1,0:T(8,128)S(1)}, u32[]{:S(2)}, u32[]{:S(2)}) collective-permute-start(f32[64,128]{1,0:T(8,128)S(1)} %get-tuple-element.83), channel_id=1, source_target_pairs={{0,3},{1,2},{2,1},{3,0},{4,7},{5,6},{6,5},{7,4},{8,11},{9,10},{10,... | collective-permute-start | bytes 98312 | tf_op jit(solution)/shard_map/ppermute | solution.py:340
  56.7 4.0 %collective-permute-start.19 = (f32[64,128]{1,0:T(8,128)S(1)}, f32[64,128]{1,0:T(8,128)S(1)}, u32[]{:S(2)}, u32[]{:S(2)}) collective-permute-start(f32[64,128]{1,0:T(8,128)S(1)} %get-tuple-element.84), channel_id=1, source_target_pairs={{0,2},{1,3},{2,0},{3,1},{4,6},{5,7},{6,4},{7,5},{8,10},{9,11},{10,... | collective-permute-start | bytes 98312 | tf_op jit(solution)/shard_map/ppermute | solution.py:340
  60.8 5.2 %collective-permute-start.21 = (f32[64,128]{1,0:T(8,128)S(1)}, f32[64,128]{1,0:T(8,128)S(1)}, u32[]{:S(2)}, u32[]{:S(2)}) collective-permute-start(f32[64,128]{1,0:T(8,128)S(1)} %solve_up.7.refs_0_.refs_3_), channel_id=1, source_target_pairs={{0,16},{4,20},{8,24},{12,28},{16,0},{20,4},{24,8},{28,12},{1,17},{... | collective-permute-start | bytes 98312 | tf_op jit(solution)/shard_map/ppermute | solution.py:284
  66.1 4.3 %collective-permute-start.23 = (f32[2,64,128]{2,1,0:T(8,128)S(1)}, f32[2,64,128]{2,1,0:T(8,128)S(1)}, u32[]{:S(2)}, u32[]{:S(2)}) collective-permute-start(f32[2,64,128]{2,1,0:T(8,128)S(1)} %combine.18.refs_0_), channel_id=1, source_target_pairs={{0,8},{1,5},{2,10},{3,7},{4,12},{5,1},{6,14},{7,3},{8,0},{9,13},{1... | collective-permute-start | bytes 196616 | tf_op jit(solution)/shard_map/ppermute | solution.py:299
  67.0 4.6 %collective-permute-start.22 = (f32[2,64,128]{2,1,0:T(8,128)S(1)}, f32[2,64,128]{2,1,0:T(8,128)S(1)}, u32[]{:S(2)}, u32[]{:S(2)}) collective-permute-start(f32[2,64,128]{2,1,0:T(8,128)S(1)} %combine.18.refs_0_), channel_id=1, source_target_pairs={{0,4},{1,9},{2,6},{3,11},{4,0},{5,13},{6,2},{7,15},{8,12},{9,1},{1... | collective-permute-start | bytes 196616 | tf_op jit(solution)/shard_map/ppermute | solution.py:299
  70.4 4.3 %collective-permute-start.24 = (f32[2,64,128]{2,1,0:T(8,128)S(1)}, f32[2,64,128]{2,1,0:T(8,128)S(1)}, u32[]{:S(2)}, u32[]{:S(2)}) collective-permute-start(f32[2,64,128]{2,1,0:T(8,128)S(1)} %collective-permute-done.23.refs_2_), channel_id=1, source_target_pairs={{0,4},{1,9},{2,6},{3,11},{4,0},{5,13},{6,2},{7,15},{8,12},{9,1},{1... | collective-permute-start | bytes 196616 | tf_op jit(solution)/shard_map/ppermute | solution.py:299
  75.0 4.1 %collective-permute-start.25 = (f32[64,128]{1,0:T(8,128)S(1)}, f32[64,128]{1,0:T(8,128)S(1)}, u32[]{:S(2)}, u32[]{:S(2)}) collective-permute-start(f32[64,128]{1,0:T(8,128)S(1)} %get-tuple-element.90), channel_id=1, source_target_pairs={{0,3},{1,2},{2,1},{3,0},{4,7},{5,6},{6,5},{7,4},{8,11},{9,10},{10,... | collective-permute-start | bytes 98312 | tf_op jit(solution)/shard_map/ppermute | solution.py:340
  75.1 4.0 %collective-permute-start.26 = (f32[64,128]{1,0:T(8,128)S(1)}, f32[64,128]{1,0:T(8,128)S(1)}, u32[]{:S(2)}, u32[]{:S(2)}) collective-permute-start(f32[64,128]{1,0:T(8,128)S(1)} %get-tuple-element.91), channel_id=1, source_target_pairs={{0,2},{1,3},{2,0},{3,1},{4,6},{5,7},{6,4},{7,5},{8,10},{9,11},{10,... | collective-permute-start | bytes 98312 | tf_op jit(solution)/shard_map/ppermute | solution.py:340
  79.3 5.5 %collective-permute-start.28 = (f32[64,128]{1,0:T(8,128)S(1)}, f32[64,128]{1,0:T(8,128)S(1)}, u32[]{:S(2)}, u32[]{:S(2)}) collective-permute-start(f32[64,128]{1,0:T(8,128)S(1)} %solve_up.8.refs_0_.refs_4_), channel_id=1, source_target_pairs={{0,16},{4,20},{8,24},{12,28},{16,0},{20,4},{24,8},{28,12},{1,17},{... | collective-permute-start | bytes 98312 | tf_op jit(solution)/shard_map/ppermute | solution.py:284
  84.8 4.3 %collective-permute-start.30 = (f32[2,64,128]{2,1,0:T(8,128)S(1)}, f32[2,64,128]{2,1,0:T(8,128)S(1)}, u32[]{:S(2)}, u32[]{:S(2)}) collective-permute-start(f32[2,64,128]{2,1,0:T(8,128)S(1)} %combine.19.refs_0_), channel_id=1, source_target_pairs={{0,8},{1,5},{2,10},{3,7},{4,12},{5,1},{6,14},{7,3},{8,0},{9,13},{1... | collective-permute-start | bytes 196616 | tf_op jit(solution)/shard_map/ppermute | solution.py:299
  85.1 5.5 %collective-permute-start.29 = (f32[2,64,128]{2,1,0:T(8,128)S(1)}, f32[2,64,128]{2,1,0:T(8,128)S(1)}, u32[]{:S(2)}, u32[]{:S(2)}) collective-permute-start(f32[2,64,128]{2,1,0:T(8,128)S(1)} %combine.19.refs_0_), channel_id=1, source_target_pairs={{0,4},{1,9},{2,6},{3,11},{4,0},{5,13},{6,2},{7,15},{8,12},{9,1},{1... | collective-permute-start | bytes 196616 | tf_op jit(solution)/shard_map/ppermute | solution.py:299
  89.0 4.3 %collective-permute-start.31 = (f32[2,64,128]{2,1,0:T(8,128)S(1)}, f32[2,64,128]{2,1,0:T(8,128)S(1)}, u32[]{:S(2)}, u32[]{:S(2)}) collective-permute-start(f32[2,64,128]{2,1,0:T(8,128)S(1)} %collective-permute-done.30.refs_2_), channel_id=1, source_target_pairs={{0,4},{1,9},{2,6},{3,11},{4,0},{5,13},{6,2},{7,15},{8,12},{9,1},{1... | collective-permute-start | bytes 196616 | tf_op jit(solution)/shard_map/ppermute | solution.py:299
  93.7 3.6 %collective-permute-start.32 = (f32[64,128]{1,0:T(8,128)S(1)}, f32[64,128]{1,0:T(8,128)S(1)}, u32[]{:S(2)}, u32[]{:S(2)}) collective-permute-start(f32[64,128]{1,0:T(8,128)S(1)} %get-tuple-element.97), channel_id=1, source_target_pairs={{0,3},{1,2},{2,1},{3,0},{4,7},{5,6},{6,5},{7,4},{8,11},{9,10},{10,... | collective-permute-start | bytes 98312 | tf_op jit(solution)/shard_map/ppermute | solution.py:340
  93.8 4.4 %collective-permute-start.33 = (f32[64,128]{1,0:T(8,128)S(1)}, f32[64,128]{1,0:T(8,128)S(1)}, u32[]{:S(2)}, u32[]{:S(2)}) collective-permute-start(f32[64,128]{1,0:T(8,128)S(1)} %get-tuple-element.98), channel_id=1, source_target_pairs={{0,2},{1,3},{2,0},{3,1},{4,6},{5,7},{6,4},{7,5},{8,10},{9,11},{10,... | collective-permute-start | bytes 98312 | tf_op jit(solution)/shard_map/ppermute | solution.py:340
  98.5 3.4 %collective-permute-start.37 = (f32[64,128]{1,0:T(8,128)S(1)}, f32[64,128]{1,0:T(8,128)S(1)}, u32[]{:S(2)}, u32[]{:S(2)}) collective-permute-start(f32[64,128]{1,0:T(8,128)S(1)} %solve_down.6.refs_0_.refs_5_), channel_id=1, source_target_pairs={{0,3},{1,2},{2,1},{3,0},{4,7},{5,6},{6,5},{7,4},{8,11},{9,10},{10,... | collective-permute-start | bytes 98312 | tf_op jit(solution)/shard_map/ppermute | solution.py:340
  99.9 3.9 %collective-permute-start.36 = (f32[64,128]{1,0:T(8,128)S(1)}, f32[64,128]{1,0:T(8,128)S(1)}, u32[]{:S(2)}, u32[]{:S(2)}) collective-permute-start(f32[64,128]{1,0:T(8,128)S(1)} %solve_down.6.refs_0_.refs_5_), channel_id=1, source_target_pairs={{0,2},{1,3},{2,0},{3,1},{4,6},{5,7},{6,4},{7,5},{8,10},{9,11},{10,... | collective-permute-start | bytes 98312 | tf_op jit(solution)/shard_map/ppermute | solution.py:340
  104.1 4.3 %collective-permute-start.39 = (f32[2,64,128]{2,1,0:T(8,128)S(1)}, f32[2,64,128]{2,1,0:T(8,128)S(1)}, u32[]{:S(2)}, u32[]{:S(2)}) collective-permute-start(f32[2,64,128]{2,1,0:T(8,128)S(1)} %couple.31), channel_id=1, source_target_pairs={{0,4},{1,9},{2,6},{3,11},{4,0},{5,13},{6,2},{7,15},{8,12},{9,1},{1... | collective-permute-start | bytes 196616 | tf_op jit(solution)/shard_map/ppermute | solution.py:299
  105.0 4.3 %collective-permute-start.38 = (f32[2,64,128]{2,1,0:T(8,128)S(1)}, f32[2,64,128]{2,1,0:T(8,128)S(1)}, u32[]{:S(2)}, u32[]{:S(2)}) collective-permute-start(f32[2,64,128]{2,1,0:T(8,128)S(1)} %get-tuple-element.108), channel_id=1, source_target_pairs={{0,4},{1,9},{2,6},{3,11},{4,0},{5,13},{6,2},{7,15},{8,12},{9,1},{1... | collective-permute-start | bytes 196616 | tf_op jit(solution)/shard_map/ppermute | solution.py:299
  108.4 4.3 %collective-permute-start.40 = (f32[2,64,128]{2,1,0:T(8,128)S(1)}, f32[2,64,128]{2,1,0:T(8,128)S(1)}, u32[]{:S(2)}, u32[]{:S(2)}) collective-permute-start(f32[2,64,128]{2,1,0:T(8,128)S(1)} %combine.20), channel_id=1, source_target_pairs={{0,8},{1,5},{2,10},{3,7},{4,12},{5,1},{6,14},{7,3},{8,0},{9,13},{1... | collective-permute-start | bytes 196616 | tf_op jit(solution)/shard_map/ppermute | solution.py:299
  112.8 5.0 %collective-permute-start.41 = (f32[64,128]{1,0:T(8,128)S(1)}, f32[64,128]{1,0:T(8,128)S(1)}, u32[]{:S(2)}, u32[]{:S(2)}) collective-permute-start(f32[64,128]{1,0:T(8,128)S(1)} %get-tuple-element.111), channel_id=1, source_target_pairs={{0,16},{4,20},{8,24},{12,28},{16,0},{20,4},{24,8},{28,12},{1,17},{... | collective-permute-start | bytes 98312 | tf_op jit(solution)/shard_map/ppermute | solution.py:284
  118.9 3.4 %collective-permute-start.44 = (f32[64,128]{1,0:T(8,128)S(1)}, f32[64,128]{1,0:T(8,128)S(1)}, u32[]{:S(2)}, u32[]{:S(2)}) collective-permute-start(f32[64,128]{1,0:T(8,128)S(1)} %solve_down.7.refs_0_.refs_4_), channel_id=1, source_target_pairs={{0,3},{1,2},{2,1},{3,0},{4,7},{5,6},{6,5},{7,4},{8,11},{9,10},{10,... | collective-permute-start | bytes 98312 | tf_op jit(solution)/shard_map/ppermute | solution.py:340
  118.9 4.3 %collective-permute-start.43 = (f32[64,128]{1,0:T(8,128)S(1)}, f32[64,128]{1,0:T(8,128)S(1)}, u32[]{:S(2)}, u32[]{:S(2)}) collective-permute-start(f32[64,128]{1,0:T(8,128)S(1)} %solve_down.7.refs_0_.refs_4_), channel_id=1, source_target_pairs={{0,2},{1,3},{2,0},{3,1},{4,6},{5,7},{6,4},{7,5},{8,10},{9,11},{10,... | collective-permute-start | bytes 98312 | tf_op jit(solution)/shard_map/ppermute | solution.py:340
  119.9 3.3 %collective-permute-start.42 = (f32[64,128]{1,0:T(8,128)S(1)}, f32[64,128]{1,0:T(8,128)S(1)}, u32[]{:S(2)}, u32[]{:S(2)}) collective-permute-start(f32[64,128]{1,0:T(8,128)S(1)} %solve_down.7.refs_0_.refs_4_), channel_id=1, source_target_pairs={{0,1},{1,0},{2,3},{3,2},{4,5},{5,4},{6,7},{7,6},{8,9},{9,8},{10,11... | collective-permute-start | bytes 98312 | tf_op jit(solution)/shard_map/ppermute | solution.py:340
  123.5 4.3 %collective-permute-start.46 = (f32[2,64,128]{2,1,0:T(8,128)S(1)}, f32[2,64,128]{2,1,0:T(8,128)S(1)}, u32[]{:S(2)}, u32[]{:S(2)}) collective-permute-start(f32[2,64,128]{2,1,0:T(8,128)S(1)} %couple.33), channel_id=1, source_target_pairs={{0,4},{1,9},{2,6},{3,11},{4,0},{5,13},{6,2},{7,15},{8,12},{9,1},{1... | collective-permute-start | bytes 196616 | tf_op jit(solution)/shard_map/ppermute | solution.py:299
  124.6 4.3 %collective-permute-start.45 = (f32[2,64,128]{2,1,0:T(8,128)S(1)}, f32[2,64,128]{2,1,0:T(8,128)S(1)}, u32[]{:S(2)}, u32[]{:S(2)}) collective-permute-start(f32[2,64,128]{2,1,0:T(8,128)S(1)} %get-tuple-element.113), channel_id=1, source_target_pairs={{0,4},{1,9},{2,6},{3,11},{4,0},{5,13},{6,2},{7,15},{8,12},{9,1},{1... | collective-permute-start | bytes 196616 | tf_op jit(solution)/shard_map/ppermute | solution.py:299
  127.8 4.3 %collective-permute-start.47 = (f32[2,64,128]{2,1,0:T(8,128)S(1)}, f32[2,64,128]{2,1,0:T(8,128)S(1)}, u32[]{:S(2)}, u32[]{:S(2)}) collective-permute-start(f32[2,64,128]{2,1,0:T(8,128)S(1)} %combine.22), channel_id=1, source_target_pairs={{0,8},{1,5},{2,10},{3,7},{4,12},{5,1},{6,14},{7,3},{8,0},{9,13},{1... | collective-permute-start | bytes 196616 | tf_op jit(solution)/shard_map/ppermute | solution.py:299
  132.2 4.9 %collective-permute-start.48 = (f32[64,128]{1,0:T(8,128)S(1)}, f32[64,128]{1,0:T(8,128)S(1)}, u32[]{:S(2)}, u32[]{:S(2)}) collective-permute-start(f32[64,128]{1,0:T(8,128)S(1)} %get-tuple-element.116), channel_id=1, source_target_pairs={{0,16},{4,20},{8,24},{12,28},{16,0},{20,4},{24,8},{28,12},{1,17},{... | collective-permute-start | bytes 98312 | tf_op jit(solution)/shard_map/ppermute | solution.py:284
  137.2 3.4 %collective-permute-start.51 = (f32[64,128]{1,0:T(8,128)S(1)}, f32[64,128]{1,0:T(8,128)S(1)}, u32[]{:S(2)}, u32[]{:S(2)}) collective-permute-start(f32[64,128]{1,0:T(8,128)S(1)} %solve_down.8.refs_0_.refs_3_), channel_id=1, source_target_pairs={{0,3},{1,2},{2,1},{3,0},{4,7},{5,6},{6,5},{7,4},{8,11},{9,10},{10,... | collective-permute-start | bytes 98312 | tf_op jit(solution)/shard_map/ppermute | solution.py:340
  137.3 4.1 %collective-permute-start.50 = (f32[64,128]{1,0:T(8,128)S(1)}, f32[64,128]{1,0:T(8,128)S(1)}, u32[]{:S(2)}, u32[]{:S(2)}) collective-permute-start(f32[64,128]{1,0:T(8,128)S(1)} %solve_down.8.refs_0_.refs_3_), channel_id=1, source_target_pairs={{0,2},{1,3},{2,0},{3,1},{4,6},{5,7},{6,4},{7,5},{8,10},{9,11},{10,... | collective-permute-start | bytes 98312 | tf_op jit(solution)/shard_map/ppermute | solution.py:340
  138.1 3.3 %collective-permute-start.49 = (f32[64,128]{1,0:T(8,128)S(1)}, f32[64,128]{1,0:T(8,128)S(1)}, u32[]{:S(2)}, u32[]{:S(2)}) collective-permute-start(f32[64,128]{1,0:T(8,128)S(1)} %solve_down.8.refs_0_.refs_3_), channel_id=1, source_target_pairs={{0,1},{1,0},{2,3},{3,2},{4,5},{5,4},{6,7},{7,6},{8,9},{9,8},{10,11... | collective-permute-start | bytes 98312 | tf_op jit(solution)/shard_map/ppermute | solution.py:340
  141.7 4.3 %collective-permute-start.53 = (f32[2,64,128]{2,1,0:T(8,128)S(1)}, f32[2,64,128]{2,1,0:T(8,128)S(1)}, u32[]{:S(2)}, u32[]{:S(2)}) collective-permute-start(f32[2,64,128]{2,1,0:T(8,128)S(1)} %couple.35), channel_id=1, source_target_pairs={{0,4},{1,9},{2,6},{3,11},{4,0},{5,13},{6,2},{7,15},{8,12},{9,1},{1... | collective-permute-start | bytes 196616 | tf_op jit(solution)/shard_map/ppermute | solution.py:299
  143.3 4.6 %collective-permute-start.52 = (f32[2,64,128]{2,1,0:T(8,128)S(1)}, f32[2,64,128]{2,1,0:T(8,128)S(1)}, u32[]{:S(2)}, u32[]{:S(2)}) collective-permute-start(f32[2,64,128]{2,1,0:T(8,128)S(1)} %get-tuple-element.118), channel_id=1, source_target_pairs={{0,4},{1,9},{2,6},{3,11},{4,0},{5,13},{6,2},{7,15},{8,12},{9,1},{1... | collective-permute-start | bytes 196616 | tf_op jit(solution)/shard_map/ppermute | solution.py:299
  146.0 4.3 %collective-permute-start.54 = (f32[2,64,128]{2,1,0:T(8,128)S(1)}, f32[2,64,128]{2,1,0:T(8,128)S(1)}, u32[]{:S(2)}, u32[]{:S(2)}) collective-permute-start(f32[2,64,128]{2,1,0:T(8,128)S(1)} %combine.24), channel_id=1, source_target_pairs={{0,8},{1,5},{2,10},{3,7},{4,12},{5,1},{6,14},{7,3},{8,0},{9,13},{1... | collective-permute-start | bytes 196616 | tf_op jit(solution)/shard_map/ppermute | solution.py:299
  150.4 4.9 %collective-permute-start.55 = (f32[64,128]{1,0:T(8,128)S(1)}, f32[64,128]{1,0:T(8,128)S(1)}, u32[]{:S(2)}, u32[]{:S(2)}) collective-permute-start(f32[64,128]{1,0:T(8,128)S(1)} %get-tuple-element.121), channel_id=1, source_target_pairs={{0,16},{4,20},{8,24},{12,28},{16,0},{20,4},{24,8},{28,12},{1,17},{... | collective-permute-start | bytes 98312 | tf_op jit(solution)/shard_map/ppermute | solution.py:284
  155.4 3.4 %collective-permute-start.58 = (f32[64,128]{1,0:T(8,128)S(1)}, f32[64,128]{1,0:T(8,128)S(1)}, u32[]{:S(2)}, u32[]{:S(2)}) collective-permute-start(f32[64,128]{1,0:T(8,128)S(1)} %solve_down.9.refs_0_.refs_2_), channel_id=1, source_target_pairs={{0,3},{1,2},{2,1},{3,0},{4,7},{5,6},{6,5},{7,4},{8,11},{9,10},{10,... | collective-permute-start | bytes 98312 | tf_op jit(solution)/shard_map/ppermute | solution.py:340
  155.5 4.0 %collective-permute-start.57 = (f32[64,128]{1,0:T(8,128)S(1)}, f32[64,128]{1,0:T(8,128)S(1)}, u32[]{:S(2)}, u32[]{:S(2)}) collective-permute-start(f32[64,128]{1,0:T(8,128)S(1)} %solve_down.9.refs_0_.refs_2_), channel_id=1, source_target_pairs={{0,2},{1,3},{2,0},{3,1},{4,6},{5,7},{6,4},{7,5},{8,10},{9,11},{10,... | collective-permute-start | bytes 98312 | tf_op jit(solution)/shard_map/ppermute | solution.py:340
  156.1 3.4 %collective-permute-start.56 = (f32[64,128]{1,0:T(8,128)S(1)}, f32[64,128]{1,0:T(8,128)S(1)}, u32[]{:S(2)}, u32[]{:S(2)}) collective-permute-start(f32[64,128]{1,0:T(8,128)S(1)} %solve_down.9.refs_0_.refs_2_), channel_id=1, source_target_pairs={{0,1},{1,0},{2,3},{3,2},{4,5},{5,4},{6,7},{7,6},{8,9},{9,8},{10,11... | collective-permute-start | bytes 98312 | tf_op jit(solution)/shard_map/ppermute | solution.py:340
  159.8 4.3 %collective-permute-start.60 = (f32[2,64,128]{2,1,0:T(8,128)S(1)}, f32[2,64,128]{2,1,0:T(8,128)S(1)}, u32[]{:S(2)}, u32[]{:S(2)}) collective-permute-start(f32[2,64,128]{2,1,0:T(8,128)S(1)} %couple.37), channel_id=1, source_target_pairs={{0,4},{1,9},{2,6},{3,11},{4,0},{5,13},{6,2},{7,15},{8,12},{9,1},{1... | collective-permute-start | bytes 196616 | tf_op jit(solution)/shard_map/ppermute | solution.py:299
  161.5 4.7 %collective-permute-start.59 = (f32[2,64,128]{2,1,0:T(8,128)S(1)}, f32[2,64,128]{2,1,0:T(8,128)S(1)}, u32[]{:S(2)}, u32[]{:S(2)}) collective-permute-start(f32[2,64,128]{2,1,0:T(8,128)S(1)} %get-tuple-element.123), channel_id=1, source_target_pairs={{0,4},{1,9},{2,6},{3,11},{4,0},{5,13},{6,2},{7,15},{8,12},{9,1},{1... | collective-permute-start | bytes 196616 | tf_op jit(solution)/shard_map/ppermute | solution.py:299
  164.1 4.3 %collective-permute-start.61 = (f32[2,64,128]{2,1,0:T(8,128)S(1)}, f32[2,64,128]{2,1,0:T(8,128)S(1)}, u32[]{:S(2)}, u32[]{:S(2)}) collective-permute-start(f32[2,64,128]{2,1,0:T(8,128)S(1)} %combine.26), channel_id=1, source_target_pairs={{0,8},{1,5},{2,10},{3,7},{4,12},{5,1},{6,14},{7,3},{8,0},{9,13},{1... | collective-permute-start | bytes 196616 | tf_op jit(solution)/shard_map/ppermute | solution.py:299
  168.5 4.9 %collective-permute-start.62 = (f32[64,128]{1,0:T(8,128)S(1)}, f32[64,128]{1,0:T(8,128)S(1)}, u32[]{:S(2)}, u32[]{:S(2)}) collective-permute-start(f32[64,128]{1,0:T(8,128)S(1)} %get-tuple-element.126), channel_id=1, source_target_pairs={{0,16},{4,20},{8,24},{12,28},{16,0},{20,4},{24,8},{28,12},{1,17},{... | collective-permute-start | bytes 98312 | tf_op jit(solution)/shard_map/ppermute | solution.py:284
  173.5 3.4 %collective-permute-start.65 = (f32[64,128]{1,0:T(8,128)S(1)}, f32[64,128]{1,0:T(8,128)S(1)}, u32[]{:S(2)}, u32[]{:S(2)}) collective-permute-start(f32[64,128]{1,0:T(8,128)S(1)} %solve_down.10.refs_0_.refs_1_), channel_id=1, source_target_pairs={{0,3},{1,2},{2,1},{3,0},{4,7},{5,6},{6,5},{7,4},{8,11},{9,10},{10,... | collective-permute-start | bytes 98312 | tf_op jit(solution)/shard_map/ppermute | solution.py:340
  173.6 4.0 %collective-permute-start.64 = (f32[64,128]{1,0:T(8,128)S(1)}, f32[64,128]{1,0:T(8,128)S(1)}, u32[]{:S(2)}, u32[]{:S(2)}) collective-permute-start(f32[64,128]{1,0:T(8,128)S(1)} %solve_down.10.refs_0_.refs_1_), channel_id=1, source_target_pairs={{0,2},{1,3},{2,0},{3,1},{4,6},{5,7},{6,4},{7,5},{8,10},{9,11},{10,... | collective-permute-start | bytes 98312 | tf_op jit(solution)/shard_map/ppermute | solution.py:340
  174.3 3.4 %collective-permute-start.63 = (f32[64,128]{1,0:T(8,128)S(1)}, f32[64,128]{1,0:T(8,128)S(1)}, u32[]{:S(2)}, u32[]{:S(2)}) collective-permute-start(f32[64,128]{1,0:T(8,128)S(1)} %solve_down.10.refs_0_.refs_1_), channel_id=1, source_target_pairs={{0,1},{1,0},{2,3},{3,2},{4,5},{5,4},{6,7},{7,6},{8,9},{9,8},{10,11... | collective-permute-start | bytes 98312 | tf_op jit(solution)/shard_map/ppermute | solution.py:340
  177.9 4.3 %collective-permute-start.67 = (f32[2,64,128]{2,1,0:T(8,128)S(1)}, f32[2,64,128]{2,1,0:T(8,128)S(1)}, u32[]{:S(2)}, u32[]{:S(2)}) collective-permute-start(f32[2,64,128]{2,1,0:T(8,128)S(1)} %couple.39), channel_id=1, source_target_pairs={{0,4},{1,9},{2,6},{3,11},{4,0},{5,13},{6,2},{7,15},{8,12},{9,1},{1... | collective-permute-start | bytes 196616 | tf_op jit(solution)/shard_map/ppermute | solution.py:299
  179.6 4.7 %collective-permute-start.66 = (f32[2,64,128]{2,1,0:T(8,128)S(1)}, f32[2,64,128]{2,1,0:T(8,128)S(1)}, u32[]{:S(2)}, u32[]{:S(2)}) collective-permute-start(f32[2,64,128]{2,1,0:T(8,128)S(1)} %get-tuple-element.128), channel_id=1, source_target_pairs={{0,4},{1,9},{2,6},{3,11},{4,0},{5,13},{6,2},{7,15},{8,12},{9,1},{1... | collective-permute-start | bytes 196616 | tf_op jit(solution)/shard_map/ppermute | solution.py:299
  182.2 4.3 %collective-permute-start.68 = (f32[2,64,128]{2,1,0:T(8,128)S(1)}, f32[2,64,128]{2,1,0:T(8,128)S(1)}, u32[]{:S(2)}, u32[]{:S(2)}) collective-permute-start(f32[2,64,128]{2,1,0:T(8,128)S(1)} %combine.28), channel_id=1, source_target_pairs={{0,8},{1,5},{2,10},{3,7},{4,12},{5,1},{6,14},{7,3},{8,0},{9,13},{1... | collective-permute-start | bytes 196616 | tf_op jit(solution)/shard_map/ppermute | solution.py:299
  186.6 4.9 %collective-permute-start.69 = (f32[64,128]{1,0:T(8,128)S(1)}, f32[64,128]{1,0:T(8,128)S(1)}, u32[]{:S(2)}, u32[]{:S(2)}) collective-permute-start(f32[64,128]{1,0:T(8,128)S(1)} %get-tuple-element.131), channel_id=1, source_target_pairs={{0,16},{4,20},{8,24},{12,28},{16,0},{20,4},{24,8},{28,12},{1,17},{... | collective-permute-start | bytes 98312 | tf_op jit(solution)/shard_map/ppermute | solution.py:284
  (13 other events, 60.6 us)

commit v11 on v9

--- a/solution.py
+++ b/solution.py
@@ -50,7 +50,7 @@
         pl.when(lax.rem(slot, chunk) == 0)(fetch(slot // chunk).wait)
         source = slots_ref[level, slot_count + slot]
         near = lax.rem(source, half) ^ lax.rem(row, half)
-        near = jnp.where(lax.rem(col, 2) == 1, mirrored(near, half), near)
+        near = jnp.where(lax.rem(col, 2) == 1, lax.rem(half - near, half), near)
         below = near * 2 + ((source // half) ^ side)
         above = slots_ref[level, slot] ^ col
         total[below * n_col + above] += slots[slot]
@@ -285,8 +285,7 @@
 
 
 def mirrored(number, size):
-    bits = size.bit_length() - 1
-    return sum(((number >> bit) & 1) << (bits - 1 - bit) for bit in range(bits))
+    return (size - number) % size
 
 
 def near_exchange(messages):

time: 176 us -> 177 us (level)
    ppermute x10, starting transfers between devices: 8.01 us -> 9.78 us  [far_exchange(): lax.ppermute(segment, axis, [(i, i ^ size // 2) for i in range(size)])]
where the time goes in v11:
time: 177 us; the launch traced here: 176 us
  waiting for transfers between devices  82.2 us (46%)
  starting transfers between devices  64.6 us (36%)
  Pallas kernels  26 us (15%)
  local copies, waits for them, and re-layouts  2.48 us (1%)
    ppermute x10, waiting for transfers between devices, far_exchange(): lax.ppermute(segment, axis, [(i, i ^ size // 2) for i in range(size)])  35.6 us
    ppermute x30, starting transfers between devices, near_exchange(): received[d] = lax.ppermute(messages[d], ('row', 'col'), pairs)  35.3 us
    ppermute x30, waiting for transfers between devices, near_exchange(): received[d] = lax.ppermute(messages[d], ('row', 'col'), pairs)  31.8 us
    ppermute x30, starting transfers between devices, exchange_each(): lax.ppermute(messages[d], axis, [(i, i ^ d) for i in range(size)])  19.5 us
    ppermute x30, waiting for transfers between devices, exchange_each(): lax.ppermute(messages[d], axis, [(i, i ^ d) for i in range(size)])  14.8 us
    ppermute x10, starting transfers between devices, far_exchange(): lax.ppermute(segment, axis, [(i, i ^ size // 2) for i in range(size)])  9.78 us
    pallas_call x5, Pallas kernels, gather_blocks(): pl.pallas_call(functools.partial(gather_blocks_kernel, n_row, n_col, leve...  7.88 us
    pallas_call x20, Pallas kernels, couple(): pl.pallas_call(functools.partial(couple_kernel, terms, span), out_shape=[...  7.87 us
  transfers between devices with their start and end apart: 70, of which 53 were waited for; matrix products, arithmetic and copies ran while one was open for 1% of the time, Pallas kernels for 10%

profile of v11, /device:TPU:0, one launch (start us, length us, event | category | flops | bytes accessed | tf_op | source)
XLA Modules:
  0.0 176.4 jit_solution(1818706150702375564)
XLA Ops:
  0.6 1.7 first_solve.1.refs_0_
  2.3 4.1 %collective-permute-start = (f32[64,128]{1,0:T(8,128)}, f32[64,128]{1,0:T(8,128)S(1)}, u32[]{:S(2)}, u32[]{:S(2)}) collective-permute-start(f32[64,128]{1,0:T(8,128)} %first_solve.1.refs_0_), channel_id=1, source_target_pairs={{0,16},{4,20},{8,24},{12,28},{16,0},{20,4},{24,8},{28,12},{1,17},{... | collective-permute-start | bytes 98312 | tf_op jit(solution)/shard_map/ppermute | solution.py:284
  7.9 2.5 %gather_blocks_0.1.total_ref = f32[32,128,128]{2,1,0:T(8,128)S(1)} custom-call(s32[5,67]{1,0:T(8,128)S(1)} %concatenate.3.slots_ref, f32[5,32,128,128]{3,2,1,0:T(8,128)} %bitcast.14), custom_call_target="tpu_custom_call" | custom-call | flops 524288 | bytes 4194304 | tf_op jit(solution)/shard_map/gather_blocks_0/pallas_call | solution.py:67
  10.8 2.6 %collective-permute-start.3 = (f32[2,64,128]{2,1,0:T(8,128)S(1)}, f32[2,64,128]{2,1,0:T(8,128)S(1)}, u32[]{:S(2)}, u32[]{:S(2)}) collective-permute-start(f32[2,64,128]{2,1,0:T(8,128)S(1)} %combine.10.refs_0_), channel_id=1, source_target_pairs={{0,12},{1,5},{2,14},{3,7},{4,8},{5,1},{6,10},{7,3},{8,4},{9,13},{1... | collective-permute-start | bytes 196616 | tf_op jit(solution)/shard_map/ppermute | solution.py:301
  14.4 1.7 collective-permute-done.3.refs_3_
  16.0 1.6 collective-permute-done.2.refs_2_
  19.0 1.2 collective-permute-start.5
  20.8 1.1 gather_blocks_1.1.refs_6_.total_ref
  21.9 1.2 collective-permute-done.5.refs_3_
  24.6 4.1 %collective-permute-done.7.refs_1_ = f32[64,128]{1,0:T(8,128)S(1)} collective-permute-done((f32[64,128]{1,0:T(8,128)S(1)}, f32[64,128]{1,0:T(8,128)S(1)}, u32[]{:S(2)}, u32[]{:S(2)}) %collective-permute-start.7) | collective-permute-done | bytes 32800 | tf_op jit(solution)/shard_map/ppermute | solution.py:284
  29.1 1.5 collective-permute-start.9
  30.6 1.6 collective-permute-start.8
  32.2 1.7 collective-permute-done.10.refs_3_
  36.6 1.1 collective-permute-start.13
  37.7 1.1 gather_blocks_2.1.refs_6_.total_ref
  40.8 3.9 %collective-permute-done.14.refs_1_ = f32[64,128]{1,0:T(8,128)S(1)} collective-permute-done((f32[64,128]{1,0:T(8,128)S(1)}, f32[64,128]{1,0:T(8,128)S(1)}, u32[]{:S(2)}, u32[]{:S(2)}) %collective-permute-start.14) | collective-permute-done | bytes 32800 | tf_op jit(solution)/shard_map/ppermute | solution.py:284
  44.7 1.2 collective-permute-start.17
  46.0 1.8 %collective-permute-start.16 = (f32[2,64,128]{2,1,0:T(8,128)S(1)}, f32[2,64,128]{2,1,0:T(8,128)S(1)}, u32[]{:S(2)}, u32[]{:S(2)}) collective-permute-start(f32[2,64,128]{2,1,0:T(8,128)S(1)} %combine.12.refs_0_), channel_id=1, source_target_pairs={{0,8},{1,9},{2,10},{3,11},{4,12},{5,13},{6,14},{7,15},{8,0},{9,1},... | collective-permute-start | bytes 196616 | tf_op jit(solution)/shard_map/ppermute | solution.py:301
  48.2 2.0 %collective-permute-done.17.refs_3_ = f32[2,64,128]{2,1,0:T(8,128)S(1)} collective-permute-done((f32[2,64,128]{2,1,0:T(8,128)S(1)}, f32[2,64,128]{2,1,0:T(8,128)S(1)}, u32[]{:S(2)}, u32[]{:S(2)}) %collective-permute-start.17) | collective-permute-done | bytes 65568 | tf_op jit(solution)/shard_map/ppermute | solution.py:301
  50.7 1.3 collective-permute-done.15.refs_1_
  53.6 1.3 collective-permute-start.20
  54.8 1.1 gather_blocks_3.1.refs_6_.total_ref
  57.9 3.9 %collective-permute-done.21.refs_1_ = f32[64,128]{1,0:T(8,128)S(1)} collective-permute-done((f32[64,128]{1,0:T(8,128)S(1)}, f32[64,128]{1,0:T(8,128)S(1)}, u32[]{:S(2)}, u32[]{:S(2)}) %collective-permute-start.21) | collective-permute-done | bytes 32800 | tf_op jit(solution)/shard_map/ppermute | solution.py:284
  61.8 1.8 collective-permute-start.23
  63.5 1.7 collective-permute-start.22
  65.3 1.7 collective-permute-done.24.refs_3_
  69.3 1.3 collective-permute-start.27
  70.6 2.0 %gather_blocks_4.1.refs_6_.total_ref = f32[32,128,128]{2,1,0:T(8,128)S(1)} custom-call(s32[5,67]{1,0:T(8,128)S(1)} %concatenate.3.slots_ref, f32[5,32,128,128]{3,2,1,0:T(8,128)S(1)} %bitcast.20, f32[64,128]{1,0:T(8,128)S(1)} %get-tuple-element.93.refs_0_.refs_5_), custom_call_target="tpu_custom_call" | custom-call | flops 524288 | bytes 4194304 | tf_op jit(solution)/shard_map/gather_blocks_4/pallas_call | solution.py:67
  74.3 3.4 %collective-permute-done.28.refs_1_ = f32[64,128]{1,0:T(8,128)S(1)} collective-permute-done((f32[64,128]{1,0:T(8,128)S(1)}, f32[64,128]{1,0:T(8,128)S(1)}, u32[]{:S(2)}, u32[]{:S(2)}) %collective-permute-start.28) | collective-permute-done | bytes 32800 | tf_op jit(solution)/shard_map/ppermute | solution.py:284
  77.7 1.1 collective-permute-start.31
  78.8 1.8 %collective-permute-start.30 = (f32[2,64,128]{2,1,0:T(8,128)S(1)}, f32[2,64,128]{2,1,0:T(8,128)S(1)}, u32[]{:S(2)}, u32[]{:S(2)}) collective-permute-start(f32[2,64,128]{2,1,0:T(8,128)S(1)} %combine.14.refs_0_), channel_id=1, source_target_pairs={{0,8},{1,9},{2,10},{3,11},{4,12},{5,13},{6,14},{7,15},{8,0},{9,1},... | collective-permute-start | bytes 196616 | tf_op jit(solution)/shard_map/ppermute | solution.py:301
  81.2 1.8 %collective-permute-done.31.refs_3_ = f32[2,64,128]{2,1,0:T(8,128)S(1)} collective-permute-done((f32[2,64,128]{2,1,0:T(8,128)S(1)}, f32[2,64,128]{2,1,0:T(8,128)S(1)}, u32[]{:S(2)}, u32[]{:S(2)}) %collective-permute-start.31) | collective-permute-done | bytes 65568 | tf_op jit(solution)/shard_map/ppermute | solution.py:301
  83.5 1.3 collective-permute-done.29.refs_1_
  86.3 1.3 collective-permute-start.34
  91.6 1.8 %collective-permute-done.37.refs_3_ = f32[64,128]{1,0:T(8,128)S(1)} collective-permute-done((f32[64,128]{1,0:T(8,128)S(1)}, f32[64,128]{1,0:T(8,128)S(1)}, u32[]{:S(2)}, u32[]{:S(2)}) %collective-permute-start.37) | collective-permute-done | bytes 32800 | tf_op jit(solution)/shard_map/ppermute | solution.py:328
  95.4 1.4 collective-permute-start.39
  96.8 1.4 collective-permute-start.40
  98.5 1.6 collective-permute-done.38.refs_1_
  102.7 3.6 %collective-permute-done.41.refs_3_ = f32[64,128]{1,0:T(8,128)S(1)} collective-permute-done((f32[64,128]{1,0:T(8,128)S(1)}, f32[64,128]{1,0:T(8,128)S(1)}, u32[]{:S(2)}, u32[]{:S(2)}) %collective-permute-start.41) | collective-permute-done | bytes 32800 | tf_op jit(solution)/shard_map/ppermute | solution.py:284
  108.3 1.0 collective-permute-start.42
  109.4 1.5 collective-permute-done.44.refs_3_
  112.2 1.5 collective-permute-start.45
  113.7 1.5 collective-permute-start.46
  116.0 1.6 collective-permute-done.45.refs_1_
  117.6 1.4 collective-permute-done.46.refs_2_
  120.3 4.1 %collective-permute-done.48.refs_3_ = f32[64,128]{1,0:T(8,128)S(1)} collective-permute-done((f32[64,128]{1,0:T(8,128)S(1)}, f32[64,128]{1,0:T(8,128)S(1)}, u32[]{:S(2)}, u32[]{:S(2)}) %collective-permute-start.48) | collective-permute-done | bytes 32800 | tf_op jit(solution)/shard_map/ppermute | solution.py:284
  124.6 1.2 collective-permute-start.50
  126.5 1.5 collective-permute-done.51.refs_3_
  130.3 1.8 %collective-permute-start.53 = (f32[2,64,128]{2,1,0:T(8,128)S(1)}, f32[2,64,128]{2,1,0:T(8,128)S(1)}, u32[]{:S(2)}, u32[]{:S(2)}) collective-permute-start(f32[2,64,128]{2,1,0:T(8,128)S(1)} %get-tuple-element.118), channel_id=1, source_target_pairs={{0,8},{1,9},{2,10},{3,11},{4,12},{5,13},{6,14},{7,15},{8,0},{9,1},... | collective-permute-start | bytes 196616 | tf_op jit(solution)/shard_map/ppermute | solution.py:301
  133.1 2.1 %collective-permute-done.52.refs_1_ = f32[2,64,128]{2,1,0:T(8,128)S(1)} collective-permute-done((f32[2,64,128]{2,1,0:T(8,128)S(1)}, f32[2,64,128]{2,1,0:T(8,128)S(1)}, u32[]{:S(2)}, u32[]{:S(2)}) %collective-permute-start.52) | collective-permute-done | bytes 65568 | tf_op jit(solution)/shard_map/ppermute | solution.py:301
  136.4 1.1 collective-permute-start.55
  137.5 4.1 %collective-permute-done.55.refs_3_ = f32[64,128]{1,0:T(8,128)S(1)} collective-permute-done((f32[64,128]{1,0:T(8,128)S(1)}, f32[64,128]{1,0:T(8,128)S(1)}, u32[]{:S(2)}, u32[]{:S(2)}) %collective-permute-start.55) | collective-permute-done | bytes 32800 | tf_op jit(solution)/shard_map/ppermute | solution.py:284
  141.9 1.3 collective-permute-start.57
  143.7 1.6 collective-permute-done.58.refs_3_
  146.4 1.2 collective-permute-start.59
  147.6 1.4 collective-permute-start.60
  150.2 2.0 %collective-permute-done.59.refs_1_ = f32[2,64,128]{2,1,0:T(8,128)S(1)} collective-permute-done((f32[2,64,128]{2,1,0:T(8,128)S(1)}, f32[2,64,128]{2,1,0:T(8,128)S(1)}, u32[]{:S(2)}, u32[]{:S(2)}) %collective-permute-start.59) | collective-permute-done | bytes 65568 | tf_op jit(solution)/shard_map/ppermute | solution.py:301
  154.4 4.2 %collective-permute-done.62.refs_3_ = f32[64,128]{1,0:T(8,128)S(1)} collective-permute-done((f32[64,128]{1,0:T(8,128)S(1)}, f32[64,128]{1,0:T(8,128)S(1)}, u32[]{:S(2)}, u32[]{:S(2)}) %collective-permute-start.62) | collective-permute-done | bytes 32800 | tf_op jit(solution)/shard_map/ppermute | solution.py:284
  158.8 1.3 collective-permute-start.64
  160.7 1.7 collective-permute-done.65.refs_3_
  163.3 1.1 collective-permute-start.66
  164.5 1.4 collective-permute-start.67
  167.2 2.0 %collective-permute-done.66.refs_1_ = f32[2,64,128]{2,1,0:T(8,128)S(1)} collective-permute-done((f32[2,64,128]{2,1,0:T(8,128)S(1)}, f32[2,64,128]{2,1,0:T(8,128)S(1)}, u32[]{:S(2)}, u32[]{:S(2)}) %collective-permute-start.66) | collective-permute-done | bytes 65568 | tf_op jit(solution)/shard_map/ppermute | solution.py:301
  171.2 4.3 %collective-permute-done.69.refs_3_ = f32[64,128]{1,0:T(8,128)S(1)} collective-permute-done((f32[64,128]{1,0:T(8,128)S(1)}, f32[64,128]{1,0:T(8,128)S(1)}, u32[]{:S(2)}, u32[]{:S(2)}) %collective-permute-start.69) | collective-permute-done | bytes 32800 | tf_op jit(solution)/shard_map/ppermute | solution.py:284
  (155 shorter events, 53.1 us)
Async XLA Ops:
  2.3 8.5 %collective-permute-start = (f32[64,128]{1,0:T(8,128)}, f32[64,128]{1,0:T(8,128)S(1)}, u32[]{:S(2)}, u32[]{:S(2)}) collective-permute-start(f32[64,128]{1,0:T(8,128)} %first_solve.1.refs_0_), channel_id=1, source_target_pairs={{0,16},{4,20},{8,24},{12,28},{16,0},{20,4},{24,8},{28,12},{1,17},{... | collective-permute-start | bytes 98312 | tf_op jit(solution)/shard_map/ppermute | solution.py:284
  10.8 5.2 %collective-permute-start.3 = (f32[2,64,128]{2,1,0:T(8,128)S(1)}, f32[2,64,128]{2,1,0:T(8,128)S(1)}, u32[]{:S(2)}, u32[]{:S(2)}) collective-permute-start(f32[2,64,128]{2,1,0:T(8,128)S(1)} %combine.10.refs_0_), channel_id=1, source_target_pairs={{0,12},{1,5},{2,14},{3,7},{4,8},{5,1},{6,10},{7,3},{8,4},{9,13},{1... | collective-permute-start | bytes 196616 | tf_op jit(solution)/shard_map/ppermute | solution.py:301
  13.4 4.3 %collective-permute-start.2 = (f32[2,64,128]{2,1,0:T(8,128)S(1)}, f32[2,64,128]{2,1,0:T(8,128)S(1)}, u32[]{:S(2)}, u32[]{:S(2)}) collective-permute-start(f32[2,64,128]{2,1,0:T(8,128)S(1)} %combine.10.refs_0_), channel_id=1, source_target_pairs={{0,8},{1,9},{2,10},{3,11},{4,12},{5,13},{6,14},{7,15},{8,0},{9,1},... | collective-permute-start | bytes 196616 | tf_op jit(solution)/shard_map/ppermute | solution.py:301
  13.6 4.4 %collective-permute-start.1 = (f32[2,64,128]{2,1,0:T(8,128)S(1)}, f32[2,64,128]{2,1,0:T(8,128)S(1)}, u32[]{:S(2)}, u32[]{:S(2)}) collective-permute-start(f32[2,64,128]{2,1,0:T(8,128)S(1)} %combine.10.refs_0_), channel_id=1, source_target_pairs={{0,4},{1,13},{2,6},{3,15},{4,0},{5,9},{6,2},{7,11},{8,12},{9,5},{1... | collective-permute-start | bytes 196616 | tf_op jit(solution)/shard_map/ppermute | solution.py:301
  18.4 3.6 %collective-permute-start.4 = (f32[64,128]{1,0:T(8,128)S(1)}, f32[64,128]{1,0:T(8,128)S(1)}, u32[]{:S(2)}, u32[]{:S(2)}) collective-permute-start(f32[64,128]{1,0:T(8,128)S(1)} %get-tuple-element.69), channel_id=1, source_target_pairs={{0,3},{1,2},{2,1},{3,0},{4,7},{5,6},{6,5},{7,4},{8,11},{9,10},{10,... | collective-permute-start | bytes 98312 | tf_op jit(solution)/shard_map/ppermute | solution.py:328
  19.0 4.1 %collective-permute-start.5 = (f32[64,128]{1,0:T(8,128)S(1)}, f32[64,128]{1,0:T(8,128)S(1)}, u32[]{:S(2)}, u32[]{:S(2)}) collective-permute-start(f32[64,128]{1,0:T(8,128)S(1)} %get-tuple-element.70), channel_id=1, source_target_pairs={{0,2},{1,3},{2,0},{3,1},{4,6},{5,7},{6,4},{7,5},{8,10},{9,11},{10,... | collective-permute-start | bytes 98312 | tf_op jit(solution)/shard_map/ppermute | solution.py:328
  23.3 5.4 %collective-permute-start.7 = (f32[64,128]{1,0:T(8,128)S(1)}, f32[64,128]{1,0:T(8,128)S(1)}, u32[]{:S(2)}, u32[]{:S(2)}) collective-permute-start(f32[64,128]{1,0:T(8,128)S(1)} %solve_up.5.refs_0_.refs_1_), channel_id=1, source_target_pairs={{0,16},{4,20},{8,24},{12,28},{16,0},{20,4},{24,8},{28,12},{1,17},{... | collective-permute-start | bytes 98312 | tf_op jit(solution)/shard_map/ppermute | solution.py:284
  28.7 5.2 %collective-permute-start.10 = (f32[2,64,128]{2,1,0:T(8,128)S(1)}, f32[2,64,128]{2,1,0:T(8,128)S(1)}, u32[]{:S(2)}, u32[]{:S(2)}) collective-permute-start(f32[2,64,128]{2,1,0:T(8,128)S(1)} %combine.11.refs_0_), channel_id=1, source_target_pairs={{0,12},{1,5},{2,14},{3,7},{4,8},{5,1},{6,10},{7,3},{8,4},{9,13},{1... | collective-permute-start | bytes 196616 | tf_op jit(solution)/shard_map/ppermute | solution.py:301
  29.1 4.9 %collective-permute-start.9 = (f32[2,64,128]{2,1,0:T(8,128)S(1)}, f32[2,64,128]{2,1,0:T(8,128)S(1)}, u32[]{:S(2)}, u32[]{:S(2)}) collective-permute-start(f32[2,64,128]{2,1,0:T(8,128)S(1)} %combine.11.refs_0_), channel_id=1, source_target_pairs={{0,8},{1,9},{2,10},{3,11},{4,12},{5,13},{6,14},{7,15},{8,0},{9,1},... | collective-permute-start | bytes 196616 | tf_op jit(solution)/shard_map/ppermute | solution.py:301
  30.6 4.3 %collective-permute-start.8 = (f32[2,64,128]{2,1,0:T(8,128)S(1)}, f32[2,64,128]{2,1,0:T(8,128)S(1)}, u32[]{:S(2)}, u32[]{:S(2)}) collective-permute-start(f32[2,64,128]{2,1,0:T(8,128)S(1)} %combine.11.refs_0_), channel_id=1, source_target_pairs={{0,4},{1,13},{2,6},{3,15},{4,0},{5,9},{6,2},{7,11},{8,12},{9,5},{1... | collective-permute-start | bytes 196616 | tf_op jit(solution)/shard_map/ppermute | solution.py:301
  35.3 3.6 %collective-permute-start.11 = (f32[64,128]{1,0:T(8,128)S(1)}, f32[64,128]{1,0:T(8,128)S(1)}, u32[]{:S(2)}, u32[]{:S(2)}) collective-permute-start(f32[64,128]{1,0:T(8,128)S(1)} %get-tuple-element.76), channel_id=1, source_target_pairs={{0,3},{1,2},{2,1},{3,0},{4,7},{5,6},{6,5},{7,4},{8,11},{9,10},{10,... | collective-permute-start | bytes 98312 | tf_op jit(solution)/shard_map/ppermute | solution.py:328
  35.4 4.1 %collective-permute-start.12 = (f32[64,128]{1,0:T(8,128)S(1)}, f32[64,128]{1,0:T(8,128)S(1)}, u32[]{:S(2)}, u32[]{:S(2)}) collective-permute-start(f32[64,128]{1,0:T(8,128)S(1)} %get-tuple-element.77), channel_id=1, source_target_pairs={{0,2},{1,3},{2,0},{3,1},{4,6},{5,7},{6,4},{7,5},{8,10},{9,11},{10,... | collective-permute-start | bytes 98312 | tf_op jit(solution)/shard_map/ppermute | solution.py:328
  39.7 5.1 %collective-permute-start.14 = (f32[64,128]{1,0:T(8,128)S(1)}, f32[64,128]{1,0:T(8,128)S(1)}, u32[]{:S(2)}, u32[]{:S(2)}) collective-permute-start(f32[64,128]{1,0:T(8,128)S(1)} %solve_up.6.refs_0_.refs_2_), channel_id=1, source_target_pairs={{0,16},{4,20},{8,24},{12,28},{16,0},{20,4},{24,8},{28,12},{1,17},{... | collective-permute-start | bytes 98312 | tf_op jit(solution)/shard_map/ppermute | solution.py:284
  44.7 5.5 %collective-permute-start.17 = (f32[2,64,128]{2,1,0:T(8,128)S(1)}, f32[2,64,128]{2,1,0:T(8,128)S(1)}, u32[]{:S(2)}, u32[]{:S(2)}) collective-permute-start(f32[2,64,128]{2,1,0:T(8,128)S(1)} %combine.12.refs_0_), channel_id=1, source_target_pairs={{0,12},{1,5},{2,14},{3,7},{4,8},{5,1},{6,10},{7,3},{8,4},{9,13},{1... | collective-permute-start | bytes 196616 | tf_op jit(solution)/shard_map/ppermute | solution.py:301
  46.0 4.7 %collective-permute-start.16 = (f32[2,64,128]{2,1,0:T(8,128)S(1)}, f32[2,64,128]{2,1,0:T(8,128)S(1)}, u32[]{:S(2)}, u32[]{:S(2)}) collective-permute-start(f32[2,64,128]{2,1,0:T(8,128)S(1)} %combine.12.refs_0_), channel_id=1, source_target_pairs={{0,8},{1,9},{2,10},{3,11},{4,12},{5,13},{6,14},{7,15},{8,0},{9,1},... | collective-permute-start | bytes 196616 | tf_op jit(solution)/shard_map/ppermute | solution.py:301
  47.8 4.3 %collective-permute-start.15 = (f32[2,64,128]{2,1,0:T(8,128)S(1)}, f32[2,64,128]{2,1,0:T(8,128)S(1)}, u32[]{:S(2)}, u32[]{:S(2)}) collective-permute-start(f32[2,64,128]{2,1,0:T(8,128)S(1)} %combine.12.refs_0_), channel_id=1, source_target_pairs={{0,4},{1,13},{2,6},{3,15},{4,0},{5,9},{6,2},{7,11},{8,12},{9,5},{1... | collective-permute-start | bytes 196616 | tf_op jit(solution)/shard_map/ppermute | solution.py:301
  52.4 3.5 %collective-permute-start.18 = (f32[64,128]{1,0:T(8,128)S(1)}, f32[64,128]{1,0:T(8,128)S(1)}, u32[]{:S(2)}, u32[]{:S(2)}) collective-permute-start(f32[64,128]{1,0:T(8,128)S(1)} %get-tuple-element.83), channel_id=1, source_target_pairs={{0,3},{1,2},{2,1},{3,0},{4,7},{5,6},{6,5},{7,4},{8,11},{9,10},{10,... | collective-permute-start | bytes 98312 | tf_op jit(solution)/shard_map/ppermute | solution.py:328
  52.5 4.0 %collective-permute-start.19 = (f32[64,128]{1,0:T(8,128)S(1)}, f32[64,128]{1,0:T(8,128)S(1)}, u32[]{:S(2)}, u32[]{:S(2)}) collective-permute-start(f32[64,128]{1,0:T(8,128)S(1)} %get-tuple-element.84), channel_id=1, source_target_pairs={{0,2},{1,3},{2,0},{3,1},{4,6},{5,7},{6,4},{7,5},{8,10},{9,11},{10,... | collective-permute-start | bytes 98312 | tf_op jit(solution)/shard_map/ppermute | solution.py:328
  53.6 3.0 %collective-permute-start.20 = (f32[64,128]{1,0:T(8,128)S(1)}, f32[64,128]{1,0:T(8,128)S(1)}, u32[]{:S(2)}, u32[]{:S(2)}) collective-permute-start(f32[64,128]{1,0:T(8,128)S(1)} %get-tuple-element.85), channel_id=1, source_target_pairs={{0,1},{1,0},{2,3},{3,2},{4,5},{5,4},{6,7},{7,6},{8,9},{9,8},{10,11... | collective-permute-start | bytes 98312 | tf_op jit(solution)/shard_map/ppermute | solution.py:328
  56.7 5.1 %collective-permute-start.21 = (f32[64,128]{1,0:T(8,128)S(1)}, f32[64,128]{1,0:T(8,128)S(1)}, u32[]{:S(2)}, u32[]{:S(2)}) collective-permute-start(f32[64,128]{1,0:T(8,128)S(1)} %solve_up.7.refs_0_.refs_3_), channel_id=1, source_target_pairs={{0,16},{4,20},{8,24},{12,28},{16,0},{20,4},{24,8},{28,12},{1,17},{... | collective-permute-start | bytes 98312 | tf_op jit(solution)/shard_map/ppermute | solution.py:284
  61.8 5.2 %collective-permute-start.24 = (f32[2,64,128]{2,1,0:T(8,128)S(1)}, f32[2,64,128]{2,1,0:T(8,128)S(1)}, u32[]{:S(2)}, u32[]{:S(2)}) collective-permute-start(f32[2,64,128]{2,1,0:T(8,128)S(1)} %combine.13.refs_0_), channel_id=1, source_target_pairs={{0,12},{1,5},{2,14},{3,7},{4,8},{5,1},{6,10},{7,3},{8,4},{9,13},{1... | collective-permute-start | bytes 196616 | tf_op jit(solution)/shard_map/ppermute | solution.py:301
  61.8 5.2 %collective-permute-start.23 = (f32[2,64,128]{2,1,0:T(8,128)S(1)}, f32[2,64,128]{2,1,0:T(8,128)S(1)}, u32[]{:S(2)}, u32[]{:S(2)}) collective-permute-start(f32[2,64,128]{2,1,0:T(8,128)S(1)} %combine.13.refs_0_), channel_id=1, source_target_pairs={{0,8},{1,9},{2,10},{3,11},{4,12},{5,13},{6,14},{7,15},{8,0},{9,1},... | collective-permute-start | bytes 196616 | tf_op jit(solution)/shard_map/ppermute | solution.py:301
  63.5 4.3 %collective-permute-start.22 = (f32[2,64,128]{2,1,0:T(8,128)S(1)}, f32[2,64,128]{2,1,0:T(8,128)S(1)}, u32[]{:S(2)}, u32[]{:S(2)}) collective-permute-start(f32[2,64,128]{2,1,0:T(8,128)S(1)} %combine.13.refs_0_), channel_id=1, source_target_pairs={{0,4},{1,13},{2,6},{3,15},{4,0},{5,9},{6,2},{7,11},{8,12},{9,5},{1... | collective-permute-start | bytes 196616 | tf_op jit(solution)/shard_map/ppermute | solution.py:301
  68.2 4.4 %collective-permute-start.25 = (f32[64,128]{1,0:T(8,128)S(1)}, f32[64,128]{1,0:T(8,128)S(1)}, u32[]{:S(2)}, u32[]{:S(2)}) collective-permute-start(f32[64,128]{1,0:T(8,128)S(1)} %get-tuple-element.90), channel_id=1, source_target_pairs={{0,3},{1,2},{2,1},{3,0},{4,7},{5,6},{6,5},{7,4},{8,11},{9,10},{10,... | collective-permute-start | bytes 98312 | tf_op jit(solution)/shard_map/ppermute | solution.py:328
  68.3 4.3 %collective-permute-start.26 = (f32[64,128]{1,0:T(8,128)S(1)}, f32[64,128]{1,0:T(8,128)S(1)}, u32[]{:S(2)}, u32[]{:S(2)}) collective-permute-start(f32[64,128]{1,0:T(8,128)S(1)} %get-tuple-element.91), channel_id=1, source_target_pairs={{0,2},{1,3},{2,0},{3,1},{4,6},{5,7},{6,4},{7,5},{8,10},{9,11},{10,... | collective-permute-start | bytes 98312 | tf_op jit(solution)/shard_map/ppermute | solution.py:328
  69.3 3.3 %collective-permute-start.27 = (f32[64,128]{1,0:T(8,128)S(1)}, f32[64,128]{1,0:T(8,128)S(1)}, u32[]{:S(2)}, u32[]{:S(2)}) collective-permute-start(f32[64,128]{1,0:T(8,128)S(1)} %get-tuple-element.92), channel_id=1, source_target_pairs={{0,1},{1,0},{2,3},{3,2},{4,5},{5,4},{6,7},{7,6},{8,9},{9,8},{10,11... | collective-permute-start | bytes 98312 | tf_op jit(solution)/shard_map/ppermute | solution.py:328
  72.8 4.9 %collective-permute-start.28 = (f32[64,128]{1,0:T(8,128)S(1)}, f32[64,128]{1,0:T(8,128)S(1)}, u32[]{:S(2)}, u32[]{:S(2)}) collective-permute-start(f32[64,128]{1,0:T(8,128)S(1)} %solve_up.8.refs_0_.refs_4_), channel_id=1, source_target_pairs={{0,16},{4,20},{8,24},{12,28},{16,0},{20,4},{24,8},{28,12},{1,17},{... | collective-permute-start | bytes 98312 | tf_op jit(solution)/shard_map/ppermute | solution.py:284
  77.7 5.3 %collective-permute-start.31 = (f32[2,64,128]{2,1,0:T(8,128)S(1)}, f32[2,64,128]{2,1,0:T(8,128)S(1)}, u32[]{:S(2)}, u32[]{:S(2)}) collective-permute-start(f32[2,64,128]{2,1,0:T(8,128)S(1)} %combine.14.refs_0_), channel_id=1, source_target_pairs={{0,12},{1,5},{2,14},{3,7},{4,8},{5,1},{6,10},{7,3},{8,4},{9,13},{1... | collective-permute-start | bytes 196616 | tf_op jit(solution)/shard_map/ppermute | solution.py:301
  78.8 4.8 %collective-permute-start.30 = (f32[2,64,128]{2,1,0:T(8,128)S(1)}, f32[2,64,128]{2,1,0:T(8,128)S(1)}, u32[]{:S(2)}, u32[]{:S(2)}) collective-permute-start(f32[2,64,128]{2,1,0:T(8,128)S(1)} %combine.14.refs_0_), channel_id=1, source_target_pairs={{0,8},{1,9},{2,10},{3,11},{4,12},{5,13},{6,14},{7,15},{8,0},{9,1},... | collective-permute-start | bytes 196616 | tf_op jit(solution)/shard_map/ppermute | solution.py:301
  80.6 4.3 %collective-permute-start.29 = (f32[2,64,128]{2,1,0:T(8,128)S(1)}, f32[2,64,128]{2,1,0:T(8,128)S(1)}, u32[]{:S(2)}, u32[]{:S(2)}) collective-permute-start(f32[2,64,128]{2,1,0:T(8,128)S(1)} %combine.14.refs_0_), channel_id=1, source_target_pairs={{0,4},{1,13},{2,6},{3,15},{4,0},{5,9},{6,2},{7,11},{8,12},{9,5},{1... | collective-permute-start | bytes 196616 | tf_op jit(solution)/shard_map/ppermute | solution.py:301
  85.2 3.4 %collective-permute-start.32 = (f32[64,128]{1,0:T(8,128)S(1)}, f32[64,128]{1,0:T(8,128)S(1)}, u32[]{:S(2)}, u32[]{:S(2)}) collective-permute-start(f32[64,128]{1,0:T(8,128)S(1)} %get-tuple-element.97), channel_id=1, source_target_pairs={{0,3},{1,2},{2,1},{3,0},{4,7},{5,6},{6,5},{7,4},{8,11},{9,10},{10,... | collective-permute-start | bytes 98312 | tf_op jit(solution)/shard_map/ppermute | solution.py:328
  85.3 4.0 %collective-permute-start.33 = (f32[64,128]{1,0:T(8,128)S(1)}, f32[64,128]{1,0:T(8,128)S(1)}, u32[]{:S(2)}, u32[]{:S(2)}) collective-permute-start(f32[64,128]{1,0:T(8,128)S(1)} %get-tuple-element.98), channel_id=1, source_target_pairs={{0,2},{1,3},{2,0},{3,1},{4,6},{5,7},{6,4},{7,5},{8,10},{9,11},{10,... | collective-permute-start | bytes 98312 | tf_op jit(solution)/shard_map/ppermute | solution.py:328
  86.3 3.0 %collective-permute-start.34 = (f32[64,128]{1,0:T(8,128)S(1)}, f32[64,128]{1,0:T(8,128)S(1)}, u32[]{:S(2)}, u32[]{:S(2)}) collective-permute-start(f32[64,128]{1,0:T(8,128)S(1)} %get-tuple-element.99), channel_id=1, source_target_pairs={{0,1},{1,0},{2,3},{3,2},{4,5},{5,4},{6,7},{7,6},{8,9},{9,8},{10,11... | collective-permute-start | bytes 98312 | tf_op jit(solution)/shard_map/ppermute | solution.py:328
  89.7 3.7 %collective-permute-start.37 = (f32[64,128]{1,0:T(8,128)S(1)}, f32[64,128]{1,0:T(8,128)S(1)}, u32[]{:S(2)}, u32[]{:S(2)}) collective-permute-start(f32[64,128]{1,0:T(8,128)S(1)} %solve_down.6.refs_0_.refs_5_), channel_id=1, source_target_pairs={{0,3},{1,2},{2,1},{3,0},{4,7},{5,6},{6,5},{7,4},{8,11},{9,10},{10,... | collective-permute-start | bytes 98312 | tf_op jit(solution)/shard_map/ppermute | solution.py:328
  90.2 3.9 %collective-permute-start.36 = (f32[64,128]{1,0:T(8,128)S(1)}, f32[64,128]{1,0:T(8,128)S(1)}, u32[]{:S(2)}, u32[]{:S(2)}) collective-permute-start(f32[64,128]{1,0:T(8,128)S(1)} %solve_down.6.refs_0_.refs_5_), channel_id=1, source_target_pairs={{0,2},{1,3},{2,0},{3,1},{4,6},{5,7},{6,4},{7,5},{8,10},{9,11},{10,... | collective-permute-start | bytes 98312 | tf_op jit(solution)/shard_map/ppermute | solution.py:328
  94.7 5.4 %collective-permute-start.38 = (f32[2,64,128]{2,1,0:T(8,128)S(1)}, f32[2,64,128]{2,1,0:T(8,128)S(1)}, u32[]{:S(2)}, u32[]{:S(2)}) collective-permute-start(f32[2,64,128]{2,1,0:T(8,128)S(1)} %get-tuple-element.107), channel_id=1, source_target_pairs={{0,12},{1,5},{2,14},{3,7},{4,8},{5,1},{6,10},{7,3},{8,4},{9,13},{1... | collective-permute-start | bytes 196616 | tf_op jit(solution)/shard_map/ppermute | solution.py:301
  95.4 5.0 %collective-permute-start.39 = (f32[2,64,128]{2,1,0:T(8,128)S(1)}, f32[2,64,128]{2,1,0:T(8,128)S(1)}, u32[]{:S(2)}, u32[]{:S(2)}) collective-permute-start(f32[2,64,128]{2,1,0:T(8,128)S(1)} %get-tuple-element.108), channel_id=1, source_target_pairs={{0,8},{1,9},{2,10},{3,11},{4,12},{5,13},{6,14},{7,15},{8,0},{9,1},... | collective-permute-start | bytes 196616 | tf_op jit(solution)/shard_map/ppermute | solution.py:301
  96.8 4.3 %collective-permute-start.40 = (f32[2,64,128]{2,1,0:T(8,128)S(1)}, f32[2,64,128]{2,1,0:T(8,128)S(1)}, u32[]{:S(2)}, u32[]{:S(2)}) collective-permute-start(f32[2,64,128]{2,1,0:T(8,128)S(1)} %get-tuple-element.109), channel_id=1, source_target_pairs={{0,4},{1,13},{2,6},{3,15},{4,0},{5,9},{6,2},{7,11},{8,12},{9,5},{1... | collective-permute-start | bytes 196616 | tf_op jit(solution)/shard_map/ppermute | solution.py:301
  101.1 5.2 %collective-permute-start.41 = (f32[64,128]{1,0:T(8,128)S(1)}, f32[64,128]{1,0:T(8,128)S(1)}, u32[]{:S(2)}, u32[]{:S(2)}) collective-permute-start(f32[64,128]{1,0:T(8,128)S(1)} %get-tuple-element.111), channel_id=1, source_target_pairs={{0,16},{4,20},{8,24},{12,28},{16,0},{20,4},{24,8},{28,12},{1,17},{... | collective-permute-start | bytes 98312 | tf_op jit(solution)/shard_map/ppermute | solution.py:284
  107.4 3.4 %collective-permute-start.44 = (f32[64,128]{1,0:T(8,128)S(1)}, f32[64,128]{1,0:T(8,128)S(1)}, u32[]{:S(2)}, u32[]{:S(2)}) collective-permute-start(f32[64,128]{1,0:T(8,128)S(1)} %solve_down.7.refs_0_.refs_4_), channel_id=1, source_target_pairs={{0,3},{1,2},{2,1},{3,0},{4,7},{5,6},{6,5},{7,4},{8,11},{9,10},{10,... | collective-permute-start | bytes 98312 | tf_op jit(solution)/shard_map/ppermute | solution.py:328
  107.5 4.1 %collective-permute-start.43 = (f32[64,128]{1,0:T(8,128)S(1)}, f32[64,128]{1,0:T(8,128)S(1)}, u32[]{:S(2)}, u32[]{:S(2)}) collective-permute-start(f32[64,128]{1,0:T(8,128)S(1)} %solve_down.7.refs_0_.refs_4_), channel_id=1, source_target_pairs={{0,2},{1,3},{2,0},{3,1},{4,6},{5,7},{6,4},{7,5},{8,10},{9,11},{10,... | collective-permute-start | bytes 98312 | tf_op jit(solution)/shard_map/ppermute | solution.py:328
  108.3 3.3 %collective-permute-start.42 = (f32[64,128]{1,0:T(8,128)S(1)}, f32[64,128]{1,0:T(8,128)S(1)}, u32[]{:S(2)}, u32[]{:S(2)}) collective-permute-start(f32[64,128]{1,0:T(8,128)S(1)} %solve_down.7.refs_0_.refs_4_), channel_id=1, source_target_pairs={{0,1},{1,0},{2,3},{3,2},{4,5},{5,4},{6,7},{7,6},{8,9},{9,8},{10,11... | collective-permute-start | bytes 98312 | tf_op jit(solution)/shard_map/ppermute | solution.py:328
  112.2 5.4 %collective-permute-start.45 = (f32[2,64,128]{2,1,0:T(8,128)S(1)}, f32[2,64,128]{2,1,0:T(8,128)S(1)}, u32[]{:S(2)}, u32[]{:S(2)}) collective-permute-start(f32[2,64,128]{2,1,0:T(8,128)S(1)} %get-tuple-element.112), channel_id=1, source_target_pairs={{0,12},{1,5},{2,14},{3,7},{4,8},{5,1},{6,10},{7,3},{8,4},{9,13},{1... | collective-permute-start | bytes 196616 | tf_op jit(solution)/shard_map/ppermute | solution.py:301
  113.7 5.3 %collective-permute-start.46 = (f32[2,64,128]{2,1,0:T(8,128)S(1)}, f32[2,64,128]{2,1,0:T(8,128)S(1)}, u32[]{:S(2)}, u32[]{:S(2)}) collective-permute-start(f32[2,64,128]{2,1,0:T(8,128)S(1)} %get-tuple-element.113), channel_id=1, source_target_pairs={{0,8},{1,9},{2,10},{3,11},{4,12},{5,13},{6,14},{7,15},{8,0},{9,1},... | collective-permute-start | bytes 196616 | tf_op jit(solution)/shard_map/ppermute | solution.py:301
  115.2 4.3 %collective-permute-start.47 = (f32[2,64,128]{2,1,0:T(8,128)S(1)}, f32[2,64,128]{2,1,0:T(8,128)S(1)}, u32[]{:S(2)}, u32[]{:S(2)}) collective-permute-start(f32[2,64,128]{2,1,0:T(8,128)S(1)} %get-tuple-element.114), channel_id=1, source_target_pairs={{0,4},{1,13},{2,6},{3,15},{4,0},{5,9},{6,2},{7,11},{8,12},{9,5},{1... | collective-permute-start | bytes 196616 | tf_op jit(solution)/shard_map/ppermute | solution.py:301
  119.5 4.9 %collective-permute-start.48 = (f32[64,128]{1,0:T(8,128)S(1)}, f32[64,128]{1,0:T(8,128)S(1)}, u32[]{:S(2)}, u32[]{:S(2)}) collective-permute-start(f32[64,128]{1,0:T(8,128)S(1)} %get-tuple-element.116), channel_id=1, source_target_pairs={{0,16},{4,20},{8,24},{12,28},{16,0},{20,4},{24,8},{28,12},{1,17},{... | collective-permute-start | bytes 98312 | tf_op jit(solution)/shard_map/ppermute | solution.py:284
  124.5 3.4 %collective-permute-start.51 = (f32[64,128]{1,0:T(8,128)S(1)}, f32[64,128]{1,0:T(8,128)S(1)}, u32[]{:S(2)}, u32[]{:S(2)}) collective-permute-start(f32[64,128]{1,0:T(8,128)S(1)} %solve_down.8.refs_0_.refs_3_), channel_id=1, source_target_pairs={{0,3},{1,2},{2,1},{3,0},{4,7},{5,6},{6,5},{7,4},{8,11},{9,10},{10,... | collective-permute-start | bytes 98312 | tf_op jit(solution)/shard_map/ppermute | solution.py:328
  124.6 4.1 %collective-permute-start.50 = (f32[64,128]{1,0:T(8,128)S(1)}, f32[64,128]{1,0:T(8,128)S(1)}, u32[]{:S(2)}, u32[]{:S(2)}) collective-permute-start(f32[64,128]{1,0:T(8,128)S(1)} %solve_down.8.refs_0_.refs_3_), channel_id=1, source_target_pairs={{0,2},{1,3},{2,0},{3,1},{4,6},{5,7},{6,4},{7,5},{8,10},{9,11},{10,... | collective-permute-start | bytes 98312 | tf_op jit(solution)/shard_map/ppermute | solution.py:328
  129.3 5.9 %collective-permute-start.52 = (f32[2,64,128]{2,1,0:T(8,128)S(1)}, f32[2,64,128]{2,1,0:T(8,128)S(1)}, u32[]{:S(2)}, u32[]{:S(2)}) collective-permute-start(f32[2,64,128]{2,1,0:T(8,128)S(1)} %get-tuple-element.117), channel_id=1, source_target_pairs={{0,12},{1,5},{2,14},{3,7},{4,8},{5,1},{6,10},{7,3},{8,4},{9,13},{1... | collective-permute-start | bytes 196616 | tf_op jit(solution)/shard_map/ppermute | solution.py:301
  130.3 5.6 %collective-permute-start.53 = (f32[2,64,128]{2,1,0:T(8,128)S(1)}, f32[2,64,128]{2,1,0:T(8,128)S(1)}, u32[]{:S(2)}, u32[]{:S(2)}) collective-permute-start(f32[2,64,128]{2,1,0:T(8,128)S(1)} %get-tuple-element.118), channel_id=1, source_target_pairs={{0,8},{1,9},{2,10},{3,11},{4,12},{5,13},{6,14},{7,15},{8,0},{9,1},... | collective-permute-start | bytes 196616 | tf_op jit(solution)/shard_map/ppermute | solution.py:301
  132.1 4.3 %collective-permute-start.54 = (f32[2,64,128]{2,1,0:T(8,128)S(1)}, f32[2,64,128]{2,1,0:T(8,128)S(1)}, u32[]{:S(2)}, u32[]{:S(2)}) collective-permute-start(f32[2,64,128]{2,1,0:T(8,128)S(1)} %get-tuple-element.119), channel_id=1, source_target_pairs={{0,4},{1,13},{2,6},{3,15},{4,0},{5,9},{6,2},{7,11},{8,12},{9,5},{1... | collective-permute-start | bytes 196616 | tf_op jit(solution)/shard_map/ppermute | solution.py:301
  136.4 5.2 %collective-permute-start.55 = (f32[64,128]{1,0:T(8,128)S(1)}, f32[64,128]{1,0:T(8,128)S(1)}, u32[]{:S(2)}, u32[]{:S(2)}) collective-permute-start(f32[64,128]{1,0:T(8,128)S(1)} %get-tuple-element.121), channel_id=1, source_target_pairs={{0,16},{4,20},{8,24},{12,28},{16,0},{20,4},{24,8},{28,12},{1,17},{... | collective-permute-start | bytes 98312 | tf_op jit(solution)/shard_map/ppermute | solution.py:284
  141.8 3.6 %collective-permute-start.58 = (f32[64,128]{1,0:T(8,128)S(1)}, f32[64,128]{1,0:T(8,128)S(1)}, u32[]{:S(2)}, u32[]{:S(2)}) collective-permute-start(f32[64,128]{1,0:T(8,128)S(1)} %solve_down.9.refs_0_.refs_2_), channel_id=1, source_target_pairs={{0,3},{1,2},{2,1},{3,0},{4,7},{5,6},{6,5},{7,4},{8,11},{9,10},{10,... | collective-permute-start | bytes 98312 | tf_op jit(solution)/shard_map/ppermute | solution.py:328
  141.9 4.0 %collective-permute-start.57 = (f32[64,128]{1,0:T(8,128)S(1)}, f32[64,128]{1,0:T(8,128)S(1)}, u32[]{:S(2)}, u32[]{:S(2)}) collective-permute-start(f32[64,128]{1,0:T(8,128)S(1)} %solve_down.9.refs_0_.refs_2_), channel_id=1, source_target_pairs={{0,2},{1,3},{2,0},{3,1},{4,6},{5,7},{6,4},{7,5},{8,10},{9,11},{10,... | collective-permute-start | bytes 98312 | tf_op jit(solution)/shard_map/ppermute | solution.py:328
  146.4 5.9 %collective-permute-start.59 = (f32[2,64,128]{2,1,0:T(8,128)S(1)}, f32[2,64,128]{2,1,0:T(8,128)S(1)}, u32[]{:S(2)}, u32[]{:S(2)}) collective-permute-start(f32[2,64,128]{2,1,0:T(8,128)S(1)} %get-tuple-element.122), channel_id=1, source_target_pairs={{0,12},{1,5},{2,14},{3,7},{4,8},{5,1},{6,10},{7,3},{8,4},{9,13},{1... | collective-permute-start | bytes 196616 | tf_op jit(solution)/shard_map/ppermute | solution.py:301
  147.6 5.1 %collective-permute-start.60 = (f32[2,64,128]{2,1,0:T(8,128)S(1)}, f32[2,64,128]{2,1,0:T(8,128)S(1)}, u32[]{:S(2)}, u32[]{:S(2)}) collective-permute-start(f32[2,64,128]{2,1,0:T(8,128)S(1)} %get-tuple-element.123), channel_id=1, source_target_pairs={{0,8},{1,9},{2,10},{3,11},{4,12},{5,13},{6,14},{7,15},{8,0},{9,1},... | collective-permute-start | bytes 196616 | tf_op jit(solution)/shard_map/ppermute | solution.py:301
  148.9 4.4 %collective-permute-start.61 = (f32[2,64,128]{2,1,0:T(8,128)S(1)}, f32[2,64,128]{2,1,0:T(8,128)S(1)}, u32[]{:S(2)}, u32[]{:S(2)}) collective-permute-start(f32[2,64,128]{2,1,0:T(8,128)S(1)} %get-tuple-element.124), channel_id=1, source_target_pairs={{0,4},{1,13},{2,6},{3,15},{4,0},{5,9},{6,2},{7,11},{8,12},{9,5},{1... | collective-permute-start | bytes 196616 | tf_op jit(solution)/shard_map/ppermute | solution.py:301
  153.3 5.2 %collective-permute-start.62 = (f32[64,128]{1,0:T(8,128)S(1)}, f32[64,128]{1,0:T(8,128)S(1)}, u32[]{:S(2)}, u32[]{:S(2)}) collective-permute-start(f32[64,128]{1,0:T(8,128)S(1)} %get-tuple-element.126), channel_id=1, source_target_pairs={{0,16},{4,20},{8,24},{12,28},{16,0},{20,4},{24,8},{28,12},{1,17},{... | collective-permute-start | bytes 98312 | tf_op jit(solution)/shard_map/ppermute | solution.py:284
  158.7 3.6 %collective-permute-start.65 = (f32[64,128]{1,0:T(8,128)S(1)}, f32[64,128]{1,0:T(8,128)S(1)}, u32[]{:S(2)}, u32[]{:S(2)}) collective-permute-start(f32[64,128]{1,0:T(8,128)S(1)} %solve_down.10.refs_0_.refs_1_), channel_id=1, source_target_pairs={{0,3},{1,2},{2,1},{3,0},{4,7},{5,6},{6,5},{7,4},{8,11},{9,10},{10,... | collective-permute-start | bytes 98312 | tf_op jit(solution)/shard_map/ppermute | solution.py:328
  158.8 4.0 %collective-permute-start.64 = (f32[64,128]{1,0:T(8,128)S(1)}, f32[64,128]{1,0:T(8,128)S(1)}, u32[]{:S(2)}, u32[]{:S(2)}) collective-permute-start(f32[64,128]{1,0:T(8,128)S(1)} %solve_down.10.refs_0_.refs_1_), channel_id=1, source_target_pairs={{0,2},{1,3},{2,0},{3,1},{4,6},{5,7},{6,4},{7,5},{8,10},{9,11},{10,... | collective-permute-start | bytes 98312 | tf_op jit(solution)/shard_map/ppermute | solution.py:328
  163.3 5.9 %collective-permute-start.66 = (f32[2,64,128]{2,1,0:T(8,128)S(1)}, f32[2,64,128]{2,1,0:T(8,128)S(1)}, u32[]{:S(2)}, u32[]{:S(2)}) collective-permute-start(f32[2,64,128]{2,1,0:T(8,128)S(1)} %get-tuple-element.127), channel_id=1, source_target_pairs={{0,12},{1,5},{2,14},{3,7},{4,8},{5,1},{6,10},{7,3},{8,4},{9,13},{1... | collective-permute-start | bytes 196616 | tf_op jit(solution)/shard_map/ppermute | solution.py:301
  164.5 5.3 %collective-permute-start.67 = (f32[2,64,128]{2,1,0:T(8,128)S(1)}, f32[2,64,128]{2,1,0:T(8,128)S(1)}, u32[]{:S(2)}, u32[]{:S(2)}) collective-permute-start(f32[2,64,128]{2,1,0:T(8,128)S(1)} %get-tuple-element.128), channel_id=1, source_target_pairs={{0,8},{1,9},{2,10},{3,11},{4,12},{5,13},{6,14},{7,15},{8,0},{9,1},... | collective-permute-start | bytes 196616 | tf_op jit(solution)/shard_map/ppermute | solution.py:301
  165.9 4.4 %collective-permute-start.68 = (f32[2,64,128]{2,1,0:T(8,128)S(1)}, f32[2,64,128]{2,1,0:T(8,128)S(1)}, u32[]{:S(2)}, u32[]{:S(2)}) collective-permute-start(f32[2,64,128]{2,1,0:T(8,128)S(1)} %get-tuple-element.129), channel_id=1, source_target_pairs={{0,4},{1,13},{2,6},{3,15},{4,0},{5,9},{6,2},{7,11},{8,12},{9,5},{1... | collective-permute-start | bytes 196616 | tf_op jit(solution)/shard_map/ppermute | solution.py:301
  170.3 5.2 %collective-permute-start.69 = (f32[64,128]{1,0:T(8,128)S(1)}, f32[64,128]{1,0:T(8,128)S(1)}, u32[]{:S(2)}, u32[]{:S(2)}) collective-permute-start(f32[64,128]{1,0:T(8,128)S(1)} %get-tuple-element.131), channel_id=1, source_target_pairs={{0,16},{4,20},{8,24},{12,28},{16,0},{20,4},{24,8},{28,12},{1,17},{... | collective-permute-start | bytes 98312 | tf_op jit(solution)/shard_map/ppermute | solution.py:284
  (13 other events, 61.1 us)

commit v12 on v9

--- a/solution.py
+++ b/solution.py
@@ -145,38 +145,47 @@
         return len(self.arrays) - 1, place
 
 
-def couple_kernel(terms, span, high_ref, low_ref, *refs):
-    n_in = 1 + max(number for number, _ in terms)
-    ins, outs = refs[:n_in], refs[n_in:]
+def couple_kernel(terms, entries, span, n_in, high_ref, low_ref, *refs):
+    ins, bases, outs = refs[:n_in], refs[n_in:-span[2]], refs[-span[2] :]
     block = ins[0].shape[-1]
     joined = jnp.concatenate([read(term, ins) for term in terms], axis=1)
     wanted = pl.ds(span[0] * block, (span[1] - span[0]) * block)
-    result = product(halves(joined), (high_ref[:, wanted], low_ref[:, wanted]), False)
+    parts = [
+        jnp.concatenate([ref[pl.ds(entry * block, block), wanted] for entry in entries], axis=0)
+        for ref in (high_ref, low_ref)
+    ]
+    result = product(halves(joined), parts, False)
+    for base_ref in bases:
+        result += base_ref[:, wanted]
+    if len(outs) == 1 and outs[0].shape == result.shape:
+        outs[0][...] = result
+        return
     pieces = [result[:, at : at + block] for at in range(0, result.shape[1], block)]
     each = len(pieces) // len(outs)
     for number, ref in enumerate(outs):
         write(ref, pieces[number * each : (number + 1) * each])
 
 
-def couple(pieces, high, low, span, each):
+def couple(pieces, entries, high, low, span, each, base=()):
     operands = Operands()
-    terms = [operands.term(piece) for piece in pieces]
+    terms = [operands.term(pieces[entry]) for entry in entries]
     rows, block = operands.arrays[0].shape[-2:]
-    shape = (rows, block) if each == 1 else (each, rows, block)
-    n_out = (span[1] - span[0]) // each
+    width = span[1] - span[0]
+    shape = {0: (rows, width * block), 1: (rows, block)}.get(each, (each, rows, block))
+    n_out = width // each if each else 1
     whole = pl.BlockSpec(memory_space=VMEM)
-    work = rows * block * block * len(terms) * (span[1] - span[0])
-    return pl.pallas_call(
-        functools.partial(couple_kernel, terms, span),
+    work = rows * block * block * len(terms) * width
+    return pl.pallas_call(
+        functools.partial(couple_kernel, terms, entries, (*span, n_out), len(operands.arrays)),
         out_shape=[jax.ShapeDtypeStruct(shape, jnp.float32)] * n_out,
-        in_specs=[whole] * (2 + len(operands.arrays)),
+        in_specs=[whole] * (2 + len(operands.arrays) + len(base)),
         out_specs=[whole] * n_out,
         compiler_params=pltpu.CompilerParams(vmem_limit_bytes=16 * MIB),
         cost_estimate=pl.CostEstimate(
             flops=6 * work, bytes_accessed=4 * work // rows, transcendentals=0
         ),
-        name="couple",
-    )(high, low, *operands.arrays)
+        name="couple" if each else "couple_early",
+    )(high, low, *operands.arrays, *base)
 
 
 def first_solve_kernel(right_ref, inverse_ref, out_ref, right, inverse, arrived):
@@ -354,8 +363,9 @@
         if level > 1:
             down.append(tidy(level - 2, True, solved))
         pieces = gather_row(forward[-1], [pair[0] for pair in up[-1:] + down[-1:]])
-        far = couple(pieces, *up[-1], (n_col // 2, n_col), 1)
-        near = couple(pieces, *up[-1], (0, n_col // 2), 1)
+        base = couple(pieces, [0, 1, *range(4, n_row)], *up[-1], (0, n_col), 0)
+        far = couple(pieces, [2, 3], *up[-1], (n_col // 2, n_col), 1, base)
+        near = couple(pieces, [2, 3], *up[-1], (0, n_col // 2), 1, base)
         if level < levels - 1:
             totals.append(gather(level, near[:1]))
             after = totals[-1:]
@@ -368,8 +378,10 @@
     backward[-1] = solve(forward[-1], inverse, levels - 1, [], True)
     for level in range(levels - 2, -1, -1):
         pieces = plain(exchange_each([backward[level + 1]] * n_col, "col"))
-        sent = couple(pieces, *down[level], (2, n_row), 2)
-        kept = couple(pieces, *down[level], (0, 2), 2)
+        late = list(range(n_col - 2, 0, -1))
+        base = couple(pieces, [0, n_col - 1], *down[level], (0, n_row), 0)
+        sent = couple(pieces, late, *down[level], (2, n_row), 2, base)
+        kept = couple(pieces, late, *down[level], (0, 2), 2, base)
         if level == levels - 2:
             forward_out = stack(forward, kept[:1])
         pieces = deliver_row(kept + sent)
@@ -495,7 +507,7 @@
     def local(rhs, diag_inv, blocks, blk_target, blk_source, blk_count):
         sizes = (n_row, n_col)
         dense = n_row * n_col <= blocks.shape[3] and rhs.shape[3] == 1
-        even = all(size > 1 and size & (size - 1) == 0 for size in sizes)
+        even = n_row > 2 and n_col > 2 and all(size & (size - 1) == 0 for size in sizes)
         run = direct_shards if dense and even else shards
         return run(rhs, diag_inv, blocks, blk_target, blk_source, blk_count)
 

time: 176 us -> 178 us (1.011)
  waiting for transfers between devices: 83.1 us -> 81.3 us
    ppermute x30, waiting for transfers between devices: 31.5 us -> 27.5 us  [near_exchange(): received[d] = lax.ppermute(messages[d], ('row', 'col'), pairs)]
    ppermute x30, waiting for transfers between devices: 14.3 us -> 18.2 us  [exchange_each(): lax.ppermute(messages[d], axis, [(i, i ^ d) for i in range(size)])]
    pallas_call x20 -> x30, Pallas kernels: 7.88 us -> 8.93 us  [couple(): pl.pallas_call(functools.partial(couple_kernel, terms, entries, (*span, n...]
  transfers between devices with their start and end apart: 70 -> 70, of which waited for: 53 -> 52; matrix products, arithmetic and copies ran while one was open for 1% -> 1% of each run, Pallas kernels for 10% -> 11%
where the time goes in v12:
time: 178 us; the launch traced here: 177 us
  waiting for transfers between devices  81.3 us (46%)
  starting transfers between devices  64.7 us (36%)
  Pallas kernels  27.1 us (15%)
  local copies, waits for them, and re-layouts  2.87 us (2%)
    ppermute x10, waiting for transfers between devices, far_exchange(): lax.ppermute(segment, axis, [(i, i ^ size // 2) for i in range(size)])  35.6 us
    ppermute x30, starting transfers between devices, near_exchange(): received[d] = lax.ppermute(messages[d], ('row', 'col'), pairs)  35.2 us
    ppermute x30, waiting for transfers between devices, near_exchange(): received[d] = lax.ppermute(messages[d], ('row', 'col'), pairs)  27.5 us
    ppermute x30, starting transfers between devices, exchange_each(): lax.ppermute(messages[d], axis, [(i, i ^ d) for i in range(size)])  20.9 us
    ppermute x30, waiting for transfers between devices, exchange_each(): lax.ppermute(messages[d], axis, [(i, i ^ d) for i in range(size)])  18.2 us
    pallas_call x30, Pallas kernels, couple(): pl.pallas_call(functools.partial(couple_kernel, terms, entries, (*span, n...  8.93 us
    ppermute x10, starting transfers between devices, far_exchange(): lax.ppermute(segment, axis, [(i, i ^ size // 2) for i in range(size)])  8.5 us
    pallas_call x5, Pallas kernels, gather_blocks(): pl.pallas_call(functools.partial(gather_blocks_kernel, n_row, n_col, leve...  7.97 us
  transfers between devices with their start and end apart: 70, of which 52 were waited for; matrix products, arithmetic and copies ran while one was open for 1% of the time, Pallas kernels for 11%

profile of v12, /device:TPU:0, one launch (start us, length us, event | category | flops | bytes accessed | tf_op | source)
XLA Modules:
  0.0 177.4 jit_solution(17168959038315539203)
XLA Ops:
  0.6 1.7 first_solve.1.refs_0_
  2.3 4.1 %collective-permute-start = (f32[64,128]{1,0:T(8,128)}, f32[64,128]{1,0:T(8,128)S(1)}, u32[]{:S(2)}, u32[]{:S(2)}) collective-permute-start(f32[64,128]{1,0:T(8,128)} %first_solve.1.refs_0_), channel_id=1, source_target_pairs={{0,16},{4,20},{8,24},{12,28},{16,0},{20,4},{24,8},{28,12},{1,17},{... | collective-permute-start | bytes 98312 | tf_op jit(solution)/shard_map/ppermute | solution.py:293
  7.9 2.5 %gather_blocks_0.1.total_ref = f32[32,128,128]{2,1,0:T(8,128)S(1)} custom-call(s32[5,67]{1,0:T(8,128)S(1)} %concatenate.3.slots_ref, f32[5,32,128,128]{3,2,1,0:T(8,128)} %bitcast.14), custom_call_target="tpu_custom_call" | custom-call | flops 524288 | bytes 4194304 | tf_op jit(solution)/shard_map/gather_blocks_0/pallas_call | solution.py:67
  11.2 2.9 %collective-permute-start.3 = (f32[2,64,128]{2,1,0:T(8,128)S(1)}, f32[2,64,128]{2,1,0:T(8,128)S(1)}, u32[]{:S(2)}, u32[]{:S(2)}) collective-permute-start(f32[2,64,128]{2,1,0:T(8,128)S(1)} %combine.10.refs_0_), channel_id=1, source_target_pairs={{0,12},{1,13},{2,14},{3,15},{4,8},{5,9},{6,10},{7,11},{8,4},{9,5},... | collective-permute-start | bytes 196616 | tf_op jit(solution)/shard_map/ppermute | solution.py:311
  14.7 1.8 %collective-permute-done.3.refs_2_ = f32[2,64,128]{2,1,0:T(8,128)S(1)} collective-permute-done((f32[2,64,128]{2,1,0:T(8,128)S(1)}, f32[2,64,128]{2,1,0:T(8,128)S(1)}, u32[]{:S(2)}, u32[]{:S(2)}) %collective-permute-start.3) | collective-permute-done | bytes 65568 | tf_op jit(solution)/shard_map/ppermute | solution.py:311
  16.5 1.8 %collective-permute-done.2.refs_1_ = f32[2,64,128]{2,1,0:T(8,128)S(1)} collective-permute-done((f32[2,64,128]{2,1,0:T(8,128)S(1)}, f32[2,64,128]{2,1,0:T(8,128)S(1)}, u32[]{:S(2)}, u32[]{:S(2)}) %collective-permute-start.2) | collective-permute-done | bytes 65568 | tf_op jit(solution)/shard_map/ppermute | solution.py:311
  21.3 1.4 gather_blocks_1.1.refs_6_.total_ref
  24.8 4.1 %collective-permute-done.7.refs_1_ = f32[64,128]{1,0:T(8,128)S(1)} collective-permute-done((f32[64,128]{1,0:T(8,128)S(1)}, f32[64,128]{1,0:T(8,128)S(1)}, u32[]{:S(2)}, u32[]{:S(2)}) %collective-permute-start.7) | collective-permute-done | bytes 32800 | tf_op jit(solution)/shard_map/ppermute | solution.py:293
  29.3 1.9 %collective-permute-start.9 = (f32[2,64,128]{2,1,0:T(8,128)S(1)}, f32[2,64,128]{2,1,0:T(8,128)S(1)}, u32[]{:S(2)}, u32[]{:S(2)}) collective-permute-start(f32[2,64,128]{2,1,0:T(8,128)S(1)} %combine.11.refs_0_), channel_id=1, source_target_pairs={{0,8},{1,5},{2,10},{3,7},{4,12},{5,1},{6,14},{7,3},{8,0},{9,13},{1... | collective-permute-start | bytes 196616 | tf_op jit(solution)/shard_map/ppermute | solution.py:311
  31.2 1.2 collective-permute-start.8
  32.3 1.8 %collective-permute-done.10.refs_2_ = f32[2,64,128]{2,1,0:T(8,128)S(1)} collective-permute-done((f32[2,64,128]{2,1,0:T(8,128)S(1)}, f32[2,64,128]{2,1,0:T(8,128)S(1)}, u32[]{:S(2)}, u32[]{:S(2)}) %collective-permute-start.10) | collective-permute-done | bytes 65568 | tf_op jit(solution)/shard_map/ppermute | solution.py:311
  36.7 1.1 collective-permute-start.13
  37.8 1.4 gather_blocks_2.1.refs_6_.total_ref
  41.5 3.4 %collective-permute-done.14.refs_1_ = f32[64,128]{1,0:T(8,128)S(1)} collective-permute-done((f32[64,128]{1,0:T(8,128)S(1)}, f32[64,128]{1,0:T(8,128)S(1)}, u32[]{:S(2)}, u32[]{:S(2)}) %collective-permute-start.14) | collective-permute-done | bytes 32800 | tf_op jit(solution)/shard_map/ppermute | solution.py:293
  44.9 1.9 %collective-permute-start.17 = (f32[2,64,128]{2,1,0:T(8,128)S(1)}, f32[2,64,128]{2,1,0:T(8,128)S(1)}, u32[]{:S(2)}, u32[]{:S(2)}) collective-permute-start(f32[2,64,128]{2,1,0:T(8,128)S(1)} %combine.12.refs_0_), channel_id=1, source_target_pairs={{0,12},{1,13},{2,14},{3,15},{4,8},{5,9},{6,10},{7,11},{8,4},{9,5},... | collective-permute-start | bytes 196616 | tf_op jit(solution)/shard_map/ppermute | solution.py:311
  48.4 2.3 %collective-permute-done.17.refs_2_ = f32[2,64,128]{2,1,0:T(8,128)S(1)} collective-permute-done((f32[2,64,128]{2,1,0:T(8,128)S(1)}, f32[2,64,128]{2,1,0:T(8,128)S(1)}, u32[]{:S(2)}, u32[]{:S(2)}) %collective-permute-start.17) | collective-permute-done | bytes 65568 | tf_op jit(solution)/shard_map/ppermute | solution.py:311
  54.4 1.3 gather_blocks_3.1.refs_6_.total_ref
  57.8 3.7 %collective-permute-done.21.refs_1_ = f32[64,128]{1,0:T(8,128)S(1)} collective-permute-done((f32[64,128]{1,0:T(8,128)S(1)}, f32[64,128]{1,0:T(8,128)S(1)}, u32[]{:S(2)}, u32[]{:S(2)}) %collective-permute-start.21) | collective-permute-done | bytes 32800 | tf_op jit(solution)/shard_map/ppermute | solution.py:293
  62.3 1.1 collective-permute-start.23
  63.4 1.5 collective-permute-start.22
  65.0 1.7 collective-permute-done.24.refs_2_
  70.1 1.4 gather_blocks_4.1.refs_6_.total_ref
  73.7 4.0 %collective-permute-done.28.refs_1_ = f32[64,128]{1,0:T(8,128)S(1)} collective-permute-done((f32[64,128]{1,0:T(8,128)S(1)}, f32[64,128]{1,0:T(8,128)S(1)}, u32[]{:S(2)}, u32[]{:S(2)}) %collective-permute-start.28) | collective-permute-done | bytes 32800 | tf_op jit(solution)/shard_map/ppermute | solution.py:293
  77.7 1.4 collective-permute-start.31
  81.2 1.7 collective-permute-done.31.refs_2_
  84.6 1.2 collective-permute-start.33
  91.3 1.3 collective-permute-done.37.refs_1_
  93.0 1.5 collective-permute-done.35.refs_0_
  95.2 1.5 collective-permute-start.39
  96.7 1.7 collective-permute-start.40
  98.6 1.5 collective-permute-done.38.refs_1_
  100.9 1.2 collective-permute-start.41
  102.9 3.3 %collective-permute-done.41.refs_3_ = f32[64,128]{1,0:T(8,128)S(1)} collective-permute-done((f32[64,128]{1,0:T(8,128)S(1)}, f32[64,128]{1,0:T(8,128)S(1)}, u32[]{:S(2)}, u32[]{:S(2)}) %collective-permute-start.41) | collective-permute-done | bytes 32800 | tf_op jit(solution)/shard_map/ppermute | solution.py:293
  107.4 1.5 collective-permute-start.43
  109.5 1.5 collective-permute-done.44.refs_1_
  111.4 1.4 collective-permute-done.42.refs_0_
  113.1 1.1 collective-permute-start.45
  114.2 1.1 collective-permute-start.46
  115.3 1.3 collective-permute-start.47
  116.9 1.5 collective-permute-done.45.refs_1_
  118.5 1.1 collective-permute-done.47.refs_3_
  120.1 4.4 %collective-permute-done.48.refs_3_ = f32[64,128]{1,0:T(8,128)S(1)} collective-permute-done((f32[64,128]{1,0:T(8,128)S(1)}, f32[64,128]{1,0:T(8,128)S(1)}, u32[]{:S(2)}, u32[]{:S(2)}) %collective-permute-start.48) | collective-permute-done | bytes 32800 | tf_op jit(solution)/shard_map/ppermute | solution.py:293
  124.8 1.4 collective-permute-start.50
  126.9 1.4 collective-permute-done.51.refs_1_
  128.7 1.4 collective-permute-done.49.refs_0_
  130.9 1.8 %collective-permute-start.53 = (f32[2,64,128]{2,1,0:T(8,128)S(1)}, f32[2,64,128]{2,1,0:T(8,128)S(1)}, u32[]{:S(2)}, u32[]{:S(2)}) collective-permute-start(f32[2,64,128]{2,1,0:T(8,128)S(1)} %get-tuple-element.118), channel_id=1, source_target_pairs={{0,8},{1,5},{2,10},{3,7},{4,12},{5,1},{6,14},{7,3},{8,0},{9,13},{1... | collective-permute-start | bytes 196616 | tf_op jit(solution)/shard_map/ppermute | solution.py:311
  132.7 1.3 collective-permute-start.54
  134.2 1.5 collective-permute-done.52.refs_1_
  135.6 1.3 collective-permute-done.54.refs_3_
  137.7 4.1 %collective-permute-done.55.refs_3_ = f32[64,128]{1,0:T(8,128)S(1)} collective-permute-done((f32[64,128]{1,0:T(8,128)S(1)}, f32[64,128]{1,0:T(8,128)S(1)}, u32[]{:S(2)}, u32[]{:S(2)}) %collective-permute-start.55) | collective-permute-done | bytes 32800 | tf_op jit(solution)/shard_map/ppermute | solution.py:293
  142.1 1.4 collective-permute-start.57
  144.2 1.4 collective-permute-done.58.refs_1_
  146.1 1.4 collective-permute-done.56.refs_0_
  150.0 1.4 collective-permute-start.61
  151.5 1.5 collective-permute-done.59.refs_1_
  154.7 4.4 %collective-permute-done.62.refs_3_ = f32[64,128]{1,0:T(8,128)S(1)} collective-permute-done((f32[64,128]{1,0:T(8,128)S(1)}, f32[64,128]{1,0:T(8,128)S(1)}, u32[]{:S(2)}, u32[]{:S(2)}) %collective-permute-start.62) | collective-permute-done | bytes 32800 | tf_op jit(solution)/shard_map/ppermute | solution.py:293
  159.4 1.4 collective-permute-start.64
  161.5 1.4 collective-permute-done.65.refs_1_
  163.3 1.4 collective-permute-done.63.refs_0_
  165.5 1.8 %collective-permute-start.67 = (f32[2,64,128]{2,1,0:T(8,128)S(1)}, f32[2,64,128]{2,1,0:T(8,128)S(1)}, u32[]{:S(2)}, u32[]{:S(2)}) collective-permute-start(f32[2,64,128]{2,1,0:T(8,128)S(1)} %get-tuple-element.128), channel_id=1, source_target_pairs={{0,8},{1,5},{2,10},{3,7},{4,12},{5,1},{6,14},{7,3},{8,0},{9,13},{1... | collective-permute-start | bytes 196616 | tf_op jit(solution)/shard_map/ppermute | solution.py:311
  167.3 1.3 collective-permute-start.68
  168.8 1.5 collective-permute-done.66.refs_1_
  170.2 1.3 collective-permute-done.68.refs_3_
  172.3 4.1 %collective-permute-done.69.refs_3_ = f32[64,128]{1,0:T(8,128)S(1)} collective-permute-done((f32[64,128]{1,0:T(8,128)S(1)}, f32[64,128]{1,0:T(8,128)S(1)}, u32[]{:S(2)}, u32[]{:S(2)}) %collective-permute-start.69) | collective-permute-done | bytes 32800 | tf_op jit(solution)/shard_map/ppermute | solution.py:293
  (165 shorter events, 55.1 us)
Async XLA Ops:
  2.3 8.5 %collective-permute-start = (f32[64,128]{1,0:T(8,128)}, f32[64,128]{1,0:T(8,128)S(1)}, u32[]{:S(2)}, u32[]{:S(2)}) collective-permute-start(f32[64,128]{1,0:T(8,128)} %first_solve.1.refs_0_), channel_id=1, source_target_pairs={{0,16},{4,20},{8,24},{12,28},{16,0},{20,4},{24,8},{28,12},{1,17},{... | collective-permute-start | bytes 98312 | tf_op jit(solution)/shard_map/ppermute | solution.py:293
  11.2 5.3 %collective-permute-start.3 = (f32[2,64,128]{2,1,0:T(8,128)S(1)}, f32[2,64,128]{2,1,0:T(8,128)S(1)}, u32[]{:S(2)}, u32[]{:S(2)}) collective-permute-start(f32[2,64,128]{2,1,0:T(8,128)S(1)} %combine.10.refs_0_), channel_id=1, source_target_pairs={{0,12},{1,13},{2,14},{3,15},{4,8},{5,9},{6,10},{7,11},{8,4},{9,5},... | collective-permute-start | bytes 196616 | tf_op jit(solution)/shard_map/ppermute | solution.py:311
  14.1 4.3 %collective-permute-start.2 = (f32[2,64,128]{2,1,0:T(8,128)S(1)}, f32[2,64,128]{2,1,0:T(8,128)S(1)}, u32[]{:S(2)}, u32[]{:S(2)}) collective-permute-start(f32[2,64,128]{2,1,0:T(8,128)S(1)} %combine.10.refs_0_), channel_id=1, source_target_pairs={{0,8},{1,5},{2,10},{3,7},{4,12},{5,1},{6,14},{7,3},{8,0},{9,13},{1... | collective-permute-start | bytes 196616 | tf_op jit(solution)/shard_map/ppermute | solution.py:311
  14.1 4.8 %collective-permute-start.1 = (f32[2,64,128]{2,1,0:T(8,128)S(1)}, f32[2,64,128]{2,1,0:T(8,128)S(1)}, u32[]{:S(2)}, u32[]{:S(2)}) collective-permute-start(f32[2,64,128]{2,1,0:T(8,128)S(1)} %combine.10.refs_0_), channel_id=1, source_target_pairs={{0,4},{1,9},{2,6},{3,11},{4,0},{5,13},{6,2},{7,15},{8,12},{9,1},{1... | collective-permute-start | bytes 196616 | tf_op jit(solution)/shard_map/ppermute | solution.py:311
  19.1 3.7 %collective-permute-start.4 = (f32[64,128]{1,0:T(8,128)S(1)}, f32[64,128]{1,0:T(8,128)S(1)}, u32[]{:S(2)}, u32[]{:S(2)}) collective-permute-start(f32[64,128]{1,0:T(8,128)S(1)} %get-tuple-element.69), channel_id=1, source_target_pairs={{0,3},{1,2},{2,1},{3,0},{4,7},{5,6},{6,5},{7,4},{8,11},{9,10},{10,... | collective-permute-start | bytes 98312 | tf_op jit(solution)/shard_map/ppermute | solution.py:338
  19.2 4.3 %collective-permute-start.5 = (f32[64,128]{1,0:T(8,128)S(1)}, f32[64,128]{1,0:T(8,128)S(1)}, u32[]{:S(2)}, u32[]{:S(2)}) collective-permute-start(f32[64,128]{1,0:T(8,128)S(1)} %get-tuple-element.70), channel_id=1, source_target_pairs={{0,2},{1,3},{2,0},{3,1},{4,6},{5,7},{6,4},{7,5},{8,10},{9,11},{10,... | collective-permute-start | bytes 98312 | tf_op jit(solution)/shard_map/ppermute | solution.py:338
  23.6 5.2 %collective-permute-start.7 = (f32[64,128]{1,0:T(8,128)S(1)}, f32[64,128]{1,0:T(8,128)S(1)}, u32[]{:S(2)}, u32[]{:S(2)}) collective-permute-start(f32[64,128]{1,0:T(8,128)S(1)} %solve_up.5.refs_0_.refs_1_), channel_id=1, source_target_pairs={{0,16},{4,20},{8,24},{12,28},{16,0},{20,4},{24,8},{28,12},{1,17},{... | collective-permute-start | bytes 98312 | tf_op jit(solution)/shard_map/ppermute | solution.py:293
  28.8 5.3 %collective-permute-start.10 = (f32[2,64,128]{2,1,0:T(8,128)S(1)}, f32[2,64,128]{2,1,0:T(8,128)S(1)}, u32[]{:S(2)}, u32[]{:S(2)}) collective-permute-start(f32[2,64,128]{2,1,0:T(8,128)S(1)} %combine.11.refs_0_), channel_id=1, source_target_pairs={{0,12},{1,13},{2,14},{3,15},{4,8},{5,9},{6,10},{7,11},{8,4},{9,5},... | collective-permute-start | bytes 196616 | tf_op jit(solution)/shard_map/ppermute | solution.py:311
  29.3 5.3 %collective-permute-start.9 = (f32[2,64,128]{2,1,0:T(8,128)S(1)}, f32[2,64,128]{2,1,0:T(8,128)S(1)}, u32[]{:S(2)}, u32[]{:S(2)}) collective-permute-start(f32[2,64,128]{2,1,0:T(8,128)S(1)} %combine.11.refs_0_), channel_id=1, source_target_pairs={{0,8},{1,5},{2,10},{3,7},{4,12},{5,1},{6,14},{7,3},{8,0},{9,13},{1... | collective-permute-start | bytes 196616 | tf_op jit(solution)/shard_map/ppermute | solution.py:311
  31.2 4.3 %collective-permute-start.8 = (f32[2,64,128]{2,1,0:T(8,128)S(1)}, f32[2,64,128]{2,1,0:T(8,128)S(1)}, u32[]{:S(2)}, u32[]{:S(2)}) collective-permute-start(f32[2,64,128]{2,1,0:T(8,128)S(1)} %combine.11.refs_0_), channel_id=1, source_target_pairs={{0,4},{1,9},{2,6},{3,11},{4,0},{5,13},{6,2},{7,15},{8,12},{9,1},{1... | collective-permute-start | bytes 196616 | tf_op jit(solution)/shard_map/ppermute | solution.py:311
  35.6 3.6 %collective-permute-start.11 = (f32[64,128]{1,0:T(8,128)S(1)}, f32[64,128]{1,0:T(8,128)S(1)}, u32[]{:S(2)}, u32[]{:S(2)}) collective-permute-start(f32[64,128]{1,0:T(8,128)S(1)} %get-tuple-element.76), channel_id=1, source_target_pairs={{0,3},{1,2},{2,1},{3,0},{4,7},{5,6},{6,5},{7,4},{8,11},{9,10},{10,... | collective-permute-start | bytes 98312 | tf_op jit(solution)/shard_map/ppermute | solution.py:338
  35.7 4.1 %collective-permute-start.12 = (f32[64,128]{1,0:T(8,128)S(1)}, f32[64,128]{1,0:T(8,128)S(1)}, u32[]{:S(2)}, u32[]{:S(2)}) collective-permute-start(f32[64,128]{1,0:T(8,128)S(1)} %get-tuple-element.77), channel_id=1, source_target_pairs={{0,2},{1,3},{2,0},{3,1},{4,6},{5,7},{6,4},{7,5},{8,10},{9,11},{10,... | collective-permute-start | bytes 98312 | tf_op jit(solution)/shard_map/ppermute | solution.py:338
  40.0 4.9 %collective-permute-start.14 = (f32[64,128]{1,0:T(8,128)S(1)}, f32[64,128]{1,0:T(8,128)S(1)}, u32[]{:S(2)}, u32[]{:S(2)}) collective-permute-start(f32[64,128]{1,0:T(8,128)S(1)} %solve_up.6.refs_0_.refs_2_), channel_id=1, source_target_pairs={{0,16},{4,20},{8,24},{12,28},{16,0},{20,4},{24,8},{28,12},{1,17},{... | collective-permute-start | bytes 98312 | tf_op jit(solution)/shard_map/ppermute | solution.py:293
  44.9 5.8 %collective-permute-start.17 = (f32[2,64,128]{2,1,0:T(8,128)S(1)}, f32[2,64,128]{2,1,0:T(8,128)S(1)}, u32[]{:S(2)}, u32[]{:S(2)}) collective-permute-start(f32[2,64,128]{2,1,0:T(8,128)S(1)} %combine.12.refs_0_), channel_id=1, source_target_pairs={{0,12},{1,13},{2,14},{3,15},{4,8},{5,9},{6,10},{7,11},{8,4},{9,5},... | collective-permute-start | bytes 196616 | tf_op jit(solution)/shard_map/ppermute | solution.py:311
  46.8 4.3 %collective-permute-start.16 = (f32[2,64,128]{2,1,0:T(8,128)S(1)}, f32[2,64,128]{2,1,0:T(8,128)S(1)}, u32[]{:S(2)}, u32[]{:S(2)}) collective-permute-start(f32[2,64,128]{2,1,0:T(8,128)S(1)} %combine.12.refs_0_), channel_id=1, source_target_pairs={{0,8},{1,5},{2,10},{3,7},{4,12},{5,1},{6,14},{7,3},{8,0},{9,13},{1... | collective-permute-start | bytes 196616 | tf_op jit(solution)/shard_map/ppermute | solution.py:311
  47.8 4.3 %collective-permute-start.15 = (f32[2,64,128]{2,1,0:T(8,128)S(1)}, f32[2,64,128]{2,1,0:T(8,128)S(1)}, u32[]{:S(2)}, u32[]{:S(2)}) collective-permute-start(f32[2,64,128]{2,1,0:T(8,128)S(1)} %combine.12.refs_0_), channel_id=1, source_target_pairs={{0,4},{1,9},{2,6},{3,11},{4,0},{5,13},{6,2},{7,15},{8,12},{9,1},{1... | collective-permute-start | bytes 196616 | tf_op jit(solution)/shard_map/ppermute | solution.py:311
  52.2 3.5 %collective-permute-start.18 = (f32[64,128]{1,0:T(8,128)S(1)}, f32[64,128]{1,0:T(8,128)S(1)}, u32[]{:S(2)}, u32[]{:S(2)}) collective-permute-start(f32[64,128]{1,0:T(8,128)S(1)} %get-tuple-element.83), channel_id=1, source_target_pairs={{0,3},{1,2},{2,1},{3,0},{4,7},{5,6},{6,5},{7,4},{8,11},{9,10},{10,... | collective-permute-start | bytes 98312 | tf_op jit(solution)/shard_map/ppermute | solution.py:338
  52.3 4.2 %collective-permute-start.19 = (f32[64,128]{1,0:T(8,128)S(1)}, f32[64,128]{1,0:T(8,128)S(1)}, u32[]{:S(2)}, u32[]{:S(2)}) collective-permute-start(f32[64,128]{1,0:T(8,128)S(1)} %get-tuple-element.84), channel_id=1, source_target_pairs={{0,2},{1,3},{2,0},{3,1},{4,6},{5,7},{6,4},{7,5},{8,10},{9,11},{10,... | collective-permute-start | bytes 98312 | tf_op jit(solution)/shard_map/ppermute | solution.py:338
  56.6 4.9 %collective-permute-start.21 = (f32[64,128]{1,0:T(8,128)S(1)}, f32[64,128]{1,0:T(8,128)S(1)}, u32[]{:S(2)}, u32[]{:S(2)}) collective-permute-start(f32[64,128]{1,0:T(8,128)S(1)} %solve_up.7.refs_0_.refs_3_), channel_id=1, source_target_pairs={{0,16},{4,20},{8,24},{12,28},{16,0},{20,4},{24,8},{28,12},{1,17},{... | collective-permute-start | bytes 98312 | tf_op jit(solution)/shard_map/ppermute | solution.py:293
  61.5 5.2 %collective-permute-start.24 = (f32[2,64,128]{2,1,0:T(8,128)S(1)}, f32[2,64,128]{2,1,0:T(8,128)S(1)}, u32[]{:S(2)}, u32[]{:S(2)}) collective-permute-start(f32[2,64,128]{2,1,0:T(8,128)S(1)} %combine.13.refs_0_), channel_id=1, source_target_pairs={{0,12},{1,13},{2,14},{3,15},{4,8},{5,9},{6,10},{7,11},{8,4},{9,5},... | collective-permute-start | bytes 196616 | tf_op jit(solution)/shard_map/ppermute | solution.py:311
  62.3 4.6 %collective-permute-start.23 = (f32[2,64,128]{2,1,0:T(8,128)S(1)}, f32[2,64,128]{2,1,0:T(8,128)S(1)}, u32[]{:S(2)}, u32[]{:S(2)}) collective-permute-start(f32[2,64,128]{2,1,0:T(8,128)S(1)} %combine.13.refs_0_), channel_id=1, source_target_pairs={{0,8},{1,5},{2,10},{3,7},{4,12},{5,1},{6,14},{7,3},{8,0},{9,13},{1... | collective-permute-start | bytes 196616 | tf_op jit(solution)/shard_map/ppermute | solution.py:311
  63.4 4.3 %collective-permute-start.22 = (f32[2,64,128]{2,1,0:T(8,128)S(1)}, f32[2,64,128]{2,1,0:T(8,128)S(1)}, u32[]{:S(2)}, u32[]{:S(2)}) collective-permute-start(f32[2,64,128]{2,1,0:T(8,128)S(1)} %combine.13.refs_0_), channel_id=1, source_target_pairs={{0,4},{1,9},{2,6},{3,11},{4,0},{5,13},{6,2},{7,15},{8,12},{9,1},{1... | collective-permute-start | bytes 196616 | tf_op jit(solution)/shard_map/ppermute | solution.py:311
  67.9 3.6 %collective-permute-start.25 = (f32[64,128]{1,0:T(8,128)S(1)}, f32[64,128]{1,0:T(8,128)S(1)}, u32[]{:S(2)}, u32[]{:S(2)}) collective-permute-start(f32[64,128]{1,0:T(8,128)S(1)} %get-tuple-element.90), channel_id=1, source_target_pairs={{0,3},{1,2},{2,1},{3,0},{4,7},{5,6},{6,5},{7,4},{8,11},{9,10},{10,... | collective-permute-start | bytes 98312 | tf_op jit(solution)/shard_map/ppermute | solution.py:338
  68.0 4.3 %collective-permute-start.26 = (f32[64,128]{1,0:T(8,128)S(1)}, f32[64,128]{1,0:T(8,128)S(1)}, u32[]{:S(2)}, u32[]{:S(2)}) collective-permute-start(f32[64,128]{1,0:T(8,128)S(1)} %get-tuple-element.91), channel_id=1, source_target_pairs={{0,2},{1,3},{2,0},{3,1},{4,6},{5,7},{6,4},{7,5},{8,10},{9,11},{10,... | collective-permute-start | bytes 98312 | tf_op jit(solution)/shard_map/ppermute | solution.py:338
  72.5 5.2 %collective-permute-start.28 = (f32[64,128]{1,0:T(8,128)S(1)}, f32[64,128]{1,0:T(8,128)S(1)}, u32[]{:S(2)}, u32[]{:S(2)}) collective-permute-start(f32[64,128]{1,0:T(8,128)S(1)} %solve_up.8.refs_0_.refs_4_), channel_id=1, source_target_pairs={{0,16},{4,20},{8,24},{12,28},{16,0},{20,4},{24,8},{28,12},{1,17},{... | collective-permute-start | bytes 98312 | tf_op jit(solution)/shard_map/ppermute | solution.py:293
  77.7 5.2 %collective-permute-start.31 = (f32[2,64,128]{2,1,0:T(8,128)S(1)}, f32[2,64,128]{2,1,0:T(8,128)S(1)}, u32[]{:S(2)}, u32[]{:S(2)}) collective-permute-start(f32[2,64,128]{2,1,0:T(8,128)S(1)} %combine.14.refs_0_), channel_id=1, source_target_pairs={{0,12},{1,13},{2,14},{3,15},{4,8},{5,9},{6,10},{7,11},{8,4},{9,5},... | collective-permute-start | bytes 196616 | tf_op jit(solution)/shard_map/ppermute | solution.py:311
  79.1 4.3 %collective-permute-start.30 = (f32[2,64,128]{2,1,0:T(8,128)S(1)}, f32[2,64,128]{2,1,0:T(8,128)S(1)}, u32[]{:S(2)}, u32[]{:S(2)}) collective-permute-start(f32[2,64,128]{2,1,0:T(8,128)S(1)} %combine.14.refs_0_), channel_id=1, source_target_pairs={{0,8},{1,5},{2,10},{3,7},{4,12},{5,1},{6,14},{7,3},{8,0},{9,13},{1... | collective-permute-start | bytes 196616 | tf_op jit(solution)/shard_map/ppermute | solution.py:311
  80.1 4.3 %collective-permute-start.29 = (f32[2,64,128]{2,1,0:T(8,128)S(1)}, f32[2,64,128]{2,1,0:T(8,128)S(1)}, u32[]{:S(2)}, u32[]{:S(2)}) collective-permute-start(f32[2,64,128]{2,1,0:T(8,128)S(1)} %combine.14.refs_0_), channel_id=1, source_target_pairs={{0,4},{1,9},{2,6},{3,11},{4,0},{5,13},{6,2},{7,15},{8,12},{9,1},{1... | collective-permute-start | bytes 196616 | tf_op jit(solution)/shard_map/ppermute | solution.py:311
  84.5 3.4 %collective-permute-start.32 = (f32[64,128]{1,0:T(8,128)S(1)}, f32[64,128]{1,0:T(8,128)S(1)}, u32[]{:S(2)}, u32[]{:S(2)}) collective-permute-start(f32[64,128]{1,0:T(8,128)S(1)} %get-tuple-element.97), channel_id=1, source_target_pairs={{0,3},{1,2},{2,1},{3,0},{4,7},{5,6},{6,5},{7,4},{8,11},{9,10},{10,... | collective-permute-start | bytes 98312 | tf_op jit(solution)/shard_map/ppermute | solution.py:338
  84.6 4.2 %collective-permute-start.33 = (f32[64,128]{1,0:T(8,128)S(1)}, f32[64,128]{1,0:T(8,128)S(1)}, u32[]{:S(2)}, u32[]{:S(2)}) collective-permute-start(f32[64,128]{1,0:T(8,128)S(1)} %get-tuple-element.98), channel_id=1, source_target_pairs={{0,2},{1,3},{2,0},{3,1},{4,6},{5,7},{6,4},{7,5},{8,10},{9,11},{10,... | collective-permute-start | bytes 98312 | tf_op jit(solution)/shard_map/ppermute | solution.py:338
  89.1 3.5 %collective-permute-start.37 = (f32[64,128]{1,0:T(8,128)S(1)}, f32[64,128]{1,0:T(8,128)S(1)}, u32[]{:S(2)}, u32[]{:S(2)}) collective-permute-start(f32[64,128]{1,0:T(8,128)S(1)} %solve_down.6.refs_0_.refs_5_), channel_id=1, source_target_pairs={{0,3},{1,2},{2,1},{3,0},{4,7},{5,6},{6,5},{7,4},{8,11},{9,10},{10,... | collective-permute-start | bytes 98312 | tf_op jit(solution)/shard_map/ppermute | solution.py:338
  90.6 3.9 %collective-permute-start.35 = (f32[64,128]{1,0:T(8,128)S(1)}, f32[64,128]{1,0:T(8,128)S(1)}, u32[]{:S(2)}, u32[]{:S(2)}) collective-permute-start(f32[64,128]{1,0:T(8,128)S(1)} %solve_down.6.refs_0_.refs_5_), channel_id=1, source_target_pairs={{0,2},{1,3},{2,0},{3,1},{4,6},{5,7},{6,4},{7,5},{8,10},{9,11},{10,... | collective-permute-start | bytes 98312 | tf_op jit(solution)/shard_map/ppermute | solution.py:338
  94.8 5.2 %collective-permute-start.38 = (f32[2,64,128]{2,1,0:T(8,128)S(1)}, f32[2,64,128]{2,1,0:T(8,128)S(1)}, u32[]{:S(2)}, u32[]{:S(2)}) collective-permute-start(f32[2,64,128]{2,1,0:T(8,128)S(1)} %get-tuple-element.107), channel_id=1, source_target_pairs={{0,12},{1,13},{2,14},{3,15},{4,8},{5,9},{6,10},{7,11},{8,4},{9,5},... | collective-permute-start | bytes 196616 | tf_op jit(solution)/shard_map/ppermute | solution.py:311
  95.2 5.1 %collective-permute-start.39 = (f32[2,64,128]{2,1,0:T(8,128)S(1)}, f32[2,64,128]{2,1,0:T(8,128)S(1)}, u32[]{:S(2)}, u32[]{:S(2)}) collective-permute-start(f32[2,64,128]{2,1,0:T(8,128)S(1)} %get-tuple-element.108), channel_id=1, source_target_pairs={{0,8},{1,5},{2,10},{3,7},{4,12},{5,1},{6,14},{7,3},{8,0},{9,13},{1... | collective-permute-start | bytes 196616 | tf_op jit(solution)/shard_map/ppermute | solution.py:311
  96.7 4.3 %collective-permute-start.40 = (f32[2,64,128]{2,1,0:T(8,128)S(1)}, f32[2,64,128]{2,1,0:T(8,128)S(1)}, u32[]{:S(2)}, u32[]{:S(2)}) collective-permute-start(f32[2,64,128]{2,1,0:T(8,128)S(1)} %get-tuple-element.109), channel_id=1, source_target_pairs={{0,4},{1,9},{2,6},{3,11},{4,0},{5,13},{6,2},{7,15},{8,12},{9,1},{1... | collective-permute-start | bytes 196616 | tf_op jit(solution)/shard_map/ppermute | solution.py:311
  100.9 5.2 %collective-permute-start.41 = (f32[64,128]{1,0:T(8,128)S(1)}, f32[64,128]{1,0:T(8,128)S(1)}, u32[]{:S(2)}, u32[]{:S(2)}) collective-permute-start(f32[64,128]{1,0:T(8,128)S(1)} %get-tuple-element.111), channel_id=1, source_target_pairs={{0,16},{4,20},{8,24},{12,28},{16,0},{20,4},{24,8},{28,12},{1,17},{... | collective-permute-start | bytes 98312 | tf_op jit(solution)/shard_map/ppermute | solution.py:293
  107.3 3.7 %collective-permute-start.44 = (f32[64,128]{1,0:T(8,128)S(1)}, f32[64,128]{1,0:T(8,128)S(1)}, u32[]{:S(2)}, u32[]{:S(2)}) collective-permute-start(f32[64,128]{1,0:T(8,128)S(1)} %solve_down.7.refs_0_.refs_4_), channel_id=1, source_target_pairs={{0,3},{1,2},{2,1},{3,0},{4,7},{5,6},{6,5},{7,4},{8,11},{9,10},{10,... | collective-permute-start | bytes 98312 | tf_op jit(solution)/shard_map/ppermute | solution.py:338
  107.4 4.0 %collective-permute-start.43 = (f32[64,128]{1,0:T(8,128)S(1)}, f32[64,128]{1,0:T(8,128)S(1)}, u32[]{:S(2)}, u32[]{:S(2)}) collective-permute-start(f32[64,128]{1,0:T(8,128)S(1)} %solve_down.7.refs_0_.refs_4_), channel_id=1, source_target_pairs={{0,1},{1,0},{2,3},{3,2},{4,5},{5,4},{6,7},{7,6},{8,9},{9,8},{10,11... | collective-permute-start | bytes 98312 | tf_op jit(solution)/shard_map/ppermute | solution.py:338
  108.9 3.9 %collective-permute-start.42 = (f32[64,128]{1,0:T(8,128)S(1)}, f32[64,128]{1,0:T(8,128)S(1)}, u32[]{:S(2)}, u32[]{:S(2)}) collective-permute-start(f32[64,128]{1,0:T(8,128)S(1)} %solve_down.7.refs_0_.refs_4_), channel_id=1, source_target_pairs={{0,2},{1,3},{2,0},{3,1},{4,6},{5,7},{6,4},{7,5},{8,10},{9,11},{10,... | collective-permute-start | bytes 98312 | tf_op jit(solution)/shard_map/ppermute | solution.py:338
  113.1 5.2 %collective-permute-start.45 = (f32[2,64,128]{2,1,0:T(8,128)S(1)}, f32[2,64,128]{2,1,0:T(8,128)S(1)}, u32[]{:S(2)}, u32[]{:S(2)}) collective-permute-start(f32[2,64,128]{2,1,0:T(8,128)S(1)} %get-tuple-element.112), channel_id=1, source_target_pairs={{0,12},{1,13},{2,14},{3,15},{4,8},{5,9},{6,10},{7,11},{8,4},{9,5},... | collective-permute-start | bytes 196616 | tf_op jit(solution)/shard_map/ppermute | solution.py:311
  114.2 4.3 %collective-permute-start.46 = (f32[2,64,128]{2,1,0:T(8,128)S(1)}, f32[2,64,128]{2,1,0:T(8,128)S(1)}, u32[]{:S(2)}, u32[]{:S(2)}) collective-permute-start(f32[2,64,128]{2,1,0:T(8,128)S(1)} %get-tuple-element.113), channel_id=1, source_target_pairs={{0,8},{1,5},{2,10},{3,7},{4,12},{5,1},{6,14},{7,3},{8,0},{9,13},{1... | collective-permute-start | bytes 196616 | tf_op jit(solution)/shard_map/ppermute | solution.py:311
  115.3 4.3 %collective-permute-start.47 = (f32[2,64,128]{2,1,0:T(8,128)S(1)}, f32[2,64,128]{2,1,0:T(8,128)S(1)}, u32[]{:S(2)}, u32[]{:S(2)}) collective-permute-start(f32[2,64,128]{2,1,0:T(8,128)S(1)} %get-tuple-element.114), channel_id=1, source_target_pairs={{0,4},{1,9},{2,6},{3,11},{4,0},{5,13},{6,2},{7,15},{8,12},{9,1},{1... | collective-permute-start | bytes 196616 | tf_op jit(solution)/shard_map/ppermute | solution.py:311
  119.6 4.9 %collective-permute-start.48 = (f32[64,128]{1,0:T(8,128)S(1)}, f32[64,128]{1,0:T(8,128)S(1)}, u32[]{:S(2)}, u32[]{:S(2)}) collective-permute-start(f32[64,128]{1,0:T(8,128)S(1)} %get-tuple-element.116), channel_id=1, source_target_pairs={{0,16},{4,20},{8,24},{12,28},{16,0},{20,4},{24,8},{28,12},{1,17},{... | collective-permute-start | bytes 98312 | tf_op jit(solution)/shard_map/ppermute | solution.py:293
  124.7 3.6 %collective-permute-start.51 = (f32[64,128]{1,0:T(8,128)S(1)}, f32[64,128]{1,0:T(8,128)S(1)}, u32[]{:S(2)}, u32[]{:S(2)}) collective-permute-start(f32[64,128]{1,0:T(8,128)S(1)} %solve_down.8.refs_0_.refs_3_), channel_id=1, source_target_pairs={{0,3},{1,2},{2,1},{3,0},{4,7},{5,6},{6,5},{7,4},{8,11},{9,10},{10,... | collective-permute-start | bytes 98312 | tf_op jit(solution)/shard_map/ppermute | solution.py:338
  124.8 3.9 %collective-permute-start.50 = (f32[64,128]{1,0:T(8,128)S(1)}, f32[64,128]{1,0:T(8,128)S(1)}, u32[]{:S(2)}, u32[]{:S(2)}) collective-permute-start(f32[64,128]{1,0:T(8,128)S(1)} %solve_down.8.refs_0_.refs_3_), channel_id=1, source_target_pairs={{0,1},{1,0},{2,3},{3,2},{4,5},{5,4},{6,7},{7,6},{8,9},{9,8},{10,11... | collective-permute-start | bytes 98312 | tf_op jit(solution)/shard_map/ppermute | solution.py:338
  126.1 3.9 %collective-permute-start.49 = (f32[64,128]{1,0:T(8,128)S(1)}, f32[64,128]{1,0:T(8,128)S(1)}, u32[]{:S(2)}, u32[]{:S(2)}) collective-permute-start(f32[64,128]{1,0:T(8,128)S(1)} %solve_down.8.refs_0_.refs_3_), channel_id=1, source_target_pairs={{0,2},{1,3},{2,0},{3,1},{4,6},{5,7},{6,4},{7,5},{8,10},{9,11},{10,... | collective-permute-start | bytes 98312 | tf_op jit(solution)/shard_map/ppermute | solution.py:338
  130.4 5.2 %collective-permute-start.52 = (f32[2,64,128]{2,1,0:T(8,128)S(1)}, f32[2,64,128]{2,1,0:T(8,128)S(1)}, u32[]{:S(2)}, u32[]{:S(2)}) collective-permute-start(f32[2,64,128]{2,1,0:T(8,128)S(1)} %get-tuple-element.117), channel_id=1, source_target_pairs={{0,12},{1,13},{2,14},{3,15},{4,8},{5,9},{6,10},{7,11},{8,4},{9,5},... | collective-permute-start | bytes 196616 | tf_op jit(solution)/shard_map/ppermute | solution.py:311
  130.9 4.8 %collective-permute-start.53 = (f32[2,64,128]{2,1,0:T(8,128)S(1)}, f32[2,64,128]{2,1,0:T(8,128)S(1)}, u32[]{:S(2)}, u32[]{:S(2)}) collective-permute-start(f32[2,64,128]{2,1,0:T(8,128)S(1)} %get-tuple-element.118), channel_id=1, source_target_pairs={{0,8},{1,5},{2,10},{3,7},{4,12},{5,1},{6,14},{7,3},{8,0},{9,13},{1... | collective-permute-start | bytes 196616 | tf_op jit(solution)/shard_map/ppermute | solution.py:311
  132.7 4.3 %collective-permute-start.54 = (f32[2,64,128]{2,1,0:T(8,128)S(1)}, f32[2,64,128]{2,1,0:T(8,128)S(1)}, u32[]{:S(2)}, u32[]{:S(2)}) collective-permute-start(f32[2,64,128]{2,1,0:T(8,128)S(1)} %get-tuple-element.119), channel_id=1, source_target_pairs={{0,4},{1,9},{2,6},{3,11},{4,0},{5,13},{6,2},{7,15},{8,12},{9,1},{1... | collective-permute-start | bytes 196616 | tf_op jit(solution)/shard_map/ppermute | solution.py:311
  137.0 4.9 %collective-permute-start.55 = (f32[64,128]{1,0:T(8,128)S(1)}, f32[64,128]{1,0:T(8,128)S(1)}, u32[]{:S(2)}, u32[]{:S(2)}) collective-permute-start(f32[64,128]{1,0:T(8,128)S(1)} %get-tuple-element.121), channel_id=1, source_target_pairs={{0,16},{4,20},{8,24},{12,28},{16,0},{20,4},{24,8},{28,12},{1,17},{... | collective-permute-start | bytes 98312 | tf_op jit(solution)/shard_map/ppermute | solution.py:293
  142.0 3.6 %collective-permute-start.58 = (f32[64,128]{1,0:T(8,128)S(1)}, f32[64,128]{1,0:T(8,128)S(1)}, u32[]{:S(2)}, u32[]{:S(2)}) collective-permute-start(f32[64,128]{1,0:T(8,128)S(1)} %solve_down.9.refs_0_.refs_2_), channel_id=1, source_target_pairs={{0,3},{1,2},{2,1},{3,0},{4,7},{5,6},{6,5},{7,4},{8,11},{9,10},{10,... | collective-permute-start | bytes 98312 | tf_op jit(solution)/shard_map/ppermute | solution.py:338
  142.1 4.0 %collective-permute-start.57 = (f32[64,128]{1,0:T(8,128)S(1)}, f32[64,128]{1,0:T(8,128)S(1)}, u32[]{:S(2)}, u32[]{:S(2)}) collective-permute-start(f32[64,128]{1,0:T(8,128)S(1)} %solve_down.9.refs_0_.refs_2_), channel_id=1, source_target_pairs={{0,1},{1,0},{2,3},{3,2},{4,5},{5,4},{6,7},{7,6},{8,9},{9,8},{10,11... | collective-permute-start | bytes 98312 | tf_op jit(solution)/shard_map/ppermute | solution.py:338
  143.5 3.9 %collective-permute-start.56 = (f32[64,128]{1,0:T(8,128)S(1)}, f32[64,128]{1,0:T(8,128)S(1)}, u32[]{:S(2)}, u32[]{:S(2)}) collective-permute-start(f32[64,128]{1,0:T(8,128)S(1)} %solve_down.9.refs_0_.refs_2_), channel_id=1, source_target_pairs={{0,2},{1,3},{2,0},{3,1},{4,6},{5,7},{6,4},{7,5},{8,10},{9,11},{10,... | collective-permute-start | bytes 98312 | tf_op jit(solution)/shard_map/ppermute | solution.py:338
  147.8 5.2 %collective-permute-start.59 = (f32[2,64,128]{2,1,0:T(8,128)S(1)}, f32[2,64,128]{2,1,0:T(8,128)S(1)}, u32[]{:S(2)}, u32[]{:S(2)}) collective-permute-start(f32[2,64,128]{2,1,0:T(8,128)S(1)} %get-tuple-element.122), channel_id=1, source_target_pairs={{0,12},{1,13},{2,14},{3,15},{4,8},{5,9},{6,10},{7,11},{8,4},{9,5},... | collective-permute-start | bytes 196616 | tf_op jit(solution)/shard_map/ppermute | solution.py:311
  148.9 4.3 %collective-permute-start.60 = (f32[2,64,128]{2,1,0:T(8,128)S(1)}, f32[2,64,128]{2,1,0:T(8,128)S(1)}, u32[]{:S(2)}, u32[]{:S(2)}) collective-permute-start(f32[2,64,128]{2,1,0:T(8,128)S(1)} %get-tuple-element.123), channel_id=1, source_target_pairs={{0,8},{1,5},{2,10},{3,7},{4,12},{5,1},{6,14},{7,3},{8,0},{9,13},{1... | collective-permute-start | bytes 196616 | tf_op jit(solution)/shard_map/ppermute | solution.py:311
  150.0 4.3 %collective-permute-start.61 = (f32[2,64,128]{2,1,0:T(8,128)S(1)}, f32[2,64,128]{2,1,0:T(8,128)S(1)}, u32[]{:S(2)}, u32[]{:S(2)}) collective-permute-start(f32[2,64,128]{2,1,0:T(8,128)S(1)} %get-tuple-element.124), channel_id=1, source_target_pairs={{0,4},{1,9},{2,6},{3,11},{4,0},{5,13},{6,2},{7,15},{8,12},{9,1},{1... | collective-permute-start | bytes 196616 | tf_op jit(solution)/shard_map/ppermute | solution.py:311
  154.2 4.9 %collective-permute-start.62 = (f32[64,128]{1,0:T(8,128)S(1)}, f32[64,128]{1,0:T(8,128)S(1)}, u32[]{:S(2)}, u32[]{:S(2)}) collective-permute-start(f32[64,128]{1,0:T(8,128)S(1)} %get-tuple-element.126), channel_id=1, source_target_pairs={{0,16},{4,20},{8,24},{12,28},{16,0},{20,4},{24,8},{28,12},{1,17},{... | collective-permute-start | bytes 98312 | tf_op jit(solution)/shard_map/ppermute | solution.py:293
  159.3 3.6 %collective-permute-start.65 = (f32[64,128]{1,0:T(8,128)S(1)}, f32[64,128]{1,0:T(8,128)S(1)}, u32[]{:S(2)}, u32[]{:S(2)}) collective-permute-start(f32[64,128]{1,0:T(8,128)S(1)} %solve_down.10.refs_0_.refs_1_), channel_id=1, source_target_pairs={{0,3},{1,2},{2,1},{3,0},{4,7},{5,6},{6,5},{7,4},{8,11},{9,10},{10,... | collective-permute-start | bytes 98312 | tf_op jit(solution)/shard_map/ppermute | solution.py:338
  159.4 3.9 %collective-permute-start.64 = (f32[64,128]{1,0:T(8,128)S(1)}, f32[64,128]{1,0:T(8,128)S(1)}, u32[]{:S(2)}, u32[]{:S(2)}) collective-permute-start(f32[64,128]{1,0:T(8,128)S(1)} %solve_down.10.refs_0_.refs_1_), channel_id=1, source_target_pairs={{0,1},{1,0},{2,3},{3,2},{4,5},{5,4},{6,7},{7,6},{8,9},{9,8},{10,11... | collective-permute-start | bytes 98312 | tf_op jit(solution)/shard_map/ppermute | solution.py:338
  160.8 3.9 %collective-permute-start.63 = (f32[64,128]{1,0:T(8,128)S(1)}, f32[64,128]{1,0:T(8,128)S(1)}, u32[]{:S(2)}, u32[]{:S(2)}) collective-permute-start(f32[64,128]{1,0:T(8,128)S(1)} %solve_down.10.refs_0_.refs_1_), channel_id=1, source_target_pairs={{0,2},{1,3},{2,0},{3,1},{4,6},{5,7},{6,4},{7,5},{8,10},{9,11},{10,... | collective-permute-start | bytes 98312 | tf_op jit(solution)/shard_map/ppermute | solution.py:338
  165.0 5.2 %collective-permute-start.66 = (f32[2,64,128]{2,1,0:T(8,128)S(1)}, f32[2,64,128]{2,1,0:T(8,128)S(1)}, u32[]{:S(2)}, u32[]{:S(2)}) collective-permute-start(f32[2,64,128]{2,1,0:T(8,128)S(1)} %get-tuple-element.127), channel_id=1, source_target_pairs={{0,12},{1,13},{2,14},{3,15},{4,8},{5,9},{6,10},{7,11},{8,4},{9,5},... | collective-permute-start | bytes 196616 | tf_op jit(solution)/shard_map/ppermute | solution.py:311
  165.5 4.8 %collective-permute-start.67 = (f32[2,64,128]{2,1,0:T(8,128)S(1)}, f32[2,64,128]{2,1,0:T(8,128)S(1)}, u32[]{:S(2)}, u32[]{:S(2)}) collective-permute-start(f32[2,64,128]{2,1,0:T(8,128)S(1)} %get-tuple-element.128), channel_id=1, source_target_pairs={{0,8},{1,5},{2,10},{3,7},{4,12},{5,1},{6,14},{7,3},{8,0},{9,13},{1... | collective-permute-start | bytes 196616 | tf_op jit(solution)/shard_map/ppermute | solution.py:311
  167.3 4.3 %collective-permute-start.68 = (f32[2,64,128]{2,1,0:T(8,128)S(1)}, f32[2,64,128]{2,1,0:T(8,128)S(1)}, u32[]{:S(2)}, u32[]{:S(2)}) collective-permute-start(f32[2,64,128]{2,1,0:T(8,128)S(1)} %get-tuple-element.129), channel_id=1, source_target_pairs={{0,4},{1,9},{2,6},{3,11},{4,0},{5,13},{6,2},{7,15},{8,12},{9,1},{1... | collective-permute-start | bytes 196616 | tf_op jit(solution)/shard_map/ppermute | solution.py:311
  171.6 4.9 %collective-permute-start.69 = (f32[64,128]{1,0:T(8,128)S(1)}, f32[64,128]{1,0:T(8,128)S(1)}, u32[]{:S(2)}, u32[]{:S(2)}) collective-permute-start(f32[64,128]{1,0:T(8,128)S(1)} %get-tuple-element.131), channel_id=1, source_target_pairs={{0,16},{4,20},{8,24},{12,28},{16,0},{20,4},{24,8},{28,12},{1,17},{... | collective-permute-start | bytes 98312 | tf_op jit(solution)/shard_map/ppermute | solution.py:293
  (13 other events, 60.9 us)

commit v13 on v8

--- a/solution.py
+++ b/solution.py
@@ -50,6 +50,7 @@
         pl.when(lax.rem(slot, chunk) == 0)(fetch(slot // chunk).wait)
         source = slots_ref[level, slot_count + slot]
         near = lax.rem(source, half) ^ lax.rem(row, half)
+        near = jnp.where(lax.rem(col, 2) == 1, mirrored(near, half), near)
         below = near * 2 + ((source // half) ^ side)
         above = slots_ref[level, slot] ^ col
         total[below * n_col + above] += slots[slot]
@@ -283,16 +284,39 @@
     return lax.ppermute(segment, axis, [(i, i ^ (size // 2)) for i in range(size)])
 
 
+def mirrored(number, size):
+    bits = size.bit_length() - 1
+    return sum(((number >> bit) & 1) << (bits - 1 - bit) for bit in range(bits))
+
+
+def near_exchange(message, d):
+    n_row, n_col = lax.axis_size("row"), lax.axis_size("col")
+    half = n_row // 2
+    pairs = []
+    for row in range(n_row):
+        for col in range(n_col):
+            partner = row ^ (mirrored(d, half) if col % 2 else d)
+            pairs.append((row * n_col + col, partner * n_col + col))
+    return lax.ppermute(message, ("row", "col"), pairs)
+
+
 def gather_row(segment, after):
     half = lax.axis_size("row") // 2
+    last = half - 1
     received = far_exchange(segment, "row")
+    (again,) = combine([[[(segment, None)]]], after)
+    early = near_exchange(again, last)
+    late = near_exchange(received, last)
     (both,) = combine([[[(segment, None)], [(received, None)]]], after)
-    messages = exchange_each([both] * half, "row")
-    return [(message, side) for message in messages for side in range(2)]
+    held = {d: near_exchange(both, d) for d in reversed(range(1, last))}
+    held[0] = both
+    pieces = [(held[d], side) for d in range(last) for side in range(2)]
+    return pieces + [(early, None), (late, None)]
 
 
 def deliver_row(messages):
-    received = exchange_each(messages, "row")
+    received = {d: near_exchange(messages[d], d) for d in reversed(range(1, len(messages)))}
+    received = [messages[0]] + [received[d] for d in range(1, len(messages))]
     mine, other = combine(
         [
             [[(message, side) for message in [received[0], *reversed(received[1:])]]]
@@ -342,7 +366,7 @@
         else:
             down.append(tidy(level - 1, True, near[:1]))
             after = down[-1][:1]
-        pieces = plain(exchange_each(near + far, "col"))
+        pieces = plain(reversed(exchange_each(near + far, "col")))
         forward.append(solve(right, inverse, level, pieces, False, after))
     backward = [None] * levels
     backward[-1] = solve(forward[-1], inverse, levels - 1, [], True)
@@ -475,7 +499,7 @@
     def local(rhs, diag_inv, blocks, blk_target, blk_source, blk_count):
         sizes = (n_row, n_col)
         dense = n_row * n_col <= blocks.shape[3] and rhs.shape[3] == 1
-        even = all(size > 1 and size & (size - 1) == 0 for size in sizes)
+        even = n_row > 2 and n_col > 1 and all(size & (size - 1) == 0 for size in sizes)
         run = direct_shards if dense and even else shards
         return run(rhs, diag_inv, blocks, blk_target, blk_source, blk_count)
 

time: 177 us -> 183 us (1.034)
  starting transfers between devices: 64.8 us -> 71.4 us
    ppermute x0 -> x35, starting transfers between devices: none -> 43.1 us  [near_exchange(): return lax.ppermute(message, ('row', 'col'), pairs)]
    ppermute x60 -> x30, starting transfers between devices: 56.2 us -> 19.5 us  [exchange_each(): lax.ppermute(messages[d], axis, [(i, i ^ d) for i in range(size)])]
    ppermute x60 -> x30, waiting for transfers between devices: 47.2 us -> 13.7 us  [exchange_each(): lax.ppermute(messages[d], axis, [(i, i ^ d) for i in range(size)])]
    ppermute x0 -> x35, waiting for transfers between devices: none -> 32.1 us  [near_exchange(): return lax.ppermute(message, ('row', 'col'), pairs)]
  transfers between devices with their start and end apart: 70 -> 75, of which waited for: 52 -> 49; matrix products, arithmetic and copies ran while one was open for 1% -> 1% of each run, Pallas kernels for 10% -> 9%
where the time goes in v13:
time: 183 us
  waiting for transfers between devices  81.7 us (45%)
  starting transfers between devices  71.4 us (39%)
  Pallas kernels  26.1 us (14%)
  local copies, waits for them, and re-layouts  2.48 us (1%)
    ppermute x35, starting transfers between devices, near_exchange(): return lax.ppermute(message, ('row', 'col'), pairs)  43.1 us
    ppermute x10, waiting for transfers between devices, far_exchange(): lax.ppermute(segment, axis, [(i, i ^ size // 2) for i in range(size)])  36 us
    ppermute x35, waiting for transfers between devices, near_exchange(): return lax.ppermute(message, ('row', 'col'), pairs)  32.1 us
    ppermute x30, starting transfers between devices, exchange_each(): lax.ppermute(messages[d], axis, [(i, i ^ d) for i in range(size)])  19.5 us
    ppermute x30, waiting for transfers between devices, exchange_each(): lax.ppermute(messages[d], axis, [(i, i ^ d) for i in range(size)])  13.7 us
    ppermute x10, starting transfers between devices, far_exchange(): lax.ppermute(segment, axis, [(i, i ^ size // 2) for i in range(size)])  8.76 us
    pallas_call x5, Pallas kernels, gather_blocks(): pl.pallas_call(functools.partial(gather_blocks_kernel, n_row, n_col, leve...  8.02 us
    pallas_call x20, Pallas kernels, couple(): pl.pallas_call(functools.partial(couple_kernel, terms, span), out_shape=[...  7.9 us
  transfers between devices with their start and end apart: 75, of which 49 were waited for; matrix products, arithmetic and copies ran while one was open for 1% of the time, Pallas kernels for 9%

profile of v13, /device:TPU:0, one launch (start us, length us, event | category | flops | bytes accessed | tf_op | source)
XLA Modules:
  0.0 182.9 jit_solution(7543136581074209571)
XLA Ops:
  0.6 1.7 first_solve.1.refs_0_
  2.3 4.1 %collective-permute-start = (f32[64,128]{1,0:T(8,128)}, f32[64,128]{1,0:T(8,128)S(1)}, u32[]{:S(2)}, u32[]{:S(2)}) collective-permute-start(f32[64,128]{1,0:T(8,128)} %first_solve.1.refs_0_), channel_id=1, source_target_pairs={{0,16},{4,20},{8,24},{12,28},{16,0},{20,4},{24,8},{28,12},{1,17},{... | collective-permute-start | bytes 98312 | tf_op jit(solution)/shard_map/ppermute | solution.py:284
  7.9 2.4 %gather_blocks_0.1.total_ref = f32[32,128,128]{2,1,0:T(8,128)S(1)} custom-call(s32[5,67]{1,0:T(8,128)S(1)} %concatenate.3.slots_ref, f32[5,32,128,128]{3,2,1,0:T(8,128)} %bitcast.14), custom_call_target="tpu_custom_call" | custom-call | flops 524288 | bytes 4194304 | tf_op jit(solution)/shard_map/gather_blocks_0/pallas_call | solution.py:67
  10.7 1.6 collective-permute-start.2
  12.3 1.5 collective-permute-start.1
  14.3 2.4 %collective-permute-start.4 = (f32[64,128]{1,0:T(8,128)S(1)}, f32[64,128]{1,0:T(8,128)S(1)}, u32[]{:S(2)}, u32[]{:S(2)}) collective-permute-start(f32[64,128]{1,0:T(8,128)S(1)} %collective-permute-done.refs_1_), channel_id=1, source_target_pairs={{0,12},{1,13},{2,14},{3,15},{4,8},{5,9},{6,10},{7,11},{8,4},{9,5},... | collective-permute-start | bytes 98312 | tf_op jit(solution)/shard_map/ppermute | solution.py:300
  16.7 1.9 %collective-permute-done.3.refs_3_ = f32[64,128]{1,0:T(8,128)S(1)} collective-permute-done((f32[64,128]{1,0:T(8,128)S(1)}, f32[64,128]{1,0:T(8,128)S(1)}, u32[]{:S(2)}, u32[]{:S(2)}) %collective-permute-start.3) | collective-permute-done | bytes 32800 | tf_op jit(solution)/shard_map/ppermute | solution.py:300
  19.6 1.7 collective-permute-start.6
  21.9 1.3 gather_blocks_1.1.refs_6_.total_ref
  25.8 2.8 %collective-permute-done.8.refs_1_ = f32[64,128]{1,0:T(8,128)S(1)} collective-permute-done((f32[64,128]{1,0:T(8,128)S(1)}, f32[64,128]{1,0:T(8,128)S(1)}, u32[]{:S(2)}, u32[]{:S(2)}) %collective-permute-start.8) | collective-permute-done | bytes 32800 | tf_op jit(solution)/shard_map/ppermute | solution.py:284
  28.6 1.5 collective-permute-start.10
  30.1 1.4 collective-permute-start.9
  32.5 2.0 %collective-permute-start.12 = (f32[64,128]{1,0:T(8,128)S(1)}, f32[64,128]{1,0:T(8,128)S(1)}, u32[]{:S(2)}, u32[]{:S(2)}) collective-permute-start(f32[64,128]{1,0:T(8,128)S(1)} %collective-permute-done.8.refs_1_), channel_id=1, source_target_pairs={{0,12},{1,13},{2,14},{3,15},{4,8},{5,9},{6,10},{7,11},{8,4},{9,5},... | collective-permute-start | bytes 98312 | tf_op jit(solution)/shard_map/ppermute | solution.py:300
  34.5 1.9 %collective-permute-done.11.refs_3_ = f32[64,128]{1,0:T(8,128)S(1)} collective-permute-done((f32[64,128]{1,0:T(8,128)S(1)}, f32[64,128]{1,0:T(8,128)S(1)}, u32[]{:S(2)}, u32[]{:S(2)}) %collective-permute-start.11) | collective-permute-done | bytes 32800 | tf_op jit(solution)/shard_map/ppermute | solution.py:300
  37.8 1.3 collective-permute-start.14
  40.1 1.5 gather_blocks_2.1.refs_6_.total_ref
  43.9 3.7 %collective-permute-done.16.refs_1_ = f32[64,128]{1,0:T(8,128)S(1)} collective-permute-done((f32[64,128]{1,0:T(8,128)S(1)}, f32[64,128]{1,0:T(8,128)S(1)}, u32[]{:S(2)}, u32[]{:S(2)}) %collective-permute-start.16) | collective-permute-done | bytes 32800 | tf_op jit(solution)/shard_map/ppermute | solution.py:284
  48.0 1.5 collective-permute-start.17
  49.5 1.6 collective-permute-start.19
  51.0 1.4 collective-permute-start.20
  52.4 1.9 %collective-permute-done.19.refs_3_ = f32[64,128]{1,0:T(8,128)S(1)} collective-permute-done((f32[64,128]{1,0:T(8,128)S(1)}, f32[64,128]{1,0:T(8,128)S(1)}, u32[]{:S(2)}, u32[]{:S(2)}) %collective-permute-start.19) | collective-permute-done | bytes 32800 | tf_op jit(solution)/shard_map/ppermute | solution.py:300
  54.3 1.6 collective-permute-done.20.refs_4_
  57.6 1.1 collective-permute-start.23
  58.7 1.3 gather_blocks_3.1.refs_6_.total_ref
  61.8 4.1 %collective-permute-done.24.refs_1_ = f32[64,128]{1,0:T(8,128)S(1)} collective-permute-done((f32[64,128]{1,0:T(8,128)S(1)}, f32[64,128]{1,0:T(8,128)S(1)}, u32[]{:S(2)}, u32[]{:S(2)}) %collective-permute-start.24) | collective-permute-done | bytes 32800 | tf_op jit(solution)/shard_map/ppermute | solution.py:284
  66.2 1.2 collective-permute-start.25
  67.3 2.1 %collective-permute-start.27 = (f32[64,128]{1,0:T(8,128)S(1)}, f32[64,128]{1,0:T(8,128)S(1)}, u32[]{:S(2)}, u32[]{:S(2)}) collective-permute-start(f32[64,128]{1,0:T(8,128)S(1)} %combine.22), channel_id=1, source_target_pairs={{0,12},{1,13},{2,14},{3,15},{4,8},{5,9},{6,10},{7,11},{8,4},{9,5},... | collective-permute-start | bytes 98312 | tf_op jit(solution)/shard_map/ppermute | solution.py:300
  70.3 1.9 %collective-permute-done.27.refs_3_ = f32[64,128]{1,0:T(8,128)S(1)} collective-permute-done((f32[64,128]{1,0:T(8,128)S(1)}, f32[64,128]{1,0:T(8,128)S(1)}, u32[]{:S(2)}, u32[]{:S(2)}) %collective-permute-start.27) | collective-permute-done | bytes 32800 | tf_op jit(solution)/shard_map/ppermute | solution.py:300
  72.2 2.1 %collective-permute-done.28.refs_4_ = f32[64,128]{1,0:T(8,128)S(1)} collective-permute-done((f32[64,128]{1,0:T(8,128)S(1)}, f32[64,128]{1,0:T(8,128)S(1)}, u32[]{:S(2)}, u32[]{:S(2)}) %collective-permute-start.28) | collective-permute-done | bytes 32800 | tf_op jit(solution)/shard_map/ppermute | solution.py:300
  75.5 1.5 collective-permute-start.31
  77.0 1.6 gather_blocks_4.1.refs_6_.total_ref
  80.1 3.7 %collective-permute-done.32.refs_1_ = f32[64,128]{1,0:T(8,128)S(1)} collective-permute-done((f32[64,128]{1,0:T(8,128)S(1)}, f32[64,128]{1,0:T(8,128)S(1)}, u32[]{:S(2)}, u32[]{:S(2)}) %collective-permute-start.32) | collective-permute-done | bytes 32800 | tf_op jit(solution)/shard_map/ppermute | solution.py:284
  84.0 1.2 collective-permute-start.33
  85.2 2.1 %collective-permute-start.35 = (f32[64,128]{1,0:T(8,128)S(1)}, f32[64,128]{1,0:T(8,128)S(1)}, u32[]{:S(2)}, u32[]{:S(2)}) collective-permute-start(f32[64,128]{1,0:T(8,128)S(1)} %combine.24), channel_id=1, source_target_pairs={{0,12},{1,13},{2,14},{3,15},{4,8},{5,9},{6,10},{7,11},{8,4},{9,5},... | collective-permute-start | bytes 98312 | tf_op jit(solution)/shard_map/ppermute | solution.py:300
  88.1 1.9 %collective-permute-done.35.refs_3_ = f32[64,128]{1,0:T(8,128)S(1)} collective-permute-done((f32[64,128]{1,0:T(8,128)S(1)}, f32[64,128]{1,0:T(8,128)S(1)}, u32[]{:S(2)}, u32[]{:S(2)}) %collective-permute-start.35) | collective-permute-done | bytes 32800 | tf_op jit(solution)/shard_map/ppermute | solution.py:300
  90.0 2.1 %collective-permute-done.36.refs_4_ = f32[64,128]{1,0:T(8,128)S(1)} collective-permute-done((f32[64,128]{1,0:T(8,128)S(1)}, f32[64,128]{1,0:T(8,128)S(1)}, u32[]{:S(2)}, u32[]{:S(2)}) %collective-permute-start.36) | collective-permute-done | bytes 32800 | tf_op jit(solution)/shard_map/ppermute | solution.py:300
  93.7 1.2 collective-permute-start.39
  98.9 1.8 collective-permute-done.42.refs_3_
  102.0 1.5 collective-permute-start.43
  103.5 1.2 collective-permute-start.44
  105.8 1.8 collective-permute-done.43.refs_1_
  110.1 3.7 %collective-permute-done.46.refs_3_ = f32[64,128]{1,0:T(8,128)S(1)} collective-permute-done((f32[64,128]{1,0:T(8,128)S(1)}, f32[64,128]{1,0:T(8,128)S(1)}, u32[]{:S(2)}, u32[]{:S(2)}) %collective-permute-start.46) | collective-permute-done | bytes 32800 | tf_op jit(solution)/shard_map/ppermute | solution.py:284
  115.0 1.5 collective-permute-start.48
  116.9 1.8 collective-permute-done.49.refs_3_
  119.6 1.4 collective-permute-start.50
  120.9 1.6 collective-permute-start.51
  123.4 1.8 collective-permute-done.50.refs_1_
  127.3 4.7 %collective-permute-done.53.refs_3_ = f32[64,128]{1,0:T(8,128)S(1)} collective-permute-done((f32[64,128]{1,0:T(8,128)S(1)}, f32[64,128]{1,0:T(8,128)S(1)}, u32[]{:S(2)}, u32[]{:S(2)}) %collective-permute-start.53) | collective-permute-done | bytes 32800 | tf_op jit(solution)/shard_map/ppermute | solution.py:284
  132.2 1.1 collective-permute-start.55
  134.0 1.5 collective-permute-done.56.refs_3_
  138.7 1.8 collective-permute-start.59
  140.8 2.1 %collective-permute-done.57.refs_1_ = f32[2,64,128]{2,1,0:T(8,128)S(1)} collective-permute-done((f32[2,64,128]{2,1,0:T(8,128)S(1)}, f32[2,64,128]{2,1,0:T(8,128)S(1)}, u32[]{:S(2)}, u32[]{:S(2)}) %collective-permute-start.57) | collective-permute-done | bytes 65568 | tf_op jit(solution)/shard_map/ppermute | solution.py:300
  144.1 4.4 %collective-permute-done.60.refs_3_ = f32[64,128]{1,0:T(8,128)S(1)} collective-permute-done((f32[64,128]{1,0:T(8,128)S(1)}, f32[64,128]{1,0:T(8,128)S(1)}, u32[]{:S(2)}, u32[]{:S(2)}) %collective-permute-start.60) | collective-permute-done | bytes 32800 | tf_op jit(solution)/shard_map/ppermute | solution.py:284
  148.8 1.5 collective-permute-start.62
  150.6 1.8 collective-permute-done.63.refs_3_
  153.3 1.1 collective-permute-start.64
  154.4 1.8 %collective-permute-start.65 = (f32[2,64,128]{2,1,0:T(8,128)S(1)}, f32[2,64,128]{2,1,0:T(8,128)S(1)}, u32[]{:S(2)}, u32[]{:S(2)}) collective-permute-start(f32[2,64,128]{2,1,0:T(8,128)S(1)} %get-tuple-element.123), channel_id=1, source_target_pairs={{0,8},{1,5},{2,10},{3,7},{4,12},{5,1},{6,14},{7,3},{8,0},{9,13},{1... | collective-permute-start | bytes 196616 | tf_op jit(solution)/shard_map/ppermute | solution.py:300
  157.1 1.9 %collective-permute-done.64.refs_1_ = f32[2,64,128]{2,1,0:T(8,128)S(1)} collective-permute-done((f32[2,64,128]{2,1,0:T(8,128)S(1)}, f32[2,64,128]{2,1,0:T(8,128)S(1)}, u32[]{:S(2)}, u32[]{:S(2)}) %collective-permute-start.64) | collective-permute-done | bytes 65568 | tf_op jit(solution)/shard_map/ppermute | solution.py:300
  160.8 4.6 %collective-permute-done.67.refs_3_ = f32[64,128]{1,0:T(8,128)S(1)} collective-permute-done((f32[64,128]{1,0:T(8,128)S(1)}, f32[64,128]{1,0:T(8,128)S(1)}, u32[]{:S(2)}, u32[]{:S(2)}) %collective-permute-start.67) | collective-permute-done | bytes 32800 | tf_op jit(solution)/shard_map/ppermute | solution.py:284
  165.6 1.3 collective-permute-start.69
  167.5 1.6 collective-permute-done.70.refs_3_
  171.0 1.7 collective-permute-start.72
  174.0 2.1 %collective-permute-done.71.refs_1_ = f32[2,64,128]{2,1,0:T(8,128)S(1)} collective-permute-done((f32[2,64,128]{2,1,0:T(8,128)S(1)}, f32[2,64,128]{2,1,0:T(8,128)S(1)}, u32[]{:S(2)}, u32[]{:S(2)}) %collective-permute-start.71) | collective-permute-done | bytes 65568 | tf_op jit(solution)/shard_map/ppermute | solution.py:300
  177.7 4.3 %collective-permute-done.74.refs_3_ = f32[64,128]{1,0:T(8,128)S(1)} collective-permute-done((f32[64,128]{1,0:T(8,128)S(1)}, f32[64,128]{1,0:T(8,128)S(1)}, u32[]{:S(2)}, u32[]{:S(2)}) %collective-permute-start.74) | collective-permute-done | bytes 32800 | tf_op jit(solution)/shard_map/ppermute | solution.py:284
  (170 shorter events, 53.3 us)
Async XLA Ops:
  2.3 8.4 %collective-permute-start = (f32[64,128]{1,0:T(8,128)}, f32[64,128]{1,0:T(8,128)S(1)}, u32[]{:S(2)}, u32[]{:S(2)}) collective-permute-start(f32[64,128]{1,0:T(8,128)} %first_solve.1.refs_0_), channel_id=1, source_target_pairs={{0,16},{4,20},{8,24},{12,28},{16,0},{20,4},{24,8},{28,12},{1,17},{... | collective-permute-start | bytes 98312 | tf_op jit(solution)/shard_map/ppermute | solution.py:284
  10.7 8.4 %collective-permute-start.2 = (f32[2,64,128]{2,1,0:T(8,128)S(1)}, f32[2,64,128]{2,1,0:T(8,128)S(1)}, u32[]{:S(2)}, u32[]{:S(2)}) collective-permute-start(f32[2,64,128]{2,1,0:T(8,128)S(1)} %combine.15.refs_0_), channel_id=1, source_target_pairs={{0,8},{1,5},{2,10},{3,7},{4,12},{5,1},{6,14},{7,3},{8,0},{9,13},{1... | collective-permute-start | bytes 196616 | tf_op jit(solution)/shard_map/ppermute | solution.py:300
  12.3 6.8 %collective-permute-start.1 = (f32[2,64,128]{2,1,0:T(8,128)S(1)}, f32[2,64,128]{2,1,0:T(8,128)S(1)}, u32[]{:S(2)}, u32[]{:S(2)}) collective-permute-start(f32[2,64,128]{2,1,0:T(8,128)S(1)} %combine.15.refs_0_), channel_id=1, source_target_pairs={{0,4},{1,9},{2,6},{3,11},{4,0},{5,13},{6,2},{7,15},{8,12},{9,1},{1... | collective-permute-start | bytes 196616 | tf_op jit(solution)/shard_map/ppermute | solution.py:300
  13.7 4.8 %collective-permute-start.3 = (f32[64,128]{1,0:T(8,128)S(1)}, f32[64,128]{1,0:T(8,128)S(1)}, u32[]{:S(2)}, u32[]{:S(2)}) collective-permute-start(f32[64,128]{1,0:T(8,128)S(1)} %combine.16), channel_id=1, source_target_pairs={{0,12},{1,13},{2,14},{3,15},{4,8},{5,9},{6,10},{7,11},{8,4},{9,5},... | collective-permute-start | bytes 98312 | tf_op jit(solution)/shard_map/ppermute | solution.py:300
  14.3 4.8 %collective-permute-start.4 = (f32[64,128]{1,0:T(8,128)S(1)}, f32[64,128]{1,0:T(8,128)S(1)}, u32[]{:S(2)}, u32[]{:S(2)}) collective-permute-start(f32[64,128]{1,0:T(8,128)S(1)} %collective-permute-done.refs_1_), channel_id=1, source_target_pairs={{0,12},{1,13},{2,14},{3,15},{4,8},{5,9},{6,10},{7,11},{8,4},{9,5},... | collective-permute-start | bytes 98312 | tf_op jit(solution)/shard_map/ppermute | solution.py:300
  19.5 3.7 %collective-permute-start.5 = (f32[64,128]{1,0:T(8,128)S(1)}, f32[64,128]{1,0:T(8,128)S(1)}, u32[]{:S(2)}, u32[]{:S(2)}) collective-permute-start(f32[64,128]{1,0:T(8,128)S(1)} %get-tuple-element.69), channel_id=1, source_target_pairs={{0,3},{1,2},{2,1},{3,0},{4,7},{5,6},{6,5},{7,4},{8,11},{9,10},{10,... | collective-permute-start | bytes 98312 | tf_op jit(solution)/shard_map/ppermute | solution.py:333
  19.6 4.0 %collective-permute-start.6 = (f32[64,128]{1,0:T(8,128)S(1)}, f32[64,128]{1,0:T(8,128)S(1)}, u32[]{:S(2)}, u32[]{:S(2)}) collective-permute-start(f32[64,128]{1,0:T(8,128)S(1)} %get-tuple-element.70), channel_id=1, source_target_pairs={{0,2},{1,3},{2,0},{3,1},{4,6},{5,7},{6,4},{7,5},{8,10},{9,11},{10,... | collective-permute-start | bytes 98312 | tf_op jit(solution)/shard_map/ppermute | solution.py:333
  23.8 4.9 %collective-permute-start.8 = (f32[64,128]{1,0:T(8,128)S(1)}, f32[64,128]{1,0:T(8,128)S(1)}, u32[]{:S(2)}, u32[]{:S(2)}) collective-permute-start(f32[64,128]{1,0:T(8,128)S(1)} %solve_up.5.refs_0_.refs_1_), channel_id=1, source_target_pairs={{0,16},{4,20},{8,24},{12,28},{16,0},{20,4},{24,8},{28,12},{1,17},{... | collective-permute-start | bytes 98312 | tf_op jit(solution)/shard_map/ppermute | solution.py:284
  28.6 8.7 %collective-permute-start.10 = (f32[2,64,128]{2,1,0:T(8,128)S(1)}, f32[2,64,128]{2,1,0:T(8,128)S(1)}, u32[]{:S(2)}, u32[]{:S(2)}) collective-permute-start(f32[2,64,128]{2,1,0:T(8,128)S(1)} %combine.17.refs_0_), channel_id=1, source_target_pairs={{0,8},{1,5},{2,10},{3,7},{4,12},{5,1},{6,14},{7,3},{8,0},{9,13},{1... | collective-permute-start | bytes 196616 | tf_op jit(solution)/shard_map/ppermute | solution.py:300
  30.1 7.2 %collective-permute-start.9 = (f32[2,64,128]{2,1,0:T(8,128)S(1)}, f32[2,64,128]{2,1,0:T(8,128)S(1)}, u32[]{:S(2)}, u32[]{:S(2)}) collective-permute-start(f32[2,64,128]{2,1,0:T(8,128)S(1)} %combine.17.refs_0_), channel_id=1, source_target_pairs={{0,4},{1,9},{2,6},{3,11},{4,0},{5,13},{6,2},{7,15},{8,12},{9,1},{1... | collective-permute-start | bytes 196616 | tf_op jit(solution)/shard_map/ppermute | solution.py:300
  31.6 4.8 %collective-permute-start.11 = (f32[64,128]{1,0:T(8,128)S(1)}, f32[64,128]{1,0:T(8,128)S(1)}, u32[]{:S(2)}, u32[]{:S(2)}) collective-permute-start(f32[64,128]{1,0:T(8,128)S(1)} %combine.18), channel_id=1, source_target_pairs={{0,12},{1,13},{2,14},{3,15},{4,8},{5,9},{6,10},{7,11},{8,4},{9,5},... | collective-permute-start | bytes 98312 | tf_op jit(solution)/shard_map/ppermute | solution.py:300
  32.5 4.8 %collective-permute-start.12 = (f32[64,128]{1,0:T(8,128)S(1)}, f32[64,128]{1,0:T(8,128)S(1)}, u32[]{:S(2)}, u32[]{:S(2)}) collective-permute-start(f32[64,128]{1,0:T(8,128)S(1)} %collective-permute-done.8.refs_1_), channel_id=1, source_target_pairs={{0,12},{1,13},{2,14},{3,15},{4,8},{5,9},{6,10},{7,11},{8,4},{9,5},... | collective-permute-start | bytes 98312 | tf_op jit(solution)/shard_map/ppermute | solution.py:300
  37.7 3.9 %collective-permute-start.13 = (f32[64,128]{1,0:T(8,128)S(1)}, f32[64,128]{1,0:T(8,128)S(1)}, u32[]{:S(2)}, u32[]{:S(2)}) collective-permute-start(f32[64,128]{1,0:T(8,128)S(1)} %get-tuple-element.76), channel_id=1, source_target_pairs={{0,3},{1,2},{2,1},{3,0},{4,7},{5,6},{6,5},{7,4},{8,11},{9,10},{10,... | collective-permute-start | bytes 98312 | tf_op jit(solution)/shard_map/ppermute | solution.py:333
  37.8 4.0 %collective-permute-start.14 = (f32[64,128]{1,0:T(8,128)S(1)}, f32[64,128]{1,0:T(8,128)S(1)}, u32[]{:S(2)}, u32[]{:S(2)}) collective-permute-start(f32[64,128]{1,0:T(8,128)S(1)} %get-tuple-element.77), channel_id=1, source_target_pairs={{0,2},{1,3},{2,0},{3,1},{4,6},{5,7},{6,4},{7,5},{8,10},{9,11},{10,... | collective-permute-start | bytes 98312 | tf_op jit(solution)/shard_map/ppermute | solution.py:333
  42.0 5.6 %collective-permute-start.16 = (f32[64,128]{1,0:T(8,128)S(1)}, f32[64,128]{1,0:T(8,128)S(1)}, u32[]{:S(2)}, u32[]{:S(2)}) collective-permute-start(f32[64,128]{1,0:T(8,128)S(1)} %solve_up.6.refs_0_.refs_2_), channel_id=1, source_target_pairs={{0,16},{4,20},{8,24},{12,28},{16,0},{20,4},{24,8},{28,12},{1,17},{... | collective-permute-start | bytes 98312 | tf_op jit(solution)/shard_map/ppermute | solution.py:284
  47.6 8.3 %collective-permute-start.18 = (f32[2,64,128]{2,1,0:T(8,128)S(1)}, f32[2,64,128]{2,1,0:T(8,128)S(1)}, u32[]{:S(2)}, u32[]{:S(2)}) collective-permute-start(f32[2,64,128]{2,1,0:T(8,128)S(1)} %combine.19.refs_0_), channel_id=1, source_target_pairs={{0,8},{1,5},{2,10},{3,7},{4,12},{5,1},{6,14},{7,3},{8,0},{9,13},{1... | collective-permute-start | bytes 196616 | tf_op jit(solution)/shard_map/ppermute | solution.py:300
  48.0 7.9 %collective-permute-start.17 = (f32[2,64,128]{2,1,0:T(8,128)S(1)}, f32[2,64,128]{2,1,0:T(8,128)S(1)}, u32[]{:S(2)}, u32[]{:S(2)}) collective-permute-start(f32[2,64,128]{2,1,0:T(8,128)S(1)} %combine.19.refs_0_), channel_id=1, source_target_pairs={{0,4},{1,9},{2,6},{3,11},{4,0},{5,13},{6,2},{7,15},{8,12},{9,1},{1... | collective-permute-start | bytes 196616 | tf_op jit(solution)/shard_map/ppermute | solution.py:300
  49.5 4.8 %collective-permute-start.19 = (f32[64,128]{1,0:T(8,128)S(1)}, f32[64,128]{1,0:T(8,128)S(1)}, u32[]{:S(2)}, u32[]{:S(2)}) collective-permute-start(f32[64,128]{1,0:T(8,128)S(1)} %combine.20), channel_id=1, source_target_pairs={{0,12},{1,13},{2,14},{3,15},{4,8},{5,9},{6,10},{7,11},{8,4},{9,5},... | collective-permute-start | bytes 98312 | tf_op jit(solution)/shard_map/ppermute | solution.py:300
  51.0 4.8 %collective-permute-start.20 = (f32[64,128]{1,0:T(8,128)S(1)}, f32[64,128]{1,0:T(8,128)S(1)}, u32[]{:S(2)}, u32[]{:S(2)}) collective-permute-start(f32[64,128]{1,0:T(8,128)S(1)} %collective-permute-done.16.refs_1_), channel_id=1, source_target_pairs={{0,12},{1,13},{2,14},{3,15},{4,8},{5,9},{6,10},{7,11},{8,4},{9,5},... | collective-permute-start | bytes 98312 | tf_op jit(solution)/shard_map/ppermute | solution.py:300
  56.3 3.7 %collective-permute-start.21 = (f32[64,128]{1,0:T(8,128)S(1)}, f32[64,128]{1,0:T(8,128)S(1)}, u32[]{:S(2)}, u32[]{:S(2)}) collective-permute-start(f32[64,128]{1,0:T(8,128)S(1)} %get-tuple-element.83), channel_id=1, source_target_pairs={{0,3},{1,2},{2,1},{3,0},{4,7},{5,6},{6,5},{7,4},{8,11},{9,10},{10,... | collective-permute-start | bytes 98312 | tf_op jit(solution)/shard_map/ppermute | solution.py:333
  56.3 4.2 %collective-permute-start.22 = (f32[64,128]{1,0:T(8,128)S(1)}, f32[64,128]{1,0:T(8,128)S(1)}, u32[]{:S(2)}, u32[]{:S(2)}) collective-permute-start(f32[64,128]{1,0:T(8,128)S(1)} %get-tuple-element.84), channel_id=1, source_target_pairs={{0,2},{1,3},{2,0},{3,1},{4,6},{5,7},{6,4},{7,5},{8,10},{9,11},{10,... | collective-permute-start | bytes 98312 | tf_op jit(solution)/shard_map/ppermute | solution.py:333
  60.7 5.2 %collective-permute-start.24 = (f32[64,128]{1,0:T(8,128)S(1)}, f32[64,128]{1,0:T(8,128)S(1)}, u32[]{:S(2)}, u32[]{:S(2)}) collective-permute-start(f32[64,128]{1,0:T(8,128)S(1)} %solve_up.7.refs_0_.refs_3_), channel_id=1, source_target_pairs={{0,16},{4,20},{8,24},{12,28},{16,0},{20,4},{24,8},{28,12},{1,17},{... | collective-permute-start | bytes 98312 | tf_op jit(solution)/shard_map/ppermute | solution.py:284
  65.9 8.3 %collective-permute-start.26 = (f32[2,64,128]{2,1,0:T(8,128)S(1)}, f32[2,64,128]{2,1,0:T(8,128)S(1)}, u32[]{:S(2)}, u32[]{:S(2)}) collective-permute-start(f32[2,64,128]{2,1,0:T(8,128)S(1)} %combine.21.refs_0_), channel_id=1, source_target_pairs={{0,8},{1,5},{2,10},{3,7},{4,12},{5,1},{6,14},{7,3},{8,0},{9,13},{1... | collective-permute-start | bytes 196616 | tf_op jit(solution)/shard_map/ppermute | solution.py:300
  66.2 8.1 %collective-permute-start.25 = (f32[2,64,128]{2,1,0:T(8,128)S(1)}, f32[2,64,128]{2,1,0:T(8,128)S(1)}, u32[]{:S(2)}, u32[]{:S(2)}) collective-permute-start(f32[2,64,128]{2,1,0:T(8,128)S(1)} %combine.21.refs_0_), channel_id=1, source_target_pairs={{0,4},{1,9},{2,6},{3,11},{4,0},{5,13},{6,2},{7,15},{8,12},{9,1},{1... | collective-permute-start | bytes 196616 | tf_op jit(solution)/shard_map/ppermute | solution.py:300
  67.3 4.8 %collective-permute-start.27 = (f32[64,128]{1,0:T(8,128)S(1)}, f32[64,128]{1,0:T(8,128)S(1)}, u32[]{:S(2)}, u32[]{:S(2)}) collective-permute-start(f32[64,128]{1,0:T(8,128)S(1)} %combine.22), channel_id=1, source_target_pairs={{0,12},{1,13},{2,14},{3,15},{4,8},{5,9},{6,10},{7,11},{8,4},{9,5},... | collective-permute-start | bytes 98312 | tf_op jit(solution)/shard_map/ppermute | solution.py:300
  69.4 4.8 %collective-permute-start.28 = (f32[64,128]{1,0:T(8,128)S(1)}, f32[64,128]{1,0:T(8,128)S(1)}, u32[]{:S(2)}, u32[]{:S(2)}) collective-permute-start(f32[64,128]{1,0:T(8,128)S(1)} %collective-permute-done.24.refs_1_), channel_id=1, source_target_pairs={{0,12},{1,13},{2,14},{3,15},{4,8},{5,9},{6,10},{7,11},{8,4},{9,5},... | collective-permute-start | bytes 98312 | tf_op jit(solution)/shard_map/ppermute | solution.py:300
  74.6 4.0 %collective-permute-start.29 = (f32[64,128]{1,0:T(8,128)S(1)}, f32[64,128]{1,0:T(8,128)S(1)}, u32[]{:S(2)}, u32[]{:S(2)}) collective-permute-start(f32[64,128]{1,0:T(8,128)S(1)} %get-tuple-element.90), channel_id=1, source_target_pairs={{0,3},{1,2},{2,1},{3,0},{4,7},{5,6},{6,5},{7,4},{8,11},{9,10},{10,... | collective-permute-start | bytes 98312 | tf_op jit(solution)/shard_map/ppermute | solution.py:333
  74.7 4.0 %collective-permute-start.30 = (f32[64,128]{1,0:T(8,128)S(1)}, f32[64,128]{1,0:T(8,128)S(1)}, u32[]{:S(2)}, u32[]{:S(2)}) collective-permute-start(f32[64,128]{1,0:T(8,128)S(1)} %get-tuple-element.91), channel_id=1, source_target_pairs={{0,2},{1,3},{2,0},{3,1},{4,6},{5,7},{6,4},{7,5},{8,10},{9,11},{10,... | collective-permute-start | bytes 98312 | tf_op jit(solution)/shard_map/ppermute | solution.py:333
  78.9 4.9 %collective-permute-start.32 = (f32[64,128]{1,0:T(8,128)S(1)}, f32[64,128]{1,0:T(8,128)S(1)}, u32[]{:S(2)}, u32[]{:S(2)}) collective-permute-start(f32[64,128]{1,0:T(8,128)S(1)} %solve_up.8.refs_0_.refs_4_), channel_id=1, source_target_pairs={{0,16},{4,20},{8,24},{12,28},{16,0},{20,4},{24,8},{28,12},{1,17},{... | collective-permute-start | bytes 98312 | tf_op jit(solution)/shard_map/ppermute | solution.py:284
  83.8 8.3 %collective-permute-start.34 = (f32[2,64,128]{2,1,0:T(8,128)S(1)}, f32[2,64,128]{2,1,0:T(8,128)S(1)}, u32[]{:S(2)}, u32[]{:S(2)}) collective-permute-start(f32[2,64,128]{2,1,0:T(8,128)S(1)} %combine.23.refs_0_), channel_id=1, source_target_pairs={{0,8},{1,5},{2,10},{3,7},{4,12},{5,1},{6,14},{7,3},{8,0},{9,13},{1... | collective-permute-start | bytes 196616 | tf_op jit(solution)/shard_map/ppermute | solution.py:300
  84.0 8.1 %collective-permute-start.33 = (f32[2,64,128]{2,1,0:T(8,128)S(1)}, f32[2,64,128]{2,1,0:T(8,128)S(1)}, u32[]{:S(2)}, u32[]{:S(2)}) collective-permute-start(f32[2,64,128]{2,1,0:T(8,128)S(1)} %combine.23.refs_0_), channel_id=1, source_target_pairs={{0,4},{1,9},{2,6},{3,11},{4,0},{5,13},{6,2},{7,15},{8,12},{9,1},{1... | collective-permute-start | bytes 196616 | tf_op jit(solution)/shard_map/ppermute | solution.py:300
  85.2 4.8 %collective-permute-start.35 = (f32[64,128]{1,0:T(8,128)S(1)}, f32[64,128]{1,0:T(8,128)S(1)}, u32[]{:S(2)}, u32[]{:S(2)}) collective-permute-start(f32[64,128]{1,0:T(8,128)S(1)} %combine.24), channel_id=1, source_target_pairs={{0,12},{1,13},{2,14},{3,15},{4,8},{5,9},{6,10},{7,11},{8,4},{9,5},... | collective-permute-start | bytes 98312 | tf_op jit(solution)/shard_map/ppermute | solution.py:300
  87.3 4.8 %collective-permute-start.36 = (f32[64,128]{1,0:T(8,128)S(1)}, f32[64,128]{1,0:T(8,128)S(1)}, u32[]{:S(2)}, u32[]{:S(2)}) collective-permute-start(f32[64,128]{1,0:T(8,128)S(1)} %collective-permute-done.32.refs_1_), channel_id=1, source_target_pairs={{0,12},{1,13},{2,14},{3,15},{4,8},{5,9},{6,10},{7,11},{8,4},{9,5},... | collective-permute-start | bytes 98312 | tf_op jit(solution)/shard_map/ppermute | solution.py:300
  92.5 3.4 %collective-permute-start.37 = (f32[64,128]{1,0:T(8,128)S(1)}, f32[64,128]{1,0:T(8,128)S(1)}, u32[]{:S(2)}, u32[]{:S(2)}) collective-permute-start(f32[64,128]{1,0:T(8,128)S(1)} %get-tuple-element.97), channel_id=1, source_target_pairs={{0,3},{1,2},{2,1},{3,0},{4,7},{5,6},{6,5},{7,4},{8,11},{9,10},{10,... | collective-permute-start | bytes 98312 | tf_op jit(solution)/shard_map/ppermute | solution.py:333
  92.6 4.1 %collective-permute-start.38 = (f32[64,128]{1,0:T(8,128)S(1)}, f32[64,128]{1,0:T(8,128)S(1)}, u32[]{:S(2)}, u32[]{:S(2)}) collective-permute-start(f32[64,128]{1,0:T(8,128)S(1)} %get-tuple-element.98), channel_id=1, source_target_pairs={{0,2},{1,3},{2,0},{3,1},{4,6},{5,7},{6,4},{7,5},{8,10},{9,11},{10,... | collective-permute-start | bytes 98312 | tf_op jit(solution)/shard_map/ppermute | solution.py:333
  97.0 3.7 %collective-permute-start.42 = (f32[64,128]{1,0:T(8,128)S(1)}, f32[64,128]{1,0:T(8,128)S(1)}, u32[]{:S(2)}, u32[]{:S(2)}) collective-permute-start(f32[64,128]{1,0:T(8,128)S(1)} %solve_down.6.refs_0_.refs_5_), channel_id=1, source_target_pairs={{0,3},{1,2},{2,1},{3,0},{4,7},{5,6},{6,5},{7,4},{8,11},{9,10},{10,... | collective-permute-start | bytes 98312 | tf_op jit(solution)/shard_map/ppermute | solution.py:333
  97.5 4.0 %collective-permute-start.41 = (f32[64,128]{1,0:T(8,128)S(1)}, f32[64,128]{1,0:T(8,128)S(1)}, u32[]{:S(2)}, u32[]{:S(2)}) collective-permute-start(f32[64,128]{1,0:T(8,128)S(1)} %solve_down.6.refs_0_.refs_5_), channel_id=1, source_target_pairs={{0,2},{1,3},{2,0},{3,1},{4,6},{5,7},{6,4},{7,5},{8,10},{9,11},{10,... | collective-permute-start | bytes 98312 | tf_op jit(solution)/shard_map/ppermute | solution.py:333
  102.0 5.6 %collective-permute-start.43 = (f32[2,64,128]{2,1,0:T(8,128)S(1)}, f32[2,64,128]{2,1,0:T(8,128)S(1)}, u32[]{:S(2)}, u32[]{:S(2)}) collective-permute-start(f32[2,64,128]{2,1,0:T(8,128)S(1)} %get-tuple-element.107), channel_id=1, source_target_pairs={{0,12},{1,13},{2,14},{3,15},{4,8},{5,9},{6,10},{7,11},{8,4},{9,5},... | collective-permute-start | bytes 196616 | tf_op jit(solution)/shard_map/ppermute | solution.py:300
  103.5 4.6 %collective-permute-start.44 = (f32[2,64,128]{2,1,0:T(8,128)S(1)}, f32[2,64,128]{2,1,0:T(8,128)S(1)}, u32[]{:S(2)}, u32[]{:S(2)}) collective-permute-start(f32[2,64,128]{2,1,0:T(8,128)S(1)} %get-tuple-element.108), channel_id=1, source_target_pairs={{0,8},{1,5},{2,10},{3,7},{4,12},{5,1},{6,14},{7,3},{8,0},{9,13},{1... | collective-permute-start | bytes 196616 | tf_op jit(solution)/shard_map/ppermute | solution.py:300
  104.7 4.3 %collective-permute-start.45 = (f32[2,64,128]{2,1,0:T(8,128)S(1)}, f32[2,64,128]{2,1,0:T(8,128)S(1)}, u32[]{:S(2)}, u32[]{:S(2)}) collective-permute-start(f32[2,64,128]{2,1,0:T(8,128)S(1)} %get-tuple-element.109), channel_id=1, source_target_pairs={{0,4},{1,9},{2,6},{3,11},{4,0},{5,13},{6,2},{7,15},{8,12},{9,1},{1... | collective-permute-start | bytes 196616 | tf_op jit(solution)/shard_map/ppermute | solution.py:300
  109.0 4.9 %collective-permute-start.46 = (f32[64,128]{1,0:T(8,128)S(1)}, f32[64,128]{1,0:T(8,128)S(1)}, u32[]{:S(2)}, u32[]{:S(2)}) collective-permute-start(f32[64,128]{1,0:T(8,128)S(1)} %get-tuple-element.111), channel_id=1, source_target_pairs={{0,16},{4,20},{8,24},{12,28},{16,0},{20,4},{24,8},{28,12},{1,17},{... | collective-permute-start | bytes 98312 | tf_op jit(solution)/shard_map/ppermute | solution.py:284
  115.0 3.7 %collective-permute-start.49 = (f32[64,128]{1,0:T(8,128)S(1)}, f32[64,128]{1,0:T(8,128)S(1)}, u32[]{:S(2)}, u32[]{:S(2)}) collective-permute-start(f32[64,128]{1,0:T(8,128)S(1)} %solve_down.7.refs_0_.refs_4_), channel_id=1, source_target_pairs={{0,3},{1,2},{2,1},{3,0},{4,7},{5,6},{6,5},{7,4},{8,11},{9,10},{10,... | collective-permute-start | bytes 98312 | tf_op jit(solution)/shard_map/ppermute | solution.py:333
  115.0 4.0 %collective-permute-start.48 = (f32[64,128]{1,0:T(8,128)S(1)}, f32[64,128]{1,0:T(8,128)S(1)}, u32[]{:S(2)}, u32[]{:S(2)}) collective-permute-start(f32[64,128]{1,0:T(8,128)S(1)} %solve_down.7.refs_0_.refs_4_), channel_id=1, source_target_pairs={{0,2},{1,3},{2,0},{3,1},{4,6},{5,7},{6,4},{7,5},{8,10},{9,11},{10,... | collective-permute-start | bytes 98312 | tf_op jit(solution)/shard_map/ppermute | solution.py:333
  119.6 5.6 %collective-permute-start.50 = (f32[2,64,128]{2,1,0:T(8,128)S(1)}, f32[2,64,128]{2,1,0:T(8,128)S(1)}, u32[]{:S(2)}, u32[]{:S(2)}) collective-permute-start(f32[2,64,128]{2,1,0:T(8,128)S(1)} %get-tuple-element.112), channel_id=1, source_target_pairs={{0,12},{1,13},{2,14},{3,15},{4,8},{5,9},{6,10},{7,11},{8,4},{9,5},... | collective-permute-start | bytes 196616 | tf_op jit(solution)/shard_map/ppermute | solution.py:300
  120.9 5.2 %collective-permute-start.51 = (f32[2,64,128]{2,1,0:T(8,128)S(1)}, f32[2,64,128]{2,1,0:T(8,128)S(1)}, u32[]{:S(2)}, u32[]{:S(2)}) collective-permute-start(f32[2,64,128]{2,1,0:T(8,128)S(1)} %get-tuple-element.113), channel_id=1, source_target_pairs={{0,8},{1,5},{2,10},{3,7},{4,12},{5,1},{6,14},{7,3},{8,0},{9,13},{1... | collective-permute-start | bytes 196616 | tf_op jit(solution)/shard_map/ppermute | solution.py:300
  122.5 4.3 %collective-permute-start.52 = (f32[2,64,128]{2,1,0:T(8,128)S(1)}, f32[2,64,128]{2,1,0:T(8,128)S(1)}, u32[]{:S(2)}, u32[]{:S(2)}) collective-permute-start(f32[2,64,128]{2,1,0:T(8,128)S(1)} %get-tuple-element.114), channel_id=1, source_target_pairs={{0,4},{1,9},{2,6},{3,11},{4,0},{5,13},{6,2},{7,15},{8,12},{9,1},{1... | collective-permute-start | bytes 196616 | tf_op jit(solution)/shard_map/ppermute | solution.py:300
  126.8 5.1 %collective-permute-start.53 = (f32[64,128]{1,0:T(8,128)S(1)}, f32[64,128]{1,0:T(8,128)S(1)}, u32[]{:S(2)}, u32[]{:S(2)}) collective-permute-start(f32[64,128]{1,0:T(8,128)S(1)} %get-tuple-element.116), channel_id=1, source_target_pairs={{0,16},{4,20},{8,24},{12,28},{16,0},{20,4},{24,8},{28,12},{1,17},{... | collective-permute-start | bytes 98312 | tf_op jit(solution)/shard_map/ppermute | solution.py:284
  132.2 4.2 %collective-permute-start.55 = (f32[64,128]{1,0:T(8,128)S(1)}, f32[64,128]{1,0:T(8,128)S(1)}, u32[]{:S(2)}, u32[]{:S(2)}) collective-permute-start(f32[64,128]{1,0:T(8,128)S(1)} %solve_down.8.refs_0_.refs_3_), channel_id=1, source_target_pairs={{0,2},{1,3},{2,0},{3,1},{4,6},{5,7},{6,4},{7,5},{8,10},{9,11},{10,... | collective-permute-start | bytes 98312 | tf_op jit(solution)/shard_map/ppermute | solution.py:333
  136.9 5.9 %collective-permute-start.57 = (f32[2,64,128]{2,1,0:T(8,128)S(1)}, f32[2,64,128]{2,1,0:T(8,128)S(1)}, u32[]{:S(2)}, u32[]{:S(2)}) collective-permute-start(f32[2,64,128]{2,1,0:T(8,128)S(1)} %get-tuple-element.117), channel_id=1, source_target_pairs={{0,12},{1,13},{2,14},{3,15},{4,8},{5,9},{6,10},{7,11},{8,4},{9,5},... | collective-permute-start | bytes 196616 | tf_op jit(solution)/shard_map/ppermute | solution.py:300
  137.8 5.0 %collective-permute-start.58 = (f32[2,64,128]{2,1,0:T(8,128)S(1)}, f32[2,64,128]{2,1,0:T(8,128)S(1)}, u32[]{:S(2)}, u32[]{:S(2)}) collective-permute-start(f32[2,64,128]{2,1,0:T(8,128)S(1)} %get-tuple-element.118), channel_id=1, source_target_pairs={{0,8},{1,5},{2,10},{3,7},{4,12},{5,1},{6,14},{7,3},{8,0},{9,13},{1... | collective-permute-start | bytes 196616 | tf_op jit(solution)/shard_map/ppermute | solution.py:300
  138.7 4.6 %collective-permute-start.59 = (f32[2,64,128]{2,1,0:T(8,128)S(1)}, f32[2,64,128]{2,1,0:T(8,128)S(1)}, u32[]{:S(2)}, u32[]{:S(2)}) collective-permute-start(f32[2,64,128]{2,1,0:T(8,128)S(1)} %get-tuple-element.119), channel_id=1, source_target_pairs={{0,4},{1,9},{2,6},{3,11},{4,0},{5,13},{6,2},{7,15},{8,12},{9,1},{1... | collective-permute-start | bytes 196616 | tf_op jit(solution)/shard_map/ppermute | solution.py:300
  143.3 5.2 %collective-permute-start.60 = (f32[64,128]{1,0:T(8,128)S(1)}, f32[64,128]{1,0:T(8,128)S(1)}, u32[]{:S(2)}, u32[]{:S(2)}) collective-permute-start(f32[64,128]{1,0:T(8,128)S(1)} %get-tuple-element.121), channel_id=1, source_target_pairs={{0,16},{4,20},{8,24},{12,28},{16,0},{20,4},{24,8},{28,12},{1,17},{... | collective-permute-start | bytes 98312 | tf_op jit(solution)/shard_map/ppermute | solution.py:284
  148.7 3.7 %collective-permute-start.63 = (f32[64,128]{1,0:T(8,128)S(1)}, f32[64,128]{1,0:T(8,128)S(1)}, u32[]{:S(2)}, u32[]{:S(2)}) collective-permute-start(f32[64,128]{1,0:T(8,128)S(1)} %solve_down.9.refs_0_.refs_2_), channel_id=1, source_target_pairs={{0,3},{1,2},{2,1},{3,0},{4,7},{5,6},{6,5},{7,4},{8,11},{9,10},{10,... | collective-permute-start | bytes 98312 | tf_op jit(solution)/shard_map/ppermute | solution.py:333
  148.8 4.0 %collective-permute-start.62 = (f32[64,128]{1,0:T(8,128)S(1)}, f32[64,128]{1,0:T(8,128)S(1)}, u32[]{:S(2)}, u32[]{:S(2)}) collective-permute-start(f32[64,128]{1,0:T(8,128)S(1)} %solve_down.9.refs_0_.refs_2_), channel_id=1, source_target_pairs={{0,2},{1,3},{2,0},{3,1},{4,6},{5,7},{6,4},{7,5},{8,10},{9,11},{10,... | collective-permute-start | bytes 98312 | tf_op jit(solution)/shard_map/ppermute | solution.py:333
  153.3 5.7 %collective-permute-start.64 = (f32[2,64,128]{2,1,0:T(8,128)S(1)}, f32[2,64,128]{2,1,0:T(8,128)S(1)}, u32[]{:S(2)}, u32[]{:S(2)}) collective-permute-start(f32[2,64,128]{2,1,0:T(8,128)S(1)} %get-tuple-element.122), channel_id=1, source_target_pairs={{0,12},{1,13},{2,14},{3,15},{4,8},{5,9},{6,10},{7,11},{8,4},{9,5},... | collective-permute-start | bytes 196616 | tf_op jit(solution)/shard_map/ppermute | solution.py:300
  154.4 5.4 %collective-permute-start.65 = (f32[2,64,128]{2,1,0:T(8,128)S(1)}, f32[2,64,128]{2,1,0:T(8,128)S(1)}, u32[]{:S(2)}, u32[]{:S(2)}) collective-permute-start(f32[2,64,128]{2,1,0:T(8,128)S(1)} %get-tuple-element.123), channel_id=1, source_target_pairs={{0,8},{1,5},{2,10},{3,7},{4,12},{5,1},{6,14},{7,3},{8,0},{9,13},{1... | collective-permute-start | bytes 196616 | tf_op jit(solution)/shard_map/ppermute | solution.py:300
  156.2 4.3 %collective-permute-start.66 = (f32[2,64,128]{2,1,0:T(8,128)S(1)}, f32[2,64,128]{2,1,0:T(8,128)S(1)}, u32[]{:S(2)}, u32[]{:S(2)}) collective-permute-start(f32[2,64,128]{2,1,0:T(8,128)S(1)} %get-tuple-element.124), channel_id=1, source_target_pairs={{0,4},{1,9},{2,6},{3,11},{4,0},{5,13},{6,2},{7,15},{8,12},{9,1},{1... | collective-permute-start | bytes 196616 | tf_op jit(solution)/shard_map/ppermute | solution.py:300
  160.5 4.9 %collective-permute-start.67 = (f32[64,128]{1,0:T(8,128)S(1)}, f32[64,128]{1,0:T(8,128)S(1)}, u32[]{:S(2)}, u32[]{:S(2)}) collective-permute-start(f32[64,128]{1,0:T(8,128)S(1)} %get-tuple-element.126), channel_id=1, source_target_pairs={{0,16},{4,20},{8,24},{12,28},{16,0},{20,4},{24,8},{28,12},{1,17},{... | collective-permute-start | bytes 98312 | tf_op jit(solution)/shard_map/ppermute | solution.py:284
  165.5 3.5 %collective-permute-start.70 = (f32[64,128]{1,0:T(8,128)S(1)}, f32[64,128]{1,0:T(8,128)S(1)}, u32[]{:S(2)}, u32[]{:S(2)}) collective-permute-start(f32[64,128]{1,0:T(8,128)S(1)} %solve_down.10.refs_0_.refs_1_), channel_id=1, source_target_pairs={{0,3},{1,2},{2,1},{3,0},{4,7},{5,6},{6,5},{7,4},{8,11},{9,10},{10,... | collective-permute-start | bytes 98312 | tf_op jit(solution)/shard_map/ppermute | solution.py:333
  165.6 4.0 %collective-permute-start.69 = (f32[64,128]{1,0:T(8,128)S(1)}, f32[64,128]{1,0:T(8,128)S(1)}, u32[]{:S(2)}, u32[]{:S(2)}) collective-permute-start(f32[64,128]{1,0:T(8,128)S(1)} %solve_down.10.refs_0_.refs_1_), channel_id=1, source_target_pairs={{0,2},{1,3},{2,0},{3,1},{4,6},{5,7},{6,4},{7,5},{8,10},{9,11},{10,... | collective-permute-start | bytes 98312 | tf_op jit(solution)/shard_map/ppermute | solution.py:333
  170.2 5.9 %collective-permute-start.71 = (f32[2,64,128]{2,1,0:T(8,128)S(1)}, f32[2,64,128]{2,1,0:T(8,128)S(1)}, u32[]{:S(2)}, u32[]{:S(2)}) collective-permute-start(f32[2,64,128]{2,1,0:T(8,128)S(1)} %get-tuple-element.127), channel_id=1, source_target_pairs={{0,12},{1,13},{2,14},{3,15},{4,8},{5,9},{6,10},{7,11},{8,4},{9,5},... | collective-permute-start | bytes 196616 | tf_op jit(solution)/shard_map/ppermute | solution.py:300
  171.0 5.3 %collective-permute-start.72 = (f32[2,64,128]{2,1,0:T(8,128)S(1)}, f32[2,64,128]{2,1,0:T(8,128)S(1)}, u32[]{:S(2)}, u32[]{:S(2)}) collective-permute-start(f32[2,64,128]{2,1,0:T(8,128)S(1)} %get-tuple-element.128), channel_id=1, source_target_pairs={{0,8},{1,5},{2,10},{3,7},{4,12},{5,1},{6,14},{7,3},{8,0},{9,13},{1... | collective-permute-start | bytes 196616 | tf_op jit(solution)/shard_map/ppermute | solution.py:300
  172.7 4.3 %collective-permute-start.73 = (f32[2,64,128]{2,1,0:T(8,128)S(1)}, f32[2,64,128]{2,1,0:T(8,128)S(1)}, u32[]{:S(2)}, u32[]{:S(2)}) collective-permute-start(f32[2,64,128]{2,1,0:T(8,128)S(1)} %get-tuple-element.129), channel_id=1, source_target_pairs={{0,4},{1,9},{2,6},{3,11},{4,0},{5,13},{6,2},{7,15},{8,12},{9,1},{1... | collective-permute-start | bytes 196616 | tf_op jit(solution)/shard_map/ppermute | solution.py:300
  177.0 5.0 %collective-permute-start.74 = (f32[64,128]{1,0:T(8,128)S(1)}, f32[64,128]{1,0:T(8,128)S(1)}, u32[]{:S(2)}, u32[]{:S(2)}) collective-permute-start(f32[64,128]{1,0:T(8,128)S(1)} %get-tuple-element.131), channel_id=1, source_target_pairs={{0,16},{4,20},{8,24},{12,28},{16,0},{20,4},{24,8},{28,12},{1,17},{... | collective-permute-start | bytes 98312 | tf_op jit(solution)/shard_map/ppermute | solution.py:284
  (18 other events, 77.2 us)

commit v14 on v9

--- a/solution.py
+++ b/solution.py
@@ -260,6 +260,29 @@
         ),
         name="combine",
     )(*operands.arrays, *after)
+
+
+def last_solve_kernel(terms, n_ins, right_ref, inverse_ref, *refs):
+    ins, others, out_ref = refs[:n_ins], refs[n_ins:-1], refs[-1]
+    for level, other_ref in enumerate(others):
+        out_ref[level + 1] = other_ref[...]
+    value = right_ref[...] - total_of(terms, ins)
+    out_ref[0] = product(halves(value), halves(inverse_ref[0]), True)
+
+
+def last_solve(right, inverse, pieces, others):
+    operands = Operands()
+    terms = [operands.term(piece) for piece in pieces]
+    whole = pl.BlockSpec(memory_space=VMEM)
+    shape = (len(others) + 1,) + right.shape
+    return pl.pallas_call(
+        functools.partial(last_solve_kernel, terms, len(operands.arrays)),
+        out_shape=jax.ShapeDtypeStruct(shape, jnp.float32),
+        in_specs=[whole] * (2 + len(operands.arrays) + len(others)),
+        out_specs=whole,
+        compiler_params=pltpu.CompilerParams(vmem_limit_bytes=8 * MIB),
+        name="last_solve",
+    )(right, inverse, *operands.arrays, *others)
 
 
 def stack_kernel(n_ins, *refs):
@@ -374,8 +397,11 @@
             forward_out = stack(forward, kept[:1])
         pieces = deliver_row(kept + sent)
         after = (forward_out,) if level == levels - 2 else ()
+        if level == 0:
+            backward_out = last_solve(forward[0], inverse, pieces, backward[1:])
+            break
         backward[level] = solve(forward[level], inverse, level, pieces, True, after)
-    return forward_out.reshape(rhs.shape), stack(backward).reshape(rhs.shape)
+    return forward_out.reshape(rhs.shape), backward_out.reshape(rhs.shape)
 
 
 def plain(messages):

time: 176 us -> 175 us (level)
  transfers between devices with their start and end apart: 70 -> 70, of which waited for: 53 -> 54; matrix products, arithmetic and copies ran while one was open for 1% -> 1% of each run, Pallas kernels for 10% -> 10%
where the time goes in v14:
time: 175 us; the launch traced here: 176 us
  waiting for transfers between devices  83.4 us (48%)
  starting transfers between devices  62.2 us (36%)
  Pallas kernels  26.4 us (15%)
  local copies, waits for them, and re-layouts  2.48 us (1%)
    ppermute x10, waiting for transfers between devices, far_exchange(): lax.ppermute(segment, axis, [(i, i ^ size // 2) for i in range(size)])  37 us
    ppermute x30, starting transfers between devices, near_exchange(): received[d] = lax.ppermute(messages[d], ('row', 'col'), pairs)  35.3 us
    ppermute x30, waiting for transfers between devices, near_exchange(): received[d] = lax.ppermute(messages[d], ('row', 'col'), pairs)  31.4 us
    ppermute x30, starting transfers between devices, exchange_each(): lax.ppermute(messages[d], axis, [(i, i ^ d) for i in range(size)])  19.6 us
    ppermute x30, waiting for transfers between devices, exchange_each(): lax.ppermute(messages[d], axis, [(i, i ^ d) for i in range(size)])  15 us
    pallas_call x5, Pallas kernels, gather_blocks(): pl.pallas_call(functools.partial(gather_blocks_kernel, n_row, n_col, leve...  8.39 us
    pallas_call x20, Pallas kernels, couple(): pl.pallas_call(functools.partial(couple_kernel, terms, span), out_shape=[...  7.87 us
    ppermute x10, starting transfers between devices, far_exchange(): lax.ppermute(segment, axis, [(i, i ^ size // 2) for i in range(size)])  7.38 us
  transfers between devices with their start and end apart: 70, of which 54 were waited for; matrix products, arithmetic and copies ran while one was open for 1% of the time, Pallas kernels for 10%

profile of v14, /device:TPU:0, one launch (start us, length us, event | category | flops | bytes accessed | tf_op | source)
XLA Modules:
  0.0 175.7 jit_solution(16466794414613815794)
XLA Ops:
  0.6 1.7 first_solve.1.refs_0_.right_ref
  2.3 4.1 %collective-permute-start = (f32[64,128]{1,0:T(8,128)}, f32[64,128]{1,0:T(8,128)S(1)}, u32[]{:S(2)}, u32[]{:S(2)}) collective-permute-start(f32[64,128]{1,0:T(8,128)} %first_solve.1.refs_0_.right_ref), channel_id=1, source_target_pairs={{0,16},{4,20},{8,24},{12,28},{16,0},{20,4},{24,8},{28,12},{1,17},{... | collective-permute-start | bytes 98312 | tf_op jit(solution)/shard_map/ppermute | solution.py:307
  7.9 2.8 %gather_blocks_0.1.total_ref = f32[32,128,128]{2,1,0:T(8,128)S(1)} custom-call(s32[5,67]{1,0:T(8,128)S(1)} %concatenate.3.slots_ref, f32[5,32,128,128]{3,2,1,0:T(8,128)} %bitcast.14), custom_call_target="tpu_custom_call" | custom-call | flops 524288 | bytes 4194304 | tf_op jit(solution)/shard_map/gather_blocks_0/pallas_call | solution.py:67
  11.1 2.1 %collective-permute-start.3 = (f32[2,64,128]{2,1,0:T(8,128)S(1)}, f32[2,64,128]{2,1,0:T(8,128)S(1)}, u32[]{:S(2)}, u32[]{:S(2)}) collective-permute-start(f32[2,64,128]{2,1,0:T(8,128)S(1)} %combine.10.refs_0_), channel_id=1, source_target_pairs={{0,12},{1,13},{2,14},{3,15},{4,8},{5,9},{6,10},{7,11},{8,4},{9,5},... | collective-permute-start | bytes 196616 | tf_op jit(solution)/shard_map/ppermute | solution.py:325
  14.7 1.8 %collective-permute-done.3.refs_3_ = f32[2,64,128]{2,1,0:T(8,128)S(1)} collective-permute-done((f32[2,64,128]{2,1,0:T(8,128)S(1)}, f32[2,64,128]{2,1,0:T(8,128)S(1)}, u32[]{:S(2)}, u32[]{:S(2)}) %collective-permute-start.3) | collective-permute-done | bytes 65568 | tf_op jit(solution)/shard_map/ppermute | solution.py:325
  16.5 1.0 collective-permute-done.2.refs_2_
  18.5 1.5 collective-permute-start.5
  20.8 1.3 gather_blocks_1.1.refs_6_.total_ref
  22.6 1.1 collective-permute-start.7
  24.8 2.7 %collective-permute-done.7.refs_1_ = f32[64,128]{1,0:T(8,128)S(1)} collective-permute-done((f32[64,128]{1,0:T(8,128)S(1)}, f32[64,128]{1,0:T(8,128)S(1)}, u32[]{:S(2)}, u32[]{:S(2)}) %collective-permute-start.7) | collective-permute-done | bytes 32800 | tf_op jit(solution)/shard_map/ppermute | solution.py:307
  27.5 1.8 %collective-permute-start.10 = (f32[2,64,128]{2,1,0:T(8,128)S(1)}, f32[2,64,128]{2,1,0:T(8,128)S(1)}, u32[]{:S(2)}, u32[]{:S(2)}) collective-permute-start(f32[2,64,128]{2,1,0:T(8,128)S(1)} %combine.11.refs_0_), channel_id=1, source_target_pairs={{0,12},{1,13},{2,14},{3,15},{4,8},{5,9},{6,10},{7,11},{8,4},{9,5},... | collective-permute-start | bytes 196616 | tf_op jit(solution)/shard_map/ppermute | solution.py:325
  29.3 1.1 collective-permute-start.9
  31.0 2.0 %collective-permute-done.10.refs_3_ = f32[2,64,128]{2,1,0:T(8,128)S(1)} collective-permute-done((f32[2,64,128]{2,1,0:T(8,128)S(1)}, f32[2,64,128]{2,1,0:T(8,128)S(1)}, u32[]{:S(2)}, u32[]{:S(2)}) %collective-permute-start.10) | collective-permute-done | bytes 65568 | tf_op jit(solution)/shard_map/ppermute | solution.py:325
  33.0 1.0 collective-permute-done.9.refs_2_
  35.1 1.2 collective-permute-start.12
  37.4 1.5 gather_blocks_2.1.refs_6_.total_ref
  40.8 3.5 %collective-permute-done.14.refs_1_ = f32[64,128]{1,0:T(8,128)S(1)} collective-permute-done((f32[64,128]{1,0:T(8,128)S(1)}, f32[64,128]{1,0:T(8,128)S(1)}, u32[]{:S(2)}, u32[]{:S(2)}) %collective-permute-start.14) | collective-permute-done | bytes 32800 | tf_op jit(solution)/shard_map/ppermute | solution.py:307
  44.3 1.5 collective-permute-start.17
  46.4 1.4 collective-permute-start.15
  47.8 2.3 %collective-permute-done.17.refs_3_ = f32[2,64,128]{2,1,0:T(8,128)S(1)} collective-permute-done((f32[2,64,128]{2,1,0:T(8,128)S(1)}, f32[2,64,128]{2,1,0:T(8,128)S(1)}, u32[]{:S(2)}, u32[]{:S(2)}) %collective-permute-start.17) | collective-permute-done | bytes 65568 | tf_op jit(solution)/shard_map/ppermute | solution.py:325
  51.2 1.8 %collective-permute-start.19 = (f32[64,128]{1,0:T(8,128)S(1)}, f32[64,128]{1,0:T(8,128)S(1)}, u32[]{:S(2)}, u32[]{:S(2)}) collective-permute-start(f32[64,128]{1,0:T(8,128)S(1)} %get-tuple-element.84), channel_id=1, source_target_pairs={{0,2},{1,3},{2,0},{3,1},{4,6},{5,7},{6,4},{7,5},{8,10},{9,11},{10,... | collective-permute-start | bytes 98312 | tf_op jit(solution)/shard_map/ppermute | solution.py:352
  53.6 1.2 gather_blocks_3.1.refs_6_.total_ref
  57.4 2.9 %collective-permute-done.21.refs_1_ = f32[64,128]{1,0:T(8,128)S(1)} collective-permute-done((f32[64,128]{1,0:T(8,128)S(1)}, f32[64,128]{1,0:T(8,128)S(1)}, u32[]{:S(2)}, u32[]{:S(2)}) %collective-permute-start.21) | collective-permute-done | bytes 32800 | tf_op jit(solution)/shard_map/ppermute | solution.py:307
  60.3 1.6 collective-permute-start.24
  61.9 1.1 collective-permute-start.23
  63.8 2.0 %collective-permute-done.24.refs_3_ = f32[2,64,128]{2,1,0:T(8,128)S(1)} collective-permute-done((f32[2,64,128]{2,1,0:T(8,128)S(1)}, f32[2,64,128]{2,1,0:T(8,128)S(1)}, u32[]{:S(2)}, u32[]{:S(2)}) %collective-permute-start.24) | collective-permute-done | bytes 65568 | tf_op jit(solution)/shard_map/ppermute | solution.py:325
  67.8 1.5 collective-permute-start.26
  70.1 1.5 gather_blocks_4.1.refs_6_.total_ref
  73.4 3.8 %collective-permute-done.28.refs_1_ = f32[64,128]{1,0:T(8,128)S(1)} collective-permute-done((f32[64,128]{1,0:T(8,128)S(1)}, f32[64,128]{1,0:T(8,128)S(1)}, u32[]{:S(2)}, u32[]{:S(2)}) %collective-permute-start.28) | collective-permute-done | bytes 32800 | tf_op jit(solution)/shard_map/ppermute | solution.py:307
  77.2 1.2 collective-permute-start.31
  78.4 1.5 collective-permute-start.30
  80.7 2.0 %collective-permute-done.31.refs_3_ = f32[2,64,128]{2,1,0:T(8,128)S(1)} collective-permute-done((f32[2,64,128]{2,1,0:T(8,128)S(1)}, f32[2,64,128]{2,1,0:T(8,128)S(1)}, u32[]{:S(2)}, u32[]{:S(2)}) %collective-permute-start.31) | collective-permute-done | bytes 65568 | tf_op jit(solution)/shard_map/ppermute | solution.py:325
  82.9 1.3 collective-permute-done.29.refs_1_
  84.7 1.1 collective-permute-start.33
  89.2 1.0 collective-permute-start.37
  91.2 1.5 collective-permute-done.37.refs_3_
  92.7 1.5 collective-permute-done.36.refs_2_
  95.3 1.6 collective-permute-start.39
  97.0 1.3 collective-permute-start.40
  98.5 1.5 collective-permute-done.38.refs_1_
  102.0 4.4 %collective-permute-done.41.refs_3_ = f32[64,128]{1,0:T(8,128)S(1)} collective-permute-done((f32[64,128]{1,0:T(8,128)S(1)}, f32[64,128]{1,0:T(8,128)S(1)}, u32[]{:S(2)}, u32[]{:S(2)}) %collective-permute-start.41) | collective-permute-done | bytes 32800 | tf_op jit(solution)/shard_map/ppermute | solution.py:307
  109.4 1.5 collective-permute-done.44.refs_3_
  112.4 1.0 collective-permute-start.45
  113.4 1.8 %collective-permute-start.46 = (f32[2,64,128]{2,1,0:T(8,128)S(1)}, f32[2,64,128]{2,1,0:T(8,128)S(1)}, u32[]{:S(2)}, u32[]{:S(2)}) collective-permute-start(f32[2,64,128]{2,1,0:T(8,128)S(1)} %get-tuple-element.113), channel_id=1, source_target_pairs={{0,8},{1,5},{2,10},{3,7},{4,12},{5,1},{6,14},{7,3},{8,0},{9,13},{1... | collective-permute-start | bytes 196616 | tf_op jit(solution)/shard_map/ppermute | solution.py:325
  116.2 2.0 %collective-permute-done.45.refs_1_ = f32[2,64,128]{2,1,0:T(8,128)S(1)} collective-permute-done((f32[2,64,128]{2,1,0:T(8,128)S(1)}, f32[2,64,128]{2,1,0:T(8,128)S(1)}, u32[]{:S(2)}, u32[]{:S(2)}) %collective-permute-start.45) | collective-permute-done | bytes 65568 | tf_op jit(solution)/shard_map/ppermute | solution.py:325
  119.6 4.8 %collective-permute-done.48.refs_3_ = f32[64,128]{1,0:T(8,128)S(1)} collective-permute-done((f32[64,128]{1,0:T(8,128)S(1)}, f32[64,128]{1,0:T(8,128)S(1)}, u32[]{:S(2)}, u32[]{:S(2)}) %collective-permute-start.48) | collective-permute-done | bytes 32800 | tf_op jit(solution)/shard_map/ppermute | solution.py:307
  124.6 1.1 collective-permute-start.50
  126.5 1.5 collective-permute-done.51.refs_3_
  130.2 1.7 collective-permute-start.53
  131.9 1.0 collective-permute-start.54
  133.2 2.0 %collective-permute-done.52.refs_1_ = f32[2,64,128]{2,1,0:T(8,128)S(1)} collective-permute-done((f32[2,64,128]{2,1,0:T(8,128)S(1)}, f32[2,64,128]{2,1,0:T(8,128)S(1)}, u32[]{:S(2)}, u32[]{:S(2)}) %collective-permute-start.52) | collective-permute-done | bytes 65568 | tf_op jit(solution)/shard_map/ppermute | solution.py:325
  136.3 4.9 %collective-permute-done.55.refs_3_ = f32[64,128]{1,0:T(8,128)S(1)} collective-permute-done((f32[64,128]{1,0:T(8,128)S(1)}, f32[64,128]{1,0:T(8,128)S(1)}, u32[]{:S(2)}, u32[]{:S(2)}) %collective-permute-start.55) | collective-permute-done | bytes 32800 | tf_op jit(solution)/shard_map/ppermute | solution.py:307
  141.5 1.0 collective-permute-start.57
  143.3 1.5 collective-permute-done.58.refs_3_
  146.6 1.9 %collective-permute-start.60 = (f32[2,64,128]{2,1,0:T(8,128)S(1)}, f32[2,64,128]{2,1,0:T(8,128)S(1)}, u32[]{:S(2)}, u32[]{:S(2)}) collective-permute-start(f32[2,64,128]{2,1,0:T(8,128)S(1)} %get-tuple-element.123), channel_id=1, source_target_pairs={{0,8},{1,5},{2,10},{3,7},{4,12},{5,1},{6,14},{7,3},{8,0},{9,13},{1... | collective-permute-start | bytes 196616 | tf_op jit(solution)/shard_map/ppermute | solution.py:325
  148.5 1.4 collective-permute-start.61
  150.1 2.0 %collective-permute-done.59.refs_1_ = f32[2,64,128]{2,1,0:T(8,128)S(1)} collective-permute-done((f32[2,64,128]{2,1,0:T(8,128)S(1)}, f32[2,64,128]{2,1,0:T(8,128)S(1)}, u32[]{:S(2)}, u32[]{:S(2)}) %collective-permute-start.59) | collective-permute-done | bytes 65568 | tf_op jit(solution)/shard_map/ppermute | solution.py:325
  152.9 5.1 %collective-permute-done.62.refs_3_ = f32[64,128]{1,0:T(8,128)S(1)} collective-permute-done((f32[64,128]{1,0:T(8,128)S(1)}, f32[64,128]{1,0:T(8,128)S(1)}, u32[]{:S(2)}, u32[]{:S(2)}) %collective-permute-start.62) | collective-permute-done | bytes 32800 | tf_op jit(solution)/shard_map/ppermute | solution.py:307
  158.3 1.1 collective-permute-start.64
  160.1 1.5 collective-permute-done.65.refs_3_
  163.4 2.0 %collective-permute-start.67 = (f32[2,64,128]{2,1,0:T(8,128)S(1)}, f32[2,64,128]{2,1,0:T(8,128)S(1)}, u32[]{:S(2)}, u32[]{:S(2)}) collective-permute-start(f32[2,64,128]{2,1,0:T(8,128)S(1)} %get-tuple-element.128), channel_id=1, source_target_pairs={{0,8},{1,5},{2,10},{3,7},{4,12},{5,1},{6,14},{7,3},{8,0},{9,13},{1... | collective-permute-start | bytes 196616 | tf_op jit(solution)/shard_map/ppermute | solution.py:325
  165.4 1.2 collective-permute-start.68
  166.9 2.0 %collective-permute-done.66.refs_1_ = f32[2,64,128]{2,1,0:T(8,128)S(1)} collective-permute-done((f32[2,64,128]{2,1,0:T(8,128)S(1)}, f32[2,64,128]{2,1,0:T(8,128)S(1)}, u32[]{:S(2)}, u32[]{:S(2)}) %collective-permute-start.66) | collective-permute-done | bytes 65568 | tf_op jit(solution)/shard_map/ppermute | solution.py:325
  170.0 4.9 %collective-permute-done.69.refs_1_ = f32[64,128]{1,0:T(8,128)S(1)} collective-permute-done((f32[64,128]{1,0:T(8,128)S(1)}, f32[64,128]{1,0:T(8,128)S(1)}, u32[]{:S(2)}, u32[]{:S(2)}) %collective-permute-start.69) | collective-permute-done | bytes 32800 | tf_op jit(solution)/shard_map/ppermute | solution.py:307
  (154 shorter events, 50.8 us)
Async XLA Ops:
  2.3 8.8 %collective-permute-start = (f32[64,128]{1,0:T(8,128)}, f32[64,128]{1,0:T(8,128)S(1)}, u32[]{:S(2)}, u32[]{:S(2)}) collective-permute-start(f32[64,128]{1,0:T(8,128)} %first_solve.1.refs_0_.right_ref), channel_id=1, source_target_pairs={{0,16},{4,20},{8,24},{12,28},{16,0},{20,4},{24,8},{28,12},{1,17},{... | collective-permute-start | bytes 98312 | tf_op jit(solution)/shard_map/ppermute | solution.py:307
  11.1 5.4 %collective-permute-start.3 = (f32[2,64,128]{2,1,0:T(8,128)S(1)}, f32[2,64,128]{2,1,0:T(8,128)S(1)}, u32[]{:S(2)}, u32[]{:S(2)}) collective-permute-start(f32[2,64,128]{2,1,0:T(8,128)S(1)} %combine.10.refs_0_), channel_id=1, source_target_pairs={{0,12},{1,13},{2,14},{3,15},{4,8},{5,9},{6,10},{7,11},{8,4},{9,5},... | collective-permute-start | bytes 196616 | tf_op jit(solution)/shard_map/ppermute | solution.py:325
  13.2 4.3 %collective-permute-start.2 = (f32[2,64,128]{2,1,0:T(8,128)S(1)}, f32[2,64,128]{2,1,0:T(8,128)S(1)}, u32[]{:S(2)}, u32[]{:S(2)}) collective-permute-start(f32[2,64,128]{2,1,0:T(8,128)S(1)} %combine.10.refs_0_), channel_id=1, source_target_pairs={{0,8},{1,5},{2,10},{3,7},{4,12},{5,1},{6,14},{7,3},{8,0},{9,13},{1... | collective-permute-start | bytes 196616 | tf_op jit(solution)/shard_map/ppermute | solution.py:325
  13.7 4.3 %collective-permute-start.1 = (f32[2,64,128]{2,1,0:T(8,128)S(1)}, f32[2,64,128]{2,1,0:T(8,128)S(1)}, u32[]{:S(2)}, u32[]{:S(2)}) collective-permute-start(f32[2,64,128]{2,1,0:T(8,128)S(1)} %combine.10.refs_0_), channel_id=1, source_target_pairs={{0,4},{1,9},{2,6},{3,11},{4,0},{5,13},{6,2},{7,15},{8,12},{9,1},{1... | collective-permute-start | bytes 196616 | tf_op jit(solution)/shard_map/ppermute | solution.py:325
  18.4 3.8 %collective-permute-start.4 = (f32[64,128]{1,0:T(8,128)S(1)}, f32[64,128]{1,0:T(8,128)S(1)}, u32[]{:S(2)}, u32[]{:S(2)}) collective-permute-start(f32[64,128]{1,0:T(8,128)S(1)} %get-tuple-element.69), channel_id=1, source_target_pairs={{0,3},{1,2},{2,1},{3,0},{4,7},{5,6},{6,5},{7,4},{8,11},{9,10},{10,... | collective-permute-start | bytes 98312 | tf_op jit(solution)/shard_map/ppermute | solution.py:352
  18.5 4.0 %collective-permute-start.5 = (f32[64,128]{1,0:T(8,128)S(1)}, f32[64,128]{1,0:T(8,128)S(1)}, u32[]{:S(2)}, u32[]{:S(2)}) collective-permute-start(f32[64,128]{1,0:T(8,128)S(1)} %get-tuple-element.70), channel_id=1, source_target_pairs={{0,2},{1,3},{2,0},{3,1},{4,6},{5,7},{6,4},{7,5},{8,10},{9,11},{10,... | collective-permute-start | bytes 98312 | tf_op jit(solution)/shard_map/ppermute | solution.py:352
  22.6 4.9 %collective-permute-start.7 = (f32[64,128]{1,0:T(8,128)S(1)}, f32[64,128]{1,0:T(8,128)S(1)}, u32[]{:S(2)}, u32[]{:S(2)}) collective-permute-start(f32[64,128]{1,0:T(8,128)S(1)} %solve_up.5.refs_0_.refs_1_), channel_id=1, source_target_pairs={{0,16},{4,20},{8,24},{12,28},{16,0},{20,4},{24,8},{28,12},{1,17},{... | collective-permute-start | bytes 98312 | tf_op jit(solution)/shard_map/ppermute | solution.py:307
  27.5 5.5 %collective-permute-start.10 = (f32[2,64,128]{2,1,0:T(8,128)S(1)}, f32[2,64,128]{2,1,0:T(8,128)S(1)}, u32[]{:S(2)}, u32[]{:S(2)}) collective-permute-start(f32[2,64,128]{2,1,0:T(8,128)S(1)} %combine.11.refs_0_), channel_id=1, source_target_pairs={{0,12},{1,13},{2,14},{3,15},{4,8},{5,9},{6,10},{7,11},{8,4},{9,5},... | collective-permute-start | bytes 196616 | tf_op jit(solution)/shard_map/ppermute | solution.py:325
  29.3 4.7 %collective-permute-start.9 = (f32[2,64,128]{2,1,0:T(8,128)S(1)}, f32[2,64,128]{2,1,0:T(8,128)S(1)}, u32[]{:S(2)}, u32[]{:S(2)}) collective-permute-start(f32[2,64,128]{2,1,0:T(8,128)S(1)} %combine.11.refs_0_), channel_id=1, source_target_pairs={{0,8},{1,5},{2,10},{3,7},{4,12},{5,1},{6,14},{7,3},{8,0},{9,13},{1... | collective-permute-start | bytes 196616 | tf_op jit(solution)/shard_map/ppermute | solution.py:325
  30.4 4.3 %collective-permute-start.8 = (f32[2,64,128]{2,1,0:T(8,128)S(1)}, f32[2,64,128]{2,1,0:T(8,128)S(1)}, u32[]{:S(2)}, u32[]{:S(2)}) collective-permute-start(f32[2,64,128]{2,1,0:T(8,128)S(1)} %combine.11.refs_0_), channel_id=1, source_target_pairs={{0,4},{1,9},{2,6},{3,11},{4,0},{5,13},{6,2},{7,15},{8,12},{9,1},{1... | collective-permute-start | bytes 196616 | tf_op jit(solution)/shard_map/ppermute | solution.py:325
  35.0 3.9 %collective-permute-start.11 = (f32[64,128]{1,0:T(8,128)S(1)}, f32[64,128]{1,0:T(8,128)S(1)}, u32[]{:S(2)}, u32[]{:S(2)}) collective-permute-start(f32[64,128]{1,0:T(8,128)S(1)} %get-tuple-element.76), channel_id=1, source_target_pairs={{0,3},{1,2},{2,1},{3,0},{4,7},{5,6},{6,5},{7,4},{8,11},{9,10},{10,... | collective-permute-start | bytes 98312 | tf_op jit(solution)/shard_map/ppermute | solution.py:352
  35.1 4.1 %collective-permute-start.12 = (f32[64,128]{1,0:T(8,128)S(1)}, f32[64,128]{1,0:T(8,128)S(1)}, u32[]{:S(2)}, u32[]{:S(2)}) collective-permute-start(f32[64,128]{1,0:T(8,128)S(1)} %get-tuple-element.77), channel_id=1, source_target_pairs={{0,2},{1,3},{2,0},{3,1},{4,6},{5,7},{6,4},{7,5},{8,10},{9,11},{10,... | collective-permute-start | bytes 98312 | tf_op jit(solution)/shard_map/ppermute | solution.py:352
  39.4 4.9 %collective-permute-start.14 = (f32[64,128]{1,0:T(8,128)S(1)}, f32[64,128]{1,0:T(8,128)S(1)}, u32[]{:S(2)}, u32[]{:S(2)}) collective-permute-start(f32[64,128]{1,0:T(8,128)S(1)} %solve_up.6.refs_0_.refs_2_), channel_id=1, source_target_pairs={{0,16},{4,20},{8,24},{12,28},{16,0},{20,4},{24,8},{28,12},{1,17},{... | collective-permute-start | bytes 98312 | tf_op jit(solution)/shard_map/ppermute | solution.py:307
  44.3 5.8 %collective-permute-start.17 = (f32[2,64,128]{2,1,0:T(8,128)S(1)}, f32[2,64,128]{2,1,0:T(8,128)S(1)}, u32[]{:S(2)}, u32[]{:S(2)}) collective-permute-start(f32[2,64,128]{2,1,0:T(8,128)S(1)} %combine.12.refs_0_), channel_id=1, source_target_pairs={{0,12},{1,13},{2,14},{3,15},{4,8},{5,9},{6,10},{7,11},{8,4},{9,5},... | collective-permute-start | bytes 196616 | tf_op jit(solution)/shard_map/ppermute | solution.py:325
  45.8 4.3 %collective-permute-start.16 = (f32[2,64,128]{2,1,0:T(8,128)S(1)}, f32[2,64,128]{2,1,0:T(8,128)S(1)}, u32[]{:S(2)}, u32[]{:S(2)}) collective-permute-start(f32[2,64,128]{2,1,0:T(8,128)S(1)} %combine.12.refs_0_), channel_id=1, source_target_pairs={{0,8},{1,5},{2,10},{3,7},{4,12},{5,1},{6,14},{7,3},{8,0},{9,13},{1... | collective-permute-start | bytes 196616 | tf_op jit(solution)/shard_map/ppermute | solution.py:325
  46.4 4.4 %collective-permute-start.15 = (f32[2,64,128]{2,1,0:T(8,128)S(1)}, f32[2,64,128]{2,1,0:T(8,128)S(1)}, u32[]{:S(2)}, u32[]{:S(2)}) collective-permute-start(f32[2,64,128]{2,1,0:T(8,128)S(1)} %combine.12.refs_0_), channel_id=1, source_target_pairs={{0,4},{1,9},{2,6},{3,11},{4,0},{5,13},{6,2},{7,15},{8,12},{9,1},{1... | collective-permute-start | bytes 196616 | tf_op jit(solution)/shard_map/ppermute | solution.py:325
  51.2 3.7 %collective-permute-start.18 = (f32[64,128]{1,0:T(8,128)S(1)}, f32[64,128]{1,0:T(8,128)S(1)}, u32[]{:S(2)}, u32[]{:S(2)}) collective-permute-start(f32[64,128]{1,0:T(8,128)S(1)} %get-tuple-element.83), channel_id=1, source_target_pairs={{0,3},{1,2},{2,1},{3,0},{4,7},{5,6},{6,5},{7,4},{8,11},{9,10},{10,... | collective-permute-start | bytes 98312 | tf_op jit(solution)/shard_map/ppermute | solution.py:352
  51.2 4.0 %collective-permute-start.19 = (f32[64,128]{1,0:T(8,128)S(1)}, f32[64,128]{1,0:T(8,128)S(1)}, u32[]{:S(2)}, u32[]{:S(2)}) collective-permute-start(f32[64,128]{1,0:T(8,128)S(1)} %get-tuple-element.84), channel_id=1, source_target_pairs={{0,2},{1,3},{2,0},{3,1},{4,6},{5,7},{6,4},{7,5},{8,10},{9,11},{10,... | collective-permute-start | bytes 98312 | tf_op jit(solution)/shard_map/ppermute | solution.py:352
  55.4 4.9 %collective-permute-start.21 = (f32[64,128]{1,0:T(8,128)S(1)}, f32[64,128]{1,0:T(8,128)S(1)}, u32[]{:S(2)}, u32[]{:S(2)}) collective-permute-start(f32[64,128]{1,0:T(8,128)S(1)} %solve_up.7.refs_0_.refs_3_), channel_id=1, source_target_pairs={{0,16},{4,20},{8,24},{12,28},{16,0},{20,4},{24,8},{28,12},{1,17},{... | collective-permute-start | bytes 98312 | tf_op jit(solution)/shard_map/ppermute | solution.py:307
  60.3 5.5 %collective-permute-start.24 = (f32[2,64,128]{2,1,0:T(8,128)S(1)}, f32[2,64,128]{2,1,0:T(8,128)S(1)}, u32[]{:S(2)}, u32[]{:S(2)}) collective-permute-start(f32[2,64,128]{2,1,0:T(8,128)S(1)} %combine.13.refs_0_), channel_id=1, source_target_pairs={{0,12},{1,13},{2,14},{3,15},{4,8},{5,9},{6,10},{7,11},{8,4},{9,5},... | collective-permute-start | bytes 196616 | tf_op jit(solution)/shard_map/ppermute | solution.py:325
  61.9 4.7 %collective-permute-start.23 = (f32[2,64,128]{2,1,0:T(8,128)S(1)}, f32[2,64,128]{2,1,0:T(8,128)S(1)}, u32[]{:S(2)}, u32[]{:S(2)}) collective-permute-start(f32[2,64,128]{2,1,0:T(8,128)S(1)} %combine.13.refs_0_), channel_id=1, source_target_pairs={{0,8},{1,5},{2,10},{3,7},{4,12},{5,1},{6,14},{7,3},{8,0},{9,13},{1... | collective-permute-start | bytes 196616 | tf_op jit(solution)/shard_map/ppermute | solution.py:325
  63.0 4.3 %collective-permute-start.22 = (f32[2,64,128]{2,1,0:T(8,128)S(1)}, f32[2,64,128]{2,1,0:T(8,128)S(1)}, u32[]{:S(2)}, u32[]{:S(2)}) collective-permute-start(f32[2,64,128]{2,1,0:T(8,128)S(1)} %combine.13.refs_0_), channel_id=1, source_target_pairs={{0,4},{1,9},{2,6},{3,11},{4,0},{5,13},{6,2},{7,15},{8,12},{9,1},{1... | collective-permute-start | bytes 196616 | tf_op jit(solution)/shard_map/ppermute | solution.py:325
  67.7 3.9 %collective-permute-start.25 = (f32[64,128]{1,0:T(8,128)S(1)}, f32[64,128]{1,0:T(8,128)S(1)}, u32[]{:S(2)}, u32[]{:S(2)}) collective-permute-start(f32[64,128]{1,0:T(8,128)S(1)} %get-tuple-element.90), channel_id=1, source_target_pairs={{0,3},{1,2},{2,1},{3,0},{4,7},{5,6},{6,5},{7,4},{8,11},{9,10},{10,... | collective-permute-start | bytes 98312 | tf_op jit(solution)/shard_map/ppermute | solution.py:352
  67.8 4.0 %collective-permute-start.26 = (f32[64,128]{1,0:T(8,128)S(1)}, f32[64,128]{1,0:T(8,128)S(1)}, u32[]{:S(2)}, u32[]{:S(2)}) collective-permute-start(f32[64,128]{1,0:T(8,128)S(1)} %get-tuple-element.91), channel_id=1, source_target_pairs={{0,2},{1,3},{2,0},{3,1},{4,6},{5,7},{6,4},{7,5},{8,10},{9,11},{10,... | collective-permute-start | bytes 98312 | tf_op jit(solution)/shard_map/ppermute | solution.py:352
  72.0 5.2 %collective-permute-start.28 = (f32[64,128]{1,0:T(8,128)S(1)}, f32[64,128]{1,0:T(8,128)S(1)}, u32[]{:S(2)}, u32[]{:S(2)}) collective-permute-start(f32[64,128]{1,0:T(8,128)S(1)} %solve_up.8.refs_0_.refs_4_), channel_id=1, source_target_pairs={{0,16},{4,20},{8,24},{12,28},{16,0},{20,4},{24,8},{28,12},{1,17},{... | collective-permute-start | bytes 98312 | tf_op jit(solution)/shard_map/ppermute | solution.py:307
  77.2 5.5 %collective-permute-start.31 = (f32[2,64,128]{2,1,0:T(8,128)S(1)}, f32[2,64,128]{2,1,0:T(8,128)S(1)}, u32[]{:S(2)}, u32[]{:S(2)}) collective-permute-start(f32[2,64,128]{2,1,0:T(8,128)S(1)} %combine.14.refs_0_), channel_id=1, source_target_pairs={{0,12},{1,13},{2,14},{3,15},{4,8},{5,9},{6,10},{7,11},{8,4},{9,5},... | collective-permute-start | bytes 196616 | tf_op jit(solution)/shard_map/ppermute | solution.py:325
  78.4 4.5 %collective-permute-start.30 = (f32[2,64,128]{2,1,0:T(8,128)S(1)}, f32[2,64,128]{2,1,0:T(8,128)S(1)}, u32[]{:S(2)}, u32[]{:S(2)}) collective-permute-start(f32[2,64,128]{2,1,0:T(8,128)S(1)} %combine.14.refs_0_), channel_id=1, source_target_pairs={{0,8},{1,5},{2,10},{3,7},{4,12},{5,1},{6,14},{7,3},{8,0},{9,13},{1... | collective-permute-start | bytes 196616 | tf_op jit(solution)/shard_map/ppermute | solution.py:325
  80.0 4.3 %collective-permute-start.29 = (f32[2,64,128]{2,1,0:T(8,128)S(1)}, f32[2,64,128]{2,1,0:T(8,128)S(1)}, u32[]{:S(2)}, u32[]{:S(2)}) collective-permute-start(f32[2,64,128]{2,1,0:T(8,128)S(1)} %combine.14.refs_0_), channel_id=1, source_target_pairs={{0,4},{1,9},{2,6},{3,11},{4,0},{5,13},{6,2},{7,15},{8,12},{9,1},{1... | collective-permute-start | bytes 196616 | tf_op jit(solution)/shard_map/ppermute | solution.py:325
  84.6 3.4 %collective-permute-start.32 = (f32[64,128]{1,0:T(8,128)S(1)}, f32[64,128]{1,0:T(8,128)S(1)}, u32[]{:S(2)}, u32[]{:S(2)}) collective-permute-start(f32[64,128]{1,0:T(8,128)S(1)} %get-tuple-element.97), channel_id=1, source_target_pairs={{0,3},{1,2},{2,1},{3,0},{4,7},{5,6},{6,5},{7,4},{8,11},{9,10},{10,... | collective-permute-start | bytes 98312 | tf_op jit(solution)/shard_map/ppermute | solution.py:352
  84.7 4.2 %collective-permute-start.33 = (f32[64,128]{1,0:T(8,128)S(1)}, f32[64,128]{1,0:T(8,128)S(1)}, u32[]{:S(2)}, u32[]{:S(2)}) collective-permute-start(f32[64,128]{1,0:T(8,128)S(1)} %get-tuple-element.98), channel_id=1, source_target_pairs={{0,2},{1,3},{2,0},{3,1},{4,6},{5,7},{6,4},{7,5},{8,10},{9,11},{10,... | collective-permute-start | bytes 98312 | tf_op jit(solution)/shard_map/ppermute | solution.py:352
  89.2 3.5 %collective-permute-start.37 = (f32[64,128]{1,0:T(8,128)S(1)}, f32[64,128]{1,0:T(8,128)S(1)}, u32[]{:S(2)}, u32[]{:S(2)}) collective-permute-start(f32[64,128]{1,0:T(8,128)S(1)} %solve_down.5.refs_0_.refs_6_), channel_id=1, source_target_pairs={{0,3},{1,2},{2,1},{3,0},{4,7},{5,6},{6,5},{7,4},{8,11},{9,10},{10,... | collective-permute-start | bytes 98312 | tf_op jit(solution)/shard_map/ppermute | solution.py:352
  90.2 3.9 %collective-permute-start.36 = (f32[64,128]{1,0:T(8,128)S(1)}, f32[64,128]{1,0:T(8,128)S(1)}, u32[]{:S(2)}, u32[]{:S(2)}) collective-permute-start(f32[64,128]{1,0:T(8,128)S(1)} %solve_down.5.refs_0_.refs_6_), channel_id=1, source_target_pairs={{0,2},{1,3},{2,0},{3,1},{4,6},{5,7},{6,4},{7,5},{8,10},{9,11},{10,... | collective-permute-start | bytes 98312 | tf_op jit(solution)/shard_map/ppermute | solution.py:352
  94.7 5.4 %collective-permute-start.38 = (f32[2,64,128]{2,1,0:T(8,128)S(1)}, f32[2,64,128]{2,1,0:T(8,128)S(1)}, u32[]{:S(2)}, u32[]{:S(2)}) collective-permute-start(f32[2,64,128]{2,1,0:T(8,128)S(1)} %get-tuple-element.107), channel_id=1, source_target_pairs={{0,12},{1,13},{2,14},{3,15},{4,8},{5,9},{6,10},{7,11},{8,4},{9,5},... | collective-permute-start | bytes 196616 | tf_op jit(solution)/shard_map/ppermute | solution.py:325
  95.3 5.3 %collective-permute-start.39 = (f32[2,64,128]{2,1,0:T(8,128)S(1)}, f32[2,64,128]{2,1,0:T(8,128)S(1)}, u32[]{:S(2)}, u32[]{:S(2)}) collective-permute-start(f32[2,64,128]{2,1,0:T(8,128)S(1)} %get-tuple-element.108), channel_id=1, source_target_pairs={{0,8},{1,5},{2,10},{3,7},{4,12},{5,1},{6,14},{7,3},{8,0},{9,13},{1... | collective-permute-start | bytes 196616 | tf_op jit(solution)/shard_map/ppermute | solution.py:325
  97.0 4.3 %collective-permute-start.40 = (f32[2,64,128]{2,1,0:T(8,128)S(1)}, f32[2,64,128]{2,1,0:T(8,128)S(1)}, u32[]{:S(2)}, u32[]{:S(2)}) collective-permute-start(f32[2,64,128]{2,1,0:T(8,128)S(1)} %get-tuple-element.109), channel_id=1, source_target_pairs={{0,4},{1,9},{2,6},{3,11},{4,0},{5,13},{6,2},{7,15},{8,12},{9,1},{1... | collective-permute-start | bytes 196616 | tf_op jit(solution)/shard_map/ppermute | solution.py:325
  101.3 5.2 %collective-permute-start.41 = (f32[64,128]{1,0:T(8,128)S(1)}, f32[64,128]{1,0:T(8,128)S(1)}, u32[]{:S(2)}, u32[]{:S(2)}) collective-permute-start(f32[64,128]{1,0:T(8,128)S(1)} %get-tuple-element.111), channel_id=1, source_target_pairs={{0,16},{4,20},{8,24},{12,28},{16,0},{20,4},{24,8},{28,12},{1,17},{... | collective-permute-start | bytes 98312 | tf_op jit(solution)/shard_map/ppermute | solution.py:307
  107.5 3.4 %collective-permute-start.44 = (f32[64,128]{1,0:T(8,128)S(1)}, f32[64,128]{1,0:T(8,128)S(1)}, u32[]{:S(2)}, u32[]{:S(2)}) collective-permute-start(f32[64,128]{1,0:T(8,128)S(1)} %solve_down.6.refs_0_.refs_5_), channel_id=1, source_target_pairs={{0,3},{1,2},{2,1},{3,0},{4,7},{5,6},{6,5},{7,4},{8,11},{9,10},{10,... | collective-permute-start | bytes 98312 | tf_op jit(solution)/shard_map/ppermute | solution.py:352
  107.6 4.3 %collective-permute-start.43 = (f32[64,128]{1,0:T(8,128)S(1)}, f32[64,128]{1,0:T(8,128)S(1)}, u32[]{:S(2)}, u32[]{:S(2)}) collective-permute-start(f32[64,128]{1,0:T(8,128)S(1)} %solve_down.6.refs_0_.refs_5_), channel_id=1, source_target_pairs={{0,2},{1,3},{2,0},{3,1},{4,6},{5,7},{6,4},{7,5},{8,10},{9,11},{10,... | collective-permute-start | bytes 98312 | tf_op jit(solution)/shard_map/ppermute | solution.py:352
  108.5 3.3 %collective-permute-start.42 = (f32[64,128]{1,0:T(8,128)S(1)}, f32[64,128]{1,0:T(8,128)S(1)}, u32[]{:S(2)}, u32[]{:S(2)}) collective-permute-start(f32[64,128]{1,0:T(8,128)S(1)} %solve_down.6.refs_0_.refs_5_), channel_id=1, source_target_pairs={{0,1},{1,0},{2,3},{3,2},{4,5},{5,4},{6,7},{7,6},{8,9},{9,8},{10,11... | collective-permute-start | bytes 98312 | tf_op jit(solution)/shard_map/ppermute | solution.py:352
  112.4 5.8 %collective-permute-start.45 = (f32[2,64,128]{2,1,0:T(8,128)S(1)}, f32[2,64,128]{2,1,0:T(8,128)S(1)}, u32[]{:S(2)}, u32[]{:S(2)}) collective-permute-start(f32[2,64,128]{2,1,0:T(8,128)S(1)} %get-tuple-element.112), channel_id=1, source_target_pairs={{0,12},{1,13},{2,14},{3,15},{4,8},{5,9},{6,10},{7,11},{8,4},{9,5},... | collective-permute-start | bytes 196616 | tf_op jit(solution)/shard_map/ppermute | solution.py:325
  113.4 5.2 %collective-permute-start.46 = (f32[2,64,128]{2,1,0:T(8,128)S(1)}, f32[2,64,128]{2,1,0:T(8,128)S(1)}, u32[]{:S(2)}, u32[]{:S(2)}) collective-permute-start(f32[2,64,128]{2,1,0:T(8,128)S(1)} %get-tuple-element.113), channel_id=1, source_target_pairs={{0,8},{1,5},{2,10},{3,7},{4,12},{5,1},{6,14},{7,3},{8,0},{9,13},{1... | collective-permute-start | bytes 196616 | tf_op jit(solution)/shard_map/ppermute | solution.py:325
  115.2 4.3 %collective-permute-start.47 = (f32[2,64,128]{2,1,0:T(8,128)S(1)}, f32[2,64,128]{2,1,0:T(8,128)S(1)}, u32[]{:S(2)}, u32[]{:S(2)}) collective-permute-start(f32[2,64,128]{2,1,0:T(8,128)S(1)} %get-tuple-element.114), channel_id=1, source_target_pairs={{0,4},{1,9},{2,6},{3,11},{4,0},{5,13},{6,2},{7,15},{8,12},{9,1},{1... | collective-permute-start | bytes 196616 | tf_op jit(solution)/shard_map/ppermute | solution.py:325
  119.5 4.9 %collective-permute-start.48 = (f32[64,128]{1,0:T(8,128)S(1)}, f32[64,128]{1,0:T(8,128)S(1)}, u32[]{:S(2)}, u32[]{:S(2)}) collective-permute-start(f32[64,128]{1,0:T(8,128)S(1)} %get-tuple-element.116), channel_id=1, source_target_pairs={{0,16},{4,20},{8,24},{12,28},{16,0},{20,4},{24,8},{28,12},{1,17},{... | collective-permute-start | bytes 98312 | tf_op jit(solution)/shard_map/ppermute | solution.py:307
  124.5 3.4 %collective-permute-start.51 = (f32[64,128]{1,0:T(8,128)S(1)}, f32[64,128]{1,0:T(8,128)S(1)}, u32[]{:S(2)}, u32[]{:S(2)}) collective-permute-start(f32[64,128]{1,0:T(8,128)S(1)} %solve_down.7.refs_0_.refs_4_), channel_id=1, source_target_pairs={{0,3},{1,2},{2,1},{3,0},{4,7},{5,6},{6,5},{7,4},{8,11},{9,10},{10,... | collective-permute-start | bytes 98312 | tf_op jit(solution)/shard_map/ppermute | solution.py:352
  124.6 4.2 %collective-permute-start.50 = (f32[64,128]{1,0:T(8,128)S(1)}, f32[64,128]{1,0:T(8,128)S(1)}, u32[]{:S(2)}, u32[]{:S(2)}) collective-permute-start(f32[64,128]{1,0:T(8,128)S(1)} %solve_down.7.refs_0_.refs_4_), channel_id=1, source_target_pairs={{0,2},{1,3},{2,0},{3,1},{4,6},{5,7},{6,4},{7,5},{8,10},{9,11},{10,... | collective-permute-start | bytes 98312 | tf_op jit(solution)/shard_map/ppermute | solution.py:352
  125.7 3.1 %collective-permute-start.49 = (f32[64,128]{1,0:T(8,128)S(1)}, f32[64,128]{1,0:T(8,128)S(1)}, u32[]{:S(2)}, u32[]{:S(2)}) collective-permute-start(f32[64,128]{1,0:T(8,128)S(1)} %solve_down.7.refs_0_.refs_4_), channel_id=1, source_target_pairs={{0,1},{1,0},{2,3},{3,2},{4,5},{5,4},{6,7},{7,6},{8,9},{9,8},{10,11... | collective-permute-start | bytes 98312 | tf_op jit(solution)/shard_map/ppermute | solution.py:352
  129.4 5.9 %collective-permute-start.52 = (f32[2,64,128]{2,1,0:T(8,128)S(1)}, f32[2,64,128]{2,1,0:T(8,128)S(1)}, u32[]{:S(2)}, u32[]{:S(2)}) collective-permute-start(f32[2,64,128]{2,1,0:T(8,128)S(1)} %get-tuple-element.117), channel_id=1, source_target_pairs={{0,12},{1,13},{2,14},{3,15},{4,8},{5,9},{6,10},{7,11},{8,4},{9,5},... | collective-permute-start | bytes 196616 | tf_op jit(solution)/shard_map/ppermute | solution.py:325
  130.2 5.2 %collective-permute-start.53 = (f32[2,64,128]{2,1,0:T(8,128)S(1)}, f32[2,64,128]{2,1,0:T(8,128)S(1)}, u32[]{:S(2)}, u32[]{:S(2)}) collective-permute-start(f32[2,64,128]{2,1,0:T(8,128)S(1)} %get-tuple-element.118), channel_id=1, source_target_pairs={{0,8},{1,5},{2,10},{3,7},{4,12},{5,1},{6,14},{7,3},{8,0},{9,13},{1... | collective-permute-start | bytes 196616 | tf_op jit(solution)/shard_map/ppermute | solution.py:325
  131.9 4.3 %collective-permute-start.54 = (f32[2,64,128]{2,1,0:T(8,128)S(1)}, f32[2,64,128]{2,1,0:T(8,128)S(1)}, u32[]{:S(2)}, u32[]{:S(2)}) collective-permute-start(f32[2,64,128]{2,1,0:T(8,128)S(1)} %get-tuple-element.119), channel_id=1, source_target_pairs={{0,4},{1,9},{2,6},{3,11},{4,0},{5,13},{6,2},{7,15},{8,12},{9,1},{1... | collective-permute-start | bytes 196616 | tf_op jit(solution)/shard_map/ppermute | solution.py:325
  136.2 5.0 %collective-permute-start.55 = (f32[64,128]{1,0:T(8,128)S(1)}, f32[64,128]{1,0:T(8,128)S(1)}, u32[]{:S(2)}, u32[]{:S(2)}) collective-permute-start(f32[64,128]{1,0:T(8,128)S(1)} %get-tuple-element.121), channel_id=1, source_target_pairs={{0,16},{4,20},{8,24},{12,28},{16,0},{20,4},{24,8},{28,12},{1,17},{... | collective-permute-start | bytes 98312 | tf_op jit(solution)/shard_map/ppermute | solution.py:307
  141.4 3.4 %collective-permute-start.58 = (f32[64,128]{1,0:T(8,128)S(1)}, f32[64,128]{1,0:T(8,128)S(1)}, u32[]{:S(2)}, u32[]{:S(2)}) collective-permute-start(f32[64,128]{1,0:T(8,128)S(1)} %solve_down.8.refs_0_.refs_3_), channel_id=1, source_target_pairs={{0,3},{1,2},{2,1},{3,0},{4,7},{5,6},{6,5},{7,4},{8,11},{9,10},{10,... | collective-permute-start | bytes 98312 | tf_op jit(solution)/shard_map/ppermute | solution.py:352
  141.5 4.3 %collective-permute-start.57 = (f32[64,128]{1,0:T(8,128)S(1)}, f32[64,128]{1,0:T(8,128)S(1)}, u32[]{:S(2)}, u32[]{:S(2)}) collective-permute-start(f32[64,128]{1,0:T(8,128)S(1)} %solve_down.8.refs_0_.refs_3_), channel_id=1, source_target_pairs={{0,2},{1,3},{2,0},{3,1},{4,6},{5,7},{6,4},{7,5},{8,10},{9,11},{10,... | collective-permute-start | bytes 98312 | tf_op jit(solution)/shard_map/ppermute | solution.py:352
  142.5 3.2 %collective-permute-start.56 = (f32[64,128]{1,0:T(8,128)S(1)}, f32[64,128]{1,0:T(8,128)S(1)}, u32[]{:S(2)}, u32[]{:S(2)}) collective-permute-start(f32[64,128]{1,0:T(8,128)S(1)} %solve_down.8.refs_0_.refs_3_), channel_id=1, source_target_pairs={{0,1},{1,0},{2,3},{3,2},{4,5},{5,4},{6,7},{7,6},{8,9},{9,8},{10,11... | collective-permute-start | bytes 98312 | tf_op jit(solution)/shard_map/ppermute | solution.py:352
  146.3 5.8 %collective-permute-start.59 = (f32[2,64,128]{2,1,0:T(8,128)S(1)}, f32[2,64,128]{2,1,0:T(8,128)S(1)}, u32[]{:S(2)}, u32[]{:S(2)}) collective-permute-start(f32[2,64,128]{2,1,0:T(8,128)S(1)} %get-tuple-element.122), channel_id=1, source_target_pairs={{0,12},{1,13},{2,14},{3,15},{4,8},{5,9},{6,10},{7,11},{8,4},{9,5},... | collective-permute-start | bytes 196616 | tf_op jit(solution)/shard_map/ppermute | solution.py:325
  146.6 5.5 %collective-permute-start.60 = (f32[2,64,128]{2,1,0:T(8,128)S(1)}, f32[2,64,128]{2,1,0:T(8,128)S(1)}, u32[]{:S(2)}, u32[]{:S(2)}) collective-permute-start(f32[2,64,128]{2,1,0:T(8,128)S(1)} %get-tuple-element.123), channel_id=1, source_target_pairs={{0,8},{1,5},{2,10},{3,7},{4,12},{5,1},{6,14},{7,3},{8,0},{9,13},{1... | collective-permute-start | bytes 196616 | tf_op jit(solution)/shard_map/ppermute | solution.py:325
  148.5 4.3 %collective-permute-start.61 = (f32[2,64,128]{2,1,0:T(8,128)S(1)}, f32[2,64,128]{2,1,0:T(8,128)S(1)}, u32[]{:S(2)}, u32[]{:S(2)}) collective-permute-start(f32[2,64,128]{2,1,0:T(8,128)S(1)} %get-tuple-element.124), channel_id=1, source_target_pairs={{0,4},{1,9},{2,6},{3,11},{4,0},{5,13},{6,2},{7,15},{8,12},{9,1},{1... | collective-permute-start | bytes 196616 | tf_op jit(solution)/shard_map/ppermute | solution.py:325
  152.8 5.2 %collective-permute-start.62 = (f32[64,128]{1,0:T(8,128)S(1)}, f32[64,128]{1,0:T(8,128)S(1)}, u32[]{:S(2)}, u32[]{:S(2)}) collective-permute-start(f32[64,128]{1,0:T(8,128)S(1)} %get-tuple-element.126), channel_id=1, source_target_pairs={{0,16},{4,20},{8,24},{12,28},{16,0},{20,4},{24,8},{28,12},{1,17},{... | collective-permute-start | bytes 98312 | tf_op jit(solution)/shard_map/ppermute | solution.py:307
  158.2 3.4 %collective-permute-start.65 = (f32[64,128]{1,0:T(8,128)S(1)}, f32[64,128]{1,0:T(8,128)S(1)}, u32[]{:S(2)}, u32[]{:S(2)}) collective-permute-start(f32[64,128]{1,0:T(8,128)S(1)} %solve_down.9.refs_0_.refs_2_), channel_id=1, source_target_pairs={{0,3},{1,2},{2,1},{3,0},{4,7},{5,6},{6,5},{7,4},{8,11},{9,10},{10,... | collective-permute-start | bytes 98312 | tf_op jit(solution)/shard_map/ppermute | solution.py:352
  158.3 4.3 %collective-permute-start.64 = (f32[64,128]{1,0:T(8,128)S(1)}, f32[64,128]{1,0:T(8,128)S(1)}, u32[]{:S(2)}, u32[]{:S(2)}) collective-permute-start(f32[64,128]{1,0:T(8,128)S(1)} %solve_down.9.refs_0_.refs_2_), channel_id=1, source_target_pairs={{0,2},{1,3},{2,0},{3,1},{4,6},{5,7},{6,4},{7,5},{8,10},{9,11},{10,... | collective-permute-start | bytes 98312 | tf_op jit(solution)/shard_map/ppermute | solution.py:352
  159.3 3.2 %collective-permute-start.63 = (f32[64,128]{1,0:T(8,128)S(1)}, f32[64,128]{1,0:T(8,128)S(1)}, u32[]{:S(2)}, u32[]{:S(2)}) collective-permute-start(f32[64,128]{1,0:T(8,128)S(1)} %solve_down.9.refs_0_.refs_2_), channel_id=1, source_target_pairs={{0,1},{1,0},{2,3},{3,2},{4,5},{5,4},{6,7},{7,6},{8,9},{9,8},{10,11... | collective-permute-start | bytes 98312 | tf_op jit(solution)/shard_map/ppermute | solution.py:352
  163.1 5.8 %collective-permute-start.66 = (f32[2,64,128]{2,1,0:T(8,128)S(1)}, f32[2,64,128]{2,1,0:T(8,128)S(1)}, u32[]{:S(2)}, u32[]{:S(2)}) collective-permute-start(f32[2,64,128]{2,1,0:T(8,128)S(1)} %get-tuple-element.127), channel_id=1, source_target_pairs={{0,12},{1,13},{2,14},{3,15},{4,8},{5,9},{6,10},{7,11},{8,4},{9,5},... | collective-permute-start | bytes 196616 | tf_op jit(solution)/shard_map/ppermute | solution.py:325
  163.4 5.6 %collective-permute-start.67 = (f32[2,64,128]{2,1,0:T(8,128)S(1)}, f32[2,64,128]{2,1,0:T(8,128)S(1)}, u32[]{:S(2)}, u32[]{:S(2)}) collective-permute-start(f32[2,64,128]{2,1,0:T(8,128)S(1)} %get-tuple-element.128), channel_id=1, source_target_pairs={{0,8},{1,5},{2,10},{3,7},{4,12},{5,1},{6,14},{7,3},{8,0},{9,13},{1... | collective-permute-start | bytes 196616 | tf_op jit(solution)/shard_map/ppermute | solution.py:325
  165.4 4.3 %collective-permute-start.68 = (f32[2,64,128]{2,1,0:T(8,128)S(1)}, f32[2,64,128]{2,1,0:T(8,128)S(1)}, u32[]{:S(2)}, u32[]{:S(2)}) collective-permute-start(f32[2,64,128]{2,1,0:T(8,128)S(1)} %get-tuple-element.129), channel_id=1, source_target_pairs={{0,4},{1,9},{2,6},{3,11},{4,0},{5,13},{6,2},{7,15},{8,12},{9,1},{1... | collective-permute-start | bytes 196616 | tf_op jit(solution)/shard_map/ppermute | solution.py:325
  169.7 5.1 %collective-permute-start.69 = (f32[64,128]{1,0:T(8,128)S(1)}, f32[64,128]{1,0:T(8,128)S(1)}, u32[]{:S(2)}, u32[]{:S(2)}) collective-permute-start(f32[64,128]{1,0:T(8,128)S(1)} %get-tuple-element.131), channel_id=1, source_target_pairs={{0,16},{4,20},{8,24},{12,28},{16,0},{20,4},{24,8},{28,12},{1,17},{... | collective-permute-start | bytes 98312 | tf_op jit(solution)/shard_map/ppermute | solution.py:307
  (13 other events, 57.6 us)
